TPU v7x, 32 devices: a whole 2x2x4 slice. The times are simulated.
32 devices in a mesh: seq: 8 (over z, x), head: 4 (over y, core).
Axes of the slice: x: 2, y: 2, z: 4, core: 2. Of those that a mesh axis runs over, the one named last changes fastest.
Arguments:
- query_rows: bfloat16 [2048, 4096], P('seq', 'head'), may hold values from -6 to 6
- key_rows: bfloat16 [2048, 4096], P('seq', 'head'), may hold values from -6 to 6
- value_rows: bfloat16 [2048, 4096], P('seq', 'head'), may hold values from -150 to 150
- log_decay: float32 [32, 2048], P('head', 'seq'), may hold values from -3 to 0
- out_grad: bfloat16 [2048, 4096], P('seq', 'head'), may hold values from -6 to 6
- norm_gain: float32 [4096], P('head'), may hold values from 0.1 to 1.9
- state_in: float32 [32, 128, 128], P('head'), may hold values from -96 to 96
- state_out_grad: float32 [32, 128, 128], P('head'), may hold values from -0.4375 to 0.4375
Outputs:
- query_grad: bfloat16 [2048, 4096], P('seq', 'head')
- key_grad: bfloat16 [2048, 4096], P('seq', 'head')
- value_grad: bfloat16 [2048, 4096], P('seq', 'head')
- state_in_grad: float32 [32, 128, 128], P('head')
All inputs are finite; a program needn't handle non-finite values.
Results may differ from a plain program's by a relative error of at most 0.0059.
Values sent between devices are 32-bit elements; how exact they have to be, the bound alone decides.
No kernel may reach another device: no remote copies, remote signals or barrier semaphores. Data moves between devices by JAX's collectives and lax.ppermute only.
A program may use at most 128 MiB of HBM per device.

v0:
```python
import jax
import jax.numpy as jnp
from jax import lax
from jax.sharding import PartitionSpec as P

EPSILON = 1e-06


def prefix(value, axis, join, neutral, backward):
    count, mine = (lax.axis_size(axis), lax.axis_index(axis))
    pieces = jax.tree.map(lambda part: lax.all_gather(part, axis), value)
    if backward:
        pieces = jax.tree.map(lambda part: part[::-1], pieces)
        mine = count - 1 - mine
    total = jax.tree.map(
        lambda part, zero: jnp.full_like(part, 0) + jnp.asarray(zero, part.dtype), value, neutral
    )

    def step(position, total):
        longer = join(total, jax.tree.map(lambda part: part[position], pieces))
        return jax.tree.map(lambda new, old: jnp.where(position < mine, new, old), longer, total)

    return lax.fori_loop(0, count - 1, step, total)


def decay_tables(decay_rows):
    cum_log = jnp.cumsum(decay_rows, axis=1)
    block_log = cum_log[:, -1]
    length = decay_rows.shape[1]
    causal = jnp.arange(length)[:, None] >= jnp.arange(length)[None, :]
    spread = cum_log[:, :, None] - cum_log[:, None, :]
    decay_mat = jnp.where(causal[None], jnp.exp(jnp.minimum(spread, 0.0)), 0.0)
    return (cum_log, block_log, decay_mat)


def forward_combine(earlier_part, later_part):
    log_early, states_early = earlier_part
    log_late, states_late = later_part
    return (log_early + log_late, jnp.exp(log_late)[:, None, None] * states_early + states_late)


def reverse_combine(earlier_part, later_part):
    log_high, grads_high = earlier_part
    log_low, grads_low = later_part
    return (log_low + log_high, grads_low + jnp.exp(log_low)[:, None, None] * grads_high)


def head_major(rows, head_local, head_size):
    return rows.reshape(rows.shape[0], head_local, head_size).transpose(1, 0, 2)


def token_major(heads):
    return heads.astype(jnp.bfloat16).transpose(1, 0, 2).reshape(heads.shape[1], -1)


def on_device(
    query_rows, key_rows, value_rows, log_decay, out_grad, norm_gain, state_in, state_out_grad
):
    head_local = log_decay.shape[0]
    head_size = state_in.shape[1]
    feature_count = query_rows.shape[1] * lax.axis_size("head")
    query_heads = head_major(query_rows, head_local, head_size)
    key_heads = head_major(key_rows, head_local, head_size)
    value_heads = head_major(value_rows, head_local, head_size)
    upstream = head_major(out_grad, head_local, head_size)
    cum_log, block_log, decay_mat = decay_tables(log_decay)
    growth = jnp.exp(cum_log)[:, :, None]
    shrink = jnp.exp(block_log[:, None] - cum_log)[:, :, None]
    seq_index = lax.axis_index("seq")
    is_last = seq_index == lax.axis_size("seq") - 1
    key_decayed = (key_heads * shrink).astype(jnp.bfloat16)
    summary = jnp.einsum(
        "hsd,hse->hde", key_decayed, value_heads, preferred_element_type=jnp.float32
    )
    prefix_log, prefix_states = prefix(
        (block_log, summary),
        "seq",
        forward_combine,
        (jnp.zeros_like(block_log), jnp.zeros_like(summary)),
        False,
    )
    states_prev = prefix_states + jnp.exp(prefix_log)[:, None, None] * state_in
    states_bf = states_prev.astype(jnp.bfloat16)
    raw_scores = jnp.einsum(
        "htd,hsd->hts", query_heads, key_heads, preferred_element_type=jnp.float32
    )
    weights = (raw_scores * decay_mat).astype(jnp.bfloat16)
    attended = jnp.einsum("hts,hsd->htd", weights, value_heads, preferred_element_type=jnp.float32)
    attended = attended + growth * jnp.einsum(
        "htd,hde->hte", query_heads, states_bf, preferred_element_type=jnp.float32
    )
    gain_heads = norm_gain.reshape(head_local, 1, head_size)
    gained = gain_heads * upstream
    local_square = jnp.sum(attended * attended, axis=(0, 2))
    local_inner = jnp.sum(gained * attended, axis=(0, 2))
    total_square, total_inner = lax.psum((local_square, local_inner), "head")
    inv_rms = lax.rsqrt(total_square / feature_count + EPSILON)
    coefficient = total_inner * inv_rms**3 / feature_count
    attn_grad = (gained * inv_rms[None, :, None] - attended * coefficient[None, :, None]).astype(
        jnp.bfloat16
    )
    query_decayed = (query_heads * growth).astype(jnp.bfloat16)
    grad_summary = jnp.einsum(
        "htd,hte->hde", query_decayed, attn_grad, preferred_element_type=jnp.float32
    )
    suffix_log, suffix_states = prefix(
        (block_log, grad_summary),
        "seq",
        reverse_combine,
        (jnp.zeros_like(block_log), jnp.zeros_like(grad_summary)),
        True,
    )
    grads_next = suffix_states + jnp.exp(suffix_log)[:, None, None] * state_out_grad
    grads_bf = grads_next.astype(jnp.bfloat16)
    score_grad = (
        jnp.einsum("hte,hse->hts", attn_grad, value_heads, preferred_element_type=jnp.float32)
        * decay_mat
    ).astype(jnp.bfloat16)
    query_grad = jnp.einsum(
        "hts,hsd->htd", score_grad, key_heads, preferred_element_type=jnp.float32
    )
    query_grad = query_grad + growth * jnp.einsum(
        "hte,hde->htd", attn_grad, states_bf, preferred_element_type=jnp.float32
    )
    key_grad = jnp.einsum(
        "hts,htd->hsd", score_grad, query_heads, preferred_element_type=jnp.float32
    )
    key_grad = key_grad + shrink * jnp.einsum(
        "hde,hse->hsd", grads_bf, value_heads, preferred_element_type=jnp.float32
    )
    value_grad = jnp.einsum("hts,hte->hse", weights, attn_grad, preferred_element_type=jnp.float32)
    value_grad = value_grad + shrink * jnp.einsum(
        "hde,hsd->hse", grads_bf, key_heads, preferred_element_type=jnp.float32
    )
    own_term = jnp.exp(prefix_log)[:, None, None] * grad_summary
    own_term = own_term + jnp.where(
        is_last, jnp.exp(prefix_log + block_log)[:, None, None] * state_out_grad, 0.0
    )
    state_in_grad = lax.psum(own_term, "seq")
    return (token_major(query_grad), token_major(key_grad), token_major(value_grad), state_in_grad)


def solution(mesh):
    return jax.shard_map(
        on_device,
        mesh=mesh,
        in_specs=(
            P("seq", "head"),
            P("seq", "head"),
            P("seq", "head"),
            P("head", "seq"),
            P("seq", "head"),
            P("head"),
            P("head", None, None),
            P("head", None, None),
        ),
        out_specs=(P("seq", "head"), P("seq", "head"), P("seq", "head"), P("head", None, None)),
        check_vma=False,
    )
```

profile of v0, /device:TPU:0, one launch (start us, length us, event | category | flops | bytes accessed | tf_op | source)
XLA Modules:
  0.0 274.6 jit_solution(1497770968794582795)
XLA Ops:
  7.2 1.3 reduce-window.6
  9.1 2.9 %fusion.16 = f32[8,128,128]{2,1,0:T(8,128)} fusion(f32[8,256]{1,0:T(8,128)S(1)} %get-tuple-element.323, bf16[256,1024]{1,0:T(8,128)(2,1)} %param.14, bf16[256,1024]{1,0:T(8,128)(2,1)} %param.13), kind=kOutput, calls=%fused_computation.41 | convolution fusion | flops 67895296 | bytes 1581056 | tf_op jit(solution)/shard_map/hsd,hse->hde/dot_general | solution.py:72
  12.1 0.6 dynamic-slice
  13.4 0.2 dynamic-update-slice
  13.6 23.4 %all-reduce = f32[64]{0:T(128)S(1)} all-reduce(f32[64]{0:T(128)S(1)} %dynamic-update-slice), channel_id=2, replica_groups=mesh['seq'=8,'head'=4] {'seq'}, use_global_device_ids=true, to_apply=%add | all-reduce | flops 64 | bytes 512
  37.1 0.2 copy.97
  37.3 0.9 copy.104
  38.5 0.8 multiply_convert_fusion.1
  39.3 1.0 copy-done.1
  40.2 0.5 fusion.19
  40.7 47.7 %all-gather.6.cloned.1.call-done = f32[64,128,128]{2,1,0:T(8,128)} async-done(((f32[8,128,128]{2,1,0:T(8,128)}), f32[64,128,128]{2,1,0:T(8,128)}) %all-gather.6.cloned.1.call-update) | async-done | bytes 4194320 | tf_op jit(solution)/shard_map/all_gather | solution.py:11
  88.5 8.5 %while.32 = (s32[]{:T(128)}, f32[8]{0:T(128)S(1)}, f32[8,128,128]{2,1,0:T(8,128)S(1)}, s32[]{:T(128)}, f32[8,8]{1,0:T(8,128)S(1)}, /*index=5*/f32[8,8,128,128]{3,2,1,0:T(8,128)}, s32[]{:T(128)}, s32[]{:T(128)}) while((s32[]{:T(128)}, f32[8]{0:T(128)S(1)}, f32[8,128,128]{2,1,0:T(8,128)S(1)}, s32[]{:T(128)}, f32[8,8]{1,0:T(8,128)S(1)}, ...), condition=%wide.region_3.4_spmd.clone, body=%wide.region_2.3_spmd.clone.sunk | while | flops 524316 | bytes 1573139 | solution.py:23
  88.5 1.2 fusion.55
  89.7 1.2 fusion.55
  90.9 1.2 fusion.55
  92.1 1.2 fusion.55
  93.3 1.2 fusion.55
  94.6 1.2 fusion.55
  95.8 1.2 fusion.55
  97.0 1.2 add_convert_fusion.1
  98.2 1.5 multiply_reduce_fusion
  99.6 5.6 %all-reduce.1 = (f32[256]{0:T(256)S(1)}, f32[256]{0:T(256)S(1)}) all-reduce(f32[256]{0:T(256)S(1)} %get-tuple-element.287, f32[256]{0:T(256)S(1)} %get-tuple-element.286), channel_id=1, replica_groups=mesh['seq'=8,'head'=4] {'head'}, use_global_device_ids=true, to_apply=%region_7.8 | all-reduce | flops 512 | bytes 4096 | tf_op jit(solution)/shard_map/psum | solution.py:96
  105.3 1.5 fusion.14
  106.8 1.1 fusion.17
  108.2 0.8 multiply_convert_fusion
  108.9 1.0 copy-done.4
  109.9 0.5 convolution_bitcast_fusion.5
  110.4 0.3 fusion.12
  110.7 1.0 copy.84
  111.7 1.4 convolution_bitcast_fusion.3
  113.1 0.3 convolution_bitcast_fusion.4
  113.4 66.6 %all-gather.8.cloned.1.call-done = f32[64,128,128]{2,1,0:T(8,128)} async-done(((f32[8,128,128]{2,1,0:T(8,128)}), f32[64,128,128]{2,1,0:T(8,128)}) %all-gather.8.cloned.1.call-update) | async-done | bytes 4194320 | tf_op jit(solution)/shard_map/all_gather | solution.py:11
  180.0 4.7 %rev.7 = f32[8,8,128,128]{3,2,1,0:T(8,128)} reverse(f32[8,8,128,128]{3,2,1,0:T(8,128)} %bitcast.156), dimensions={0} | reverse | bytes 8388608 | tf_op jit(solution)/shard_map/rev | solution.py:13
  184.7 8.6 %while.33 = (s32[]{:T(128)}, f32[8]{0:T(128)S(1)}, f32[8,128,128]{2,1,0:T(8,128)S(1)}, s32[]{:T(128)}, f32[8,8]{1,0:T(8,128)S(1)}, /*index=5*/f32[8,8,128,128]{3,2,1,0:T(8,128)}, s32[]{:T(128)}, s32[]{:T(128)}) while((s32[]{:T(128)}, f32[8]{0:T(128)S(1)}, f32[8,128,128]{2,1,0:T(8,128)S(1)}, s32[]{:T(128)}, f32[8,8]{1,0:T(8,128)S(1)}, ...), condition=%wide.region_9.10_spmd.clone, body=%wide.region_8.9_spmd.clone.sunk | while | flops 524316 | bytes 1573139 | solution.py:23
  184.7 1.2 fusion.56
  186.0 1.2 fusion.56
  187.2 1.2 fusion.56
  188.4 1.2 fusion.56
  189.6 1.2 fusion.56
  190.9 1.2 fusion.56
  192.1 1.2 fusion.56
  193.3 2.1 select_add_fusion
  195.5 1.4 fusion.11
  196.9 1.0 copy.86
  197.9 0.3 fusion.10
  198.2 1.0 copy.85
  199.2 67.0 %all-reduce.4.cloned.1.call-done = f32[8,128,128]{2,1,0:T(8,128)} async-done(((f32[8,128,128]{2,1,0:T(8,128)}), f32[8,128,128]{2,1,0:T(8,128)}) %all-reduce.4.cloned.1.call-update) | async-done | bytes 524304 | tf_op jit(solution)/shard_map/psum | solution.py:139
  266.2 1.9 copy.154
  (69 shorter events, 1.5 us)
Async XLA Ops:
  7.2 5.0 %copy-start.15 = (u32[32]{0:T(128)S(1)}, u32[32]{0:T(128)}, u32[]{:S(2)}) copy-start(u32[32]{0:T(128)} %constant.70) | copy-start | bytes 388
  7.2 30.2 %copy-start.9 = (bf16[256,1024]{1,0:T(8,128)(2,1)S(1)}, bf16[256,1024]{1,0:T(8,128)(2,1)}, u32[]{:S(2)}) copy-start(bf16[256,1024]{1,0:T(8,128)(2,1)} %param.14) | copy-start | bytes 1572868
  7.2 29.9 %copy-start.13 = (bf16[256,1024]{1,0:T(8,128)(2,1)S(1)}, bf16[256,1024]{1,0:T(8,128)(2,1)}, u32[]{:S(2)}) copy-start(bf16[256,1024]{1,0:T(8,128)(2,1)} %param.12) | copy-start | bytes 1572868
  7.2 81.3 %all-gather.6.cloned.1.call-start = ((), (), s32[]{:S(2)}) async-start(), calls=%async_computation.1 | async-start | bytes 4718592 | tf_op jit(solution)/shard_map/all_gather | solution.py:11
  9.1 29.1 %copy-start.12 = (bf16[256,1024]{1,0:T(8,128)(2,1)S(1)}, bf16[256,1024]{1,0:T(8,128)(2,1)}, u32[]{:S(2)}) copy-start(bf16[256,1024]{1,0:T(8,128)(2,1)} %param.16) | copy-start | bytes 1572868
  12.0 26.5 %copy-start.7 = (bf16[256,1024]{1,0:T(8,128)(2,1)S(1)}, bf16[256,1024]{1,0:T(8,128)(2,1)}, u32[]{:S(2)}) copy-start(bf16[256,1024]{1,0:T(8,128)(2,1)} %param.13) | copy-start | bytes 1572868
  12.0 168.0 %all-gather.8.cloned.1.call-start = ((), (), s32[]{:S(2)}) async-start(), calls=%async_computation.2 | async-start | bytes 4718592 | tf_op jit(solution)/shard_map/all_gather | solution.py:11
  38.5 1.7 copy-start.6
  39.3 1.0 copy-start.1
  88.5 9.7 %copy-start.14 = (f32[1024]{0:T(1024)S(1)}, f32[1024]{0:T(1024)}, u32[]{:S(2)}) copy-start(f32[1024]{0:T(1024)} %param.17) | copy-start | bytes 12292
  105.3 2.8 %copy-start.8 = (bf16[256,1024]{1,0:T(8,128)(2,1)S(1)}, bf16[256,1024]{1,0:T(8,128)(2,1)}, u32[]{:S(2)}) copy-start(bf16[256,1024]{1,0:T(8,128)(2,1)} %param.13) | copy-start | bytes 1572868
  106.8 1.3 copy-start.10
  108.0 158.2 %all-reduce.4.cloned.1.call-start = ((), (), s32[]{:S(2)}) async-start(), calls=%async_computation | async-start | bytes 1048576 | tf_op jit(solution)/shard_map/psum | solution.py:139
  108.9 1.0 copy-start.4
  110.4 1.3 copy-start.2
  111.7 1.4 copy-start.5
  184.7 8.6 %copy-start = (f32[8,128,128]{2,1,0:T(8,128)S(1)}, f32[8,128,128]{2,1,0:T(8,128)}, u32[]{:S(2)}) copy-start(f32[8,128,128]{2,1,0:T(8,128)} %fusion.17) | copy-start | bytes 1572868
  193.3 2.2 copy-start.3
  195.4 2.5 copy-start.11
Sparse Core Ops, SparseCore 0:
  12.2 76.2 all-gather.5
  108.1 71.9 all-gather.7
  195.6 70.5 all-reduce.3
where the time goes:
time: 276 us; the launch traced here: 275 us
  waiting for transfers between devices  181 us (66%)
  blocking collectives  29.1 us (11%)
  other arithmetic  23.1 us (8%)
  between operations  14.7 us (5%)
  local copies, waits for them, and re-layouts  14.2 us (5%)
  matrix products  11.6 us (4%)
    all_gather x2, waiting for transfers between devices, prefix(): pieces = jax.tree.map(lambda part: lax.all_gather(part, axis), value)  114 us
    psum x1, waiting for transfers between devices, on_device(): state_in_grad = lax.psum(own_term, 'seq')  67 us
    unnamed x1, blocking collectives  23.4 us
    select_n x14, other arithmetic, step(): jnp.where(position < mine, new, old)  16.5 us
    unnamed x41, local copies, waits for them, and re-layouts  8.7 us
    psum x1, blocking collectives, on_device(): total_square, total_inner = lax.psum((local_square, local_inner), 'head')  5.63 us
  transfers between devices with their start and end apart: 3, of which 3 were waited for; matrix products, arithmetic and copies ran while one was open for 4% of the time, Pallas kernels for 0%

commit v1 on v0

v1 whole, which is shorter than its diff:
```python
import functools

import jax
import jax.numpy as jnp
from jax import lax
from jax.experimental import pallas as pl
from jax.experimental.pallas import tpu as pltpu
from jax.sharding import PartitionSpec as P

EPSILON = 1e-06
F32 = jnp.float32
BF16 = jnp.bfloat16
LOG_ROWS = 8
MASKED = -1e30

CONTRACT_ROWS = (((0,), (0,)), ((), ()))
CONTRACT_COLS = (((1,), (1,)), ((), ()))
VMEM = pl.BlockSpec(memory_space=pltpu.VMEM)


def call(body, outs, operands, scratch=(), flops=0):
    size = sum(x.size * x.dtype.itemsize for x in (*operands, *outs))
    return pl.pallas_call(
        body,
        out_shape=outs,
        in_specs=[VMEM] * len(operands),
        out_specs=[VMEM] * len(outs),
        scratch_shapes=list(scratch),
        compiler_params=pltpu.CompilerParams(vmem_limit_bytes=40 * 1024 * 1024),
        cost_estimate=pl.CostEstimate(flops=flops, bytes_accessed=size, transcendentals=0),
    )(*operands)


def shaped(shape, dtype=F32):
    return jax.ShapeDtypeStruct(shape, dtype)


def dot(a, b, dims=(((1,), (0,)), ((), ()))):
    return lax.dot_general(a, b, dims, preferred_element_type=F32)


def exact_dot(a, b, dims=(((1,), (0,)), ((), ()))):
    return lax.dot_general(
        a, b, dims, precision=lax.Precision.HIGHEST, preferred_element_type=F32
    )


def lanes(h, size):
    return slice(h * size, (h + 1) * size)


def share_rows(rows, count):
    share = 8
    while share * count < rows:
        share *= 2
    return share


def causal_mask(length):
    row = lax.broadcasted_iota(jnp.int32, (length, length), 0)
    col = lax.broadcasted_iota(jnp.int32, (length, length), 1)
    return row >= col


def summary_body(heads, size, share, key_ref, value_ref, decay_ref, send_ref, cum_ref, cum_col_ref):
    length = key_ref.shape[0]
    decay = decay_ref[...]
    causal = jnp.where(causal_mask(length), 1.0, 0.0)
    cum_col = exact_dot(causal, decay, CONTRACT_COLS)
    cum_ref[...] = exact_dot(decay, causal, CONTRACT_COLS)
    cum_col_ref[...] = cum_col
    block_log = cum_col[length - 1 : length, :]
    shrink = jnp.exp(block_log - cum_col)
    per_head = size // share
    for h in range(heads):
        key_decayed = (key_ref[:, lanes(h, size)].astype(F32) * shrink[:, h : h + 1]).astype(BF16)
        summary = dot(key_decayed, value_ref[:, lanes(h, size)], CONTRACT_ROWS)
        log_rows = jnp.broadcast_to(block_log[:, h : h + 1], (LOG_ROWS, size))
        for part in range(per_head):
            send_ref[h * per_head + part, :share] = summary[part * share : (part + 1) * share]
            send_ref[h * per_head + part, share:] = log_rows
    for spare in range(heads * per_head, send_ref.shape[0]):
        send_ref[spare] = jnp.zeros(send_ref.shape[1:], F32)


def own_rows(ref, share):
    start = lax.axis_index("seq") * share
    start = jnp.where(start < ref.shape[0], start, 0)
    return ref[pl.ds(pl.multiple_of(start, share), share), :]


def forward_scan_body(share, parts_ref, state_ref, states_ref, logs_ref):
    state = own_rows(state_ref, share)
    for b in range(parts_ref.shape[0]):
        states_ref[b] = state
        logs = parts_ref[b, share:]
        logs_ref[b] = logs
        state = jnp.exp(logs[:1]) * state + parts_ref[b, :share]


def reverse_scan_body(share, parts_ref, logs_ref, state_ref, grads_ref, total_ref):
    grad = own_rows(state_ref, share)
    for b in reversed(range(parts_ref.shape[0])):
        grads_ref[b] = grad
        grad = jnp.exp(logs_ref[b][:1]) * grad + parts_ref[b]
    total_ref[...] = grad


def decay_matrix(cum_ref, cum_col, causal, h):
    spread = cum_col[:, h : h + 1] - cum_ref[h : h + 1, :]
    return jnp.exp(jnp.where(causal, jnp.minimum(spread, 0.0), MASKED))


def intra_body(heads, size, query_ref, key_ref, value_ref, cum_ref, cum_col_ref, weight_ref, intra_ref):
    causal = causal_mask(query_ref.shape[0])
    cum_col = cum_col_ref[...]
    for h in range(heads):
        cut = lanes(h, size)
        scores = dot(query_ref[:, cut], key_ref[:, cut], CONTRACT_COLS)
        weights = (scores * decay_matrix(cum_ref, cum_col, causal, h)).astype(BF16)
        weight_ref[h] = weights
        intra_ref[:, cut] = dot(weights, value_ref[:, cut])


def attended_body(
    heads, size, intra_ref, query_ref, states_ref, cum_col_ref, upstream_ref, gain_ref, attended_ref, sums_ref
):
    length = query_ref.shape[0]
    growth = jnp.exp(cum_col_ref[...])
    square = jnp.zeros((length, size), F32)
    inner = jnp.zeros((length, size), F32)
    for h in range(heads):
        cut = lanes(h, size)
        carried = dot(query_ref[:, cut], states_ref[h].astype(BF16))
        attended = intra_ref[:, cut] + growth[:, h : h + 1] * carried
        attended_ref[:, cut] = attended
        square += attended * attended
        inner += gain_ref[:, cut] * upstream_ref[:, cut].astype(F32) * attended
    ones = jnp.ones((1, size), F32)
    sums_ref[...] = jnp.concatenate(
        [exact_dot(ones, square, CONTRACT_COLS), exact_dot(ones, inner, CONTRACT_COLS)]
        + [jnp.zeros((6, length), F32)],
        axis=0,
    )


def attn_grad_body(
    heads,
    size,
    share,
    feature_count,
    attended_ref,
    sums_ref,
    query_ref,
    cum_col_ref,
    upstream_ref,
    gain_ref,
    attn_grad_ref,
    send_ref,
):
    sums = jnp.sum(sums_ref[...], axis=0)
    inv_row = lax.rsqrt(sums[:1] / feature_count + EPSILON)
    coefficient_row = sums[1:2] * inv_row * inv_row * inv_row / feature_count
    columns = jnp.transpose(
        jnp.concatenate([inv_row, coefficient_row, jnp.zeros_like(sums[2:])], axis=0)
    )
    inv_rms, coefficient = columns[:, :1], columns[:, 1:2]
    growth = jnp.exp(cum_col_ref[...])
    per_head = size // share
    for h in range(heads):
        cut = lanes(h, size)
        gained = gain_ref[:, cut] * upstream_ref[:, cut].astype(F32)
        attn_grad = (gained * inv_rms - attended_ref[:, cut] * coefficient).astype(BF16)
        attn_grad_ref[:, cut] = attn_grad
        query_decayed = (query_ref[:, cut].astype(F32) * growth[:, h : h + 1]).astype(BF16)
        summary = dot(query_decayed, attn_grad, CONTRACT_ROWS)
        for part in range(per_head):
            send_ref[h * per_head + part] = summary[part * share : (part + 1) * share]
    for spare in range(heads * per_head, send_ref.shape[0]):
        send_ref[spare] = jnp.zeros(send_ref.shape[1:], F32)


def score_grad_body(
    heads,
    size,
    attn_grad_ref,
    query_ref,
    key_ref,
    value_ref,
    states_ref,
    weight_ref,
    cum_ref,
    cum_col_ref,
    query_grad_ref,
    key_part_ref,
    value_part_ref,
):
    causal = causal_mask(query_ref.shape[0])
    cum_col = cum_col_ref[...]
    growth = jnp.exp(cum_col)
    for h in range(heads):
        cut = lanes(h, size)
        attn_grad = attn_grad_ref[:, cut]
        scores = dot(attn_grad, value_ref[:, cut], CONTRACT_COLS)
        score_grad = (scores * decay_matrix(cum_ref, cum_col, causal, h)).astype(BF16)
        carried = dot(attn_grad, states_ref[h].astype(BF16), CONTRACT_COLS)
        query_grad = dot(score_grad, key_ref[:, cut]) + growth[:, h : h + 1] * carried
        query_grad_ref[:, cut] = query_grad.astype(BF16)
        key_part_ref[:, cut] = dot(score_grad, query_ref[:, cut], CONTRACT_ROWS)
        value_part_ref[:, cut] = dot(weight_ref[h], attn_grad, CONTRACT_ROWS)


def finish_body(
    heads, size, key_part_ref, value_part_ref, key_ref, value_ref, grads_ref, cum_col_ref, key_grad_ref, value_grad_ref
):
    length = key_ref.shape[0]
    cum_col = cum_col_ref[...]
    shrink = jnp.exp(cum_col[length - 1 : length, :] - cum_col)
    for h in range(heads):
        cut = lanes(h, size)
        grads = grads_ref[h].astype(BF16)
        column = shrink[:, h : h + 1]
        key_state = dot(value_ref[:, cut], grads, CONTRACT_COLS)
        key_grad_ref[:, cut] = (key_part_ref[:, cut] + column * key_state).astype(BF16)
        value_state = dot(key_ref[:, cut], grads)
        value_grad_ref[:, cut] = (value_part_ref[:, cut] + column * value_state).astype(BF16)


def swap(parts):
    return lax.all_to_all(parts, "seq", 0, 0)


def on_device(
    query_rows, key_rows, value_rows, log_decay, out_grad, norm_gain, state_in, state_out_grad
):
    heads, length = log_decay.shape
    size = state_in.shape[1]
    width = heads * size
    blocks = lax.axis_size("seq")
    share = share_rows(width, blocks)
    feature_count = width * lax.axis_size("head")
    gain = norm_gain.reshape(1, width)

    send, cum_log, cum_col = call(
        functools.partial(summary_body, heads, size, share),
        [
            shaped((blocks, share + LOG_ROWS, size)),
            shaped((heads, length)),
            shaped((length, heads)),
        ],
        [key_rows, value_rows, log_decay],
    )
    parts = swap(send)
    weights, intra = call(
        functools.partial(intra_body, heads, size),
        [shaped((heads, length, length), BF16), shaped((length, width))],
        [query_rows, key_rows, value_rows, cum_log, cum_col],
        flops=4 * heads * length * length * size,
    )
    states, logs = call(
        functools.partial(forward_scan_body, share),
        [shaped((blocks, share, size)), shaped((blocks, LOG_ROWS, size))],
        [parts, state_in.reshape(width, size)],
    )
    states = swap(states).reshape(-1, size)[:width].reshape(heads, size, size)
    attended, sums = call(
        functools.partial(attended_body, heads, size),
        [shaped((length, width)), shaped((8, length))],
        [intra, query_rows, states, cum_col, out_grad, gain],
    )
    all_sums = lax.psum(sums, "head")[None]
    attn_grad, send = call(
        functools.partial(attn_grad_body, heads, size, share, feature_count),
        [shaped((length, width), BF16), shaped((blocks, share, size))],
        [attended, all_sums, query_rows, cum_col, out_grad, gain],
    )
    parts = swap(send)
    query_grad, key_part, value_part = call(
        functools.partial(score_grad_body, heads, size),
        [shaped((length, width), BF16), shaped((length, width)), shaped((length, width))],
        [attn_grad, query_rows, key_rows, value_rows, states, weights, cum_log, cum_col],
        flops=10 * heads * length * length * size,
    )
    grads, total = call(
        functools.partial(reverse_scan_body, share),
        [shaped((blocks, share, size)), shaped((share, size))],
        [parts, logs, state_out_grad.reshape(width, size)],
    )
    grads = swap(grads).reshape(-1, size)[:width].reshape(heads, size, size)
    state_in_grad = lax.all_gather(total, "seq").reshape(-1, size)[:width]
    key_grad, value_grad = call(
        functools.partial(finish_body, heads, size),
        [shaped((length, width), BF16), shaped((length, width), BF16)],
        [key_part, value_part, key_rows, value_rows, grads, cum_col],
    )
    return (query_grad, key_grad, value_grad, state_in_grad.reshape(heads, size, size))


def solution(mesh):
    return jax.shard_map(
        on_device,
        mesh=mesh,
        in_specs=(
            P("seq", "head"),
            P("seq", "head"),
            P("seq", "head"),
            P("head", "seq"),
            P("seq", "head"),
            P("head"),
            P("head", None, None),
            P("head", None, None),
        ),
        out_specs=(P("seq", "head"), P("seq", "head"), P("seq", "head"), P("head", None, None)),
        check_vma=False,
    )
```

time: 276 us -> 124 us (0.45)
  waiting for transfers between devices: 181 us -> 10.8 us
  blocking collectives: 29.1 us -> 78.8 us
  other arithmetic: 23.1 us -> 0 us
  between operations: 14.7 us -> 0.76 us
  matrix products: 11.6 us -> 0 us
  Pallas kernels: 0 us -> 10.9 us
  starting transfers between devices: 0.12 us -> 7.26 us
    all_gather x2 -> x0, waiting for transfers between devices: 114 us -> none  [prefix(): pieces = jax.tree.map(lambda part: lax.all_gather(part, axis), value)]
    psum x1 -> x0, waiting for transfers between devices: 67 us -> none  [on_device(): state_in_grad = lax.psum(own_term, 'seq')]
    all_to_all x0 -> x2, blocking collectives: none -> 41.2 us  [swap(): return lax.all_to_all(parts, 'seq', 0, 0)]
    all_gather x0 -> x1, blocking collectives: none -> 31.9 us  [on_device(): state_in_grad = lax.all_gather(total, 'seq').reshape(-1, size)[:width]]
    unnamed x1 -> x0, blocking collectives: 23.4 us -> none
    select_n x14 -> x0, other arithmetic: 16.5 us -> none  [step(): jnp.where(position < mine, new, old)]
    dot_general x12 -> x0, matrix products: 11.6 us -> none  [the longest x1 2.88 us: on_device(): jnp.einsum('hsd,hse->hde', key_decayed, value_heads, preferred_element_ty...]
    pallas_call x0 -> x8, Pallas kernels: none -> 10.9 us  [call(): pl.pallas_call(body, out_shape=outs, in_specs=[VMEM] * len(operands), out...]
  transfers between devices with their start and end apart: 3 -> 2, of which waited for: 3 -> 1; matrix products, arithmetic and copies ran while one was open for 4% -> 0% of each run, Pallas kernels for 0% -> 4%
where the time goes in v1:
time: 124 us; the launch traced here: 123 us
  blocking collectives  78.8 us (64%)
  local copies, waits for them, and re-layouts  14.6 us (12%)
  Pallas kernels  10.9 us (9%)
  waiting for transfers between devices  10.8 us (9%)
  starting transfers between devices  7.26 us (6%)
    all_to_all x2, blocking collectives, swap(): return lax.all_to_all(parts, 'seq', 0, 0)  41.2 us
    all_gather x1, blocking collectives, on_device(): state_in_grad = lax.all_gather(total, 'seq').reshape(-1, size)[:width]  31.9 us
    unnamed x41, local copies, waits for them, and re-layouts  14.6 us
    pallas_call x8, Pallas kernels, call(): pl.pallas_call(body, out_shape=outs, in_specs=[VMEM] * len(operands), out...  10.9 us
    all_to_all x2, waiting for transfers between devices, swap(): return lax.all_to_all(parts, 'seq', 0, 0)  10.8 us
    all_to_all x2, starting transfers between devices, swap(): return lax.all_to_all(parts, 'seq', 0, 0)  7.26 us
    psum x1, blocking collectives, on_device(): all_sums = lax.psum(sums, 'head')[None]  5.73 us
  transfers between devices with their start and end apart: 2, of which 1 were waited for; matrix products, arithmetic and copies ran while one was open for 0% of the time, Pallas kernels for 4%

profile of v1, /device:TPU:0, one launch (start us, length us, event | category | flops | bytes accessed | tf_op | source)
XLA Modules:
  0.0 123.1 jit_solution(15715479682903571387)
XLA Ops:
  0.6 0.0 copy-start.1
  0.6 1.0 copy-done.1
  1.7 1.0 copy-done.3
  2.7 0.0 copy-start.19
  2.7 0.7 copy-done.19
  3.4 1.2 shard_map.111
  4.6 0.0 copy-start.16
  4.6 23.2 %all_to_all.20.parts_ref = f32[8,136,128]{2,1,0:T(8,128)S(1)} all-to-all(f32[8,136,128]{2,1,0:T(8,128)S(1)} %get-tuple-element.25), channel_id=1, replica_groups=mesh['seq'=8,'head'=4] {'seq'}, dimensions={0} | all-to-all | bytes 1114112 | tf_op jit(solution)/shard_map/all_to_all | solution.py:230
  27.8 0.0 copy-done.16
  27.8 0.0 copy-start.4
  27.8 0.8 shard_map.113
  28.7 0.0 copy-start
  28.7 0.0 copy-start.2
  28.7 3.6 %all-to-all-start.1 = ((f32[8,128,128]{2,1,0:T(8,128)}), f32[8,128,128]{2,1,0:T(8,128)S(1)}, u32[]{:S(2)}, u32[]{:S(2)}) async-start(f32[8,128,128]{2,1,0:T(8,128)} %get-tuple-element.26), calls=%async_computation.1 | async-start | bytes 1048576 | tf_op jit(solution)/shard_map/all_to_all | solution.py:230
  32.3 0.0 copy-done.4
  32.3 0.0 copy-done
  32.3 0.0 copy-done.2
  32.3 0.0 copy-start.5
  32.3 0.0 copy-start.18
  32.3 0.9 shard_map.112
  33.3 0.0 copy-start.6
  33.3 0.9 copy-done.6
  34.2 1.0 copy-done.10
  35.2 10.8 %all-to-all-done.1.states_ref = f32[8,128,128]{2,1,0:T(8,128)S(1)} async-done(((f32[8,128,128]{2,1,0:T(8,128)}), f32[8,128,128]{2,1,0:T(8,128)S(1)}, u32[]{:S(2)}, u32[]{:S(2)}) %all-to-all-start.1) | async-done | bytes 524320 | tf_op jit(solution)/shard_map/all_to_all | solution.py:230
  46.0 0.0 copy-done.5
  46.1 0.0 copy-done.18
  46.1 1.2 copy-done.7
  47.3 0.8 shard_map.114
  48.1 1.0 copy-done.8
  49.0 5.7 %psum.7.sums_ref = f32[1,8,256]{2,1,0:T(8,128)S(1)} all-reduce(f32[1,8,256]{2,1,0:T(8,128)S(1)} %bitcast.9), channel_id=1, replica_groups=mesh['seq'=8,'head'=4] {'head'}, use_global_device_ids=true, to_apply=%region_0.0 | all-reduce | flops 2048 | bytes 16384 | tf_op jit(solution)/shard_map/psum | solution.py:271
  54.8 0.0 copy-start.9
  54.8 1.2 copy-done.9
  56.0 1.3 %shard_map.115 = (bf16[256,1024]{1,0:T(8,128)(2,1)S(1)}, f32[8,128,128]{2,1,0:T(8,128)S(1)}) custom-call(f32[256,1024]{1,0:T(8,128)S(1)} %copy-done.9, f32[1,8,256]{2,1,0:T(8,128)S(1)} %psum.7.sums_ref, bf16[256,1024]{1,0:T(8,128)(2,1)S(1)} %copy-done, f32[256,8]{1,0:T(8,128)S(1)} %get-tuple-element.23.cum_col_ref, bf16[256,1024]{1,0:T(8,128)(2,1)S(1)} %copy-done.5, ...), custom_call_target="tpu_custom_call" | custom-call | bytes 3166208 | tf_op jit(solution)/shard_map/pallas_call | solution.py:23
  57.3 0.0 copy-start.17
  57.4 18.0 %all_to_all.21.parts_ref = f32[8,128,128]{2,1,0:T(8,128)S(1)} all-to-all(f32[8,128,128]{2,1,0:T(8,128)S(1)} %get-tuple-element.34), channel_id=1, replica_groups=mesh['seq'=8,'head'=4] {'seq'}, dimensions={0} | all-to-all | bytes 1048576 | tf_op jit(solution)/shard_map/all_to_all | solution.py:230
  75.4 0.0 copy-done.17
  75.4 0.8 shard_map.117
  76.2 3.6 %all-to-all-start.3 = ((f32[8,128,128]{2,1,0:T(8,128)}), f32[8,128,128]{2,1,0:T(8,128)S(1)}, u32[]{:S(2)}, u32[]{:S(2)}) async-start(f32[8,128,128]{2,1,0:T(8,128)} %get-tuple-element.36), calls=%async_computation.3 | async-start | bytes 1048576 | tf_op jit(solution)/shard_map/all_to_all | solution.py:230
  79.9 1.2 copy-done.11
  81.1 3.5 %shard_map.116 = (bf16[256,1024]{1,0:T(8,128)(2,1)}, f32[256,1024]{1,0:T(8,128)S(1)}, f32[256,1024]{1,0:T(8,128)S(1)}) custom-call(bf16[256,1024]{1,0:T(8,128)(2,1)S(1)} %get-tuple-element.29.attn_grad_ref, bf16[256,1024]{1,0:T(8,128)(2,1)S(1)} %copy-done, bf16[256,1024]{1,0:T(8,128)(2,1)S(1)} %copy-done.2, bf16[256,1024]{1,0:T(8,128)(2,1)S(1)} %copy-done.4, ...), custom_call_target="tpu_custom_call" | custom-call | flops 671088640 | bytes 6307840 | tf_op jit(solution)/shard_map/pallas_call | solution.py:23
  84.5 1.0 copy-done.12
  85.5 1.0 copy-done.14
  86.5 31.9 %all-gather = f32[1024,128]{1,0:T(8,128)S(1)} all-gather(f32[128,128]{1,0:T(8,128)S(1)} %get-tuple-element.39), channel_id=2, replica_groups=mesh['seq'=8,'head'=4] {'seq'}, dimensions={0}, use_global_device_ids=true | all-gather | bytes 589824 | tf_op jit(solution)/shard_map/all_gather | solution.py:290
  118.3 0.0 all-to-all-done.3.grads_ref
  118.4 1.2 copy-done.13
  119.6 1.2 copy-done.15
  120.8 1.5 %shard_map.118 = (bf16[256,1024]{1,0:T(8,128)(2,1)}, bf16[256,1024]{1,0:T(8,128)(2,1)}) custom-call(f32[256,1024]{1,0:T(8,128)S(1)} %copy-done.13, f32[256,1024]{1,0:T(8,128)S(1)} %copy-done.15, bf16[256,1024]{1,0:T(8,128)(2,1)S(1)} %copy-done.2, bf16[256,1024]{1,0:T(8,128)(2,1)S(1)} %copy-done.4, f32[8,128,128]{2,1,0:T(8,128)S(1)} %all-to-all-done.3.grads_ref, ...), custom_call_target="tpu_custom_call" | custom-call | bytes 4726784 | tf_op jit(solution)/shard_map/pallas_call | solution.py:23
  122.3 0.8 copy.13
  (9 shorter events, 0.0 us)
Async XLA Ops:
  0.6 1.0 copy-start.1
  1.7 1.0 copy-start.3
  2.7 0.7 copy-start.19
  4.6 23.2 %copy-start.16 = (f32[8,128,128]{2,1,0:T(8,128)S(1)}, f32[8,128,128]{2,1,0:T(8,128)}, u32[]{:S(2)}) copy-start(f32[8,128,128]{2,1,0:T(8,128)} %param.14) | copy-start | bytes 1572868
  27.8 4.5 %copy-start.4 = (bf16[256,1024]{1,0:T(8,128)(2,1)S(1)}, bf16[256,1024]{1,0:T(8,128)(2,1)}, u32[]{:S(2)}) copy-start(bf16[256,1024]{1,0:T(8,128)(2,1)} %value_ref.7) | copy-start | bytes 1572868
  28.7 3.6 %copy-start = (bf16[256,1024]{1,0:T(8,128)(2,1)S(1)}, bf16[256,1024]{1,0:T(8,128)(2,1)}, u32[]{:S(2)}) copy-start(bf16[256,1024]{1,0:T(8,128)(2,1)} %query_ref.7) | copy-start | bytes 1572868
  28.7 3.7 %copy-start.2 = (bf16[256,1024]{1,0:T(8,128)(2,1)S(1)}, bf16[256,1024]{1,0:T(8,128)(2,1)}, u32[]{:S(2)}) copy-start(bf16[256,1024]{1,0:T(8,128)(2,1)} %key_ref.7) | copy-start | bytes 1572868
  28.7 17.4 %all-to-all-start.1 = ((f32[8,128,128]{2,1,0:T(8,128)}), f32[8,128,128]{2,1,0:T(8,128)S(1)}, u32[]{:S(2)}, u32[]{:S(2)}) async-start(f32[8,128,128]{2,1,0:T(8,128)} %get-tuple-element.26), calls=%async_computation.1 | async-start | bytes 1048576 | tf_op jit(solution)/shard_map/all_to_all | solution.py:230
  32.3 13.7 %copy-start.5 = (bf16[256,1024]{1,0:T(8,128)(2,1)S(1)}, bf16[256,1024]{1,0:T(8,128)(2,1)}, u32[]{:S(2)}) copy-start(bf16[256,1024]{1,0:T(8,128)(2,1)} %upstream_ref.3) | copy-start | bytes 1572868
  32.3 13.7 %copy-start.18 = (f32[1024]{0:T(1024)S(1)}, f32[1024]{0:T(1024)}, u32[]{:S(2)}) copy-start(f32[1024]{0:T(1024)} %param.13) | copy-start | bytes 12292
  33.3 1.0 copy-start.6
  34.2 1.0 copy-start.10
  46.1 1.2 copy-start.7
  48.1 1.0 copy-start.8
  54.8 1.2 copy-start.9
  57.3 18.0 %copy-start.17 = (f32[8,128,128]{2,1,0:T(8,128)S(1)}, f32[8,128,128]{2,1,0:T(8,128)}, u32[]{:S(2)}) copy-start(f32[8,128,128]{2,1,0:T(8,128)} %param.15) | copy-start | bytes 1572868
  76.2 42.1 %all-to-all-start.3 = ((f32[8,128,128]{2,1,0:T(8,128)}), f32[8,128,128]{2,1,0:T(8,128)S(1)}, u32[]{:S(2)}, u32[]{:S(2)}) async-start(f32[8,128,128]{2,1,0:T(8,128)} %get-tuple-element.36), calls=%async_computation.3 | async-start | bytes 1048576 | tf_op jit(solution)/shard_map/all_to_all | solution.py:230
  79.9 1.2 copy-start.11
  84.5 1.0 copy-start.12
  85.5 1.0 copy-start.14
  118.3 1.2 copy-start.13
  119.6 1.2 copy-start.15

commit v2 on v1

v2 whole, which is shorter than its diff:
```python
import functools

import jax
import jax.numpy as jnp
from jax import lax
from jax.experimental import pallas as pl
from jax.experimental.pallas import tpu as pltpu
from jax.sharding import PartitionSpec as P

EPSILON = 1e-06
F32 = jnp.float32
BF16 = jnp.bfloat16
LOG_ROWS = 8
MASKED = -1e30

CONTRACT_ROWS = (((0,), (0,)), ((), ()))
CONTRACT_COLS = (((1,), (1,)), ((), ()))
VMEM = pl.BlockSpec(memory_space=pltpu.VMEM)


def call(body, outs, operands, scratch=(), flops=0):
    size = sum(x.size * x.dtype.itemsize for x in (*operands, *outs))
    return pl.pallas_call(
        body,
        out_shape=outs,
        in_specs=[VMEM] * len(operands),
        out_specs=[VMEM] * len(outs),
        scratch_shapes=list(scratch),
        compiler_params=pltpu.CompilerParams(vmem_limit_bytes=24 * 1024 * 1024),
        cost_estimate=pl.CostEstimate(flops=flops, bytes_accessed=size, transcendentals=0),
    )(*operands)


def shaped(shape, dtype=F32):
    return jax.ShapeDtypeStruct(shape, dtype)


def dot(a, b, dims=(((1,), (0,)), ((), ()))):
    return lax.dot_general(a, b, dims, preferred_element_type=F32)


def exact_dot(a, b, dims=(((1,), (0,)), ((), ()))):
    return lax.dot_general(
        a, b, dims, precision=lax.Precision.HIGHEST, preferred_element_type=F32
    )


def lanes(h, size):
    return slice(h * size, (h + 1) * size)


def causal_mask(length):
    row = lax.broadcasted_iota(jnp.int32, (length, length), 0)
    col = lax.broadcasted_iota(jnp.int32, (length, length), 1)
    return row >= col


class Plan:
    def __init__(self, heads, size, blocks):
        self.heads, self.size, self.blocks = heads, size, blocks
        self.members = next(m for m in (4, 2, 1) if heads % m == 0 and blocks % m == 0)
        self.groups = blocks // self.members
        self.own = heads // self.members
        self.rows = self.own * size

    def member(self):
        return lax.rem(lax.axis_index("seq"), self.members)

    def group(self):
        return lax.div(lax.axis_index("seq"), self.members)

    def peer(self, k):
        return lax.bitwise_xor(self.member(), k)

    def rows_of(self, member):
        return pl.ds(pl.multiple_of(member * self.rows, self.rows), self.rows)

    def swap_in_group(self, pieces):
        span = self.members
        return [pieces[0]] + [
            lax.ppermute(
                pieces[k], "seq", [(i, i // span * span + (i % span ^ k)) for i in range(self.blocks)]
            )
            for k in range(1, span)
        ]

    def from_groups(self, piece, earlier_only):
        received = []
        for step in range(1, self.groups):
            pairs = [(i, i + step * self.members) for i in range(self.blocks)]
            if earlier_only:
                pairs = [(i, j) for i, j in pairs if j < self.blocks]
            else:
                pairs = [(i, j % self.blocks) for i, j in pairs]
            received.append(lax.ppermute(piece, "seq", pairs))
        return received


def own_decays(plan, log_tile_ref, base):
    first = base + plan.member() * plan.own
    rows = [log_tile_ref[pl.ds(first + j, 1), :] for j in range(plan.own)]
    return jnp.concatenate([jnp.broadcast_to(jnp.exp(row), (plan.size, plan.size)) for row in rows])


def summary_body(plan, key_ref, value_ref, decay_ref, *refs):
    send_refs, (cum_ref, cum_col_ref, held_ref) = refs[: plan.members], refs[plan.members :]
    length, heads, size = key_ref.shape[0], plan.heads, plan.size
    decay = decay_ref[...]
    causal = jnp.where(causal_mask(length), 1.0, 0.0)
    cum_col = exact_dot(causal, decay, CONTRACT_COLS)
    cum_row = exact_dot(decay, causal, CONTRACT_COLS)
    cum_ref[...] = cum_row
    cum_col_ref[...] = cum_col
    block_log = cum_col[length - 1 : length, :]
    shrink = jnp.exp(block_log - cum_col)
    for h in range(heads):
        key_decayed = (key_ref[:, lanes(h, size)].astype(F32) * shrink[:, h : h + 1]).astype(BF16)
        held_ref[h * size : (h + 1) * size] = dot(
            key_decayed, value_ref[:, lanes(h, size)], CONTRACT_ROWS
        )
    log_tile = jnp.broadcast_to(cum_row[:, length - 1 : length], (heads, size))
    if heads < LOG_ROWS:
        log_tile = jnp.concatenate([log_tile, jnp.zeros((LOG_ROWS - heads, size), F32)])
    for k, send_ref in enumerate(send_refs):
        send_ref[: plan.rows] = held_ref[plan.rows_of(plan.peer(k))]
        send_ref[plan.rows :] = log_tile


def group_total_body(plan, *refs):
    part_refs, (total_ref, logs_ref, held_ref) = refs[: plan.members], refs[plan.members :]
    for k, part_ref in enumerate(part_refs):
        held_ref[plan.peer(k)] = part_ref[...]
    total = jnp.zeros((plan.rows, plan.size), F32)
    log_total = jnp.zeros((LOG_ROWS, plan.size), F32)
    for b in range(plan.members):
        total = own_decays(plan, held_ref.at[b], plan.rows) * total + held_ref[b, : plan.rows]
        logs_ref[b] = held_ref[b, plan.rows :]
        log_total += held_ref[b, plan.rows :]
    total_ref[: plan.rows] = total
    total_ref[plan.rows :] = log_total


def stage_groups(plan, total_refs, held_ref):
    for step, total_ref in enumerate(total_refs):
        held_ref[lax.rem(plan.group() - step + plan.groups, plan.groups)] = total_ref[...]


def forward_scan_body(plan, *refs):
    part_refs, refs = refs[: plan.members], refs[plan.members :]
    total_refs, refs = refs[: plan.groups], refs[plan.groups :]
    state_ref, refs = refs[0], refs[1:]
    send_refs, (groups_ref, held_ref) = refs[: plan.members], refs[plan.members :]
    stage_groups(plan, total_refs, groups_ref)
    state = state_ref[plan.rows_of(plan.member())]
    for group in range(plan.groups - 1):
        after = own_decays(plan, groups_ref.at[group], plan.rows) * state + groups_ref[group, : plan.rows]
        state = jnp.where(group < plan.group(), after, state)
    for k, part_ref in enumerate(part_refs):
        held_ref[plan.peer(k)] = part_ref[...]
    for b in range(plan.members):
        summary = held_ref[b, : plan.rows]
        decays = own_decays(plan, held_ref.at[b], plan.rows)
        held_ref[b, : plan.rows] = state
        state = decays * state + summary
    for k, send_ref in enumerate(send_refs):
        send_ref[...] = held_ref[plan.peer(k), : plan.rows]


def group_grad_body(plan, *refs):
    part_refs, (logs_ref, total_ref, held_ref) = refs[: plan.members], refs[plan.members :]
    for k, part_ref in enumerate(part_refs):
        held_ref[plan.peer(k)] = part_ref[...]
    total = jnp.zeros((plan.rows, plan.size), F32)
    log_total = jnp.zeros((LOG_ROWS, plan.size), F32)
    for b in reversed(range(plan.members)):
        total = own_decays(plan, logs_ref.at[b], 0) * total + held_ref[b]
        log_total += logs_ref[b]
    total_ref[: plan.rows] = total
    total_ref[plan.rows :] = log_total


def reverse_scan_body(plan, *refs):
    part_refs, refs = refs[: plan.members], refs[plan.members :]
    total_refs, refs = refs[: plan.groups], refs[plan.groups :]
    (logs_ref, grad_ref), refs = refs[:2], refs[2:]
    send_refs, (all_ref, groups_ref, held_ref) = refs[: plan.members], refs[plan.members :]
    stage_groups(plan, total_refs, groups_ref)
    grad = grad_ref[plan.rows_of(plan.member())]
    leaving = grad
    for group in reversed(range(plan.groups)):
        leaving = jnp.where(group == plan.group(), grad, leaving)
        grad = own_decays(plan, groups_ref.at[group], plan.rows) * grad + groups_ref[group, : plan.rows]
    all_ref[...] = grad
    for k, part_ref in enumerate(part_refs):
        held_ref[plan.peer(k)] = part_ref[...]
    grad = leaving
    for b in reversed(range(plan.members)):
        summary = held_ref[b]
        held_ref[b] = grad
        grad = own_decays(plan, logs_ref.at[b], 0) * grad + summary
    for k, send_ref in enumerate(send_refs):
        send_ref[...] = held_ref[plan.peer(k)]


def decay_matrix(cum_ref, cum_col, causal, h):
    spread = cum_col[:, h : h + 1] - cum_ref[h : h + 1, :]
    return jnp.exp(jnp.where(causal, jnp.minimum(spread, 0.0), MASKED))


def intra_body(plan, query_ref, key_ref, value_ref, cum_ref, cum_col_ref, weight_ref, intra_ref):
    causal = causal_mask(query_ref.shape[0])
    cum_col = cum_col_ref[...]
    for h in range(plan.heads):
        cut = lanes(h, plan.size)
        scores = dot(query_ref[:, cut], key_ref[:, cut], CONTRACT_COLS)
        weights = (scores * decay_matrix(cum_ref, cum_col, causal, h)).astype(BF16)
        weight_ref[h] = weights
        intra_ref[:, cut] = dot(weights, value_ref[:, cut])


def gather_rounded(plan, piece_refs, whole_ref):
    for k, piece_ref in enumerate(piece_refs):
        whole_ref[plan.rows_of(plan.peer(k))] = piece_ref[...].astype(BF16)


def attended_body(plan, *refs):
    state_refs, refs = refs[: plan.members], refs[plan.members :]
    intra_ref, query_ref, cum_col_ref, upstream_ref, gain_ref = refs[:5]
    attended_ref, sums_ref, states_ref = refs[5:]
    size, length = plan.size, query_ref.shape[0]
    gather_rounded(plan, state_refs, states_ref)
    growth = jnp.exp(cum_col_ref[...])
    square = jnp.zeros((length, size), F32)
    inner = jnp.zeros((length, size), F32)
    for h in range(plan.heads):
        cut = lanes(h, size)
        carried = dot(query_ref[:, cut], states_ref[cut])
        attended = intra_ref[:, cut] + growth[:, h : h + 1] * carried
        attended_ref[:, cut] = attended
        square += attended * attended
        inner += gain_ref[:, cut] * upstream_ref[:, cut].astype(F32) * attended
    ones = jnp.ones((1, size), F32)
    sums_ref[...] = jnp.concatenate(
        [exact_dot(ones, square, CONTRACT_COLS), exact_dot(ones, inner, CONTRACT_COLS)]
        + [jnp.zeros((6, length), F32)],
        axis=0,
    )


def attn_grad_body(plan, parties, *refs):
    sums_refs, refs = refs[:parties], refs[parties:]
    attended_ref, query_ref, cum_col_ref, upstream_ref, gain_ref = refs[:5]
    attn_grad_ref, refs = refs[5], refs[6:]
    send_refs, (held_ref,) = refs[: plan.members], refs[plan.members :]
    size = plan.size
    feature_count = plan.heads * size * parties
    sums = sum(ref[...] for ref in sums_refs)
    inv_row = lax.rsqrt(sums[:1] / feature_count + EPSILON)
    coefficient_row = sums[1:2] * inv_row * inv_row * inv_row / feature_count
    columns = jnp.transpose(
        jnp.concatenate([inv_row, coefficient_row, jnp.zeros_like(sums[2:])], axis=0)
    )
    inv_rms, coefficient = columns[:, :1], columns[:, 1:2]
    growth = jnp.exp(cum_col_ref[...])
    for h in range(plan.heads):
        cut = lanes(h, size)
        gained = gain_ref[:, cut] * upstream_ref[:, cut].astype(F32)
        attn_grad = (gained * inv_rms - attended_ref[:, cut] * coefficient).astype(BF16)
        attn_grad_ref[:, cut] = attn_grad
        query_decayed = (query_ref[:, cut].astype(F32) * growth[:, h : h + 1]).astype(BF16)
        held_ref[cut] = dot(query_decayed, attn_grad, CONTRACT_ROWS)
    for k, send_ref in enumerate(send_refs):
        send_ref[...] = held_ref[plan.rows_of(plan.peer(k))]


def score_grad_body(
    plan,
    attn_grad_ref,
    query_ref,
    key_ref,
    value_ref,
    states_ref,
    weight_ref,
    cum_ref,
    cum_col_ref,
    query_grad_ref,
    key_part_ref,
    value_part_ref,
):
    causal = causal_mask(query_ref.shape[0])
    cum_col = cum_col_ref[...]
    growth = jnp.exp(cum_col)
    for h in range(plan.heads):
        cut = lanes(h, plan.size)
        attn_grad = attn_grad_ref[:, cut]
        scores = dot(attn_grad, value_ref[:, cut], CONTRACT_COLS)
        score_grad = (scores * decay_matrix(cum_ref, cum_col, causal, h)).astype(BF16)
        carried = dot(attn_grad, states_ref[cut], CONTRACT_COLS)
        query_grad = dot(score_grad, key_ref[:, cut]) + growth[:, h : h + 1] * carried
        query_grad_ref[:, cut] = query_grad.astype(BF16)
        key_part_ref[:, cut] = dot(score_grad, query_ref[:, cut], CONTRACT_ROWS)
        value_part_ref[:, cut] = dot(weight_ref[h], attn_grad, CONTRACT_ROWS)


def finish_body(plan, *refs):
    grad_refs, refs = refs[: plan.members], refs[plan.members :]
    key_part_ref, value_part_ref, key_ref, value_ref, cum_col_ref = refs[:5]
    key_grad_ref, value_grad_ref, grads_ref = refs[5:]
    length = key_ref.shape[0]
    gather_rounded(plan, grad_refs, grads_ref)
    cum_col = cum_col_ref[...]
    shrink = jnp.exp(cum_col[length - 1 : length, :] - cum_col)
    for h in range(plan.heads):
        cut = lanes(h, plan.size)
        grads = grads_ref[cut]
        column = shrink[:, h : h + 1]
        key_state = dot(value_ref[:, cut], grads, CONTRACT_COLS)
        key_grad_ref[:, cut] = (key_part_ref[:, cut] + column * key_state).astype(BF16)
        value_state = dot(key_ref[:, cut], grads)
        value_grad_ref[:, cut] = (value_part_ref[:, cut] + column * value_state).astype(BF16)


def join_body(plan, *refs):
    for k, piece_ref in enumerate(refs[:-1]):
        refs[-1][plan.rows_of(plan.peer(k))] = piece_ref[...]


def on_device(
    query_rows, key_rows, value_rows, log_decay, out_grad, norm_gain, state_in, state_out_grad
):
    heads, length = log_decay.shape
    size = state_in.shape[1]
    width = heads * size
    parties = lax.axis_size("head")
    plan = Plan(heads, size, lax.axis_size("seq"))
    bind = lambda body, *extra: functools.partial(body, plan, *extra)
    gain = norm_gain.reshape(1, width)
    piece = shaped((plan.rows, size))
    logged = shaped((plan.rows + LOG_ROWS, size))
    pieces = [piece] * plan.members
    table = shaped((length, width))
    rounded = shaped((length, width), BF16)
    hold = pltpu.VMEM((plan.members, plan.rows, size), F32)
    hold_logged = pltpu.VMEM((plan.members, plan.rows + LOG_ROWS, size), F32)
    hold_groups = pltpu.VMEM((plan.groups, plan.rows + LOG_ROWS, size), F32)
    hold_whole = pltpu.VMEM((width, size), F32)

    *sends, cum_log, cum_col = call(
        bind(summary_body),
        [logged] * plan.members + [shaped((heads, length)), shaped((length, heads))],
        [key_rows, value_rows, log_decay],
        [hold_whole],
    )
    parts = plan.swap_in_group(sends)
    weights, intra = call(
        bind(intra_body),
        [shaped((heads, length, length), BF16), table],
        [query_rows, key_rows, value_rows, cum_log, cum_col],
        flops=4 * heads * length * length * size,
    )
    total, logs = call(
        bind(group_total_body),
        [logged, shaped((plan.members, LOG_ROWS, size))],
        parts,
        [hold_logged],
    )
    totals = [total] + plan.from_groups(total, True)
    sends = call(
        bind(forward_scan_body),
        pieces,
        [*parts, *totals, state_in.reshape(width, size)],
        [hold_groups, hold_logged],
    )
    states = plan.swap_in_group(sends)
    attended, sums, states = call(
        bind(attended_body),
        [table, shaped((8, length)), shaped((width, size), BF16)],
        [*states, intra, query_rows, cum_col, out_grad, gain],
    )
    all_sums = [sums] + [
        lax.ppermute(sums, "head", [(i, (i + step) % parties) for i in range(parties)])
        for step in range(1, parties)
    ]
    attn_grad, *sends = call(
        bind(attn_grad_body, parties),
        [rounded] + pieces,
        [*all_sums, attended, query_rows, cum_col, out_grad, gain],
        [hold_whole],
    )
    parts = plan.swap_in_group(sends)
    query_grad, key_part, value_part = call(
        bind(score_grad_body),
        [rounded, table, table],
        [attn_grad, query_rows, key_rows, value_rows, states, weights, cum_log, cum_col],
        flops=10 * heads * length * length * size,
    )
    (total,) = call(bind(group_grad_body), [logged], [*parts, logs], [hold])
    totals = [total] + plan.from_groups(total, False)
    *sends, whole_total = call(
        bind(reverse_scan_body),
        pieces + [piece],
        [*parts, *totals, logs, state_out_grad.reshape(width, size)],
        [hold_groups, hold],
    )
    grads = plan.swap_in_group(sends)
    totals = plan.swap_in_group([whole_total] * plan.members)
    key_grad, value_grad = call(
        bind(finish_body),
        [rounded, rounded],
        [*grads, key_part, value_part, key_rows, value_rows, cum_col],
        [pltpu.VMEM((width, size), BF16)],
    )
    (state_in_grad,) = call(bind(join_body), [shaped((width, size))], totals)
    return (query_grad, key_grad, value_grad, state_in_grad.reshape(heads, size, size))


def solution(mesh):
    return jax.shard_map(
        on_device,
        mesh=mesh,
        in_specs=(
            P("seq", "head"),
            P("seq", "head"),
            P("seq", "head"),
            P("head", "seq"),
            P("seq", "head"),
            P("head"),
            P("head", None, None),
            P("head", None, None),
        ),
        out_specs=(P("seq", "head"), P("seq", "head"), P("seq", "head"), P("head", None, None)),
        check_vma=False,
    )
```

time: 124 us -> 76.5 us (0.62)
  blocking collectives: 78.8 us -> 0 us
  starting transfers between devices: 7.26 us -> 29.9 us
  waiting for transfers between devices: 10.8 us -> 32 us
  local copies, waits for them, and re-layouts: 14.6 us -> 2.81 us
    all_to_all x2 -> x0, blocking collectives: 41.2 us -> none  [swap(): return lax.all_to_all(parts, 'seq', 0, 0)]
    ppermute x0 -> x20, waiting for transfers between devices: none -> 32 us  [the longest x15 22 us: swap_in_group(): lax.ppermute(pieces[k], 'seq', [(i, i // span * span + (i % span ^ k)) fo...]
    all_gather x1 -> x0, blocking collectives: 31.9 us -> none  [on_device(): state_in_grad = lax.all_gather(total, 'seq').reshape(-1, size)[:width]]
    ppermute x0 -> x20, starting transfers between devices: none -> 29.9 us  [the longest x15 18.6 us: swap_in_group(): lax.ppermute(pieces[k], 'seq', [(i, i // span * span + (i % span ^ k)) fo...]
    unnamed x41 -> x20, local copies, waits for them, and re-layouts: 14.6 us -> 2.81 us
    all_to_all x2 -> x0, waiting for transfers between devices: 10.8 us -> none  [swap(): return lax.all_to_all(parts, 'seq', 0, 0)]
    all_to_all x2 -> x0, starting transfers between devices: 7.26 us -> none  [swap(): return lax.all_to_all(parts, 'seq', 0, 0)]
    psum x1 -> x0, blocking collectives: 5.73 us -> none  [on_device(): all_sums = lax.psum(sums, 'head')[None]]
  transfers between devices with their start and end apart: 2 -> 20, of which waited for: 1 -> 17; matrix products, arithmetic and copies ran while one was open for 0% -> 0% of each run, Pallas kernels for 4% -> 7%
where the time goes in v2:
time: 76.5 us; the launch traced here: 76.2 us
  waiting for transfers between devices  32 us (42%)
  starting transfers between devices  29.9 us (39%)
  Pallas kernels  10.8 us (14%)
  local copies, waits for them, and re-layouts  2.81 us (4%)
    ppermute x15, waiting for transfers between devices, swap_in_group(): lax.ppermute(pieces[k], 'seq', [(i, i // span * span + (i % span ^ k)) fo...  22 us
    ppermute x15, starting transfers between devices, swap_in_group(): lax.ppermute(pieces[k], 'seq', [(i, i // span * span + (i % span ^ k)) fo...  18.6 us
    pallas_call x11, Pallas kernels, call(): pl.pallas_call(body, out_shape=outs, in_specs=[VMEM] * len(operands), out...  10.8 us
    ppermute x2, waiting for transfers between devices, from_groups(): received.append(lax.ppermute(piece, 'seq', pairs))  8.68 us
    ppermute x2, starting transfers between devices, from_groups(): received.append(lax.ppermute(piece, 'seq', pairs))  8.25 us
    ppermute x3, starting transfers between devices, on_device(): lax.ppermute(sums, 'head', [(i, (i + step) % parties) for i in range(part...  3.02 us
    unnamed x20, local copies, waits for them, and re-layouts  2.81 us
  transfers between devices with their start and end apart: 20, of which 17 were waited for; matrix products, arithmetic and copies ran while one was open for 0% of the time, Pallas kernels for 7%

profile of v2, /device:TPU:0, one launch (start us, length us, event | category | flops | bytes accessed | tf_op | source)
XLA Modules:
  0.0 76.2 jit_solution(9592386711605408033)
XLA Ops:
  0.6 1.0 %copy-done.1 = bf16[256,1024]{1,0:T(8,128)(2,1)S(1)} copy-done((bf16[256,1024]{1,0:T(8,128)(2,1)S(1)}, bf16[256,1024]{1,0:T(8,128)(2,1)}, u32[]{:S(2)}) %copy-start.1) | copy-done | bytes 524312
  1.7 1.0 %copy-done.3 = bf16[256,1024]{1,0:T(8,128)(2,1)S(1)} copy-done((bf16[256,1024]{1,0:T(8,128)(2,1)S(1)}, bf16[256,1024]{1,0:T(8,128)(2,1)}, u32[]{:S(2)}) %copy-start.3) | copy-done | bytes 524312
  2.7 0.7 copy-done.9
  3.4 1.2 %shard_map.111 = (f32[264,128]{1,0:T(8,128)S(1)}, f32[264,128]{1,0:T(8,128)S(1)}, f32[264,128]{1,0:T(8,128)S(1)}, f32[264,128]{1,0:T(8,128)S(1)}, f32[8,256]{1,0:T(8,128)S(1)}, /*index=5*/f32[256,8]{1,0:T(8,128)S(1)}) custom-call(bf16[256,1024]{1,0:T(8,128)(2,1)S(1)} %copy-done.1, bf16[256,1024]{1,0:T(8,128)(2,1)S(1)} %copy-done.3, f32[8,256]{1,0:T(8,128)S(1)} %copy-done.9), custom_call_target="tpu_custom_call" | custom-call | bytes 1613824 | tf_op jit(solution)/shard_map/pallas_call | solution.py:23
  4.6 3.0 %collective-permute-start = (f32[264,128]{1,0:T(8,128)S(1)}, f32[264,128]{1,0:T(8,128)S(1)}, u32[]{:S(2)}, u32[]{:S(2)}) collective-permute-start(f32[264,128]{1,0:T(8,128)S(1)} %get-tuple-element.37), channel_id=1, source_target_pairs={{0,4},{4,0},{8,12},{12,8},{16,20},{20,16},{24,28},{28,24},{1,5},{5... | collective-permute-start | bytes 405512 | tf_op jit(solution)/shard_map/ppermute | solution.py:81
  7.6 1.6 %collective-permute-start.1 = (f32[264,128]{1,0:T(8,128)S(1)}, f32[264,128]{1,0:T(8,128)S(1)}, u32[]{:S(2)}, u32[]{:S(2)}) collective-permute-start(f32[264,128]{1,0:T(8,128)S(1)} %get-tuple-element.38), channel_id=1, source_target_pairs={{0,8},{4,12},{8,0},{12,4},{16,24},{20,28},{24,16},{28,20},{1,9},{5... | collective-permute-start | bytes 405512 | tf_op jit(solution)/shard_map/ppermute | solution.py:81
  9.2 2.0 %collective-permute-done.refs_1_ = f32[264,128]{1,0:T(8,128)S(1)} collective-permute-done((f32[264,128]{1,0:T(8,128)S(1)}, f32[264,128]{1,0:T(8,128)S(1)}, u32[]{:S(2)}, u32[]{:S(2)}) %collective-permute-start) | collective-permute-done | bytes 135200 | tf_op jit(solution)/shard_map/ppermute | solution.py:81
  11.2 2.9 %collective-permute-done.1.refs_2_ = f32[264,128]{1,0:T(8,128)S(1)} collective-permute-done((f32[264,128]{1,0:T(8,128)S(1)}, f32[264,128]{1,0:T(8,128)S(1)}, u32[]{:S(2)}, u32[]{:S(2)}) %collective-permute-start.1) | collective-permute-done | bytes 135200 | tf_op jit(solution)/shard_map/ppermute | solution.py:81
  14.1 1.3 %collective-permute-done.2.refs_3_ = f32[264,128]{1,0:T(8,128)S(1)} collective-permute-done((f32[264,128]{1,0:T(8,128)S(1)}, f32[264,128]{1,0:T(8,128)S(1)}, u32[]{:S(2)}, u32[]{:S(2)}) %collective-permute-start.2) | collective-permute-done | bytes 135200 | tf_op jit(solution)/shard_map/ppermute | solution.py:81
  15.4 0.1 shard_map.112
  15.5 4.8 %collective-permute-start.3 = (f32[264,128]{1,0:T(8,128)S(1)}, f32[264,128]{1,0:T(8,128)S(1)}, u32[]{:S(2)}, u32[]{:S(2)}) collective-permute-start(f32[264,128]{1,0:T(8,128)S(1)} %get-tuple-element.40.refs_4_), channel_id=1, source_target_pairs={{0,16},{4,20},{8,24},{12,28},{1,17},{5,21},{9,25},{13,29},{2,18},{... | collective-permute-start | bytes 405512 | tf_op jit(solution)/shard_map/ppermute | solution.py:95
  20.3 2.5 %collective-permute-done.3.refs_5_ = f32[264,128]{1,0:T(8,128)S(1)} collective-permute-done((f32[264,128]{1,0:T(8,128)S(1)}, f32[264,128]{1,0:T(8,128)S(1)}, u32[]{:S(2)}, u32[]{:S(2)}) %collective-permute-start.3) | collective-permute-done | bytes 135200 | tf_op jit(solution)/shard_map/ppermute | solution.py:95
  22.8 0.2 shard_map.113
  23.0 1.6 %collective-permute-start.4 = (f32[256,128]{1,0:T(8,128)S(1)}, f32[256,128]{1,0:T(8,128)S(1)}, u32[]{:S(2)}, u32[]{:S(2)}) collective-permute-start(f32[256,128]{1,0:T(8,128)S(1)} %get-tuple-element.42), channel_id=1, source_target_pairs={{0,4},{4,0},{8,12},{12,8},{16,20},{20,16},{24,28},{28,24},{1,5},{5... | collective-permute-start | bytes 393224 | tf_op jit(solution)/shard_map/ppermute | solution.py:81
  24.6 3.1 %collective-permute-start.5 = (f32[256,128]{1,0:T(8,128)S(1)}, f32[256,128]{1,0:T(8,128)S(1)}, u32[]{:S(2)}, u32[]{:S(2)}) collective-permute-start(f32[256,128]{1,0:T(8,128)S(1)} %get-tuple-element.43), channel_id=1, source_target_pairs={{0,8},{4,12},{8,0},{12,4},{16,24},{20,28},{24,16},{28,20},{1,9},{5... | collective-permute-start | bytes 393224 | tf_op jit(solution)/shard_map/ppermute | solution.py:81
  27.8 0.1 collective-permute-start.6
  27.9 0.9 %shard_map.114 = (bf16[8,256,256]{2,1,0:T(8,128)(2,1)S(1)}, f32[256,1024]{1,0:T(8,128)S(1)}) custom-call(bf16[256,1024]{1,0:T(8,128)(2,1)S(1)} %copy-done, bf16[256,1024]{1,0:T(8,128)(2,1)S(1)} %copy-done.2, bf16[256,1024]{1,0:T(8,128)(2,1)S(1)} %copy-done.4, f32[8,256]{1,0:T(8,128)S(1)} %get-tuple-element.45.cum_ref, ...), custom_call_target="tpu_custom_call" | custom-call | flops 268435456 | bytes 3686400 | tf_op jit(solution)/shard_map/pallas_call | solution.py:23
  28.8 2.7 %collective-permute-done.5.refs_2_ = f32[256,128]{1,0:T(8,128)S(1)} collective-permute-done((f32[256,128]{1,0:T(8,128)S(1)}, f32[256,128]{1,0:T(8,128)S(1)}, u32[]{:S(2)}, u32[]{:S(2)}) %collective-permute-start.5) | collective-permute-done | bytes 131104 | tf_op jit(solution)/shard_map/ppermute | solution.py:81
  31.5 2.1 %collective-permute-done.6.refs_3_ = f32[256,128]{1,0:T(8,128)S(1)} collective-permute-done((f32[256,128]{1,0:T(8,128)S(1)}, f32[256,128]{1,0:T(8,128)S(1)}, u32[]{:S(2)}, u32[]{:S(2)}) %collective-permute-start.6) | collective-permute-done | bytes 131104 | tf_op jit(solution)/shard_map/ppermute | solution.py:81
  33.6 0.8 %shard_map.115 = (f32[256,1024]{1,0:T(8,128)S(1)}, f32[8,256]{1,0:T(8,128)S(1)}, bf16[1024,128]{1,0:T(8,128)(2,1)S(1)}) custom-call(f32[256,128]{1,0:T(8,128)S(1)} %get-tuple-element.41.refs_0_, f32[256,128]{1,0:T(8,128)S(1)} %collective-permute-done.4.refs_1_, f32[256,128]{1,0:T(8,128)S(1)} %collective-permute-done.5.refs_2_, ...), custom_call_target="tpu_custom_call" | custom-call | bytes 3952640 | tf_op jit(solution)/shard_map/pallas_call | solution.py:23
  34.4 1.6 %collective-permute-start.8 = (f32[8,256]{1,0:T(8,128)S(1)}, f32[8,256]{1,0:T(8,128)S(1)}, u32[]{:S(2)}, u32[]{:S(2)}) collective-permute-start(f32[8,256]{1,0:T(8,128)S(1)} %get-tuple-element.48.refs_0_), channel_id=1, source_target_pairs={{0,2},{1,3},{2,0},{3,1},{4,6},{5,7},{6,4},{7,5},{8,10},{9,11},{10,... | collective-permute-start | bytes 24584 | tf_op jit(solution)/shard_map/ppermute | solution.py:381
  36.0 1.4 %collective-permute-start.9 = (f32[8,256]{1,0:T(8,128)S(1)}, f32[8,256]{1,0:T(8,128)S(1)}, u32[]{:S(2)}, u32[]{:S(2)}) collective-permute-start(f32[8,256]{1,0:T(8,128)S(1)} %get-tuple-element.48.refs_0_), channel_id=1, source_target_pairs={{0,3},{1,0},{2,1},{3,2},{4,7},{5,4},{6,5},{7,6},{8,11},{9,8},{10,9... | collective-permute-start | bytes 24584 | tf_op jit(solution)/shard_map/ppermute | solution.py:381
  37.6 0.6 collective-permute-done.8.refs_2_
  38.2 0.7 collective-permute-done.9.refs_3_
  38.8 1.4 %shard_map.116 = (bf16[256,1024]{1,0:T(8,128)(2,1)S(1)}, f32[256,128]{1,0:T(8,128)S(1)}, f32[256,128]{1,0:T(8,128)S(1)}, f32[256,128]{1,0:T(8,128)S(1)}, f32[256,128]{1,0:T(8,128)S(1)}) custom-call(f32[8,256]{1,0:T(8,128)S(1)} %get-tuple-element.48.refs_0_, f32[8,256]{1,0:T(8,128)S(1)} %collective-permute-done.7.refs_1_, ...), custom_call_target="tpu_custom_call" | custom-call | bytes 3190784 | tf_op jit(solution)/shard_map/pallas_call | solution.py:23
  40.2 0.8 %collective-permute-start.10 = (f32[256,128]{1,0:T(8,128)S(1)}, f32[256,128]{1,0:T(8,128)S(1)}, u32[]{:S(2)}, u32[]{:S(2)}) collective-permute-start(f32[256,128]{1,0:T(8,128)S(1)} %get-tuple-element.55), channel_id=1, source_target_pairs={{0,4},{4,0},{8,12},{12,8},{16,20},{20,16},{24,28},{28,24},{1,5},{5... | collective-permute-start | bytes 393224 | tf_op jit(solution)/shard_map/ppermute | solution.py:81
  41.1 1.2 %collective-permute-start.11 = (f32[256,128]{1,0:T(8,128)S(1)}, f32[256,128]{1,0:T(8,128)S(1)}, u32[]{:S(2)}, u32[]{:S(2)}) collective-permute-start(f32[256,128]{1,0:T(8,128)S(1)} %get-tuple-element.56), channel_id=1, source_target_pairs={{0,8},{4,12},{8,0},{12,4},{16,24},{20,28},{24,16},{28,20},{1,9},{5... | collective-permute-start | bytes 393224 | tf_op jit(solution)/shard_map/ppermute | solution.py:81
  42.3 1.5 %collective-permute-start.12 = (f32[256,128]{1,0:T(8,128)S(1)}, f32[256,128]{1,0:T(8,128)S(1)}, u32[]{:S(2)}, u32[]{:S(2)}) collective-permute-start(f32[256,128]{1,0:T(8,128)S(1)} %get-tuple-element.57), channel_id=1, source_target_pairs={{0,12},{4,8},{8,4},{12,0},{16,28},{20,24},{24,20},{28,16},{1,13},{... | collective-permute-start | bytes 393224 | tf_op jit(solution)/shard_map/ppermute | solution.py:81
  43.8 2.5 %collective-permute-done.10.refs_1_ = f32[256,128]{1,0:T(8,128)S(1)} collective-permute-done((f32[256,128]{1,0:T(8,128)S(1)}, f32[256,128]{1,0:T(8,128)S(1)}, u32[]{:S(2)}, u32[]{:S(2)}) %collective-permute-start.10) | collective-permute-done | bytes 131104 | tf_op jit(solution)/shard_map/ppermute | solution.py:81
  46.3 1.1 %collective-permute-done.11.refs_2_ = f32[256,128]{1,0:T(8,128)S(1)} collective-permute-done((f32[256,128]{1,0:T(8,128)S(1)}, f32[256,128]{1,0:T(8,128)S(1)}, u32[]{:S(2)}, u32[]{:S(2)}) %collective-permute-start.11) | collective-permute-done | bytes 131104 | tf_op jit(solution)/shard_map/ppermute | solution.py:81
  47.4 2.9 %collective-permute-done.12.refs_3_ = f32[256,128]{1,0:T(8,128)S(1)} collective-permute-done((f32[256,128]{1,0:T(8,128)S(1)}, f32[256,128]{1,0:T(8,128)S(1)}, u32[]{:S(2)}, u32[]{:S(2)}) %collective-permute-start.12) | collective-permute-done | bytes 131104 | tf_op jit(solution)/shard_map/ppermute | solution.py:81
  50.3 0.1 shard_map.118.refs_4_
  50.4 3.4 %collective-permute-start.13 = (f32[264,128]{1,0:T(8,128)S(1)}, f32[264,128]{1,0:T(8,128)S(1)}, u32[]{:S(2)}, u32[]{:S(2)}) collective-permute-start(f32[264,128]{1,0:T(8,128)S(1)} %shard_map.118.refs_4_), channel_id=1, source_target_pairs={{0,16},{4,20},{8,24},{12,28},{16,0},{20,4},{24,8},{28,12},{1,17},{... | collective-permute-start | bytes 405512 | tf_op jit(solution)/shard_map/ppermute | solution.py:95
  53.8 6.1 %collective-permute-done.13.refs_5_ = f32[264,128]{1,0:T(8,128)S(1)} collective-permute-done((f32[264,128]{1,0:T(8,128)S(1)}, f32[264,128]{1,0:T(8,128)S(1)}, u32[]{:S(2)}, u32[]{:S(2)}) %collective-permute-start.13) | collective-permute-done | bytes 135200 | tf_op jit(solution)/shard_map/ppermute | solution.py:95
  60.0 0.2 shard_map.119
  60.2 1.0 %collective-permute-start.17 = (f32[256,128]{1,0:T(8,128)S(1)}, f32[256,128]{1,0:T(8,128)S(1)}, u32[]{:S(2)}, u32[]{:S(2)}) collective-permute-start(f32[256,128]{1,0:T(8,128)S(1)} %get-tuple-element.67.refs_0_), channel_id=1, source_target_pairs={{0,4},{4,0},{8,12},{12,8},{16,20},{20,16},{24,28},{28,24},{1,5},{5... | collective-permute-start | bytes 393224 | tf_op jit(solution)/shard_map/ppermute | solution.py:81
  61.2 0.7 collective-permute-start.18
  61.9 1.8 %collective-permute-start.19 = (f32[256,128]{1,0:T(8,128)S(1)}, f32[256,128]{1,0:T(8,128)S(1)}, u32[]{:S(2)}, u32[]{:S(2)}) collective-permute-start(f32[256,128]{1,0:T(8,128)S(1)} %get-tuple-element.67.refs_0_), channel_id=1, source_target_pairs={{0,12},{4,8},{8,4},{12,0},{16,28},{20,24},{24,20},{28,16},{1,13},{... | collective-permute-start | bytes 393224 | tf_op jit(solution)/shard_map/ppermute | solution.py:81
  63.7 1.0 %collective-permute-start.14 = (f32[256,128]{1,0:T(8,128)S(1)}, f32[256,128]{1,0:T(8,128)S(1)}, u32[]{:S(2)}, u32[]{:S(2)}) collective-permute-start(f32[256,128]{1,0:T(8,128)S(1)} %get-tuple-element.60), channel_id=1, source_target_pairs={{0,4},{4,0},{8,12},{12,8},{16,20},{20,16},{24,28},{28,24},{1,5},{5... | collective-permute-start | bytes 393224 | tf_op jit(solution)/shard_map/ppermute | solution.py:81
  64.7 0.7 collective-permute-start.15
  65.4 1.4 %collective-permute-done.17.refs_1_ = f32[256,128]{1,0:T(8,128)S(1)} collective-permute-done((f32[256,128]{1,0:T(8,128)S(1)}, f32[256,128]{1,0:T(8,128)S(1)}, u32[]{:S(2)}, u32[]{:S(2)}) %collective-permute-start.17) | collective-permute-done | bytes 131104 | tf_op jit(solution)/shard_map/ppermute | solution.py:81
  66.8 0.4 collective-permute-start.16
  67.2 3.5 %shard_map.117 = (bf16[256,1024]{1,0:T(8,128)(2,1)}, f32[256,1024]{1,0:T(8,128)S(1)}, f32[256,1024]{1,0:T(8,128)S(1)}) custom-call(bf16[256,1024]{1,0:T(8,128)(2,1)S(1)} %get-tuple-element.50.attn_grad_ref, bf16[256,1024]{1,0:T(8,128)(2,1)S(1)} %copy-done, bf16[256,1024]{1,0:T(8,128)(2,1)S(1)} %copy-done.2, bf16[256,1024]{1,0:T(8,128)(2,1)S(1)} %copy-done.4, ...), custom_call_target="tpu_custom_call" | custom-call | flops 671088640 | bytes 6045696 | tf_op jit(solution)/shard_map/pallas_call | solution.py:23
  70.7 0.4 collective-permute-done.19.refs_3_
  71.0 0.8 %shard_map.121 = f32[1024,128]{1,0:T(8,128)} custom-call(f32[256,128]{1,0:T(8,128)S(1)} %get-tuple-element.67.refs_0_, f32[256,128]{1,0:T(8,128)S(1)} %collective-permute-done.17.refs_1_, f32[256,128]{1,0:T(8,128)S(1)} %collective-permute-done.18.refs_2_, f32[256,128]{1,0:T(8,128)S(1)} %collective-permute-done.19.refs_3_), custom_call_target="tpu_custom_call" | custom-call | bytes 1048576 | tf_op jit(solution)/shard_map/pallas_call | solution.py:23
  71.9 0.6 collective-permute-done.15.refs_2_
  72.5 2.2 %collective-permute-done.16.refs_3_ = f32[256,128]{1,0:T(8,128)S(1)} collective-permute-done((f32[256,128]{1,0:T(8,128)S(1)}, f32[256,128]{1,0:T(8,128)S(1)}, u32[]{:S(2)}, u32[]{:S(2)}) %collective-permute-start.16) | collective-permute-done | bytes 131104 | tf_op jit(solution)/shard_map/ppermute | solution.py:81
  74.7 1.6 %shard_map.120 = (bf16[256,1024]{1,0:T(8,128)(2,1)}, bf16[256,1024]{1,0:T(8,128)(2,1)}) custom-call(f32[256,128]{1,0:T(8,128)S(1)} %get-tuple-element.59.refs_0_, f32[256,128]{1,0:T(8,128)S(1)} %collective-permute-done.14.refs_1_, f32[256,128]{1,0:T(8,128)S(1)} %collective-permute-done.15.refs_2_, f32[256,128]{1,0:T(8,128)S(1)} %collective-permute-done.16.refs_3_, ...), custom_call_target="tpu_custom_call" | custom-call | bytes 4726784 | tf_op jit(solution)/shard_map/pallas_call | solution.py:23
  (23 shorter events, 0.1 us)
Async XLA Ops:
  0.6 1.0 %copy-start.1 = (bf16[256,1024]{1,0:T(8,128)(2,1)S(1)}, bf16[256,1024]{1,0:T(8,128)(2,1)}, u32[]{:S(2)}) copy-start(bf16[256,1024]{1,0:T(8,128)(2,1)} %refs_6_.1) | copy-start | bytes 1572868
  1.7 1.0 %copy-start.3 = (bf16[256,1024]{1,0:T(8,128)(2,1)S(1)}, bf16[256,1024]{1,0:T(8,128)(2,1)}, u32[]{:S(2)}) copy-start(bf16[256,1024]{1,0:T(8,128)(2,1)} %refs_7_.5) | copy-start | bytes 1572868
  2.7 0.7 copy-start.9
  3.4 19.4 %copy-start.6 = (f32[8,128,128]{2,1,0:T(8,128)S(1)}, f32[8,128,128]{2,1,0:T(8,128)}, u32[]{:S(2)}) copy-start(f32[8,128,128]{2,1,0:T(8,128)} %param.14) | copy-start | bytes 1572868
  4.6 6.6 %collective-permute-start = (f32[264,128]{1,0:T(8,128)S(1)}, f32[264,128]{1,0:T(8,128)S(1)}, u32[]{:S(2)}, u32[]{:S(2)}) collective-permute-start(f32[264,128]{1,0:T(8,128)S(1)} %get-tuple-element.37), channel_id=1, source_target_pairs={{0,4},{4,0},{8,12},{12,8},{16,20},{20,16},{24,28},{28,24},{1,5},{5... | collective-permute-start | bytes 405512 | tf_op jit(solution)/shard_map/ppermute | solution.py:81
  7.6 6.5 %collective-permute-start.1 = (f32[264,128]{1,0:T(8,128)S(1)}, f32[264,128]{1,0:T(8,128)S(1)}, u32[]{:S(2)}, u32[]{:S(2)}) collective-permute-start(f32[264,128]{1,0:T(8,128)S(1)} %get-tuple-element.38), channel_id=1, source_target_pairs={{0,8},{4,12},{8,0},{12,4},{16,24},{20,28},{24,16},{28,20},{1,9},{5... | collective-permute-start | bytes 405512 | tf_op jit(solution)/shard_map/ppermute | solution.py:81
  9.2 6.1 %collective-permute-start.2 = (f32[264,128]{1,0:T(8,128)S(1)}, f32[264,128]{1,0:T(8,128)S(1)}, u32[]{:S(2)}, u32[]{:S(2)}) collective-permute-start(f32[264,128]{1,0:T(8,128)S(1)} %get-tuple-element.39), channel_id=1, source_target_pairs={{0,12},{4,8},{8,4},{12,0},{16,28},{20,24},{24,20},{28,16},{1,13},{... | collective-permute-start | bytes 405512 | tf_op jit(solution)/shard_map/ppermute | solution.py:81
  15.4 12.5 %copy-start.4 = (bf16[256,1024]{1,0:T(8,128)(2,1)S(1)}, bf16[256,1024]{1,0:T(8,128)(2,1)}, u32[]{:S(2)}) copy-start(bf16[256,1024]{1,0:T(8,128)(2,1)} %refs_7_.5) | copy-start | bytes 1572868
  15.5 7.3 %collective-permute-start.3 = (f32[264,128]{1,0:T(8,128)S(1)}, f32[264,128]{1,0:T(8,128)S(1)}, u32[]{:S(2)}, u32[]{:S(2)}) collective-permute-start(f32[264,128]{1,0:T(8,128)S(1)} %get-tuple-element.40.refs_4_), channel_id=1, source_target_pairs={{0,16},{4,20},{8,24},{12,28},{1,17},{5,21},{9,25},{13,29},{2,18},{... | collective-permute-start | bytes 405512 | tf_op jit(solution)/shard_map/ppermute | solution.py:95
  22.8 5.0 %copy-start = (bf16[256,1024]{1,0:T(8,128)(2,1)S(1)}, bf16[256,1024]{1,0:T(8,128)(2,1)}, u32[]{:S(2)}) copy-start(bf16[256,1024]{1,0:T(8,128)(2,1)} %query_ref.3) | copy-start | bytes 1572868
  22.8 5.0 %copy-start.2 = (bf16[256,1024]{1,0:T(8,128)(2,1)S(1)}, bf16[256,1024]{1,0:T(8,128)(2,1)}, u32[]{:S(2)}) copy-start(bf16[256,1024]{1,0:T(8,128)(2,1)} %refs_6_.1) | copy-start | bytes 1572868
  23.0 5.8 %collective-permute-start.4 = (f32[256,128]{1,0:T(8,128)S(1)}, f32[256,128]{1,0:T(8,128)S(1)}, u32[]{:S(2)}, u32[]{:S(2)}) collective-permute-start(f32[256,128]{1,0:T(8,128)S(1)} %get-tuple-element.42), channel_id=1, source_target_pairs={{0,4},{4,0},{8,12},{12,8},{16,20},{20,16},{24,28},{28,24},{1,5},{5... | collective-permute-start | bytes 393224 | tf_op jit(solution)/shard_map/ppermute | solution.py:81
  24.6 6.9 %collective-permute-start.5 = (f32[256,128]{1,0:T(8,128)S(1)}, f32[256,128]{1,0:T(8,128)S(1)}, u32[]{:S(2)}, u32[]{:S(2)}) collective-permute-start(f32[256,128]{1,0:T(8,128)S(1)} %get-tuple-element.43), channel_id=1, source_target_pairs={{0,8},{4,12},{8,0},{12,4},{16,24},{20,28},{24,16},{28,20},{1,9},{5... | collective-permute-start | bytes 393224 | tf_op jit(solution)/shard_map/ppermute | solution.py:81
  27.8 5.9 %collective-permute-start.6 = (f32[256,128]{1,0:T(8,128)S(1)}, f32[256,128]{1,0:T(8,128)S(1)}, u32[]{:S(2)}, u32[]{:S(2)}) collective-permute-start(f32[256,128]{1,0:T(8,128)S(1)} %get-tuple-element.44), channel_id=1, source_target_pairs={{0,12},{4,8},{8,4},{12,0},{16,28},{20,24},{24,20},{28,16},{1,13},{... | collective-permute-start | bytes 393224 | tf_op jit(solution)/shard_map/ppermute | solution.py:81
  27.9 5.8 %copy-start.5 = (bf16[256,1024]{1,0:T(8,128)(2,1)S(1)}, bf16[256,1024]{1,0:T(8,128)(2,1)}, u32[]{:S(2)}) copy-start(bf16[256,1024]{1,0:T(8,128)(2,1)} %refs_7_.4) | copy-start | bytes 1572868
  28.8 4.8 %copy-start.8 = (f32[1024]{0:T(1024)S(1)}, f32[1024]{0:T(1024)}, u32[]{:S(2)}) copy-start(f32[1024]{0:T(1024)} %param.13) | copy-start | bytes 12292
  34.4 3.1 %collective-permute-start.7 = (f32[8,256]{1,0:T(8,128)S(1)}, f32[8,256]{1,0:T(8,128)S(1)}, u32[]{:S(2)}, u32[]{:S(2)}) collective-permute-start(f32[8,256]{1,0:T(8,128)S(1)} %get-tuple-element.48.refs_0_), channel_id=1, source_target_pairs={{0,1},{1,2},{2,3},{3,0},{4,5},{5,6},{6,7},{7,4},{8,9},{9,10},{10,1... | collective-permute-start | bytes 24584 | tf_op jit(solution)/shard_map/ppermute | solution.py:381
  34.4 3.7 %collective-permute-start.8 = (f32[8,256]{1,0:T(8,128)S(1)}, f32[8,256]{1,0:T(8,128)S(1)}, u32[]{:S(2)}, u32[]{:S(2)}) collective-permute-start(f32[8,256]{1,0:T(8,128)S(1)} %get-tuple-element.48.refs_0_), channel_id=1, source_target_pairs={{0,2},{1,3},{2,0},{3,1},{4,6},{5,7},{6,4},{7,5},{8,10},{9,11},{10,... | collective-permute-start | bytes 24584 | tf_op jit(solution)/shard_map/ppermute | solution.py:381
  36.0 2.8 %collective-permute-start.9 = (f32[8,256]{1,0:T(8,128)S(1)}, f32[8,256]{1,0:T(8,128)S(1)}, u32[]{:S(2)}, u32[]{:S(2)}) collective-permute-start(f32[8,256]{1,0:T(8,128)S(1)} %get-tuple-element.48.refs_0_), channel_id=1, source_target_pairs={{0,3},{1,0},{2,1},{3,2},{4,7},{5,4},{6,5},{7,6},{8,11},{9,8},{10,9... | collective-permute-start | bytes 24584 | tf_op jit(solution)/shard_map/ppermute | solution.py:381
  40.2 19.7 %copy-start.7 = (f32[8,128,128]{2,1,0:T(8,128)S(1)}, f32[8,128,128]{2,1,0:T(8,128)}, u32[]{:S(2)}) copy-start(f32[8,128,128]{2,1,0:T(8,128)} %param.15) | copy-start | bytes 1572868
  40.2 6.1 %collective-permute-start.10 = (f32[256,128]{1,0:T(8,128)S(1)}, f32[256,128]{1,0:T(8,128)S(1)}, u32[]{:S(2)}, u32[]{:S(2)}) collective-permute-start(f32[256,128]{1,0:T(8,128)S(1)} %get-tuple-element.55), channel_id=1, source_target_pairs={{0,4},{4,0},{8,12},{12,8},{16,20},{20,16},{24,28},{28,24},{1,5},{5... | collective-permute-start | bytes 393224 | tf_op jit(solution)/shard_map/ppermute | solution.py:81
  41.1 6.3 %collective-permute-start.11 = (f32[256,128]{1,0:T(8,128)S(1)}, f32[256,128]{1,0:T(8,128)S(1)}, u32[]{:S(2)}, u32[]{:S(2)}) collective-permute-start(f32[256,128]{1,0:T(8,128)S(1)} %get-tuple-element.56), channel_id=1, source_target_pairs={{0,8},{4,12},{8,0},{12,4},{16,24},{20,28},{24,16},{28,20},{1,9},{5... | collective-permute-start | bytes 393224 | tf_op jit(solution)/shard_map/ppermute | solution.py:81
  42.3 8.0 %collective-permute-start.12 = (f32[256,128]{1,0:T(8,128)S(1)}, f32[256,128]{1,0:T(8,128)S(1)}, u32[]{:S(2)}, u32[]{:S(2)}) collective-permute-start(f32[256,128]{1,0:T(8,128)S(1)} %get-tuple-element.57), channel_id=1, source_target_pairs={{0,12},{4,8},{8,4},{12,0},{16,28},{20,24},{24,20},{28,16},{1,13},{... | collective-permute-start | bytes 393224 | tf_op jit(solution)/shard_map/ppermute | solution.py:81
  50.4 9.6 %collective-permute-start.13 = (f32[264,128]{1,0:T(8,128)S(1)}, f32[264,128]{1,0:T(8,128)S(1)}, u32[]{:S(2)}, u32[]{:S(2)}) collective-permute-start(f32[264,128]{1,0:T(8,128)S(1)} %shard_map.118.refs_4_), channel_id=1, source_target_pairs={{0,16},{4,20},{8,24},{12,28},{16,0},{20,4},{24,8},{28,12},{1,17},{... | collective-permute-start | bytes 405512 | tf_op jit(solution)/shard_map/ppermute | solution.py:95
  60.2 6.6 %collective-permute-start.17 = (f32[256,128]{1,0:T(8,128)S(1)}, f32[256,128]{1,0:T(8,128)S(1)}, u32[]{:S(2)}, u32[]{:S(2)}) collective-permute-start(f32[256,128]{1,0:T(8,128)S(1)} %get-tuple-element.67.refs_0_), channel_id=1, source_target_pairs={{0,4},{4,0},{8,12},{12,8},{16,20},{20,16},{24,28},{28,24},{1,5},{5... | collective-permute-start | bytes 393224 | tf_op jit(solution)/shard_map/ppermute | solution.py:81
  61.2 9.5 %collective-permute-start.18 = (f32[256,128]{1,0:T(8,128)S(1)}, f32[256,128]{1,0:T(8,128)S(1)}, u32[]{:S(2)}, u32[]{:S(2)}) collective-permute-start(f32[256,128]{1,0:T(8,128)S(1)} %get-tuple-element.67.refs_0_), channel_id=1, source_target_pairs={{0,8},{4,12},{8,0},{12,4},{16,24},{20,28},{24,16},{28,20},{1,9},{5... | collective-permute-start | bytes 393224 | tf_op jit(solution)/shard_map/ppermute | solution.py:81
  61.9 9.2 %collective-permute-start.19 = (f32[256,128]{1,0:T(8,128)S(1)}, f32[256,128]{1,0:T(8,128)S(1)}, u32[]{:S(2)}, u32[]{:S(2)}) collective-permute-start(f32[256,128]{1,0:T(8,128)S(1)} %get-tuple-element.67.refs_0_), channel_id=1, source_target_pairs={{0,12},{4,8},{8,4},{12,0},{16,28},{20,24},{24,20},{28,16},{1,13},{... | collective-permute-start | bytes 393224 | tf_op jit(solution)/shard_map/ppermute | solution.py:81
  63.7 8.2 %collective-permute-start.14 = (f32[256,128]{1,0:T(8,128)S(1)}, f32[256,128]{1,0:T(8,128)S(1)}, u32[]{:S(2)}, u32[]{:S(2)}) collective-permute-start(f32[256,128]{1,0:T(8,128)S(1)} %get-tuple-element.60), channel_id=1, source_target_pairs={{0,4},{4,0},{8,12},{12,8},{16,20},{20,16},{24,28},{28,24},{1,5},{5... | collective-permute-start | bytes 393224 | tf_op jit(solution)/shard_map/ppermute | solution.py:81
  64.7 7.8 %collective-permute-start.15 = (f32[256,128]{1,0:T(8,128)S(1)}, f32[256,128]{1,0:T(8,128)S(1)}, u32[]{:S(2)}, u32[]{:S(2)}) collective-permute-start(f32[256,128]{1,0:T(8,128)S(1)} %get-tuple-element.61), channel_id=1, source_target_pairs={{0,8},{4,12},{8,0},{12,4},{16,24},{20,28},{24,16},{28,20},{1,9},{5... | collective-permute-start | bytes 393224 | tf_op jit(solution)/shard_map/ppermute | solution.py:81
  66.8 7.9 %collective-permute-start.16 = (f32[256,128]{1,0:T(8,128)S(1)}, f32[256,128]{1,0:T(8,128)S(1)}, u32[]{:S(2)}, u32[]{:S(2)}) collective-permute-start(f32[256,128]{1,0:T(8,128)S(1)} %get-tuple-element.62), channel_id=1, source_target_pairs={{0,12},{4,8},{8,4},{12,0},{16,28},{20,24},{24,20},{28,16},{1,13},{... | collective-permute-start | bytes 393224 | tf_op jit(solution)/shard_map/ppermute | solution.py:81

commit v3 on v2

--- a/solution.py
+++ b/solution.py
@@ -16,14 +16,16 @@
 CONTRACT_ROWS = (((0,), (0,)), ((), ()))
 CONTRACT_COLS = (((1,), (1,)), ((), ()))
 VMEM = pl.BlockSpec(memory_space=pltpu.VMEM)
-
-
-def call(body, outs, operands, scratch=(), flops=0):
+HBM = pl.BlockSpec(memory_space=pltpu.HBM)
+ANY = pl.BlockSpec(memory_space=pl.ANY)
+
+
+def call(body, outs, operands, scratch=(), flops=0, specs=None):
     size = sum(x.size * x.dtype.itemsize for x in (*operands, *outs))
     return pl.pallas_call(
         body,
         out_shape=outs,
-        in_specs=[VMEM] * len(operands),
+        in_specs=specs or [VMEM] * len(operands),
         out_specs=[VMEM] * len(outs),
         scratch_shapes=list(scratch),
         compiler_params=pltpu.CompilerParams(vmem_limit_bytes=24 * 1024 * 1024),
@@ -62,6 +64,7 @@
         self.groups = blocks // self.members
         self.own = heads // self.members
         self.rows = self.own * size
+        self.ways = sorted(range(self.members), key=lambda way: (way > 0, -way.bit_count()))
 
     def member(self):
         return lax.rem(lax.axis_index("seq"), self.members)
@@ -70,30 +73,28 @@
         return lax.div(lax.axis_index("seq"), self.members)
 
     def peer(self, k):
-        return lax.bitwise_xor(self.member(), k)
+        return lax.bitwise_xor(self.member(), self.ways[k])
 
     def rows_of(self, member):
         return pl.ds(pl.multiple_of(member * self.rows, self.rows), self.rows)
 
     def swap_in_group(self, pieces):
         span = self.members
-        return [pieces[0]] + [
+        swapped = [pieces[0]]
+        for way, piece in zip(self.ways[1:], pieces[1:]):
+            pairs = [(i, i // span * span + (i % span ^ way)) for i in range(self.blocks)]
+            swapped.append(lax.ppermute(piece, "seq", pairs))
+        return swapped
+
+    def from_groups(self, piece):
+        return [
             lax.ppermute(
-                pieces[k], "seq", [(i, i // span * span + (i % span ^ k)) for i in range(self.blocks)]
+                piece,
+                "seq",
+                [(i, (i + step * self.members) % self.blocks) for i in range(self.blocks)],
             )
-            for k in range(1, span)
+            for step in range(1, self.groups)
         ]
-
-    def from_groups(self, piece, earlier_only):
-        received = []
-        for step in range(1, self.groups):
-            pairs = [(i, i + step * self.members) for i in range(self.blocks)]
-            if earlier_only:
-                pairs = [(i, j) for i, j in pairs if j < self.blocks]
-            else:
-                pairs = [(i, j % self.blocks) for i, j in pairs]
-            received.append(lax.ppermute(piece, "seq", pairs))
-        return received
 
 
 def own_decays(plan, log_tile_ref, base):
@@ -102,9 +103,24 @@
     return jnp.concatenate([jnp.broadcast_to(jnp.exp(row), (plan.size, plan.size)) for row in rows])
 
 
-def summary_body(plan, key_ref, value_ref, decay_ref, *refs):
-    send_refs, (cum_ref, cum_col_ref, held_ref) = refs[: plan.members], refs[plan.members :]
+def summary_body(plan, key_hbm, value_hbm, decay_hbm, *refs):
+    send_refs, refs = refs[: plan.members], refs[plan.members :]
+    cum_ref, cum_col_ref, held_ref, key_ref, value_ref, decay_ref, sems, decay_sem = refs
     length, heads, size = key_ref.shape[0], plan.heads, plan.size
+    decay_copy = pltpu.make_async_copy(decay_hbm, decay_ref, decay_sem)
+    decay_copy.start()
+    copies = []
+    for part in range(plan.members):
+        cut = lanes(part, plan.rows)
+        copies.append(
+            [
+                pltpu.make_async_copy(source.at[:, cut], target.at[:, cut], sems.at[part, i])
+                for i, (source, target) in enumerate([(key_hbm, key_ref), (value_hbm, value_ref)])
+            ]
+        )
+        for copy in copies[-1]:
+            copy.start()
+    decay_copy.wait()
     decay = decay_ref[...]
     causal = jnp.where(causal_mask(length), 1.0, 0.0)
     cum_col = exact_dot(causal, decay, CONTRACT_COLS)
@@ -114,6 +130,9 @@
     block_log = cum_col[length - 1 : length, :]
     shrink = jnp.exp(block_log - cum_col)
     for h in range(heads):
+        if h % plan.own == 0:
+            for copy in copies[h // plan.own]:
+                copy.wait()
         key_decayed = (key_ref[:, lanes(h, size)].astype(F32) * shrink[:, h : h + 1]).astype(BF16)
         held_ref[h * size : (h + 1) * size] = dot(
             key_decayed, value_ref[:, lanes(h, size)], CONTRACT_ROWS
@@ -182,7 +201,7 @@
 def reverse_scan_body(plan, *refs):
     part_refs, refs = refs[: plan.members], refs[plan.members :]
     total_refs, refs = refs[: plan.groups], refs[plan.groups :]
-    (logs_ref, grad_ref), refs = refs[:2], refs[2:]
+    (logs_ref, grad_ref, _), refs = refs[:3], refs[3:]
     send_refs, (all_ref, groups_ref, held_ref) = refs[: plan.members], refs[plan.members :]
     stage_groups(plan, total_refs, groups_ref)
     grad = grad_ref[plan.rows_of(plan.member())]
@@ -305,7 +324,8 @@
 def finish_body(plan, *refs):
     grad_refs, refs = refs[: plan.members], refs[plan.members :]
     key_part_ref, value_part_ref, key_ref, value_ref, cum_col_ref = refs[:5]
-    key_grad_ref, value_grad_ref, grads_ref = refs[5:]
+    key_grad_ref, value_grad_ref, done_ref, grads_ref = refs[5:]
+    done_ref[...] = jnp.zeros_like(done_ref)
     length = key_ref.shape[0]
     gather_rounded(plan, grad_refs, grads_ref)
     cum_col = cum_col_ref[...]
@@ -321,7 +341,7 @@
 
 
 def join_body(plan, *refs):
-    for k, piece_ref in enumerate(refs[:-1]):
+    for k, piece_ref in enumerate(refs[:-2]):
         refs[-1][plan.rows_of(plan.peer(k))] = piece_ref[...]
 
 
@@ -348,8 +368,16 @@
     *sends, cum_log, cum_col = call(
         bind(summary_body),
         [logged] * plan.members + [shaped((heads, length)), shaped((length, heads))],
-        [key_rows, value_rows, log_decay],
-        [hold_whole],
+        [pltpu.with_memory_space_constraint(x, pltpu.HBM) for x in (key_rows, value_rows, log_decay)],
+        [
+            hold_whole,
+            pltpu.VMEM((length, width), BF16),
+            pltpu.VMEM((length, width), BF16),
+            pltpu.VMEM((heads, length), F32),
+            pltpu.SemaphoreType.DMA((plan.members, 2)),
+            pltpu.SemaphoreType.DMA,
+        ],
+        specs=[HBM] * 3,
     )
     parts = plan.swap_in_group(sends)
     weights, intra = call(
@@ -364,7 +392,7 @@
         parts,
         [hold_logged],
     )
-    totals = [total] + plan.from_groups(total, True)
+    totals = [total] + plan.from_groups(total)
     sends = call(
         bind(forward_scan_body),
         pieces,
@@ -395,22 +423,27 @@
         flops=10 * heads * length * length * size,
     )
     (total,) = call(bind(group_grad_body), [logged], [*parts, logs], [hold])
-    totals = [total] + plan.from_groups(total, False)
+    totals = [total] + plan.from_groups(total)
     *sends, whole_total = call(
         bind(reverse_scan_body),
         pieces + [piece],
-        [*parts, *totals, logs, state_out_grad.reshape(width, size)],
+        [*parts, *totals, logs, state_out_grad.reshape(width, size), key_part],
         [hold_groups, hold],
+        specs=[VMEM] * (plan.members + plan.groups + 2) + [ANY],
     )
     grads = plan.swap_in_group(sends)
     totals = plan.swap_in_group([whole_total] * plan.members)
-    key_grad, value_grad = call(
+    key_grad, value_grad, done = call(
         bind(finish_body),
-        [rounded, rounded],
+        [rounded, rounded, shaped((8, size))],
         [*grads, key_part, value_part, key_rows, value_rows, cum_col],
         [pltpu.VMEM((width, size), BF16)],
     )
-    (state_in_grad,) = call(bind(join_body), [shaped((width, size))], totals)
+    (state_in_grad,) = call(
+        bind(join_body),
+        [shaped((width, size))],
+        [*totals, done],
+    )
     return (query_grad, key_grad, value_grad, state_in_grad.reshape(heads, size, size))
 
 

time: 76.5 us -> 74.6 us (0.975)
  starting transfers between devices: 29.9 us -> 25 us
  waiting for transfers between devices: 32 us -> 35.8 us
  local copies, waits for them, and re-layouts: 2.81 us -> 0.03 us
  Pallas kernels: 10.8 us -> 12.9 us
    ppermute x17, starting transfers between devices: 26.8 us -> 21.9 us  [the longest x15 17 us: swap_in_group(): swapped.append(lax.ppermute(piece, 'seq', pairs))]
    ppermute x17, waiting for transfers between devices: 30.7 us -> 34.4 us  [the longest x15 24.1 us: swap_in_group(): swapped.append(lax.ppermute(piece, 'seq', pairs))]
    unnamed x20 -> x14, local copies, waits for them, and re-layouts: 2.81 us -> 0.03 us
    pallas_call x11, Pallas kernels: 10.8 us -> 12.9 us  [call(): pl.pallas_call(body, out_shape=outs, in_specs=specs or [VMEM] * len(opera...]
  transfers between devices with their start and end apart: 20 -> 20, of which waited for: 17 -> 18; matrix products, arithmetic and copies ran while one was open for 0% -> 0% of each run, Pallas kernels for 7% -> 8%
where the time goes in v3:
time: 74.6 us; the launch traced here: 74.5 us
  waiting for transfers between devices  35.8 us (48%)
  starting transfers between devices  25 us (34%)
  Pallas kernels  12.9 us (17%)
    ppermute x15, waiting for transfers between devices, swap_in_group(): swapped.append(lax.ppermute(piece, 'seq', pairs))  24.1 us
    ppermute x15, starting transfers between devices, swap_in_group(): swapped.append(lax.ppermute(piece, 'seq', pairs))  17 us
    pallas_call x11, Pallas kernels, call(): pl.pallas_call(body, out_shape=outs, in_specs=specs or [VMEM] * len(opera...  12.9 us
    ppermute x2, waiting for transfers between devices, from_groups(): lax.ppermute(piece, 'seq', [(i, (i + step * self.members) % self.blocks)...  10.4 us
    ppermute x2, starting transfers between devices, from_groups(): lax.ppermute(piece, 'seq', [(i, (i + step * self.members) % self.blocks)...  4.84 us
    ppermute x3, starting transfers between devices, on_device(): lax.ppermute(sums, 'head', [(i, (i + step) % parties) for i in range(part...  3.11 us
  transfers between devices with their start and end apart: 20, of which 18 were waited for; matrix products, arithmetic and copies ran while one was open for 0% of the time, Pallas kernels for 8%

profile of v3, /device:TPU:0, one launch (start us, length us, event | category | flops | bytes accessed | tf_op | source)
XLA Modules:
  0.0 74.5 jit_solution(12625242200560015038)
XLA Ops:
  0.6 3.3 %shard_map.111 = (f32[264,128]{1,0:T(8,128)S(1)}, f32[264,128]{1,0:T(8,128)S(1)}, f32[264,128]{1,0:T(8,128)S(1)}, f32[264,128]{1,0:T(8,128)S(1)}, f32[8,256]{1,0:T(8,128)S(1)}, /*index=5*/f32[256,8]{1,0:T(8,128)S(1)}) custom-call(bf16[256,1024]{1,0:T(8,128)(2,1)} %refs_6_.1, bf16[256,1024]{1,0:T(8,128)(2,1)} %refs_7_.5, f32[8,256]{1,0:T(8,128)} %decay_hbm.1), custom_call_target="tpu_custom_call" | custom-call | bytes 1613824 | tf_op jit(solution)/shard_map/pallas_call | solution.py:25
  3.9 4.0 %collective-permute-start = (f32[264,128]{1,0:T(8,128)S(1)}, f32[264,128]{1,0:T(8,128)S(1)}, u32[]{:S(2)}, u32[]{:S(2)}) collective-permute-start(f32[264,128]{1,0:T(8,128)S(1)} %get-tuple-element.38), channel_id=1, source_target_pairs={{0,12},{4,8},{8,4},{12,0},{16,28},{20,24},{24,20},{28,16},{1,13},{... | collective-permute-start | bytes 405512 | tf_op jit(solution)/shard_map/ppermute | solution.py:86
  8.0 0.5 collective-permute-start.1
  8.5 0.1 collective-permute-start.2
  8.6 3.4 %collective-permute-done.refs_1_ = f32[264,128]{1,0:T(8,128)S(1)} collective-permute-done((f32[264,128]{1,0:T(8,128)S(1)}, f32[264,128]{1,0:T(8,128)S(1)}, u32[]{:S(2)}, u32[]{:S(2)}) %collective-permute-start) | collective-permute-done | bytes 135200 | tf_op jit(solution)/shard_map/ppermute | solution.py:86
  12.0 2.5 %collective-permute-done.1.refs_2_ = f32[264,128]{1,0:T(8,128)S(1)} collective-permute-done((f32[264,128]{1,0:T(8,128)S(1)}, f32[264,128]{1,0:T(8,128)S(1)}, u32[]{:S(2)}, u32[]{:S(2)}) %collective-permute-start.1) | collective-permute-done | bytes 135200 | tf_op jit(solution)/shard_map/ppermute | solution.py:86
  14.4 0.1 collective-permute-done.2.refs_3_
  14.6 0.1 shard_map.112
  14.7 2.7 %collective-permute-start.3 = (f32[264,128]{1,0:T(8,128)S(1)}, f32[264,128]{1,0:T(8,128)S(1)}, u32[]{:S(2)}, u32[]{:S(2)}) collective-permute-start(f32[264,128]{1,0:T(8,128)S(1)} %get-tuple-element.41.refs_4_), channel_id=1, source_target_pairs={{0,16},{4,20},{8,24},{12,28},{16,0},{20,4},{24,8},{28,12},{1,17},{... | collective-permute-start | bytes 405512 | tf_op jit(solution)/shard_map/ppermute | solution.py:91
  17.3 6.6 %collective-permute-done.3.refs_5_ = f32[264,128]{1,0:T(8,128)S(1)} collective-permute-done((f32[264,128]{1,0:T(8,128)S(1)}, f32[264,128]{1,0:T(8,128)S(1)}, u32[]{:S(2)}, u32[]{:S(2)}) %collective-permute-start.3) | collective-permute-done | bytes 135200 | tf_op jit(solution)/shard_map/ppermute | solution.py:91
  24.0 0.2 shard_map.113
  24.2 0.3 collective-permute-start.4
  24.4 2.0 %collective-permute-start.5 = (f32[256,128]{1,0:T(8,128)S(1)}, f32[256,128]{1,0:T(8,128)S(1)}, u32[]{:S(2)}, u32[]{:S(2)}) collective-permute-start(f32[256,128]{1,0:T(8,128)S(1)} %get-tuple-element.44), channel_id=1, source_target_pairs={{0,4},{4,0},{8,12},{12,8},{16,20},{20,16},{24,28},{28,24},{1,5},{5... | collective-permute-start | bytes 393224 | tf_op jit(solution)/shard_map/ppermute | solution.py:86
  26.5 1.3 %collective-permute-start.6 = (f32[256,128]{1,0:T(8,128)S(1)}, f32[256,128]{1,0:T(8,128)S(1)}, u32[]{:S(2)}, u32[]{:S(2)}) collective-permute-start(f32[256,128]{1,0:T(8,128)S(1)} %get-tuple-element.45), channel_id=1, source_target_pairs={{0,8},{4,12},{8,0},{12,4},{16,24},{20,28},{24,16},{28,20},{1,9},{5... | collective-permute-start | bytes 393224 | tf_op jit(solution)/shard_map/ppermute | solution.py:86
  27.7 0.9 %shard_map.114 = (bf16[8,256,256]{2,1,0:T(8,128)(2,1)S(1)}, f32[256,1024]{1,0:T(8,128)S(1)}) custom-call(bf16[256,1024]{1,0:T(8,128)(2,1)S(1)} %copy-done, bf16[256,1024]{1,0:T(8,128)(2,1)S(1)} %copy-done.1, bf16[256,1024]{1,0:T(8,128)(2,1)S(1)} %copy-done.2, f32[8,256]{1,0:T(8,128)S(1)} %get-tuple-element.46.cum_ref, ...), custom_call_target="tpu_custom_call" | custom-call | flops 268435456 | bytes 3686400 | tf_op jit(solution)/shard_map/pallas_call | solution.py:25
  28.7 2.5 %collective-permute-done.4.refs_1_ = f32[256,128]{1,0:T(8,128)S(1)} collective-permute-done((f32[256,128]{1,0:T(8,128)S(1)}, f32[256,128]{1,0:T(8,128)S(1)}, u32[]{:S(2)}, u32[]{:S(2)}) %collective-permute-start.4) | collective-permute-done | bytes 131104 | tf_op jit(solution)/shard_map/ppermute | solution.py:86
  31.2 1.2 %collective-permute-done.5.refs_2_ = f32[256,128]{1,0:T(8,128)S(1)} collective-permute-done((f32[256,128]{1,0:T(8,128)S(1)}, f32[256,128]{1,0:T(8,128)S(1)}, u32[]{:S(2)}, u32[]{:S(2)}) %collective-permute-start.5) | collective-permute-done | bytes 131104 | tf_op jit(solution)/shard_map/ppermute | solution.py:86
  32.4 0.4 collective-permute-done.6.refs_3_
  32.8 0.8 %shard_map.115 = (f32[256,1024]{1,0:T(8,128)S(1)}, f32[8,256]{1,0:T(8,128)S(1)}, bf16[1024,128]{1,0:T(8,128)(2,1)S(1)}) custom-call(f32[256,128]{1,0:T(8,128)S(1)} %get-tuple-element.42.refs_0_, f32[256,128]{1,0:T(8,128)S(1)} %collective-permute-done.4.refs_1_, f32[256,128]{1,0:T(8,128)S(1)} %collective-permute-done.5.refs_2_, ...), custom_call_target="tpu_custom_call" | custom-call | bytes 3952640 | tf_op jit(solution)/shard_map/pallas_call | solution.py:25
  33.6 1.7 %collective-permute-start.8 = (f32[8,256]{1,0:T(8,128)S(1)}, f32[8,256]{1,0:T(8,128)S(1)}, u32[]{:S(2)}, u32[]{:S(2)}) collective-permute-start(f32[8,256]{1,0:T(8,128)S(1)} %get-tuple-element.49.refs_0_), channel_id=1, source_target_pairs={{0,2},{1,3},{2,0},{3,1},{4,6},{5,7},{6,4},{7,5},{8,10},{9,11},{10,... | collective-permute-start | bytes 24584 | tf_op jit(solution)/shard_map/ppermute | solution.py:409
  35.3 1.4 %collective-permute-start.9 = (f32[8,256]{1,0:T(8,128)S(1)}, f32[8,256]{1,0:T(8,128)S(1)}, u32[]{:S(2)}, u32[]{:S(2)}) collective-permute-start(f32[8,256]{1,0:T(8,128)S(1)} %get-tuple-element.49.refs_0_), channel_id=1, source_target_pairs={{0,3},{1,0},{2,1},{3,2},{4,7},{5,4},{6,5},{7,6},{8,11},{9,8},{10,9... | collective-permute-start | bytes 24584 | tf_op jit(solution)/shard_map/ppermute | solution.py:409
  36.7 0.6 collective-permute-done.8.refs_2_
  37.3 0.8 %collective-permute-done.9.refs_3_ = f32[8,256]{1,0:T(8,128)S(1)} collective-permute-done((f32[8,256]{1,0:T(8,128)S(1)}, f32[8,256]{1,0:T(8,128)S(1)}, u32[]{:S(2)}, u32[]{:S(2)}) %collective-permute-start.9) | collective-permute-done | bytes 8224 | tf_op jit(solution)/shard_map/ppermute | solution.py:409
  38.1 1.4 %shard_map.116 = (bf16[256,1024]{1,0:T(8,128)(2,1)S(1)}, f32[256,128]{1,0:T(8,128)S(1)}, f32[256,128]{1,0:T(8,128)S(1)}, f32[256,128]{1,0:T(8,128)S(1)}, f32[256,128]{1,0:T(8,128)S(1)}) custom-call(f32[8,256]{1,0:T(8,128)S(1)} %get-tuple-element.49.refs_0_, f32[8,256]{1,0:T(8,128)S(1)} %collective-permute-done.7.refs_1_, ...), custom_call_target="tpu_custom_call" | custom-call | bytes 3190784 | tf_op jit(solution)/shard_map/pallas_call | solution.py:25
  39.5 1.3 %collective-permute-start.10 = (f32[256,128]{1,0:T(8,128)S(1)}, f32[256,128]{1,0:T(8,128)S(1)}, u32[]{:S(2)}, u32[]{:S(2)}) collective-permute-start(f32[256,128]{1,0:T(8,128)S(1)} %get-tuple-element.56), channel_id=1, source_target_pairs={{0,12},{4,8},{8,4},{12,0},{16,28},{20,24},{24,20},{28,16},{1,13},{... | collective-permute-start | bytes 393224 | tf_op jit(solution)/shard_map/ppermute | solution.py:86
  40.8 1.5 %collective-permute-start.11 = (f32[256,128]{1,0:T(8,128)S(1)}, f32[256,128]{1,0:T(8,128)S(1)}, u32[]{:S(2)}, u32[]{:S(2)}) collective-permute-start(f32[256,128]{1,0:T(8,128)S(1)} %get-tuple-element.57), channel_id=1, source_target_pairs={{0,4},{4,0},{8,12},{12,8},{16,20},{20,16},{24,28},{28,24},{1,5},{5... | collective-permute-start | bytes 393224 | tf_op jit(solution)/shard_map/ppermute | solution.py:86
  42.3 0.8 %collective-permute-start.12 = (f32[256,128]{1,0:T(8,128)S(1)}, f32[256,128]{1,0:T(8,128)S(1)}, u32[]{:S(2)}, u32[]{:S(2)}) collective-permute-start(f32[256,128]{1,0:T(8,128)S(1)} %get-tuple-element.58), channel_id=1, source_target_pairs={{0,8},{4,12},{8,0},{12,4},{16,24},{20,28},{24,16},{28,20},{1,9},{5... | collective-permute-start | bytes 393224 | tf_op jit(solution)/shard_map/ppermute | solution.py:86
  43.1 3.7 %collective-permute-done.10.refs_1_ = f32[256,128]{1,0:T(8,128)S(1)} collective-permute-done((f32[256,128]{1,0:T(8,128)S(1)}, f32[256,128]{1,0:T(8,128)S(1)}, u32[]{:S(2)}, u32[]{:S(2)}) %collective-permute-start.10) | collective-permute-done | bytes 131104 | tf_op jit(solution)/shard_map/ppermute | solution.py:86
  46.8 2.4 %collective-permute-done.11.refs_2_ = f32[256,128]{1,0:T(8,128)S(1)} collective-permute-done((f32[256,128]{1,0:T(8,128)S(1)}, f32[256,128]{1,0:T(8,128)S(1)}, u32[]{:S(2)}, u32[]{:S(2)}) %collective-permute-start.11) | collective-permute-done | bytes 131104 | tf_op jit(solution)/shard_map/ppermute | solution.py:86
  49.2 0.0 collective-permute-done.12.refs_3_
  49.2 0.1 shard_map.118.refs_4_
  49.3 2.2 %collective-permute-start.13 = (f32[264,128]{1,0:T(8,128)S(1)}, f32[264,128]{1,0:T(8,128)S(1)}, u32[]{:S(2)}, u32[]{:S(2)}) collective-permute-start(f32[264,128]{1,0:T(8,128)S(1)} %shard_map.118.refs_4_), channel_id=1, source_target_pairs={{0,16},{4,20},{8,24},{12,28},{16,0},{20,4},{24,8},{28,12},{1,17},{... | collective-permute-start | bytes 405512 | tf_op jit(solution)/shard_map/ppermute | solution.py:91
  51.5 3.5 %shard_map.117 = (bf16[256,1024]{1,0:T(8,128)(2,1)}, f32[256,1024]{1,0:T(8,128)S(1)}, f32[256,1024]{1,0:T(8,128)S(1)}) custom-call(bf16[256,1024]{1,0:T(8,128)(2,1)S(1)} %get-tuple-element.51.attn_grad_ref, bf16[256,1024]{1,0:T(8,128)(2,1)S(1)} %copy-done, bf16[256,1024]{1,0:T(8,128)(2,1)S(1)} %copy-done.1, bf16[256,1024]{1,0:T(8,128)(2,1)S(1)} %copy-done.2, ...), custom_call_target="tpu_custom_call" | custom-call | flops 671088640 | bytes 6045696 | tf_op jit(solution)/shard_map/pallas_call | solution.py:25
  55.0 3.7 %collective-permute-done.13.refs_5_ = f32[264,128]{1,0:T(8,128)S(1)} collective-permute-done((f32[264,128]{1,0:T(8,128)S(1)}, f32[264,128]{1,0:T(8,128)S(1)}, u32[]{:S(2)}, u32[]{:S(2)}) %collective-permute-start.13) | collective-permute-done | bytes 135200 | tf_op jit(solution)/shard_map/ppermute | solution.py:91
  58.7 0.2 shard_map.119
  58.9 0.4 collective-permute-start.14
  59.3 1.4 %collective-permute-start.15 = (f32[256,128]{1,0:T(8,128)S(1)}, f32[256,128]{1,0:T(8,128)S(1)}, u32[]{:S(2)}, u32[]{:S(2)}) collective-permute-start(f32[256,128]{1,0:T(8,128)S(1)} %get-tuple-element.63), channel_id=1, source_target_pairs={{0,4},{4,0},{8,12},{12,8},{16,20},{20,16},{24,28},{28,24},{1,5},{5... | collective-permute-start | bytes 393224 | tf_op jit(solution)/shard_map/ppermute | solution.py:86
  60.6 1.8 %collective-permute-start.16 = (f32[256,128]{1,0:T(8,128)S(1)}, f32[256,128]{1,0:T(8,128)S(1)}, u32[]{:S(2)}, u32[]{:S(2)}) collective-permute-start(f32[256,128]{1,0:T(8,128)S(1)} %get-tuple-element.64), channel_id=1, source_target_pairs={{0,8},{4,12},{8,0},{12,4},{16,24},{20,28},{24,16},{28,20},{1,9},{5... | collective-permute-start | bytes 393224 | tf_op jit(solution)/shard_map/ppermute | solution.py:86
  62.4 0.8 %collective-permute-start.17 = (f32[256,128]{1,0:T(8,128)S(1)}, f32[256,128]{1,0:T(8,128)S(1)}, u32[]{:S(2)}, u32[]{:S(2)}) collective-permute-start(f32[256,128]{1,0:T(8,128)S(1)} %get-tuple-element.68.refs_0_), channel_id=1, source_target_pairs={{0,12},{4,8},{8,4},{12,0},{16,28},{20,24},{24,20},{28,16},{1,13},{... | collective-permute-start | bytes 393224 | tf_op jit(solution)/shard_map/ppermute | solution.py:86
  63.2 0.9 %collective-permute-start.18 = (f32[256,128]{1,0:T(8,128)S(1)}, f32[256,128]{1,0:T(8,128)S(1)}, u32[]{:S(2)}, u32[]{:S(2)}) collective-permute-start(f32[256,128]{1,0:T(8,128)S(1)} %get-tuple-element.68.refs_0_), channel_id=1, source_target_pairs={{0,4},{4,0},{8,12},{12,8},{16,20},{20,16},{24,28},{28,24},{1,5},{5... | collective-permute-start | bytes 393224 | tf_op jit(solution)/shard_map/ppermute | solution.py:86
  64.1 2.0 %collective-permute-done.14.refs_1_ = f32[256,128]{1,0:T(8,128)S(1)} collective-permute-done((f32[256,128]{1,0:T(8,128)S(1)}, f32[256,128]{1,0:T(8,128)S(1)}, u32[]{:S(2)}, u32[]{:S(2)}) %collective-permute-start.14) | collective-permute-done | bytes 131104 | tf_op jit(solution)/shard_map/ppermute | solution.py:86
  66.1 2.5 %collective-permute-done.15.refs_2_ = f32[256,128]{1,0:T(8,128)S(1)} collective-permute-done((f32[256,128]{1,0:T(8,128)S(1)}, f32[256,128]{1,0:T(8,128)S(1)}, u32[]{:S(2)}, u32[]{:S(2)}) %collective-permute-start.15) | collective-permute-done | bytes 131104 | tf_op jit(solution)/shard_map/ppermute | solution.py:86
  68.6 0.3 collective-permute-done.16.refs_3_
  68.9 1.6 %shard_map.120 = (bf16[256,1024]{1,0:T(8,128)(2,1)}, bf16[256,1024]{1,0:T(8,128)(2,1)}, f32[8,128]{1,0:T(8,128)S(1)}) custom-call(f32[256,128]{1,0:T(8,128)S(1)} %get-tuple-element.61.refs_0_, f32[256,128]{1,0:T(8,128)S(1)} %collective-permute-done.14.refs_1_, f32[256,128]{1,0:T(8,128)S(1)} %collective-permute-done.15.refs_2_, ...), custom_call_target="tpu_custom_call" | custom-call | bytes 4730880 | tf_op jit(solution)/shard_map/pallas_call | solution.py:25
  70.5 1.2 %collective-permute-done.17.refs_1_ = f32[256,128]{1,0:T(8,128)S(1)} collective-permute-done((f32[256,128]{1,0:T(8,128)S(1)}, f32[256,128]{1,0:T(8,128)S(1)}, u32[]{:S(2)}, u32[]{:S(2)}) %collective-permute-start.17) | collective-permute-done | bytes 131104 | tf_op jit(solution)/shard_map/ppermute | solution.py:86
  71.7 0.7 collective-permute-done.18.refs_2_
  72.5 1.2 %collective-permute-done.19.refs_3_ = f32[256,128]{1,0:T(8,128)S(1)} collective-permute-done((f32[256,128]{1,0:T(8,128)S(1)}, f32[256,128]{1,0:T(8,128)S(1)}, u32[]{:S(2)}, u32[]{:S(2)}) %collective-permute-start.19) | collective-permute-done | bytes 131104 | tf_op jit(solution)/shard_map/ppermute | solution.py:86
  73.6 0.8 %shard_map.121 = f32[1024,128]{1,0:T(8,128)} custom-call(f32[256,128]{1,0:T(8,128)S(1)} %get-tuple-element.68.refs_0_, f32[256,128]{1,0:T(8,128)S(1)} %collective-permute-done.17.refs_1_, f32[256,128]{1,0:T(8,128)S(1)} %collective-permute-done.18.refs_2_, f32[256,128]{1,0:T(8,128)S(1)} %collective-permute-done.19.refs_3_, f32[8,128]{1,0:T(8,128)S(1)} %get-tuple-element.69.refs_4_), custom_call_target="tpu_custom_call" | custom-call | bytes 1052672 | tf_op jit(solution)/shard_map/pallas_call | solution.py:25
  (17 shorter events, 0.0 us)
Async XLA Ops:
  0.6 23.4 %copy-start.4 = (f32[8,128,128]{2,1,0:T(8,128)S(1)}, f32[8,128,128]{2,1,0:T(8,128)}, u32[]{:S(2)}) copy-start(f32[8,128,128]{2,1,0:T(8,128)} %param.14) | copy-start | bytes 1572868
  3.9 8.0 %collective-permute-start = (f32[264,128]{1,0:T(8,128)S(1)}, f32[264,128]{1,0:T(8,128)S(1)}, u32[]{:S(2)}, u32[]{:S(2)}) collective-permute-start(f32[264,128]{1,0:T(8,128)S(1)} %get-tuple-element.38), channel_id=1, source_target_pairs={{0,12},{4,8},{8,4},{12,0},{16,28},{20,24},{24,20},{28,16},{1,13},{... | collective-permute-start | bytes 405512 | tf_op jit(solution)/shard_map/ppermute | solution.py:86
  8.0 6.5 %collective-permute-start.1 = (f32[264,128]{1,0:T(8,128)S(1)}, f32[264,128]{1,0:T(8,128)S(1)}, u32[]{:S(2)}, u32[]{:S(2)}) collective-permute-start(f32[264,128]{1,0:T(8,128)S(1)} %get-tuple-element.39), channel_id=1, source_target_pairs={{0,4},{4,0},{8,12},{12,8},{16,20},{20,16},{24,28},{28,24},{1,5},{5... | collective-permute-start | bytes 405512 | tf_op jit(solution)/shard_map/ppermute | solution.py:86
  8.5 6.1 %collective-permute-start.2 = (f32[264,128]{1,0:T(8,128)S(1)}, f32[264,128]{1,0:T(8,128)S(1)}, u32[]{:S(2)}, u32[]{:S(2)}) collective-permute-start(f32[264,128]{1,0:T(8,128)S(1)} %get-tuple-element.40), channel_id=1, source_target_pairs={{0,8},{4,12},{8,0},{12,4},{16,24},{20,28},{24,16},{28,20},{1,9},{5... | collective-permute-start | bytes 405512 | tf_op jit(solution)/shard_map/ppermute | solution.py:86
  14.6 13.2 %copy-start.2 = (bf16[256,1024]{1,0:T(8,128)(2,1)S(1)}, bf16[256,1024]{1,0:T(8,128)(2,1)}, u32[]{:S(2)}) copy-start(bf16[256,1024]{1,0:T(8,128)(2,1)} %refs_7_.5) | copy-start | bytes 1572868
  14.7 9.3 %collective-permute-start.3 = (f32[264,128]{1,0:T(8,128)S(1)}, f32[264,128]{1,0:T(8,128)S(1)}, u32[]{:S(2)}, u32[]{:S(2)}) collective-permute-start(f32[264,128]{1,0:T(8,128)S(1)} %get-tuple-element.41.refs_4_), channel_id=1, source_target_pairs={{0,16},{4,20},{8,24},{12,28},{16,0},{20,4},{24,8},{28,12},{1,17},{... | collective-permute-start | bytes 405512 | tf_op jit(solution)/shard_map/ppermute | solution.py:91
  24.0 3.8 %copy-start = (bf16[256,1024]{1,0:T(8,128)(2,1)S(1)}, bf16[256,1024]{1,0:T(8,128)(2,1)}, u32[]{:S(2)}) copy-start(bf16[256,1024]{1,0:T(8,128)(2,1)} %query_ref.3) | copy-start | bytes 1572868
  24.0 3.8 %copy-start.1 = (bf16[256,1024]{1,0:T(8,128)(2,1)S(1)}, bf16[256,1024]{1,0:T(8,128)(2,1)}, u32[]{:S(2)}) copy-start(bf16[256,1024]{1,0:T(8,128)(2,1)} %refs_6_.1) | copy-start | bytes 1572868
  24.2 7.0 %collective-permute-start.4 = (f32[256,128]{1,0:T(8,128)S(1)}, f32[256,128]{1,0:T(8,128)S(1)}, u32[]{:S(2)}, u32[]{:S(2)}) collective-permute-start(f32[256,128]{1,0:T(8,128)S(1)} %get-tuple-element.43), channel_id=1, source_target_pairs={{0,12},{4,8},{8,4},{12,0},{16,28},{20,24},{24,20},{28,16},{1,13},{... | collective-permute-start | bytes 393224 | tf_op jit(solution)/shard_map/ppermute | solution.py:86
  24.4 8.0 %collective-permute-start.5 = (f32[256,128]{1,0:T(8,128)S(1)}, f32[256,128]{1,0:T(8,128)S(1)}, u32[]{:S(2)}, u32[]{:S(2)}) collective-permute-start(f32[256,128]{1,0:T(8,128)S(1)} %get-tuple-element.44), channel_id=1, source_target_pairs={{0,4},{4,0},{8,12},{12,8},{16,20},{20,16},{24,28},{28,24},{1,5},{5... | collective-permute-start | bytes 393224 | tf_op jit(solution)/shard_map/ppermute | solution.py:86
  26.5 6.3 %collective-permute-start.6 = (f32[256,128]{1,0:T(8,128)S(1)}, f32[256,128]{1,0:T(8,128)S(1)}, u32[]{:S(2)}, u32[]{:S(2)}) collective-permute-start(f32[256,128]{1,0:T(8,128)S(1)} %get-tuple-element.45), channel_id=1, source_target_pairs={{0,8},{4,12},{8,0},{12,4},{16,24},{20,28},{24,16},{28,20},{1,9},{5... | collective-permute-start | bytes 393224 | tf_op jit(solution)/shard_map/ppermute | solution.py:86
  27.7 5.1 %copy-start.3 = (bf16[256,1024]{1,0:T(8,128)(2,1)S(1)}, bf16[256,1024]{1,0:T(8,128)(2,1)}, u32[]{:S(2)}) copy-start(bf16[256,1024]{1,0:T(8,128)(2,1)} %refs_7_.4) | copy-start | bytes 1572868
  28.7 4.1 %copy-start.6 = (f32[1024]{0:T(1024)S(1)}, f32[1024]{0:T(1024)}, u32[]{:S(2)}) copy-start(f32[1024]{0:T(1024)} %param.13) | copy-start | bytes 12292
  33.6 3.1 %collective-permute-start.7 = (f32[8,256]{1,0:T(8,128)S(1)}, f32[8,256]{1,0:T(8,128)S(1)}, u32[]{:S(2)}, u32[]{:S(2)}) collective-permute-start(f32[8,256]{1,0:T(8,128)S(1)} %get-tuple-element.49.refs_0_), channel_id=1, source_target_pairs={{0,1},{1,2},{2,3},{3,0},{4,5},{5,6},{6,7},{7,4},{8,9},{9,10},{10,1... | collective-permute-start | bytes 24584 | tf_op jit(solution)/shard_map/ppermute | solution.py:409
  33.6 3.7 %collective-permute-start.8 = (f32[8,256]{1,0:T(8,128)S(1)}, f32[8,256]{1,0:T(8,128)S(1)}, u32[]{:S(2)}, u32[]{:S(2)}) collective-permute-start(f32[8,256]{1,0:T(8,128)S(1)} %get-tuple-element.49.refs_0_), channel_id=1, source_target_pairs={{0,2},{1,3},{2,0},{3,1},{4,6},{5,7},{6,4},{7,5},{8,10},{9,11},{10,... | collective-permute-start | bytes 24584 | tf_op jit(solution)/shard_map/ppermute | solution.py:409
  35.3 2.8 %collective-permute-start.9 = (f32[8,256]{1,0:T(8,128)S(1)}, f32[8,256]{1,0:T(8,128)S(1)}, u32[]{:S(2)}, u32[]{:S(2)}) collective-permute-start(f32[8,256]{1,0:T(8,128)S(1)} %get-tuple-element.49.refs_0_), channel_id=1, source_target_pairs={{0,3},{1,0},{2,1},{3,2},{4,7},{5,4},{6,5},{7,6},{8,11},{9,8},{10,9... | collective-permute-start | bytes 24584 | tf_op jit(solution)/shard_map/ppermute | solution.py:409
  39.5 7.3 %collective-permute-start.10 = (f32[256,128]{1,0:T(8,128)S(1)}, f32[256,128]{1,0:T(8,128)S(1)}, u32[]{:S(2)}, u32[]{:S(2)}) collective-permute-start(f32[256,128]{1,0:T(8,128)S(1)} %get-tuple-element.56), channel_id=1, source_target_pairs={{0,12},{4,8},{8,4},{12,0},{16,28},{20,24},{24,20},{28,16},{1,13},{... | collective-permute-start | bytes 393224 | tf_op jit(solution)/shard_map/ppermute | solution.py:86
  40.8 8.4 %collective-permute-start.11 = (f32[256,128]{1,0:T(8,128)S(1)}, f32[256,128]{1,0:T(8,128)S(1)}, u32[]{:S(2)}, u32[]{:S(2)}) collective-permute-start(f32[256,128]{1,0:T(8,128)S(1)} %get-tuple-element.57), channel_id=1, source_target_pairs={{0,4},{4,0},{8,12},{12,8},{16,20},{20,16},{24,28},{28,24},{1,5},{5... | collective-permute-start | bytes 393224 | tf_op jit(solution)/shard_map/ppermute | solution.py:86
  42.3 6.9 %collective-permute-start.12 = (f32[256,128]{1,0:T(8,128)S(1)}, f32[256,128]{1,0:T(8,128)S(1)}, u32[]{:S(2)}, u32[]{:S(2)}) collective-permute-start(f32[256,128]{1,0:T(8,128)S(1)} %get-tuple-element.58), channel_id=1, source_target_pairs={{0,8},{4,12},{8,0},{12,4},{16,24},{20,28},{24,16},{28,20},{1,9},{5... | collective-permute-start | bytes 393224 | tf_op jit(solution)/shard_map/ppermute | solution.py:86
  49.3 9.4 %collective-permute-start.13 = (f32[264,128]{1,0:T(8,128)S(1)}, f32[264,128]{1,0:T(8,128)S(1)}, u32[]{:S(2)}, u32[]{:S(2)}) collective-permute-start(f32[264,128]{1,0:T(8,128)S(1)} %shard_map.118.refs_4_), channel_id=1, source_target_pairs={{0,16},{4,20},{8,24},{12,28},{16,0},{20,4},{24,8},{28,12},{1,17},{... | collective-permute-start | bytes 405512 | tf_op jit(solution)/shard_map/ppermute | solution.py:91
  51.5 7.2 %copy-start.5 = (f32[8,128,128]{2,1,0:T(8,128)S(1)}, f32[8,128,128]{2,1,0:T(8,128)}, u32[]{:S(2)}) copy-start(f32[8,128,128]{2,1,0:T(8,128)} %param.15) | copy-start | bytes 1572868
  58.9 7.2 %collective-permute-start.14 = (f32[256,128]{1,0:T(8,128)S(1)}, f32[256,128]{1,0:T(8,128)S(1)}, u32[]{:S(2)}, u32[]{:S(2)}) collective-permute-start(f32[256,128]{1,0:T(8,128)S(1)} %get-tuple-element.62), channel_id=1, source_target_pairs={{0,12},{4,8},{8,4},{12,0},{16,28},{20,24},{24,20},{28,16},{1,13},{... | collective-permute-start | bytes 393224 | tf_op jit(solution)/shard_map/ppermute | solution.py:86
  59.3 9.4 %collective-permute-start.15 = (f32[256,128]{1,0:T(8,128)S(1)}, f32[256,128]{1,0:T(8,128)S(1)}, u32[]{:S(2)}, u32[]{:S(2)}) collective-permute-start(f32[256,128]{1,0:T(8,128)S(1)} %get-tuple-element.63), channel_id=1, source_target_pairs={{0,4},{4,0},{8,12},{12,8},{16,20},{20,16},{24,28},{28,24},{1,5},{5... | collective-permute-start | bytes 393224 | tf_op jit(solution)/shard_map/ppermute | solution.py:86
  60.6 8.3 %collective-permute-start.16 = (f32[256,128]{1,0:T(8,128)S(1)}, f32[256,128]{1,0:T(8,128)S(1)}, u32[]{:S(2)}, u32[]{:S(2)}) collective-permute-start(f32[256,128]{1,0:T(8,128)S(1)} %get-tuple-element.64), channel_id=1, source_target_pairs={{0,8},{4,12},{8,0},{12,4},{16,24},{20,28},{24,16},{28,20},{1,9},{5... | collective-permute-start | bytes 393224 | tf_op jit(solution)/shard_map/ppermute | solution.py:86
  62.4 9.3 %collective-permute-start.17 = (f32[256,128]{1,0:T(8,128)S(1)}, f32[256,128]{1,0:T(8,128)S(1)}, u32[]{:S(2)}, u32[]{:S(2)}) collective-permute-start(f32[256,128]{1,0:T(8,128)S(1)} %get-tuple-element.68.refs_0_), channel_id=1, source_target_pairs={{0,12},{4,8},{8,4},{12,0},{16,28},{20,24},{24,20},{28,16},{1,13},{... | collective-permute-start | bytes 393224 | tf_op jit(solution)/shard_map/ppermute | solution.py:86
  63.2 9.3 %collective-permute-start.18 = (f32[256,128]{1,0:T(8,128)S(1)}, f32[256,128]{1,0:T(8,128)S(1)}, u32[]{:S(2)}, u32[]{:S(2)}) collective-permute-start(f32[256,128]{1,0:T(8,128)S(1)} %get-tuple-element.68.refs_0_), channel_id=1, source_target_pairs={{0,4},{4,0},{8,12},{12,8},{16,20},{20,16},{24,28},{28,24},{1,5},{5... | collective-permute-start | bytes 393224 | tf_op jit(solution)/shard_map/ppermute | solution.py:86
  66.1 7.5 %collective-permute-start.19 = (f32[256,128]{1,0:T(8,128)S(1)}, f32[256,128]{1,0:T(8,128)S(1)}, u32[]{:S(2)}, u32[]{:S(2)}) collective-permute-start(f32[256,128]{1,0:T(8,128)S(1)} %get-tuple-element.68.refs_0_), channel_id=1, source_target_pairs={{0,8},{4,12},{8,0},{12,4},{16,24},{20,28},{24,16},{28,20},{1,9},{5... | collective-permute-start | bytes 393224 | tf_op jit(solution)/shard_map/ppermute | solution.py:86

commit v4 on v3

--- a/solution.py
+++ b/solution.py
@@ -168,12 +168,14 @@
     part_refs, refs = refs[: plan.members], refs[plan.members :]
     total_refs, refs = refs[: plan.groups], refs[plan.groups :]
     state_ref, refs = refs[0], refs[1:]
-    send_refs, (groups_ref, held_ref) = refs[: plan.members], refs[plan.members :]
+    send_refs, (before_ref, groups_ref, held_ref) = refs[: plan.members], refs[plan.members :]
     stage_groups(plan, total_refs, groups_ref)
+    before = jnp.zeros((LOG_ROWS, plan.size), F32)
     state = state_ref[plan.rows_of(plan.member())]
     for group in range(plan.groups - 1):
         after = own_decays(plan, groups_ref.at[group], plan.rows) * state + groups_ref[group, : plan.rows]
         state = jnp.where(group < plan.group(), after, state)
+        before += jnp.where(group < plan.group(), groups_ref[group, plan.rows :], 0.0)
     for k, part_ref in enumerate(part_refs):
         held_ref[plan.peer(k)] = part_ref[...]
     for b in range(plan.members):
@@ -181,44 +183,80 @@
         decays = own_decays(plan, held_ref.at[b], plan.rows)
         held_ref[b, : plan.rows] = state
         state = decays * state + summary
+        before += jnp.where(b < plan.member(), held_ref[b, plan.rows :], 0.0)
+    before_ref[...] = before
     for k, send_ref in enumerate(send_refs):
         send_ref[...] = held_ref[plan.peer(k), : plan.rows]
 
 
+def suffixes(plan, held_ref, logs_ref, grad):
+    found = []
+    for b in reversed(range(plan.members)):
+        found.append(grad)
+        grad = own_decays(plan, logs_ref.at[b], 0) * grad + held_ref[b]
+    return found[::-1], grad
+
+
+def prefixes(plan, held_ref, logs_ref, total, scale):
+    found = []
+    for b in range(plan.members):
+        found.append(total)
+        total = total + scale * held_ref[b]
+        scale = scale * own_decays(plan, logs_ref.at[b], 0)
+    return found
+
+
 def group_grad_body(plan, *refs):
-    part_refs, (logs_ref, total_ref, held_ref) = refs[: plan.members], refs[plan.members :]
+    part_refs, refs = refs[: plan.members], refs[plan.members :]
+    (logs_ref, grad_ref, _, total_ref), refs = refs[:4], refs[4:]
+    send_refs, (held_ref,) = refs[:-1], refs[-1:]
     for k, part_ref in enumerate(part_refs):
         held_ref[plan.peer(k)] = part_ref[...]
-    total = jnp.zeros((plan.rows, plan.size), F32)
-    log_total = jnp.zeros((LOG_ROWS, plan.size), F32)
-    for b in reversed(range(plan.members)):
-        total = own_decays(plan, logs_ref.at[b], 0) * total + held_ref[b]
-        log_total += logs_ref[b]
-    total_ref[: plan.rows] = total
-    total_ref[plan.rows :] = log_total
+    zero = jnp.zeros((plan.rows, plan.size), F32)
+    total_ref[: plan.rows] = suffixes(plan, held_ref, logs_ref, zero)[1]
+    total_ref[plan.rows :] = sum(logs_ref[b] for b in range(plan.members))
+    if send_refs:
+        first = plan.group() == 0
+        before = prefixes(plan, held_ref, logs_ref, zero, zero + 1.0)
+        after = suffixes(plan, held_ref, logs_ref, grad_ref[plan.rows_of(plan.member())])[0]
+        for b in range(plan.members):
+            held_ref[b] = jnp.where(first, before[b], after[b])
+        for k, send_ref in enumerate(send_refs):
+            send_ref[...] = held_ref[plan.peer(k)]
 
 
 def reverse_scan_body(plan, *refs):
     part_refs, refs = refs[: plan.members], refs[plan.members :]
     total_refs, refs = refs[: plan.groups], refs[plan.groups :]
-    (logs_ref, grad_ref, _), refs = refs[:3], refs[3:]
-    send_refs, (all_ref, groups_ref, held_ref) = refs[: plan.members], refs[plan.members :]
+    (logs_ref, grad_ref), refs = refs[:2], refs[2:]
+    send_refs, (groups_ref, held_ref) = refs[:-2], refs[-2:]
     stage_groups(plan, total_refs, groups_ref)
+    for k, part_ref in enumerate(part_refs):
+        held_ref[plan.peer(k)] = part_ref[...]
     grad = grad_ref[plan.rows_of(plan.member())]
     leaving = grad
     for group in reversed(range(plan.groups)):
         leaving = jnp.where(group == plan.group(), grad, leaving)
         grad = own_decays(plan, groups_ref.at[group], plan.rows) * grad + groups_ref[group, : plan.rows]
-    all_ref[...] = grad
-    for k, part_ref in enumerate(part_refs):
-        held_ref[plan.peer(k)] = part_ref[...]
-    grad = leaving
-    for b in reversed(range(plan.members)):
-        summary = held_ref[b]
-        held_ref[b] = grad
-        grad = own_decays(plan, logs_ref.at[b], 0) * grad + summary
-    for k, send_ref in enumerate(send_refs):
-        send_ref[...] = held_ref[plan.peer(k)]
+    total = jnp.zeros((plan.rows, plan.size), F32)
+    scale = total + 1.0
+    for group in range(plan.groups - 1):
+        earlier = group < plan.group()
+        total = jnp.where(earlier, total + scale * groups_ref[group, : plan.rows], total)
+        decays = own_decays(plan, groups_ref.at[group], plan.rows)
+        scale = jnp.where(earlier, scale * decays, scale)
+    after = suffixes(plan, held_ref, logs_ref, leaving)[0]
+    before = prefixes(plan, held_ref, logs_ref, total, scale)
+    if plan.groups == 2:
+        first = plan.group() == 0
+        found = [[jnp.where(first, after[b], before[b]) for b in range(plan.members)]]
+    else:
+        found = [before, after]
+    for i, values in enumerate(found):
+        for b in range(plan.members):
+            held_ref[b] = values[b]
+        for k in range(plan.members):
+            send_refs[i * plan.members + k][...] = held_ref[plan.peer(k)]
 
 
 def decay_matrix(cum_ref, cum_col, causal, h):
@@ -269,8 +307,7 @@
 def attn_grad_body(plan, parties, *refs):
     sums_refs, refs = refs[:parties], refs[parties:]
     attended_ref, query_ref, cum_col_ref, upstream_ref, gain_ref = refs[:5]
-    attn_grad_ref, refs = refs[5], refs[6:]
-    send_refs, (held_ref,) = refs[: plan.members], refs[plan.members :]
+    (attn_grad_ref, held_ref), send_refs = refs[5:7], refs[7:]
     size = plan.size
     feature_count = plan.heads * size * parties
     sums = sum(ref[...] for ref in sums_refs)
@@ -322,27 +359,30 @@
 
 
 def finish_body(plan, *refs):
-    grad_refs, refs = refs[: plan.members], refs[plan.members :]
-    key_part_ref, value_part_ref, key_ref, value_ref, cum_col_ref = refs[:5]
-    key_grad_ref, value_grad_ref, done_ref, grads_ref = refs[5:]
-    done_ref[...] = jnp.zeros_like(done_ref)
-    length = key_ref.shape[0]
-    gather_rounded(plan, grad_refs, grads_ref)
+    first_refs, refs = refs[: plan.members], refs[plan.members :]
+    second_refs, refs = refs[: plan.members], refs[plan.members :]
+    key_part_ref, value_part_ref, key_ref, value_ref, cum_col_ref, summary_ref, before_ref = refs[:7]
+    key_grad_ref, value_grad_ref, total_ref, held_ref = refs[7:]
+    length, size = key_ref.shape[0], plan.size
+    swapped = jnp.where(plan.group() == 0, 0, 1) if plan.groups == 2 else 0
+    for k in range(plan.members):
+        held_ref[swapped, plan.rows_of(plan.peer(k))] = first_refs[k][...]
+        held_ref[1 - swapped, plan.rows_of(plan.peer(k))] = second_refs[k][...]
     cum_col = cum_col_ref[...]
-    shrink = jnp.exp(cum_col[length - 1 : length, :] - cum_col)
+    block_log = cum_col[length - 1 : length, :]
+    shrink = jnp.exp(block_log - cum_col)
     for h in range(plan.heads):
-        cut = lanes(h, plan.size)
-        grads = grads_ref[cut]
+        cut = lanes(h, size)
+        grads = held_ref[1, cut]
+        scale = jnp.exp(before_ref[h : h + 1])
+        scale_next = jnp.exp(before_ref[h : h + 1] + block_log[:, h : h + 1])
+        total_ref[cut] = held_ref[0, cut] + scale * summary_ref[cut] + scale_next * grads
+        grads = grads.astype(BF16)
         column = shrink[:, h : h + 1]
         key_state = dot(value_ref[:, cut], grads, CONTRACT_COLS)
         key_grad_ref[:, cut] = (key_part_ref[:, cut] + column * key_state).astype(BF16)
         value_state = dot(key_ref[:, cut], grads)
         value_grad_ref[:, cut] = (value_part_ref[:, cut] + column * value_state).astype(BF16)
-
-
-def join_body(plan, *refs):
-    for k, piece_ref in enumerate(refs[:-2]):
-        refs[-1][plan.rows_of(plan.peer(k))] = piece_ref[...]
 
 
 def on_device(
@@ -393,9 +433,9 @@
         [hold_logged],
     )
     totals = [total] + plan.from_groups(total)
-    sends = call(
+    *sends, before = call(
         bind(forward_scan_body),
-        pieces,
+        pieces + [shaped((LOG_ROWS, size))],
         [*parts, *totals, state_in.reshape(width, size)],
         [hold_groups, hold_logged],
     )
@@ -409,11 +449,10 @@
         lax.ppermute(sums, "head", [(i, (i + step) % parties) for i in range(parties)])
         for step in range(1, parties)
     ]
-    attn_grad, *sends = call(
+    attn_grad, summary, *sends = call(
         bind(attn_grad_body, parties),
-        [rounded] + pieces,
+        [rounded, shaped((width, size))] + pieces,
         [*all_sums, attended, query_rows, cum_col, out_grad, gain],
-        [hold_whole],
     )
     parts = plan.swap_in_group(sends)
     query_grad, key_part, value_part = call(
@@ -422,27 +461,30 @@
         [attn_grad, query_rows, key_rows, value_rows, states, weights, cum_log, cum_col],
         flops=10 * heads * length * length * size,
     )
-    (total,) = call(bind(group_grad_body), [logged], [*parts, logs], [hold])
+    grad_rows = state_out_grad.reshape(width, size)
+    two_sided = plan.groups == 2
+    total, *sends = call(
+        bind(group_grad_body),
+        [logged] + pieces * two_sided,
+        [*parts, logs, grad_rows, key_part],
+        [hold],
+        specs=[VMEM] * (plan.members + 2) + [ANY],
+    )
     totals = [total] + plan.from_groups(total)
-    *sends, whole_total = call(
+    swapped = [plan.swap_in_group(sends)] if two_sided else []
+    sends = call(
         bind(reverse_scan_body),
-        pieces + [piece],
-        [*parts, *totals, logs, state_out_grad.reshape(width, size), key_part],
+        pieces * (1 if two_sided else 2),
+        [*parts, *totals, logs, grad_rows],
         [hold_groups, hold],
-        specs=[VMEM] * (plan.members + plan.groups + 2) + [ANY],
-    )
-    grads = plan.swap_in_group(sends)
-    totals = plan.swap_in_group([whole_total] * plan.members)
-    key_grad, value_grad, done = call(
+    )
+    for first in range(0, len(sends), plan.members):
+        swapped.append(plan.swap_in_group(sends[first : first + plan.members]))
+    key_grad, value_grad, state_in_grad = call(
         bind(finish_body),
-        [rounded, rounded, shaped((8, size))],
-        [*grads, key_part, value_part, key_rows, value_rows, cum_col],
-        [pltpu.VMEM((width, size), BF16)],
-    )
-    (state_in_grad,) = call(
-        bind(join_body),
-        [shaped((width, size))],
-        [*totals, done],
+        [rounded, rounded, shaped((width, size))],
+        [*swapped[0], *swapped[1], key_part, value_part, key_rows, value_rows, cum_col, summary, before],
+        [pltpu.VMEM((2, width, size), F32)],
     )
     return (query_grad, key_grad, value_grad, state_in_grad.reshape(heads, size, size))
 

time: 74.6 us -> 68 us (0.912)
  waiting for transfers between devices: 35.8 us -> 29.6 us
    ppermute x15, waiting for transfers between devices: 24.1 us -> 17.3 us  [swap_in_group(): swapped.append(lax.ppermute(piece, 'seq', pairs))]
    ppermute x3, waiting for transfers between devices: 1.37 us -> 2.85 us  [on_device(): lax.ppermute(sums, 'head', [(i, (i + step) % parties) for i in range(part...]
    ppermute x3, starting transfers between devices: 3.11 us -> 1.85 us  [on_device(): lax.ppermute(sums, 'head', [(i, (i + step) % parties) for i in range(part...]
    ppermute x15, starting transfers between devices: 17 us -> 18.3 us  [swap_in_group(): swapped.append(lax.ppermute(piece, 'seq', pairs))]
    ppermute x2, waiting for transfers between devices: 10.4 us -> 9.48 us  [from_groups(): lax.ppermute(piece, 'seq', [(i, (i + step * self.members) % self.blocks)...]
    pallas_call x11 -> x10, Pallas kernels: 12.9 us -> 12.6 us  [call(): pl.pallas_call(body, out_shape=outs, in_specs=specs or [VMEM] * len(opera...]
  transfers between devices with their start and end apart: 20 -> 20, of which waited for: 18 -> 16; matrix products, arithmetic and copies ran while one was open for 0% -> 0% of each run, Pallas kernels for 8% -> 7%
where the time goes in v4:
time: 68 us; the launch traced here: 67.9 us
  waiting for transfers between devices  29.6 us (44%)
  starting transfers between devices  24.9 us (37%)
  Pallas kernels  12.6 us (19%)
  between operations  0.72 us (1%)
    ppermute x15, starting transfers between devices, swap_in_group(): swapped.append(lax.ppermute(piece, 'seq', pairs))  18.3 us
    ppermute x15, waiting for transfers between devices, swap_in_group(): swapped.append(lax.ppermute(piece, 'seq', pairs))  17.3 us
    pallas_call x10, Pallas kernels, call(): pl.pallas_call(body, out_shape=outs, in_specs=specs or [VMEM] * len(opera...  12.6 us
    ppermute x2, waiting for transfers between devices, from_groups(): lax.ppermute(piece, 'seq', [(i, (i + step * self.members) % self.blocks)...  9.48 us
    ppermute x2, starting transfers between devices, from_groups(): lax.ppermute(piece, 'seq', [(i, (i + step * self.members) % self.blocks)...  4.79 us
    ppermute x3, waiting for transfers between devices, on_device(): lax.ppermute(sums, 'head', [(i, (i + step) % parties) for i in range(part...  2.85 us
    ppermute x3, starting transfers between devices, on_device(): lax.ppermute(sums, 'head', [(i, (i + step) % parties) for i in range(part...  1.85 us
  transfers between devices with their start and end apart: 20, of which 16 were waited for; matrix products, arithmetic and copies ran while one was open for 0% of the time, Pallas kernels for 7%

profile of v4, /device:TPU:0, one launch (start us, length us, event | category | flops | bytes accessed | tf_op | source)
XLA Modules:
  0.0 67.9 jit_solution(15403956608237914535)
XLA Ops:
  0.6 3.3 %shard_map.111 = (f32[264,128]{1,0:T(8,128)S(1)}, f32[264,128]{1,0:T(8,128)S(1)}, f32[264,128]{1,0:T(8,128)S(1)}, f32[264,128]{1,0:T(8,128)S(1)}, f32[8,256]{1,0:T(8,128)S(1)}, /*index=5*/f32[256,8]{1,0:T(8,128)S(1)}) custom-call(bf16[256,1024]{1,0:T(8,128)(2,1)} %refs_10_.1, bf16[256,1024]{1,0:T(8,128)(2,1)} %refs_11_.1, f32[8,256]{1,0:T(8,128)} %decay_hbm.1), custom_call_target="tpu_custom_call" | custom-call | bytes 1613824 | tf_op jit(solution)/shard_map/pallas_call | solution.py:25
  3.9 4.0 %collective-permute-start = (f32[264,128]{1,0:T(8,128)S(1)}, f32[264,128]{1,0:T(8,128)S(1)}, u32[]{:S(2)}, u32[]{:S(2)}) collective-permute-start(f32[264,128]{1,0:T(8,128)S(1)} %get-tuple-element.44), channel_id=1, source_target_pairs={{0,12},{4,8},{8,4},{12,0},{16,28},{20,24},{24,20},{28,16},{1,13},{... | collective-permute-start | bytes 405512 | tf_op jit(solution)/shard_map/ppermute | solution.py:86
  8.0 0.5 collective-permute-start.1
  8.5 0.1 collective-permute-start.2
  8.6 3.4 %collective-permute-done.refs_1_ = f32[264,128]{1,0:T(8,128)S(1)} collective-permute-done((f32[264,128]{1,0:T(8,128)S(1)}, f32[264,128]{1,0:T(8,128)S(1)}, u32[]{:S(2)}, u32[]{:S(2)}) %collective-permute-start) | collective-permute-done | bytes 135200 | tf_op jit(solution)/shard_map/ppermute | solution.py:86
  12.0 2.5 %collective-permute-done.1.refs_2_ = f32[264,128]{1,0:T(8,128)S(1)} collective-permute-done((f32[264,128]{1,0:T(8,128)S(1)}, f32[264,128]{1,0:T(8,128)S(1)}, u32[]{:S(2)}, u32[]{:S(2)}) %collective-permute-start.1) | collective-permute-done | bytes 135200 | tf_op jit(solution)/shard_map/ppermute | solution.py:86
  14.4 0.1 collective-permute-done.2.refs_3_
  14.6 0.1 shard_map.112
  14.7 2.7 %collective-permute-start.3 = (f32[264,128]{1,0:T(8,128)S(1)}, f32[264,128]{1,0:T(8,128)S(1)}, u32[]{:S(2)}, u32[]{:S(2)}) collective-permute-start(f32[264,128]{1,0:T(8,128)S(1)} %get-tuple-element.47.refs_4_), channel_id=1, source_target_pairs={{0,16},{4,20},{8,24},{12,28},{16,0},{20,4},{24,8},{28,12},{1,17},{... | collective-permute-start | bytes 405512 | tf_op jit(solution)/shard_map/ppermute | solution.py:91
  17.3 6.6 %collective-permute-done.3.refs_5_ = f32[264,128]{1,0:T(8,128)S(1)} collective-permute-done((f32[264,128]{1,0:T(8,128)S(1)}, f32[264,128]{1,0:T(8,128)S(1)}, u32[]{:S(2)}, u32[]{:S(2)}) %collective-permute-start.3) | collective-permute-done | bytes 135200 | tf_op jit(solution)/shard_map/ppermute | solution.py:91
  24.0 0.2 shard_map.113
  24.2 0.3 collective-permute-start.4
  24.4 2.0 %collective-permute-start.5 = (f32[256,128]{1,0:T(8,128)S(1)}, f32[256,128]{1,0:T(8,128)S(1)}, u32[]{:S(2)}, u32[]{:S(2)}) collective-permute-start(f32[256,128]{1,0:T(8,128)S(1)} %get-tuple-element.50), channel_id=1, source_target_pairs={{0,4},{4,0},{8,12},{12,8},{16,20},{20,16},{24,28},{28,24},{1,5},{5... | collective-permute-start | bytes 393224 | tf_op jit(solution)/shard_map/ppermute | solution.py:86
  26.5 1.3 %collective-permute-start.6 = (f32[256,128]{1,0:T(8,128)S(1)}, f32[256,128]{1,0:T(8,128)S(1)}, u32[]{:S(2)}, u32[]{:S(2)}) collective-permute-start(f32[256,128]{1,0:T(8,128)S(1)} %get-tuple-element.51), channel_id=1, source_target_pairs={{0,8},{4,12},{8,0},{12,4},{16,24},{20,28},{24,16},{28,20},{1,9},{5... | collective-permute-start | bytes 393224 | tf_op jit(solution)/shard_map/ppermute | solution.py:86
  27.7 0.9 %shard_map.114 = (bf16[8,256,256]{2,1,0:T(8,128)(2,1)S(1)}, f32[256,1024]{1,0:T(8,128)S(1)}) custom-call(bf16[256,1024]{1,0:T(8,128)(2,1)S(1)} %copy-done, bf16[256,1024]{1,0:T(8,128)(2,1)S(1)} %copy-done.1, bf16[256,1024]{1,0:T(8,128)(2,1)S(1)} %copy-done.2, f32[8,256]{1,0:T(8,128)S(1)} %get-tuple-element.52.cum_ref, ...), custom_call_target="tpu_custom_call" | custom-call | flops 268435456 | bytes 3686400 | tf_op jit(solution)/shard_map/pallas_call | solution.py:25
  28.7 0.0 copy-start.6
  28.7 2.5 %collective-permute-done.4.refs_1_ = f32[256,128]{1,0:T(8,128)S(1)} collective-permute-done((f32[256,128]{1,0:T(8,128)S(1)}, f32[256,128]{1,0:T(8,128)S(1)}, u32[]{:S(2)}, u32[]{:S(2)}) %collective-permute-start.4) | collective-permute-done | bytes 131104 | tf_op jit(solution)/shard_map/ppermute | solution.py:86
  31.2 1.2 %collective-permute-done.5.refs_2_ = f32[256,128]{1,0:T(8,128)S(1)} collective-permute-done((f32[256,128]{1,0:T(8,128)S(1)}, f32[256,128]{1,0:T(8,128)S(1)}, u32[]{:S(2)}, u32[]{:S(2)}) %collective-permute-start.5) | collective-permute-done | bytes 131104 | tf_op jit(solution)/shard_map/ppermute | solution.py:86
  32.4 0.4 collective-permute-done.6.refs_3_
  32.8 0.8 %shard_map.115 = (f32[256,1024]{1,0:T(8,128)S(1)}, f32[8,256]{1,0:T(8,128)S(1)}, bf16[1024,128]{1,0:T(8,128)(2,1)S(1)}) custom-call(f32[256,128]{1,0:T(8,128)S(1)} %get-tuple-element.48.refs_0_, f32[256,128]{1,0:T(8,128)S(1)} %collective-permute-done.4.refs_1_, f32[256,128]{1,0:T(8,128)S(1)} %collective-permute-done.5.refs_2_, ...), custom_call_target="tpu_custom_call" | custom-call | bytes 3952640 | tf_op jit(solution)/shard_map/pallas_call | solution.py:25
  33.6 0.9 %collective-permute-start.9 = (f32[8,256]{1,0:T(8,128)S(1)}, f32[8,256]{1,0:T(8,128)S(1)}, u32[]{:S(2)}, u32[]{:S(2)}) collective-permute-start(f32[8,256]{1,0:T(8,128)S(1)} %get-tuple-element.55.refs_0_), channel_id=1, source_target_pairs={{0,3},{1,0},{2,1},{3,2},{4,7},{5,4},{6,5},{7,6},{8,11},{9,8},{10,9... | collective-permute-start | bytes 24584 | tf_op jit(solution)/shard_map/ppermute | solution.py:449
  34.5 0.7 %collective-permute-start.8 = (f32[8,256]{1,0:T(8,128)S(1)}, f32[8,256]{1,0:T(8,128)S(1)}, u32[]{:S(2)}, u32[]{:S(2)}) collective-permute-start(f32[8,256]{1,0:T(8,128)S(1)} %get-tuple-element.55.refs_0_), channel_id=1, source_target_pairs={{0,2},{1,3},{2,0},{3,1},{4,6},{5,7},{6,4},{7,5},{8,10},{9,11},{10,... | collective-permute-start | bytes 24584 | tf_op jit(solution)/shard_map/ppermute | solution.py:449
  35.3 0.2 collective-permute-start.7
  35.5 0.4 collective-permute-done.9.refs_3_
  35.9 2.3 %collective-permute-done.8.refs_2_ = f32[8,256]{1,0:T(8,128)S(1)} collective-permute-done((f32[8,256]{1,0:T(8,128)S(1)}, f32[8,256]{1,0:T(8,128)S(1)}, u32[]{:S(2)}, u32[]{:S(2)}) %collective-permute-start.8) | collective-permute-done | bytes 8224 | tf_op jit(solution)/shard_map/ppermute | solution.py:449
  38.2 0.1 collective-permute-done.7.refs_1_
  38.4 1.4 %shard_map.116 = (bf16[256,1024]{1,0:T(8,128)(2,1)S(1)}, f32[1024,128]{1,0:T(8,128)S(1)}, f32[256,128]{1,0:T(8,128)S(1)}, f32[256,128]{1,0:T(8,128)S(1)}, f32[25...) custom-call(f32[8,256]{1,0:T(8,128)S(1)} %get-tuple-element.55.refs_0_, f32[8,256]{1,0:T(8,128)S(1)} %collective-permute-done.7.refs_1_, ...), custom_call_target="tpu_custom_call" | custom-call | bytes 3715072 | tf_op jit(solution)/shard_map/pallas_call | solution.py:25
  39.8 1.3 %collective-permute-start.10 = (f32[256,128]{1,0:T(8,128)S(1)}, f32[256,128]{1,0:T(8,128)S(1)}, u32[]{:S(2)}, u32[]{:S(2)}) collective-permute-start(f32[256,128]{1,0:T(8,128)S(1)} %get-tuple-element.62), channel_id=1, source_target_pairs={{0,12},{4,8},{8,4},{12,0},{16,28},{20,24},{24,20},{28,16},{1,13},{... | collective-permute-start | bytes 393224 | tf_op jit(solution)/shard_map/ppermute | solution.py:86
  41.1 1.7 %collective-permute-start.11 = (f32[256,128]{1,0:T(8,128)S(1)}, f32[256,128]{1,0:T(8,128)S(1)}, u32[]{:S(2)}, u32[]{:S(2)}) collective-permute-start(f32[256,128]{1,0:T(8,128)S(1)} %get-tuple-element.63), channel_id=1, source_target_pairs={{0,4},{4,0},{8,12},{12,8},{16,20},{20,16},{24,28},{28,24},{1,5},{5... | collective-permute-start | bytes 393224 | tf_op jit(solution)/shard_map/ppermute | solution.py:86
  42.8 0.5 collective-permute-start.12
  43.3 3.5 %shard_map.117 = (bf16[256,1024]{1,0:T(8,128)(2,1)}, f32[256,1024]{1,0:T(8,128)S(1)}, f32[256,1024]{1,0:T(8,128)S(1)}) custom-call(bf16[256,1024]{1,0:T(8,128)(2,1)S(1)} %get-tuple-element.57.attn_grad_ref, bf16[256,1024]{1,0:T(8,128)(2,1)S(1)} %copy-done, bf16[256,1024]{1,0:T(8,128)(2,1)S(1)} %copy-done.1, bf16[256,1024]{1,0:T(8,128)(2,1)S(1)} %copy-done.2, ...), custom_call_target="tpu_custom_call" | custom-call | flops 671088640 | bytes 6045696 | tf_op jit(solution)/shard_map/pallas_call | solution.py:25
  46.8 0.0 collective-permute-done.10.refs_1_
  46.8 1.3 %collective-permute-done.11.refs_2_ = f32[256,128]{1,0:T(8,128)S(1)} collective-permute-done((f32[256,128]{1,0:T(8,128)S(1)}, f32[256,128]{1,0:T(8,128)S(1)}, u32[]{:S(2)}, u32[]{:S(2)}) %collective-permute-start.11) | collective-permute-done | bytes 131104 | tf_op jit(solution)/shard_map/ppermute | solution.py:86
  48.1 0.3 collective-permute-done.12.refs_3_
  48.4 0.2 shard_map.118
  48.6 2.1 %collective-permute-start.16 = (f32[264,128]{1,0:T(8,128)S(1)}, f32[264,128]{1,0:T(8,128)S(1)}, u32[]{:S(2)}, u32[]{:S(2)}) collective-permute-start(f32[264,128]{1,0:T(8,128)S(1)} %get-tuple-element.71.refs_4_), channel_id=1, source_target_pairs={{0,16},{4,20},{8,24},{12,28},{16,0},{20,4},{24,8},{28,12},{1,17},{... | collective-permute-start | bytes 405512 | tf_op jit(solution)/shard_map/ppermute | solution.py:91
  50.7 1.5 %collective-permute-start.13 = (f32[256,128]{1,0:T(8,128)S(1)}, f32[256,128]{1,0:T(8,128)S(1)}, u32[]{:S(2)}, u32[]{:S(2)}) collective-permute-start(f32[256,128]{1,0:T(8,128)S(1)} %get-tuple-element.68), channel_id=1, source_target_pairs={{0,12},{4,8},{8,4},{12,0},{16,28},{20,24},{24,20},{28,16},{1,13},{... | collective-permute-start | bytes 393224 | tf_op jit(solution)/shard_map/ppermute | solution.py:86
  52.2 1.0 %collective-permute-start.14 = (f32[256,128]{1,0:T(8,128)S(1)}, f32[256,128]{1,0:T(8,128)S(1)}, u32[]{:S(2)}, u32[]{:S(2)}) collective-permute-start(f32[256,128]{1,0:T(8,128)S(1)} %get-tuple-element.69), channel_id=1, source_target_pairs={{0,4},{4,0},{8,12},{12,8},{16,20},{20,16},{24,28},{28,24},{1,5},{5... | collective-permute-start | bytes 393224 | tf_op jit(solution)/shard_map/ppermute | solution.py:86
  53.2 1.0 %collective-permute-start.15 = (f32[256,128]{1,0:T(8,128)S(1)}, f32[256,128]{1,0:T(8,128)S(1)}, u32[]{:S(2)}, u32[]{:S(2)}) collective-permute-start(f32[256,128]{1,0:T(8,128)S(1)} %get-tuple-element.70), channel_id=1, source_target_pairs={{0,8},{4,12},{8,0},{12,4},{16,24},{20,28},{24,16},{28,20},{1,9},{5... | collective-permute-start | bytes 393224 | tf_op jit(solution)/shard_map/ppermute | solution.py:86
  54.2 2.8 %collective-permute-done.16.refs_5_ = f32[264,128]{1,0:T(8,128)S(1)} collective-permute-done((f32[264,128]{1,0:T(8,128)S(1)}, f32[264,128]{1,0:T(8,128)S(1)}, u32[]{:S(2)}, u32[]{:S(2)}) %collective-permute-start.16) | collective-permute-done | bytes 135200 | tf_op jit(solution)/shard_map/ppermute | solution.py:91
  57.1 0.2 shard_map.119
  57.3 0.5 collective-permute-start.17
  57.8 1.3 %collective-permute-start.18 = (f32[256,128]{1,0:T(8,128)S(1)}, f32[256,128]{1,0:T(8,128)S(1)}, u32[]{:S(2)}, u32[]{:S(2)}) collective-permute-start(f32[256,128]{1,0:T(8,128)S(1)} %get-tuple-element.74), channel_id=1, source_target_pairs={{0,4},{4,0},{8,12},{12,8},{16,20},{20,16},{24,28},{28,24},{1,5},{5... | collective-permute-start | bytes 393224 | tf_op jit(solution)/shard_map/ppermute | solution.py:86
  59.2 0.6 collective-permute-done.13.refs_1_
  59.7 1.1 %collective-permute-start.19 = (f32[256,128]{1,0:T(8,128)S(1)}, f32[256,128]{1,0:T(8,128)S(1)}, u32[]{:S(2)}, u32[]{:S(2)}) collective-permute-start(f32[256,128]{1,0:T(8,128)S(1)} %get-tuple-element.75), channel_id=1, source_target_pairs={{0,8},{4,12},{8,0},{12,4},{16,24},{20,28},{24,16},{28,20},{1,9},{5... | collective-permute-start | bytes 393224 | tf_op jit(solution)/shard_map/ppermute | solution.py:86
  60.9 4.2 %collective-permute-done.17.refs_5_ = f32[256,128]{1,0:T(8,128)S(1)} collective-permute-done((f32[256,128]{1,0:T(8,128)S(1)}, f32[256,128]{1,0:T(8,128)S(1)}, u32[]{:S(2)}, u32[]{:S(2)}) %collective-permute-start.17) | collective-permute-done | bytes 131104 | tf_op jit(solution)/shard_map/ppermute | solution.py:86
  65.1 0.9 %collective-permute-done.19.refs_7_ = f32[256,128]{1,0:T(8,128)S(1)} collective-permute-done((f32[256,128]{1,0:T(8,128)S(1)}, f32[256,128]{1,0:T(8,128)S(1)}, u32[]{:S(2)}, u32[]{:S(2)}) %collective-permute-start.19) | collective-permute-done | bytes 131104 | tf_op jit(solution)/shard_map/ppermute | solution.py:86
  65.9 2.0 %shard_map.120 = (bf16[256,1024]{1,0:T(8,128)(2,1)}, bf16[256,1024]{1,0:T(8,128)(2,1)}, f32[1024,128]{1,0:T(8,128)}) custom-call(f32[256,128]{1,0:T(8,128)S(1)} %get-tuple-element.67.refs_0_, f32[256,128]{1,0:T(8,128)S(1)} %collective-permute-done.13.refs_1_, f32[256,128]{1,0:T(8,128)S(1)} %collective-permute-done.14.refs_2_, ...), custom_call_target="tpu_custom_call" | custom-call | bytes 6303744 | tf_op jit(solution)/shard_map/pallas_call | solution.py:25
  (16 shorter events, 0.0 us)
Async XLA Ops:
  0.6 23.4 %copy-start.5 = (f32[8,128,128]{2,1,0:T(8,128)S(1)}, f32[8,128,128]{2,1,0:T(8,128)}, u32[]{:S(2)}) copy-start(f32[8,128,128]{2,1,0:T(8,128)} %param.14) | copy-start | bytes 1572868
  3.9 8.0 %collective-permute-start = (f32[264,128]{1,0:T(8,128)S(1)}, f32[264,128]{1,0:T(8,128)S(1)}, u32[]{:S(2)}, u32[]{:S(2)}) collective-permute-start(f32[264,128]{1,0:T(8,128)S(1)} %get-tuple-element.44), channel_id=1, source_target_pairs={{0,12},{4,8},{8,4},{12,0},{16,28},{20,24},{24,20},{28,16},{1,13},{... | collective-permute-start | bytes 405512 | tf_op jit(solution)/shard_map/ppermute | solution.py:86
  8.0 6.5 %collective-permute-start.1 = (f32[264,128]{1,0:T(8,128)S(1)}, f32[264,128]{1,0:T(8,128)S(1)}, u32[]{:S(2)}, u32[]{:S(2)}) collective-permute-start(f32[264,128]{1,0:T(8,128)S(1)} %get-tuple-element.45), channel_id=1, source_target_pairs={{0,4},{4,0},{8,12},{12,8},{16,20},{20,16},{24,28},{28,24},{1,5},{5... | collective-permute-start | bytes 405512 | tf_op jit(solution)/shard_map/ppermute | solution.py:86
  8.5 6.1 %collective-permute-start.2 = (f32[264,128]{1,0:T(8,128)S(1)}, f32[264,128]{1,0:T(8,128)S(1)}, u32[]{:S(2)}, u32[]{:S(2)}) collective-permute-start(f32[264,128]{1,0:T(8,128)S(1)} %get-tuple-element.46), channel_id=1, source_target_pairs={{0,8},{4,12},{8,0},{12,4},{16,24},{20,28},{24,16},{28,20},{1,9},{5... | collective-permute-start | bytes 405512 | tf_op jit(solution)/shard_map/ppermute | solution.py:86
  14.6 13.2 %copy-start.2 = (bf16[256,1024]{1,0:T(8,128)(2,1)S(1)}, bf16[256,1024]{1,0:T(8,128)(2,1)}, u32[]{:S(2)}) copy-start(bf16[256,1024]{1,0:T(8,128)(2,1)} %refs_11_.1) | copy-start | bytes 1572868
  14.7 9.3 %collective-permute-start.3 = (f32[264,128]{1,0:T(8,128)S(1)}, f32[264,128]{1,0:T(8,128)S(1)}, u32[]{:S(2)}, u32[]{:S(2)}) collective-permute-start(f32[264,128]{1,0:T(8,128)S(1)} %get-tuple-element.47.refs_4_), channel_id=1, source_target_pairs={{0,16},{4,20},{8,24},{12,28},{16,0},{20,4},{24,8},{28,12},{1,17},{... | collective-permute-start | bytes 405512 | tf_op jit(solution)/shard_map/ppermute | solution.py:91
  24.0 3.8 %copy-start = (bf16[256,1024]{1,0:T(8,128)(2,1)S(1)}, bf16[256,1024]{1,0:T(8,128)(2,1)}, u32[]{:S(2)}) copy-start(bf16[256,1024]{1,0:T(8,128)(2,1)} %query_ref.3) | copy-start | bytes 1572868
  24.0 3.8 %copy-start.1 = (bf16[256,1024]{1,0:T(8,128)(2,1)S(1)}, bf16[256,1024]{1,0:T(8,128)(2,1)}, u32[]{:S(2)}) copy-start(bf16[256,1024]{1,0:T(8,128)(2,1)} %refs_10_.1) | copy-start | bytes 1572868
  24.2 7.0 %collective-permute-start.4 = (f32[256,128]{1,0:T(8,128)S(1)}, f32[256,128]{1,0:T(8,128)S(1)}, u32[]{:S(2)}, u32[]{:S(2)}) collective-permute-start(f32[256,128]{1,0:T(8,128)S(1)} %get-tuple-element.49), channel_id=1, source_target_pairs={{0,12},{4,8},{8,4},{12,0},{16,28},{20,24},{24,20},{28,16},{1,13},{... | collective-permute-start | bytes 393224 | tf_op jit(solution)/shard_map/ppermute | solution.py:86
  24.4 8.0 %collective-permute-start.5 = (f32[256,128]{1,0:T(8,128)S(1)}, f32[256,128]{1,0:T(8,128)S(1)}, u32[]{:S(2)}, u32[]{:S(2)}) collective-permute-start(f32[256,128]{1,0:T(8,128)S(1)} %get-tuple-element.50), channel_id=1, source_target_pairs={{0,4},{4,0},{8,12},{12,8},{16,20},{20,16},{24,28},{28,24},{1,5},{5... | collective-permute-start | bytes 393224 | tf_op jit(solution)/shard_map/ppermute | solution.py:86
  26.5 6.3 %collective-permute-start.6 = (f32[256,128]{1,0:T(8,128)S(1)}, f32[256,128]{1,0:T(8,128)S(1)}, u32[]{:S(2)}, u32[]{:S(2)}) collective-permute-start(f32[256,128]{1,0:T(8,128)S(1)} %get-tuple-element.51), channel_id=1, source_target_pairs={{0,8},{4,12},{8,0},{12,4},{16,24},{20,28},{24,16},{28,20},{1,9},{5... | collective-permute-start | bytes 393224 | tf_op jit(solution)/shard_map/ppermute | solution.py:86
  27.7 5.1 %copy-start.3 = (bf16[256,1024]{1,0:T(8,128)(2,1)S(1)}, bf16[256,1024]{1,0:T(8,128)(2,1)}, u32[]{:S(2)}) copy-start(bf16[256,1024]{1,0:T(8,128)(2,1)} %refs_7_.3) | copy-start | bytes 1572868
  28.7 4.1 %copy-start.6 = (f32[1024]{0:T(1024)S(1)}, f32[1024]{0:T(1024)}, u32[]{:S(2)}) copy-start(f32[1024]{0:T(1024)} %param.13) | copy-start | bytes 12292
  33.6 2.3 %collective-permute-start.9 = (f32[8,256]{1,0:T(8,128)S(1)}, f32[8,256]{1,0:T(8,128)S(1)}, u32[]{:S(2)}, u32[]{:S(2)}) collective-permute-start(f32[8,256]{1,0:T(8,128)S(1)} %get-tuple-element.55.refs_0_), channel_id=1, source_target_pairs={{0,3},{1,0},{2,1},{3,2},{4,7},{5,4},{6,5},{7,6},{8,11},{9,8},{10,9... | collective-permute-start | bytes 24584 | tf_op jit(solution)/shard_map/ppermute | solution.py:449
  34.5 3.7 %collective-permute-start.8 = (f32[8,256]{1,0:T(8,128)S(1)}, f32[8,256]{1,0:T(8,128)S(1)}, u32[]{:S(2)}, u32[]{:S(2)}) collective-permute-start(f32[8,256]{1,0:T(8,128)S(1)} %get-tuple-element.55.refs_0_), channel_id=1, source_target_pairs={{0,2},{1,3},{2,0},{3,1},{4,6},{5,7},{6,4},{7,5},{8,10},{9,11},{10,... | collective-permute-start | bytes 24584 | tf_op jit(solution)/shard_map/ppermute | solution.py:449
  35.3 3.1 %collective-permute-start.7 = (f32[8,256]{1,0:T(8,128)S(1)}, f32[8,256]{1,0:T(8,128)S(1)}, u32[]{:S(2)}, u32[]{:S(2)}) collective-permute-start(f32[8,256]{1,0:T(8,128)S(1)} %get-tuple-element.55.refs_0_), channel_id=1, source_target_pairs={{0,1},{1,2},{2,3},{3,0},{4,5},{5,6},{6,7},{7,4},{8,9},{9,10},{10,1... | collective-permute-start | bytes 24584 | tf_op jit(solution)/shard_map/ppermute | solution.py:449
  39.8 7.0 %collective-permute-start.10 = (f32[256,128]{1,0:T(8,128)S(1)}, f32[256,128]{1,0:T(8,128)S(1)}, u32[]{:S(2)}, u32[]{:S(2)}) collective-permute-start(f32[256,128]{1,0:T(8,128)S(1)} %get-tuple-element.62), channel_id=1, source_target_pairs={{0,12},{4,8},{8,4},{12,0},{16,28},{20,24},{24,20},{28,16},{1,13},{... | collective-permute-start | bytes 393224 | tf_op jit(solution)/shard_map/ppermute | solution.py:86
  41.1 7.0 %collective-permute-start.11 = (f32[256,128]{1,0:T(8,128)S(1)}, f32[256,128]{1,0:T(8,128)S(1)}, u32[]{:S(2)}, u32[]{:S(2)}) collective-permute-start(f32[256,128]{1,0:T(8,128)S(1)} %get-tuple-element.63), channel_id=1, source_target_pairs={{0,4},{4,0},{8,12},{12,8},{16,20},{20,16},{24,28},{28,24},{1,5},{5... | collective-permute-start | bytes 393224 | tf_op jit(solution)/shard_map/ppermute | solution.py:86
  42.8 5.6 %collective-permute-start.12 = (f32[256,128]{1,0:T(8,128)S(1)}, f32[256,128]{1,0:T(8,128)S(1)}, u32[]{:S(2)}, u32[]{:S(2)}) collective-permute-start(f32[256,128]{1,0:T(8,128)S(1)} %get-tuple-element.64), channel_id=1, source_target_pairs={{0,8},{4,12},{8,0},{12,4},{16,24},{20,28},{24,16},{28,20},{1,9},{5... | collective-permute-start | bytes 393224 | tf_op jit(solution)/shard_map/ppermute | solution.py:86
  43.3 5.1 %copy-start.4 = (f32[8,128,128]{2,1,0:T(8,128)S(1)}, f32[8,128,128]{2,1,0:T(8,128)}, u32[]{:S(2)}) copy-start(f32[8,128,128]{2,1,0:T(8,128)} %param.15) | copy-start | bytes 1572868
  48.6 8.5 %collective-permute-start.16 = (f32[264,128]{1,0:T(8,128)S(1)}, f32[264,128]{1,0:T(8,128)S(1)}, u32[]{:S(2)}, u32[]{:S(2)}) collective-permute-start(f32[264,128]{1,0:T(8,128)S(1)} %get-tuple-element.71.refs_4_), channel_id=1, source_target_pairs={{0,16},{4,20},{8,24},{12,28},{16,0},{20,4},{24,8},{28,12},{1,17},{... | collective-permute-start | bytes 405512 | tf_op jit(solution)/shard_map/ppermute | solution.py:91
  50.7 9.0 %collective-permute-start.13 = (f32[256,128]{1,0:T(8,128)S(1)}, f32[256,128]{1,0:T(8,128)S(1)}, u32[]{:S(2)}, u32[]{:S(2)}) collective-permute-start(f32[256,128]{1,0:T(8,128)S(1)} %get-tuple-element.68), channel_id=1, source_target_pairs={{0,12},{4,8},{8,4},{12,0},{16,28},{20,24},{24,20},{28,16},{1,13},{... | collective-permute-start | bytes 393224 | tf_op jit(solution)/shard_map/ppermute | solution.py:86
  52.2 8.7 %collective-permute-start.14 = (f32[256,128]{1,0:T(8,128)S(1)}, f32[256,128]{1,0:T(8,128)S(1)}, u32[]{:S(2)}, u32[]{:S(2)}) collective-permute-start(f32[256,128]{1,0:T(8,128)S(1)} %get-tuple-element.69), channel_id=1, source_target_pairs={{0,4},{4,0},{8,12},{12,8},{16,20},{20,16},{24,28},{28,24},{1,5},{5... | collective-permute-start | bytes 393224 | tf_op jit(solution)/shard_map/ppermute | solution.py:86
  53.2 7.7 %collective-permute-start.15 = (f32[256,128]{1,0:T(8,128)S(1)}, f32[256,128]{1,0:T(8,128)S(1)}, u32[]{:S(2)}, u32[]{:S(2)}) collective-permute-start(f32[256,128]{1,0:T(8,128)S(1)} %get-tuple-element.70), channel_id=1, source_target_pairs={{0,8},{4,12},{8,0},{12,4},{16,24},{20,28},{24,16},{28,20},{1,9},{5... | collective-permute-start | bytes 393224 | tf_op jit(solution)/shard_map/ppermute | solution.py:86
  57.3 7.7 %collective-permute-start.17 = (f32[256,128]{1,0:T(8,128)S(1)}, f32[256,128]{1,0:T(8,128)S(1)}, u32[]{:S(2)}, u32[]{:S(2)}) collective-permute-start(f32[256,128]{1,0:T(8,128)S(1)} %get-tuple-element.73), channel_id=1, source_target_pairs={{0,12},{4,8},{8,4},{12,0},{16,28},{20,24},{24,20},{28,16},{1,13},{... | collective-permute-start | bytes 393224 | tf_op jit(solution)/shard_map/ppermute | solution.py:86
  57.8 7.2 %collective-permute-start.18 = (f32[256,128]{1,0:T(8,128)S(1)}, f32[256,128]{1,0:T(8,128)S(1)}, u32[]{:S(2)}, u32[]{:S(2)}) collective-permute-start(f32[256,128]{1,0:T(8,128)S(1)} %get-tuple-element.74), channel_id=1, source_target_pairs={{0,4},{4,0},{8,12},{12,8},{16,20},{20,16},{24,28},{28,24},{1,5},{5... | collective-permute-start | bytes 393224 | tf_op jit(solution)/shard_map/ppermute | solution.py:86
  59.7 6.2 %collective-permute-start.19 = (f32[256,128]{1,0:T(8,128)S(1)}, f32[256,128]{1,0:T(8,128)S(1)}, u32[]{:S(2)}, u32[]{:S(2)}) collective-permute-start(f32[256,128]{1,0:T(8,128)S(1)} %get-tuple-element.75), channel_id=1, source_target_pairs={{0,8},{4,12},{8,0},{12,4},{16,24},{20,28},{24,16},{28,20},{1,9},{5... | collective-permute-start | bytes 393224 | tf_op jit(solution)/shard_map/ppermute | solution.py:86

commit v5 on v4

v5 whole, which is shorter than its diff:
```python
import functools

import jax
import jax.numpy as jnp
from jax import lax
from jax.experimental import pallas as pl
from jax.experimental.pallas import tpu as pltpu
from jax.sharding import PartitionSpec as P

EPSILON = 1e-06
F32 = jnp.float32
BF16 = jnp.bfloat16
LOG_ROWS = 8
MASKED = -1e30

CONTRACT_ROWS = (((0,), (0,)), ((), ()))
CONTRACT_COLS = (((1,), (1,)), ((), ()))
VMEM = pl.BlockSpec(memory_space=pltpu.VMEM)
HBM = pl.BlockSpec(memory_space=pltpu.HBM)
ANY = pl.BlockSpec(memory_space=pl.ANY)


def call(body, outs, operands, scratch=(), flops=0, specs=None):
    return pl.pallas_call(
        body,
        out_shape=outs,
        in_specs=specs or [VMEM] * len(operands),
        out_specs=[VMEM] * len(outs),
        scratch_shapes=list(scratch),
        compiler_params=pltpu.CompilerParams(vmem_limit_bytes=24 * 1024 * 1024),
        cost_estimate=pl.CostEstimate(flops=flops, bytes_accessed=0, transcendentals=0),
    )(*operands)


def shaped(shape, dtype=F32):
    return jax.ShapeDtypeStruct(shape, dtype)


def dot(a, b, dims=(((1,), (0,)), ((), ()))):
    return lax.dot_general(a, b, dims, preferred_element_type=F32)


def exact_dot(a, b, dims=(((1,), (0,)), ((), ()))):
    return lax.dot_general(
        a, b, dims, precision=lax.Precision.HIGHEST, preferred_element_type=F32
    )


def lanes(h, size):
    return slice(h * size, (h + 1) * size)


def causal_mask(length):
    row = lax.broadcasted_iota(jnp.int32, (length, length), 0)
    col = lax.broadcasted_iota(jnp.int32, (length, length), 1)
    return row >= col


class Plan:
    def __init__(self, heads, size, blocks):
        self.heads, self.size, self.blocks = heads, size, blocks
        self.members = next(m for m in (4, 2, 1) if heads % m == 0 and blocks % m == 0)
        self.groups = blocks // self.members
        self.own = heads // self.members
        self.rows = self.own * size
        self.chunks = self.own
        self.chunk_rows = self.rows // self.chunks

    def member(self):
        return lax.rem(lax.axis_index("seq"), self.members)

    def group(self):
        return lax.div(lax.axis_index("seq"), self.members)

    def rows_of(self, member):
        return pl.ds(pl.multiple_of(member * self.rows, self.rows), self.rows)

    def chunk_of(self, member, chunk):
        start = member * self.rows + chunk * self.chunk_rows
        return pl.ds(pl.multiple_of(start, self.chunk_rows), self.chunk_rows)

    def swap_in_group(self, pieces):
        span = self.members
        sets = [list(range(i, i + span)) for i in range(0, self.blocks, span)]
        return lax.all_to_all(pieces, "seq", 0, 0, axis_index_groups=sets)

    def from_groups(self, piece):
        return [
            lax.ppermute(
                piece,
                "seq",
                [(i, (i + step * self.members) % self.blocks) for i in range(self.blocks)],
            )
            for step in range(1, self.groups)
        ]


def own_decays(plan, log_tile_ref, chunk=None):
    count = plan.own if chunk is None else plan.own // plan.chunks
    first = plan.member() * plan.own + (0 if chunk is None else chunk * count)
    rows = [log_tile_ref[pl.ds(first + j, 1), :] for j in range(count)]
    return jnp.concatenate([jnp.broadcast_to(jnp.exp(row), (plan.size, plan.size)) for row in rows])


def summary_body(plan, key_hbm, value_hbm, decay_hbm, *refs):
    send_refs, refs = refs[: plan.chunks], refs[plan.chunks :]
    cum_ref, cum_col_ref, held_ref, key_ref, value_ref, decay_ref, sems, decay_sem = refs
    length, heads, size = key_ref.shape[0], plan.heads, plan.size
    decay_copy = pltpu.make_async_copy(decay_hbm, decay_ref, decay_sem)
    decay_copy.start()
    copies = []
    for part in range(plan.members):
        cut = lanes(part, plan.rows)
        copies.append(
            [
                pltpu.make_async_copy(source.at[:, cut], target.at[:, cut], sems.at[part, i])
                for i, (source, target) in enumerate([(key_hbm, key_ref), (value_hbm, value_ref)])
            ]
        )
        for copy in copies[-1]:
            copy.start()
    decay_copy.wait()
    decay = decay_ref[...]
    causal = jnp.where(causal_mask(length), 1.0, 0.0)
    cum_col = exact_dot(causal, decay, CONTRACT_COLS)
    cum_row = exact_dot(decay, causal, CONTRACT_COLS)
    cum_ref[...] = cum_row
    cum_col_ref[...] = cum_col
    block_log = cum_col[length - 1 : length, :]
    shrink = jnp.exp(block_log - cum_col)
    for h in range(heads):
        if h % plan.own == 0:
            for copy in copies[h // plan.own]:
                copy.wait()
        key_decayed = (key_ref[:, lanes(h, size)].astype(F32) * shrink[:, h : h + 1]).astype(BF16)
        held_ref[h * size : (h + 1) * size] = dot(
            key_decayed, value_ref[:, lanes(h, size)], CONTRACT_ROWS
        )
    log_tile = jnp.broadcast_to(cum_row[:, length - 1 : length], (heads, size))
    if heads < LOG_ROWS:
        log_tile = jnp.concatenate([log_tile, jnp.zeros((LOG_ROWS - heads, size), F32)])
    for chunk, send_ref in enumerate(send_refs):
        for member in range(plan.members):
            send_ref[member, : plan.chunk_rows] = held_ref[plan.chunk_of(member, chunk)]
            if chunk == 0:
                send_ref[member, plan.chunk_rows :] = log_tile


def group_total_body(plan, chunk, parts_ref, *refs):
    rows = plan.chunk_rows
    if chunk == 0:
        total_ref, logs_ref = refs
        for b in range(plan.members):
            logs_ref[b] = parts_ref[b, rows:]
        total_ref[rows:] = sum(logs_ref[b] for b in range(plan.members))
    else:
        logs_ref, total_ref = refs
    total = jnp.zeros((rows, plan.size), F32)
    for b in range(plan.members):
        total = own_decays(plan, logs_ref.at[b], chunk) * total + parts_ref[b, :rows]
    total_ref[:rows] = total


def stage_groups(plan, total_refs, held_ref):
    rows = held_ref.shape[1]
    for step, total_ref in enumerate(total_refs):
        held_ref[lax.rem(plan.group() - step + plan.groups, plan.groups)] = total_ref[:rows]


def forward_scan_body(plan, chunk, parts_ref, *refs):
    total_refs, refs = refs[: plan.groups], refs[plan.groups :]
    rows = plan.chunk_rows
    if chunk == 0:
        (state_ref, logs_ref), refs = refs[:2], refs[2:]
        send_ref, before_ref, group_logs_ref, groups_ref = refs
        for step, total_ref in enumerate(total_refs):
            group = lax.rem(plan.group() - step + plan.groups, plan.groups)
            group_logs_ref[group] = total_ref[rows:]
        before = jnp.zeros((LOG_ROWS, plan.size), F32)
        for group in range(plan.groups - 1):
            before += jnp.where(group < plan.group(), group_logs_ref[group], 0.0)
        for b in range(plan.members - 1):
            before += jnp.where(b < plan.member(), logs_ref[b], 0.0)
        before_ref[...] = before
    else:
        state_ref, logs_ref, group_logs_ref, send_ref, groups_ref = refs
    stage_groups(plan, total_refs, groups_ref)
    state = state_ref[plan.chunk_of(plan.member(), chunk)]
    for group in range(plan.groups - 1):
        after = own_decays(plan, group_logs_ref.at[group], chunk) * state + groups_ref[group]
        state = jnp.where(group < plan.group(), after, state)
    for b in range(plan.members):
        send_ref[b] = state
        state = own_decays(plan, logs_ref.at[b], chunk) * state + parts_ref[b, :rows]


def suffixes(plan, parts_ref, logs_ref, grad):
    found = []
    for b in reversed(range(plan.members)):
        found.append(grad)
        grad = own_decays(plan, logs_ref.at[b]) * grad + parts_ref[b]
    return found[::-1], grad


def prefixes(plan, parts_ref, logs_ref, total, scale):
    found = []
    for b in range(plan.members):
        found.append(total)
        total = total + scale * parts_ref[b]
        scale = scale * own_decays(plan, logs_ref.at[b])
    return found


def group_grad_body(plan, parts_ref, logs_ref, grad_ref, _, total_ref, *send_refs):
    zero = jnp.zeros((plan.rows, plan.size), F32)
    total_ref[...] = suffixes(plan, parts_ref, logs_ref, zero)[1]
    for send_ref in send_refs:
        first = plan.group() == 0
        before = prefixes(plan, parts_ref, logs_ref, zero, zero + 1.0)
        after = suffixes(plan, parts_ref, logs_ref, grad_ref[plan.rows_of(plan.member())])[0]
        for b in range(plan.members):
            send_ref[b] = jnp.where(first, before[b], after[b])


def reverse_scan_body(plan, parts_ref, *refs):
    total_refs, refs = refs[: plan.groups], refs[plan.groups :]
    (logs_ref, group_logs_ref, grad_ref), refs = refs[:3], refs[3:]
    send_refs, groups_ref = refs[:-1], refs[-1]
    stage_groups(plan, total_refs, groups_ref)
    grad = grad_ref[plan.rows_of(plan.member())]
    leaving = grad
    for group in reversed(range(plan.groups)):
        leaving = jnp.where(group == plan.group(), grad, leaving)
        grad = own_decays(plan, group_logs_ref.at[group]) * grad + groups_ref[group]
    total = jnp.zeros((plan.rows, plan.size), F32)
    scale = total + 1.0
    for group in range(plan.groups - 1):
        earlier = group < plan.group()
        total = jnp.where(earlier, total + scale * groups_ref[group], total)
        decays = own_decays(plan, group_logs_ref.at[group])
        scale = jnp.where(earlier, scale * decays, scale)
    after = suffixes(plan, parts_ref, logs_ref, leaving)[0]
    before = prefixes(plan, parts_ref, logs_ref, total, scale)
    first = plan.group() == 0
    for b in range(plan.members):
        if plan.groups == 2:
            send_refs[0][b] = jnp.where(first, after[b], before[b])
        else:
            send_refs[0][b] = before[b]
            send_refs[1][b] = after[b]


def decay_matrix(cum_ref, cum_col, causal, h):
    spread = cum_col[:, h : h + 1] - cum_ref[h : h + 1, :]
    return jnp.exp(jnp.where(causal, jnp.minimum(spread, 0.0), MASKED))


def intra_body(plan, query_ref, key_ref, value_ref, cum_ref, cum_col_ref, weight_ref, intra_ref):
    causal = causal_mask(query_ref.shape[0])
    cum_col = cum_col_ref[...]
    for h in range(plan.heads):
        cut = lanes(h, plan.size)
        scores = dot(query_ref[:, cut], key_ref[:, cut], CONTRACT_COLS)
        weights = (scores * decay_matrix(cum_ref, cum_col, causal, h)).astype(BF16)
        weight_ref[h] = weights
        intra_ref[:, cut] = dot(weights, value_ref[:, cut])


def attended_body(plan, *refs):
    state_refs, refs = refs[: plan.chunks], refs[plan.chunks :]
    intra_ref, query_ref, cum_col_ref, upstream_ref, gain_ref = refs[:5]
    attended_ref, sums_ref, states_ref = refs[5:]
    size, length = plan.size, query_ref.shape[0]
    for chunk, state_ref in enumerate(state_refs):
        for member in range(plan.members):
            states_ref[plan.chunk_of(member, chunk)] = state_ref[member].astype(BF16)
    growth = jnp.exp(cum_col_ref[...])
    square = jnp.zeros((length, size), F32)
    inner = jnp.zeros((length, size), F32)
    for h in range(plan.heads):
        cut = lanes(h, size)
        carried = dot(query_ref[:, cut], states_ref[cut])
        attended = intra_ref[:, cut] + growth[:, h : h + 1] * carried
        attended_ref[:, cut] = attended
        square += attended * attended
        inner += gain_ref[:, cut] * upstream_ref[:, cut].astype(F32) * attended
    ones = jnp.ones((1, size), F32)
    sums_ref[...] = jnp.concatenate(
        [exact_dot(ones, square, CONTRACT_COLS), exact_dot(ones, inner, CONTRACT_COLS)]
        + [jnp.zeros((6, length), F32)],
        axis=0,
    )


def attn_grad_body(plan, parties, *refs):
    sums_refs, refs = refs[:parties], refs[parties:]
    attended_ref, query_ref, cum_col_ref, upstream_ref, gain_ref = refs[:5]
    attn_grad_ref, send_ref = refs[5:]
    size = plan.size
    feature_count = plan.heads * size * parties
    sums = sum(ref[...] for ref in sums_refs)
    inv_row = lax.rsqrt(sums[:1] / feature_count + EPSILON)
    coefficient_row = sums[1:2] * inv_row * inv_row * inv_row / feature_count
    columns = jnp.transpose(
        jnp.concatenate([inv_row, coefficient_row, jnp.zeros_like(sums[2:])], axis=0)
    )
    inv_rms, coefficient = columns[:, :1], columns[:, 1:2]
    growth = jnp.exp(cum_col_ref[...])
    for h in range(plan.heads):
        cut = lanes(h, size)
        gained = gain_ref[:, cut] * upstream_ref[:, cut].astype(F32)
        attn_grad = (gained * inv_rms - attended_ref[:, cut] * coefficient).astype(BF16)
        attn_grad_ref[:, cut] = attn_grad
        query_decayed = (query_ref[:, cut].astype(F32) * growth[:, h : h + 1]).astype(BF16)
        member, place = divmod(h, plan.own)
        send_ref[member, lanes(place, size)] = dot(query_decayed, attn_grad, CONTRACT_ROWS)


def score_grad_body(
    plan,
    attn_grad_ref,
    query_ref,
    key_ref,
    value_ref,
    states_ref,
    weight_ref,
    cum_ref,
    cum_col_ref,
    query_grad_ref,
    key_part_ref,
    value_part_ref,
):
    causal = causal_mask(query_ref.shape[0])
    cum_col = cum_col_ref[...]
    growth = jnp.exp(cum_col)
    for h in range(plan.heads):
        cut = lanes(h, plan.size)
        attn_grad = attn_grad_ref[:, cut]
        scores = dot(attn_grad, value_ref[:, cut], CONTRACT_COLS)
        score_grad = (scores * decay_matrix(cum_ref, cum_col, causal, h)).astype(BF16)
        carried = dot(attn_grad, states_ref[cut], CONTRACT_COLS)
        query_grad = dot(score_grad, key_ref[:, cut]) + growth[:, h : h + 1] * carried
        query_grad_ref[:, cut] = query_grad.astype(BF16)
        key_part_ref[:, cut] = dot(score_grad, query_ref[:, cut], CONTRACT_ROWS)
        value_part_ref[:, cut] = dot(weight_ref[h], attn_grad, CONTRACT_ROWS)


def finish_body(plan, *refs):
    first_ref, second_ref, key_part_ref, value_part_ref, key_ref, value_ref, cum_col_ref = refs[:7]
    summary_ref, before_ref, key_grad_ref, value_grad_ref, total_ref, held_ref = refs[7:]
    length, size = key_ref.shape[0], plan.size
    swapped = jnp.where(plan.group() == 0, 0, 1) if plan.groups == 2 else 0
    held_ref[swapped] = first_ref[...]
    held_ref[1 - swapped] = second_ref[...]
    cum_col = cum_col_ref[...]
    block_log = cum_col[length - 1 : length, :]
    shrink = jnp.exp(block_log - cum_col)
    for h in range(plan.heads):
        cut = lanes(h, size)
        grads = held_ref[1, cut]
        scale = jnp.exp(before_ref[h : h + 1])
        scale_next = jnp.exp(before_ref[h : h + 1] + block_log[:, h : h + 1])
        total_ref[cut] = held_ref[0, cut] + scale * summary_ref[cut] + scale_next * grads
        grads = grads.astype(BF16)
        column = shrink[:, h : h + 1]
        key_state = dot(value_ref[:, cut], grads, CONTRACT_COLS)
        key_grad_ref[:, cut] = (key_part_ref[:, cut] + column * key_state).astype(BF16)
        value_state = dot(key_ref[:, cut], grads)
        value_grad_ref[:, cut] = (value_part_ref[:, cut] + column * value_state).astype(BF16)


def on_device(
    query_rows, key_rows, value_rows, log_decay, out_grad, norm_gain, state_in, state_out_grad
):
    heads, length = log_decay.shape
    size = state_in.shape[1]
    width = heads * size
    parties = lax.axis_size("head")
    plan = Plan(heads, size, lax.axis_size("seq"))
    bind = lambda body, *extra: functools.partial(body, plan, *extra)
    gain = norm_gain.reshape(1, width)
    chunk_piece = shaped((plan.chunk_rows, size))
    pieces = shaped((plan.members, plan.rows, size))
    chunk_pieces = shaped((plan.members, plan.chunk_rows, size))
    logged = shaped((plan.chunk_rows + LOG_ROWS, size))
    block_logs = shaped((plan.members, LOG_ROWS, size))
    group_logs = shaped((plan.groups, LOG_ROWS, size))
    table = shaped((length, width))
    rounded = shaped((length, width), BF16)
    hold_groups = pltpu.VMEM((plan.groups, plan.rows, size), F32)
    hold_chunk_groups = pltpu.VMEM((plan.groups, plan.chunk_rows, size), F32)
    chunks = range(plan.chunks)
    state_rows = state_in.reshape(width, size)

    *sends, cum_log, cum_col = call(
        bind(summary_body),
        [shaped((plan.members, plan.chunk_rows + LOG_ROWS, size))]
        + [chunk_pieces] * (plan.chunks - 1)
        + [shaped((heads, length)), shaped((length, heads))],
        [pltpu.with_memory_space_constraint(x, pltpu.HBM) for x in (key_rows, value_rows, log_decay)],
        [
            pltpu.VMEM((width, size), F32),
            pltpu.VMEM((length, width), BF16),
            pltpu.VMEM((length, width), BF16),
            pltpu.VMEM((heads, length), F32),
            pltpu.SemaphoreType.DMA((plan.members, 2)),
            pltpu.SemaphoreType.DMA,
        ],
        specs=[HBM] * 3,
    )
    parts = [plan.swap_in_group(send) for send in sends]
    weights, intra = call(
        bind(intra_body),
        [shaped((heads, length, length), BF16), table],
        [query_rows, key_rows, value_rows, cum_log, cum_col],
        flops=4 * heads * length * length * size,
    )
    totals = []
    for c in chunks:
        if c == 0:
            total, logs = call(bind(group_total_body, c), [logged, block_logs], [parts[c]])
        else:
            (total,) = call(bind(group_total_body, c), [chunk_piece], [parts[c], logs])
        totals.append([total] + plan.from_groups(total))
    states = []
    for c in chunks:
        operands = [parts[c], *totals[c], state_rows, logs]
        scratch = [hold_chunk_groups]
        if c == 0:
            send, before, all_logs = call(
                bind(forward_scan_body, c),
                [chunk_pieces, shaped((LOG_ROWS, size)), group_logs],
                operands,
                scratch,
            )
        else:
            (send,) = call(bind(forward_scan_body, c), [chunk_pieces], [*operands, all_logs], scratch)
        states.append(plan.swap_in_group(send))
    attended, sums, states = call(
        bind(attended_body),
        [table, shaped((8, length)), shaped((width, size), BF16)],
        [*states, intra, query_rows, cum_col, out_grad, gain],
    )
    all_sums = [sums] + [
        lax.ppermute(sums, "head", [(i, (i + step) % parties) for i in range(parties)])
        for step in range(1, parties)
    ]
    attn_grad, summary = call(
        bind(attn_grad_body, parties),
        [rounded, pieces],
        [*all_sums, attended, query_rows, cum_col, out_grad, gain],
    )
    parts = plan.swap_in_group(summary)
    query_grad, key_part, value_part = call(
        bind(score_grad_body),
        [rounded, table, table],
        [attn_grad, query_rows, key_rows, value_rows, states, weights, cum_log, cum_col],
        flops=10 * heads * length * length * size,
    )
    grad_rows = state_out_grad.reshape(width, size)
    two_sided = plan.groups == 2
    total, *sends = call(
        bind(group_grad_body),
        [shaped((plan.rows, size))] + [pieces] * two_sided,
        [parts, logs, grad_rows, key_part],
        specs=[VMEM] * 3 + [ANY],
    )
    totals = [total] + plan.from_groups(total)
    swapped = [plan.swap_in_group(send) for send in sends]
    sends = call(
        bind(reverse_scan_body),
        [pieces] * (1 if two_sided else 2),
        [parts, *totals, logs, all_logs, grad_rows],
        [hold_groups],
    )
    swapped += [plan.swap_in_group(send) for send in sends]
    key_grad, value_grad, state_in_grad = call(
        bind(finish_body),
        [rounded, rounded, shaped((width, size))],
        [
            *[x.reshape(width, size) for x in swapped],
            key_part,
            value_part,
            key_rows,
            value_rows,
            cum_col,
            summary.reshape(width, size),
            before,
        ],
        [pltpu.VMEM((2, width, size), F32)],
    )
    return (query_grad, key_grad, value_grad, state_in_grad.reshape(heads, size, size))


def solution(mesh):
    return jax.shard_map(
        on_device,
        mesh=mesh,
        in_specs=(
            P("seq", "head"),
            P("seq", "head"),
            P("seq", "head"),
            P("head", "seq"),
            P("seq", "head"),
            P("head"),
            P("head", None, None),
            P("head", None, None),
        ),
        out_specs=(P("seq", "head"), P("seq", "head"), P("seq", "head"), P("head", None, None)),
        check_vma=False,
    )
```

time: 68 us -> 105 us (1.54); the launches traced: 67.9 us -> 104 us
  blocking collectives: 0 us -> 24.4 us
  local copies, waits for them, and re-layouts: 0.03 us -> 14.1 us
  waiting for transfers between devices: 29.6 us -> 16.8 us
  Pallas kernels: 12.6 us -> 17.9 us
  starting transfers between devices: 24.9 us -> 29.7 us
    all_to_all x0 -> x2, blocking collectives: none -> 24.4 us  [swap_in_group(): return lax.all_to_all(pieces, 'seq', 0, 0, axis_index_groups=sets)]
    all_to_all x0 -> x5, starting transfers between devices: none -> 20.9 us  [swap_in_group(): return lax.all_to_all(pieces, 'seq', 0, 0, axis_index_groups=sets)]
    ppermute x15 -> x0, starting transfers between devices: 18.3 us -> none  [swap_in_group(): swapped.append(lax.ppermute(piece, 'seq', pairs))]
    ppermute x15 -> x0, waiting for transfers between devices: 17.3 us -> none  [swap_in_group(): swapped.append(lax.ppermute(piece, 'seq', pairs))]
    unnamed x14 -> x52, local copies, waits for them, and re-layouts: 0.03 us -> 14.1 us
    pallas_call x10 -> x12, Pallas kernels: 12.6 us -> 17.9 us  [call(): pl.pallas_call(body, out_shape=outs, in_specs=specs or [VMEM] * len(opera...]
    ppermute x2 -> x3, starting transfers between devices: 4.79 us -> 7.06 us  [from_groups(): lax.ppermute(piece, 'seq', [(i, (i + step * self.members) % self.blocks)...]
    ppermute x2 -> x3, waiting for transfers between devices: 9.48 us -> 11.7 us  [from_groups(): lax.ppermute(piece, 'seq', [(i, (i + step * self.members) % self.blocks)...]
  transfers between devices with their start and end apart: 20 -> 11, of which waited for: 16 -> 7; matrix products, arithmetic and copies ran while one was open for 0% -> 0% of each run, Pallas kernels for 7% -> 6%
where the time goes in v5:
time: 105 us; the launch traced here: 104 us
  starting transfers between devices  29.7 us (28%)
  blocking collectives  24.4 us (23%)
  Pallas kernels  17.9 us (17%)
  waiting for transfers between devices  16.8 us (16%)
  local copies, waits for them, and re-layouts  14.1 us (13%)
    all_to_all x2, blocking collectives, swap_in_group(): return lax.all_to_all(pieces, 'seq', 0, 0, axis_index_groups=sets)  24.4 us
    all_to_all x5, starting transfers between devices, swap_in_group(): return lax.all_to_all(pieces, 'seq', 0, 0, axis_index_groups=sets)  20.9 us
    pallas_call x12, Pallas kernels, call(): pl.pallas_call(body, out_shape=outs, in_specs=specs or [VMEM] * len(opera...  17.9 us
    unnamed x52, local copies, waits for them, and re-layouts  14.1 us
    ppermute x3, waiting for transfers between devices, from_groups(): lax.ppermute(piece, 'seq', [(i, (i + step * self.members) % self.blocks)...  11.7 us
    ppermute x3, starting transfers between devices, from_groups(): lax.ppermute(piece, 'seq', [(i, (i + step * self.members) % self.blocks)...  7.06 us
    ppermute x3, waiting for transfers between devices, on_device(): lax.ppermute(sums, 'head', [(i, (i + step) % parties) for i in range(part...  2.85 us
    all_to_all x5, waiting for transfers between devices, swap_in_group(): return lax.all_to_all(pieces, 'seq', 0, 0, axis_index_groups=sets)  2.22 us
  transfers between devices with their start and end apart: 11, of which 7 were waited for; matrix products, arithmetic and copies ran while one was open for 0% of the time, Pallas kernels for 6%

profile of v5, /device:TPU:0, one launch (start us, length us, event | category | flops | bytes accessed | tf_op | source)
XLA Modules:
  0.0 103.7 jit_solution(12785286159723568292)
XLA Ops:
  0.6 3.9 %shard_map.111 = (f32[4,136,128]{2,1,0:T(8,128)S(1)}, f32[4,128,128]{2,1,0:T(8,128)}, f32[8,256]{1,0:T(8,128)S(1)}, f32[256,8]{1,0:T(8,128)S(1)}) custom-call(bf16[256,1024]{1,0:T(8,128)(2,1)} %refs_4_.1, bf16[256,1024]{1,0:T(8,128)(2,1)} %refs_5_.5, f32[8,256]{1,0:T(8,128)} %decay_hbm.1), custom_call_target="tpu_custom_call" | custom-call | tf_op jit(solution)/shard_map/pallas_call | solution.py:24
  4.5 0.0 copy-start.19
  4.5 11.2 %all_to_all.35.parts_ref = f32[4,136,128]{2,1,0:T(8,128)S(1)} all-to-all(f32[4,136,128]{2,1,0:T(8,128)S(1)} %get-tuple-element.28), channel_id=1, replica_groups={{0,4,8,12},{16,20,24,28},{1,5,9,13},{17,21,25,29},{2,6,10,14},{18,22,26..., dimensions={0} | all-to-all | bytes 557056 | tf_op jit(solution)/shard_map/all_to_all | solution.py:85
  15.8 3.5 %all-to-all-start.2 = ((f32[4,128,128]{2,1,0:T(8,128)}), f32[4,128,128]{2,1,0:T(8,128)S(1)}, u32[]{:S(2)}, u32[]{:S(2)}) async-start(f32[4,128,128]{2,1,0:T(8,128)} %get-tuple-element.32), calls=%async_computation.2 | async-start | bytes 524288 | tf_op jit(solution)/shard_map/all_to_all | solution.py:85
  19.4 2.7 %collective-permute-start = (f32[136,128]{1,0:T(8,128)S(1)}, f32[136,128]{1,0:T(8,128)S(1)}, u32[]{:S(2)}, u32[]{:S(2)}) collective-permute-start(f32[136,128]{1,0:T(8,128)S(1)} %get-tuple-element.29.refs_0_), channel_id=1, source_target_pairs={{0,16},{4,20},{8,24},{12,28},{16,0},{20,4},{24,8},{28,12},{1,17},{... | collective-permute-start | bytes 208904 | tf_op jit(solution)/shard_map/ppermute | solution.py:89
  22.0 3.3 %collective-permute-done.refs_1_ = f32[136,128]{1,0:T(8,128)S(1)} collective-permute-done((f32[136,128]{1,0:T(8,128)S(1)}, f32[136,128]{1,0:T(8,128)S(1)}, u32[]{:S(2)}, u32[]{:S(2)}) %collective-permute-start) | collective-permute-done | bytes 69664 | tf_op jit(solution)/shard_map/ppermute | solution.py:89
  25.3 0.8 shard_map.113
  26.1 0.6 copy-done.24
  26.7 4.6 %all-to-all-start.1 = ((f32[4,128,128]{2,1,0:T(8,128)}), f32[4,128,128]{2,1,0:T(8,128)S(1)}, u32[]{:S(2)}, u32[]{:S(2)}) async-start(f32[4,128,128]{2,1,0:T(8,128)} %get-tuple-element.31), calls=%async_computation.1 | async-start | bytes 524288 | tf_op jit(solution)/shard_map/all_to_all | solution.py:85
  31.3 2.2 %collective-permute-start.1 = (f32[128,128]{1,0:T(8,128)S(1)}, f32[128,128]{1,0:T(8,128)S(1)}, u32[]{:S(2)}, u32[]{:S(2)}) collective-permute-start(f32[128,128]{1,0:T(8,128)S(1)} %shard_map.114.refs_0_), channel_id=1, source_target_pairs={{0,16},{4,20},{8,24},{12,28},{16,0},{20,4},{24,8},{28,12},{1,17},{... | collective-permute-start | bytes 196616 | tf_op jit(solution)/shard_map/ppermute | solution.py:89
  33.6 3.1 %collective-permute-done.1.refs_1_ = f32[128,128]{1,0:T(8,128)S(1)} collective-permute-done((f32[128,128]{1,0:T(8,128)S(1)}, f32[128,128]{1,0:T(8,128)S(1)}, u32[]{:S(2)}, u32[]{:S(2)}) %collective-permute-start.1) | collective-permute-done | bytes 65568 | tf_op jit(solution)/shard_map/ppermute | solution.py:89
  36.7 0.8 shard_map.115
  37.4 0.0 all-to-all-done.1.refs_0_
  37.4 5.0 %all-to-all-start.3 = ((f32[4,128,128]{2,1,0:T(8,128)}), f32[4,128,128]{2,1,0:T(8,128)}, u32[]{:S(2)}, u32[]{:S(2)}) async-start(f32[4,128,128]{2,1,0:T(8,128)} %shard_map.115), calls=%async_computation.3 | async-start | bytes 524288 | tf_op jit(solution)/shard_map/all_to_all | solution.py:85
  42.4 0.0 copy-start.20
  42.4 0.7 copy-done.20
  43.1 0.9 shard_map.116
  44.1 1.0 copy-done.7
  45.1 1.0 copy-done.9
  46.1 1.8 %all-to-all-done.3.refs_1_ = f32[4,128,128]{2,1,0:T(8,128)} async-done(((f32[4,128,128]{2,1,0:T(8,128)}), f32[4,128,128]{2,1,0:T(8,128)}, u32[]{:S(2)}, u32[]{:S(2)}) %all-to-all-start.3) | async-done | bytes 262176 | tf_op jit(solution)/shard_map/all_to_all | solution.py:85
  47.9 1.2 %copy-done.10 = f32[256,1024]{1,0:T(8,128)S(1)} copy-done((f32[256,1024]{1,0:T(8,128)S(1)}, f32[256,1024]{1,0:T(8,128)}, u32[]{:S(2)}) %copy-start.10) | copy-done | bytes 1048600
  49.1 0.7 copy-done.22
  49.8 1.8 %shard_map.117 = (f32[256,1024]{1,0:T(8,128)S(1)}, f32[8,256]{1,0:T(8,128)S(1)}, bf16[1024,128]{1,0:T(8,128)(2,1)S(1)}) custom-call(f32[4,128,128]{2,1,0:T(8,128)S(1)} %all-to-all-done.1.refs_0_, f32[4,128,128]{2,1,0:T(8,128)} %all-to-all-done.3.refs_1_, f32[256,1024]{1,0:T(8,128)S(1)} %copy-done.10, bf16[256,1024]{1,0:T(8,128)(2,1)S(1)} %copy-done, ...), custom_call_target="tpu_custom_call" | custom-call | tf_op jit(solution)/shard_map/pallas_call | solution.py:24
  51.6 0.7 copy-done.15
  52.3 1.5 %collective-permute-start.3 = (f32[8,256]{1,0:T(8,128)S(1)}, f32[8,256]{1,0:T(8,128)S(1)}, u32[]{:S(2)}, u32[]{:S(2)}) collective-permute-start(f32[8,256]{1,0:T(8,128)S(1)} %get-tuple-element.37.refs_0_), channel_id=1, source_target_pairs={{0,2},{1,3},{2,0},{3,1},{4,6},{5,7},{6,4},{7,5},{8,10},{9,11},{10,... | collective-permute-start | bytes 24584 | tf_op jit(solution)/shard_map/ppermute | solution.py:445
  53.8 0.2 collective-permute-start.2
  54.1 1.9 %collective-permute-done.3.refs_2_ = f32[8,256]{1,0:T(8,128)S(1)} collective-permute-done((f32[8,256]{1,0:T(8,128)S(1)}, f32[8,256]{1,0:T(8,128)S(1)}, u32[]{:S(2)}, u32[]{:S(2)}) %collective-permute-start.3) | collective-permute-done | bytes 8224 | tf_op jit(solution)/shard_map/ppermute | solution.py:445
  56.0 0.9 collective-permute-done.2.refs_1_
  56.9 2.1 %shard_map.118 = (bf16[256,1024]{1,0:T(8,128)(2,1)S(1)}, f32[4,256,128]{2,1,0:T(8,128)}) custom-call(f32[8,256]{1,0:T(8,128)S(1)} %get-tuple-element.37.refs_0_, f32[8,256]{1,0:T(8,128)S(1)} %collective-permute-done.2.refs_1_, f32[8,256]{1,0:T(8,128)S(1)} %collective-permute-done.3.refs_2_, f32[8,256]{1,0:T(8,128)S(1)} %collective-permute-done.4.refs_3_, ...), custom_call_target="tpu_custom_call" | custom-call | tf_op jit(solution)/shard_map/pallas_call | solution.py:24
  59.0 0.8 copy-done.13
  59.8 3.6 %all-to-all-start.4 = ((f32[4,256,128]{2,1,0:T(8,128)}), f32[4,256,128]{2,1,0:T(8,128)S(1)}, u32[]{:S(2)}, u32[]{:S(2)}) async-start(f32[4,256,128]{2,1,0:T(8,128)} %get-tuple-element.43), calls=%async_computation.4 | async-start | bytes 1048576 | tf_op jit(solution)/shard_map/all_to_all | solution.py:85
  63.5 1.2 %copy-done.8 = bf16[8,256,256]{2,1,0:T(8,128)(2,1)S(1)} copy-done((bf16[8,256,256]{2,1,0:T(8,128)(2,1)S(1)}, bf16[8,256,256]{2,1,0:T(8,128)(2,1)}, u32[]{:S(2)}) %copy-start.8) | copy-done | bytes 1048600
  64.7 1.0 %copy-done.14 = bf16[256,1024]{1,0:T(8,128)(2,1)S(1)} copy-done((bf16[256,1024]{1,0:T(8,128)(2,1)S(1)}, bf16[256,1024]{1,0:T(8,128)(2,1)}, u32[]{:S(2)}) %copy-start.14) | copy-done | bytes 524312
  65.7 0.7 copy-done.21
  66.4 3.4 %shard_map.119 = (bf16[256,1024]{1,0:T(8,128)(2,1)}, f32[256,1024]{1,0:T(8,128)S(1)}, f32[256,1024]{1,0:T(8,128)S(1)}) custom-call(bf16[256,1024]{1,0:T(8,128)(2,1)S(1)} %copy-done.14, bf16[256,1024]{1,0:T(8,128)(2,1)S(1)} %copy-done, bf16[256,1024]{1,0:T(8,128)(2,1)S(1)} %copy-done.1, bf16[256,1024]{1,0:T(8,128)(2,1)S(1)} %copy-done.2, ...), custom_call_target="tpu_custom_call" | custom-call | flops 671088640 | tf_op jit(solution)/shard_map/pallas_call | solution.py:24
  69.9 1.0 copy-done.11
  70.9 1.0 %copy-done.5 = f32[8,128,128]{2,1,0:T(8,128)S(1)} copy-done((f32[8,128,128]{2,1,0:T(8,128)S(1)}, f32[8,128,128]{2,1,0:T(8,128)}, u32[]{:S(2)}) %copy-start.5) | copy-done | bytes 524312
  71.9 0.9 shard_map.120
  72.8 4.2 %all-to-all-start.5 = ((f32[4,256,128]{2,1,0:T(8,128)}), f32[4,256,128]{2,1,0:T(8,128)}, u32[]{:S(2)}, u32[]{:S(2)}) async-start(f32[4,256,128]{2,1,0:T(8,128)} %get-tuple-element.45), calls=%async_computation.5 | async-start | bytes 1048576 | tf_op jit(solution)/shard_map/all_to_all | solution.py:85
  76.9 2.2 %collective-permute-start.5 = (f32[256,128]{1,0:T(8,128)S(1)}, f32[256,128]{1,0:T(8,128)S(1)}, u32[]{:S(2)}, u32[]{:S(2)}) collective-permute-start(f32[256,128]{1,0:T(8,128)S(1)} %get-tuple-element.46.refs_0_), channel_id=1, source_target_pairs={{0,16},{4,20},{8,24},{12,28},{16,0},{20,4},{24,8},{28,12},{1,17},{... | collective-permute-start | bytes 393224 | tf_op jit(solution)/shard_map/ppermute | solution.py:89
  79.1 5.3 %collective-permute-done.5.refs_1_ = f32[256,128]{1,0:T(8,128)S(1)} collective-permute-done((f32[256,128]{1,0:T(8,128)S(1)}, f32[256,128]{1,0:T(8,128)S(1)}, u32[]{:S(2)}, u32[]{:S(2)}) %collective-permute-start.5) | collective-permute-done | bytes 131104 | tf_op jit(solution)/shard_map/ppermute | solution.py:89
  84.4 1.0 %copy-done.6 = f32[8,128,128]{2,1,0:T(8,128)S(1)} copy-done((f32[8,128,128]{2,1,0:T(8,128)S(1)}, f32[8,128,128]{2,1,0:T(8,128)}, u32[]{:S(2)}) %copy-start.6) | copy-done | bytes 524312
  85.5 0.7 copy-done.18
  86.1 0.2 shard_map.121
  86.3 0.4 all-to-all-done.5
  86.7 13.2 %all_to_all.36 = f32[4,256,128]{2,1,0:T(8,128)S(1)} all-to-all(f32[4,256,128]{2,1,0:T(8,128)S(1)} %shard_map.121), channel_id=1, replica_groups={{0,4,8,12},{16,20,24,28},{1,5,9,13},{17,21,25,29},{2,6,10,14},{18,22,26..., dimensions={0} | all-to-all | bytes 1048576 | tf_op jit(solution)/shard_map/all_to_all | solution.py:85
  99.9 0.7 copy-done.25
  100.6 3.1 %shard_map.122 = (bf16[256,1024]{1,0:T(8,128)(2,1)}, bf16[256,1024]{1,0:T(8,128)(2,1)}, f32[1024,128]{1,0:T(8,128)}) custom-call(f32[1024,128]{1,0:T(8,128)} %bitcast.3.refs_0_, f32[1024,128]{1,0:T(8,128)S(1)} %bitcast.11, f32[256,1024]{1,0:T(8,128)S(1)} %get-tuple-element.44._.refs_2_, f32[256,1024]{1,0:T(8,128)S(1)} %copy-done.12, ...), custom_call_target="tpu_custom_call" | custom-call | tf_op jit(solution)/shard_map/pallas_call | solution.py:24
  (40 shorter events, 0.1 us)
Async XLA Ops:
  4.5 11.2 %copy-start.19 = (f32[8,256]{1,0:T(8,128)}, f32[8,256]{1,0:T(8,128)S(1)}, u32[]{:S(2)}) copy-start(f32[8,256]{1,0:T(8,128)S(1)} %get-tuple-element.34.cum_ref) | copy-start | bytes 24580
  15.8 9.6 %copy-start.3 = (f32[8,128,128]{2,1,0:T(8,128)S(1)}, f32[8,128,128]{2,1,0:T(8,128)}, u32[]{:S(2)}) copy-start(f32[8,128,128]{2,1,0:T(8,128)} %param.14) | copy-start | bytes 1572868
  15.8 10.9 %all-to-all-start.2 = ((f32[4,128,128]{2,1,0:T(8,128)}), f32[4,128,128]{2,1,0:T(8,128)S(1)}, u32[]{:S(2)}, u32[]{:S(2)}) async-start(f32[4,128,128]{2,1,0:T(8,128)} %get-tuple-element.32), calls=%async_computation.2 | async-start | bytes 524288 | tf_op jit(solution)/shard_map/all_to_all | solution.py:85
  19.4 6.0 %collective-permute-start = (f32[136,128]{1,0:T(8,128)S(1)}, f32[136,128]{1,0:T(8,128)S(1)}, u32[]{:S(2)}, u32[]{:S(2)}) collective-permute-start(f32[136,128]{1,0:T(8,128)S(1)} %get-tuple-element.29.refs_0_), channel_id=1, source_target_pairs={{0,16},{4,20},{8,24},{12,28},{16,0},{20,4},{24,8},{28,12},{1,17},{... | collective-permute-start | bytes 208904 | tf_op jit(solution)/shard_map/ppermute | solution.py:89
  26.1 0.6 copy-start.24
  26.7 10.0 %copy-start.17 = (f32[2,8,128]{2,1,0:T(8,128)}, f32[2,8,128]{2,1,0:T(8,128)S(1)}, u32[]{:S(2)}) copy-start(f32[2,8,128]{2,1,0:T(8,128)S(1)} %get-tuple-element.33.refs_4_.refs_3_) | copy-start | bytes 24580
  26.7 10.8 %all-to-all-start.1 = ((f32[4,128,128]{2,1,0:T(8,128)}), f32[4,128,128]{2,1,0:T(8,128)S(1)}, u32[]{:S(2)}, u32[]{:S(2)}) async-start(f32[4,128,128]{2,1,0:T(8,128)} %get-tuple-element.31), calls=%async_computation.1 | async-start | bytes 524288 | tf_op jit(solution)/shard_map/all_to_all | solution.py:85
  31.3 5.3 %collective-permute-start.1 = (f32[128,128]{1,0:T(8,128)S(1)}, f32[128,128]{1,0:T(8,128)S(1)}, u32[]{:S(2)}, u32[]{:S(2)}) collective-permute-start(f32[128,128]{1,0:T(8,128)S(1)} %shard_map.114.refs_0_), channel_id=1, source_target_pairs={{0,16},{4,20},{8,24},{12,28},{16,0},{20,4},{24,8},{28,12},{1,17},{... | collective-permute-start | bytes 196616 | tf_op jit(solution)/shard_map/ppermute | solution.py:89
  36.7 5.7 %copy-start.1 = (bf16[256,1024]{1,0:T(8,128)(2,1)S(1)}, bf16[256,1024]{1,0:T(8,128)(2,1)}, u32[]{:S(2)}) copy-start(bf16[256,1024]{1,0:T(8,128)(2,1)} %refs_4_.1) | copy-start | bytes 1572868
  36.7 5.7 %copy-start.2 = (bf16[256,1024]{1,0:T(8,128)(2,1)S(1)}, bf16[256,1024]{1,0:T(8,128)(2,1)}, u32[]{:S(2)}) copy-start(bf16[256,1024]{1,0:T(8,128)(2,1)} %refs_5_.5) | copy-start | bytes 1572868
  37.4 5.0 %copy-start = (bf16[256,1024]{1,0:T(8,128)(2,1)S(1)}, bf16[256,1024]{1,0:T(8,128)(2,1)}, u32[]{:S(2)}) copy-start(bf16[256,1024]{1,0:T(8,128)(2,1)} %query_ref.3) | copy-start | bytes 1572868
  37.4 10.4 %all-to-all-start.3 = ((f32[4,128,128]{2,1,0:T(8,128)}), f32[4,128,128]{2,1,0:T(8,128)}, u32[]{:S(2)}, u32[]{:S(2)}) async-start(f32[4,128,128]{2,1,0:T(8,128)} %shard_map.115), calls=%async_computation.3 | async-start | bytes 524288 | tf_op jit(solution)/shard_map/all_to_all | solution.py:85
  42.4 0.7 copy-start.20
  43.1 4.8 %copy-start.4 = (bf16[256,1024]{1,0:T(8,128)(2,1)S(1)}, bf16[256,1024]{1,0:T(8,128)(2,1)}, u32[]{:S(2)}) copy-start(bf16[256,1024]{1,0:T(8,128)(2,1)} %refs_7_.1) | copy-start | bytes 1572868
  44.1 1.0 copy-start.7
  45.1 1.0 copy-start.9
  47.9 1.2 %copy-start.10 = (f32[256,1024]{1,0:T(8,128)S(1)}, f32[256,1024]{1,0:T(8,128)}, u32[]{:S(2)}) copy-start(f32[256,1024]{1,0:T(8,128)} %copy-done.9) | copy-start | bytes 3145732
  49.1 0.7 copy-start.22
  49.8 7.1 %copy-start.23 = (f32[1024]{0:T(1024)S(1)}, f32[1024]{0:T(1024)}, u32[]{:S(2)}) copy-start(f32[1024]{0:T(1024)} %param.13) | copy-start | bytes 12292
  51.6 0.7 copy-start.15
  52.3 1.8 %collective-permute-start.4 = (f32[8,256]{1,0:T(8,128)S(1)}, f32[8,256]{1,0:T(8,128)S(1)}, u32[]{:S(2)}, u32[]{:S(2)}) collective-permute-start(f32[8,256]{1,0:T(8,128)S(1)} %get-tuple-element.37.refs_0_), channel_id=1, source_target_pairs={{0,3},{1,0},{2,1},{3,2},{4,7},{5,4},{6,5},{7,6},{8,11},{9,8},{10,9... | collective-permute-start | bytes 24584 | tf_op jit(solution)/shard_map/ppermute | solution.py:445
  52.3 3.7 %collective-permute-start.3 = (f32[8,256]{1,0:T(8,128)S(1)}, f32[8,256]{1,0:T(8,128)S(1)}, u32[]{:S(2)}, u32[]{:S(2)}) collective-permute-start(f32[8,256]{1,0:T(8,128)S(1)} %get-tuple-element.37.refs_0_), channel_id=1, source_target_pairs={{0,2},{1,3},{2,0},{3,1},{4,6},{5,7},{6,4},{7,5},{8,10},{9,11},{10,... | collective-permute-start | bytes 24584 | tf_op jit(solution)/shard_map/ppermute | solution.py:445
  53.8 3.1 %collective-permute-start.2 = (f32[8,256]{1,0:T(8,128)S(1)}, f32[8,256]{1,0:T(8,128)S(1)}, u32[]{:S(2)}, u32[]{:S(2)}) collective-permute-start(f32[8,256]{1,0:T(8,128)S(1)} %get-tuple-element.37.refs_0_), channel_id=1, source_target_pairs={{0,1},{1,2},{2,3},{3,0},{4,5},{5,6},{6,7},{7,4},{8,9},{9,10},{10,1... | collective-permute-start | bytes 24584 | tf_op jit(solution)/shard_map/ppermute | solution.py:445
  59.0 0.8 copy-start.13
  59.8 3.6 %copy-start.16 = (bf16[1024,128]{1,0:T(8,128)(2,1)S(1)}, bf16[1024,128]{1,0:T(8,128)(2,1)}, u32[]{:S(2)}) copy-start(bf16[1024,128]{1,0:T(8,128)(2,1)} %copy-done.15) | copy-start | bytes 786436
  59.8 11.0 %all-to-all-start.4 = ((f32[4,256,128]{2,1,0:T(8,128)}), f32[4,256,128]{2,1,0:T(8,128)S(1)}, u32[]{:S(2)}, u32[]{:S(2)}) async-start(f32[4,256,128]{2,1,0:T(8,128)} %get-tuple-element.43), calls=%async_computation.4 | async-start | bytes 1048576 | tf_op jit(solution)/shard_map/all_to_all | solution.py:85
  63.4 1.2 %copy-start.8 = (bf16[8,256,256]{2,1,0:T(8,128)(2,1)S(1)}, bf16[8,256,256]{2,1,0:T(8,128)(2,1)}, u32[]{:S(2)}) copy-start(bf16[8,256,256]{2,1,0:T(8,128)(2,1)} %copy-done.7) | copy-start | bytes 3145732
  64.7 1.0 %copy-start.14 = (bf16[256,1024]{1,0:T(8,128)(2,1)S(1)}, bf16[256,1024]{1,0:T(8,128)(2,1)}, u32[]{:S(2)}) copy-start(bf16[256,1024]{1,0:T(8,128)(2,1)} %copy-done.13) | copy-start | bytes 1572868
  65.7 0.7 copy-start.21
  69.9 1.0 copy-start.11
  70.9 1.0 %copy-start.5 = (f32[8,128,128]{2,1,0:T(8,128)S(1)}, f32[8,128,128]{2,1,0:T(8,128)}, u32[]{:S(2)}) copy-start(f32[8,128,128]{2,1,0:T(8,128)} %param.15) | copy-start | bytes 1572868
  72.8 13.9 %all-to-all-start.5 = ((f32[4,256,128]{2,1,0:T(8,128)}), f32[4,256,128]{2,1,0:T(8,128)}, u32[]{:S(2)}, u32[]{:S(2)}) async-start(f32[4,256,128]{2,1,0:T(8,128)} %get-tuple-element.45), calls=%async_computation.5 | async-start | bytes 1048576 | tf_op jit(solution)/shard_map/all_to_all | solution.py:85
  76.9 7.5 %collective-permute-start.5 = (f32[256,128]{1,0:T(8,128)S(1)}, f32[256,128]{1,0:T(8,128)S(1)}, u32[]{:S(2)}, u32[]{:S(2)}) collective-permute-start(f32[256,128]{1,0:T(8,128)S(1)} %get-tuple-element.46.refs_0_), channel_id=1, source_target_pairs={{0,16},{4,20},{8,24},{12,28},{16,0},{20,4},{24,8},{28,12},{1,17},{... | collective-permute-start | bytes 393224 | tf_op jit(solution)/shard_map/ppermute | solution.py:89
  84.4 1.0 %copy-start.6 = (f32[8,128,128]{2,1,0:T(8,128)S(1)}, f32[8,128,128]{2,1,0:T(8,128)}, u32[]{:S(2)}) copy-start(f32[8,128,128]{2,1,0:T(8,128)} %param.15) | copy-start | bytes 1572868
  85.5 0.7 copy-start.18
  86.7 13.2 %copy-start.12 = (f32[256,1024]{1,0:T(8,128)S(1)}, f32[256,1024]{1,0:T(8,128)}, u32[]{:S(2)}) copy-start(f32[256,1024]{1,0:T(8,128)} %copy-done.11) | copy-start | bytes 3145732
  99.9 0.7 copy-start.25

commit v6 on v4

--- a/solution.py
+++ b/solution.py
@@ -11,6 +11,7 @@
 F32 = jnp.float32
 BF16 = jnp.bfloat16
 LOG_ROWS = 8
+LONG = 10**10
 MASKED = -1e30
 
 CONTRACT_ROWS = (((0,), (0,)), ((), ()))
@@ -21,7 +22,6 @@
 
 
 def call(body, outs, operands, scratch=(), flops=0, specs=None):
-    size = sum(x.size * x.dtype.itemsize for x in (*operands, *outs))
     return pl.pallas_call(
         body,
         out_shape=outs,
@@ -29,7 +29,7 @@
         out_specs=[VMEM] * len(outs),
         scratch_shapes=list(scratch),
         compiler_params=pltpu.CompilerParams(vmem_limit_bytes=24 * 1024 * 1024),
-        cost_estimate=pl.CostEstimate(flops=flops, bytes_accessed=size, transcendentals=0),
+        cost_estimate=pl.CostEstimate(flops=flops, bytes_accessed=0, transcendentals=0),
     )(*operands)
 
 
@@ -64,6 +64,8 @@
         self.groups = blocks // self.members
         self.own = heads // self.members
         self.rows = self.own * size
+        self.chunks = self.own
+        self.chunk_rows = self.rows // self.chunks
         self.ways = sorted(range(self.members), key=lambda way: (way > 0, -way.bit_count()))
 
     def member(self):
@@ -77,6 +79,10 @@
 
     def rows_of(self, member):
         return pl.ds(pl.multiple_of(member * self.rows, self.rows), self.rows)
+
+    def chunk_of(self, member, chunk):
+        start = member * self.rows + chunk * self.chunk_rows
+        return pl.ds(pl.multiple_of(start, self.chunk_rows), self.chunk_rows)
 
     def swap_in_group(self, pieces):
         span = self.members
@@ -97,14 +103,15 @@
         ]
 
 
-def own_decays(plan, log_tile_ref, base):
-    first = base + plan.member() * plan.own
-    rows = [log_tile_ref[pl.ds(first + j, 1), :] for j in range(plan.own)]
+def own_decays(plan, log_tile_ref, chunk=None):
+    count = plan.own if chunk is None else plan.own // plan.chunks
+    first = plan.member() * plan.own + (0 if chunk is None else chunk * count)
+    rows = [log_tile_ref[pl.ds(first + j, 1), :] for j in range(count)]
     return jnp.concatenate([jnp.broadcast_to(jnp.exp(row), (plan.size, plan.size)) for row in rows])
 
 
 def summary_body(plan, key_hbm, value_hbm, decay_hbm, *refs):
-    send_refs, refs = refs[: plan.members], refs[plan.members :]
+    send_refs, refs = refs[: plan.members * plan.chunks], refs[plan.members * plan.chunks :]
     cum_ref, cum_col_ref, held_ref, key_ref, value_ref, decay_ref, sems, decay_sem = refs
     length, heads, size = key_ref.shape[0], plan.heads, plan.size
     decay_copy = pltpu.make_async_copy(decay_hbm, decay_ref, decay_sem)
@@ -140,60 +147,77 @@
     log_tile = jnp.broadcast_to(cum_row[:, length - 1 : length], (heads, size))
     if heads < LOG_ROWS:
         log_tile = jnp.concatenate([log_tile, jnp.zeros((LOG_ROWS - heads, size), F32)])
-    for k, send_ref in enumerate(send_refs):
-        send_ref[: plan.rows] = held_ref[plan.rows_of(plan.peer(k))]
-        send_ref[plan.rows :] = log_tile
-
-
-def group_total_body(plan, *refs):
-    part_refs, (total_ref, logs_ref, held_ref) = refs[: plan.members], refs[plan.members :]
+    for i, send_ref in enumerate(send_refs):
+        chunk, k = divmod(i, plan.members)
+        send_ref[: plan.chunk_rows] = held_ref[plan.chunk_of(plan.peer(k), chunk)]
+        if chunk == 0:
+            send_ref[plan.chunk_rows :] = log_tile
+
+
+def group_total_body(plan, chunk, *refs):
+    part_refs, refs = refs[: plan.members], refs[plan.members :]
+    rows = plan.chunk_rows
+    if chunk == 0:
+        total_ref, logs_ref = refs[:2]
+        for k, part_ref in enumerate(part_refs):
+            logs_ref[plan.peer(k)] = part_ref[rows:]
+        total_ref[rows:] = sum(logs_ref[b] for b in range(plan.members))
+    else:
+        logs_ref, total_ref = refs[:2]
+    held_ref = refs[2]
     for k, part_ref in enumerate(part_refs):
-        held_ref[plan.peer(k)] = part_ref[...]
-    total = jnp.zeros((plan.rows, plan.size), F32)
-    log_total = jnp.zeros((LOG_ROWS, plan.size), F32)
+        held_ref[plan.peer(k)] = part_ref[:rows]
+    total = jnp.zeros((rows, plan.size), F32)
     for b in range(plan.members):
-        total = own_decays(plan, held_ref.at[b], plan.rows) * total + held_ref[b, : plan.rows]
-        logs_ref[b] = held_ref[b, plan.rows :]
-        log_total += held_ref[b, plan.rows :]
-    total_ref[: plan.rows] = total
-    total_ref[plan.rows :] = log_total
+        total = own_decays(plan, logs_ref.at[b], chunk) * total + held_ref[b]
+    total_ref[:rows] = total
 
 
 def stage_groups(plan, total_refs, held_ref):
+    rows = held_ref.shape[1]
     for step, total_ref in enumerate(total_refs):
-        held_ref[lax.rem(plan.group() - step + plan.groups, plan.groups)] = total_ref[...]
-
-
-def forward_scan_body(plan, *refs):
+        held_ref[lax.rem(plan.group() - step + plan.groups, plan.groups)] = total_ref[:rows]
+
+
+def forward_scan_body(plan, chunk, *refs):
     part_refs, refs = refs[: plan.members], refs[plan.members :]
     total_refs, refs = refs[: plan.groups], refs[plan.groups :]
-    state_ref, refs = refs[0], refs[1:]
-    send_refs, (before_ref, groups_ref, held_ref) = refs[: plan.members], refs[plan.members :]
+    rows = plan.chunk_rows
+    if chunk == 0:
+        (state_ref, logs_ref), refs = refs[:2], refs[2:]
+        send_refs, (before_ref, group_logs_ref, groups_ref, held_ref) = refs[:-4], refs[-4:]
+        for step, total_ref in enumerate(total_refs):
+            group = lax.rem(plan.group() - step + plan.groups, plan.groups)
+            group_logs_ref[group] = total_ref[rows:]
+        before = jnp.zeros((LOG_ROWS, plan.size), F32)
+        for group in range(plan.groups - 1):
+            before += jnp.where(group < plan.group(), group_logs_ref[group], 0.0)
+        for b in range(plan.members - 1):
+            before += jnp.where(b < plan.member(), logs_ref[b], 0.0)
+        before_ref[...] = before
+    else:
+        (state_ref, logs_ref, group_logs_ref), refs = refs[:3], refs[3:]
+        send_refs, (groups_ref, held_ref) = refs[:-2], refs[-2:]
     stage_groups(plan, total_refs, groups_ref)
-    before = jnp.zeros((LOG_ROWS, plan.size), F32)
-    state = state_ref[plan.rows_of(plan.member())]
+    state = state_ref[plan.chunk_of(plan.member(), chunk)]
     for group in range(plan.groups - 1):
-        after = own_decays(plan, groups_ref.at[group], plan.rows) * state + groups_ref[group, : plan.rows]
+        after = own_decays(plan, group_logs_ref.at[group], chunk) * state + groups_ref[group]
         state = jnp.where(group < plan.group(), after, state)
-        before += jnp.where(group < plan.group(), groups_ref[group, plan.rows :], 0.0)
     for k, part_ref in enumerate(part_refs):
-        held_ref[plan.peer(k)] = part_ref[...]
+        held_ref[plan.peer(k)] = part_ref[:rows]
     for b in range(plan.members):
-        summary = held_ref[b, : plan.rows]
-        decays = own_decays(plan, held_ref.at[b], plan.rows)
-        held_ref[b, : plan.rows] = state
-        state = decays * state + summary
-        before += jnp.where(b < plan.member(), held_ref[b, plan.rows :], 0.0)
-    before_ref[...] = before
+        summary = held_ref[b]
+        held_ref[b] = state
+        state = own_decays(plan, logs_ref.at[b], chunk) * state + summary
     for k, send_ref in enumerate(send_refs):
-        send_ref[...] = held_ref[plan.peer(k), : plan.rows]
+        send_ref[...] = held_ref[plan.peer(k)]
 
 
 def suffixes(plan, held_ref, logs_ref, grad):
     found = []
     for b in reversed(range(plan.members)):
         found.append(grad)
-        grad = own_decays(plan, logs_ref.at[b], 0) * grad + held_ref[b]
+        grad = own_decays(plan, logs_ref.at[b]) * grad + held_ref[b]
     return found[::-1], grad
 
 
@@ -202,7 +226,7 @@
     for b in range(plan.members):
         found.append(total)
         total = total + scale * held_ref[b]
-        scale = scale * own_decays(plan, logs_ref.at[b], 0)
+        scale = scale * own_decays(plan, logs_ref.at[b])
     return found
 
 
@@ -213,8 +237,7 @@
     for k, part_ref in enumerate(part_refs):
         held_ref[plan.peer(k)] = part_ref[...]
     zero = jnp.zeros((plan.rows, plan.size), F32)
-    total_ref[: plan.rows] = suffixes(plan, held_ref, logs_ref, zero)[1]
-    total_ref[plan.rows :] = sum(logs_ref[b] for b in range(plan.members))
+    total_ref[...] = suffixes(plan, held_ref, logs_ref, zero)[1]
     if send_refs:
         first = plan.group() == 0
         before = prefixes(plan, held_ref, logs_ref, zero, zero + 1.0)
@@ -228,7 +251,7 @@
 def reverse_scan_body(plan, *refs):
     part_refs, refs = refs[: plan.members], refs[plan.members :]
     total_refs, refs = refs[: plan.groups], refs[plan.groups :]
-    (logs_ref, grad_ref), refs = refs[:2], refs[2:]
+    (logs_ref, group_logs_ref, grad_ref), refs = refs[:3], refs[3:]
     send_refs, (groups_ref, held_ref) = refs[:-2], refs[-2:]
     stage_groups(plan, total_refs, groups_ref)
     for k, part_ref in enumerate(part_refs):
@@ -237,13 +260,13 @@
     leaving = grad
     for group in reversed(range(plan.groups)):
         leaving = jnp.where(group == plan.group(), grad, leaving)
-        grad = own_decays(plan, groups_ref.at[group], plan.rows) * grad + groups_ref[group, : plan.rows]
+        grad = own_decays(plan, group_logs_ref.at[group]) * grad + groups_ref[group]
     total = jnp.zeros((plan.rows, plan.size), F32)
     scale = total + 1.0
     for group in range(plan.groups - 1):
         earlier = group < plan.group()
-        total = jnp.where(earlier, total + scale * groups_ref[group, : plan.rows], total)
-        decays = own_decays(plan, groups_ref.at[group], plan.rows)
+        total = jnp.where(earlier, total + scale * groups_ref[group], total)
+        decays = own_decays(plan, group_logs_ref.at[group])
         scale = jnp.where(earlier, scale * decays, scale)
     after = suffixes(plan, held_ref, logs_ref, leaving)[0]
     before = prefixes(plan, held_ref, logs_ref, total, scale)
@@ -275,17 +298,14 @@
         intra_ref[:, cut] = dot(weights, value_ref[:, cut])
 
 
-def gather_rounded(plan, piece_refs, whole_ref):
-    for k, piece_ref in enumerate(piece_refs):
-        whole_ref[plan.rows_of(plan.peer(k))] = piece_ref[...].astype(BF16)
-
-
 def attended_body(plan, *refs):
-    state_refs, refs = refs[: plan.members], refs[plan.members :]
+    state_refs, refs = refs[: plan.members * plan.chunks], refs[plan.members * plan.chunks :]
     intra_ref, query_ref, cum_col_ref, upstream_ref, gain_ref = refs[:5]
     attended_ref, sums_ref, states_ref = refs[5:]
     size, length = plan.size, query_ref.shape[0]
-    gather_rounded(plan, state_refs, states_ref)
+    for i, state_ref in enumerate(state_refs):
+        chunk, k = divmod(i, plan.members)
+        states_ref[plan.chunk_of(plan.peer(k), chunk)] = state_ref[...].astype(BF16)
     growth = jnp.exp(cum_col_ref[...])
     square = jnp.zeros((length, size), F32)
     inner = jnp.zeros((length, size), F32)
@@ -396,21 +416,29 @@
     bind = lambda body, *extra: functools.partial(body, plan, *extra)
     gain = norm_gain.reshape(1, width)
     piece = shaped((plan.rows, size))
-    logged = shaped((plan.rows + LOG_ROWS, size))
     pieces = [piece] * plan.members
+    chunk_piece = shaped((plan.chunk_rows, size))
+    chunk_pieces = [chunk_piece] * plan.members
+    logged = shaped((plan.chunk_rows + LOG_ROWS, size))
+    block_logs = shaped((plan.members, LOG_ROWS, size))
+    group_logs = shaped((plan.groups, LOG_ROWS, size))
     table = shaped((length, width))
     rounded = shaped((length, width), BF16)
     hold = pltpu.VMEM((plan.members, plan.rows, size), F32)
-    hold_logged = pltpu.VMEM((plan.members, plan.rows + LOG_ROWS, size), F32)
-    hold_groups = pltpu.VMEM((plan.groups, plan.rows + LOG_ROWS, size), F32)
-    hold_whole = pltpu.VMEM((width, size), F32)
+    hold_groups = pltpu.VMEM((plan.groups, plan.rows, size), F32)
+    hold_chunk = pltpu.VMEM((plan.members, plan.chunk_rows, size), F32)
+    hold_chunk_groups = pltpu.VMEM((plan.groups, plan.chunk_rows, size), F32)
+    chunks = range(plan.chunks)
+    state_rows = state_in.reshape(width, size)
 
     *sends, cum_log, cum_col = call(
         bind(summary_body),
-        [logged] * plan.members + [shaped((heads, length)), shaped((length, heads))],
+        [logged] * plan.members
+        + chunk_pieces * (plan.chunks - 1)
+        + [shaped((heads, length)), shaped((length, heads))],
         [pltpu.with_memory_space_constraint(x, pltpu.HBM) for x in (key_rows, value_rows, log_decay)],
         [
-            hold_whole,
+            pltpu.VMEM((width, size), F32),
             pltpu.VMEM((length, width), BF16),
             pltpu.VMEM((length, width), BF16),
             pltpu.VMEM((heads, length), F32),
@@ -419,27 +447,44 @@
         ],
         specs=[HBM] * 3,
     )
-    parts = plan.swap_in_group(sends)
+    parts = [
+        plan.swap_in_group(sends[c * plan.members : (c + 1) * plan.members]) for c in chunks
+    ]
     weights, intra = call(
         bind(intra_body),
         [shaped((heads, length, length), BF16), table],
         [query_rows, key_rows, value_rows, cum_log, cum_col],
         flops=4 * heads * length * length * size,
     )
-    total, logs = call(
-        bind(group_total_body),
-        [logged, shaped((plan.members, LOG_ROWS, size))],
-        parts,
-        [hold_logged],
-    )
-    totals = [total] + plan.from_groups(total)
-    *sends, before = call(
-        bind(forward_scan_body),
-        pieces + [shaped((LOG_ROWS, size))],
-        [*parts, *totals, state_in.reshape(width, size)],
-        [hold_groups, hold_logged],
-    )
-    states = plan.swap_in_group(sends)
+    totals = []
+    for c in chunks:
+        if c == 0:
+            total, logs = call(
+                bind(group_total_body, c), [logged, block_logs], parts[c], [hold_chunk]
+            )
+        else:
+            (total,) = call(
+                bind(group_total_body, c),
+                [chunk_piece],
+                [*parts[c], logs],
+                [hold_chunk],
+                flops=LONG,
+            )
+        totals.append([total] + plan.from_groups(total))
+    states = []
+    for c in chunks:
+        operands = [*parts[c], *totals[c], state_rows, logs]
+        scratch = [hold_chunk_groups, hold_chunk]
+        if c == 0:
+            *sends, before, all_logs = call(
+                bind(forward_scan_body, c),
+                chunk_pieces + [shaped((LOG_ROWS, size)), group_logs],
+                operands,
+                scratch,
+            )
+        else:
+            sends = call(bind(forward_scan_body, c), chunk_pieces, [*operands, all_logs], scratch)
+        states += plan.swap_in_group(sends)
     attended, sums, states = call(
         bind(attended_body),
         [table, shaped((8, length)), shaped((width, size), BF16)],
@@ -465,7 +510,7 @@
     two_sided = plan.groups == 2
     total, *sends = call(
         bind(group_grad_body),
-        [logged] + pieces * two_sided,
+        [piece] + pieces * two_sided,
         [*parts, logs, grad_rows, key_part],
         [hold],
         specs=[VMEM] * (plan.members + 2) + [ANY],
@@ -475,7 +520,7 @@
     sends = call(
         bind(reverse_scan_body),
         pieces * (1 if two_sided else 2),
-        [*parts, *totals, logs, grad_rows],
+        [*parts, *totals, logs, all_logs, grad_rows],
         [hold_groups, hold],
     )
     for first in range(0, len(sends), plan.members):

time: 68 us -> 64.1 us (0.943)
  waiting for transfers between devices: 29.6 us -> 13.6 us
  starting transfers between devices: 24.9 us -> 36.9 us
    ppermute x15 -> x21, starting transfers between devices: 18.3 us -> 27.2 us  [swap_in_group(): swapped.append(lax.ppermute(piece, 'seq', pairs))]
    ppermute x15 -> x21, waiting for transfers between devices: 17.3 us -> 8.68 us  [swap_in_group(): swapped.append(lax.ppermute(piece, 'seq', pairs))]
    ppermute x2 -> x3, waiting for transfers between devices: 9.48 us -> 2.12 us  [from_groups(): lax.ppermute(piece, 'seq', [(i, (i + step * self.members) % self.blocks)...]
    ppermute x2 -> x3, starting transfers between devices: 4.79 us -> 7.94 us  [from_groups(): lax.ppermute(piece, 'seq', [(i, (i + step * self.members) % self.blocks)...]
    pallas_call x10 -> x12, Pallas kernels: 12.6 us -> 12.5 us  [call(): pl.pallas_call(body, out_shape=outs, in_specs=specs or [VMEM] * len(opera...]
  transfers between devices with their start and end apart: 20 -> 27, of which waited for: 16 -> 18; matrix products, arithmetic and copies ran while one was open for 0% -> 0% of each run, Pallas kernels for 7% -> 8%
where the time goes in v6:
time: 64.1 us; the launch traced here: 63.9 us
  starting transfers between devices  36.9 us (58%)
  waiting for transfers between devices  13.6 us (21%)
  Pallas kernels  12.5 us (20%)
  between operations  0.76 us (1%)
    ppermute x21, starting transfers between devices, swap_in_group(): swapped.append(lax.ppermute(piece, 'seq', pairs))  27.2 us
    pallas_call x12, Pallas kernels, call(): pl.pallas_call(body, out_shape=outs, in_specs=specs or [VMEM] * len(opera...  12.5 us
    ppermute x21, waiting for transfers between devices, swap_in_group(): swapped.append(lax.ppermute(piece, 'seq', pairs))  8.68 us
    ppermute x3, starting transfers between devices, from_groups(): lax.ppermute(piece, 'seq', [(i, (i + step * self.members) % self.blocks)...  7.94 us
    ppermute x3, waiting for transfers between devices, on_device(): lax.ppermute(sums, 'head', [(i, (i + step) % parties) for i in range(part...  2.85 us
    ppermute x3, waiting for transfers between devices, from_groups(): lax.ppermute(piece, 'seq', [(i, (i + step * self.members) % self.blocks)...  2.12 us
    ppermute x3, starting transfers between devices, on_device(): lax.ppermute(sums, 'head', [(i, (i + step) % parties) for i in range(part...  1.75 us
  transfers between devices with their start and end apart: 27, of which 18 were waited for; matrix products, arithmetic and copies ran while one was open for 0% of the time, Pallas kernels for 8%

profile of v6, /device:TPU:0, one launch (start us, length us, event | category | flops | bytes accessed | tf_op | source)
XLA Modules:
  0.0 63.9 jit_solution(2405108513874477300)
XLA Ops:
  0.6 3.2 %shard_map.111 = (f32[136,128]{1,0:T(8,128)S(1)}, f32[136,128]{1,0:T(8,128)S(1)}, f32[136,128]{1,0:T(8,128)S(1)}, f32[136,128]{1,0:T(8,128)S(1)}, f32[128,128]{1...) custom-call(bf16[256,1024]{1,0:T(8,128)(2,1)} %refs_10_.1, ...), custom_call_target="tpu_custom_call" | custom-call | tf_op jit(solution)/shard_map/pallas_call | solution.py:25
  3.9 4.0 %collective-permute-start = (f32[136,128]{1,0:T(8,128)S(1)}, f32[136,128]{1,0:T(8,128)S(1)}, u32[]{:S(2)}, u32[]{:S(2)}) collective-permute-start(f32[136,128]{1,0:T(8,128)S(1)} %get-tuple-element.53), channel_id=1, source_target_pairs={{0,12},{4,8},{8,4},{12,0},{16,28},{20,24},{24,20},{28,16},{1,13},{... | collective-permute-start | bytes 208904 | tf_op jit(solution)/shard_map/ppermute | solution.py:92
  7.9 0.5 collective-permute-start.1
  8.5 2.8 %collective-permute-start.7 = (f32[128,128]{1,0:T(8,128)S(1)}, f32[128,128]{1,0:T(8,128)S(1)}, u32[]{:S(2)}, u32[]{:S(2)}) collective-permute-start(f32[128,128]{1,0:T(8,128)S(1)} %get-tuple-element.63), channel_id=1, source_target_pairs={{0,12},{4,8},{8,4},{12,0},{16,28},{20,24},{24,20},{28,16},{1,13},{... | collective-permute-start | bytes 196616 | tf_op jit(solution)/shard_map/ppermute | solution.py:92
  11.4 0.5 collective-permute-start.8
  11.9 0.7 %collective-permute-start.9 = (f32[128,128]{1,0:T(8,128)S(1)}, f32[128,128]{1,0:T(8,128)S(1)}, u32[]{:S(2)}, u32[]{:S(2)}) collective-permute-start(f32[128,128]{1,0:T(8,128)S(1)} %get-tuple-element.65), channel_id=1, source_target_pairs={{0,8},{4,12},{8,0},{12,4},{16,24},{20,28},{24,16},{28,20},{1,9},{5... | collective-permute-start | bytes 196616 | tf_op jit(solution)/shard_map/ppermute | solution.py:92
  12.6 0.4 collective-permute-done.1.refs_2_
  13.1 2.6 %collective-permute-start.3 = (f32[136,128]{1,0:T(8,128)S(1)}, f32[136,128]{1,0:T(8,128)S(1)}, u32[]{:S(2)}, u32[]{:S(2)}) collective-permute-start(f32[136,128]{1,0:T(8,128)S(1)} %get-tuple-element.56.refs_4_), channel_id=1, source_target_pairs={{0,16},{4,20},{8,24},{12,28},{16,0},{20,4},{24,8},{28,12},{1,17},{... | collective-permute-start | bytes 208904 | tf_op jit(solution)/shard_map/ppermute | solution.py:97
  15.7 0.5 collective-permute-done.9.refs_3_
  16.3 2.6 %collective-permute-start.10 = (f32[128,128]{1,0:T(8,128)S(1)}, f32[128,128]{1,0:T(8,128)S(1)}, u32[]{:S(2)}, u32[]{:S(2)}) collective-permute-start(f32[128,128]{1,0:T(8,128)S(1)} %shard_map.114.refs_4_), channel_id=1, source_target_pairs={{0,16},{4,20},{8,24},{12,28},{16,0},{20,4},{24,8},{28,12},{1,17},{... | collective-permute-start | bytes 196616 | tf_op jit(solution)/shard_map/ppermute | solution.py:97
  18.9 1.6 %collective-permute-done.3.refs_5_ = f32[136,128]{1,0:T(8,128)S(1)} collective-permute-done((f32[136,128]{1,0:T(8,128)S(1)}, f32[136,128]{1,0:T(8,128)S(1)}, u32[]{:S(2)}, u32[]{:S(2)}) %collective-permute-start.3) | collective-permute-done | bytes 69664 | tf_op jit(solution)/shard_map/ppermute | solution.py:97
  20.6 0.9 %collective-permute-start.4 = (f32[128,128]{1,0:T(8,128)S(1)}, f32[128,128]{1,0:T(8,128)S(1)}, u32[]{:S(2)}, u32[]{:S(2)}) collective-permute-start(f32[128,128]{1,0:T(8,128)S(1)} %get-tuple-element.59), channel_id=1, source_target_pairs={{0,12},{4,8},{8,4},{12,0},{16,28},{20,24},{24,20},{28,16},{1,13},{... | collective-permute-start | bytes 196616 | tf_op jit(solution)/shard_map/ppermute | solution.py:92
  21.4 0.6 collective-permute-start.5
  22.0 2.1 %collective-permute-start.6 = (f32[128,128]{1,0:T(8,128)S(1)}, f32[128,128]{1,0:T(8,128)S(1)}, u32[]{:S(2)}, u32[]{:S(2)}) collective-permute-start(f32[128,128]{1,0:T(8,128)S(1)} %get-tuple-element.61), channel_id=1, source_target_pairs={{0,8},{4,12},{8,0},{12,4},{16,24},{20,28},{24,16},{28,20},{1,9},{5... | collective-permute-start | bytes 196616 | tf_op jit(solution)/shard_map/ppermute | solution.py:92
  24.2 0.9 %collective-permute-start.11 = (f32[128,128]{1,0:T(8,128)S(1)}, f32[128,128]{1,0:T(8,128)S(1)}, u32[]{:S(2)}, u32[]{:S(2)}) collective-permute-start(f32[128,128]{1,0:T(8,128)S(1)} %get-tuple-element.68), channel_id=1, source_target_pairs={{0,12},{4,8},{8,4},{12,0},{16,28},{20,24},{24,20},{28,16},{1,13},{... | collective-permute-start | bytes 196616 | tf_op jit(solution)/shard_map/ppermute | solution.py:92
  25.1 0.7 %collective-permute-start.12 = (f32[128,128]{1,0:T(8,128)S(1)}, f32[128,128]{1,0:T(8,128)S(1)}, u32[]{:S(2)}, u32[]{:S(2)}) collective-permute-start(f32[128,128]{1,0:T(8,128)S(1)} %get-tuple-element.69), channel_id=1, source_target_pairs={{0,4},{4,0},{8,12},{12,8},{16,20},{20,16},{24,28},{28,24},{1,5},{5... | collective-permute-start | bytes 196616 | tf_op jit(solution)/shard_map/ppermute | solution.py:92
  25.7 0.4 collective-permute-done.4.refs_1_
  26.1 1.6 %collective-permute-start.13 = (f32[128,128]{1,0:T(8,128)S(1)}, f32[128,128]{1,0:T(8,128)S(1)}, u32[]{:S(2)}, u32[]{:S(2)}) collective-permute-start(f32[128,128]{1,0:T(8,128)S(1)} %get-tuple-element.70), channel_id=1, source_target_pairs={{0,8},{4,12},{8,0},{12,4},{16,24},{20,28},{24,16},{28,20},{1,9},{5... | collective-permute-start | bytes 196616 | tf_op jit(solution)/shard_map/ppermute | solution.py:92
  27.8 0.9 %shard_map.116 = (bf16[8,256,256]{2,1,0:T(8,128)(2,1)S(1)}, f32[256,1024]{1,0:T(8,128)S(1)}) custom-call(bf16[256,1024]{1,0:T(8,128)(2,1)S(1)} %copy-done, bf16[256,1024]{1,0:T(8,128)(2,1)S(1)} %copy-done.1, bf16[256,1024]{1,0:T(8,128)(2,1)S(1)} %copy-done.2, f32[8,256]{1,0:T(8,128)S(1)} %get-tuple-element.71.cum_ref, ...), custom_call_target="tpu_custom_call" | custom-call | flops 268435456 | tf_op jit(solution)/shard_map/pallas_call | solution.py:25
  28.8 0.8 %collective-permute-done.11.refs_5_ = f32[128,128]{1,0:T(8,128)S(1)} collective-permute-done((f32[128,128]{1,0:T(8,128)S(1)}, f32[128,128]{1,0:T(8,128)S(1)}, u32[]{:S(2)}, u32[]{:S(2)}) %collective-permute-start.11) | collective-permute-done | bytes 65568 | tf_op jit(solution)/shard_map/ppermute | solution.py:92
  29.5 0.5 collective-permute-done.12.refs_6_
  30.1 0.4 collective-permute-done.13.refs_7_
  30.4 0.8 %shard_map.117 = (f32[256,1024]{1,0:T(8,128)S(1)}, f32[8,256]{1,0:T(8,128)S(1)}, bf16[1024,128]{1,0:T(8,128)(2,1)S(1)}) custom-call(f32[128,128]{1,0:T(8,128)S(1)} %get-tuple-element.58.refs_0_, f32[128,128]{1,0:T(8,128)S(1)} %collective-permute-done.4.refs_1_, f32[128,128]{1,0:T(8,128)S(1)} %collective-permute-done.5.refs_2_, ...), custom_call_target="tpu_custom_call" | custom-call | tf_op jit(solution)/shard_map/pallas_call | solution.py:25
  31.2 1.5 %collective-permute-start.15 = (f32[8,256]{1,0:T(8,128)S(1)}, f32[8,256]{1,0:T(8,128)S(1)}, u32[]{:S(2)}, u32[]{:S(2)}) collective-permute-start(f32[8,256]{1,0:T(8,128)S(1)} %get-tuple-element.74.refs_0_), channel_id=1, source_target_pairs={{0,2},{1,3},{2,0},{3,1},{4,6},{5,7},{6,4},{7,5},{8,10},{9,11},{10,... | collective-permute-start | bytes 24584 | tf_op jit(solution)/shard_map/ppermute | solution.py:494
  32.8 0.2 collective-permute-start.14
  33.0 1.9 %collective-permute-done.15.refs_2_ = f32[8,256]{1,0:T(8,128)S(1)} collective-permute-done((f32[8,256]{1,0:T(8,128)S(1)}, f32[8,256]{1,0:T(8,128)S(1)}, u32[]{:S(2)}, u32[]{:S(2)}) %collective-permute-start.15) | collective-permute-done | bytes 8224 | tf_op jit(solution)/shard_map/ppermute | solution.py:494
  34.9 0.9 %collective-permute-done.14.refs_1_ = f32[8,256]{1,0:T(8,128)S(1)} collective-permute-done((f32[8,256]{1,0:T(8,128)S(1)}, f32[8,256]{1,0:T(8,128)S(1)}, u32[]{:S(2)}, u32[]{:S(2)}) %collective-permute-start.14) | collective-permute-done | bytes 8224 | tf_op jit(solution)/shard_map/ppermute | solution.py:494
  35.8 1.4 %shard_map.118 = (bf16[256,1024]{1,0:T(8,128)(2,1)S(1)}, f32[1024,128]{1,0:T(8,128)S(1)}, f32[256,128]{1,0:T(8,128)S(1)}, f32[256,128]{1,0:T(8,128)S(1)}, f32[25...) custom-call(f32[8,256]{1,0:T(8,128)S(1)} %get-tuple-element.74.refs_0_, f32[8,256]{1,0:T(8,128)S(1)} %collective-permute-done.14.refs_1_, ...), custom_call_target="tpu_custom_call" | custom-call | tf_op jit(solution)/shard_map/pallas_call | solution.py:25
  37.2 2.2 %collective-permute-start.17 = (f32[256,128]{1,0:T(8,128)S(1)}, f32[256,128]{1,0:T(8,128)S(1)}, u32[]{:S(2)}, u32[]{:S(2)}) collective-permute-start(f32[256,128]{1,0:T(8,128)S(1)} %get-tuple-element.81), channel_id=1, source_target_pairs={{0,12},{4,8},{8,4},{12,0},{16,28},{20,24},{24,20},{28,16},{1,13},{... | collective-permute-start | bytes 393224 | tf_op jit(solution)/shard_map/ppermute | solution.py:92
  39.5 0.9 %collective-permute-start.18 = (f32[256,128]{1,0:T(8,128)S(1)}, f32[256,128]{1,0:T(8,128)S(1)}, u32[]{:S(2)}, u32[]{:S(2)}) collective-permute-start(f32[256,128]{1,0:T(8,128)S(1)} %get-tuple-element.82), channel_id=1, source_target_pairs={{0,4},{4,0},{8,12},{12,8},{16,20},{20,16},{24,28},{28,24},{1,5},{5... | collective-permute-start | bytes 393224 | tf_op jit(solution)/shard_map/ppermute | solution.py:92
  40.4 0.4 collective-permute-start.19
  40.8 3.5 %shard_map.119 = (bf16[256,1024]{1,0:T(8,128)(2,1)}, f32[256,1024]{1,0:T(8,128)S(1)}, f32[256,1024]{1,0:T(8,128)S(1)}) custom-call(bf16[256,1024]{1,0:T(8,128)(2,1)S(1)} %get-tuple-element.76.attn_grad_ref, bf16[256,1024]{1,0:T(8,128)(2,1)S(1)} %copy-done, bf16[256,1024]{1,0:T(8,128)(2,1)S(1)} %copy-done.1, bf16[256,1024]{1,0:T(8,128)(2,1)S(1)} %copy-done.2, ...), custom_call_target="tpu_custom_call" | custom-call | flops 671088640 | tf_op jit(solution)/shard_map/pallas_call | solution.py:25
  44.4 0.9 %collective-permute-done.18.refs_2_ = f32[256,128]{1,0:T(8,128)S(1)} collective-permute-done((f32[256,128]{1,0:T(8,128)S(1)}, f32[256,128]{1,0:T(8,128)S(1)}, u32[]{:S(2)}, u32[]{:S(2)}) %collective-permute-start.18) | collective-permute-done | bytes 131104 | tf_op jit(solution)/shard_map/ppermute | solution.py:92
  45.6 2.7 %collective-permute-start.23 = (f32[256,128]{1,0:T(8,128)S(1)}, f32[256,128]{1,0:T(8,128)S(1)}, u32[]{:S(2)}, u32[]{:S(2)}) collective-permute-start(f32[256,128]{1,0:T(8,128)S(1)} %get-tuple-element.89.refs_4_), channel_id=1, source_target_pairs={{0,16},{4,20},{8,24},{12,28},{16,0},{20,4},{24,8},{28,12},{1,17},{... | collective-permute-start | bytes 393224 | tf_op jit(solution)/shard_map/ppermute | solution.py:97
  48.3 1.6 %collective-permute-start.20 = (f32[256,128]{1,0:T(8,128)S(1)}, f32[256,128]{1,0:T(8,128)S(1)}, u32[]{:S(2)}, u32[]{:S(2)}) collective-permute-start(f32[256,128]{1,0:T(8,128)S(1)} %get-tuple-element.86), channel_id=1, source_target_pairs={{0,12},{4,8},{8,4},{12,0},{16,28},{20,24},{24,20},{28,16},{1,13},{... | collective-permute-start | bytes 393224 | tf_op jit(solution)/shard_map/ppermute | solution.py:92
  49.9 0.7 %collective-permute-start.21 = (f32[256,128]{1,0:T(8,128)S(1)}, f32[256,128]{1,0:T(8,128)S(1)}, u32[]{:S(2)}, u32[]{:S(2)}) collective-permute-start(f32[256,128]{1,0:T(8,128)S(1)} %get-tuple-element.87), channel_id=1, source_target_pairs={{0,4},{4,0},{8,12},{12,8},{16,20},{20,16},{24,28},{28,24},{1,5},{5... | collective-permute-start | bytes 393224 | tf_op jit(solution)/shard_map/ppermute | solution.py:92
  50.6 1.2 %collective-permute-start.22 = (f32[256,128]{1,0:T(8,128)S(1)}, f32[256,128]{1,0:T(8,128)S(1)}, u32[]{:S(2)}, u32[]{:S(2)}) collective-permute-start(f32[256,128]{1,0:T(8,128)S(1)} %get-tuple-element.88), channel_id=1, source_target_pairs={{0,8},{4,12},{8,0},{12,4},{16,24},{20,28},{24,16},{28,20},{1,9},{5... | collective-permute-start | bytes 393224 | tf_op jit(solution)/shard_map/ppermute | solution.py:92
  51.8 0.6 collective-permute-done.23.refs_5_
  52.4 0.2 shard_map.121
  52.6 2.0 %collective-permute-start.24 = (f32[256,128]{1,0:T(8,128)S(1)}, f32[256,128]{1,0:T(8,128)S(1)}, u32[]{:S(2)}, u32[]{:S(2)}) collective-permute-start(f32[256,128]{1,0:T(8,128)S(1)} %get-tuple-element.91), channel_id=1, source_target_pairs={{0,12},{4,8},{8,4},{12,0},{16,28},{20,24},{24,20},{28,16},{1,13},{... | collective-permute-start | bytes 393224 | tf_op jit(solution)/shard_map/ppermute | solution.py:92
  54.6 1.0 %collective-permute-start.25 = (f32[256,128]{1,0:T(8,128)S(1)}, f32[256,128]{1,0:T(8,128)S(1)}, u32[]{:S(2)}, u32[]{:S(2)}) collective-permute-start(f32[256,128]{1,0:T(8,128)S(1)} %get-tuple-element.92), channel_id=1, source_target_pairs={{0,4},{4,0},{8,12},{12,8},{16,20},{20,16},{24,28},{28,24},{1,5},{5... | collective-permute-start | bytes 393224 | tf_op jit(solution)/shard_map/ppermute | solution.py:92
  55.6 0.4 collective-permute-done.20.refs_1_
  56.0 1.7 %collective-permute-start.26 = (f32[256,128]{1,0:T(8,128)S(1)}, f32[256,128]{1,0:T(8,128)S(1)}, u32[]{:S(2)}, u32[]{:S(2)}) collective-permute-start(f32[256,128]{1,0:T(8,128)S(1)} %get-tuple-element.93), channel_id=1, source_target_pairs={{0,8},{4,12},{8,0},{12,4},{16,24},{20,28},{24,16},{28,20},{1,9},{5... | collective-permute-start | bytes 393224 | tf_op jit(solution)/shard_map/ppermute | solution.py:92
  57.7 1.1 %collective-permute-done.21.refs_2_ = f32[256,128]{1,0:T(8,128)S(1)} collective-permute-done((f32[256,128]{1,0:T(8,128)S(1)}, f32[256,128]{1,0:T(8,128)S(1)}, u32[]{:S(2)}, u32[]{:S(2)}) %collective-permute-start.21) | collective-permute-done | bytes 131104 | tf_op jit(solution)/shard_map/ppermute | solution.py:92
  58.7 2.4 %collective-permute-done.24.refs_5_ = f32[256,128]{1,0:T(8,128)S(1)} collective-permute-done((f32[256,128]{1,0:T(8,128)S(1)}, f32[256,128]{1,0:T(8,128)S(1)}, u32[]{:S(2)}, u32[]{:S(2)}) %collective-permute-start.24) | collective-permute-done | bytes 131104 | tf_op jit(solution)/shard_map/ppermute | solution.py:92
  61.1 0.4 collective-permute-done.25.refs_6_
  61.5 0.4 collective-permute-done.26.refs_7_
  61.9 2.0 %shard_map.122 = (bf16[256,1024]{1,0:T(8,128)(2,1)}, bf16[256,1024]{1,0:T(8,128)(2,1)}, f32[1024,128]{1,0:T(8,128)}) custom-call(f32[256,128]{1,0:T(8,128)S(1)} %get-tuple-element.85.refs_0_, f32[256,128]{1,0:T(8,128)S(1)} %collective-permute-done.20.refs_1_, f32[256,128]{1,0:T(8,128)S(1)} %collective-permute-done.21.refs_2_, ...), custom_call_target="tpu_custom_call" | custom-call | tf_op jit(solution)/shard_map/pallas_call | solution.py:25
  (32 shorter events, 0.9 us)
Async XLA Ops:
  3.9 8.0 %collective-permute-start = (f32[136,128]{1,0:T(8,128)S(1)}, f32[136,128]{1,0:T(8,128)S(1)}, u32[]{:S(2)}, u32[]{:S(2)}) collective-permute-start(f32[136,128]{1,0:T(8,128)S(1)} %get-tuple-element.53), channel_id=1, source_target_pairs={{0,12},{4,8},{8,4},{12,0},{16,28},{20,24},{24,20},{28,16},{1,13},{... | collective-permute-start | bytes 208904 | tf_op jit(solution)/shard_map/ppermute | solution.py:92
  7.9 5.1 %collective-permute-start.1 = (f32[136,128]{1,0:T(8,128)S(1)}, f32[136,128]{1,0:T(8,128)S(1)}, u32[]{:S(2)}, u32[]{:S(2)}) collective-permute-start(f32[136,128]{1,0:T(8,128)S(1)} %get-tuple-element.54), channel_id=1, source_target_pairs={{0,4},{4,0},{8,12},{12,8},{16,20},{20,16},{24,28},{28,24},{1,5},{5... | collective-permute-start | bytes 208904 | tf_op jit(solution)/shard_map/ppermute | solution.py:92
  8.4 4.6 %collective-permute-start.2 = (f32[136,128]{1,0:T(8,128)S(1)}, f32[136,128]{1,0:T(8,128)S(1)}, u32[]{:S(2)}, u32[]{:S(2)}) collective-permute-start(f32[136,128]{1,0:T(8,128)S(1)} %get-tuple-element.55), channel_id=1, source_target_pairs={{0,8},{4,12},{8,0},{12,4},{16,24},{20,28},{24,16},{28,20},{1,9},{5... | collective-permute-start | bytes 208904 | tf_op jit(solution)/shard_map/ppermute | solution.py:92
  8.5 7.2 %collective-permute-start.7 = (f32[128,128]{1,0:T(8,128)S(1)}, f32[128,128]{1,0:T(8,128)S(1)}, u32[]{:S(2)}, u32[]{:S(2)}) collective-permute-start(f32[128,128]{1,0:T(8,128)S(1)} %get-tuple-element.63), channel_id=1, source_target_pairs={{0,12},{4,8},{8,4},{12,0},{16,28},{20,24},{24,20},{28,16},{1,13},{... | collective-permute-start | bytes 196616 | tf_op jit(solution)/shard_map/ppermute | solution.py:92
  11.4 4.3 %collective-permute-start.8 = (f32[128,128]{1,0:T(8,128)S(1)}, f32[128,128]{1,0:T(8,128)S(1)}, u32[]{:S(2)}, u32[]{:S(2)}) collective-permute-start(f32[128,128]{1,0:T(8,128)S(1)} %get-tuple-element.64), channel_id=1, source_target_pairs={{0,4},{4,0},{8,12},{12,8},{16,20},{20,16},{24,28},{28,24},{1,5},{5... | collective-permute-start | bytes 196616 | tf_op jit(solution)/shard_map/ppermute | solution.py:92
  11.9 4.3 %collective-permute-start.9 = (f32[128,128]{1,0:T(8,128)S(1)}, f32[128,128]{1,0:T(8,128)S(1)}, u32[]{:S(2)}, u32[]{:S(2)}) collective-permute-start(f32[128,128]{1,0:T(8,128)S(1)} %get-tuple-element.65), channel_id=1, source_target_pairs={{0,8},{4,12},{8,0},{12,4},{16,24},{20,28},{24,16},{28,20},{1,9},{5... | collective-permute-start | bytes 196616 | tf_op jit(solution)/shard_map/ppermute | solution.py:92
  13.1 7.4 %collective-permute-start.3 = (f32[136,128]{1,0:T(8,128)S(1)}, f32[136,128]{1,0:T(8,128)S(1)}, u32[]{:S(2)}, u32[]{:S(2)}) collective-permute-start(f32[136,128]{1,0:T(8,128)S(1)} %get-tuple-element.56.refs_4_), channel_id=1, source_target_pairs={{0,16},{4,20},{8,24},{12,28},{16,0},{20,4},{24,8},{28,12},{1,17},{... | collective-permute-start | bytes 208904 | tf_op jit(solution)/shard_map/ppermute | solution.py:97
  16.2 4.2 %copy-start.3 = (f32[8,128,128]{2,1,0:T(8,128)S(1)}, f32[8,128,128]{2,1,0:T(8,128)}, u32[]{:S(2)}) copy-start(f32[8,128,128]{2,1,0:T(8,128)} %param.14) | copy-start | bytes 1572868
  16.3 7.8 %collective-permute-start.10 = (f32[128,128]{1,0:T(8,128)S(1)}, f32[128,128]{1,0:T(8,128)S(1)}, u32[]{:S(2)}, u32[]{:S(2)}) collective-permute-start(f32[128,128]{1,0:T(8,128)S(1)} %shard_map.114.refs_4_), channel_id=1, source_target_pairs={{0,16},{4,20},{8,24},{12,28},{16,0},{20,4},{24,8},{28,12},{1,17},{... | collective-permute-start | bytes 196616 | tf_op jit(solution)/shard_map/ppermute | solution.py:97
  20.4 7.3 %copy-start.1 = (bf16[256,1024]{1,0:T(8,128)(2,1)S(1)}, bf16[256,1024]{1,0:T(8,128)(2,1)}, u32[]{:S(2)}) copy-start(bf16[256,1024]{1,0:T(8,128)(2,1)} %refs_10_.1) | copy-start | bytes 1572868
  20.4 7.3 %copy-start.2 = (bf16[256,1024]{1,0:T(8,128)(2,1)S(1)}, bf16[256,1024]{1,0:T(8,128)(2,1)}, u32[]{:S(2)}) copy-start(bf16[256,1024]{1,0:T(8,128)(2,1)} %refs_11_.3) | copy-start | bytes 1572868
  20.5 7.2 %copy-start = (bf16[256,1024]{1,0:T(8,128)(2,1)S(1)}, bf16[256,1024]{1,0:T(8,128)(2,1)}, u32[]{:S(2)}) copy-start(bf16[256,1024]{1,0:T(8,128)(2,1)} %query_ref.3) | copy-start | bytes 1572868
  20.6 5.6 %collective-permute-start.4 = (f32[128,128]{1,0:T(8,128)S(1)}, f32[128,128]{1,0:T(8,128)S(1)}, u32[]{:S(2)}, u32[]{:S(2)}) collective-permute-start(f32[128,128]{1,0:T(8,128)S(1)} %get-tuple-element.59), channel_id=1, source_target_pairs={{0,12},{4,8},{8,4},{12,0},{16,28},{20,24},{24,20},{28,16},{1,13},{... | collective-permute-start | bytes 196616 | tf_op jit(solution)/shard_map/ppermute | solution.py:92
  21.4 7.3 %collective-permute-start.5 = (f32[128,128]{1,0:T(8,128)S(1)}, f32[128,128]{1,0:T(8,128)S(1)}, u32[]{:S(2)}, u32[]{:S(2)}) collective-permute-start(f32[128,128]{1,0:T(8,128)S(1)} %get-tuple-element.60), channel_id=1, source_target_pairs={{0,4},{4,0},{8,12},{12,8},{16,20},{20,16},{24,28},{28,24},{1,5},{5... | collective-permute-start | bytes 196616 | tf_op jit(solution)/shard_map/ppermute | solution.py:92
  22.0 6.7 %collective-permute-start.6 = (f32[128,128]{1,0:T(8,128)S(1)}, f32[128,128]{1,0:T(8,128)S(1)}, u32[]{:S(2)}, u32[]{:S(2)}) collective-permute-start(f32[128,128]{1,0:T(8,128)S(1)} %get-tuple-element.61), channel_id=1, source_target_pairs={{0,8},{4,12},{8,0},{12,4},{16,24},{20,28},{24,16},{28,20},{1,9},{5... | collective-permute-start | bytes 196616 | tf_op jit(solution)/shard_map/ppermute | solution.py:92
  24.2 5.3 %collective-permute-start.11 = (f32[128,128]{1,0:T(8,128)S(1)}, f32[128,128]{1,0:T(8,128)S(1)}, u32[]{:S(2)}, u32[]{:S(2)}) collective-permute-start(f32[128,128]{1,0:T(8,128)S(1)} %get-tuple-element.68), channel_id=1, source_target_pairs={{0,12},{4,8},{8,4},{12,0},{16,28},{20,24},{24,20},{28,16},{1,13},{... | collective-permute-start | bytes 196616 | tf_op jit(solution)/shard_map/ppermute | solution.py:92
  25.1 5.0 %collective-permute-start.12 = (f32[128,128]{1,0:T(8,128)S(1)}, f32[128,128]{1,0:T(8,128)S(1)}, u32[]{:S(2)}, u32[]{:S(2)}) collective-permute-start(f32[128,128]{1,0:T(8,128)S(1)} %get-tuple-element.69), channel_id=1, source_target_pairs={{0,4},{4,0},{8,12},{12,8},{16,20},{20,16},{24,28},{28,24},{1,5},{5... | collective-permute-start | bytes 196616 | tf_op jit(solution)/shard_map/ppermute | solution.py:92
  26.1 4.3 %collective-permute-start.13 = (f32[128,128]{1,0:T(8,128)S(1)}, f32[128,128]{1,0:T(8,128)S(1)}, u32[]{:S(2)}, u32[]{:S(2)}) collective-permute-start(f32[128,128]{1,0:T(8,128)S(1)} %get-tuple-element.70), channel_id=1, source_target_pairs={{0,8},{4,12},{8,0},{12,4},{16,24},{20,28},{24,16},{28,20},{1,9},{5... | collective-permute-start | bytes 196616 | tf_op jit(solution)/shard_map/ppermute | solution.py:92
  27.8 2.6 %copy-start.4 = (bf16[256,1024]{1,0:T(8,128)(2,1)S(1)}, bf16[256,1024]{1,0:T(8,128)(2,1)}, u32[]{:S(2)}) copy-start(bf16[256,1024]{1,0:T(8,128)(2,1)} %refs_7_.1) | copy-start | bytes 1572868
  28.7 1.7 %copy-start.6 = (f32[1024]{0:T(1024)S(1)}, f32[1024]{0:T(1024)}, u32[]{:S(2)}) copy-start(f32[1024]{0:T(1024)} %param.13) | copy-start | bytes 12292
  31.2 1.8 %collective-permute-start.16 = (f32[8,256]{1,0:T(8,128)S(1)}, f32[8,256]{1,0:T(8,128)S(1)}, u32[]{:S(2)}, u32[]{:S(2)}) collective-permute-start(f32[8,256]{1,0:T(8,128)S(1)} %get-tuple-element.74.refs_0_), channel_id=1, source_target_pairs={{0,3},{1,0},{2,1},{3,2},{4,7},{5,4},{6,5},{7,6},{8,11},{9,8},{10,9... | collective-permute-start | bytes 24584 | tf_op jit(solution)/shard_map/ppermute | solution.py:494
  31.2 3.7 %collective-permute-start.15 = (f32[8,256]{1,0:T(8,128)S(1)}, f32[8,256]{1,0:T(8,128)S(1)}, u32[]{:S(2)}, u32[]{:S(2)}) collective-permute-start(f32[8,256]{1,0:T(8,128)S(1)} %get-tuple-element.74.refs_0_), channel_id=1, source_target_pairs={{0,2},{1,3},{2,0},{3,1},{4,6},{5,7},{6,4},{7,5},{8,10},{9,11},{10,... | collective-permute-start | bytes 24584 | tf_op jit(solution)/shard_map/ppermute | solution.py:494
  32.8 3.1 %collective-permute-start.14 = (f32[8,256]{1,0:T(8,128)S(1)}, f32[8,256]{1,0:T(8,128)S(1)}, u32[]{:S(2)}, u32[]{:S(2)}) collective-permute-start(f32[8,256]{1,0:T(8,128)S(1)} %get-tuple-element.74.refs_0_), channel_id=1, source_target_pairs={{0,1},{1,2},{2,3},{3,0},{4,5},{5,6},{6,7},{7,4},{8,9},{9,10},{10,1... | collective-permute-start | bytes 24584 | tf_op jit(solution)/shard_map/ppermute | solution.py:494
  37.2 7.1 %collective-permute-start.17 = (f32[256,128]{1,0:T(8,128)S(1)}, f32[256,128]{1,0:T(8,128)S(1)}, u32[]{:S(2)}, u32[]{:S(2)}) collective-permute-start(f32[256,128]{1,0:T(8,128)S(1)} %get-tuple-element.81), channel_id=1, source_target_pairs={{0,12},{4,8},{8,4},{12,0},{16,28},{20,24},{24,20},{28,16},{1,13},{... | collective-permute-start | bytes 393224 | tf_op jit(solution)/shard_map/ppermute | solution.py:92
  39.5 5.7 %collective-permute-start.18 = (f32[256,128]{1,0:T(8,128)S(1)}, f32[256,128]{1,0:T(8,128)S(1)}, u32[]{:S(2)}, u32[]{:S(2)}) collective-permute-start(f32[256,128]{1,0:T(8,128)S(1)} %get-tuple-element.82), channel_id=1, source_target_pairs={{0,4},{4,0},{8,12},{12,8},{16,20},{20,16},{24,28},{28,24},{1,5},{5... | collective-permute-start | bytes 393224 | tf_op jit(solution)/shard_map/ppermute | solution.py:92
  40.4 5.0 %collective-permute-start.19 = (f32[256,128]{1,0:T(8,128)S(1)}, f32[256,128]{1,0:T(8,128)S(1)}, u32[]{:S(2)}, u32[]{:S(2)}) collective-permute-start(f32[256,128]{1,0:T(8,128)S(1)} %get-tuple-element.83), channel_id=1, source_target_pairs={{0,8},{4,12},{8,0},{12,4},{16,24},{20,28},{24,16},{28,20},{1,9},{5... | collective-permute-start | bytes 393224 | tf_op jit(solution)/shard_map/ppermute | solution.py:92
  40.8 4.6 %copy-start.5 = (f32[8,128,128]{2,1,0:T(8,128)S(1)}, f32[8,128,128]{2,1,0:T(8,128)}, u32[]{:S(2)}) copy-start(f32[8,128,128]{2,1,0:T(8,128)} %param.15) | copy-start | bytes 1572868
  45.6 6.8 %collective-permute-start.23 = (f32[256,128]{1,0:T(8,128)S(1)}, f32[256,128]{1,0:T(8,128)S(1)}, u32[]{:S(2)}, u32[]{:S(2)}) collective-permute-start(f32[256,128]{1,0:T(8,128)S(1)} %get-tuple-element.89.refs_4_), channel_id=1, source_target_pairs={{0,16},{4,20},{8,24},{12,28},{16,0},{20,4},{24,8},{28,12},{1,17},{... | collective-permute-start | bytes 393224 | tf_op jit(solution)/shard_map/ppermute | solution.py:97
  48.3 7.7 %collective-permute-start.20 = (f32[256,128]{1,0:T(8,128)S(1)}, f32[256,128]{1,0:T(8,128)S(1)}, u32[]{:S(2)}, u32[]{:S(2)}) collective-permute-start(f32[256,128]{1,0:T(8,128)S(1)} %get-tuple-element.86), channel_id=1, source_target_pairs={{0,12},{4,8},{8,4},{12,0},{16,28},{20,24},{24,20},{28,16},{1,13},{... | collective-permute-start | bytes 393224 | tf_op jit(solution)/shard_map/ppermute | solution.py:92
  49.9 8.8 %collective-permute-start.21 = (f32[256,128]{1,0:T(8,128)S(1)}, f32[256,128]{1,0:T(8,128)S(1)}, u32[]{:S(2)}, u32[]{:S(2)}) collective-permute-start(f32[256,128]{1,0:T(8,128)S(1)} %get-tuple-element.87), channel_id=1, source_target_pairs={{0,4},{4,0},{8,12},{12,8},{16,20},{20,16},{24,28},{28,24},{1,5},{5... | collective-permute-start | bytes 393224 | tf_op jit(solution)/shard_map/ppermute | solution.py:92
  50.6 8.1 %collective-permute-start.22 = (f32[256,128]{1,0:T(8,128)S(1)}, f32[256,128]{1,0:T(8,128)S(1)}, u32[]{:S(2)}, u32[]{:S(2)}) collective-permute-start(f32[256,128]{1,0:T(8,128)S(1)} %get-tuple-element.88), channel_id=1, source_target_pairs={{0,8},{4,12},{8,0},{12,4},{16,24},{20,28},{24,16},{28,20},{1,9},{5... | collective-permute-start | bytes 393224 | tf_op jit(solution)/shard_map/ppermute | solution.py:92
  52.6 8.5 %collective-permute-start.24 = (f32[256,128]{1,0:T(8,128)S(1)}, f32[256,128]{1,0:T(8,128)S(1)}, u32[]{:S(2)}, u32[]{:S(2)}) collective-permute-start(f32[256,128]{1,0:T(8,128)S(1)} %get-tuple-element.91), channel_id=1, source_target_pairs={{0,12},{4,8},{8,4},{12,0},{16,28},{20,24},{24,20},{28,16},{1,13},{... | collective-permute-start | bytes 393224 | tf_op jit(solution)/shard_map/ppermute | solution.py:92
  54.6 6.9 %collective-permute-start.25 = (f32[256,128]{1,0:T(8,128)S(1)}, f32[256,128]{1,0:T(8,128)S(1)}, u32[]{:S(2)}, u32[]{:S(2)}) collective-permute-start(f32[256,128]{1,0:T(8,128)S(1)} %get-tuple-element.92), channel_id=1, source_target_pairs={{0,4},{4,0},{8,12},{12,8},{16,20},{20,16},{24,28},{28,24},{1,5},{5... | collective-permute-start | bytes 393224 | tf_op jit(solution)/shard_map/ppermute | solution.py:92
  56.0 5.9 %collective-permute-start.26 = (f32[256,128]{1,0:T(8,128)S(1)}, f32[256,128]{1,0:T(8,128)S(1)}, u32[]{:S(2)}, u32[]{:S(2)}) collective-permute-start(f32[256,128]{1,0:T(8,128)S(1)} %get-tuple-element.93), channel_id=1, source_target_pairs={{0,8},{4,12},{8,0},{12,4},{16,24},{20,28},{24,16},{28,20},{1,9},{5... | collective-permute-start | bytes 393224 | tf_op jit(solution)/shard_map/ppermute | solution.py:92

commit v7 on v6

--- a/solution.py
+++ b/solution.py
@@ -21,12 +21,12 @@
 ANY = pl.BlockSpec(memory_space=pl.ANY)
 
 
-def call(body, outs, operands, scratch=(), flops=0, specs=None):
+def call(body, outs, operands, scratch=(), flops=0, specs=None, out_specs=None):
     return pl.pallas_call(
         body,
         out_shape=outs,
         in_specs=specs or [VMEM] * len(operands),
-        out_specs=[VMEM] * len(outs),
+        out_specs=out_specs or [VMEM] * len(outs),
         scratch_shapes=list(scratch),
         compiler_params=pltpu.CompilerParams(vmem_limit_bytes=24 * 1024 * 1024),
         cost_estimate=pl.CostEstimate(flops=flops, bytes_accessed=0, transcendentals=0),
@@ -41,10 +41,16 @@
     return lax.dot_general(a, b, dims, preferred_element_type=F32)
 
 
-def exact_dot(a, b, dims=(((1,), (0,)), ((), ()))):
-    return lax.dot_general(
-        a, b, dims, precision=lax.Precision.HIGHEST, preferred_element_type=F32
-    )
+def split(x):
+    high = x.astype(BF16)
+    rest = x - high.astype(F32)
+    middle = rest.astype(BF16)
+    low = (rest - middle.astype(F32)).astype(BF16)
+    return jnp.concatenate([high, middle, low], axis=1)
+
+
+def thrice(x):
+    return jnp.concatenate([x, x, x], axis=1)
 
 
 def lanes(h, size):
@@ -66,7 +72,9 @@
         self.rows = self.own * size
         self.chunks = self.own
         self.chunk_rows = self.rows // self.chunks
-        self.ways = sorted(range(self.members), key=lambda way: (way > 0, -way.bit_count()))
+        self.near = [way for way in range(self.members) if way.bit_count() == 1]
+        self.far = [way for way in range(self.members) if way.bit_count() > 1]
+        self.ways = [0] + self.far + self.near
 
     def member(self):
         return lax.rem(lax.axis_index("seq"), self.members)
@@ -75,7 +83,10 @@
         return lax.div(lax.axis_index("seq"), self.members)
 
     def peer(self, k):
-        return lax.bitwise_xor(self.member(), self.ways[k])
+        return self.toward(self.ways[k])
+
+    def toward(self, way):
+        return lax.bitwise_xor(self.member(), way)
 
     def rows_of(self, member):
         return pl.ds(pl.multiple_of(member * self.rows, self.rows), self.rows)
@@ -84,13 +95,21 @@
         start = member * self.rows + chunk * self.chunk_rows
         return pl.ds(pl.multiple_of(start, self.chunk_rows), self.chunk_rows)
 
+    def swap(self, piece, way):
+        span = self.members
+        pairs = [(i, i // span * span + (i % span ^ way)) for i in range(self.blocks)]
+        return lax.ppermute(piece, "seq", pairs) if way else piece
+
     def swap_in_group(self, pieces):
-        span = self.members
-        swapped = [pieces[0]]
-        for way, piece in zip(self.ways[1:], pieces[1:]):
-            pairs = [(i, i // span * span + (i % span ^ way)) for i in range(self.blocks)]
-            swapped.append(lax.ppermute(piece, "seq", pairs))
-        return swapped
+        return [self.swap(piece, way) for way, piece in zip(self.ways, pieces)]
+
+    def first_messages(self):
+        cuts = [(way, c) for c in range(self.chunks) for way in [0] + self.near]
+        return cuts + [(way, None) for way in self.far]
+
+    def part_of(self, ref, way, chunk):
+        start = chunk * self.chunk_rows if way in self.far else 0
+        return ref[start : start + self.chunk_rows]
 
     def from_groups(self, piece):
         return [
@@ -111,35 +130,29 @@
 
 
 def summary_body(plan, key_hbm, value_hbm, decay_hbm, *refs):
-    send_refs, refs = refs[: plan.members * plan.chunks], refs[plan.members * plan.chunks :]
-    cum_ref, cum_col_ref, held_ref, key_ref, value_ref, decay_ref, sems, decay_sem = refs
+    count = len(plan.first_messages())
+    send_refs, refs = refs[:count], refs[count:]
+    cum_ref, cum_col_ref, held_ref, key_ref, value_ref, decay_ref, sems = refs
     length, heads, size = key_ref.shape[0], plan.heads, plan.size
-    decay_copy = pltpu.make_async_copy(decay_hbm, decay_ref, decay_sem)
-    decay_copy.start()
-    copies = []
-    for part in range(plan.members):
-        cut = lanes(part, plan.rows)
-        copies.append(
-            [
-                pltpu.make_async_copy(source.at[:, cut], target.at[:, cut], sems.at[part, i])
-                for i, (source, target) in enumerate([(key_hbm, key_ref), (value_hbm, value_ref)])
-            ]
+    copies = [
+        pltpu.make_async_copy(source, target, sems.at[i])
+        for i, (source, target) in enumerate(
+            [(decay_hbm, decay_ref), (key_hbm, key_ref), (value_hbm, value_ref)]
         )
-        for copy in copies[-1]:
-            copy.start()
-    decay_copy.wait()
-    decay = decay_ref[...]
-    causal = jnp.where(causal_mask(length), 1.0, 0.0)
-    cum_col = exact_dot(causal, decay, CONTRACT_COLS)
-    cum_row = exact_dot(decay, causal, CONTRACT_COLS)
+    ]
+    for copy in copies:
+        copy.start()
+    causal = thrice(jnp.where(causal_mask(length), 1.0, 0.0).astype(BF16))
+    copies[0].wait()
+    decay = split(decay_ref[...])
+    cum_col = dot(causal, decay, CONTRACT_COLS)
+    cum_row = dot(decay, causal, CONTRACT_COLS)
     cum_ref[...] = cum_row
     cum_col_ref[...] = cum_col
-    block_log = cum_col[length - 1 : length, :]
-    shrink = jnp.exp(block_log - cum_col)
+    shrink = jnp.exp(cum_col[length - 1 : length, :] - cum_col)
+    copies[1].wait()
+    copies[2].wait()
     for h in range(heads):
-        if h % plan.own == 0:
-            for copy in copies[h // plan.own]:
-                copy.wait()
         key_decayed = (key_ref[:, lanes(h, size)].astype(F32) * shrink[:, h : h + 1]).astype(BF16)
         held_ref[h * size : (h + 1) * size] = dot(
             key_decayed, value_ref[:, lanes(h, size)], CONTRACT_ROWS
@@ -147,11 +160,14 @@
     log_tile = jnp.broadcast_to(cum_row[:, length - 1 : length], (heads, size))
     if heads < LOG_ROWS:
         log_tile = jnp.concatenate([log_tile, jnp.zeros((LOG_ROWS - heads, size), F32)])
-    for i, send_ref in enumerate(send_refs):
-        chunk, k = divmod(i, plan.members)
-        send_ref[: plan.chunk_rows] = held_ref[plan.chunk_of(plan.peer(k), chunk)]
-        if chunk == 0:
-            send_ref[plan.chunk_rows :] = log_tile
+    for (way, chunk), send_ref in zip(plan.first_messages(), send_refs):
+        member = plan.toward(way)
+        whole = chunk is None
+        part = plan.rows_of(member) if whole else plan.chunk_of(member, chunk)
+        rows = plan.rows if whole else plan.chunk_rows
+        send_ref[:rows] = held_ref[part]
+        if not chunk:
+            send_ref[rows:] = log_tile
 
 
 def group_total_body(plan, chunk, *refs):
@@ -160,13 +176,13 @@
     if chunk == 0:
         total_ref, logs_ref = refs[:2]
         for k, part_ref in enumerate(part_refs):
-            logs_ref[plan.peer(k)] = part_ref[rows:]
+            logs_ref[plan.peer(k)] = part_ref[part_ref.shape[0] - LOG_ROWS :]
         total_ref[rows:] = sum(logs_ref[b] for b in range(plan.members))
     else:
         logs_ref, total_ref = refs[:2]
     held_ref = refs[2]
-    for k, part_ref in enumerate(part_refs):
-        held_ref[plan.peer(k)] = part_ref[:rows]
+    for way, part_ref in zip(plan.ways, part_refs):
+        held_ref[plan.toward(way)] = plan.part_of(part_ref, way, chunk)
     total = jnp.zeros((rows, plan.size), F32)
     for b in range(plan.members):
         total = own_decays(plan, logs_ref.at[b], chunk) * total + held_ref[b]
@@ -180,12 +196,18 @@
 
 
 def forward_scan_body(plan, chunk, *refs):
+    last = chunk == plan.chunks - 1
     part_refs, refs = refs[: plan.members], refs[plan.members :]
     total_refs, refs = refs[: plan.groups], refs[plan.groups :]
+    (state_ref, logs_ref), refs = refs[:2], refs[2:]
     rows = plan.chunk_rows
+    if chunk > 0:
+        group_logs_ref, refs = refs[0], refs[1:]
+    far_parts = chunk * len(plan.far) if last else 0
+    far_refs, refs = refs[:far_parts], refs[far_parts:]
+    send_refs, refs = refs[: plan.members], refs[plan.members :]
     if chunk == 0:
-        (state_ref, logs_ref), refs = refs[:2], refs[2:]
-        send_refs, (before_ref, group_logs_ref, groups_ref, held_ref) = refs[:-4], refs[-4:]
+        before_ref, group_logs_ref = refs[:2]
         for step, total_ref in enumerate(total_refs):
             group = lax.rem(plan.group() - step + plan.groups, plan.groups)
             group_logs_ref[group] = total_ref[rows:]
@@ -195,22 +217,25 @@
         for b in range(plan.members - 1):
             before += jnp.where(b < plan.member(), logs_ref[b], 0.0)
         before_ref[...] = before
-    else:
-        (state_ref, logs_ref, group_logs_ref), refs = refs[:3], refs[3:]
-        send_refs, (groups_ref, held_ref) = refs[:-2], refs[-2:]
+    groups_ref, held_ref = refs[-2:]
     stage_groups(plan, total_refs, groups_ref)
     state = state_ref[plan.chunk_of(plan.member(), chunk)]
     for group in range(plan.groups - 1):
         after = own_decays(plan, group_logs_ref.at[group], chunk) * state + groups_ref[group]
         state = jnp.where(group < plan.group(), after, state)
-    for k, part_ref in enumerate(part_refs):
-        held_ref[plan.peer(k)] = part_ref[:rows]
+    for way, part_ref in zip(plan.ways, part_refs):
+        held_ref[plan.toward(way)] = plan.part_of(part_ref, way, chunk)
     for b in range(plan.members):
         summary = held_ref[b]
         held_ref[b] = state
         state = own_decays(plan, logs_ref.at[b], chunk) * state + summary
-    for k, send_ref in enumerate(send_refs):
-        send_ref[...] = held_ref[plan.peer(k)]
+    for i, (way, send_ref) in enumerate(zip(plan.ways, send_refs)):
+        if way in plan.far and last:
+            for c in range(chunk):
+                send_ref[c * rows : (c + 1) * rows] = far_refs[c * len(plan.far) + i - 1][...]
+            send_ref[chunk * rows :] = held_ref[plan.toward(way)]
+        else:
+            send_ref[...] = held_ref[plan.toward(way)]
 
 
 def suffixes(plan, held_ref, logs_ref, grad):
@@ -287,25 +312,43 @@
     return jnp.exp(jnp.where(causal, jnp.minimum(spread, 0.0), MASKED))
 
 
-def intra_body(plan, query_ref, key_ref, value_ref, cum_ref, cum_col_ref, weight_ref, intra_ref):
+def intra_body(
+    plan,
+    query_ref,
+    key_ref,
+    value_ref,
+    cum_ref,
+    cum_col_ref,
+    upstream_ref,
+    gain_ref,
+    *refs,
+):
+    weight_ref, intra_ref, gained_ref, query_decayed_ref = refs[-4:]
     causal = causal_mask(query_ref.shape[0])
     cum_col = cum_col_ref[...]
+    growth = jnp.exp(cum_col)
     for h in range(plan.heads):
         cut = lanes(h, plan.size)
-        scores = dot(query_ref[:, cut], key_ref[:, cut], CONTRACT_COLS)
+        query = query_ref[:, cut]
+        scores = dot(query, key_ref[:, cut], CONTRACT_COLS)
         weights = (scores * decay_matrix(cum_ref, cum_col, causal, h)).astype(BF16)
         weight_ref[h] = weights
         intra_ref[:, cut] = dot(weights, value_ref[:, cut])
+        gained_ref[:, cut] = gain_ref[:, cut] * upstream_ref[:, cut].astype(F32)
+        query_decayed = query.astype(F32) * growth[:, h : h + 1]
+        query_decayed_ref[h] = jnp.transpose(query_decayed).astype(BF16)
 
 
 def attended_body(plan, *refs):
-    state_refs, refs = refs[: plan.members * plan.chunks], refs[plan.members * plan.chunks :]
-    intra_ref, query_ref, cum_col_ref, upstream_ref, gain_ref = refs[:5]
-    attended_ref, sums_ref, states_ref = refs[5:]
+    count = len(plan.first_messages())
+    state_refs, refs = refs[:count], refs[count:]
+    intra_ref, query_ref, cum_col_ref, gained_ref = refs[:4]
+    attended_ref, sums_ref, states_ref = refs[4:]
     size, length = plan.size, query_ref.shape[0]
-    for i, state_ref in enumerate(state_refs):
-        chunk, k = divmod(i, plan.members)
-        states_ref[plan.chunk_of(plan.peer(k), chunk)] = state_ref[...].astype(BF16)
+    for (way, chunk), state_ref in zip(plan.first_messages(), state_refs):
+        member = plan.toward(way)
+        part = plan.rows_of(member) if chunk is None else plan.chunk_of(member, chunk)
+        states_ref[part] = state_ref[...].astype(BF16)
     growth = jnp.exp(cum_col_ref[...])
     square = jnp.zeros((length, size), F32)
     inner = jnp.zeros((length, size), F32)
@@ -315,36 +358,35 @@
         attended = intra_ref[:, cut] + growth[:, h : h + 1] * carried
         attended_ref[:, cut] = attended
         square += attended * attended
-        inner += gain_ref[:, cut] * upstream_ref[:, cut].astype(F32) * attended
-    ones = jnp.ones((1, size), F32)
-    sums_ref[...] = jnp.concatenate(
-        [exact_dot(ones, square, CONTRACT_COLS), exact_dot(ones, inner, CONTRACT_COLS)]
-        + [jnp.zeros((6, length), F32)],
-        axis=0,
+        inner += gained_ref[:, cut] * attended
+    ones = jnp.ones((8, 3 * size), BF16)
+    is_square = lax.broadcasted_iota(jnp.int32, (8, length), 0) == 0
+    sums_ref[...] = jnp.where(
+        is_square,
+        dot(ones, split(square), CONTRACT_COLS),
+        dot(ones, split(inner), CONTRACT_COLS),
     )
 
 
 def attn_grad_body(plan, parties, *refs):
     sums_refs, refs = refs[:parties], refs[parties:]
-    attended_ref, query_ref, cum_col_ref, upstream_ref, gain_ref = refs[:5]
-    (attn_grad_ref, held_ref), send_refs = refs[5:7], refs[7:]
-    size = plan.size
+    attended_ref, query_decayed_ref, gained_ref, attn_grad_ref, held_ref = refs[:5]
+    send_refs = refs[5:]
+    size, length = plan.size, attended_ref.shape[0]
     feature_count = plan.heads * size * parties
     sums = sum(ref[...] for ref in sums_refs)
     inv_row = lax.rsqrt(sums[:1] / feature_count + EPSILON)
     coefficient_row = sums[1:2] * inv_row * inv_row * inv_row / feature_count
-    columns = jnp.transpose(
-        jnp.concatenate([inv_row, coefficient_row, jnp.zeros_like(sums[2:])], axis=0)
-    )
-    inv_rms, coefficient = columns[:, :1], columns[:, 1:2]
-    growth = jnp.exp(cum_col_ref[...])
+    is_inverse = lax.broadcasted_iota(jnp.int32, (8, length), 0) == 0
+    columns = jnp.transpose(jnp.where(is_inverse, inv_row, coefficient_row))
+    inv_rms = jnp.broadcast_to(columns[:, :1], (length, size))
+    coefficient = jnp.broadcast_to(columns[:, 1:2], (length, size))
     for h in range(plan.heads):
         cut = lanes(h, size)
-        gained = gain_ref[:, cut] * upstream_ref[:, cut].astype(F32)
-        attn_grad = (gained * inv_rms - attended_ref[:, cut] * coefficient).astype(BF16)
+        attn_grad = gained_ref[:, cut] * inv_rms - attended_ref[:, cut] * coefficient
+        attn_grad = attn_grad.astype(BF16)
         attn_grad_ref[:, cut] = attn_grad
-        query_decayed = (query_ref[:, cut].astype(F32) * growth[:, h : h + 1]).astype(BF16)
-        held_ref[cut] = dot(query_decayed, attn_grad, CONTRACT_ROWS)
+        held_ref[cut] = dot(query_decayed_ref[h], attn_grad)
     for k, send_ref in enumerate(send_refs):
         send_ref[...] = held_ref[plan.rows_of(plan.peer(k))]
 
@@ -382,7 +424,7 @@
     first_refs, refs = refs[: plan.members], refs[plan.members :]
     second_refs, refs = refs[: plan.members], refs[plan.members :]
     key_part_ref, value_part_ref, key_ref, value_ref, cum_col_ref, summary_ref, before_ref = refs[:7]
-    key_grad_ref, value_grad_ref, total_ref, held_ref = refs[7:]
+    key_out, value_out, total_out, held_ref, key_grad_ref, value_grad_ref, total_ref, sems = refs[7:]
     length, size = key_ref.shape[0], plan.size
     swapped = jnp.where(plan.group() == 0, 0, 1) if plan.groups == 2 else 0
     for k in range(plan.members):
@@ -391,6 +433,8 @@
     cum_col = cum_col_ref[...]
     block_log = cum_col[length - 1 : length, :]
     shrink = jnp.exp(block_log - cum_col)
+    copies = []
+    half = max(plan.heads // 2, 1)
     for h in range(plan.heads):
         cut = lanes(h, size)
         grads = held_ref[1, cut]
@@ -403,6 +447,19 @@
         key_grad_ref[:, cut] = (key_part_ref[:, cut] + column * key_state).astype(BF16)
         value_state = dot(key_ref[:, cut], grads)
         value_grad_ref[:, cut] = (value_part_ref[:, cut] + column * value_state).astype(BF16)
+        if (h + 1) % half == 0:
+            done = slice((h + 1 - half) * size, (h + 1) * size)
+            for source, target, index in [
+                (total_ref, total_out, (done,)),
+                (key_grad_ref, key_out, (slice(None), done)),
+                (value_grad_ref, value_out, (slice(None), done)),
+            ]:
+                copies.append(
+                    pltpu.make_async_copy(source.at[index], target.at[index], sems.at[len(copies)])
+                )
+                copies[-1].start()
+    for copy in copies:
+        copy.wait()
 
 
 def on_device(
@@ -431,10 +488,18 @@
     chunks = range(plan.chunks)
     state_rows = state_in.reshape(width, size)
 
+    messages = plan.first_messages()
     *sends, cum_log, cum_col = call(
         bind(summary_body),
-        [logged] * plan.members
-        + chunk_pieces * (plan.chunks - 1)
+        [
+            shaped(
+                (
+                    (plan.rows if chunk is None else plan.chunk_rows) + (0 if chunk else LOG_ROWS),
+                    size,
+                )
+            )
+            for _, chunk in messages
+        ]
         + [shaped((heads, length)), shaped((length, heads))],
         [pltpu.with_memory_space_constraint(x, pltpu.HBM) for x in (key_rows, value_rows, log_decay)],
         [
@@ -442,20 +507,12 @@
             pltpu.VMEM((length, width), BF16),
             pltpu.VMEM((length, width), BF16),
             pltpu.VMEM((heads, length), F32),
-            pltpu.SemaphoreType.DMA((plan.members, 2)),
-            pltpu.SemaphoreType.DMA,
+            pltpu.SemaphoreType.DMA((3,)),
         ],
         specs=[HBM] * 3,
     )
-    parts = [
-        plan.swap_in_group(sends[c * plan.members : (c + 1) * plan.members]) for c in chunks
-    ]
-    weights, intra = call(
-        bind(intra_body),
-        [shaped((heads, length, length), BF16), table],
-        [query_rows, key_rows, value_rows, cum_log, cum_col],
-        flops=4 * heads * length * length * size,
-    )
+    received = {key: plan.swap(send, key[0]) for key, send in zip(messages, sends)}
+    parts = [[received[way, None if way in plan.far else c] for way in plan.ways] for c in chunks]
     totals = []
     for c in chunks:
         if c == 0:
@@ -471,24 +528,48 @@
                 flops=LONG,
             )
         totals.append([total] + plan.from_groups(total))
-    states = []
+    states = {}
+    far_parts = []
     for c in chunks:
+        last = c == plan.chunks - 1
         operands = [*parts[c], *totals[c], state_rows, logs]
-        scratch = [hold_chunk_groups, hold_chunk]
+        outs = [piece if way in plan.far and last else chunk_piece for way in plan.ways]
         if c == 0:
-            *sends, before, all_logs = call(
-                bind(forward_scan_body, c),
-                chunk_pieces + [shaped((LOG_ROWS, size)), group_logs],
-                operands,
-                scratch,
-            )
+            outs += [shaped((LOG_ROWS, size)), group_logs]
         else:
-            sends = call(bind(forward_scan_body, c), chunk_pieces, [*operands, all_logs], scratch)
-        states += plan.swap_in_group(sends)
+            operands += [all_logs]
+        sends = call(
+            bind(forward_scan_body, c),
+            outs,
+            operands + (far_parts if last else []),
+            [hold_chunk_groups, hold_chunk],
+        )
+        if c == 0:
+            before, all_logs = sends[plan.members :]
+        for way, send in zip(plan.ways, sends):
+            if way not in plan.far:
+                states[way, c] = plan.swap(send, way)
+            elif last:
+                states[way, None] = plan.swap(send, way)
+            else:
+                far_parts.append(send)
+    early = [states[way, 0] for way in plan.near] if plan.chunks > 1 else []
+    weights, intra, gained, query_decayed = call(
+        bind(intra_body),
+        [
+            shaped((heads, length, length), BF16),
+            table,
+            table,
+            shaped((heads, size, length), BF16),
+        ],
+        [query_rows, key_rows, value_rows, cum_log, cum_col, out_grad, gain, *early],
+        specs=[VMEM] * 7 + [ANY] * len(early),
+        flops=LONG // 10,
+    )
     attended, sums, states = call(
         bind(attended_body),
         [table, shaped((8, length)), shaped((width, size), BF16)],
-        [*states, intra, query_rows, cum_col, out_grad, gain],
+        [*[states[key] for key in messages], intra, query_rows, cum_col, gained],
     )
     all_sums = [sums] + [
         lax.ppermute(sums, "head", [(i, (i + step) % parties) for i in range(parties)])
@@ -497,7 +578,7 @@
     attn_grad, summary, *sends = call(
         bind(attn_grad_body, parties),
         [rounded, shaped((width, size))] + pieces,
-        [*all_sums, attended, query_rows, cum_col, out_grad, gain],
+        [*all_sums, attended, query_decayed, gained],
     )
     parts = plan.swap_in_group(sends)
     query_grad, key_part, value_part = call(
@@ -529,7 +610,14 @@
         bind(finish_body),
         [rounded, rounded, shaped((width, size))],
         [*swapped[0], *swapped[1], key_part, value_part, key_rows, value_rows, cum_col, summary, before],
-        [pltpu.VMEM((2, width, size), F32)],
+        [
+            pltpu.VMEM((2, width, size), F32),
+            pltpu.VMEM((length, width), BF16),
+            pltpu.VMEM((length, width), BF16),
+            pltpu.VMEM((width, size), F32),
+            pltpu.SemaphoreType.DMA((6,)),
+        ],
+        out_specs=[HBM] * 3,
     )
     return (query_grad, key_grad, value_grad, state_in_grad.reshape(heads, size, size))
 

time: 64.1 us -> 62.8 us (0.980)
  Pallas kernels: 12.5 us -> 10.7 us
    pallas_call x12, Pallas kernels: 12.5 us -> 10.7 us  [call(): pl.pallas_call(body, out_shape=outs, in_specs=specs or [VMEM] * len(opera...]
    ppermute x3, starting transfers between devices: 7.94 us -> 6.9 us  [from_groups(): lax.ppermute(piece, 'seq', [(i, (i + step * self.members) % self.blocks)...]
    ppermute x21 -> x19, starting transfers between devices: 27.2 us -> 28.2 us  [swap(): return lax.ppermute(piece, 'seq', pairs) if way else piece]
    ppermute x21 -> x19, waiting for transfers between devices: 8.68 us -> 8.88 us  [swap(): return lax.ppermute(piece, 'seq', pairs) if way else piece]
  transfers between devices with their start and end apart: 27 -> 25, of which waited for: 18 -> 11; matrix products, arithmetic and copies ran while one was open for 0% -> 0% of each run, Pallas kernels for 8% -> 8%
where the time goes in v7:
time: 62.8 us; the launch traced here: 62.6 us
  starting transfers between devices  36.9 us (59%)
  waiting for transfers between devices  14.2 us (23%)
  Pallas kernels  10.7 us (17%)
  between operations  0.75 us (1%)
    ppermute x19, starting transfers between devices, swap(): return lax.ppermute(piece, 'seq', pairs) if way else piece  28.2 us
    pallas_call x12, Pallas kernels, call(): pl.pallas_call(body, out_shape=outs, in_specs=specs or [VMEM] * len(opera...  10.7 us
    ppermute x19, waiting for transfers between devices, swap(): return lax.ppermute(piece, 'seq', pairs) if way else piece  8.88 us
    ppermute x3, starting transfers between devices, from_groups(): lax.ppermute(piece, 'seq', [(i, (i + step * self.members) % self.blocks)...  6.9 us
    ppermute x3, waiting for transfers between devices, on_device(): lax.ppermute(sums, 'head', [(i, (i + step) % parties) for i in range(part...  2.85 us
    ppermute x3, waiting for transfers between devices, from_groups(): lax.ppermute(piece, 'seq', [(i, (i + step * self.members) % self.blocks)...  2.48 us
    ppermute x3, starting transfers between devices, on_device(): lax.ppermute(sums, 'head', [(i, (i + step) % parties) for i in range(part...  1.78 us
  transfers between devices with their start and end apart: 25, of which 11 were waited for; matrix products, arithmetic and copies ran while one was open for 0% of the time, Pallas kernels for 8%

profile of v7, /device:TPU:0, one launch (start us, length us, event | category | flops | bytes accessed | tf_op | source)
XLA Modules:
  0.0 62.6 jit_solution(10703928254653114068)
XLA Ops:
  0.6 2.2 %shard_map.111 = (f32[136,128]{1,0:T(8,128)S(1)}, f32[136,128]{1,0:T(8,128)S(1)}, f32[136,128]{1,0:T(8,128)S(1)}, f32[128,128]{1,0:T(8,128)S(1)}, f32[128,128]{1...) custom-call(bf16[256,1024]{1,0:T(8,128)(2,1)} %refs_10_.1, ...), custom_call_target="tpu_custom_call" | custom-call | tf_op jit(solution)/shard_map/pallas_call | solution.py:25
  2.8 4.0 %collective-permute-start = (f32[264,128]{1,0:T(8,128)S(1)}, f32[264,128]{1,0:T(8,128)S(1)}, u32[]{:S(2)}, u32[]{:S(2)}) collective-permute-start(f32[264,128]{1,0:T(8,128)S(1)} %get-tuple-element.54), channel_id=1, source_target_pairs={{0,12},{4,8},{8,4},{12,0},{16,28},{20,24},{24,20},{28,16},{1,13},{... | collective-permute-start | bytes 405512 | tf_op jit(solution)/shard_map/ppermute | solution.py:101
  6.9 0.5 collective-permute-start.1
  7.4 0.1 collective-permute-start.2
  7.5 1.8 %collective-permute-start.6 = (f32[128,128]{1,0:T(8,128)S(1)}, f32[128,128]{1,0:T(8,128)S(1)}, u32[]{:S(2)}, u32[]{:S(2)}) collective-permute-start(f32[128,128]{1,0:T(8,128)S(1)} %get-tuple-element.63), channel_id=1, source_target_pairs={{0,4},{4,0},{8,12},{12,8},{16,20},{20,16},{24,28},{28,24},{1,5},{5... | collective-permute-start | bytes 196616 | tf_op jit(solution)/shard_map/ppermute | solution.py:101
  9.3 1.6 %collective-permute-start.7 = (f32[128,128]{1,0:T(8,128)S(1)}, f32[128,128]{1,0:T(8,128)S(1)}, u32[]{:S(2)}, u32[]{:S(2)}) collective-permute-start(f32[128,128]{1,0:T(8,128)S(1)} %get-tuple-element.64), channel_id=1, source_target_pairs={{0,8},{4,12},{8,0},{12,4},{16,24},{20,28},{24,16},{28,20},{1,9},{5... | collective-permute-start | bytes 196616 | tf_op jit(solution)/shard_map/ppermute | solution.py:101
  10.9 1.1 %collective-permute-done.1.refs_2_ = f32[136,128]{1,0:T(8,128)S(1)} collective-permute-done((f32[136,128]{1,0:T(8,128)S(1)}, f32[136,128]{1,0:T(8,128)S(1)}, u32[]{:S(2)}, u32[]{:S(2)}) %collective-permute-start.1) | collective-permute-done | bytes 69664 | tf_op jit(solution)/shard_map/ppermute | solution.py:101
  12.0 0.7 %collective-permute-done.2.refs_3_ = f32[136,128]{1,0:T(8,128)S(1)} collective-permute-done((f32[136,128]{1,0:T(8,128)S(1)}, f32[136,128]{1,0:T(8,128)S(1)}, u32[]{:S(2)}, u32[]{:S(2)}) %collective-permute-start.2) | collective-permute-done | bytes 69664 | tf_op jit(solution)/shard_map/ppermute | solution.py:101
  12.8 0.1 shard_map.112
  12.8 2.7 %collective-permute-start.3 = (f32[136,128]{1,0:T(8,128)S(1)}, f32[136,128]{1,0:T(8,128)S(1)}, u32[]{:S(2)}, u32[]{:S(2)}) collective-permute-start(f32[136,128]{1,0:T(8,128)S(1)} %get-tuple-element.57.refs_4_), channel_id=1, source_target_pairs={{0,16},{4,20},{8,24},{12,28},{16,0},{20,4},{24,8},{28,12},{1,17},{... | collective-permute-start | bytes 208904 | tf_op jit(solution)/shard_map/ppermute | solution.py:116
  15.5 0.1 shard_map.114.refs_4_
  15.6 0.7 %collective-permute-start.8 = (f32[128,128]{1,0:T(8,128)S(1)}, f32[128,128]{1,0:T(8,128)S(1)}, u32[]{:S(2)}, u32[]{:S(2)}) collective-permute-start(f32[128,128]{1,0:T(8,128)S(1)} %shard_map.114.refs_4_), channel_id=1, source_target_pairs={{0,16},{4,20},{8,24},{12,28},{16,0},{20,4},{24,8},{28,12},{1,17},{... | collective-permute-start | bytes 196616 | tf_op jit(solution)/shard_map/ppermute | solution.py:116
  16.3 2.0 %collective-permute-done.3.refs_5_ = f32[136,128]{1,0:T(8,128)S(1)} collective-permute-done((f32[136,128]{1,0:T(8,128)S(1)}, f32[136,128]{1,0:T(8,128)S(1)}, u32[]{:S(2)}, u32[]{:S(2)}) %collective-permute-start.3) | collective-permute-done | bytes 69664 | tf_op jit(solution)/shard_map/ppermute | solution.py:116
  18.3 0.1 shard_map.113
  18.4 2.3 %collective-permute-start.4 = (f32[128,128]{1,0:T(8,128)S(1)}, f32[128,128]{1,0:T(8,128)S(1)}, u32[]{:S(2)}, u32[]{:S(2)}) collective-permute-start(f32[128,128]{1,0:T(8,128)S(1)} %get-tuple-element.60), channel_id=1, source_target_pairs={{0,4},{4,0},{8,12},{12,8},{16,20},{20,16},{24,28},{28,24},{1,5},{5... | collective-permute-start | bytes 196616 | tf_op jit(solution)/shard_map/ppermute | solution.py:101
  20.7 1.6 %collective-permute-start.5 = (f32[128,128]{1,0:T(8,128)S(1)}, f32[128,128]{1,0:T(8,128)S(1)}, u32[]{:S(2)}, u32[]{:S(2)}) collective-permute-start(f32[128,128]{1,0:T(8,128)S(1)} %get-tuple-element.61), channel_id=1, source_target_pairs={{0,8},{4,12},{8,0},{12,4},{16,24},{20,28},{24,16},{28,20},{1,9},{5... | collective-permute-start | bytes 196616 | tf_op jit(solution)/shard_map/ppermute | solution.py:101
  22.4 0.1 shard_map.115
  22.5 0.8 %collective-permute-start.11 = (f32[256,128]{1,0:T(8,128)S(1)}, f32[256,128]{1,0:T(8,128)S(1)}, u32[]{:S(2)}, u32[]{:S(2)}) collective-permute-start(f32[256,128]{1,0:T(8,128)S(1)} %get-tuple-element.70), channel_id=1, source_target_pairs={{0,12},{4,8},{8,4},{12,0},{16,28},{20,24},{24,20},{28,16},{1,13},{... | collective-permute-start | bytes 393224 | tf_op jit(solution)/shard_map/ppermute | solution.py:101
  23.3 1.1 %collective-permute-start.9 = (f32[128,128]{1,0:T(8,128)S(1)}, f32[128,128]{1,0:T(8,128)S(1)}, u32[]{:S(2)}, u32[]{:S(2)}) collective-permute-start(f32[128,128]{1,0:T(8,128)S(1)} %get-tuple-element.68), channel_id=1, source_target_pairs={{0,4},{4,0},{8,12},{12,8},{16,20},{20,16},{24,28},{28,24},{1,5},{5... | collective-permute-start | bytes 196616 | tf_op jit(solution)/shard_map/ppermute | solution.py:101
  24.4 1.6 %collective-permute-start.10 = (f32[128,128]{1,0:T(8,128)S(1)}, f32[128,128]{1,0:T(8,128)S(1)}, u32[]{:S(2)}, u32[]{:S(2)}) collective-permute-start(f32[128,128]{1,0:T(8,128)S(1)} %get-tuple-element.69), channel_id=1, source_target_pairs={{0,8},{4,12},{8,0},{12,4},{16,24},{20,28},{24,16},{28,20},{1,9},{5... | collective-permute-start | bytes 196616 | tf_op jit(solution)/shard_map/ppermute | solution.py:101
  26.1 1.2 %shard_map.116 = (bf16[8,256,256]{2,1,0:T(8,128)(2,1)S(1)}, f32[256,1024]{1,0:T(8,128)S(1)}, f32[256,1024]{1,0:T(8,128)S(1)}, bf16[8,128,256]{2,1,0:T(8,128)(2,1)S(1)}) custom-call(bf16[256,1024]{1,0:T(8,128)(2,1)S(1)} %copy-done.2, bf16[256,1024]{1,0:T(8,128)(2,1)S(1)} %copy-done, bf16[256,1024]{1,0:T(8,128)(2,1)S(1)} %copy-done.1, ...), custom_call_target="tpu_custom_call" | custom-call | flops 1000000000 | tf_op jit(solution)/shard_map/pallas_call | solution.py:25
  27.3 1.6 %collective-permute-done.9.refs_4_ = f32[128,128]{1,0:T(8,128)S(1)} collective-permute-done((f32[128,128]{1,0:T(8,128)S(1)}, f32[128,128]{1,0:T(8,128)S(1)}, u32[]{:S(2)}, u32[]{:S(2)}) %collective-permute-start.9) | collective-permute-done | bytes 65568 | tf_op jit(solution)/shard_map/ppermute | solution.py:101
  28.9 0.0 collective-permute-done.10.refs_5_
  29.0 0.7 %shard_map.117 = (f32[256,1024]{1,0:T(8,128)S(1)}, f32[8,256]{1,0:T(8,128)S(1)}, bf16[1024,128]{1,0:T(8,128)(2,1)S(1)}) custom-call(f32[128,128]{1,0:T(8,128)S(1)} %get-tuple-element.59.refs_0_, f32[128,128]{1,0:T(8,128)S(1)} %collective-permute-done.4.refs_0_.refs_1_, f32[128,128]{1,0:T(8,128)S(1)} %collective-permute-done.5.refs_1_.refs_2_, ...), custom_call_target="tpu_custom_call" | custom-call | tf_op jit(solution)/shard_map/pallas_call | solution.py:25
  29.7 1.6 %collective-permute-start.13 = (f32[8,256]{1,0:T(8,128)S(1)}, f32[8,256]{1,0:T(8,128)S(1)}, u32[]{:S(2)}, u32[]{:S(2)}) collective-permute-start(f32[8,256]{1,0:T(8,128)S(1)} %get-tuple-element.75.refs_0_), channel_id=1, source_target_pairs={{0,2},{1,3},{2,0},{3,1},{4,6},{5,7},{6,4},{7,5},{8,10},{9,11},{10,... | collective-permute-start | bytes 24584 | tf_op jit(solution)/shard_map/ppermute | solution.py:575
  31.2 0.2 collective-permute-start.12
  31.4 1.9 %collective-permute-done.13.refs_2_ = f32[8,256]{1,0:T(8,128)S(1)} collective-permute-done((f32[8,256]{1,0:T(8,128)S(1)}, f32[8,256]{1,0:T(8,128)S(1)}, u32[]{:S(2)}, u32[]{:S(2)}) %collective-permute-start.13) | collective-permute-done | bytes 8224 | tf_op jit(solution)/shard_map/ppermute | solution.py:575
  33.3 0.9 %collective-permute-done.12.refs_1_ = f32[8,256]{1,0:T(8,128)S(1)} collective-permute-done((f32[8,256]{1,0:T(8,128)S(1)}, f32[8,256]{1,0:T(8,128)S(1)}, u32[]{:S(2)}, u32[]{:S(2)}) %collective-permute-start.12) | collective-permute-done | bytes 8224 | tf_op jit(solution)/shard_map/ppermute | solution.py:575
  34.3 0.7 %shard_map.118 = (bf16[256,1024]{1,0:T(8,128)(2,1)S(1)}, f32[1024,128]{1,0:T(8,128)S(1)}, f32[256,128]{1,0:T(8,128)S(1)}, f32[256,128]{1,0:T(8,128)S(1)}, f32[25...) custom-call(f32[8,256]{1,0:T(8,128)S(1)} %get-tuple-element.75.refs_0_, f32[8,256]{1,0:T(8,128)S(1)} %collective-permute-done.12.refs_1_, ...), custom_call_target="tpu_custom_call" | custom-call | tf_op jit(solution)/shard_map/pallas_call | solution.py:25
  35.0 2.1 %collective-permute-start.15 = (f32[256,128]{1,0:T(8,128)S(1)}, f32[256,128]{1,0:T(8,128)S(1)}, u32[]{:S(2)}, u32[]{:S(2)}) collective-permute-start(f32[256,128]{1,0:T(8,128)S(1)} %get-tuple-element.83), channel_id=1, source_target_pairs={{0,12},{4,8},{8,4},{12,0},{16,28},{20,24},{24,20},{28,16},{1,13},{... | collective-permute-start | bytes 393224 | tf_op jit(solution)/shard_map/ppermute | solution.py:101
  37.1 0.7 %collective-permute-start.16 = (f32[256,128]{1,0:T(8,128)S(1)}, f32[256,128]{1,0:T(8,128)S(1)}, u32[]{:S(2)}, u32[]{:S(2)}) collective-permute-start(f32[256,128]{1,0:T(8,128)S(1)} %get-tuple-element.84), channel_id=1, source_target_pairs={{0,4},{4,0},{8,12},{12,8},{16,20},{20,16},{24,28},{28,24},{1,5},{5... | collective-permute-start | bytes 393224 | tf_op jit(solution)/shard_map/ppermute | solution.py:101
  37.8 0.7 %collective-permute-start.17 = (f32[256,128]{1,0:T(8,128)S(1)}, f32[256,128]{1,0:T(8,128)S(1)}, u32[]{:S(2)}, u32[]{:S(2)}) collective-permute-start(f32[256,128]{1,0:T(8,128)S(1)} %get-tuple-element.85), channel_id=1, source_target_pairs={{0,8},{4,12},{8,0},{12,4},{16,24},{20,28},{24,16},{28,20},{1,9},{5... | collective-permute-start | bytes 393224 | tf_op jit(solution)/shard_map/ppermute | solution.py:101
  38.5 3.4 %shard_map.119 = (bf16[256,1024]{1,0:T(8,128)(2,1)}, f32[256,1024]{1,0:T(8,128)S(1)}, f32[256,1024]{1,0:T(8,128)S(1)}) custom-call(bf16[256,1024]{1,0:T(8,128)(2,1)S(1)} %get-tuple-element.78.attn_grad_ref, bf16[256,1024]{1,0:T(8,128)(2,1)S(1)} %copy-done.2, bf16[256,1024]{1,0:T(8,128)(2,1)S(1)} %copy-done, bf16[256,1024]{1,0:T(8,128)(2,1)S(1)} %copy-done.1, ...), custom_call_target="tpu_custom_call" | custom-call | flops 671088640 | tf_op jit(solution)/shard_map/pallas_call | solution.py:25
  42.0 0.9 %collective-permute-done.16.refs_2_ = f32[256,128]{1,0:T(8,128)S(1)} collective-permute-done((f32[256,128]{1,0:T(8,128)S(1)}, f32[256,128]{1,0:T(8,128)S(1)}, u32[]{:S(2)}, u32[]{:S(2)}) %collective-permute-start.16) | collective-permute-done | bytes 131104 | tf_op jit(solution)/shard_map/ppermute | solution.py:101
  42.9 0.2 shard_map.120
  43.1 3.5 %collective-permute-start.21 = (f32[256,128]{1,0:T(8,128)S(1)}, f32[256,128]{1,0:T(8,128)S(1)}, u32[]{:S(2)}, u32[]{:S(2)}) collective-permute-start(f32[256,128]{1,0:T(8,128)S(1)} %get-tuple-element.91.refs_4_), channel_id=1, source_target_pairs={{0,16},{4,20},{8,24},{12,28},{16,0},{20,4},{24,8},{28,12},{1,17},{... | collective-permute-start | bytes 393224 | tf_op jit(solution)/shard_map/ppermute | solution.py:116
  46.6 1.5 %collective-permute-start.18 = (f32[256,128]{1,0:T(8,128)S(1)}, f32[256,128]{1,0:T(8,128)S(1)}, u32[]{:S(2)}, u32[]{:S(2)}) collective-permute-start(f32[256,128]{1,0:T(8,128)S(1)} %get-tuple-element.88), channel_id=1, source_target_pairs={{0,12},{4,8},{8,4},{12,0},{16,28},{20,24},{24,20},{28,16},{1,13},{... | collective-permute-start | bytes 393224 | tf_op jit(solution)/shard_map/ppermute | solution.py:101
  48.1 1.0 %collective-permute-start.19 = (f32[256,128]{1,0:T(8,128)S(1)}, f32[256,128]{1,0:T(8,128)S(1)}, u32[]{:S(2)}, u32[]{:S(2)}) collective-permute-start(f32[256,128]{1,0:T(8,128)S(1)} %get-tuple-element.89), channel_id=1, source_target_pairs={{0,4},{4,0},{8,12},{12,8},{16,20},{20,16},{24,28},{28,24},{1,5},{5... | collective-permute-start | bytes 393224 | tf_op jit(solution)/shard_map/ppermute | solution.py:101
  49.1 1.0 %collective-permute-start.20 = (f32[256,128]{1,0:T(8,128)S(1)}, f32[256,128]{1,0:T(8,128)S(1)}, u32[]{:S(2)}, u32[]{:S(2)}) collective-permute-start(f32[256,128]{1,0:T(8,128)S(1)} %get-tuple-element.90), channel_id=1, source_target_pairs={{0,8},{4,12},{8,0},{12,4},{16,24},{20,28},{24,16},{28,20},{1,9},{5... | collective-permute-start | bytes 393224 | tf_op jit(solution)/shard_map/ppermute | solution.py:101
  50.1 0.5 collective-permute-done.21.refs_5_
  50.6 0.2 shard_map.121
  50.8 2.0 %collective-permute-start.22 = (f32[256,128]{1,0:T(8,128)S(1)}, f32[256,128]{1,0:T(8,128)S(1)}, u32[]{:S(2)}, u32[]{:S(2)}) collective-permute-start(f32[256,128]{1,0:T(8,128)S(1)} %get-tuple-element.93), channel_id=1, source_target_pairs={{0,12},{4,8},{8,4},{12,0},{16,28},{20,24},{24,20},{28,16},{1,13},{... | collective-permute-start | bytes 393224 | tf_op jit(solution)/shard_map/ppermute | solution.py:101
  52.8 0.9 %collective-permute-start.23 = (f32[256,128]{1,0:T(8,128)S(1)}, f32[256,128]{1,0:T(8,128)S(1)}, u32[]{:S(2)}, u32[]{:S(2)}) collective-permute-start(f32[256,128]{1,0:T(8,128)S(1)} %get-tuple-element.94), channel_id=1, source_target_pairs={{0,4},{4,0},{8,12},{12,8},{16,20},{20,16},{24,28},{28,24},{1,5},{5... | collective-permute-start | bytes 393224 | tf_op jit(solution)/shard_map/ppermute | solution.py:101
  53.8 1.0 %collective-permute-done.18.refs_1_ = f32[256,128]{1,0:T(8,128)S(1)} collective-permute-done((f32[256,128]{1,0:T(8,128)S(1)}, f32[256,128]{1,0:T(8,128)S(1)}, u32[]{:S(2)}, u32[]{:S(2)}) %collective-permute-start.18) | collective-permute-done | bytes 131104 | tf_op jit(solution)/shard_map/ppermute | solution.py:101
  54.7 2.6 %collective-permute-start.24 = (f32[256,128]{1,0:T(8,128)S(1)}, f32[256,128]{1,0:T(8,128)S(1)}, u32[]{:S(2)}, u32[]{:S(2)}) collective-permute-start(f32[256,128]{1,0:T(8,128)S(1)} %get-tuple-element.95), channel_id=1, source_target_pairs={{0,8},{4,12},{8,0},{12,4},{16,24},{20,28},{24,16},{28,20},{1,9},{5... | collective-permute-start | bytes 393224 | tf_op jit(solution)/shard_map/ppermute | solution.py:101
  57.3 2.4 %collective-permute-done.22.refs_5_ = f32[256,128]{1,0:T(8,128)S(1)} collective-permute-done((f32[256,128]{1,0:T(8,128)S(1)}, f32[256,128]{1,0:T(8,128)S(1)}, u32[]{:S(2)}, u32[]{:S(2)}) %collective-permute-start.22) | collective-permute-done | bytes 131104 | tf_op jit(solution)/shard_map/ppermute | solution.py:101
  59.8 1.1 %collective-permute-done.24.refs_7_ = f32[256,128]{1,0:T(8,128)S(1)} collective-permute-done((f32[256,128]{1,0:T(8,128)S(1)}, f32[256,128]{1,0:T(8,128)S(1)}, u32[]{:S(2)}, u32[]{:S(2)}) %collective-permute-start.24) | collective-permute-done | bytes 131104 | tf_op jit(solution)/shard_map/ppermute | solution.py:101
  60.8 1.7 %shard_map.122 = (bf16[256,1024]{1,0:T(8,128)(2,1)}, bf16[256,1024]{1,0:T(8,128)(2,1)}, f32[1024,128]{1,0:T(8,128)}) custom-call(f32[256,128]{1,0:T(8,128)S(1)} %get-tuple-element.87.refs_0_, f32[256,128]{1,0:T(8,128)S(1)} %collective-permute-done.18.refs_1_, f32[256,128]{1,0:T(8,128)S(1)} %collective-permute-done.19.refs_2_, ...), custom_call_target="tpu_custom_call" | custom-call | tf_op jit(solution)/shard_map/pallas_call | solution.py:25
  (28 shorter events, 0.1 us)
Async XLA Ops:
  2.8 10.0 %collective-permute-start = (f32[264,128]{1,0:T(8,128)S(1)}, f32[264,128]{1,0:T(8,128)S(1)}, u32[]{:S(2)}, u32[]{:S(2)}) collective-permute-start(f32[264,128]{1,0:T(8,128)S(1)} %get-tuple-element.54), channel_id=1, source_target_pairs={{0,12},{4,8},{8,4},{12,0},{16,28},{20,24},{24,20},{28,16},{1,13},{... | collective-permute-start | bytes 405512 | tf_op jit(solution)/shard_map/ppermute | solution.py:101
  6.9 5.2 %collective-permute-start.1 = (f32[136,128]{1,0:T(8,128)S(1)}, f32[136,128]{1,0:T(8,128)S(1)}, u32[]{:S(2)}, u32[]{:S(2)}) collective-permute-start(f32[136,128]{1,0:T(8,128)S(1)} %get-tuple-element.55), channel_id=1, source_target_pairs={{0,4},{4,0},{8,12},{12,8},{16,20},{20,16},{24,28},{28,24},{1,5},{5... | collective-permute-start | bytes 208904 | tf_op jit(solution)/shard_map/ppermute | solution.py:101
  7.4 5.4 %collective-permute-start.2 = (f32[136,128]{1,0:T(8,128)S(1)}, f32[136,128]{1,0:T(8,128)S(1)}, u32[]{:S(2)}, u32[]{:S(2)}) collective-permute-start(f32[136,128]{1,0:T(8,128)S(1)} %get-tuple-element.56), channel_id=1, source_target_pairs={{0,8},{4,12},{8,0},{12,4},{16,24},{20,28},{24,16},{28,20},{1,9},{5... | collective-permute-start | bytes 208904 | tf_op jit(solution)/shard_map/ppermute | solution.py:101
  7.5 8.0 %collective-permute-start.6 = (f32[128,128]{1,0:T(8,128)S(1)}, f32[128,128]{1,0:T(8,128)S(1)}, u32[]{:S(2)}, u32[]{:S(2)}) collective-permute-start(f32[128,128]{1,0:T(8,128)S(1)} %get-tuple-element.63), channel_id=1, source_target_pairs={{0,4},{4,0},{8,12},{12,8},{16,20},{20,16},{24,28},{28,24},{1,5},{5... | collective-permute-start | bytes 196616 | tf_op jit(solution)/shard_map/ppermute | solution.py:101
  9.3 6.2 %collective-permute-start.7 = (f32[128,128]{1,0:T(8,128)S(1)}, f32[128,128]{1,0:T(8,128)S(1)}, u32[]{:S(2)}, u32[]{:S(2)}) collective-permute-start(f32[128,128]{1,0:T(8,128)S(1)} %get-tuple-element.64), channel_id=1, source_target_pairs={{0,8},{4,12},{8,0},{12,4},{16,24},{20,28},{24,16},{28,20},{1,9},{5... | collective-permute-start | bytes 196616 | tf_op jit(solution)/shard_map/ppermute | solution.py:101
  12.8 5.5 %collective-permute-start.3 = (f32[136,128]{1,0:T(8,128)S(1)}, f32[136,128]{1,0:T(8,128)S(1)}, u32[]{:S(2)}, u32[]{:S(2)}) collective-permute-start(f32[136,128]{1,0:T(8,128)S(1)} %get-tuple-element.57.refs_4_), channel_id=1, source_target_pairs={{0,16},{4,20},{8,24},{12,28},{16,0},{20,4},{24,8},{28,12},{1,17},{... | collective-permute-start | bytes 208904 | tf_op jit(solution)/shard_map/ppermute | solution.py:116
  15.5 2.8 %copy-start.3 = (f32[8,128,128]{2,1,0:T(8,128)S(1)}, f32[8,128,128]{2,1,0:T(8,128)}, u32[]{:S(2)}) copy-start(f32[8,128,128]{2,1,0:T(8,128)} %param.14) | copy-start | bytes 1572868
  15.6 6.8 %collective-permute-start.8 = (f32[128,128]{1,0:T(8,128)S(1)}, f32[128,128]{1,0:T(8,128)S(1)}, u32[]{:S(2)}, u32[]{:S(2)}) collective-permute-start(f32[128,128]{1,0:T(8,128)S(1)} %shard_map.114.refs_4_), channel_id=1, source_target_pairs={{0,16},{4,20},{8,24},{12,28},{16,0},{20,4},{24,8},{28,12},{1,17},{... | collective-permute-start | bytes 196616 | tf_op jit(solution)/shard_map/ppermute | solution.py:116
  18.3 7.7 %copy-start.2 = (bf16[256,1024]{1,0:T(8,128)(2,1)S(1)}, bf16[256,1024]{1,0:T(8,128)(2,1)}, u32[]{:S(2)}) copy-start(bf16[256,1024]{1,0:T(8,128)(2,1)} %query_ref.3) | copy-start | bytes 1572868
  18.3 7.7 %copy-start.5 = (bf16[256,1024]{1,0:T(8,128)(2,1)S(1)}, bf16[256,1024]{1,0:T(8,128)(2,1)}, u32[]{:S(2)}) copy-start(bf16[256,1024]{1,0:T(8,128)(2,1)} %upstream_ref.1) | copy-start | bytes 1572868
  18.4 7.6 %collective-permute-start.4 = (f32[128,128]{1,0:T(8,128)S(1)}, f32[128,128]{1,0:T(8,128)S(1)}, u32[]{:S(2)}, u32[]{:S(2)}) collective-permute-start(f32[128,128]{1,0:T(8,128)S(1)} %get-tuple-element.60), channel_id=1, source_target_pairs={{0,4},{4,0},{8,12},{12,8},{16,20},{20,16},{24,28},{28,24},{1,5},{5... | collective-permute-start | bytes 196616 | tf_op jit(solution)/shard_map/ppermute | solution.py:101
  20.7 5.3 %collective-permute-start.5 = (f32[128,128]{1,0:T(8,128)S(1)}, f32[128,128]{1,0:T(8,128)S(1)}, u32[]{:S(2)}, u32[]{:S(2)}) collective-permute-start(f32[128,128]{1,0:T(8,128)S(1)} %get-tuple-element.61), channel_id=1, source_target_pairs={{0,8},{4,12},{8,0},{12,4},{16,24},{20,28},{24,16},{28,20},{1,9},{5... | collective-permute-start | bytes 196616 | tf_op jit(solution)/shard_map/ppermute | solution.py:101
  22.4 3.7 %copy-start = (bf16[256,1024]{1,0:T(8,128)(2,1)S(1)}, bf16[256,1024]{1,0:T(8,128)(2,1)}, u32[]{:S(2)}) copy-start(bf16[256,1024]{1,0:T(8,128)(2,1)} %refs_10_.1) | copy-start | bytes 1572868
  22.4 3.7 %copy-start.1 = (bf16[256,1024]{1,0:T(8,128)(2,1)S(1)}, bf16[256,1024]{1,0:T(8,128)(2,1)}, u32[]{:S(2)}) copy-start(bf16[256,1024]{1,0:T(8,128)(2,1)} %refs_11_.1) | copy-start | bytes 1572868
  22.5 6.5 %collective-permute-start.11 = (f32[256,128]{1,0:T(8,128)S(1)}, f32[256,128]{1,0:T(8,128)S(1)}, u32[]{:S(2)}, u32[]{:S(2)}) collective-permute-start(f32[256,128]{1,0:T(8,128)S(1)} %get-tuple-element.70), channel_id=1, source_target_pairs={{0,12},{4,8},{8,4},{12,0},{16,28},{20,24},{24,20},{28,16},{1,13},{... | collective-permute-start | bytes 393224 | tf_op jit(solution)/shard_map/ppermute | solution.py:101
  23.3 2.8 %copy-start.6 = (f32[1024]{0:T(1024)S(1)}, f32[1024]{0:T(1024)}, u32[]{:S(2)}) copy-start(f32[1024]{0:T(1024)} %param.13) | copy-start | bytes 12292
  23.3 5.7 %collective-permute-start.9 = (f32[128,128]{1,0:T(8,128)S(1)}, f32[128,128]{1,0:T(8,128)S(1)}, u32[]{:S(2)}, u32[]{:S(2)}) collective-permute-start(f32[128,128]{1,0:T(8,128)S(1)} %get-tuple-element.68), channel_id=1, source_target_pairs={{0,4},{4,0},{8,12},{12,8},{16,20},{20,16},{24,28},{28,24},{1,5},{5... | collective-permute-start | bytes 196616 | tf_op jit(solution)/shard_map/ppermute | solution.py:101
  24.4 4.6 %collective-permute-start.10 = (f32[128,128]{1,0:T(8,128)S(1)}, f32[128,128]{1,0:T(8,128)S(1)}, u32[]{:S(2)}, u32[]{:S(2)}) collective-permute-start(f32[128,128]{1,0:T(8,128)S(1)} %get-tuple-element.69), channel_id=1, source_target_pairs={{0,8},{4,12},{8,0},{12,4},{16,24},{20,28},{24,16},{28,20},{1,9},{5... | collective-permute-start | bytes 196616 | tf_op jit(solution)/shard_map/ppermute | solution.py:101
  29.7 1.8 %collective-permute-start.14 = (f32[8,256]{1,0:T(8,128)S(1)}, f32[8,256]{1,0:T(8,128)S(1)}, u32[]{:S(2)}, u32[]{:S(2)}) collective-permute-start(f32[8,256]{1,0:T(8,128)S(1)} %get-tuple-element.75.refs_0_), channel_id=1, source_target_pairs={{0,3},{1,0},{2,1},{3,2},{4,7},{5,4},{6,5},{7,6},{8,11},{9,8},{10,9... | collective-permute-start | bytes 24584 | tf_op jit(solution)/shard_map/ppermute | solution.py:575
  29.7 3.7 %collective-permute-start.13 = (f32[8,256]{1,0:T(8,128)S(1)}, f32[8,256]{1,0:T(8,128)S(1)}, u32[]{:S(2)}, u32[]{:S(2)}) collective-permute-start(f32[8,256]{1,0:T(8,128)S(1)} %get-tuple-element.75.refs_0_), channel_id=1, source_target_pairs={{0,2},{1,3},{2,0},{3,1},{4,6},{5,7},{6,4},{7,5},{8,10},{9,11},{10,... | collective-permute-start | bytes 24584 | tf_op jit(solution)/shard_map/ppermute | solution.py:575
  31.2 3.1 %collective-permute-start.12 = (f32[8,256]{1,0:T(8,128)S(1)}, f32[8,256]{1,0:T(8,128)S(1)}, u32[]{:S(2)}, u32[]{:S(2)}) collective-permute-start(f32[8,256]{1,0:T(8,128)S(1)} %get-tuple-element.75.refs_0_), channel_id=1, source_target_pairs={{0,1},{1,2},{2,3},{3,0},{4,5},{5,6},{6,7},{7,4},{8,9},{9,10},{10,1... | collective-permute-start | bytes 24584 | tf_op jit(solution)/shard_map/ppermute | solution.py:575
  35.0 7.0 %collective-permute-start.15 = (f32[256,128]{1,0:T(8,128)S(1)}, f32[256,128]{1,0:T(8,128)S(1)}, u32[]{:S(2)}, u32[]{:S(2)}) collective-permute-start(f32[256,128]{1,0:T(8,128)S(1)} %get-tuple-element.83), channel_id=1, source_target_pairs={{0,12},{4,8},{8,4},{12,0},{16,28},{20,24},{24,20},{28,16},{1,13},{... | collective-permute-start | bytes 393224 | tf_op jit(solution)/shard_map/ppermute | solution.py:101
  37.1 5.8 %collective-permute-start.16 = (f32[256,128]{1,0:T(8,128)S(1)}, f32[256,128]{1,0:T(8,128)S(1)}, u32[]{:S(2)}, u32[]{:S(2)}) collective-permute-start(f32[256,128]{1,0:T(8,128)S(1)} %get-tuple-element.84), channel_id=1, source_target_pairs={{0,4},{4,0},{8,12},{12,8},{16,20},{20,16},{24,28},{28,24},{1,5},{5... | collective-permute-start | bytes 393224 | tf_op jit(solution)/shard_map/ppermute | solution.py:101
  37.8 5.0 %collective-permute-start.17 = (f32[256,128]{1,0:T(8,128)S(1)}, f32[256,128]{1,0:T(8,128)S(1)}, u32[]{:S(2)}, u32[]{:S(2)}) collective-permute-start(f32[256,128]{1,0:T(8,128)S(1)} %get-tuple-element.85), channel_id=1, source_target_pairs={{0,8},{4,12},{8,0},{12,4},{16,24},{20,28},{24,16},{28,20},{1,9},{5... | collective-permute-start | bytes 393224 | tf_op jit(solution)/shard_map/ppermute | solution.py:101
  38.5 4.3 %copy-start.4 = (f32[8,128,128]{2,1,0:T(8,128)S(1)}, f32[8,128,128]{2,1,0:T(8,128)}, u32[]{:S(2)}) copy-start(f32[8,128,128]{2,1,0:T(8,128)} %param.15) | copy-start | bytes 1572868
  43.1 7.5 %collective-permute-start.21 = (f32[256,128]{1,0:T(8,128)S(1)}, f32[256,128]{1,0:T(8,128)S(1)}, u32[]{:S(2)}, u32[]{:S(2)}) collective-permute-start(f32[256,128]{1,0:T(8,128)S(1)} %get-tuple-element.91.refs_4_), channel_id=1, source_target_pairs={{0,16},{4,20},{8,24},{12,28},{16,0},{20,4},{24,8},{28,12},{1,17},{... | collective-permute-start | bytes 393224 | tf_op jit(solution)/shard_map/ppermute | solution.py:116
  46.6 8.1 %collective-permute-start.18 = (f32[256,128]{1,0:T(8,128)S(1)}, f32[256,128]{1,0:T(8,128)S(1)}, u32[]{:S(2)}, u32[]{:S(2)}) collective-permute-start(f32[256,128]{1,0:T(8,128)S(1)} %get-tuple-element.88), channel_id=1, source_target_pairs={{0,12},{4,8},{8,4},{12,0},{16,28},{20,24},{24,20},{28,16},{1,13},{... | collective-permute-start | bytes 393224 | tf_op jit(solution)/shard_map/ppermute | solution.py:101
  48.1 9.2 %collective-permute-start.19 = (f32[256,128]{1,0:T(8,128)S(1)}, f32[256,128]{1,0:T(8,128)S(1)}, u32[]{:S(2)}, u32[]{:S(2)}) collective-permute-start(f32[256,128]{1,0:T(8,128)S(1)} %get-tuple-element.89), channel_id=1, source_target_pairs={{0,4},{4,0},{8,12},{12,8},{16,20},{20,16},{24,28},{28,24},{1,5},{5... | collective-permute-start | bytes 393224 | tf_op jit(solution)/shard_map/ppermute | solution.py:101
  49.1 8.2 %collective-permute-start.20 = (f32[256,128]{1,0:T(8,128)S(1)}, f32[256,128]{1,0:T(8,128)S(1)}, u32[]{:S(2)}, u32[]{:S(2)}) collective-permute-start(f32[256,128]{1,0:T(8,128)S(1)} %get-tuple-element.90), channel_id=1, source_target_pairs={{0,8},{4,12},{8,0},{12,4},{16,24},{20,28},{24,16},{28,20},{1,9},{5... | collective-permute-start | bytes 393224 | tf_op jit(solution)/shard_map/ppermute | solution.py:101
  50.8 9.0 %collective-permute-start.22 = (f32[256,128]{1,0:T(8,128)S(1)}, f32[256,128]{1,0:T(8,128)S(1)}, u32[]{:S(2)}, u32[]{:S(2)}) collective-permute-start(f32[256,128]{1,0:T(8,128)S(1)} %get-tuple-element.93), channel_id=1, source_target_pairs={{0,12},{4,8},{8,4},{12,0},{16,28},{20,24},{24,20},{28,16},{1,13},{... | collective-permute-start | bytes 393224 | tf_op jit(solution)/shard_map/ppermute | solution.py:101
  52.8 6.9 %collective-permute-start.23 = (f32[256,128]{1,0:T(8,128)S(1)}, f32[256,128]{1,0:T(8,128)S(1)}, u32[]{:S(2)}, u32[]{:S(2)}) collective-permute-start(f32[256,128]{1,0:T(8,128)S(1)} %get-tuple-element.94), channel_id=1, source_target_pairs={{0,4},{4,0},{8,12},{12,8},{16,20},{20,16},{24,28},{28,24},{1,5},{5... | collective-permute-start | bytes 393224 | tf_op jit(solution)/shard_map/ppermute | solution.py:101
  54.7 6.1 %collective-permute-start.24 = (f32[256,128]{1,0:T(8,128)S(1)}, f32[256,128]{1,0:T(8,128)S(1)}, u32[]{:S(2)}, u32[]{:S(2)}) collective-permute-start(f32[256,128]{1,0:T(8,128)S(1)} %get-tuple-element.95), channel_id=1, source_target_pairs={{0,8},{4,12},{8,0},{12,4},{16,24},{20,28},{24,16},{28,20},{1,9},{5... | collective-permute-start | bytes 393224 | tf_op jit(solution)/shard_map/ppermute | solution.py:101

commit v8 on v7

--- a/solution.py
+++ b/solution.py
@@ -104,12 +104,11 @@
         return [self.swap(piece, way) for way, piece in zip(self.ways, pieces)]
 
     def first_messages(self):
+        return [(way, c) for c in range(self.chunks) for way in self.ways]
+
+    def last_messages(self):
         cuts = [(way, c) for c in range(self.chunks) for way in [0] + self.near]
         return cuts + [(way, None) for way in self.far]
-
-    def part_of(self, ref, way, chunk):
-        start = chunk * self.chunk_rows if way in self.far else 0
-        return ref[start : start + self.chunk_rows]
 
     def from_groups(self, piece):
         return [
@@ -161,13 +160,9 @@
     if heads < LOG_ROWS:
         log_tile = jnp.concatenate([log_tile, jnp.zeros((LOG_ROWS - heads, size), F32)])
     for (way, chunk), send_ref in zip(plan.first_messages(), send_refs):
-        member = plan.toward(way)
-        whole = chunk is None
-        part = plan.rows_of(member) if whole else plan.chunk_of(member, chunk)
-        rows = plan.rows if whole else plan.chunk_rows
-        send_ref[:rows] = held_ref[part]
-        if not chunk:
-            send_ref[rows:] = log_tile
+        send_ref[: plan.chunk_rows] = held_ref[plan.chunk_of(plan.toward(way), chunk)]
+        if chunk == 0:
+            send_ref[plan.chunk_rows :] = log_tile
 
 
 def group_total_body(plan, chunk, *refs):
@@ -176,13 +171,13 @@
     if chunk == 0:
         total_ref, logs_ref = refs[:2]
         for k, part_ref in enumerate(part_refs):
-            logs_ref[plan.peer(k)] = part_ref[part_ref.shape[0] - LOG_ROWS :]
+            logs_ref[plan.peer(k)] = part_ref[rows:]
         total_ref[rows:] = sum(logs_ref[b] for b in range(plan.members))
     else:
         logs_ref, total_ref = refs[:2]
     held_ref = refs[2]
     for way, part_ref in zip(plan.ways, part_refs):
-        held_ref[plan.toward(way)] = plan.part_of(part_ref, way, chunk)
+        held_ref[plan.toward(way)] = part_ref[:rows]
     total = jnp.zeros((rows, plan.size), F32)
     for b in range(plan.members):
         total = own_decays(plan, logs_ref.at[b], chunk) * total + held_ref[b]
@@ -224,7 +219,7 @@
         after = own_decays(plan, group_logs_ref.at[group], chunk) * state + groups_ref[group]
         state = jnp.where(group < plan.group(), after, state)
     for way, part_ref in zip(plan.ways, part_refs):
-        held_ref[plan.toward(way)] = plan.part_of(part_ref, way, chunk)
+        held_ref[plan.toward(way)] = part_ref[:rows]
     for b in range(plan.members):
         summary = held_ref[b]
         held_ref[b] = state
@@ -340,12 +335,12 @@
 
 
 def attended_body(plan, *refs):
-    count = len(plan.first_messages())
+    count = len(plan.last_messages())
     state_refs, refs = refs[:count], refs[count:]
     intra_ref, query_ref, cum_col_ref, gained_ref = refs[:4]
     attended_ref, sums_ref, states_ref = refs[4:]
     size, length = plan.size, query_ref.shape[0]
-    for (way, chunk), state_ref in zip(plan.first_messages(), state_refs):
+    for (way, chunk), state_ref in zip(plan.last_messages(), state_refs):
         member = plan.toward(way)
         part = plan.rows_of(member) if chunk is None else plan.chunk_of(member, chunk)
         states_ref[part] = state_ref[...].astype(BF16)
@@ -491,15 +486,7 @@
     messages = plan.first_messages()
     *sends, cum_log, cum_col = call(
         bind(summary_body),
-        [
-            shaped(
-                (
-                    (plan.rows if chunk is None else plan.chunk_rows) + (0 if chunk else LOG_ROWS),
-                    size,
-                )
-            )
-            for _, chunk in messages
-        ]
+        [chunk_piece if chunk else logged for _, chunk in messages]
         + [shaped((heads, length)), shaped((length, heads))],
         [pltpu.with_memory_space_constraint(x, pltpu.HBM) for x in (key_rows, value_rows, log_decay)],
         [
@@ -512,7 +499,7 @@
         specs=[HBM] * 3,
     )
     received = {key: plan.swap(send, key[0]) for key, send in zip(messages, sends)}
-    parts = [[received[way, None if way in plan.far else c] for way in plan.ways] for c in chunks]
+    parts = [[received[way, c] for way in plan.ways] for c in chunks]
     totals = []
     for c in chunks:
         if c == 0:
@@ -569,11 +556,11 @@
     attended, sums, states = call(
         bind(attended_body),
         [table, shaped((8, length)), shaped((width, size), BF16)],
-        [*[states[key] for key in messages], intra, query_rows, cum_col, gained],
+        [*[states[key] for key in plan.last_messages()], intra, query_rows, cum_col, gained],
     )
     all_sums = [sums] + [
-        lax.ppermute(sums, "head", [(i, (i + step) % parties) for i in range(parties)])
-        for step in range(1, parties)
+        lax.ppermute(sums, "head", [(i, i ^ way) for i in range(parties)])
+        for way in range(1, parties)
     ]
     attn_grad, summary, *sends = call(
         bind(attn_grad_body, parties),

time: 62.8 us -> 64.4 us (1.025)
  waiting for transfers between devices: 14.2 us -> 19.2 us
  starting transfers between devices: 36.9 us -> 33.5 us
    ppermute x19 -> x20, starting transfers between devices: 28.2 us -> 23.9 us  [swap(): return lax.ppermute(piece, 'seq', pairs) if way else piece]
    ppermute x19 -> x20, waiting for transfers between devices: 8.88 us -> 12.5 us  [swap(): return lax.ppermute(piece, 'seq', pairs) if way else piece]
    ppermute x3, waiting for transfers between devices: 2.48 us -> 4.86 us  [from_groups(): lax.ppermute(piece, 'seq', [(i, (i + step * self.members) % self.blocks)...]
    ppermute x3, waiting for transfers between devices: 2.85 us -> 1.82 us  [on_device(): lax.ppermute(sums, 'head', [(i, i ^ way) for i in range(parties)])]
    ppermute x3, starting transfers between devices: 6.9 us -> 7.74 us  [from_groups(): lax.ppermute(piece, 'seq', [(i, (i + step * self.members) % self.blocks)...]
  transfers between devices with their start and end apart: 25 -> 26, of which waited for: 11 -> 16; matrix products, arithmetic and copies ran while one was open for 0% -> 0% of each run, Pallas kernels for 8% -> 8%
where the time goes in v8:
time: 64.4 us; the launch traced here: 64.2 us
  starting transfers between devices  33.5 us (52%)
  waiting for transfers between devices  19.2 us (30%)
  Pallas kernels  10.7 us (17%)
  between operations  0.75 us (1%)
    ppermute x20, starting transfers between devices, swap(): return lax.ppermute(piece, 'seq', pairs) if way else piece  23.9 us
    ppermute x20, waiting for transfers between devices, swap(): return lax.ppermute(piece, 'seq', pairs) if way else piece  12.5 us
    pallas_call x12, Pallas kernels, call(): pl.pallas_call(body, out_shape=outs, in_specs=specs or [VMEM] * len(opera...  10.7 us
    ppermute x3, starting transfers between devices, from_groups(): lax.ppermute(piece, 'seq', [(i, (i + step * self.members) % self.blocks)...  7.74 us
    ppermute x3, waiting for transfers between devices, from_groups(): lax.ppermute(piece, 'seq', [(i, (i + step * self.members) % self.blocks)...  4.86 us
    ppermute x3, starting transfers between devices, on_device(): lax.ppermute(sums, 'head', [(i, i ^ way) for i in range(parties)])  1.89 us
    ppermute x3, waiting for transfers between devices, on_device(): lax.ppermute(sums, 'head', [(i, i ^ way) for i in range(parties)])  1.82 us
  transfers between devices with their start and end apart: 26, of which 16 were waited for; matrix products, arithmetic and copies ran while one was open for 0% of the time, Pallas kernels for 8%

profile of v8, /device:TPU:0, one launch (start us, length us, event | category | flops | bytes accessed | tf_op | source)
XLA Modules:
  0.0 64.2 jit_solution(1317686835495751098)
XLA Ops:
  0.6 2.2 %shard_map.111 = (f32[136,128]{1,0:T(8,128)S(1)}, f32[136,128]{1,0:T(8,128)S(1)}, f32[136,128]{1,0:T(8,128)S(1)}, f32[136,128]{1,0:T(8,128)S(1)}, f32[128,128]{1...) custom-call(bf16[256,1024]{1,0:T(8,128)(2,1)} %refs_10_.1, ...), custom_call_target="tpu_custom_call" | custom-call | tf_op jit(solution)/shard_map/pallas_call | solution.py:25
  2.8 4.0 %collective-permute-start = (f32[136,128]{1,0:T(8,128)S(1)}, f32[136,128]{1,0:T(8,128)S(1)}, u32[]{:S(2)}, u32[]{:S(2)}) collective-permute-start(f32[136,128]{1,0:T(8,128)S(1)} %get-tuple-element.55), channel_id=1, source_target_pairs={{0,12},{4,8},{8,4},{12,0},{16,28},{20,24},{24,20},{28,16},{1,13},{... | collective-permute-start | bytes 208904 | tf_op jit(solution)/shard_map/ppermute | solution.py:101
  6.9 0.5 collective-permute-start.1
  7.5 2.8 %collective-permute-start.6 = (f32[128,128]{1,0:T(8,128)S(1)}, f32[128,128]{1,0:T(8,128)S(1)}, u32[]{:S(2)}, u32[]{:S(2)}) collective-permute-start(f32[128,128]{1,0:T(8,128)S(1)} %get-tuple-element.64), channel_id=1, source_target_pairs={{0,12},{4,8},{8,4},{12,0},{16,28},{20,24},{24,20},{28,16},{1,13},{... | collective-permute-start | bytes 196616 | tf_op jit(solution)/shard_map/ppermute | solution.py:101
  10.3 0.5 collective-permute-start.7
  10.9 0.8 %collective-permute-start.8 = (f32[128,128]{1,0:T(8,128)S(1)}, f32[128,128]{1,0:T(8,128)S(1)}, u32[]{:S(2)}, u32[]{:S(2)}) collective-permute-start(f32[128,128]{1,0:T(8,128)S(1)} %get-tuple-element.66), channel_id=1, source_target_pairs={{0,8},{4,12},{8,0},{12,4},{16,24},{20,28},{24,16},{28,20},{1,9},{5... | collective-permute-start | bytes 196616 | tf_op jit(solution)/shard_map/ppermute | solution.py:101
  11.6 0.4 collective-permute-done.1.refs_2_
  12.0 2.7 %collective-permute-start.3 = (f32[136,128]{1,0:T(8,128)S(1)}, f32[136,128]{1,0:T(8,128)S(1)}, u32[]{:S(2)}, u32[]{:S(2)}) collective-permute-start(f32[136,128]{1,0:T(8,128)S(1)} %get-tuple-element.58.refs_4_), channel_id=1, source_target_pairs={{0,16},{4,20},{8,24},{12,28},{16,0},{20,4},{24,8},{28,12},{1,17},{... | collective-permute-start | bytes 208904 | tf_op jit(solution)/shard_map/ppermute | solution.py:115
  14.7 0.5 collective-permute-done.8.refs_3_
  15.3 2.6 %collective-permute-start.9 = (f32[128,128]{1,0:T(8,128)S(1)}, f32[128,128]{1,0:T(8,128)S(1)}, u32[]{:S(2)}, u32[]{:S(2)}) collective-permute-start(f32[128,128]{1,0:T(8,128)S(1)} %shard_map.114.refs_4_), channel_id=1, source_target_pairs={{0,16},{4,20},{8,24},{12,28},{16,0},{20,4},{24,8},{28,12},{1,17},{... | collective-permute-start | bytes 196616 | tf_op jit(solution)/shard_map/ppermute | solution.py:115
  17.8 1.5 %collective-permute-done.3.refs_5_ = f32[136,128]{1,0:T(8,128)S(1)} collective-permute-done((f32[136,128]{1,0:T(8,128)S(1)}, f32[136,128]{1,0:T(8,128)S(1)}, u32[]{:S(2)}, u32[]{:S(2)}) %collective-permute-start.3) | collective-permute-done | bytes 69664 | tf_op jit(solution)/shard_map/ppermute | solution.py:115
  19.5 1.1 %collective-permute-start.4 = (f32[128,128]{1,0:T(8,128)S(1)}, f32[128,128]{1,0:T(8,128)S(1)}, u32[]{:S(2)}, u32[]{:S(2)}) collective-permute-start(f32[128,128]{1,0:T(8,128)S(1)} %get-tuple-element.61), channel_id=1, source_target_pairs={{0,4},{4,0},{8,12},{12,8},{16,20},{20,16},{24,28},{28,24},{1,5},{5... | collective-permute-start | bytes 196616 | tf_op jit(solution)/shard_map/ppermute | solution.py:101
  20.6 0.4 collective-permute-start.5
  21.1 2.1 %collective-permute-start.12 = (f32[256,128]{1,0:T(8,128)S(1)}, f32[256,128]{1,0:T(8,128)S(1)}, u32[]{:S(2)}, u32[]{:S(2)}) collective-permute-start(f32[256,128]{1,0:T(8,128)S(1)} %get-tuple-element.72), channel_id=1, source_target_pairs={{0,12},{4,8},{8,4},{12,0},{16,28},{20,24},{24,20},{28,16},{1,13},{... | collective-permute-start | bytes 393224 | tf_op jit(solution)/shard_map/ppermute | solution.py:101
  23.2 1.1 %collective-permute-start.10 = (f32[128,128]{1,0:T(8,128)S(1)}, f32[128,128]{1,0:T(8,128)S(1)}, u32[]{:S(2)}, u32[]{:S(2)}) collective-permute-start(f32[128,128]{1,0:T(8,128)S(1)} %get-tuple-element.70), channel_id=1, source_target_pairs={{0,4},{4,0},{8,12},{12,8},{16,20},{20,16},{24,28},{28,24},{1,5},{5... | collective-permute-start | bytes 196616 | tf_op jit(solution)/shard_map/ppermute | solution.py:101
  24.3 0.4 collective-permute-start.11
  24.6 0.6 collective-permute-done.4.refs_0_.refs_1_
  25.2 0.4 collective-permute-done.5.refs_1_.refs_2_
  25.7 1.2 %shard_map.116 = (bf16[8,256,256]{2,1,0:T(8,128)(2,1)S(1)}, f32[256,1024]{1,0:T(8,128)S(1)}, f32[256,1024]{1,0:T(8,128)S(1)}, bf16[8,128,256]{2,1,0:T(8,128)(2,1)S(1)}) custom-call(bf16[256,1024]{1,0:T(8,128)(2,1)S(1)} %copy-done.2, bf16[256,1024]{1,0:T(8,128)(2,1)S(1)} %copy-done, bf16[256,1024]{1,0:T(8,128)(2,1)S(1)} %copy-done.1, ...), custom_call_target="tpu_custom_call" | custom-call | flops 1000000000 | tf_op jit(solution)/shard_map/pallas_call | solution.py:25
  26.9 1.2 %collective-permute-done.10.refs_4_ = f32[128,128]{1,0:T(8,128)S(1)} collective-permute-done((f32[128,128]{1,0:T(8,128)S(1)}, f32[128,128]{1,0:T(8,128)S(1)}, u32[]{:S(2)}, u32[]{:S(2)}) %collective-permute-start.10) | collective-permute-done | bytes 65568 | tf_op jit(solution)/shard_map/ppermute | solution.py:101
  28.1 0.4 collective-permute-done.11.refs_5_
  28.5 0.7 %shard_map.117 = (f32[256,1024]{1,0:T(8,128)S(1)}, f32[8,256]{1,0:T(8,128)S(1)}, bf16[1024,128]{1,0:T(8,128)(2,1)S(1)}) custom-call(f32[128,128]{1,0:T(8,128)S(1)} %get-tuple-element.60.refs_0_, f32[128,128]{1,0:T(8,128)S(1)} %collective-permute-done.4.refs_0_.refs_1_, f32[128,128]{1,0:T(8,128)S(1)} %collective-permute-done.5.refs_1_.refs_2_, ...), custom_call_target="tpu_custom_call" | custom-call | tf_op jit(solution)/shard_map/pallas_call | solution.py:25
  29.2 1.6 %collective-permute-start.14 = (f32[8,256]{1,0:T(8,128)S(1)}, f32[8,256]{1,0:T(8,128)S(1)}, u32[]{:S(2)}, u32[]{:S(2)}) collective-permute-start(f32[8,256]{1,0:T(8,128)S(1)} %get-tuple-element.77.refs_0_), channel_id=1, source_target_pairs={{0,2},{1,3},{2,0},{3,1},{4,6},{5,7},{6,4},{7,5},{8,10},{9,11},{10,... | collective-permute-start | bytes 24584 | tf_op jit(solution)/shard_map/ppermute | solution.py:562
  30.8 0.3 collective-permute-start.13
  31.1 1.2 %collective-permute-done.15.refs_3_ = f32[8,256]{1,0:T(8,128)S(1)} collective-permute-done((f32[8,256]{1,0:T(8,128)S(1)}, f32[8,256]{1,0:T(8,128)S(1)}, u32[]{:S(2)}, u32[]{:S(2)}) %collective-permute-start.15) | collective-permute-done | bytes 8224 | tf_op jit(solution)/shard_map/ppermute | solution.py:562
  32.3 0.6 collective-permute-done.14.refs_2_
  32.9 0.7 %shard_map.118 = (bf16[256,1024]{1,0:T(8,128)(2,1)S(1)}, f32[1024,128]{1,0:T(8,128)S(1)}, f32[256,128]{1,0:T(8,128)S(1)}, f32[256,128]{1,0:T(8,128)S(1)}, f32[25...) custom-call(f32[8,256]{1,0:T(8,128)S(1)} %get-tuple-element.77.refs_0_, f32[8,256]{1,0:T(8,128)S(1)} %collective-permute-done.13.refs_1_, ...), custom_call_target="tpu_custom_call" | custom-call | tf_op jit(solution)/shard_map/pallas_call | solution.py:25
  33.6 1.4 %collective-permute-start.16 = (f32[256,128]{1,0:T(8,128)S(1)}, f32[256,128]{1,0:T(8,128)S(1)}, u32[]{:S(2)}, u32[]{:S(2)}) collective-permute-start(f32[256,128]{1,0:T(8,128)S(1)} %get-tuple-element.85), channel_id=1, source_target_pairs={{0,12},{4,8},{8,4},{12,0},{16,28},{20,24},{24,20},{28,16},{1,13},{... | collective-permute-start | bytes 393224 | tf_op jit(solution)/shard_map/ppermute | solution.py:101
  35.0 1.0 %collective-permute-start.17 = (f32[256,128]{1,0:T(8,128)S(1)}, f32[256,128]{1,0:T(8,128)S(1)}, u32[]{:S(2)}, u32[]{:S(2)}) collective-permute-start(f32[256,128]{1,0:T(8,128)S(1)} %get-tuple-element.86), channel_id=1, source_target_pairs={{0,4},{4,0},{8,12},{12,8},{16,20},{20,16},{24,28},{28,24},{1,5},{5... | collective-permute-start | bytes 393224 | tf_op jit(solution)/shard_map/ppermute | solution.py:101
  36.0 1.2 %collective-permute-start.18 = (f32[256,128]{1,0:T(8,128)S(1)}, f32[256,128]{1,0:T(8,128)S(1)}, u32[]{:S(2)}, u32[]{:S(2)}) collective-permute-start(f32[256,128]{1,0:T(8,128)S(1)} %get-tuple-element.87), channel_id=1, source_target_pairs={{0,8},{4,12},{8,0},{12,4},{16,24},{20,28},{24,16},{28,20},{1,9},{5... | collective-permute-start | bytes 393224 | tf_op jit(solution)/shard_map/ppermute | solution.py:101
  37.2 3.4 %shard_map.119 = (bf16[256,1024]{1,0:T(8,128)(2,1)}, f32[256,1024]{1,0:T(8,128)S(1)}, f32[256,1024]{1,0:T(8,128)S(1)}) custom-call(bf16[256,1024]{1,0:T(8,128)(2,1)S(1)} %get-tuple-element.80.attn_grad_ref, bf16[256,1024]{1,0:T(8,128)(2,1)S(1)} %copy-done.2, bf16[256,1024]{1,0:T(8,128)(2,1)S(1)} %copy-done, bf16[256,1024]{1,0:T(8,128)(2,1)S(1)} %copy-done.1, ...), custom_call_target="tpu_custom_call" | custom-call | flops 671088640 | tf_op jit(solution)/shard_map/pallas_call | solution.py:25
  40.6 0.3 collective-permute-done.16.refs_1_
  40.9 2.3 %collective-permute-done.17.refs_2_ = f32[256,128]{1,0:T(8,128)S(1)} collective-permute-done((f32[256,128]{1,0:T(8,128)S(1)}, f32[256,128]{1,0:T(8,128)S(1)}, u32[]{:S(2)}, u32[]{:S(2)}) %collective-permute-start.17) | collective-permute-done | bytes 131104 | tf_op jit(solution)/shard_map/ppermute | solution.py:101
  43.3 0.2 shard_map.120
  43.5 2.5 %collective-permute-start.22 = (f32[256,128]{1,0:T(8,128)S(1)}, f32[256,128]{1,0:T(8,128)S(1)}, u32[]{:S(2)}, u32[]{:S(2)}) collective-permute-start(f32[256,128]{1,0:T(8,128)S(1)} %get-tuple-element.93.refs_4_), channel_id=1, source_target_pairs={{0,16},{4,20},{8,24},{12,28},{16,0},{20,4},{24,8},{28,12},{1,17},{... | collective-permute-start | bytes 393224 | tf_op jit(solution)/shard_map/ppermute | solution.py:115
  46.0 1.7 %collective-permute-start.19 = (f32[256,128]{1,0:T(8,128)S(1)}, f32[256,128]{1,0:T(8,128)S(1)}, u32[]{:S(2)}, u32[]{:S(2)}) collective-permute-start(f32[256,128]{1,0:T(8,128)S(1)} %get-tuple-element.90), channel_id=1, source_target_pairs={{0,12},{4,8},{8,4},{12,0},{16,28},{20,24},{24,20},{28,16},{1,13},{... | collective-permute-start | bytes 393224 | tf_op jit(solution)/shard_map/ppermute | solution.py:101
  47.8 1.0 %collective-permute-start.20 = (f32[256,128]{1,0:T(8,128)S(1)}, f32[256,128]{1,0:T(8,128)S(1)}, u32[]{:S(2)}, u32[]{:S(2)}) collective-permute-start(f32[256,128]{1,0:T(8,128)S(1)} %get-tuple-element.91), channel_id=1, source_target_pairs={{0,4},{4,0},{8,12},{12,8},{16,20},{20,16},{24,28},{28,24},{1,5},{5... | collective-permute-start | bytes 393224 | tf_op jit(solution)/shard_map/ppermute | solution.py:101
  48.7 0.8 %collective-permute-start.21 = (f32[256,128]{1,0:T(8,128)S(1)}, f32[256,128]{1,0:T(8,128)S(1)}, u32[]{:S(2)}, u32[]{:S(2)}) collective-permute-start(f32[256,128]{1,0:T(8,128)S(1)} %get-tuple-element.92), channel_id=1, source_target_pairs={{0,8},{4,12},{8,0},{12,4},{16,24},{20,28},{24,16},{28,20},{1,9},{5... | collective-permute-start | bytes 393224 | tf_op jit(solution)/shard_map/ppermute | solution.py:101
  49.5 3.3 %collective-permute-done.22.refs_5_ = f32[256,128]{1,0:T(8,128)S(1)} collective-permute-done((f32[256,128]{1,0:T(8,128)S(1)}, f32[256,128]{1,0:T(8,128)S(1)}, u32[]{:S(2)}, u32[]{:S(2)}) %collective-permute-start.22) | collective-permute-done | bytes 131104 | tf_op jit(solution)/shard_map/ppermute | solution.py:115
  52.8 0.2 shard_map.121
  53.1 0.5 collective-permute-start.23
  53.6 1.3 %collective-permute-start.24 = (f32[256,128]{1,0:T(8,128)S(1)}, f32[256,128]{1,0:T(8,128)S(1)}, u32[]{:S(2)}, u32[]{:S(2)}) collective-permute-start(f32[256,128]{1,0:T(8,128)S(1)} %get-tuple-element.96), channel_id=1, source_target_pairs={{0,4},{4,0},{8,12},{12,8},{16,20},{20,16},{24,28},{28,24},{1,5},{5... | collective-permute-start | bytes 393224 | tf_op jit(solution)/shard_map/ppermute | solution.py:101
  54.9 0.5 collective-permute-done.19.refs_1_
  55.4 1.2 %collective-permute-start.25 = (f32[256,128]{1,0:T(8,128)S(1)}, f32[256,128]{1,0:T(8,128)S(1)}, u32[]{:S(2)}, u32[]{:S(2)}) collective-permute-start(f32[256,128]{1,0:T(8,128)S(1)} %get-tuple-element.97), channel_id=1, source_target_pairs={{0,8},{4,12},{8,0},{12,4},{16,24},{20,28},{24,16},{28,20},{1,9},{5... | collective-permute-start | bytes 393224 | tf_op jit(solution)/shard_map/ppermute | solution.py:101
  56.6 1.2 %collective-permute-done.21.refs_3_ = f32[256,128]{1,0:T(8,128)S(1)} collective-permute-done((f32[256,128]{1,0:T(8,128)S(1)}, f32[256,128]{1,0:T(8,128)S(1)}, u32[]{:S(2)}, u32[]{:S(2)}) %collective-permute-start.21) | collective-permute-done | bytes 131104 | tf_op jit(solution)/shard_map/ppermute | solution.py:101
  57.9 3.2 %collective-permute-done.23.refs_5_ = f32[256,128]{1,0:T(8,128)S(1)} collective-permute-done((f32[256,128]{1,0:T(8,128)S(1)}, f32[256,128]{1,0:T(8,128)S(1)}, u32[]{:S(2)}, u32[]{:S(2)}) %collective-permute-start.23) | collective-permute-done | bytes 131104 | tf_op jit(solution)/shard_map/ppermute | solution.py:101
  61.0 1.5 %collective-permute-done.25.refs_7_ = f32[256,128]{1,0:T(8,128)S(1)} collective-permute-done((f32[256,128]{1,0:T(8,128)S(1)}, f32[256,128]{1,0:T(8,128)S(1)}, u32[]{:S(2)}, u32[]{:S(2)}) %collective-permute-start.25) | collective-permute-done | bytes 131104 | tf_op jit(solution)/shard_map/ppermute | solution.py:101
  62.5 1.7 %shard_map.122 = (bf16[256,1024]{1,0:T(8,128)(2,1)}, bf16[256,1024]{1,0:T(8,128)(2,1)}, f32[1024,128]{1,0:T(8,128)}) custom-call(f32[256,128]{1,0:T(8,128)S(1)} %get-tuple-element.89.refs_0_, f32[256,128]{1,0:T(8,128)S(1)} %collective-permute-done.19.refs_1_, f32[256,128]{1,0:T(8,128)S(1)} %collective-permute-done.20.refs_2_, ...), custom_call_target="tpu_custom_call" | custom-call | tf_op jit(solution)/shard_map/pallas_call | solution.py:25
  (30 shorter events, 0.5 us)
Async XLA Ops:
  2.8 8.0 %collective-permute-start = (f32[136,128]{1,0:T(8,128)S(1)}, f32[136,128]{1,0:T(8,128)S(1)}, u32[]{:S(2)}, u32[]{:S(2)}) collective-permute-start(f32[136,128]{1,0:T(8,128)S(1)} %get-tuple-element.55), channel_id=1, source_target_pairs={{0,12},{4,8},{8,4},{12,0},{16,28},{20,24},{24,20},{28,16},{1,13},{... | collective-permute-start | bytes 208904 | tf_op jit(solution)/shard_map/ppermute | solution.py:101
  6.9 5.1 %collective-permute-start.1 = (f32[136,128]{1,0:T(8,128)S(1)}, f32[136,128]{1,0:T(8,128)S(1)}, u32[]{:S(2)}, u32[]{:S(2)}) collective-permute-start(f32[136,128]{1,0:T(8,128)S(1)} %get-tuple-element.56), channel_id=1, source_target_pairs={{0,4},{4,0},{8,12},{12,8},{16,20},{20,16},{24,28},{28,24},{1,5},{5... | collective-permute-start | bytes 208904 | tf_op jit(solution)/shard_map/ppermute | solution.py:101
  7.4 4.6 %collective-permute-start.2 = (f32[136,128]{1,0:T(8,128)S(1)}, f32[136,128]{1,0:T(8,128)S(1)}, u32[]{:S(2)}, u32[]{:S(2)}) collective-permute-start(f32[136,128]{1,0:T(8,128)S(1)} %get-tuple-element.57), channel_id=1, source_target_pairs={{0,8},{4,12},{8,0},{12,4},{16,24},{20,28},{24,16},{28,20},{1,9},{5... | collective-permute-start | bytes 208904 | tf_op jit(solution)/shard_map/ppermute | solution.py:101
  7.5 7.2 %collective-permute-start.6 = (f32[128,128]{1,0:T(8,128)S(1)}, f32[128,128]{1,0:T(8,128)S(1)}, u32[]{:S(2)}, u32[]{:S(2)}) collective-permute-start(f32[128,128]{1,0:T(8,128)S(1)} %get-tuple-element.64), channel_id=1, source_target_pairs={{0,12},{4,8},{8,4},{12,0},{16,28},{20,24},{24,20},{28,16},{1,13},{... | collective-permute-start | bytes 196616 | tf_op jit(solution)/shard_map/ppermute | solution.py:101
  10.3 4.3 %collective-permute-start.7 = (f32[128,128]{1,0:T(8,128)S(1)}, f32[128,128]{1,0:T(8,128)S(1)}, u32[]{:S(2)}, u32[]{:S(2)}) collective-permute-start(f32[128,128]{1,0:T(8,128)S(1)} %get-tuple-element.65), channel_id=1, source_target_pairs={{0,4},{4,0},{8,12},{12,8},{16,20},{20,16},{24,28},{28,24},{1,5},{5... | collective-permute-start | bytes 196616 | tf_op jit(solution)/shard_map/ppermute | solution.py:101
  10.9 4.3 %collective-permute-start.8 = (f32[128,128]{1,0:T(8,128)S(1)}, f32[128,128]{1,0:T(8,128)S(1)}, u32[]{:S(2)}, u32[]{:S(2)}) collective-permute-start(f32[128,128]{1,0:T(8,128)S(1)} %get-tuple-element.66), channel_id=1, source_target_pairs={{0,8},{4,12},{8,0},{12,4},{16,24},{20,28},{24,16},{28,20},{1,9},{5... | collective-permute-start | bytes 196616 | tf_op jit(solution)/shard_map/ppermute | solution.py:101
  12.0 7.3 %collective-permute-start.3 = (f32[136,128]{1,0:T(8,128)S(1)}, f32[136,128]{1,0:T(8,128)S(1)}, u32[]{:S(2)}, u32[]{:S(2)}) collective-permute-start(f32[136,128]{1,0:T(8,128)S(1)} %get-tuple-element.58.refs_4_), channel_id=1, source_target_pairs={{0,16},{4,20},{8,24},{12,28},{16,0},{20,4},{24,8},{28,12},{1,17},{... | collective-permute-start | bytes 208904 | tf_op jit(solution)/shard_map/ppermute | solution.py:115
  15.2 4.2 %copy-start.3 = (f32[8,128,128]{2,1,0:T(8,128)S(1)}, f32[8,128,128]{2,1,0:T(8,128)}, u32[]{:S(2)}) copy-start(f32[8,128,128]{2,1,0:T(8,128)} %param.14) | copy-start | bytes 1572868
  15.2 10.4 %copy-start.5 = (bf16[256,1024]{1,0:T(8,128)(2,1)S(1)}, bf16[256,1024]{1,0:T(8,128)(2,1)}, u32[]{:S(2)}) copy-start(bf16[256,1024]{1,0:T(8,128)(2,1)} %upstream_ref.1) | copy-start | bytes 1572868
  15.3 5.7 %collective-permute-start.9 = (f32[128,128]{1,0:T(8,128)S(1)}, f32[128,128]{1,0:T(8,128)S(1)}, u32[]{:S(2)}, u32[]{:S(2)}) collective-permute-start(f32[128,128]{1,0:T(8,128)S(1)} %shard_map.114.refs_4_), channel_id=1, source_target_pairs={{0,16},{4,20},{8,24},{12,28},{16,0},{20,4},{24,8},{28,12},{1,17},{... | collective-permute-start | bytes 196616 | tf_op jit(solution)/shard_map/ppermute | solution.py:115
  19.4 6.3 %copy-start.1 = (bf16[256,1024]{1,0:T(8,128)(2,1)S(1)}, bf16[256,1024]{1,0:T(8,128)(2,1)}, u32[]{:S(2)}) copy-start(bf16[256,1024]{1,0:T(8,128)(2,1)} %refs_11_.1) | copy-start | bytes 1572868
  19.4 6.3 %copy-start.2 = (bf16[256,1024]{1,0:T(8,128)(2,1)S(1)}, bf16[256,1024]{1,0:T(8,128)(2,1)}, u32[]{:S(2)}) copy-start(bf16[256,1024]{1,0:T(8,128)(2,1)} %query_ref.3) | copy-start | bytes 1572868
  19.5 6.2 %copy-start = (bf16[256,1024]{1,0:T(8,128)(2,1)S(1)}, bf16[256,1024]{1,0:T(8,128)(2,1)}, u32[]{:S(2)}) copy-start(bf16[256,1024]{1,0:T(8,128)(2,1)} %refs_10_.1) | copy-start | bytes 1572868
  19.5 5.7 %collective-permute-start.4 = (f32[128,128]{1,0:T(8,128)S(1)}, f32[128,128]{1,0:T(8,128)S(1)}, u32[]{:S(2)}, u32[]{:S(2)}) collective-permute-start(f32[128,128]{1,0:T(8,128)S(1)} %get-tuple-element.61), channel_id=1, source_target_pairs={{0,4},{4,0},{8,12},{12,8},{16,20},{20,16},{24,28},{28,24},{1,5},{5... | collective-permute-start | bytes 196616 | tf_op jit(solution)/shard_map/ppermute | solution.py:101
  20.6 5.0 %collective-permute-start.5 = (f32[128,128]{1,0:T(8,128)S(1)}, f32[128,128]{1,0:T(8,128)S(1)}, u32[]{:S(2)}, u32[]{:S(2)}) collective-permute-start(f32[128,128]{1,0:T(8,128)S(1)} %get-tuple-element.62), channel_id=1, source_target_pairs={{0,8},{4,12},{8,0},{12,4},{16,24},{20,28},{24,16},{28,20},{1,9},{5... | collective-permute-start | bytes 196616 | tf_op jit(solution)/shard_map/ppermute | solution.py:101
  21.1 7.5 %collective-permute-start.12 = (f32[256,128]{1,0:T(8,128)S(1)}, f32[256,128]{1,0:T(8,128)S(1)}, u32[]{:S(2)}, u32[]{:S(2)}) collective-permute-start(f32[256,128]{1,0:T(8,128)S(1)} %get-tuple-element.72), channel_id=1, source_target_pairs={{0,12},{4,8},{8,4},{12,0},{16,28},{20,24},{24,20},{28,16},{1,13},{... | collective-permute-start | bytes 393224 | tf_op jit(solution)/shard_map/ppermute | solution.py:101
  23.2 2.5 %copy-start.6 = (f32[1024]{0:T(1024)S(1)}, f32[1024]{0:T(1024)}, u32[]{:S(2)}) copy-start(f32[1024]{0:T(1024)} %param.13) | copy-start | bytes 12292
  23.2 4.9 %collective-permute-start.10 = (f32[128,128]{1,0:T(8,128)S(1)}, f32[128,128]{1,0:T(8,128)S(1)}, u32[]{:S(2)}, u32[]{:S(2)}) collective-permute-start(f32[128,128]{1,0:T(8,128)S(1)} %get-tuple-element.70), channel_id=1, source_target_pairs={{0,4},{4,0},{8,12},{12,8},{16,20},{20,16},{24,28},{28,24},{1,5},{5... | collective-permute-start | bytes 196616 | tf_op jit(solution)/shard_map/ppermute | solution.py:101
  24.3 4.3 %collective-permute-start.11 = (f32[128,128]{1,0:T(8,128)S(1)}, f32[128,128]{1,0:T(8,128)S(1)}, u32[]{:S(2)}, u32[]{:S(2)}) collective-permute-start(f32[128,128]{1,0:T(8,128)S(1)} %get-tuple-element.71), channel_id=1, source_target_pairs={{0,8},{4,12},{8,0},{12,4},{16,24},{20,28},{24,16},{28,20},{1,9},{5... | collective-permute-start | bytes 196616 | tf_op jit(solution)/shard_map/ppermute | solution.py:101
  29.2 3.1 %collective-permute-start.15 = (f32[8,256]{1,0:T(8,128)S(1)}, f32[8,256]{1,0:T(8,128)S(1)}, u32[]{:S(2)}, u32[]{:S(2)}) collective-permute-start(f32[8,256]{1,0:T(8,128)S(1)} %get-tuple-element.77.refs_0_), channel_id=1, source_target_pairs={{0,3},{1,2},{2,1},{3,0},{4,7},{5,6},{6,5},{7,4},{8,11},{9,10},{10,... | collective-permute-start | bytes 24584 | tf_op jit(solution)/shard_map/ppermute | solution.py:562
  29.2 3.7 %collective-permute-start.14 = (f32[8,256]{1,0:T(8,128)S(1)}, f32[8,256]{1,0:T(8,128)S(1)}, u32[]{:S(2)}, u32[]{:S(2)}) collective-permute-start(f32[8,256]{1,0:T(8,128)S(1)} %get-tuple-element.77.refs_0_), channel_id=1, source_target_pairs={{0,2},{1,3},{2,0},{3,1},{4,6},{5,7},{6,4},{7,5},{8,10},{9,11},{10,... | collective-permute-start | bytes 24584 | tf_op jit(solution)/shard_map/ppermute | solution.py:562
  30.8 2.1 %collective-permute-start.13 = (f32[8,256]{1,0:T(8,128)S(1)}, f32[8,256]{1,0:T(8,128)S(1)}, u32[]{:S(2)}, u32[]{:S(2)}) collective-permute-start(f32[8,256]{1,0:T(8,128)S(1)} %get-tuple-element.77.refs_0_), channel_id=1, source_target_pairs={{0,1},{1,0},{2,3},{3,2},{4,5},{5,4},{6,7},{7,6},{8,9},{9,8},{10,11... | collective-permute-start | bytes 24584 | tf_op jit(solution)/shard_map/ppermute | solution.py:562
  33.6 7.3 %collective-permute-start.16 = (f32[256,128]{1,0:T(8,128)S(1)}, f32[256,128]{1,0:T(8,128)S(1)}, u32[]{:S(2)}, u32[]{:S(2)}) collective-permute-start(f32[256,128]{1,0:T(8,128)S(1)} %get-tuple-element.85), channel_id=1, source_target_pairs={{0,12},{4,8},{8,4},{12,0},{16,28},{20,24},{24,20},{28,16},{1,13},{... | collective-permute-start | bytes 393224 | tf_op jit(solution)/shard_map/ppermute | solution.py:101
  35.0 8.2 %collective-permute-start.17 = (f32[256,128]{1,0:T(8,128)S(1)}, f32[256,128]{1,0:T(8,128)S(1)}, u32[]{:S(2)}, u32[]{:S(2)}) collective-permute-start(f32[256,128]{1,0:T(8,128)S(1)} %get-tuple-element.86), channel_id=1, source_target_pairs={{0,4},{4,0},{8,12},{12,8},{16,20},{20,16},{24,28},{28,24},{1,5},{5... | collective-permute-start | bytes 393224 | tf_op jit(solution)/shard_map/ppermute | solution.py:101
  36.0 7.3 %collective-permute-start.18 = (f32[256,128]{1,0:T(8,128)S(1)}, f32[256,128]{1,0:T(8,128)S(1)}, u32[]{:S(2)}, u32[]{:S(2)}) collective-permute-start(f32[256,128]{1,0:T(8,128)S(1)} %get-tuple-element.87), channel_id=1, source_target_pairs={{0,8},{4,12},{8,0},{12,4},{16,24},{20,28},{24,16},{28,20},{1,9},{5... | collective-permute-start | bytes 393224 | tf_op jit(solution)/shard_map/ppermute | solution.py:101
  37.2 6.1 %copy-start.4 = (f32[8,128,128]{2,1,0:T(8,128)S(1)}, f32[8,128,128]{2,1,0:T(8,128)}, u32[]{:S(2)}) copy-start(f32[8,128,128]{2,1,0:T(8,128)} %param.15) | copy-start | bytes 1572868
  43.5 9.3 %collective-permute-start.22 = (f32[256,128]{1,0:T(8,128)S(1)}, f32[256,128]{1,0:T(8,128)S(1)}, u32[]{:S(2)}, u32[]{:S(2)}) collective-permute-start(f32[256,128]{1,0:T(8,128)S(1)} %get-tuple-element.93.refs_4_), channel_id=1, source_target_pairs={{0,16},{4,20},{8,24},{12,28},{16,0},{20,4},{24,8},{28,12},{1,17},{... | collective-permute-start | bytes 393224 | tf_op jit(solution)/shard_map/ppermute | solution.py:115
  46.0 9.4 %collective-permute-start.19 = (f32[256,128]{1,0:T(8,128)S(1)}, f32[256,128]{1,0:T(8,128)S(1)}, u32[]{:S(2)}, u32[]{:S(2)}) collective-permute-start(f32[256,128]{1,0:T(8,128)S(1)} %get-tuple-element.90), channel_id=1, source_target_pairs={{0,12},{4,8},{8,4},{12,0},{16,28},{20,24},{24,20},{28,16},{1,13},{... | collective-permute-start | bytes 393224 | tf_op jit(solution)/shard_map/ppermute | solution.py:101
  47.8 8.9 %collective-permute-start.20 = (f32[256,128]{1,0:T(8,128)S(1)}, f32[256,128]{1,0:T(8,128)S(1)}, u32[]{:S(2)}, u32[]{:S(2)}) collective-permute-start(f32[256,128]{1,0:T(8,128)S(1)} %get-tuple-element.91), channel_id=1, source_target_pairs={{0,4},{4,0},{8,12},{12,8},{16,20},{20,16},{24,28},{28,24},{1,5},{5... | collective-permute-start | bytes 393224 | tf_op jit(solution)/shard_map/ppermute | solution.py:101
  48.7 9.1 %collective-permute-start.21 = (f32[256,128]{1,0:T(8,128)S(1)}, f32[256,128]{1,0:T(8,128)S(1)}, u32[]{:S(2)}, u32[]{:S(2)}) collective-permute-start(f32[256,128]{1,0:T(8,128)S(1)} %get-tuple-element.92), channel_id=1, source_target_pairs={{0,8},{4,12},{8,0},{12,4},{16,24},{20,28},{24,16},{28,20},{1,9},{5... | collective-permute-start | bytes 393224 | tf_op jit(solution)/shard_map/ppermute | solution.py:101
  53.1 7.9 %collective-permute-start.23 = (f32[256,128]{1,0:T(8,128)S(1)}, f32[256,128]{1,0:T(8,128)S(1)}, u32[]{:S(2)}, u32[]{:S(2)}) collective-permute-start(f32[256,128]{1,0:T(8,128)S(1)} %get-tuple-element.95), channel_id=1, source_target_pairs={{0,12},{4,8},{8,4},{12,0},{16,28},{20,24},{24,20},{28,16},{1,13},{... | collective-permute-start | bytes 393224 | tf_op jit(solution)/shard_map/ppermute | solution.py:101
  53.6 7.4 %collective-permute-start.24 = (f32[256,128]{1,0:T(8,128)S(1)}, f32[256,128]{1,0:T(8,128)S(1)}, u32[]{:S(2)}, u32[]{:S(2)}) collective-permute-start(f32[256,128]{1,0:T(8,128)S(1)} %get-tuple-element.96), channel_id=1, source_target_pairs={{0,4},{4,0},{8,12},{12,8},{16,20},{20,16},{24,28},{28,24},{1,5},{5... | collective-permute-start | bytes 393224 | tf_op jit(solution)/shard_map/ppermute | solution.py:101
  55.4 7.1 %collective-permute-start.25 = (f32[256,128]{1,0:T(8,128)S(1)}, f32[256,128]{1,0:T(8,128)S(1)}, u32[]{:S(2)}, u32[]{:S(2)}) collective-permute-start(f32[256,128]{1,0:T(8,128)S(1)} %get-tuple-element.97), channel_id=1, source_target_pairs={{0,8},{4,12},{8,0},{12,4},{16,24},{20,28},{24,16},{28,20},{1,9},{5... | collective-permute-start | bytes 393224 | tf_op jit(solution)/shard_map/ppermute | solution.py:101

commit v9 on v8

--- a/solution.py
+++ b/solution.py
@@ -100,8 +100,8 @@
         pairs = [(i, i // span * span + (i % span ^ way)) for i in range(self.blocks)]
         return lax.ppermute(piece, "seq", pairs) if way else piece
 
-    def swap_in_group(self, pieces):
-        return [self.swap(piece, way) for way, piece in zip(self.ways, pieces)]
+    def swap_in_group(self, pieces, order=None):
+        return [self.swap(piece, way) for way, piece in zip(order or self.ways, pieces)]
 
     def first_messages(self):
         return [(way, c) for c in range(self.chunks) for way in self.ways]
@@ -264,8 +264,8 @@
         after = suffixes(plan, held_ref, logs_ref, grad_ref[plan.rows_of(plan.member())])[0]
         for b in range(plan.members):
             held_ref[b] = jnp.where(first, before[b], after[b])
-        for k, send_ref in enumerate(send_refs):
-            send_ref[...] = held_ref[plan.peer(k)]
+        for way, send_ref in enumerate(send_refs):
+            send_ref[...] = held_ref[plan.toward(way)]
 
 
 def reverse_scan_body(plan, *refs):
@@ -422,8 +422,8 @@
     key_out, value_out, total_out, held_ref, key_grad_ref, value_grad_ref, total_ref, sems = refs[7:]
     length, size = key_ref.shape[0], plan.size
     swapped = jnp.where(plan.group() == 0, 0, 1) if plan.groups == 2 else 0
-    for k in range(plan.members):
-        held_ref[swapped, plan.rows_of(plan.peer(k))] = first_refs[k][...]
+    for k, way in enumerate(range(plan.members) if plan.groups == 2 else plan.ways):
+        held_ref[swapped, plan.rows_of(plan.toward(way))] = first_refs[k][...]
         held_ref[1 - swapped, plan.rows_of(plan.peer(k))] = second_refs[k][...]
     cum_col = cum_col_ref[...]
     block_log = cum_col[length - 1 : length, :]
@@ -559,8 +559,8 @@
         [*[states[key] for key in plan.last_messages()], intra, query_rows, cum_col, gained],
     )
     all_sums = [sums] + [
-        lax.ppermute(sums, "head", [(i, i ^ way) for i in range(parties)])
-        for way in range(1, parties)
+        lax.ppermute(sums, "head", [(i, (i + step) % parties) for i in range(parties)])
+        for step in range(1, parties)
     ]
     attn_grad, summary, *sends = call(
         bind(attn_grad_body, parties),
@@ -584,7 +584,7 @@
         specs=[VMEM] * (plan.members + 2) + [ANY],
     )
     totals = [total] + plan.from_groups(total)
-    swapped = [plan.swap_in_group(sends)] if two_sided else []
+    swapped = [plan.swap_in_group(sends, range(plan.members))] if two_sided else []
     sends = call(
         bind(reverse_scan_body),
         pieces * (1 if two_sided else 2),

time: 64.4 us -> 61.8 us (0.960); the launches traced: 64.2 us -> 60.9 us
  waiting for transfers between devices: 19.2 us -> 16 us
    ppermute x3, waiting for transfers between devices: 4.86 us -> 2.32 us  [from_groups(): lax.ppermute(piece, 'seq', [(i, (i + step * self.members) % self.blocks)...]
    ppermute x20, waiting for transfers between devices: 12.5 us -> 10.8 us  [swap(): return lax.ppermute(piece, 'seq', pairs) if way else piece]
    ppermute x3, waiting for transfers between devices: 1.82 us -> 2.85 us  [on_device(): lax.ppermute(sums, 'head', [(i, (i + step) % parties) for i in range(part...]
  transfers between devices with their start and end apart: 26 -> 26, of which waited for: 16 -> 16; matrix products, arithmetic and copies ran while one was open for 0% -> 0% of each run, Pallas kernels for 8% -> 9%
where the time goes in v9:
time: 61.8 us; the launch traced here: 60.9 us
  starting transfers between devices  33.4 us (54%)
  waiting for transfers between devices  16 us (26%)
  Pallas kernels  10.7 us (17%)
  between operations  0.75 us (1%)
    ppermute x20, starting transfers between devices, swap(): return lax.ppermute(piece, 'seq', pairs) if way else piece  23.6 us
    ppermute x20, waiting for transfers between devices, swap(): return lax.ppermute(piece, 'seq', pairs) if way else piece  10.8 us
    pallas_call x12, Pallas kernels, call(): pl.pallas_call(body, out_shape=outs, in_specs=specs or [VMEM] * len(opera...  10.7 us
    ppermute x3, starting transfers between devices, from_groups(): lax.ppermute(piece, 'seq', [(i, (i + step * self.members) % self.blocks)...  7.97 us
    ppermute x3, waiting for transfers between devices, on_device(): lax.ppermute(sums, 'head', [(i, (i + step) % parties) for i in range(part...  2.85 us
    ppermute x3, waiting for transfers between devices, from_groups(): lax.ppermute(piece, 'seq', [(i, (i + step * self.members) % self.blocks)...  2.32 us
    ppermute x3, starting transfers between devices, on_device(): lax.ppermute(sums, 'head', [(i, (i + step) % parties) for i in range(part...  1.8 us
  transfers between devices with their start and end apart: 26, of which 16 were waited for; matrix products, arithmetic and copies ran while one was open for 0% of the time, Pallas kernels for 9%

profile of v9, /device:TPU:0, one launch (start us, length us, event | category | flops | bytes accessed | tf_op | source)
XLA Modules:
  0.0 60.9 jit_solution(5660690197536799438)
XLA Ops:
  0.6 2.2 %shard_map.111 = (f32[136,128]{1,0:T(8,128)S(1)}, f32[136,128]{1,0:T(8,128)S(1)}, f32[136,128]{1,0:T(8,128)S(1)}, f32[136,128]{1,0:T(8,128)S(1)}, f32[128,128]{1...) custom-call(bf16[256,1024]{1,0:T(8,128)(2,1)} %refs_10_.1, ...), custom_call_target="tpu_custom_call" | custom-call | tf_op jit(solution)/shard_map/pallas_call | solution.py:25
  2.8 4.0 %collective-permute-start = (f32[136,128]{1,0:T(8,128)S(1)}, f32[136,128]{1,0:T(8,128)S(1)}, u32[]{:S(2)}, u32[]{:S(2)}) collective-permute-start(f32[136,128]{1,0:T(8,128)S(1)} %get-tuple-element.55), channel_id=1, source_target_pairs={{0,12},{4,8},{8,4},{12,0},{16,28},{20,24},{24,20},{28,16},{1,13},{... | collective-permute-start | bytes 208904 | tf_op jit(solution)/shard_map/ppermute | solution.py:101
  6.9 0.5 collective-permute-start.1
  7.4 0.1 collective-permute-start.2
  7.5 2.8 %collective-permute-start.6 = (f32[128,128]{1,0:T(8,128)S(1)}, f32[128,128]{1,0:T(8,128)S(1)}, u32[]{:S(2)}, u32[]{:S(2)}) collective-permute-start(f32[128,128]{1,0:T(8,128)S(1)} %get-tuple-element.64), channel_id=1, source_target_pairs={{0,12},{4,8},{8,4},{12,0},{16,28},{20,24},{24,20},{28,16},{1,13},{... | collective-permute-start | bytes 196616 | tf_op jit(solution)/shard_map/ppermute | solution.py:101
  10.3 0.5 collective-permute-start.7
  10.9 0.8 %collective-permute-start.8 = (f32[128,128]{1,0:T(8,128)S(1)}, f32[128,128]{1,0:T(8,128)S(1)}, u32[]{:S(2)}, u32[]{:S(2)}) collective-permute-start(f32[128,128]{1,0:T(8,128)S(1)} %get-tuple-element.66), channel_id=1, source_target_pairs={{0,8},{4,12},{8,0},{12,4},{16,24},{20,28},{24,16},{28,20},{1,9},{5... | collective-permute-start | bytes 196616 | tf_op jit(solution)/shard_map/ppermute | solution.py:101
  11.6 0.4 collective-permute-done.1.refs_2_
  12.0 2.7 %collective-permute-start.3 = (f32[136,128]{1,0:T(8,128)S(1)}, f32[136,128]{1,0:T(8,128)S(1)}, u32[]{:S(2)}, u32[]{:S(2)}) collective-permute-start(f32[136,128]{1,0:T(8,128)S(1)} %get-tuple-element.58.refs_4_), channel_id=1, source_target_pairs={{0,16},{4,20},{8,24},{12,28},{16,0},{20,4},{24,8},{28,12},{1,17},{... | collective-permute-start | bytes 208904 | tf_op jit(solution)/shard_map/ppermute | solution.py:115
  14.7 0.5 collective-permute-done.8.refs_3_
  15.3 2.6 %collective-permute-start.9 = (f32[128,128]{1,0:T(8,128)S(1)}, f32[128,128]{1,0:T(8,128)S(1)}, u32[]{:S(2)}, u32[]{:S(2)}) collective-permute-start(f32[128,128]{1,0:T(8,128)S(1)} %shard_map.114.refs_4_), channel_id=1, source_target_pairs={{0,16},{4,20},{8,24},{12,28},{16,0},{20,4},{24,8},{28,12},{1,17},{... | collective-permute-start | bytes 196616 | tf_op jit(solution)/shard_map/ppermute | solution.py:115
  17.8 1.5 %collective-permute-done.3.refs_5_ = f32[136,128]{1,0:T(8,128)S(1)} collective-permute-done((f32[136,128]{1,0:T(8,128)S(1)}, f32[136,128]{1,0:T(8,128)S(1)}, u32[]{:S(2)}, u32[]{:S(2)}) %collective-permute-start.3) | collective-permute-done | bytes 69664 | tf_op jit(solution)/shard_map/ppermute | solution.py:115
  19.5 1.1 %collective-permute-start.4 = (f32[128,128]{1,0:T(8,128)S(1)}, f32[128,128]{1,0:T(8,128)S(1)}, u32[]{:S(2)}, u32[]{:S(2)}) collective-permute-start(f32[128,128]{1,0:T(8,128)S(1)} %get-tuple-element.61), channel_id=1, source_target_pairs={{0,4},{4,0},{8,12},{12,8},{16,20},{20,16},{24,28},{28,24},{1,5},{5... | collective-permute-start | bytes 196616 | tf_op jit(solution)/shard_map/ppermute | solution.py:101
  20.6 0.4 collective-permute-start.5
  21.1 2.1 %collective-permute-start.12 = (f32[256,128]{1,0:T(8,128)S(1)}, f32[256,128]{1,0:T(8,128)S(1)}, u32[]{:S(2)}, u32[]{:S(2)}) collective-permute-start(f32[256,128]{1,0:T(8,128)S(1)} %get-tuple-element.72), channel_id=1, source_target_pairs={{0,12},{4,8},{8,4},{12,0},{16,28},{20,24},{24,20},{28,16},{1,13},{... | collective-permute-start | bytes 393224 | tf_op jit(solution)/shard_map/ppermute | solution.py:101
  23.2 1.1 %collective-permute-start.10 = (f32[128,128]{1,0:T(8,128)S(1)}, f32[128,128]{1,0:T(8,128)S(1)}, u32[]{:S(2)}, u32[]{:S(2)}) collective-permute-start(f32[128,128]{1,0:T(8,128)S(1)} %get-tuple-element.70), channel_id=1, source_target_pairs={{0,4},{4,0},{8,12},{12,8},{16,20},{20,16},{24,28},{28,24},{1,5},{5... | collective-permute-start | bytes 196616 | tf_op jit(solution)/shard_map/ppermute | solution.py:101
  24.3 0.4 collective-permute-start.11
  24.6 0.6 collective-permute-done.4.refs_0_.refs_1_
  25.2 0.4 collective-permute-done.5.refs_1_.refs_2_
  25.7 1.2 %shard_map.116 = (bf16[8,256,256]{2,1,0:T(8,128)(2,1)S(1)}, f32[256,1024]{1,0:T(8,128)S(1)}, f32[256,1024]{1,0:T(8,128)S(1)}, bf16[8,128,256]{2,1,0:T(8,128)(2,1)S(1)}) custom-call(bf16[256,1024]{1,0:T(8,128)(2,1)S(1)} %copy-done.2, bf16[256,1024]{1,0:T(8,128)(2,1)S(1)} %copy-done, bf16[256,1024]{1,0:T(8,128)(2,1)S(1)} %copy-done.1, ...), custom_call_target="tpu_custom_call" | custom-call | flops 1000000000 | tf_op jit(solution)/shard_map/pallas_call | solution.py:25
  26.9 1.2 %collective-permute-done.10.refs_4_ = f32[128,128]{1,0:T(8,128)S(1)} collective-permute-done((f32[128,128]{1,0:T(8,128)S(1)}, f32[128,128]{1,0:T(8,128)S(1)}, u32[]{:S(2)}, u32[]{:S(2)}) %collective-permute-start.10) | collective-permute-done | bytes 65568 | tf_op jit(solution)/shard_map/ppermute | solution.py:101
  28.1 0.4 collective-permute-done.11.refs_5_
  28.5 0.7 %shard_map.117 = (f32[256,1024]{1,0:T(8,128)S(1)}, f32[8,256]{1,0:T(8,128)S(1)}, bf16[1024,128]{1,0:T(8,128)(2,1)S(1)}) custom-call(f32[128,128]{1,0:T(8,128)S(1)} %get-tuple-element.60.refs_0_, f32[128,128]{1,0:T(8,128)S(1)} %collective-permute-done.4.refs_0_.refs_1_, f32[128,128]{1,0:T(8,128)S(1)} %collective-permute-done.5.refs_1_.refs_2_, ...), custom_call_target="tpu_custom_call" | custom-call | tf_op jit(solution)/shard_map/pallas_call | solution.py:25
  29.2 1.6 %collective-permute-start.14 = (f32[8,256]{1,0:T(8,128)S(1)}, f32[8,256]{1,0:T(8,128)S(1)}, u32[]{:S(2)}, u32[]{:S(2)}) collective-permute-start(f32[8,256]{1,0:T(8,128)S(1)} %get-tuple-element.77.refs_0_), channel_id=1, source_target_pairs={{0,2},{1,3},{2,0},{3,1},{4,6},{5,7},{6,4},{7,5},{8,10},{9,11},{10,... | collective-permute-start | bytes 24584 | tf_op jit(solution)/shard_map/ppermute | solution.py:562
  30.8 0.2 collective-permute-start.13
  31.0 1.9 %collective-permute-done.14.refs_2_ = f32[8,256]{1,0:T(8,128)S(1)} collective-permute-done((f32[8,256]{1,0:T(8,128)S(1)}, f32[8,256]{1,0:T(8,128)S(1)}, u32[]{:S(2)}, u32[]{:S(2)}) %collective-permute-start.14) | collective-permute-done | bytes 8224 | tf_op jit(solution)/shard_map/ppermute | solution.py:562
  32.9 1.0 %collective-permute-done.13.refs_1_ = f32[8,256]{1,0:T(8,128)S(1)} collective-permute-done((f32[8,256]{1,0:T(8,128)S(1)}, f32[8,256]{1,0:T(8,128)S(1)}, u32[]{:S(2)}, u32[]{:S(2)}) %collective-permute-start.13) | collective-permute-done | bytes 8224 | tf_op jit(solution)/shard_map/ppermute | solution.py:562
  33.9 0.7 %shard_map.118 = (bf16[256,1024]{1,0:T(8,128)(2,1)S(1)}, f32[1024,128]{1,0:T(8,128)S(1)}, f32[256,128]{1,0:T(8,128)S(1)}, f32[256,128]{1,0:T(8,128)S(1)}, f32[25...) custom-call(f32[8,256]{1,0:T(8,128)S(1)} %get-tuple-element.77.refs_0_, f32[8,256]{1,0:T(8,128)S(1)} %collective-permute-done.13.refs_1_, ...), custom_call_target="tpu_custom_call" | custom-call | tf_op jit(solution)/shard_map/pallas_call | solution.py:25
  34.6 1.5 %collective-permute-start.16 = (f32[256,128]{1,0:T(8,128)S(1)}, f32[256,128]{1,0:T(8,128)S(1)}, u32[]{:S(2)}, u32[]{:S(2)}) collective-permute-start(f32[256,128]{1,0:T(8,128)S(1)} %get-tuple-element.85), channel_id=1, source_target_pairs={{0,12},{4,8},{8,4},{12,0},{16,28},{20,24},{24,20},{28,16},{1,13},{... | collective-permute-start | bytes 393224 | tf_op jit(solution)/shard_map/ppermute | solution.py:101
  36.0 0.9 %collective-permute-start.17 = (f32[256,128]{1,0:T(8,128)S(1)}, f32[256,128]{1,0:T(8,128)S(1)}, u32[]{:S(2)}, u32[]{:S(2)}) collective-permute-start(f32[256,128]{1,0:T(8,128)S(1)} %get-tuple-element.86), channel_id=1, source_target_pairs={{0,4},{4,0},{8,12},{12,8},{16,20},{20,16},{24,28},{28,24},{1,5},{5... | collective-permute-start | bytes 393224 | tf_op jit(solution)/shard_map/ppermute | solution.py:101
  36.9 1.2 %collective-permute-start.18 = (f32[256,128]{1,0:T(8,128)S(1)}, f32[256,128]{1,0:T(8,128)S(1)}, u32[]{:S(2)}, u32[]{:S(2)}) collective-permute-start(f32[256,128]{1,0:T(8,128)S(1)} %get-tuple-element.87), channel_id=1, source_target_pairs={{0,8},{4,12},{8,0},{12,4},{16,24},{20,28},{24,16},{28,20},{1,9},{5... | collective-permute-start | bytes 393224 | tf_op jit(solution)/shard_map/ppermute | solution.py:101
  38.1 3.4 %shard_map.119 = (bf16[256,1024]{1,0:T(8,128)(2,1)}, f32[256,1024]{1,0:T(8,128)S(1)}, f32[256,1024]{1,0:T(8,128)S(1)}) custom-call(bf16[256,1024]{1,0:T(8,128)(2,1)S(1)} %get-tuple-element.80.attn_grad_ref, bf16[256,1024]{1,0:T(8,128)(2,1)S(1)} %copy-done.2, bf16[256,1024]{1,0:T(8,128)(2,1)S(1)} %copy-done, bf16[256,1024]{1,0:T(8,128)(2,1)S(1)} %copy-done.1, ...), custom_call_target="tpu_custom_call" | custom-call | flops 671088640 | tf_op jit(solution)/shard_map/pallas_call | solution.py:25
  41.6 0.6 %collective-permute-done.17.refs_2_ = f32[256,128]{1,0:T(8,128)S(1)} collective-permute-done((f32[256,128]{1,0:T(8,128)S(1)}, f32[256,128]{1,0:T(8,128)S(1)}, u32[]{:S(2)}, u32[]{:S(2)}) %collective-permute-start.17) | collective-permute-done | bytes 131104 | tf_op jit(solution)/shard_map/ppermute | solution.py:101
  42.2 0.2 shard_map.120
  42.4 2.7 %collective-permute-start.22 = (f32[256,128]{1,0:T(8,128)S(1)}, f32[256,128]{1,0:T(8,128)S(1)}, u32[]{:S(2)}, u32[]{:S(2)}) collective-permute-start(f32[256,128]{1,0:T(8,128)S(1)} %get-tuple-element.93.refs_4_), channel_id=1, source_target_pairs={{0,16},{4,20},{8,24},{12,28},{16,0},{20,4},{24,8},{28,12},{1,17},{... | collective-permute-start | bytes 393224 | tf_op jit(solution)/shard_map/ppermute | solution.py:115
  45.2 1.8 %collective-permute-start.19 = (f32[256,128]{1,0:T(8,128)S(1)}, f32[256,128]{1,0:T(8,128)S(1)}, u32[]{:S(2)}, u32[]{:S(2)}) collective-permute-start(f32[256,128]{1,0:T(8,128)S(1)} %get-tuple-element.90), channel_id=1, source_target_pairs={{0,4},{4,0},{8,12},{12,8},{16,20},{20,16},{24,28},{28,24},{1,5},{5... | collective-permute-start | bytes 393224 | tf_op jit(solution)/shard_map/ppermute | solution.py:101
  47.0 0.2 collective-permute-start.20
  47.2 1.4 %collective-permute-start.21 = (f32[256,128]{1,0:T(8,128)S(1)}, f32[256,128]{1,0:T(8,128)S(1)}, u32[]{:S(2)}, u32[]{:S(2)}) collective-permute-start(f32[256,128]{1,0:T(8,128)S(1)} %get-tuple-element.92), channel_id=1, source_target_pairs={{0,12},{4,8},{8,4},{12,0},{16,28},{20,24},{24,20},{28,16},{1,13},{... | collective-permute-start | bytes 393224 | tf_op jit(solution)/shard_map/ppermute | solution.py:101
  48.7 0.8 %collective-permute-done.22.refs_5_ = f32[256,128]{1,0:T(8,128)S(1)} collective-permute-done((f32[256,128]{1,0:T(8,128)S(1)}, f32[256,128]{1,0:T(8,128)S(1)}, u32[]{:S(2)}, u32[]{:S(2)}) %collective-permute-start.22) | collective-permute-done | bytes 131104 | tf_op jit(solution)/shard_map/ppermute | solution.py:115
  49.5 0.2 shard_map.121
  49.7 1.9 %collective-permute-start.23 = (f32[256,128]{1,0:T(8,128)S(1)}, f32[256,128]{1,0:T(8,128)S(1)}, u32[]{:S(2)}, u32[]{:S(2)}) collective-permute-start(f32[256,128]{1,0:T(8,128)S(1)} %get-tuple-element.95), channel_id=1, source_target_pairs={{0,12},{4,8},{8,4},{12,0},{16,28},{20,24},{24,20},{28,16},{1,13},{... | collective-permute-start | bytes 393224 | tf_op jit(solution)/shard_map/ppermute | solution.py:101
  51.6 0.9 %collective-permute-start.24 = (f32[256,128]{1,0:T(8,128)S(1)}, f32[256,128]{1,0:T(8,128)S(1)}, u32[]{:S(2)}, u32[]{:S(2)}) collective-permute-start(f32[256,128]{1,0:T(8,128)S(1)} %get-tuple-element.96), channel_id=1, source_target_pairs={{0,4},{4,0},{8,12},{12,8},{16,20},{20,16},{24,28},{28,24},{1,5},{5... | collective-permute-start | bytes 393224 | tf_op jit(solution)/shard_map/ppermute | solution.py:101
  52.4 1.7 %collective-permute-done.19.refs_1_ = f32[256,128]{1,0:T(8,128)S(1)} collective-permute-done((f32[256,128]{1,0:T(8,128)S(1)}, f32[256,128]{1,0:T(8,128)S(1)}, u32[]{:S(2)}, u32[]{:S(2)}) %collective-permute-start.19) | collective-permute-done | bytes 131104 | tf_op jit(solution)/shard_map/ppermute | solution.py:101
  54.1 2.1 %collective-permute-done.21.refs_3_ = f32[256,128]{1,0:T(8,128)S(1)} collective-permute-done((f32[256,128]{1,0:T(8,128)S(1)}, f32[256,128]{1,0:T(8,128)S(1)}, u32[]{:S(2)}, u32[]{:S(2)}) %collective-permute-start.21) | collective-permute-done | bytes 131104 | tf_op jit(solution)/shard_map/ppermute | solution.py:101
  56.2 2.1 %collective-permute-done.23.refs_5_ = f32[256,128]{1,0:T(8,128)S(1)} collective-permute-done((f32[256,128]{1,0:T(8,128)S(1)}, f32[256,128]{1,0:T(8,128)S(1)}, u32[]{:S(2)}, u32[]{:S(2)}) %collective-permute-start.23) | collective-permute-done | bytes 131104 | tf_op jit(solution)/shard_map/ppermute | solution.py:101
  58.4 0.2 collective-permute-done.24.refs_6_
  58.6 0.6 collective-permute-done.25.refs_7_
  59.1 1.7 %shard_map.122 = (bf16[256,1024]{1,0:T(8,128)(2,1)}, bf16[256,1024]{1,0:T(8,128)(2,1)}, f32[1024,128]{1,0:T(8,128)}) custom-call(f32[256,128]{1,0:T(8,128)S(1)} %get-tuple-element.89.refs_0_, f32[256,128]{1,0:T(8,128)S(1)} %collective-permute-done.19.refs_1_, f32[256,128]{1,0:T(8,128)S(1)} %collective-permute-done.20.refs_2_, ...), custom_call_target="tpu_custom_call" | custom-call | tf_op jit(solution)/shard_map/pallas_call | solution.py:25
  (30 shorter events, 0.3 us)
Async XLA Ops:
  2.8 8.0 %collective-permute-start = (f32[136,128]{1,0:T(8,128)S(1)}, f32[136,128]{1,0:T(8,128)S(1)}, u32[]{:S(2)}, u32[]{:S(2)}) collective-permute-start(f32[136,128]{1,0:T(8,128)S(1)} %get-tuple-element.55), channel_id=1, source_target_pairs={{0,12},{4,8},{8,4},{12,0},{16,28},{20,24},{24,20},{28,16},{1,13},{... | collective-permute-start | bytes 208904 | tf_op jit(solution)/shard_map/ppermute | solution.py:101
  6.9 5.1 %collective-permute-start.1 = (f32[136,128]{1,0:T(8,128)S(1)}, f32[136,128]{1,0:T(8,128)S(1)}, u32[]{:S(2)}, u32[]{:S(2)}) collective-permute-start(f32[136,128]{1,0:T(8,128)S(1)} %get-tuple-element.56), channel_id=1, source_target_pairs={{0,4},{4,0},{8,12},{12,8},{16,20},{20,16},{24,28},{28,24},{1,5},{5... | collective-permute-start | bytes 208904 | tf_op jit(solution)/shard_map/ppermute | solution.py:101
  7.4 4.6 %collective-permute-start.2 = (f32[136,128]{1,0:T(8,128)S(1)}, f32[136,128]{1,0:T(8,128)S(1)}, u32[]{:S(2)}, u32[]{:S(2)}) collective-permute-start(f32[136,128]{1,0:T(8,128)S(1)} %get-tuple-element.57), channel_id=1, source_target_pairs={{0,8},{4,12},{8,0},{12,4},{16,24},{20,28},{24,16},{28,20},{1,9},{5... | collective-permute-start | bytes 208904 | tf_op jit(solution)/shard_map/ppermute | solution.py:101
  7.5 7.2 %collective-permute-start.6 = (f32[128,128]{1,0:T(8,128)S(1)}, f32[128,128]{1,0:T(8,128)S(1)}, u32[]{:S(2)}, u32[]{:S(2)}) collective-permute-start(f32[128,128]{1,0:T(8,128)S(1)} %get-tuple-element.64), channel_id=1, source_target_pairs={{0,12},{4,8},{8,4},{12,0},{16,28},{20,24},{24,20},{28,16},{1,13},{... | collective-permute-start | bytes 196616 | tf_op jit(solution)/shard_map/ppermute | solution.py:101
  10.3 4.3 %collective-permute-start.7 = (f32[128,128]{1,0:T(8,128)S(1)}, f32[128,128]{1,0:T(8,128)S(1)}, u32[]{:S(2)}, u32[]{:S(2)}) collective-permute-start(f32[128,128]{1,0:T(8,128)S(1)} %get-tuple-element.65), channel_id=1, source_target_pairs={{0,4},{4,0},{8,12},{12,8},{16,20},{20,16},{24,28},{28,24},{1,5},{5... | collective-permute-start | bytes 196616 | tf_op jit(solution)/shard_map/ppermute | solution.py:101
  10.9 4.3 %collective-permute-start.8 = (f32[128,128]{1,0:T(8,128)S(1)}, f32[128,128]{1,0:T(8,128)S(1)}, u32[]{:S(2)}, u32[]{:S(2)}) collective-permute-start(f32[128,128]{1,0:T(8,128)S(1)} %get-tuple-element.66), channel_id=1, source_target_pairs={{0,8},{4,12},{8,0},{12,4},{16,24},{20,28},{24,16},{28,20},{1,9},{5... | collective-permute-start | bytes 196616 | tf_op jit(solution)/shard_map/ppermute | solution.py:101
  12.0 7.3 %collective-permute-start.3 = (f32[136,128]{1,0:T(8,128)S(1)}, f32[136,128]{1,0:T(8,128)S(1)}, u32[]{:S(2)}, u32[]{:S(2)}) collective-permute-start(f32[136,128]{1,0:T(8,128)S(1)} %get-tuple-element.58.refs_4_), channel_id=1, source_target_pairs={{0,16},{4,20},{8,24},{12,28},{16,0},{20,4},{24,8},{28,12},{1,17},{... | collective-permute-start | bytes 208904 | tf_op jit(solution)/shard_map/ppermute | solution.py:115
  15.2 4.2 %copy-start.3 = (f32[8,128,128]{2,1,0:T(8,128)S(1)}, f32[8,128,128]{2,1,0:T(8,128)}, u32[]{:S(2)}) copy-start(f32[8,128,128]{2,1,0:T(8,128)} %param.14) | copy-start | bytes 1572868
  15.2 10.4 %copy-start.5 = (bf16[256,1024]{1,0:T(8,128)(2,1)S(1)}, bf16[256,1024]{1,0:T(8,128)(2,1)}, u32[]{:S(2)}) copy-start(bf16[256,1024]{1,0:T(8,128)(2,1)} %upstream_ref.1) | copy-start | bytes 1572868
  15.3 5.7 %collective-permute-start.9 = (f32[128,128]{1,0:T(8,128)S(1)}, f32[128,128]{1,0:T(8,128)S(1)}, u32[]{:S(2)}, u32[]{:S(2)}) collective-permute-start(f32[128,128]{1,0:T(8,128)S(1)} %shard_map.114.refs_4_), channel_id=1, source_target_pairs={{0,16},{4,20},{8,24},{12,28},{16,0},{20,4},{24,8},{28,12},{1,17},{... | collective-permute-start | bytes 196616 | tf_op jit(solution)/shard_map/ppermute | solution.py:115
  19.4 6.3 %copy-start.1 = (bf16[256,1024]{1,0:T(8,128)(2,1)S(1)}, bf16[256,1024]{1,0:T(8,128)(2,1)}, u32[]{:S(2)}) copy-start(bf16[256,1024]{1,0:T(8,128)(2,1)} %refs_11_.1) | copy-start | bytes 1572868
  19.4 6.3 %copy-start.2 = (bf16[256,1024]{1,0:T(8,128)(2,1)S(1)}, bf16[256,1024]{1,0:T(8,128)(2,1)}, u32[]{:S(2)}) copy-start(bf16[256,1024]{1,0:T(8,128)(2,1)} %query_ref.3) | copy-start | bytes 1572868
  19.5 6.2 %copy-start = (bf16[256,1024]{1,0:T(8,128)(2,1)S(1)}, bf16[256,1024]{1,0:T(8,128)(2,1)}, u32[]{:S(2)}) copy-start(bf16[256,1024]{1,0:T(8,128)(2,1)} %refs_10_.1) | copy-start | bytes 1572868
  19.5 5.7 %collective-permute-start.4 = (f32[128,128]{1,0:T(8,128)S(1)}, f32[128,128]{1,0:T(8,128)S(1)}, u32[]{:S(2)}, u32[]{:S(2)}) collective-permute-start(f32[128,128]{1,0:T(8,128)S(1)} %get-tuple-element.61), channel_id=1, source_target_pairs={{0,4},{4,0},{8,12},{12,8},{16,20},{20,16},{24,28},{28,24},{1,5},{5... | collective-permute-start | bytes 196616 | tf_op jit(solution)/shard_map/ppermute | solution.py:101
  20.6 5.0 %collective-permute-start.5 = (f32[128,128]{1,0:T(8,128)S(1)}, f32[128,128]{1,0:T(8,128)S(1)}, u32[]{:S(2)}, u32[]{:S(2)}) collective-permute-start(f32[128,128]{1,0:T(8,128)S(1)} %get-tuple-element.62), channel_id=1, source_target_pairs={{0,8},{4,12},{8,0},{12,4},{16,24},{20,28},{24,16},{28,20},{1,9},{5... | collective-permute-start | bytes 196616 | tf_op jit(solution)/shard_map/ppermute | solution.py:101
  21.1 7.5 %collective-permute-start.12 = (f32[256,128]{1,0:T(8,128)S(1)}, f32[256,128]{1,0:T(8,128)S(1)}, u32[]{:S(2)}, u32[]{:S(2)}) collective-permute-start(f32[256,128]{1,0:T(8,128)S(1)} %get-tuple-element.72), channel_id=1, source_target_pairs={{0,12},{4,8},{8,4},{12,0},{16,28},{20,24},{24,20},{28,16},{1,13},{... | collective-permute-start | bytes 393224 | tf_op jit(solution)/shard_map/ppermute | solution.py:101
  23.2 2.5 %copy-start.6 = (f32[1024]{0:T(1024)S(1)}, f32[1024]{0:T(1024)}, u32[]{:S(2)}) copy-start(f32[1024]{0:T(1024)} %param.13) | copy-start | bytes 12292
  23.2 4.9 %collective-permute-start.10 = (f32[128,128]{1,0:T(8,128)S(1)}, f32[128,128]{1,0:T(8,128)S(1)}, u32[]{:S(2)}, u32[]{:S(2)}) collective-permute-start(f32[128,128]{1,0:T(8,128)S(1)} %get-tuple-element.70), channel_id=1, source_target_pairs={{0,4},{4,0},{8,12},{12,8},{16,20},{20,16},{24,28},{28,24},{1,5},{5... | collective-permute-start | bytes 196616 | tf_op jit(solution)/shard_map/ppermute | solution.py:101
  24.3 4.3 %collective-permute-start.11 = (f32[128,128]{1,0:T(8,128)S(1)}, f32[128,128]{1,0:T(8,128)S(1)}, u32[]{:S(2)}, u32[]{:S(2)}) collective-permute-start(f32[128,128]{1,0:T(8,128)S(1)} %get-tuple-element.71), channel_id=1, source_target_pairs={{0,8},{4,12},{8,0},{12,4},{16,24},{20,28},{24,16},{28,20},{1,9},{5... | collective-permute-start | bytes 196616 | tf_op jit(solution)/shard_map/ppermute | solution.py:101
  29.2 1.8 %collective-permute-start.15 = (f32[8,256]{1,0:T(8,128)S(1)}, f32[8,256]{1,0:T(8,128)S(1)}, u32[]{:S(2)}, u32[]{:S(2)}) collective-permute-start(f32[8,256]{1,0:T(8,128)S(1)} %get-tuple-element.77.refs_0_), channel_id=1, source_target_pairs={{0,3},{1,0},{2,1},{3,2},{4,7},{5,4},{6,5},{7,6},{8,11},{9,8},{10,9... | collective-permute-start | bytes 24584 | tf_op jit(solution)/shard_map/ppermute | solution.py:562
  29.2 3.7 %collective-permute-start.14 = (f32[8,256]{1,0:T(8,128)S(1)}, f32[8,256]{1,0:T(8,128)S(1)}, u32[]{:S(2)}, u32[]{:S(2)}) collective-permute-start(f32[8,256]{1,0:T(8,128)S(1)} %get-tuple-element.77.refs_0_), channel_id=1, source_target_pairs={{0,2},{1,3},{2,0},{3,1},{4,6},{5,7},{6,4},{7,5},{8,10},{9,11},{10,... | collective-permute-start | bytes 24584 | tf_op jit(solution)/shard_map/ppermute | solution.py:562
  30.8 3.1 %collective-permute-start.13 = (f32[8,256]{1,0:T(8,128)S(1)}, f32[8,256]{1,0:T(8,128)S(1)}, u32[]{:S(2)}, u32[]{:S(2)}) collective-permute-start(f32[8,256]{1,0:T(8,128)S(1)} %get-tuple-element.77.refs_0_), channel_id=1, source_target_pairs={{0,1},{1,2},{2,3},{3,0},{4,5},{5,6},{6,7},{7,4},{8,9},{9,10},{10,1... | collective-permute-start | bytes 24584 | tf_op jit(solution)/shard_map/ppermute | solution.py:562
  34.6 7.0 %collective-permute-start.16 = (f32[256,128]{1,0:T(8,128)S(1)}, f32[256,128]{1,0:T(8,128)S(1)}, u32[]{:S(2)}, u32[]{:S(2)}) collective-permute-start(f32[256,128]{1,0:T(8,128)S(1)} %get-tuple-element.85), channel_id=1, source_target_pairs={{0,12},{4,8},{8,4},{12,0},{16,28},{20,24},{24,20},{28,16},{1,13},{... | collective-permute-start | bytes 393224 | tf_op jit(solution)/shard_map/ppermute | solution.py:101
  36.0 6.2 %collective-permute-start.17 = (f32[256,128]{1,0:T(8,128)S(1)}, f32[256,128]{1,0:T(8,128)S(1)}, u32[]{:S(2)}, u32[]{:S(2)}) collective-permute-start(f32[256,128]{1,0:T(8,128)S(1)} %get-tuple-element.86), channel_id=1, source_target_pairs={{0,4},{4,0},{8,12},{12,8},{16,20},{20,16},{24,28},{28,24},{1,5},{5... | collective-permute-start | bytes 393224 | tf_op jit(solution)/shard_map/ppermute | solution.py:101
  36.9 5.3 %collective-permute-start.18 = (f32[256,128]{1,0:T(8,128)S(1)}, f32[256,128]{1,0:T(8,128)S(1)}, u32[]{:S(2)}, u32[]{:S(2)}) collective-permute-start(f32[256,128]{1,0:T(8,128)S(1)} %get-tuple-element.87), channel_id=1, source_target_pairs={{0,8},{4,12},{8,0},{12,4},{16,24},{20,28},{24,16},{28,20},{1,9},{5... | collective-permute-start | bytes 393224 | tf_op jit(solution)/shard_map/ppermute | solution.py:101
  38.1 4.1 %copy-start.4 = (f32[8,128,128]{2,1,0:T(8,128)S(1)}, f32[8,128,128]{2,1,0:T(8,128)}, u32[]{:S(2)}) copy-start(f32[8,128,128]{2,1,0:T(8,128)} %param.15) | copy-start | bytes 1572868
  42.4 7.0 %collective-permute-start.22 = (f32[256,128]{1,0:T(8,128)S(1)}, f32[256,128]{1,0:T(8,128)S(1)}, u32[]{:S(2)}, u32[]{:S(2)}) collective-permute-start(f32[256,128]{1,0:T(8,128)S(1)} %get-tuple-element.93.refs_4_), channel_id=1, source_target_pairs={{0,16},{4,20},{8,24},{12,28},{16,0},{20,4},{24,8},{28,12},{1,17},{... | collective-permute-start | bytes 393224 | tf_op jit(solution)/shard_map/ppermute | solution.py:115
  45.2 8.9 %collective-permute-start.19 = (f32[256,128]{1,0:T(8,128)S(1)}, f32[256,128]{1,0:T(8,128)S(1)}, u32[]{:S(2)}, u32[]{:S(2)}) collective-permute-start(f32[256,128]{1,0:T(8,128)S(1)} %get-tuple-element.90), channel_id=1, source_target_pairs={{0,4},{4,0},{8,12},{12,8},{16,20},{20,16},{24,28},{28,24},{1,5},{5... | collective-permute-start | bytes 393224 | tf_op jit(solution)/shard_map/ppermute | solution.py:101
  47.0 7.1 %collective-permute-start.20 = (f32[256,128]{1,0:T(8,128)S(1)}, f32[256,128]{1,0:T(8,128)S(1)}, u32[]{:S(2)}, u32[]{:S(2)}) collective-permute-start(f32[256,128]{1,0:T(8,128)S(1)} %get-tuple-element.91), channel_id=1, source_target_pairs={{0,8},{4,12},{8,0},{12,4},{16,24},{20,28},{24,16},{28,20},{1,9},{5... | collective-permute-start | bytes 393224 | tf_op jit(solution)/shard_map/ppermute | solution.py:101
  47.2 9.0 %collective-permute-start.21 = (f32[256,128]{1,0:T(8,128)S(1)}, f32[256,128]{1,0:T(8,128)S(1)}, u32[]{:S(2)}, u32[]{:S(2)}) collective-permute-start(f32[256,128]{1,0:T(8,128)S(1)} %get-tuple-element.92), channel_id=1, source_target_pairs={{0,12},{4,8},{8,4},{12,0},{16,28},{20,24},{24,20},{28,16},{1,13},{... | collective-permute-start | bytes 393224 | tf_op jit(solution)/shard_map/ppermute | solution.py:101
  49.7 8.7 %collective-permute-start.23 = (f32[256,128]{1,0:T(8,128)S(1)}, f32[256,128]{1,0:T(8,128)S(1)}, u32[]{:S(2)}, u32[]{:S(2)}) collective-permute-start(f32[256,128]{1,0:T(8,128)S(1)} %get-tuple-element.95), channel_id=1, source_target_pairs={{0,12},{4,8},{8,4},{12,0},{16,28},{20,24},{24,20},{28,16},{1,13},{... | collective-permute-start | bytes 393224 | tf_op jit(solution)/shard_map/ppermute | solution.py:101
  51.6 7.0 %collective-permute-start.24 = (f32[256,128]{1,0:T(8,128)S(1)}, f32[256,128]{1,0:T(8,128)S(1)}, u32[]{:S(2)}, u32[]{:S(2)}) collective-permute-start(f32[256,128]{1,0:T(8,128)S(1)} %get-tuple-element.96), channel_id=1, source_target_pairs={{0,4},{4,0},{8,12},{12,8},{16,20},{20,16},{24,28},{28,24},{1,5},{5... | collective-permute-start | bytes 393224 | tf_op jit(solution)/shard_map/ppermute | solution.py:101
  54.1 5.0 %collective-permute-start.25 = (f32[256,128]{1,0:T(8,128)S(1)}, f32[256,128]{1,0:T(8,128)S(1)}, u32[]{:S(2)}, u32[]{:S(2)}) collective-permute-start(f32[256,128]{1,0:T(8,128)S(1)} %get-tuple-element.97), channel_id=1, source_target_pairs={{0,8},{4,12},{8,0},{12,4},{16,24},{20,28},{24,16},{28,20},{1,9},{5... | collective-permute-start | bytes 393224 | tf_op jit(solution)/shard_map/ppermute | solution.py:101

commit v10 on v9

--- a/solution.py
+++ b/solution.py
@@ -75,6 +75,7 @@
         self.near = [way for way in range(self.members) if way.bit_count() == 1]
         self.far = [way for way in range(self.members) if way.bit_count() > 1]
         self.ways = [0] + self.far + self.near
+        self.early_ways = [0] + self.near[::-1] + self.far
 
     def member(self):
         return lax.rem(lax.axis_index("seq"), self.members)
@@ -250,28 +251,35 @@
     return found
 
 
+def early_body(plan, *refs):
+    part_refs, refs = refs[: plan.members], refs[plan.members :]
+    (logs_ref, grad_ref), send_refs, held_ref = refs[:2], refs[3:-1], refs[-1]
+    for k, part_ref in enumerate(part_refs):
+        held_ref[plan.peer(k)] = part_ref[...]
+    first = plan.group() == 0
+    zero = jnp.zeros((plan.rows, plan.size), F32)
+    before = prefixes(plan, held_ref, logs_ref, zero, zero + 1.0)
+    after = suffixes(plan, held_ref, logs_ref, grad_ref[plan.rows_of(plan.member())])[0]
+    for b in range(plan.members):
+        held_ref[b] = jnp.where(first, before[b], after[b])
+    for way, send_ref in zip(plan.early_ways, send_refs):
+        send_ref[: plan.rows] = held_ref[plan.toward(way)]
+        if send_ref.shape[0] > plan.rows:
+            send_ref[plan.rows :] = logs_ref[0]
+
+
 def group_grad_body(plan, *refs):
-    part_refs, refs = refs[: plan.members], refs[plan.members :]
-    (logs_ref, grad_ref, _, total_ref), refs = refs[:4], refs[4:]
-    send_refs, (held_ref,) = refs[:-1], refs[-1:]
+    part_refs, (logs_ref, _, total_ref, held_ref) = refs[: plan.members], refs[plan.members :]
     for k, part_ref in enumerate(part_refs):
         held_ref[plan.peer(k)] = part_ref[...]
     zero = jnp.zeros((plan.rows, plan.size), F32)
     total_ref[...] = suffixes(plan, held_ref, logs_ref, zero)[1]
-    if send_refs:
-        first = plan.group() == 0
-        before = prefixes(plan, held_ref, logs_ref, zero, zero + 1.0)
-        after = suffixes(plan, held_ref, logs_ref, grad_ref[plan.rows_of(plan.member())])[0]
-        for b in range(plan.members):
-            held_ref[b] = jnp.where(first, before[b], after[b])
-        for way, send_ref in enumerate(send_refs):
-            send_ref[...] = held_ref[plan.toward(way)]
 
 
 def reverse_scan_body(plan, *refs):
     part_refs, refs = refs[: plan.members], refs[plan.members :]
     total_refs, refs = refs[: plan.groups], refs[plan.groups :]
-    (logs_ref, group_logs_ref, grad_ref), refs = refs[:3], refs[3:]
+    (logs_ref, group_logs_ref, grad_ref, _), refs = refs[:4], refs[4:]
     send_refs, (groups_ref, held_ref) = refs[:-2], refs[-2:]
     stage_groups(plan, total_refs, groups_ref)
     for k, part_ref in enumerate(part_refs):
@@ -422,14 +430,14 @@
     key_out, value_out, total_out, held_ref, key_grad_ref, value_grad_ref, total_ref, sems = refs[7:]
     length, size = key_ref.shape[0], plan.size
     swapped = jnp.where(plan.group() == 0, 0, 1) if plan.groups == 2 else 0
-    for k, way in enumerate(range(plan.members) if plan.groups == 2 else plan.ways):
-        held_ref[swapped, plan.rows_of(plan.toward(way))] = first_refs[k][...]
+    for k, way in enumerate(plan.early_ways if plan.groups == 2 else plan.ways):
+        held_ref[swapped, plan.rows_of(plan.toward(way))] = first_refs[k][: plan.rows]
         held_ref[1 - swapped, plan.rows_of(plan.peer(k))] = second_refs[k][...]
     cum_col = cum_col_ref[...]
     block_log = cum_col[length - 1 : length, :]
     shrink = jnp.exp(block_log - cum_col)
     copies = []
-    half = max(plan.heads // 2, 1)
+    batch = max(plan.heads // 4, 1)
     for h in range(plan.heads):
         cut = lanes(h, size)
         grads = held_ref[1, cut]
@@ -442,8 +450,8 @@
         key_grad_ref[:, cut] = (key_part_ref[:, cut] + column * key_state).astype(BF16)
         value_state = dot(key_ref[:, cut], grads)
         value_grad_ref[:, cut] = (value_part_ref[:, cut] + column * value_state).astype(BF16)
-        if (h + 1) % half == 0:
-            done = slice((h + 1 - half) * size, (h + 1) * size)
+        if (h + 1) % batch == 0:
+            done = slice((h + 1 - batch) * size, (h + 1) * size)
             for source, target, index in [
                 (total_ref, total_out, (done,)),
                 (key_grad_ref, key_out, (slice(None), done)),
@@ -576,20 +584,31 @@
     )
     grad_rows = state_out_grad.reshape(width, size)
     two_sided = plan.groups == 2
-    total, *sends = call(
+    tie, swapped = key_part, []
+    if two_sided:
+        sends = call(
+            bind(early_body),
+            [piece, shaped((plan.rows + LOG_ROWS, size))] + pieces[2:],
+            [*parts, logs, grad_rows, key_part],
+            [hold],
+            specs=[VMEM] * (plan.members + 2) + [ANY],
+        )
+        tie = sends[0]
+        swapped = [plan.swap_in_group(sends, plan.early_ways)]
+    (total,) = call(
         bind(group_grad_body),
-        [piece] + pieces * two_sided,
-        [*parts, logs, grad_rows, key_part],
+        [piece],
+        [*parts, logs, tie],
         [hold],
-        specs=[VMEM] * (plan.members + 2) + [ANY],
+        specs=[VMEM] * (plan.members + 1) + [ANY],
     )
     totals = [total] + plan.from_groups(total)
-    swapped = [plan.swap_in_group(sends, range(plan.members))] if two_sided else []
     sends = call(
         bind(reverse_scan_body),
         pieces * (1 if two_sided else 2),
-        [*parts, *totals, logs, all_logs, grad_rows],
+        [*parts, *totals, logs, all_logs, grad_rows, swapped[0][1] if two_sided else tie],
         [hold_groups, hold],
+        specs=[VMEM] * (plan.members + plan.groups + 3) + [ANY],
     )
     for first in range(0, len(sends), plan.members):
         swapped.append(plan.swap_in_group(sends[first : first + plan.members]))
@@ -602,7 +621,7 @@
             pltpu.VMEM((length, width), BF16),
             pltpu.VMEM((length, width), BF16),
             pltpu.VMEM((width, size), F32),
-            pltpu.SemaphoreType.DMA((6,)),
+            pltpu.SemaphoreType.DMA((12,)),
         ],
         out_specs=[HBM] * 3,
     )

time: 61.8 us -> 61.2 us (level); the launches traced: 60.9 us -> 61 us
  starting transfers between devices: 33.4 us -> 35.9 us
  waiting for transfers between devices: 16 us -> 13.5 us
    ppermute x20, starting transfers between devices: 23.6 us -> 26 us  [swap(): return lax.ppermute(piece, 'seq', pairs) if way else piece]
    ppermute x20, waiting for transfers between devices: 10.8 us -> 8.46 us  [swap(): return lax.ppermute(piece, 'seq', pairs) if way else piece]
    pallas_call x12 -> x13, Pallas kernels: 10.7 us -> 10.7 us  [call(): pl.pallas_call(body, out_shape=outs, in_specs=specs or [VMEM] * len(opera...]
  transfers between devices with their start and end apart: 26 -> 26, of which waited for: 16 -> 14; matrix products, arithmetic and copies ran while one was open for 0% -> 0% of each run, Pallas kernels for 9% -> 9%
where the time goes in v10:
time: 61.2 us; the launch traced here: 61 us
  starting transfers between devices  35.9 us (59%)
  waiting for transfers between devices  13.5 us (22%)
  Pallas kernels  10.7 us (17%)
  between operations  0.75 us (1%)
    ppermute x20, starting transfers between devices, swap(): return lax.ppermute(piece, 'seq', pairs) if way else piece  26 us
    pallas_call x13, Pallas kernels, call(): pl.pallas_call(body, out_shape=outs, in_specs=specs or [VMEM] * len(opera...  10.7 us
    ppermute x20, waiting for transfers between devices, swap(): return lax.ppermute(piece, 'seq', pairs) if way else piece  8.46 us
    ppermute x3, starting transfers between devices, from_groups(): lax.ppermute(piece, 'seq', [(i, (i + step * self.members) % self.blocks)...  8.12 us
    ppermute x3, waiting for transfers between devices, on_device(): lax.ppermute(sums, 'head', [(i, (i + step) % parties) for i in range(part...  2.85 us
    ppermute x3, waiting for transfers between devices, from_groups(): lax.ppermute(piece, 'seq', [(i, (i + step * self.members) % self.blocks)...  2.21 us
    ppermute x3, starting transfers between devices, on_device(): lax.ppermute(sums, 'head', [(i, (i + step) % parties) for i in range(part...  1.81 us
  transfers between devices with their start and end apart: 26, of which 14 were waited for; matrix products, arithmetic and copies ran while one was open for 0% of the time, Pallas kernels for 9%

profile of v10, /device:TPU:0, one launch (start us, length us, event | category | flops | bytes accessed | tf_op | source)
XLA Modules:
  0.0 61.0 jit_solution(249408363204540732)
XLA Ops:
  0.6 2.2 %shard_map.111 = (f32[136,128]{1,0:T(8,128)S(1)}, f32[136,128]{1,0:T(8,128)S(1)}, f32[136,128]{1,0:T(8,128)S(1)}, f32[136,128]{1,0:T(8,128)S(1)}, f32[128,128]{1...) custom-call(bf16[256,1024]{1,0:T(8,128)(2,1)} %refs_10_.1, ...), custom_call_target="tpu_custom_call" | custom-call | tf_op jit(solution)/shard_map/pallas_call | solution.py:25
  2.8 4.0 %collective-permute-start = (f32[136,128]{1,0:T(8,128)S(1)}, f32[136,128]{1,0:T(8,128)S(1)}, u32[]{:S(2)}, u32[]{:S(2)}) collective-permute-start(f32[136,128]{1,0:T(8,128)S(1)} %get-tuple-element.54), channel_id=1, source_target_pairs={{0,12},{4,8},{8,4},{12,0},{16,28},{20,24},{24,20},{28,16},{1,13},{... | collective-permute-start | bytes 208904 | tf_op jit(solution)/shard_map/ppermute | solution.py:102
  6.9 0.5 collective-permute-start.1
  7.4 0.1 collective-permute-start.2
  7.5 2.8 %collective-permute-start.6 = (f32[128,128]{1,0:T(8,128)S(1)}, f32[128,128]{1,0:T(8,128)S(1)}, u32[]{:S(2)}, u32[]{:S(2)}) collective-permute-start(f32[128,128]{1,0:T(8,128)S(1)} %get-tuple-element.63), channel_id=1, source_target_pairs={{0,12},{4,8},{8,4},{12,0},{16,28},{20,24},{24,20},{28,16},{1,13},{... | collective-permute-start | bytes 196616 | tf_op jit(solution)/shard_map/ppermute | solution.py:102
  10.3 0.5 collective-permute-start.7
  10.9 0.8 %collective-permute-start.8 = (f32[128,128]{1,0:T(8,128)S(1)}, f32[128,128]{1,0:T(8,128)S(1)}, u32[]{:S(2)}, u32[]{:S(2)}) collective-permute-start(f32[128,128]{1,0:T(8,128)S(1)} %get-tuple-element.65), channel_id=1, source_target_pairs={{0,8},{4,12},{8,0},{12,4},{16,24},{20,28},{24,16},{28,20},{1,9},{5... | collective-permute-start | bytes 196616 | tf_op jit(solution)/shard_map/ppermute | solution.py:102
  11.6 0.4 collective-permute-done.1.refs_2_
  12.0 2.7 %collective-permute-start.3 = (f32[136,128]{1,0:T(8,128)S(1)}, f32[136,128]{1,0:T(8,128)S(1)}, u32[]{:S(2)}, u32[]{:S(2)}) collective-permute-start(f32[136,128]{1,0:T(8,128)S(1)} %get-tuple-element.57.refs_4_), channel_id=1, source_target_pairs={{0,16},{4,20},{8,24},{12,28},{16,0},{20,4},{24,8},{28,12},{1,17},{... | collective-permute-start | bytes 208904 | tf_op jit(solution)/shard_map/ppermute | solution.py:116
  14.7 0.5 collective-permute-done.8.refs_3_
  15.3 2.6 %collective-permute-start.9 = (f32[128,128]{1,0:T(8,128)S(1)}, f32[128,128]{1,0:T(8,128)S(1)}, u32[]{:S(2)}, u32[]{:S(2)}) collective-permute-start(f32[128,128]{1,0:T(8,128)S(1)} %shard_map.114.refs_4_), channel_id=1, source_target_pairs={{0,16},{4,20},{8,24},{12,28},{16,0},{20,4},{24,8},{28,12},{1,17},{... | collective-permute-start | bytes 196616 | tf_op jit(solution)/shard_map/ppermute | solution.py:116
  17.8 1.5 %collective-permute-done.3.refs_5_ = f32[136,128]{1,0:T(8,128)S(1)} collective-permute-done((f32[136,128]{1,0:T(8,128)S(1)}, f32[136,128]{1,0:T(8,128)S(1)}, u32[]{:S(2)}, u32[]{:S(2)}) %collective-permute-start.3) | collective-permute-done | bytes 69664 | tf_op jit(solution)/shard_map/ppermute | solution.py:116
  19.4 0.1 shard_map.113
  19.5 1.1 %collective-permute-start.4 = (f32[128,128]{1,0:T(8,128)S(1)}, f32[128,128]{1,0:T(8,128)S(1)}, u32[]{:S(2)}, u32[]{:S(2)}) collective-permute-start(f32[128,128]{1,0:T(8,128)S(1)} %get-tuple-element.60), channel_id=1, source_target_pairs={{0,4},{4,0},{8,12},{12,8},{16,20},{20,16},{24,28},{28,24},{1,5},{5... | collective-permute-start | bytes 196616 | tf_op jit(solution)/shard_map/ppermute | solution.py:102
  20.6 0.4 collective-permute-start.5
  21.1 2.1 %collective-permute-start.12 = (f32[256,128]{1,0:T(8,128)S(1)}, f32[256,128]{1,0:T(8,128)S(1)}, u32[]{:S(2)}, u32[]{:S(2)}) collective-permute-start(f32[256,128]{1,0:T(8,128)S(1)} %get-tuple-element.71), channel_id=1, source_target_pairs={{0,12},{4,8},{8,4},{12,0},{16,28},{20,24},{24,20},{28,16},{1,13},{... | collective-permute-start | bytes 393224 | tf_op jit(solution)/shard_map/ppermute | solution.py:102
  23.2 1.1 %collective-permute-start.10 = (f32[128,128]{1,0:T(8,128)S(1)}, f32[128,128]{1,0:T(8,128)S(1)}, u32[]{:S(2)}, u32[]{:S(2)}) collective-permute-start(f32[128,128]{1,0:T(8,128)S(1)} %get-tuple-element.69), channel_id=1, source_target_pairs={{0,4},{4,0},{8,12},{12,8},{16,20},{20,16},{24,28},{28,24},{1,5},{5... | collective-permute-start | bytes 196616 | tf_op jit(solution)/shard_map/ppermute | solution.py:102
  24.3 0.4 collective-permute-start.11
  24.6 0.6 collective-permute-done.4.refs_0_.refs_1_
  25.2 0.4 collective-permute-done.5.refs_1_.refs_2_
  25.7 1.2 %shard_map.116 = (bf16[8,256,256]{2,1,0:T(8,128)(2,1)S(1)}, f32[256,1024]{1,0:T(8,128)S(1)}, f32[256,1024]{1,0:T(8,128)S(1)}, bf16[8,128,256]{2,1,0:T(8,128)(2,1)S(1)}) custom-call(bf16[256,1024]{1,0:T(8,128)(2,1)S(1)} %copy-done.2, bf16[256,1024]{1,0:T(8,128)(2,1)S(1)} %copy-done, bf16[256,1024]{1,0:T(8,128)(2,1)S(1)} %copy-done.1, ...), custom_call_target="tpu_custom_call" | custom-call | flops 1000000000 | tf_op jit(solution)/shard_map/pallas_call | solution.py:25
  26.9 1.2 %collective-permute-done.10.refs_4_ = f32[128,128]{1,0:T(8,128)S(1)} collective-permute-done((f32[128,128]{1,0:T(8,128)S(1)}, f32[128,128]{1,0:T(8,128)S(1)}, u32[]{:S(2)}, u32[]{:S(2)}) %collective-permute-start.10) | collective-permute-done | bytes 65568 | tf_op jit(solution)/shard_map/ppermute | solution.py:102
  28.1 0.4 collective-permute-done.11.refs_5_
  28.5 0.7 %shard_map.117 = (f32[256,1024]{1,0:T(8,128)S(1)}, f32[8,256]{1,0:T(8,128)S(1)}, bf16[1024,128]{1,0:T(8,128)(2,1)S(1)}) custom-call(f32[128,128]{1,0:T(8,128)S(1)} %get-tuple-element.59.refs_0_, f32[128,128]{1,0:T(8,128)S(1)} %collective-permute-done.4.refs_0_.refs_1_, f32[128,128]{1,0:T(8,128)S(1)} %collective-permute-done.5.refs_1_.refs_2_, ...), custom_call_target="tpu_custom_call" | custom-call | tf_op jit(solution)/shard_map/pallas_call | solution.py:25
  29.2 1.6 %collective-permute-start.14 = (f32[8,256]{1,0:T(8,128)S(1)}, f32[8,256]{1,0:T(8,128)S(1)}, u32[]{:S(2)}, u32[]{:S(2)}) collective-permute-start(f32[8,256]{1,0:T(8,128)S(1)} %get-tuple-element.76.refs_0_), channel_id=1, source_target_pairs={{0,2},{1,3},{2,0},{3,1},{4,6},{5,7},{6,4},{7,5},{8,10},{9,11},{10,... | collective-permute-start | bytes 24584 | tf_op jit(solution)/shard_map/ppermute | solution.py:570
  30.8 0.2 collective-permute-start.13
  31.0 1.9 %collective-permute-done.14.refs_2_ = f32[8,256]{1,0:T(8,128)S(1)} collective-permute-done((f32[8,256]{1,0:T(8,128)S(1)}, f32[8,256]{1,0:T(8,128)S(1)}, u32[]{:S(2)}, u32[]{:S(2)}) %collective-permute-start.14) | collective-permute-done | bytes 8224 | tf_op jit(solution)/shard_map/ppermute | solution.py:570
  32.9 1.0 %collective-permute-done.13.refs_1_ = f32[8,256]{1,0:T(8,128)S(1)} collective-permute-done((f32[8,256]{1,0:T(8,128)S(1)}, f32[8,256]{1,0:T(8,128)S(1)}, u32[]{:S(2)}, u32[]{:S(2)}) %collective-permute-start.13) | collective-permute-done | bytes 8224 | tf_op jit(solution)/shard_map/ppermute | solution.py:570
  33.9 0.7 %shard_map.118 = (bf16[256,1024]{1,0:T(8,128)(2,1)S(1)}, f32[1024,128]{1,0:T(8,128)S(1)}, f32[256,128]{1,0:T(8,128)S(1)}, f32[256,128]{1,0:T(8,128)S(1)}, f32[25...) custom-call(f32[8,256]{1,0:T(8,128)S(1)} %get-tuple-element.76.refs_0_, f32[8,256]{1,0:T(8,128)S(1)} %collective-permute-done.13.refs_1_, ...), custom_call_target="tpu_custom_call" | custom-call | tf_op jit(solution)/shard_map/pallas_call | solution.py:25
  34.6 1.5 %collective-permute-start.16 = (f32[256,128]{1,0:T(8,128)S(1)}, f32[256,128]{1,0:T(8,128)S(1)}, u32[]{:S(2)}, u32[]{:S(2)}) collective-permute-start(f32[256,128]{1,0:T(8,128)S(1)} %get-tuple-element.84), channel_id=1, source_target_pairs={{0,12},{4,8},{8,4},{12,0},{16,28},{20,24},{24,20},{28,16},{1,13},{... | collective-permute-start | bytes 393224 | tf_op jit(solution)/shard_map/ppermute | solution.py:102
  36.0 0.9 %collective-permute-start.17 = (f32[256,128]{1,0:T(8,128)S(1)}, f32[256,128]{1,0:T(8,128)S(1)}, u32[]{:S(2)}, u32[]{:S(2)}) collective-permute-start(f32[256,128]{1,0:T(8,128)S(1)} %get-tuple-element.85), channel_id=1, source_target_pairs={{0,4},{4,0},{8,12},{12,8},{16,20},{20,16},{24,28},{28,24},{1,5},{5... | collective-permute-start | bytes 393224 | tf_op jit(solution)/shard_map/ppermute | solution.py:102
  37.0 1.2 %collective-permute-start.18 = (f32[256,128]{1,0:T(8,128)S(1)}, f32[256,128]{1,0:T(8,128)S(1)}, u32[]{:S(2)}, u32[]{:S(2)}) collective-permute-start(f32[256,128]{1,0:T(8,128)S(1)} %get-tuple-element.86), channel_id=1, source_target_pairs={{0,8},{4,12},{8,0},{12,4},{16,24},{20,28},{24,16},{28,20},{1,9},{5... | collective-permute-start | bytes 393224 | tf_op jit(solution)/shard_map/ppermute | solution.py:102
  38.1 3.5 %shard_map.119 = (bf16[256,1024]{1,0:T(8,128)(2,1)}, f32[256,1024]{1,0:T(8,128)S(1)}, f32[256,1024]{1,0:T(8,128)S(1)}) custom-call(bf16[256,1024]{1,0:T(8,128)(2,1)S(1)} %get-tuple-element.79.attn_grad_ref, bf16[256,1024]{1,0:T(8,128)(2,1)S(1)} %copy-done.2, bf16[256,1024]{1,0:T(8,128)(2,1)S(1)} %copy-done, bf16[256,1024]{1,0:T(8,128)(2,1)S(1)} %copy-done.1, ...), custom_call_target="tpu_custom_call" | custom-call | flops 671088640 | tf_op jit(solution)/shard_map/pallas_call | solution.py:25
  41.6 0.6 %collective-permute-done.17.refs_2_ = f32[256,128]{1,0:T(8,128)S(1)} collective-permute-done((f32[256,128]{1,0:T(8,128)S(1)}, f32[256,128]{1,0:T(8,128)S(1)}, u32[]{:S(2)}, u32[]{:S(2)}) %collective-permute-start.17) | collective-permute-done | bytes 131104 | tf_op jit(solution)/shard_map/ppermute | solution.py:102
  42.2 0.2 shard_map.120
  42.4 0.9 %collective-permute-start.19 = (f32[264,128]{1,0:T(8,128)S(1)}, f32[264,128]{1,0:T(8,128)S(1)}, u32[]{:S(2)}, u32[]{:S(2)}) collective-permute-start(f32[264,128]{1,0:T(8,128)S(1)} %get-tuple-element.89), channel_id=1, source_target_pairs={{0,8},{4,12},{8,0},{12,4},{16,24},{20,28},{24,16},{28,20},{1,9},{5... | collective-permute-start | bytes 405512 | tf_op jit(solution)/shard_map/ppermute | solution.py:102
  43.4 0.1 shard_map.121.refs_4_
  43.5 2.9 %collective-permute-start.22 = (f32[256,128]{1,0:T(8,128)S(1)}, f32[256,128]{1,0:T(8,128)S(1)}, u32[]{:S(2)}, u32[]{:S(2)}) collective-permute-start(f32[256,128]{1,0:T(8,128)S(1)} %shard_map.121.refs_4_), channel_id=1, source_target_pairs={{0,16},{4,20},{8,24},{12,28},{16,0},{20,4},{24,8},{28,12},{1,17},{... | collective-permute-start | bytes 393224 | tf_op jit(solution)/shard_map/ppermute | solution.py:116
  46.3 1.0 %collective-permute-start.20 = (f32[256,128]{1,0:T(8,128)S(1)}, f32[256,128]{1,0:T(8,128)S(1)}, u32[]{:S(2)}, u32[]{:S(2)}) collective-permute-start(f32[256,128]{1,0:T(8,128)S(1)} %get-tuple-element.90), channel_id=1, source_target_pairs={{0,4},{4,0},{8,12},{12,8},{16,20},{20,16},{24,28},{28,24},{1,5},{5... | collective-permute-start | bytes 393224 | tf_op jit(solution)/shard_map/ppermute | solution.py:102
  47.4 1.4 %collective-permute-start.21 = (f32[256,128]{1,0:T(8,128)S(1)}, f32[256,128]{1,0:T(8,128)S(1)}, u32[]{:S(2)}, u32[]{:S(2)}) collective-permute-start(f32[256,128]{1,0:T(8,128)S(1)} %get-tuple-element.91), channel_id=1, source_target_pairs={{0,12},{4,8},{8,4},{12,0},{16,28},{20,24},{24,20},{28,16},{1,13},{... | collective-permute-start | bytes 393224 | tf_op jit(solution)/shard_map/ppermute | solution.py:102
  48.8 0.7 %collective-permute-done.22.refs_5_ = f32[256,128]{1,0:T(8,128)S(1)} collective-permute-done((f32[256,128]{1,0:T(8,128)S(1)}, f32[256,128]{1,0:T(8,128)S(1)}, u32[]{:S(2)}, u32[]{:S(2)}) %collective-permute-start.22) | collective-permute-done | bytes 131104 | tf_op jit(solution)/shard_map/ppermute | solution.py:116
  49.5 0.2 shard_map.122
  49.7 4.6 %collective-permute-start.23 = (f32[256,128]{1,0:T(8,128)S(1)}, f32[256,128]{1,0:T(8,128)S(1)}, u32[]{:S(2)}, u32[]{:S(2)}) collective-permute-start(f32[256,128]{1,0:T(8,128)S(1)} %get-tuple-element.93), channel_id=1, source_target_pairs={{0,12},{4,8},{8,4},{12,0},{16,28},{20,24},{24,20},{28,16},{1,13},{... | collective-permute-start | bytes 393224 | tf_op jit(solution)/shard_map/ppermute | solution.py:102
  54.3 0.6 %collective-permute-start.25 = (f32[256,128]{1,0:T(8,128)S(1)}, f32[256,128]{1,0:T(8,128)S(1)}, u32[]{:S(2)}, u32[]{:S(2)}) collective-permute-start(f32[256,128]{1,0:T(8,128)S(1)} %get-tuple-element.95), channel_id=1, source_target_pairs={{0,8},{4,12},{8,0},{12,4},{16,24},{20,28},{24,16},{28,20},{1,9},{5... | collective-permute-start | bytes 393224 | tf_op jit(solution)/shard_map/ppermute | solution.py:102
  55.0 1.2 %collective-permute-done.20.refs_2_ = f32[256,128]{1,0:T(8,128)S(1)} collective-permute-done((f32[256,128]{1,0:T(8,128)S(1)}, f32[256,128]{1,0:T(8,128)S(1)}, u32[]{:S(2)}, u32[]{:S(2)}) %collective-permute-start.20) | collective-permute-done | bytes 131104 | tf_op jit(solution)/shard_map/ppermute | solution.py:102
  56.2 1.2 %collective-permute-done.23.refs_5_ = f32[256,128]{1,0:T(8,128)S(1)} collective-permute-done((f32[256,128]{1,0:T(8,128)S(1)}, f32[256,128]{1,0:T(8,128)S(1)}, u32[]{:S(2)}, u32[]{:S(2)}) %collective-permute-start.23) | collective-permute-done | bytes 131104 | tf_op jit(solution)/shard_map/ppermute | solution.py:102
  57.4 1.9 %collective-permute-done.24.refs_6_ = f32[256,128]{1,0:T(8,128)S(1)} collective-permute-done((f32[256,128]{1,0:T(8,128)S(1)}, f32[256,128]{1,0:T(8,128)S(1)}, u32[]{:S(2)}, u32[]{:S(2)}) %collective-permute-start.24) | collective-permute-done | bytes 131104 | tf_op jit(solution)/shard_map/ppermute | solution.py:102
  59.3 1.7 %shard_map.123 = (bf16[256,1024]{1,0:T(8,128)(2,1)}, bf16[256,1024]{1,0:T(8,128)(2,1)}, f32[1024,128]{1,0:T(8,128)}) custom-call(f32[256,128]{1,0:T(8,128)S(1)} %get-tuple-element.88.refs_5_.refs_0_, f32[264,128]{1,0:T(8,128)S(1)} %collective-permute-done.19.refs_9_.refs_1_, f32[256,128]{1,0:T(8,128)S(1)} %collective-permute-done.20.refs_2_, ...), custom_call_target="tpu_custom_call" | custom-call | tf_op jit(solution)/shard_map/pallas_call | solution.py:25
  (31 shorter events, 0.3 us)
Async XLA Ops:
  2.8 8.0 %collective-permute-start = (f32[136,128]{1,0:T(8,128)S(1)}, f32[136,128]{1,0:T(8,128)S(1)}, u32[]{:S(2)}, u32[]{:S(2)}) collective-permute-start(f32[136,128]{1,0:T(8,128)S(1)} %get-tuple-element.54), channel_id=1, source_target_pairs={{0,12},{4,8},{8,4},{12,0},{16,28},{20,24},{24,20},{28,16},{1,13},{... | collective-permute-start | bytes 208904 | tf_op jit(solution)/shard_map/ppermute | solution.py:102
  6.9 5.1 %collective-permute-start.1 = (f32[136,128]{1,0:T(8,128)S(1)}, f32[136,128]{1,0:T(8,128)S(1)}, u32[]{:S(2)}, u32[]{:S(2)}) collective-permute-start(f32[136,128]{1,0:T(8,128)S(1)} %get-tuple-element.55), channel_id=1, source_target_pairs={{0,4},{4,0},{8,12},{12,8},{16,20},{20,16},{24,28},{28,24},{1,5},{5... | collective-permute-start | bytes 208904 | tf_op jit(solution)/shard_map/ppermute | solution.py:102
  7.4 4.6 %collective-permute-start.2 = (f32[136,128]{1,0:T(8,128)S(1)}, f32[136,128]{1,0:T(8,128)S(1)}, u32[]{:S(2)}, u32[]{:S(2)}) collective-permute-start(f32[136,128]{1,0:T(8,128)S(1)} %get-tuple-element.56), channel_id=1, source_target_pairs={{0,8},{4,12},{8,0},{12,4},{16,24},{20,28},{24,16},{28,20},{1,9},{5... | collective-permute-start | bytes 208904 | tf_op jit(solution)/shard_map/ppermute | solution.py:102
  7.5 7.2 %collective-permute-start.6 = (f32[128,128]{1,0:T(8,128)S(1)}, f32[128,128]{1,0:T(8,128)S(1)}, u32[]{:S(2)}, u32[]{:S(2)}) collective-permute-start(f32[128,128]{1,0:T(8,128)S(1)} %get-tuple-element.63), channel_id=1, source_target_pairs={{0,12},{4,8},{8,4},{12,0},{16,28},{20,24},{24,20},{28,16},{1,13},{... | collective-permute-start | bytes 196616 | tf_op jit(solution)/shard_map/ppermute | solution.py:102
  10.3 4.3 %collective-permute-start.7 = (f32[128,128]{1,0:T(8,128)S(1)}, f32[128,128]{1,0:T(8,128)S(1)}, u32[]{:S(2)}, u32[]{:S(2)}) collective-permute-start(f32[128,128]{1,0:T(8,128)S(1)} %get-tuple-element.64), channel_id=1, source_target_pairs={{0,4},{4,0},{8,12},{12,8},{16,20},{20,16},{24,28},{28,24},{1,5},{5... | collective-permute-start | bytes 196616 | tf_op jit(solution)/shard_map/ppermute | solution.py:102
  10.9 4.3 %collective-permute-start.8 = (f32[128,128]{1,0:T(8,128)S(1)}, f32[128,128]{1,0:T(8,128)S(1)}, u32[]{:S(2)}, u32[]{:S(2)}) collective-permute-start(f32[128,128]{1,0:T(8,128)S(1)} %get-tuple-element.65), channel_id=1, source_target_pairs={{0,8},{4,12},{8,0},{12,4},{16,24},{20,28},{24,16},{28,20},{1,9},{5... | collective-permute-start | bytes 196616 | tf_op jit(solution)/shard_map/ppermute | solution.py:102
  12.0 7.3 %collective-permute-start.3 = (f32[136,128]{1,0:T(8,128)S(1)}, f32[136,128]{1,0:T(8,128)S(1)}, u32[]{:S(2)}, u32[]{:S(2)}) collective-permute-start(f32[136,128]{1,0:T(8,128)S(1)} %get-tuple-element.57.refs_4_), channel_id=1, source_target_pairs={{0,16},{4,20},{8,24},{12,28},{16,0},{20,4},{24,8},{28,12},{1,17},{... | collective-permute-start | bytes 208904 | tf_op jit(solution)/shard_map/ppermute | solution.py:116
  15.2 4.2 %copy-start.3 = (f32[8,128,128]{2,1,0:T(8,128)S(1)}, f32[8,128,128]{2,1,0:T(8,128)}, u32[]{:S(2)}) copy-start(f32[8,128,128]{2,1,0:T(8,128)} %param.14) | copy-start | bytes 1572868
  15.2 10.4 %copy-start.5 = (bf16[256,1024]{1,0:T(8,128)(2,1)S(1)}, bf16[256,1024]{1,0:T(8,128)(2,1)}, u32[]{:S(2)}) copy-start(bf16[256,1024]{1,0:T(8,128)(2,1)} %upstream_ref.1) | copy-start | bytes 1572868
  15.3 5.7 %collective-permute-start.9 = (f32[128,128]{1,0:T(8,128)S(1)}, f32[128,128]{1,0:T(8,128)S(1)}, u32[]{:S(2)}, u32[]{:S(2)}) collective-permute-start(f32[128,128]{1,0:T(8,128)S(1)} %shard_map.114.refs_4_), channel_id=1, source_target_pairs={{0,16},{4,20},{8,24},{12,28},{16,0},{20,4},{24,8},{28,12},{1,17},{... | collective-permute-start | bytes 196616 | tf_op jit(solution)/shard_map/ppermute | solution.py:116
  19.4 6.3 %copy-start.1 = (bf16[256,1024]{1,0:T(8,128)(2,1)S(1)}, bf16[256,1024]{1,0:T(8,128)(2,1)}, u32[]{:S(2)}) copy-start(bf16[256,1024]{1,0:T(8,128)(2,1)} %refs_11_.1) | copy-start | bytes 1572868
  19.4 6.3 %copy-start.2 = (bf16[256,1024]{1,0:T(8,128)(2,1)S(1)}, bf16[256,1024]{1,0:T(8,128)(2,1)}, u32[]{:S(2)}) copy-start(bf16[256,1024]{1,0:T(8,128)(2,1)} %query_ref.3) | copy-start | bytes 1572868
  19.5 6.2 %copy-start = (bf16[256,1024]{1,0:T(8,128)(2,1)S(1)}, bf16[256,1024]{1,0:T(8,128)(2,1)}, u32[]{:S(2)}) copy-start(bf16[256,1024]{1,0:T(8,128)(2,1)} %refs_10_.1) | copy-start | bytes 1572868
  19.5 5.7 %collective-permute-start.4 = (f32[128,128]{1,0:T(8,128)S(1)}, f32[128,128]{1,0:T(8,128)S(1)}, u32[]{:S(2)}, u32[]{:S(2)}) collective-permute-start(f32[128,128]{1,0:T(8,128)S(1)} %get-tuple-element.60), channel_id=1, source_target_pairs={{0,4},{4,0},{8,12},{12,8},{16,20},{20,16},{24,28},{28,24},{1,5},{5... | collective-permute-start | bytes 196616 | tf_op jit(solution)/shard_map/ppermute | solution.py:102
  20.6 5.0 %collective-permute-start.5 = (f32[128,128]{1,0:T(8,128)S(1)}, f32[128,128]{1,0:T(8,128)S(1)}, u32[]{:S(2)}, u32[]{:S(2)}) collective-permute-start(f32[128,128]{1,0:T(8,128)S(1)} %get-tuple-element.61), channel_id=1, source_target_pairs={{0,8},{4,12},{8,0},{12,4},{16,24},{20,28},{24,16},{28,20},{1,9},{5... | collective-permute-start | bytes 196616 | tf_op jit(solution)/shard_map/ppermute | solution.py:102
  21.1 7.5 %collective-permute-start.12 = (f32[256,128]{1,0:T(8,128)S(1)}, f32[256,128]{1,0:T(8,128)S(1)}, u32[]{:S(2)}, u32[]{:S(2)}) collective-permute-start(f32[256,128]{1,0:T(8,128)S(1)} %get-tuple-element.71), channel_id=1, source_target_pairs={{0,12},{4,8},{8,4},{12,0},{16,28},{20,24},{24,20},{28,16},{1,13},{... | collective-permute-start | bytes 393224 | tf_op jit(solution)/shard_map/ppermute | solution.py:102
  23.2 2.5 %copy-start.6 = (f32[1024]{0:T(1024)S(1)}, f32[1024]{0:T(1024)}, u32[]{:S(2)}) copy-start(f32[1024]{0:T(1024)} %param.13) | copy-start | bytes 12292
  23.2 4.9 %collective-permute-start.10 = (f32[128,128]{1,0:T(8,128)S(1)}, f32[128,128]{1,0:T(8,128)S(1)}, u32[]{:S(2)}, u32[]{:S(2)}) collective-permute-start(f32[128,128]{1,0:T(8,128)S(1)} %get-tuple-element.69), channel_id=1, source_target_pairs={{0,4},{4,0},{8,12},{12,8},{16,20},{20,16},{24,28},{28,24},{1,5},{5... | collective-permute-start | bytes 196616 | tf_op jit(solution)/shard_map/ppermute | solution.py:102
  24.3 4.3 %collective-permute-start.11 = (f32[128,128]{1,0:T(8,128)S(1)}, f32[128,128]{1,0:T(8,128)S(1)}, u32[]{:S(2)}, u32[]{:S(2)}) collective-permute-start(f32[128,128]{1,0:T(8,128)S(1)} %get-tuple-element.70), channel_id=1, source_target_pairs={{0,8},{4,12},{8,0},{12,4},{16,24},{20,28},{24,16},{28,20},{1,9},{5... | collective-permute-start | bytes 196616 | tf_op jit(solution)/shard_map/ppermute | solution.py:102
  29.2 1.8 %collective-permute-start.15 = (f32[8,256]{1,0:T(8,128)S(1)}, f32[8,256]{1,0:T(8,128)S(1)}, u32[]{:S(2)}, u32[]{:S(2)}) collective-permute-start(f32[8,256]{1,0:T(8,128)S(1)} %get-tuple-element.76.refs_0_), channel_id=1, source_target_pairs={{0,3},{1,0},{2,1},{3,2},{4,7},{5,4},{6,5},{7,6},{8,11},{9,8},{10,9... | collective-permute-start | bytes 24584 | tf_op jit(solution)/shard_map/ppermute | solution.py:570
  29.2 3.7 %collective-permute-start.14 = (f32[8,256]{1,0:T(8,128)S(1)}, f32[8,256]{1,0:T(8,128)S(1)}, u32[]{:S(2)}, u32[]{:S(2)}) collective-permute-start(f32[8,256]{1,0:T(8,128)S(1)} %get-tuple-element.76.refs_0_), channel_id=1, source_target_pairs={{0,2},{1,3},{2,0},{3,1},{4,6},{5,7},{6,4},{7,5},{8,10},{9,11},{10,... | collective-permute-start | bytes 24584 | tf_op jit(solution)/shard_map/ppermute | solution.py:570
  30.8 3.1 %collective-permute-start.13 = (f32[8,256]{1,0:T(8,128)S(1)}, f32[8,256]{1,0:T(8,128)S(1)}, u32[]{:S(2)}, u32[]{:S(2)}) collective-permute-start(f32[8,256]{1,0:T(8,128)S(1)} %get-tuple-element.76.refs_0_), channel_id=1, source_target_pairs={{0,1},{1,2},{2,3},{3,0},{4,5},{5,6},{6,7},{7,4},{8,9},{9,10},{10,1... | collective-permute-start | bytes 24584 | tf_op jit(solution)/shard_map/ppermute | solution.py:570
  34.6 7.0 %collective-permute-start.16 = (f32[256,128]{1,0:T(8,128)S(1)}, f32[256,128]{1,0:T(8,128)S(1)}, u32[]{:S(2)}, u32[]{:S(2)}) collective-permute-start(f32[256,128]{1,0:T(8,128)S(1)} %get-tuple-element.84), channel_id=1, source_target_pairs={{0,12},{4,8},{8,4},{12,0},{16,28},{20,24},{24,20},{28,16},{1,13},{... | collective-permute-start | bytes 393224 | tf_op jit(solution)/shard_map/ppermute | solution.py:102
  36.0 6.2 %collective-permute-start.17 = (f32[256,128]{1,0:T(8,128)S(1)}, f32[256,128]{1,0:T(8,128)S(1)}, u32[]{:S(2)}, u32[]{:S(2)}) collective-permute-start(f32[256,128]{1,0:T(8,128)S(1)} %get-tuple-element.85), channel_id=1, source_target_pairs={{0,4},{4,0},{8,12},{12,8},{16,20},{20,16},{24,28},{28,24},{1,5},{5... | collective-permute-start | bytes 393224 | tf_op jit(solution)/shard_map/ppermute | solution.py:102
  37.0 5.3 %collective-permute-start.18 = (f32[256,128]{1,0:T(8,128)S(1)}, f32[256,128]{1,0:T(8,128)S(1)}, u32[]{:S(2)}, u32[]{:S(2)}) collective-permute-start(f32[256,128]{1,0:T(8,128)S(1)} %get-tuple-element.86), channel_id=1, source_target_pairs={{0,8},{4,12},{8,0},{12,4},{16,24},{20,28},{24,16},{28,20},{1,9},{5... | collective-permute-start | bytes 393224 | tf_op jit(solution)/shard_map/ppermute | solution.py:102
  38.1 4.1 %copy-start.4 = (f32[8,128,128]{2,1,0:T(8,128)S(1)}, f32[8,128,128]{2,1,0:T(8,128)}, u32[]{:S(2)}) copy-start(f32[8,128,128]{2,1,0:T(8,128)} %param.15) | copy-start | bytes 1572868
  42.4 7.1 %collective-permute-start.19 = (f32[264,128]{1,0:T(8,128)S(1)}, f32[264,128]{1,0:T(8,128)S(1)}, u32[]{:S(2)}, u32[]{:S(2)}) collective-permute-start(f32[264,128]{1,0:T(8,128)S(1)} %get-tuple-element.89), channel_id=1, source_target_pairs={{0,8},{4,12},{8,0},{12,4},{16,24},{20,28},{24,16},{28,20},{1,9},{5... | collective-permute-start | bytes 405512 | tf_op jit(solution)/shard_map/ppermute | solution.py:102
  43.5 6.0 %collective-permute-start.22 = (f32[256,128]{1,0:T(8,128)S(1)}, f32[256,128]{1,0:T(8,128)S(1)}, u32[]{:S(2)}, u32[]{:S(2)}) collective-permute-start(f32[256,128]{1,0:T(8,128)S(1)} %shard_map.121.refs_4_), channel_id=1, source_target_pairs={{0,16},{4,20},{8,24},{12,28},{16,0},{20,4},{24,8},{28,12},{1,17},{... | collective-permute-start | bytes 393224 | tf_op jit(solution)/shard_map/ppermute | solution.py:116
  46.3 9.8 %collective-permute-start.20 = (f32[256,128]{1,0:T(8,128)S(1)}, f32[256,128]{1,0:T(8,128)S(1)}, u32[]{:S(2)}, u32[]{:S(2)}) collective-permute-start(f32[256,128]{1,0:T(8,128)S(1)} %get-tuple-element.90), channel_id=1, source_target_pairs={{0,4},{4,0},{8,12},{12,8},{16,20},{20,16},{24,28},{28,24},{1,5},{5... | collective-permute-start | bytes 393224 | tf_op jit(solution)/shard_map/ppermute | solution.py:102
  47.4 8.8 %collective-permute-start.21 = (f32[256,128]{1,0:T(8,128)S(1)}, f32[256,128]{1,0:T(8,128)S(1)}, u32[]{:S(2)}, u32[]{:S(2)}) collective-permute-start(f32[256,128]{1,0:T(8,128)S(1)} %get-tuple-element.91), channel_id=1, source_target_pairs={{0,12},{4,8},{8,4},{12,0},{16,28},{20,24},{24,20},{28,16},{1,13},{... | collective-permute-start | bytes 393224 | tf_op jit(solution)/shard_map/ppermute | solution.py:102
  49.7 7.6 %collective-permute-start.23 = (f32[256,128]{1,0:T(8,128)S(1)}, f32[256,128]{1,0:T(8,128)S(1)}, u32[]{:S(2)}, u32[]{:S(2)}) collective-permute-start(f32[256,128]{1,0:T(8,128)S(1)} %get-tuple-element.93), channel_id=1, source_target_pairs={{0,12},{4,8},{8,4},{12,0},{16,28},{20,24},{24,20},{28,16},{1,13},{... | collective-permute-start | bytes 393224 | tf_op jit(solution)/shard_map/ppermute | solution.py:102
  54.3 5.0 %collective-permute-start.24 = (f32[256,128]{1,0:T(8,128)S(1)}, f32[256,128]{1,0:T(8,128)S(1)}, u32[]{:S(2)}, u32[]{:S(2)}) collective-permute-start(f32[256,128]{1,0:T(8,128)S(1)} %get-tuple-element.94), channel_id=1, source_target_pairs={{0,4},{4,0},{8,12},{12,8},{16,20},{20,16},{24,28},{28,24},{1,5},{5... | collective-permute-start | bytes 393224 | tf_op jit(solution)/shard_map/ppermute | solution.py:102
  54.3 5.0 %collective-permute-start.25 = (f32[256,128]{1,0:T(8,128)S(1)}, f32[256,128]{1,0:T(8,128)S(1)}, u32[]{:S(2)}, u32[]{:S(2)}) collective-permute-start(f32[256,128]{1,0:T(8,128)S(1)} %get-tuple-element.95), channel_id=1, source_target_pairs={{0,8},{4,12},{8,0},{12,4},{16,24},{20,28},{24,16},{28,20},{1,9},{5... | collective-permute-start | bytes 393224 | tf_op jit(solution)/shard_map/ppermute | solution.py:102

commit v11 on v10

--- a/solution.py
+++ b/solution.py
@@ -21,13 +21,14 @@
 ANY = pl.BlockSpec(memory_space=pl.ANY)
 
 
-def call(body, outs, operands, scratch=(), flops=0, specs=None, out_specs=None):
+def call(body, outs, operands, scratch=(), flops=0, specs=None, out_specs=None, aliases=None):
     return pl.pallas_call(
         body,
         out_shape=outs,
         in_specs=specs or [VMEM] * len(operands),
         out_specs=out_specs or [VMEM] * len(outs),
         scratch_shapes=list(scratch),
+        input_output_aliases=aliases or {},
         compiler_params=pltpu.CompilerParams(vmem_limit_bytes=24 * 1024 * 1024),
         cost_estimate=pl.CostEstimate(flops=flops, bytes_accessed=0, transcendentals=0),
     )(*operands)
@@ -407,10 +408,14 @@
     query_grad_ref,
     key_part_ref,
     value_part_ref,
+    key_decayed_ref,
+    value_decayed_ref,
 ):
-    causal = causal_mask(query_ref.shape[0])
+    length = query_ref.shape[0]
+    causal = causal_mask(length)
     cum_col = cum_col_ref[...]
     growth = jnp.exp(cum_col)
+    shrink = jnp.exp(cum_col[length - 1 : length, :] - cum_col)
     for h in range(plan.heads):
         cut = lanes(h, plan.size)
         attn_grad = attn_grad_ref[:, cut]
@@ -421,46 +426,48 @@
         query_grad_ref[:, cut] = query_grad.astype(BF16)
         key_part_ref[:, cut] = dot(score_grad, query_ref[:, cut], CONTRACT_ROWS)
         value_part_ref[:, cut] = dot(weight_ref[h], attn_grad, CONTRACT_ROWS)
-
-
-def finish_body(plan, *refs):
-    first_refs, refs = refs[: plan.members], refs[plan.members :]
-    second_refs, refs = refs[: plan.members], refs[plan.members :]
-    key_part_ref, value_part_ref, key_ref, value_ref, cum_col_ref, summary_ref, before_ref = refs[:7]
-    key_out, value_out, total_out, held_ref, key_grad_ref, value_grad_ref, total_ref, sems = refs[7:]
-    length, size = key_ref.shape[0], plan.size
-    swapped = jnp.where(plan.group() == 0, 0, 1) if plan.groups == 2 else 0
-    for k, way in enumerate(plan.early_ways if plan.groups == 2 else plan.ways):
-        held_ref[swapped, plan.rows_of(plan.toward(way))] = first_refs[k][: plan.rows]
-        held_ref[1 - swapped, plan.rows_of(plan.peer(k))] = second_refs[k][...]
-    cum_col = cum_col_ref[...]
-    block_log = cum_col[length - 1 : length, :]
-    shrink = jnp.exp(block_log - cum_col)
+        column = shrink[:, h : h + 1]
+        key_decayed_ref[:, cut] = (key_ref[:, cut].astype(F32) * column).astype(BF16)
+        value_decayed_ref[:, cut] = (value_ref[:, cut].astype(F32) * column).astype(BF16)
+
+
+def finish_body(plan, ways, *refs):
+    early_refs, refs = refs[: len(ways)], refs[len(ways) :]
+    late_refs, refs = refs[: len(ways)], refs[len(ways) :]
+    key_part_ref, value_part_ref, key_ref, value_ref, summary_ref, before_ref, logs_ref = refs[:7]
+    key_out, value_out, total_out, key_grad_ref, value_grad_ref, total_ref, sems = refs[-7:]
+    size, rows = plan.size, plan.rows
+    first = plan.group() == 0
     copies = []
-    batch = max(plan.heads // 4, 1)
-    for h in range(plan.heads):
-        cut = lanes(h, size)
-        grads = held_ref[1, cut]
-        scale = jnp.exp(before_ref[h : h + 1])
-        scale_next = jnp.exp(before_ref[h : h + 1] + block_log[:, h : h + 1])
-        total_ref[cut] = held_ref[0, cut] + scale * summary_ref[cut] + scale_next * grads
-        grads = grads.astype(BF16)
-        column = shrink[:, h : h + 1]
-        key_state = dot(value_ref[:, cut], grads, CONTRACT_COLS)
-        key_grad_ref[:, cut] = (key_part_ref[:, cut] + column * key_state).astype(BF16)
-        value_state = dot(key_ref[:, cut], grads)
-        value_grad_ref[:, cut] = (value_part_ref[:, cut] + column * value_state).astype(BF16)
-        if (h + 1) % batch == 0:
-            done = slice((h + 1 - batch) * size, (h + 1) * size)
-            for source, target, index in [
-                (total_ref, total_out, (done,)),
-                (key_grad_ref, key_out, (slice(None), done)),
-                (value_grad_ref, value_out, (slice(None), done)),
-            ]:
-                copies.append(
-                    pltpu.make_async_copy(source.at[index], target.at[index], sems.at[len(copies)])
-                )
-                copies[-1].start()
+    for i, way in enumerate(ways):
+        owner = plan.toward(way)
+        before, after = early_refs[i][:rows], late_refs[i][:rows]
+        if plan.groups == 2:
+            before, after = jnp.where(first, before, after), jnp.where(first, after, before)
+        for j in range(plan.own):
+            head = owner * plan.own + j
+            part = pl.ds(pl.multiple_of(head * size, size), size)
+            cut = slice(i * rows + j * size, i * rows + (j + 1) * size)
+            grads = after[lanes(j, size)]
+            log_before = before_ref[pl.ds(head, 1)]
+            scale = jnp.exp(log_before)
+            scale_next = jnp.exp(log_before + logs_ref[plan.member(), pl.ds(head, 1)])
+            total_ref[cut] = (
+                before[lanes(j, size)] + scale * summary_ref[part] + scale_next * grads
+            )
+            grads = grads.astype(BF16)
+            key_state = dot(value_ref[:, part], grads, CONTRACT_COLS)
+            key_grad_ref[:, cut] = (key_part_ref[:, part] + key_state).astype(BF16)
+            value_state = dot(key_ref[:, part], grads)
+            value_grad_ref[:, cut] = (value_part_ref[:, part] + value_state).astype(BF16)
+        done, place = lanes(i, rows), plan.rows_of(owner)
+        for source, target in [
+            (total_ref.at[done], total_out.at[place]),
+            (key_grad_ref.at[:, done], key_out.at[:, place]),
+            (value_grad_ref.at[:, done], value_out.at[:, place]),
+        ]:
+            copies.append(pltpu.make_async_copy(source, target, sems.at[len(copies)]))
+            copies[-1].start()
     for copy in copies:
         copy.wait()
 
@@ -576,9 +583,9 @@
         [*all_sums, attended, query_decayed, gained],
     )
     parts = plan.swap_in_group(sends)
-    query_grad, key_part, value_part = call(
+    query_grad, key_part, value_part, key_decayed, value_decayed = call(
         bind(score_grad_body),
-        [rounded, table, table],
+        [rounded, table, table, rounded, rounded],
         [attn_grad, query_rows, key_rows, value_rows, states, weights, cum_log, cum_col],
         flops=10 * heads * length * length * size,
     )
@@ -594,7 +601,7 @@
             specs=[VMEM] * (plan.members + 2) + [ANY],
         )
         tie = sends[0]
-        swapped = [plan.swap_in_group(sends, plan.early_ways)]
+        swapped = [dict(zip(plan.early_ways, plan.swap_in_group(sends, plan.early_ways)))]
     (total,) = call(
         bind(group_grad_body),
         [piece],
@@ -606,25 +613,45 @@
     sends = call(
         bind(reverse_scan_body),
         pieces * (1 if two_sided else 2),
-        [*parts, *totals, logs, all_logs, grad_rows, swapped[0][1] if two_sided else tie],
+        [*parts, *totals, logs, all_logs, grad_rows, swapped[0][plan.early_ways[1]] if two_sided else tie],
         [hold_groups, hold],
         specs=[VMEM] * (plan.members + plan.groups + 3) + [ANY],
     )
     for first in range(0, len(sends), plan.members):
-        swapped.append(plan.swap_in_group(sends[first : first + plan.members]))
-    key_grad, value_grad, state_in_grad = call(
-        bind(finish_body),
-        [rounded, rounded, shaped((width, size))],
-        [*swapped[0], *swapped[1], key_part, value_part, key_rows, value_rows, cum_col, summary, before],
-        [
-            pltpu.VMEM((2, width, size), F32),
-            pltpu.VMEM((length, width), BF16),
-            pltpu.VMEM((length, width), BF16),
-            pltpu.VMEM((width, size), F32),
-            pltpu.SemaphoreType.DMA((12,)),
-        ],
-        out_specs=[HBM] * 3,
-    )
+        pieces_back = plan.swap_in_group(sends[first : first + plan.members])
+        swapped.append(dict(zip(plan.ways, pieces_back)))
+    outs = []
+    for ways in ([0] + plan.far, plan.near):
+        if not ways:
+            continue
+        operands = [
+            *[pieces_back[way] for pieces_back in swapped for way in ways],
+            key_part,
+            value_part,
+            key_decayed,
+            value_decayed,
+            summary,
+            before,
+            logs,
+        ]
+        if two_sided and not outs:
+            outs = [swapped[0][way] for way in plan.near]
+        count = len(operands)
+        outs = call(
+            bind(finish_body, ways),
+            [rounded, rounded, shaped((width, size))],
+            [*operands, *outs],
+            [
+                pltpu.VMEM((length, len(ways) * plan.rows), BF16),
+                pltpu.VMEM((length, len(ways) * plan.rows), BF16),
+                pltpu.VMEM((len(ways) * plan.rows, size), F32),
+                pltpu.SemaphoreType.DMA((3 * len(ways),)),
+            ],
+            specs=[VMEM] * count + [ANY] * len(outs),
+            out_specs=[HBM] * 3,
+            aliases={count + i: i for i in range(3)} if len(outs) == 3 else None,
+        )
+    key_grad, value_grad, state_in_grad = outs
     return (query_grad, key_grad, value_grad, state_in_grad.reshape(heads, size, size))
 
 

time: 61.2 us -> 60.7 us (level)
  waiting for transfers between devices: 13.5 us -> 12.4 us
    ppermute x20, waiting for transfers between devices: 8.46 us -> 7.32 us  [swap(): return lax.ppermute(piece, 'seq', pairs) if way else piece]
    pallas_call x13 -> x14, Pallas kernels: 10.7 us -> 11.3 us  [call(): pl.pallas_call(body, out_shape=outs, in_specs=specs or [VMEM] * len(opera...]
  transfers between devices with their start and end apart: 26 -> 26, of which waited for: 14 -> 14; matrix products, arithmetic and copies ran while one was open for 0% -> 0% of each run, Pallas kernels for 9% -> 11%
where the time goes in v11:
time: 60.7 us; the launch traced here: 60.5 us
  starting transfers between devices  36 us (59%)
  waiting for transfers between devices  12.4 us (20%)
  Pallas kernels  11.3 us (19%)
  between operations  0.75 us (1%)
    ppermute x20, starting transfers between devices, swap(): return lax.ppermute(piece, 'seq', pairs) if way else piece  26.1 us
    pallas_call x14, Pallas kernels, call(): pl.pallas_call(body, out_shape=outs, in_specs=specs or [VMEM] * len(opera...  11.3 us
    ppermute x3, starting transfers between devices, from_groups(): lax.ppermute(piece, 'seq', [(i, (i + step * self.members) % self.blocks)...  8.1 us
    ppermute x20, waiting for transfers between devices, swap(): return lax.ppermute(piece, 'seq', pairs) if way else piece  7.32 us
    ppermute x3, waiting for transfers between devices, on_device(): lax.ppermute(sums, 'head', [(i, (i + step) % parties) for i in range(part...  2.85 us
    ppermute x3, waiting for transfers between devices, from_groups(): lax.ppermute(piece, 'seq', [(i, (i + step * self.members) % self.blocks)...  2.25 us
    ppermute x3, starting transfers between devices, on_device(): lax.ppermute(sums, 'head', [(i, (i + step) % parties) for i in range(part...  1.8 us
  transfers between devices with their start and end apart: 26, of which 14 were waited for; matrix products, arithmetic and copies ran while one was open for 0% of the time, Pallas kernels for 11%

profile of v11, /device:TPU:0, one launch (start us, length us, event | category | flops | bytes accessed | tf_op | source)
XLA Modules:
  0.0 60.5 jit_solution(1186602677065502571)
XLA Ops:
  0.6 2.2 %shard_map.111 = (f32[136,128]{1,0:T(8,128)S(1)}, f32[136,128]{1,0:T(8,128)S(1)}, f32[136,128]{1,0:T(8,128)S(1)}, f32[136,128]{1,0:T(8,128)S(1)}, f32[128,128]{1...) custom-call(bf16[256,1024]{1,0:T(8,128)(2,1)} %key_ref.3, ...), custom_call_target="tpu_custom_call" | custom-call | tf_op jit(solution)/shard_map/pallas_call | solution.py:25
  2.8 4.0 %collective-permute-start = (f32[136,128]{1,0:T(8,128)S(1)}, f32[136,128]{1,0:T(8,128)S(1)}, u32[]{:S(2)}, u32[]{:S(2)}) collective-permute-start(f32[136,128]{1,0:T(8,128)S(1)} %get-tuple-element.59), channel_id=1, source_target_pairs={{0,12},{4,8},{8,4},{12,0},{16,28},{20,24},{24,20},{28,16},{1,13},{... | collective-permute-start | bytes 208904 | tf_op jit(solution)/shard_map/ppermute | solution.py:103
  6.9 0.5 collective-permute-start.1
  7.4 0.1 collective-permute-start.2
  7.5 2.8 %collective-permute-start.6 = (f32[128,128]{1,0:T(8,128)S(1)}, f32[128,128]{1,0:T(8,128)S(1)}, u32[]{:S(2)}, u32[]{:S(2)}) collective-permute-start(f32[128,128]{1,0:T(8,128)S(1)} %get-tuple-element.68), channel_id=1, source_target_pairs={{0,12},{4,8},{8,4},{12,0},{16,28},{20,24},{24,20},{28,16},{1,13},{... | collective-permute-start | bytes 196616 | tf_op jit(solution)/shard_map/ppermute | solution.py:103
  10.3 0.5 collective-permute-start.7
  10.9 0.8 %collective-permute-start.8 = (f32[128,128]{1,0:T(8,128)S(1)}, f32[128,128]{1,0:T(8,128)S(1)}, u32[]{:S(2)}, u32[]{:S(2)}) collective-permute-start(f32[128,128]{1,0:T(8,128)S(1)} %get-tuple-element.70), channel_id=1, source_target_pairs={{0,8},{4,12},{8,0},{12,4},{16,24},{20,28},{24,16},{28,20},{1,9},{5... | collective-permute-start | bytes 196616 | tf_op jit(solution)/shard_map/ppermute | solution.py:103
  11.6 0.4 collective-permute-done.1.refs_2_
  12.0 2.7 %collective-permute-start.3 = (f32[136,128]{1,0:T(8,128)S(1)}, f32[136,128]{1,0:T(8,128)S(1)}, u32[]{:S(2)}, u32[]{:S(2)}) collective-permute-start(f32[136,128]{1,0:T(8,128)S(1)} %get-tuple-element.62.refs_4_), channel_id=1, source_target_pairs={{0,16},{4,20},{8,24},{12,28},{16,0},{20,4},{24,8},{28,12},{1,17},{... | collective-permute-start | bytes 208904 | tf_op jit(solution)/shard_map/ppermute | solution.py:117
  14.7 0.5 collective-permute-done.8.refs_3_
  15.3 2.6 %collective-permute-start.9 = (f32[128,128]{1,0:T(8,128)S(1)}, f32[128,128]{1,0:T(8,128)S(1)}, u32[]{:S(2)}, u32[]{:S(2)}) collective-permute-start(f32[128,128]{1,0:T(8,128)S(1)} %shard_map.114.refs_4_), channel_id=1, source_target_pairs={{0,16},{4,20},{8,24},{12,28},{16,0},{20,4},{24,8},{28,12},{1,17},{... | collective-permute-start | bytes 196616 | tf_op jit(solution)/shard_map/ppermute | solution.py:117
  17.8 1.5 %collective-permute-done.3.refs_5_ = f32[136,128]{1,0:T(8,128)S(1)} collective-permute-done((f32[136,128]{1,0:T(8,128)S(1)}, f32[136,128]{1,0:T(8,128)S(1)}, u32[]{:S(2)}, u32[]{:S(2)}) %collective-permute-start.3) | collective-permute-done | bytes 69664 | tf_op jit(solution)/shard_map/ppermute | solution.py:117
  19.5 1.1 %collective-permute-start.4 = (f32[128,128]{1,0:T(8,128)S(1)}, f32[128,128]{1,0:T(8,128)S(1)}, u32[]{:S(2)}, u32[]{:S(2)}) collective-permute-start(f32[128,128]{1,0:T(8,128)S(1)} %get-tuple-element.65), channel_id=1, source_target_pairs={{0,4},{4,0},{8,12},{12,8},{16,20},{20,16},{24,28},{28,24},{1,5},{5... | collective-permute-start | bytes 196616 | tf_op jit(solution)/shard_map/ppermute | solution.py:103
  20.6 0.3 collective-permute-start.5
  21.1 2.1 %collective-permute-start.12 = (f32[256,128]{1,0:T(8,128)S(1)}, f32[256,128]{1,0:T(8,128)S(1)}, u32[]{:S(2)}, u32[]{:S(2)}) collective-permute-start(f32[256,128]{1,0:T(8,128)S(1)} %get-tuple-element.76), channel_id=1, source_target_pairs={{0,12},{4,8},{8,4},{12,0},{16,28},{20,24},{24,20},{28,16},{1,13},{... | collective-permute-start | bytes 393224 | tf_op jit(solution)/shard_map/ppermute | solution.py:103
  23.2 1.1 %collective-permute-start.10 = (f32[128,128]{1,0:T(8,128)S(1)}, f32[128,128]{1,0:T(8,128)S(1)}, u32[]{:S(2)}, u32[]{:S(2)}) collective-permute-start(f32[128,128]{1,0:T(8,128)S(1)} %get-tuple-element.74), channel_id=1, source_target_pairs={{0,4},{4,0},{8,12},{12,8},{16,20},{20,16},{24,28},{28,24},{1,5},{5... | collective-permute-start | bytes 196616 | tf_op jit(solution)/shard_map/ppermute | solution.py:103
  24.3 0.3 collective-permute-start.11
  24.6 0.6 collective-permute-done.4.refs_0_.refs_1_
  25.2 0.4 collective-permute-done.5.refs_1_.refs_2_
  25.7 1.2 %shard_map.116 = (bf16[8,256,256]{2,1,0:T(8,128)(2,1)S(1)}, f32[256,1024]{1,0:T(8,128)S(1)}, f32[256,1024]{1,0:T(8,128)S(1)}, bf16[8,128,256]{2,1,0:T(8,128)(2,1)S(1)}) custom-call(bf16[256,1024]{1,0:T(8,128)(2,1)S(1)} %copy-done, bf16[256,1024]{1,0:T(8,128)(2,1)S(1)} %copy-done.1, bf16[256,1024]{1,0:T(8,128)(2,1)S(1)} %copy-done.2, ...), custom_call_target="tpu_custom_call" | custom-call | flops 1000000000 | tf_op jit(solution)/shard_map/pallas_call | solution.py:25
  26.9 1.2 %collective-permute-done.10.refs_4_ = f32[128,128]{1,0:T(8,128)S(1)} collective-permute-done((f32[128,128]{1,0:T(8,128)S(1)}, f32[128,128]{1,0:T(8,128)S(1)}, u32[]{:S(2)}, u32[]{:S(2)}) %collective-permute-start.10) | collective-permute-done | bytes 65568 | tf_op jit(solution)/shard_map/ppermute | solution.py:103
  28.1 0.4 collective-permute-done.11.refs_5_
  28.5 0.7 %shard_map.117 = (f32[256,1024]{1,0:T(8,128)S(1)}, f32[8,256]{1,0:T(8,128)S(1)}, bf16[1024,128]{1,0:T(8,128)(2,1)S(1)}) custom-call(f32[128,128]{1,0:T(8,128)S(1)} %get-tuple-element.64.refs_0_, f32[128,128]{1,0:T(8,128)S(1)} %collective-permute-done.4.refs_0_.refs_1_, f32[128,128]{1,0:T(8,128)S(1)} %collective-permute-done.5.refs_1_.refs_2_, ...), custom_call_target="tpu_custom_call" | custom-call | tf_op jit(solution)/shard_map/pallas_call | solution.py:25
  29.2 1.6 %collective-permute-start.14 = (f32[8,256]{1,0:T(8,128)S(1)}, f32[8,256]{1,0:T(8,128)S(1)}, u32[]{:S(2)}, u32[]{:S(2)}) collective-permute-start(f32[8,256]{1,0:T(8,128)S(1)} %get-tuple-element.81.refs_0_), channel_id=1, source_target_pairs={{0,2},{1,3},{2,0},{3,1},{4,6},{5,7},{6,4},{7,5},{8,10},{9,11},{10,... | collective-permute-start | bytes 24584 | tf_op jit(solution)/shard_map/ppermute | solution.py:577
  30.8 0.2 collective-permute-start.13
  31.0 1.9 %collective-permute-done.14.refs_2_ = f32[8,256]{1,0:T(8,128)S(1)} collective-permute-done((f32[8,256]{1,0:T(8,128)S(1)}, f32[8,256]{1,0:T(8,128)S(1)}, u32[]{:S(2)}, u32[]{:S(2)}) %collective-permute-start.14) | collective-permute-done | bytes 8224 | tf_op jit(solution)/shard_map/ppermute | solution.py:577
  32.9 1.0 %collective-permute-done.13.refs_1_ = f32[8,256]{1,0:T(8,128)S(1)} collective-permute-done((f32[8,256]{1,0:T(8,128)S(1)}, f32[8,256]{1,0:T(8,128)S(1)}, u32[]{:S(2)}, u32[]{:S(2)}) %collective-permute-start.13) | collective-permute-done | bytes 8224 | tf_op jit(solution)/shard_map/ppermute | solution.py:577
  33.9 0.7 %shard_map.118 = (bf16[256,1024]{1,0:T(8,128)(2,1)S(1)}, f32[1024,128]{1,0:T(8,128)S(1)}, f32[256,128]{1,0:T(8,128)S(1)}, f32[256,128]{1,0:T(8,128)S(1)}, f32[25...) custom-call(f32[8,256]{1,0:T(8,128)S(1)} %get-tuple-element.81.refs_0_, f32[8,256]{1,0:T(8,128)S(1)} %collective-permute-done.13.refs_1_, ...), custom_call_target="tpu_custom_call" | custom-call | tf_op jit(solution)/shard_map/pallas_call | solution.py:25
  34.6 1.4 %collective-permute-start.16 = (f32[256,128]{1,0:T(8,128)S(1)}, f32[256,128]{1,0:T(8,128)S(1)}, u32[]{:S(2)}, u32[]{:S(2)}) collective-permute-start(f32[256,128]{1,0:T(8,128)S(1)} %get-tuple-element.89), channel_id=1, source_target_pairs={{0,12},{4,8},{8,4},{12,0},{16,28},{20,24},{24,20},{28,16},{1,13},{... | collective-permute-start | bytes 393224 | tf_op jit(solution)/shard_map/ppermute | solution.py:103
  36.0 0.9 %collective-permute-start.17 = (f32[256,128]{1,0:T(8,128)S(1)}, f32[256,128]{1,0:T(8,128)S(1)}, u32[]{:S(2)}, u32[]{:S(2)}) collective-permute-start(f32[256,128]{1,0:T(8,128)S(1)} %get-tuple-element.90), channel_id=1, source_target_pairs={{0,4},{4,0},{8,12},{12,8},{16,20},{20,16},{24,28},{28,24},{1,5},{5... | collective-permute-start | bytes 393224 | tf_op jit(solution)/shard_map/ppermute | solution.py:103
  37.0 1.2 %collective-permute-start.18 = (f32[256,128]{1,0:T(8,128)S(1)}, f32[256,128]{1,0:T(8,128)S(1)}, u32[]{:S(2)}, u32[]{:S(2)}) collective-permute-start(f32[256,128]{1,0:T(8,128)S(1)} %get-tuple-element.91), channel_id=1, source_target_pairs={{0,8},{4,12},{8,0},{12,4},{16,24},{20,28},{24,16},{28,20},{1,9},{5... | collective-permute-start | bytes 393224 | tf_op jit(solution)/shard_map/ppermute | solution.py:103
  38.2 3.4 %shard_map.119 = (bf16[256,1024]{1,0:T(8,128)(2,1)}, f32[256,1024]{1,0:T(8,128)S(1)}, f32[256,1024]{1,0:T(8,128)S(1)}, bf16[256,1024]{1,0:T(8,128)(2,1)S(1)}, bf16[256,1024]{1,0:T(8,128)(2,1)S(1)}) custom-call(bf16[256,1024]{1,0:T(8,128)(2,1)S(1)} %get-tuple-element.84.attn_grad_ref, bf16[256,1024]{1,0:T(8,128)(2,1)S(1)} %copy-done, ...), custom_call_target="tpu_custom_call" | custom-call | flops 671088640 | tf_op jit(solution)/shard_map/pallas_call | solution.py:25
  41.6 0.6 %collective-permute-done.17.refs_2_ = f32[256,128]{1,0:T(8,128)S(1)} collective-permute-done((f32[256,128]{1,0:T(8,128)S(1)}, f32[256,128]{1,0:T(8,128)S(1)}, u32[]{:S(2)}, u32[]{:S(2)}) %collective-permute-start.17) | collective-permute-done | bytes 131104 | tf_op jit(solution)/shard_map/ppermute | solution.py:103
  42.2 0.2 shard_map.120
  42.4 1.0 %collective-permute-start.20 = (f32[264,128]{1,0:T(8,128)S(1)}, f32[264,128]{1,0:T(8,128)S(1)}, u32[]{:S(2)}, u32[]{:S(2)}) collective-permute-start(f32[264,128]{1,0:T(8,128)S(1)} %get-tuple-element.94), channel_id=1, source_target_pairs={{0,8},{4,12},{8,0},{12,4},{16,24},{20,28},{24,16},{28,20},{1,9},{5... | collective-permute-start | bytes 405512 | tf_op jit(solution)/shard_map/ppermute | solution.py:103
  43.4 0.1 shard_map.121.refs_4_
  43.5 2.9 %collective-permute-start.21 = (f32[256,128]{1,0:T(8,128)S(1)}, f32[256,128]{1,0:T(8,128)S(1)}, u32[]{:S(2)}, u32[]{:S(2)}) collective-permute-start(f32[256,128]{1,0:T(8,128)S(1)} %shard_map.121.refs_4_), channel_id=1, source_target_pairs={{0,16},{4,20},{8,24},{12,28},{16,0},{20,4},{24,8},{28,12},{1,17},{... | collective-permute-start | bytes 393224 | tf_op jit(solution)/shard_map/ppermute | solution.py:117
  46.3 1.0 %collective-permute-start.19 = (f32[256,128]{1,0:T(8,128)S(1)}, f32[256,128]{1,0:T(8,128)S(1)}, u32[]{:S(2)}, u32[]{:S(2)}) collective-permute-start(f32[256,128]{1,0:T(8,128)S(1)} %get-tuple-element.93), channel_id=1, source_target_pairs={{0,4},{4,0},{8,12},{12,8},{16,20},{20,16},{24,28},{28,24},{1,5},{5... | collective-permute-start | bytes 393224 | tf_op jit(solution)/shard_map/ppermute | solution.py:103
  47.4 1.4 %collective-permute-start.24 = (f32[256,128]{1,0:T(8,128)S(1)}, f32[256,128]{1,0:T(8,128)S(1)}, u32[]{:S(2)}, u32[]{:S(2)}) collective-permute-start(f32[256,128]{1,0:T(8,128)S(1)} %get-tuple-element.103), channel_id=1, source_target_pairs={{0,12},{4,8},{8,4},{12,0},{16,28},{20,24},{24,20},{28,16},{1,13},{... | collective-permute-start | bytes 393224 | tf_op jit(solution)/shard_map/ppermute | solution.py:103
  48.8 0.7 %collective-permute-done.21.refs_5_ = f32[256,128]{1,0:T(8,128)S(1)} collective-permute-done((f32[256,128]{1,0:T(8,128)S(1)}, f32[256,128]{1,0:T(8,128)S(1)}, u32[]{:S(2)}, u32[]{:S(2)}) %collective-permute-start.21) | collective-permute-done | bytes 131104 | tf_op jit(solution)/shard_map/ppermute | solution.py:117
  49.5 0.2 shard_map.122
  49.8 4.6 %collective-permute-start.25 = (f32[256,128]{1,0:T(8,128)S(1)}, f32[256,128]{1,0:T(8,128)S(1)}, u32[]{:S(2)}, u32[]{:S(2)}) collective-permute-start(f32[256,128]{1,0:T(8,128)S(1)} %get-tuple-element.105), channel_id=1, source_target_pairs={{0,12},{4,8},{8,4},{12,0},{16,28},{20,24},{24,20},{28,16},{1,13},{... | collective-permute-start | bytes 393224 | tf_op jit(solution)/shard_map/ppermute | solution.py:103
  54.4 0.6 %collective-permute-start.23 = (f32[256,128]{1,0:T(8,128)S(1)}, f32[256,128]{1,0:T(8,128)S(1)}, u32[]{:S(2)}, u32[]{:S(2)}) collective-permute-start(f32[256,128]{1,0:T(8,128)S(1)} %get-tuple-element.97), channel_id=1, source_target_pairs={{0,8},{4,12},{8,0},{12,4},{16,24},{20,28},{24,16},{28,20},{1,9},{5... | collective-permute-start | bytes 393224 | tf_op jit(solution)/shard_map/ppermute | solution.py:103
  55.0 1.1 %collective-permute-done.19.refs_11_.refs_0_ = f32[256,128]{1,0:T(8,128)S(1)} collective-permute-done((f32[256,128]{1,0:T(8,128)S(1)}, f32[256,128]{1,0:T(8,128)S(1)}, u32[]{:S(2)}, u32[]{:S(2)}) %collective-permute-start.19) | collective-permute-done | bytes 131104 | tf_op jit(solution)/shard_map/ppermute | solution.py:103
  56.1 1.3 %collective-permute-done.25.refs_3_ = f32[256,128]{1,0:T(8,128)S(1)} collective-permute-done((f32[256,128]{1,0:T(8,128)S(1)}, f32[256,128]{1,0:T(8,128)S(1)}, u32[]{:S(2)}, u32[]{:S(2)}) %collective-permute-start.25) | collective-permute-done | bytes 131104 | tf_op jit(solution)/shard_map/ppermute | solution.py:103
  57.4 1.1 %shard_map.123 = (bf16[256,1024]{1,0:T(8,128)(2,1)}, bf16[256,1024]{1,0:T(8,128)(2,1)}, f32[1024,128]{1,0:T(8,128)}) custom-call(f32[256,128]{1,0:T(8,128)S(1)} %get-tuple-element.95.refs_5_.refs_0_, f32[256,128]{1,0:T(8,128)S(1)} %collective-permute-done.24.refs_1_, f32[256,128]{1,0:T(8,128)S(1)} %get-tuple-element.104.refs_2_, ...), custom_call_target="tpu_custom_call" | custom-call | tf_op jit(solution)/shard_map/pallas_call | solution.py:25
  58.6 0.8 %collective-permute-done.22.refs_2_ = f32[256,128]{1,0:T(8,128)S(1)} collective-permute-done((f32[256,128]{1,0:T(8,128)S(1)}, f32[256,128]{1,0:T(8,128)S(1)}, u32[]{:S(2)}, u32[]{:S(2)}) %collective-permute-start.22) | collective-permute-done | bytes 131104 | tf_op jit(solution)/shard_map/ppermute | solution.py:103
  59.4 1.1 %shard_map.124 = (bf16[256,1024]{1,0:T(8,128)(2,1)}, bf16[256,1024]{1,0:T(8,128)(2,1)}, f32[1024,128]{1,0:T(8,128)}) custom-call(f32[256,128]{1,0:T(8,128)S(1)} %collective-permute-done.19.refs_11_.refs_0_, f32[264,128]{1,0:T(8,128)S(1)} %collective-permute-done.20.refs_9_.refs_12_.refs_1_, ...), custom_call_target="tpu_custom_call", output_to_operand_aliasing={{0}: (11, {}), {1}: (12, {}), {2}: (13, {})} | custom-call | tf_op jit(solution)/shard_map/pallas_call | solution.py:25
  (32 shorter events, 0.3 us)
Async XLA Ops:
  2.8 8.0 %collective-permute-start = (f32[136,128]{1,0:T(8,128)S(1)}, f32[136,128]{1,0:T(8,128)S(1)}, u32[]{:S(2)}, u32[]{:S(2)}) collective-permute-start(f32[136,128]{1,0:T(8,128)S(1)} %get-tuple-element.59), channel_id=1, source_target_pairs={{0,12},{4,8},{8,4},{12,0},{16,28},{20,24},{24,20},{28,16},{1,13},{... | collective-permute-start | bytes 208904 | tf_op jit(solution)/shard_map/ppermute | solution.py:103
  6.9 5.1 %collective-permute-start.1 = (f32[136,128]{1,0:T(8,128)S(1)}, f32[136,128]{1,0:T(8,128)S(1)}, u32[]{:S(2)}, u32[]{:S(2)}) collective-permute-start(f32[136,128]{1,0:T(8,128)S(1)} %get-tuple-element.60), channel_id=1, source_target_pairs={{0,4},{4,0},{8,12},{12,8},{16,20},{20,16},{24,28},{28,24},{1,5},{5... | collective-permute-start | bytes 208904 | tf_op jit(solution)/shard_map/ppermute | solution.py:103
  7.4 4.6 %collective-permute-start.2 = (f32[136,128]{1,0:T(8,128)S(1)}, f32[136,128]{1,0:T(8,128)S(1)}, u32[]{:S(2)}, u32[]{:S(2)}) collective-permute-start(f32[136,128]{1,0:T(8,128)S(1)} %get-tuple-element.61), channel_id=1, source_target_pairs={{0,8},{4,12},{8,0},{12,4},{16,24},{20,28},{24,16},{28,20},{1,9},{5... | collective-permute-start | bytes 208904 | tf_op jit(solution)/shard_map/ppermute | solution.py:103
  7.5 7.2 %collective-permute-start.6 = (f32[128,128]{1,0:T(8,128)S(1)}, f32[128,128]{1,0:T(8,128)S(1)}, u32[]{:S(2)}, u32[]{:S(2)}) collective-permute-start(f32[128,128]{1,0:T(8,128)S(1)} %get-tuple-element.68), channel_id=1, source_target_pairs={{0,12},{4,8},{8,4},{12,0},{16,28},{20,24},{24,20},{28,16},{1,13},{... | collective-permute-start | bytes 196616 | tf_op jit(solution)/shard_map/ppermute | solution.py:103
  10.3 4.3 %collective-permute-start.7 = (f32[128,128]{1,0:T(8,128)S(1)}, f32[128,128]{1,0:T(8,128)S(1)}, u32[]{:S(2)}, u32[]{:S(2)}) collective-permute-start(f32[128,128]{1,0:T(8,128)S(1)} %get-tuple-element.69), channel_id=1, source_target_pairs={{0,4},{4,0},{8,12},{12,8},{16,20},{20,16},{24,28},{28,24},{1,5},{5... | collective-permute-start | bytes 196616 | tf_op jit(solution)/shard_map/ppermute | solution.py:103
  10.9 4.3 %collective-permute-start.8 = (f32[128,128]{1,0:T(8,128)S(1)}, f32[128,128]{1,0:T(8,128)S(1)}, u32[]{:S(2)}, u32[]{:S(2)}) collective-permute-start(f32[128,128]{1,0:T(8,128)S(1)} %get-tuple-element.70), channel_id=1, source_target_pairs={{0,8},{4,12},{8,0},{12,4},{16,24},{20,28},{24,16},{28,20},{1,9},{5... | collective-permute-start | bytes 196616 | tf_op jit(solution)/shard_map/ppermute | solution.py:103
  12.0 7.3 %collective-permute-start.3 = (f32[136,128]{1,0:T(8,128)S(1)}, f32[136,128]{1,0:T(8,128)S(1)}, u32[]{:S(2)}, u32[]{:S(2)}) collective-permute-start(f32[136,128]{1,0:T(8,128)S(1)} %get-tuple-element.62.refs_4_), channel_id=1, source_target_pairs={{0,16},{4,20},{8,24},{12,28},{16,0},{20,4},{24,8},{28,12},{1,17},{... | collective-permute-start | bytes 208904 | tf_op jit(solution)/shard_map/ppermute | solution.py:117
  15.2 4.2 %copy-start.3 = (f32[8,128,128]{2,1,0:T(8,128)S(1)}, f32[8,128,128]{2,1,0:T(8,128)}, u32[]{:S(2)}) copy-start(f32[8,128,128]{2,1,0:T(8,128)} %param.14) | copy-start | bytes 1572868
  15.2 10.4 %copy-start.5 = (bf16[256,1024]{1,0:T(8,128)(2,1)S(1)}, bf16[256,1024]{1,0:T(8,128)(2,1)}, u32[]{:S(2)}) copy-start(bf16[256,1024]{1,0:T(8,128)(2,1)} %upstream_ref.1) | copy-start | bytes 1572868
  15.3 5.7 %collective-permute-start.9 = (f32[128,128]{1,0:T(8,128)S(1)}, f32[128,128]{1,0:T(8,128)S(1)}, u32[]{:S(2)}, u32[]{:S(2)}) collective-permute-start(f32[128,128]{1,0:T(8,128)S(1)} %shard_map.114.refs_4_), channel_id=1, source_target_pairs={{0,16},{4,20},{8,24},{12,28},{16,0},{20,4},{24,8},{28,12},{1,17},{... | collective-permute-start | bytes 196616 | tf_op jit(solution)/shard_map/ppermute | solution.py:117
  19.4 6.3 %copy-start.1 = (bf16[256,1024]{1,0:T(8,128)(2,1)S(1)}, bf16[256,1024]{1,0:T(8,128)(2,1)}, u32[]{:S(2)}) copy-start(bf16[256,1024]{1,0:T(8,128)(2,1)} %key_ref.3) | copy-start | bytes 1572868
  19.4 6.3 %copy-start.2 = (bf16[256,1024]{1,0:T(8,128)(2,1)S(1)}, bf16[256,1024]{1,0:T(8,128)(2,1)}, u32[]{:S(2)}) copy-start(bf16[256,1024]{1,0:T(8,128)(2,1)} %value_ref.3) | copy-start | bytes 1572868
  19.5 6.2 %copy-start = (bf16[256,1024]{1,0:T(8,128)(2,1)S(1)}, bf16[256,1024]{1,0:T(8,128)(2,1)}, u32[]{:S(2)}) copy-start(bf16[256,1024]{1,0:T(8,128)(2,1)} %query_ref.3) | copy-start | bytes 1572868
  19.5 5.7 %collective-permute-start.4 = (f32[128,128]{1,0:T(8,128)S(1)}, f32[128,128]{1,0:T(8,128)S(1)}, u32[]{:S(2)}, u32[]{:S(2)}) collective-permute-start(f32[128,128]{1,0:T(8,128)S(1)} %get-tuple-element.65), channel_id=1, source_target_pairs={{0,4},{4,0},{8,12},{12,8},{16,20},{20,16},{24,28},{28,24},{1,5},{5... | collective-permute-start | bytes 196616 | tf_op jit(solution)/shard_map/ppermute | solution.py:103
  20.6 5.0 %collective-permute-start.5 = (f32[128,128]{1,0:T(8,128)S(1)}, f32[128,128]{1,0:T(8,128)S(1)}, u32[]{:S(2)}, u32[]{:S(2)}) collective-permute-start(f32[128,128]{1,0:T(8,128)S(1)} %get-tuple-element.66), channel_id=1, source_target_pairs={{0,8},{4,12},{8,0},{12,4},{16,24},{20,28},{24,16},{28,20},{1,9},{5... | collective-permute-start | bytes 196616 | tf_op jit(solution)/shard_map/ppermute | solution.py:103
  21.1 7.5 %collective-permute-start.12 = (f32[256,128]{1,0:T(8,128)S(1)}, f32[256,128]{1,0:T(8,128)S(1)}, u32[]{:S(2)}, u32[]{:S(2)}) collective-permute-start(f32[256,128]{1,0:T(8,128)S(1)} %get-tuple-element.76), channel_id=1, source_target_pairs={{0,12},{4,8},{8,4},{12,0},{16,28},{20,24},{24,20},{28,16},{1,13},{... | collective-permute-start | bytes 393224 | tf_op jit(solution)/shard_map/ppermute | solution.py:103
  23.2 2.5 %copy-start.6 = (f32[1024]{0:T(1024)S(1)}, f32[1024]{0:T(1024)}, u32[]{:S(2)}) copy-start(f32[1024]{0:T(1024)} %param.13) | copy-start | bytes 12292
  23.2 4.9 %collective-permute-start.10 = (f32[128,128]{1,0:T(8,128)S(1)}, f32[128,128]{1,0:T(8,128)S(1)}, u32[]{:S(2)}, u32[]{:S(2)}) collective-permute-start(f32[128,128]{1,0:T(8,128)S(1)} %get-tuple-element.74), channel_id=1, source_target_pairs={{0,4},{4,0},{8,12},{12,8},{16,20},{20,16},{24,28},{28,24},{1,5},{5... | collective-permute-start | bytes 196616 | tf_op jit(solution)/shard_map/ppermute | solution.py:103
  24.3 4.3 %collective-permute-start.11 = (f32[128,128]{1,0:T(8,128)S(1)}, f32[128,128]{1,0:T(8,128)S(1)}, u32[]{:S(2)}, u32[]{:S(2)}) collective-permute-start(f32[128,128]{1,0:T(8,128)S(1)} %get-tuple-element.75), channel_id=1, source_target_pairs={{0,8},{4,12},{8,0},{12,4},{16,24},{20,28},{24,16},{28,20},{1,9},{5... | collective-permute-start | bytes 196616 | tf_op jit(solution)/shard_map/ppermute | solution.py:103
  29.2 1.8 %collective-permute-start.15 = (f32[8,256]{1,0:T(8,128)S(1)}, f32[8,256]{1,0:T(8,128)S(1)}, u32[]{:S(2)}, u32[]{:S(2)}) collective-permute-start(f32[8,256]{1,0:T(8,128)S(1)} %get-tuple-element.81.refs_0_), channel_id=1, source_target_pairs={{0,3},{1,0},{2,1},{3,2},{4,7},{5,4},{6,5},{7,6},{8,11},{9,8},{10,9... | collective-permute-start | bytes 24584 | tf_op jit(solution)/shard_map/ppermute | solution.py:577
  29.2 3.7 %collective-permute-start.14 = (f32[8,256]{1,0:T(8,128)S(1)}, f32[8,256]{1,0:T(8,128)S(1)}, u32[]{:S(2)}, u32[]{:S(2)}) collective-permute-start(f32[8,256]{1,0:T(8,128)S(1)} %get-tuple-element.81.refs_0_), channel_id=1, source_target_pairs={{0,2},{1,3},{2,0},{3,1},{4,6},{5,7},{6,4},{7,5},{8,10},{9,11},{10,... | collective-permute-start | bytes 24584 | tf_op jit(solution)/shard_map/ppermute | solution.py:577
  30.8 3.1 %collective-permute-start.13 = (f32[8,256]{1,0:T(8,128)S(1)}, f32[8,256]{1,0:T(8,128)S(1)}, u32[]{:S(2)}, u32[]{:S(2)}) collective-permute-start(f32[8,256]{1,0:T(8,128)S(1)} %get-tuple-element.81.refs_0_), channel_id=1, source_target_pairs={{0,1},{1,2},{2,3},{3,0},{4,5},{5,6},{6,7},{7,4},{8,9},{9,10},{10,1... | collective-permute-start | bytes 24584 | tf_op jit(solution)/shard_map/ppermute | solution.py:577
  34.6 7.0 %collective-permute-start.16 = (f32[256,128]{1,0:T(8,128)S(1)}, f32[256,128]{1,0:T(8,128)S(1)}, u32[]{:S(2)}, u32[]{:S(2)}) collective-permute-start(f32[256,128]{1,0:T(8,128)S(1)} %get-tuple-element.89), channel_id=1, source_target_pairs={{0,12},{4,8},{8,4},{12,0},{16,28},{20,24},{24,20},{28,16},{1,13},{... | collective-permute-start | bytes 393224 | tf_op jit(solution)/shard_map/ppermute | solution.py:103
  36.0 6.2 %collective-permute-start.17 = (f32[256,128]{1,0:T(8,128)S(1)}, f32[256,128]{1,0:T(8,128)S(1)}, u32[]{:S(2)}, u32[]{:S(2)}) collective-permute-start(f32[256,128]{1,0:T(8,128)S(1)} %get-tuple-element.90), channel_id=1, source_target_pairs={{0,4},{4,0},{8,12},{12,8},{16,20},{20,16},{24,28},{28,24},{1,5},{5... | collective-permute-start | bytes 393224 | tf_op jit(solution)/shard_map/ppermute | solution.py:103
  37.0 5.3 %collective-permute-start.18 = (f32[256,128]{1,0:T(8,128)S(1)}, f32[256,128]{1,0:T(8,128)S(1)}, u32[]{:S(2)}, u32[]{:S(2)}) collective-permute-start(f32[256,128]{1,0:T(8,128)S(1)} %get-tuple-element.91), channel_id=1, source_target_pairs={{0,8},{4,12},{8,0},{12,4},{16,24},{20,28},{24,16},{28,20},{1,9},{5... | collective-permute-start | bytes 393224 | tf_op jit(solution)/shard_map/ppermute | solution.py:103
  38.2 4.1 %copy-start.4 = (f32[8,128,128]{2,1,0:T(8,128)S(1)}, f32[8,128,128]{2,1,0:T(8,128)}, u32[]{:S(2)}) copy-start(f32[8,128,128]{2,1,0:T(8,128)} %param.15) | copy-start | bytes 1572868
  42.4 7.1 %collective-permute-start.20 = (f32[264,128]{1,0:T(8,128)S(1)}, f32[264,128]{1,0:T(8,128)S(1)}, u32[]{:S(2)}, u32[]{:S(2)}) collective-permute-start(f32[264,128]{1,0:T(8,128)S(1)} %get-tuple-element.94), channel_id=1, source_target_pairs={{0,8},{4,12},{8,0},{12,4},{16,24},{20,28},{24,16},{28,20},{1,9},{5... | collective-permute-start | bytes 405512 | tf_op jit(solution)/shard_map/ppermute | solution.py:103
  43.5 6.0 %collective-permute-start.21 = (f32[256,128]{1,0:T(8,128)S(1)}, f32[256,128]{1,0:T(8,128)S(1)}, u32[]{:S(2)}, u32[]{:S(2)}) collective-permute-start(f32[256,128]{1,0:T(8,128)S(1)} %shard_map.121.refs_4_), channel_id=1, source_target_pairs={{0,16},{4,20},{8,24},{12,28},{16,0},{20,4},{24,8},{28,12},{1,17},{... | collective-permute-start | bytes 393224 | tf_op jit(solution)/shard_map/ppermute | solution.py:117
  46.3 9.8 %collective-permute-start.19 = (f32[256,128]{1,0:T(8,128)S(1)}, f32[256,128]{1,0:T(8,128)S(1)}, u32[]{:S(2)}, u32[]{:S(2)}) collective-permute-start(f32[256,128]{1,0:T(8,128)S(1)} %get-tuple-element.93), channel_id=1, source_target_pairs={{0,4},{4,0},{8,12},{12,8},{16,20},{20,16},{24,28},{28,24},{1,5},{5... | collective-permute-start | bytes 393224 | tf_op jit(solution)/shard_map/ppermute | solution.py:103
  47.4 8.7 %collective-permute-start.24 = (f32[256,128]{1,0:T(8,128)S(1)}, f32[256,128]{1,0:T(8,128)S(1)}, u32[]{:S(2)}, u32[]{:S(2)}) collective-permute-start(f32[256,128]{1,0:T(8,128)S(1)} %get-tuple-element.103), channel_id=1, source_target_pairs={{0,12},{4,8},{8,4},{12,0},{16,28},{20,24},{24,20},{28,16},{1,13},{... | collective-permute-start | bytes 393224 | tf_op jit(solution)/shard_map/ppermute | solution.py:103
  49.8 7.6 %collective-permute-start.25 = (f32[256,128]{1,0:T(8,128)S(1)}, f32[256,128]{1,0:T(8,128)S(1)}, u32[]{:S(2)}, u32[]{:S(2)}) collective-permute-start(f32[256,128]{1,0:T(8,128)S(1)} %get-tuple-element.105), channel_id=1, source_target_pairs={{0,12},{4,8},{8,4},{12,0},{16,28},{20,24},{24,20},{28,16},{1,13},{... | collective-permute-start | bytes 393224 | tf_op jit(solution)/shard_map/ppermute | solution.py:103
  54.4 5.0 %collective-permute-start.22 = (f32[256,128]{1,0:T(8,128)S(1)}, f32[256,128]{1,0:T(8,128)S(1)}, u32[]{:S(2)}, u32[]{:S(2)}) collective-permute-start(f32[256,128]{1,0:T(8,128)S(1)} %get-tuple-element.96), channel_id=1, source_target_pairs={{0,4},{4,0},{8,12},{12,8},{16,20},{20,16},{24,28},{28,24},{1,5},{5... | collective-permute-start | bytes 393224 | tf_op jit(solution)/shard_map/ppermute | solution.py:103
  54.4 5.0 %collective-permute-start.23 = (f32[256,128]{1,0:T(8,128)S(1)}, f32[256,128]{1,0:T(8,128)S(1)}, u32[]{:S(2)}, u32[]{:S(2)}) collective-permute-start(f32[256,128]{1,0:T(8,128)S(1)} %get-tuple-element.97), channel_id=1, source_target_pairs={{0,8},{4,12},{8,0},{12,4},{16,24},{20,28},{24,16},{28,20},{1,9},{5... | collective-permute-start | bytes 393224 | tf_op jit(solution)/shard_map/ppermute | solution.py:103

commit v12 on v11

--- a/solution.py
+++ b/solution.py
@@ -76,7 +76,7 @@
         self.near = [way for way in range(self.members) if way.bit_count() == 1]
         self.far = [way for way in range(self.members) if way.bit_count() > 1]
         self.ways = [0] + self.far + self.near
-        self.early_ways = [0] + self.near[::-1] + self.far
+        self.early_ways = [0] + self.far + self.near[::-1]
 
     def member(self):
         return lax.rem(lax.axis_index("seq"), self.members)
@@ -408,8 +408,7 @@
     query_grad_ref,
     key_part_ref,
     value_part_ref,
-    key_decayed_ref,
-    value_decayed_ref,
+    shrink_ref,
 ):
     length = query_ref.shape[0]
     causal = causal_mask(length)
@@ -426,15 +425,14 @@
         query_grad_ref[:, cut] = query_grad.astype(BF16)
         key_part_ref[:, cut] = dot(score_grad, query_ref[:, cut], CONTRACT_ROWS)
         value_part_ref[:, cut] = dot(weight_ref[h], attn_grad, CONTRACT_ROWS)
-        column = shrink[:, h : h + 1]
-        key_decayed_ref[:, cut] = (key_ref[:, cut].astype(F32) * column).astype(BF16)
-        value_decayed_ref[:, cut] = (value_ref[:, cut].astype(F32) * column).astype(BF16)
+        shrink_ref[h] = jnp.broadcast_to(shrink[:, h : h + 1], (length, plan.size))
 
 
 def finish_body(plan, ways, *refs):
     early_refs, refs = refs[: len(ways)], refs[len(ways) :]
     late_refs, refs = refs[: len(ways)], refs[len(ways) :]
-    key_part_ref, value_part_ref, key_ref, value_ref, summary_ref, before_ref, logs_ref = refs[:7]
+    key_part_ref, value_part_ref, key_ref, value_ref, shrink_ref = refs[:5]
+    summary_ref, before_ref, logs_ref = refs[5:8]
     key_out, value_out, total_out, key_grad_ref, value_grad_ref, total_ref, sems = refs[-7:]
     size, rows = plan.size, plan.rows
     first = plan.group() == 0
@@ -457,9 +455,9 @@
             )
             grads = grads.astype(BF16)
             key_state = dot(value_ref[:, part], grads, CONTRACT_COLS)
-            key_grad_ref[:, cut] = (key_part_ref[:, part] + key_state).astype(BF16)
+            key_grad_ref[:, cut] = (key_part_ref[:, part] + shrink_ref[head] * key_state).astype(BF16)
             value_state = dot(key_ref[:, part], grads)
-            value_grad_ref[:, cut] = (value_part_ref[:, part] + value_state).astype(BF16)
+            value_grad_ref[:, cut] = (value_part_ref[:, part] + shrink_ref[head] * value_state).astype(BF16)
         done, place = lanes(i, rows), plan.rows_of(owner)
         for source, target in [
             (total_ref.at[done], total_out.at[place]),
@@ -583,9 +581,9 @@
         [*all_sums, attended, query_decayed, gained],
     )
     parts = plan.swap_in_group(sends)
-    query_grad, key_part, value_part, key_decayed, value_decayed = call(
+    query_grad, key_part, value_part, shrink = call(
         bind(score_grad_body),
-        [rounded, table, table, rounded, rounded],
+        [rounded, table, table, shaped((heads, length, size))],
         [attn_grad, query_rows, key_rows, value_rows, states, weights, cum_log, cum_col],
         flops=10 * heads * length * length * size,
     )
@@ -621,21 +619,20 @@
         pieces_back = plan.swap_in_group(sends[first : first + plan.members])
         swapped.append(dict(zip(plan.ways, pieces_back)))
     outs = []
-    for ways in ([0] + plan.far, plan.near):
+    for ways in ([0], plan.far + plan.near):
         if not ways:
             continue
         operands = [
             *[pieces_back[way] for pieces_back in swapped for way in ways],
             key_part,
             value_part,
-            key_decayed,
-            value_decayed,
+            key_rows,
+            value_rows,
+            shrink,
             summary,
             before,
             logs,
         ]
-        if two_sided and not outs:
-            outs = [swapped[0][way] for way in plan.near]
         count = len(operands)
         outs = call(
             bind(finish_body, ways),
@@ -647,9 +644,9 @@
                 pltpu.VMEM((len(ways) * plan.rows, size), F32),
                 pltpu.SemaphoreType.DMA((3 * len(ways),)),
             ],
-            specs=[VMEM] * count + [ANY] * len(outs),
+            specs=[VMEM] * count + [HBM] * len(outs),
             out_specs=[HBM] * 3,
-            aliases={count + i: i for i in range(3)} if len(outs) == 3 else None,
+            aliases={count + i: i for i in range(len(outs))},
         )
     key_grad, value_grad, state_in_grad = outs
     return (query_grad, key_grad, value_grad, state_in_grad.reshape(heads, size, size))

time: 60.7 us -> 62.5 us (1.030)
  waiting for transfers between devices: 12.4 us -> 14.6 us
    ppermute x20, waiting for transfers between devices: 7.32 us -> 8.75 us  [swap(): return lax.ppermute(piece, 'seq', pairs) if way else piece]
    ppermute x3, waiting for transfers between devices: 2.25 us -> 3 us  [from_groups(): lax.ppermute(piece, 'seq', [(i, (i + step * self.members) % self.blocks)...]
  transfers between devices with their start and end apart: 26 -> 26, of which waited for: 14 -> 15; matrix products, arithmetic and copies ran while one was open for 0% -> 0% of each run, Pallas kernels for 11% -> 10%
where the time goes in v12:
time: 62.5 us; the launch traced here: 62.3 us
  starting transfers between devices  35.5 us (57%)
  waiting for transfers between devices  14.6 us (23%)
  Pallas kernels  11.3 us (18%)
  between operations  0.77 us (1%)
    ppermute x20, starting transfers between devices, swap(): return lax.ppermute(piece, 'seq', pairs) if way else piece  25.7 us
    pallas_call x14, Pallas kernels, call(): pl.pallas_call(body, out_shape=outs, in_specs=specs or [VMEM] * len(opera...  11.3 us
    ppermute x20, waiting for transfers between devices, swap(): return lax.ppermute(piece, 'seq', pairs) if way else piece  8.75 us
    ppermute x3, starting transfers between devices, from_groups(): lax.ppermute(piece, 'seq', [(i, (i + step * self.members) % self.blocks)...  8.04 us
    ppermute x3, waiting for transfers between devices, from_groups(): lax.ppermute(piece, 'seq', [(i, (i + step * self.members) % self.blocks)...  3 us
    ppermute x3, waiting for transfers between devices, on_device(): lax.ppermute(sums, 'head', [(i, (i + step) % parties) for i in range(part...  2.85 us
    ppermute x3, starting transfers between devices, on_device(): lax.ppermute(sums, 'head', [(i, (i + step) % parties) for i in range(part...  1.8 us
  transfers between devices with their start and end apart: 26, of which 15 were waited for; matrix products, arithmetic and copies ran while one was open for 0% of the time, Pallas kernels for 10%

profile of v12, /device:TPU:0, one launch (start us, length us, event | category | flops | bytes accessed | tf_op | source)
XLA Modules:
  0.0 62.3 jit_solution(8409158642788362352)
XLA Ops:
  0.6 2.2 %shard_map.111 = (f32[136,128]{1,0:T(8,128)S(1)}, f32[136,128]{1,0:T(8,128)S(1)}, f32[136,128]{1,0:T(8,128)S(1)}, f32[136,128]{1,0:T(8,128)S(1)}, f32[128,128]{1...) custom-call(bf16[256,1024]{1,0:T(8,128)(2,1)} %refs_8_.3, ...), custom_call_target="tpu_custom_call" | custom-call | tf_op jit(solution)/shard_map/pallas_call | solution.py:25
  2.8 4.0 %collective-permute-start = (f32[136,128]{1,0:T(8,128)S(1)}, f32[136,128]{1,0:T(8,128)S(1)}, u32[]{:S(2)}, u32[]{:S(2)}) collective-permute-start(f32[136,128]{1,0:T(8,128)S(1)} %get-tuple-element.58), channel_id=1, source_target_pairs={{0,12},{4,8},{8,4},{12,0},{16,28},{20,24},{24,20},{28,16},{1,13},{... | collective-permute-start | bytes 208904 | tf_op jit(solution)/shard_map/ppermute | solution.py:103
  6.9 0.5 collective-permute-start.1
  7.4 0.1 collective-permute-start.2
  7.5 2.8 %collective-permute-start.6 = (f32[128,128]{1,0:T(8,128)S(1)}, f32[128,128]{1,0:T(8,128)S(1)}, u32[]{:S(2)}, u32[]{:S(2)}) collective-permute-start(f32[128,128]{1,0:T(8,128)S(1)} %get-tuple-element.67), channel_id=1, source_target_pairs={{0,12},{4,8},{8,4},{12,0},{16,28},{20,24},{24,20},{28,16},{1,13},{... | collective-permute-start | bytes 196616 | tf_op jit(solution)/shard_map/ppermute | solution.py:103
  10.3 0.5 collective-permute-start.7
  10.9 0.8 %collective-permute-start.8 = (f32[128,128]{1,0:T(8,128)S(1)}, f32[128,128]{1,0:T(8,128)S(1)}, u32[]{:S(2)}, u32[]{:S(2)}) collective-permute-start(f32[128,128]{1,0:T(8,128)S(1)} %get-tuple-element.69), channel_id=1, source_target_pairs={{0,8},{4,12},{8,0},{12,4},{16,24},{20,28},{24,16},{28,20},{1,9},{5... | collective-permute-start | bytes 196616 | tf_op jit(solution)/shard_map/ppermute | solution.py:103
  11.6 0.4 collective-permute-done.1.refs_2_
  12.0 2.7 %collective-permute-start.3 = (f32[136,128]{1,0:T(8,128)S(1)}, f32[136,128]{1,0:T(8,128)S(1)}, u32[]{:S(2)}, u32[]{:S(2)}) collective-permute-start(f32[136,128]{1,0:T(8,128)S(1)} %get-tuple-element.61.refs_4_), channel_id=1, source_target_pairs={{0,16},{4,20},{8,24},{12,28},{16,0},{20,4},{24,8},{28,12},{1,17},{... | collective-permute-start | bytes 208904 | tf_op jit(solution)/shard_map/ppermute | solution.py:117
  14.7 0.5 collective-permute-done.8.refs_3_
  15.3 2.6 %collective-permute-start.9 = (f32[128,128]{1,0:T(8,128)S(1)}, f32[128,128]{1,0:T(8,128)S(1)}, u32[]{:S(2)}, u32[]{:S(2)}) collective-permute-start(f32[128,128]{1,0:T(8,128)S(1)} %shard_map.114.refs_4_), channel_id=1, source_target_pairs={{0,16},{4,20},{8,24},{12,28},{16,0},{20,4},{24,8},{28,12},{1,17},{... | collective-permute-start | bytes 196616 | tf_op jit(solution)/shard_map/ppermute | solution.py:117
  17.8 1.5 %collective-permute-done.3.refs_5_ = f32[136,128]{1,0:T(8,128)S(1)} collective-permute-done((f32[136,128]{1,0:T(8,128)S(1)}, f32[136,128]{1,0:T(8,128)S(1)}, u32[]{:S(2)}, u32[]{:S(2)}) %collective-permute-start.3) | collective-permute-done | bytes 69664 | tf_op jit(solution)/shard_map/ppermute | solution.py:117
  19.5 1.1 %collective-permute-start.4 = (f32[128,128]{1,0:T(8,128)S(1)}, f32[128,128]{1,0:T(8,128)S(1)}, u32[]{:S(2)}, u32[]{:S(2)}) collective-permute-start(f32[128,128]{1,0:T(8,128)S(1)} %get-tuple-element.64), channel_id=1, source_target_pairs={{0,4},{4,0},{8,12},{12,8},{16,20},{20,16},{24,28},{28,24},{1,5},{5... | collective-permute-start | bytes 196616 | tf_op jit(solution)/shard_map/ppermute | solution.py:103
  20.6 0.3 collective-permute-start.5
  21.1 2.1 %collective-permute-start.12 = (f32[256,128]{1,0:T(8,128)S(1)}, f32[256,128]{1,0:T(8,128)S(1)}, u32[]{:S(2)}, u32[]{:S(2)}) collective-permute-start(f32[256,128]{1,0:T(8,128)S(1)} %get-tuple-element.75), channel_id=1, source_target_pairs={{0,12},{4,8},{8,4},{12,0},{16,28},{20,24},{24,20},{28,16},{1,13},{... | collective-permute-start | bytes 393224 | tf_op jit(solution)/shard_map/ppermute | solution.py:103
  23.2 1.1 %collective-permute-start.10 = (f32[128,128]{1,0:T(8,128)S(1)}, f32[128,128]{1,0:T(8,128)S(1)}, u32[]{:S(2)}, u32[]{:S(2)}) collective-permute-start(f32[128,128]{1,0:T(8,128)S(1)} %get-tuple-element.73), channel_id=1, source_target_pairs={{0,4},{4,0},{8,12},{12,8},{16,20},{20,16},{24,28},{28,24},{1,5},{5... | collective-permute-start | bytes 196616 | tf_op jit(solution)/shard_map/ppermute | solution.py:103
  24.3 0.3 collective-permute-start.11
  24.6 0.6 collective-permute-done.4.refs_0_.refs_1_
  25.2 0.4 collective-permute-done.5.refs_1_.refs_2_
  25.7 1.2 %shard_map.116 = (bf16[8,256,256]{2,1,0:T(8,128)(2,1)S(1)}, f32[256,1024]{1,0:T(8,128)S(1)}, f32[256,1024]{1,0:T(8,128)S(1)}, bf16[8,128,256]{2,1,0:T(8,128)(2,1)S(1)}) custom-call(bf16[256,1024]{1,0:T(8,128)(2,1)S(1)} %copy-done.2, bf16[256,1024]{1,0:T(8,128)(2,1)S(1)} %copy-done, bf16[256,1024]{1,0:T(8,128)(2,1)S(1)} %copy-done.1, ...), custom_call_target="tpu_custom_call" | custom-call | flops 1000000000 | tf_op jit(solution)/shard_map/pallas_call | solution.py:25
  26.9 1.2 %collective-permute-done.10.refs_4_ = f32[128,128]{1,0:T(8,128)S(1)} collective-permute-done((f32[128,128]{1,0:T(8,128)S(1)}, f32[128,128]{1,0:T(8,128)S(1)}, u32[]{:S(2)}, u32[]{:S(2)}) %collective-permute-start.10) | collective-permute-done | bytes 65568 | tf_op jit(solution)/shard_map/ppermute | solution.py:103
  28.1 0.4 collective-permute-done.11.refs_5_
  28.5 0.7 %shard_map.117 = (f32[256,1024]{1,0:T(8,128)S(1)}, f32[8,256]{1,0:T(8,128)S(1)}, bf16[1024,128]{1,0:T(8,128)(2,1)S(1)}) custom-call(f32[128,128]{1,0:T(8,128)S(1)} %get-tuple-element.63.refs_0_, f32[128,128]{1,0:T(8,128)S(1)} %collective-permute-done.4.refs_0_.refs_1_, f32[128,128]{1,0:T(8,128)S(1)} %collective-permute-done.5.refs_1_.refs_2_, ...), custom_call_target="tpu_custom_call" | custom-call | tf_op jit(solution)/shard_map/pallas_call | solution.py:25
  29.2 1.6 %collective-permute-start.14 = (f32[8,256]{1,0:T(8,128)S(1)}, f32[8,256]{1,0:T(8,128)S(1)}, u32[]{:S(2)}, u32[]{:S(2)}) collective-permute-start(f32[8,256]{1,0:T(8,128)S(1)} %get-tuple-element.80.refs_0_), channel_id=1, source_target_pairs={{0,2},{1,3},{2,0},{3,1},{4,6},{5,7},{6,4},{7,5},{8,10},{9,11},{10,... | collective-permute-start | bytes 24584 | tf_op jit(solution)/shard_map/ppermute | solution.py:575
  30.8 0.2 collective-permute-start.13
  31.0 1.9 %collective-permute-done.14.refs_2_ = f32[8,256]{1,0:T(8,128)S(1)} collective-permute-done((f32[8,256]{1,0:T(8,128)S(1)}, f32[8,256]{1,0:T(8,128)S(1)}, u32[]{:S(2)}, u32[]{:S(2)}) %collective-permute-start.14) | collective-permute-done | bytes 8224 | tf_op jit(solution)/shard_map/ppermute | solution.py:575
  32.9 1.0 %collective-permute-done.13.refs_1_ = f32[8,256]{1,0:T(8,128)S(1)} collective-permute-done((f32[8,256]{1,0:T(8,128)S(1)}, f32[8,256]{1,0:T(8,128)S(1)}, u32[]{:S(2)}, u32[]{:S(2)}) %collective-permute-start.13) | collective-permute-done | bytes 8224 | tf_op jit(solution)/shard_map/ppermute | solution.py:575
  33.9 0.7 %shard_map.118 = (bf16[256,1024]{1,0:T(8,128)(2,1)S(1)}, f32[1024,128]{1,0:T(8,128)S(1)}, f32[256,128]{1,0:T(8,128)S(1)}, f32[256,128]{1,0:T(8,128)S(1)}, f32[25...) custom-call(f32[8,256]{1,0:T(8,128)S(1)} %get-tuple-element.80.refs_0_, f32[8,256]{1,0:T(8,128)S(1)} %collective-permute-done.13.refs_1_, ...), custom_call_target="tpu_custom_call" | custom-call | tf_op jit(solution)/shard_map/pallas_call | solution.py:25
  34.6 1.4 %collective-permute-start.16 = (f32[256,128]{1,0:T(8,128)S(1)}, f32[256,128]{1,0:T(8,128)S(1)}, u32[]{:S(2)}, u32[]{:S(2)}) collective-permute-start(f32[256,128]{1,0:T(8,128)S(1)} %get-tuple-element.88), channel_id=1, source_target_pairs={{0,12},{4,8},{8,4},{12,0},{16,28},{20,24},{24,20},{28,16},{1,13},{... | collective-permute-start | bytes 393224 | tf_op jit(solution)/shard_map/ppermute | solution.py:103
  36.0 0.9 %collective-permute-start.17 = (f32[256,128]{1,0:T(8,128)S(1)}, f32[256,128]{1,0:T(8,128)S(1)}, u32[]{:S(2)}, u32[]{:S(2)}) collective-permute-start(f32[256,128]{1,0:T(8,128)S(1)} %get-tuple-element.89), channel_id=1, source_target_pairs={{0,4},{4,0},{8,12},{12,8},{16,20},{20,16},{24,28},{28,24},{1,5},{5... | collective-permute-start | bytes 393224 | tf_op jit(solution)/shard_map/ppermute | solution.py:103
  37.0 1.2 %collective-permute-start.18 = (f32[256,128]{1,0:T(8,128)S(1)}, f32[256,128]{1,0:T(8,128)S(1)}, u32[]{:S(2)}, u32[]{:S(2)}) collective-permute-start(f32[256,128]{1,0:T(8,128)S(1)} %get-tuple-element.90), channel_id=1, source_target_pairs={{0,8},{4,12},{8,0},{12,4},{16,24},{20,28},{24,16},{28,20},{1,9},{5... | collective-permute-start | bytes 393224 | tf_op jit(solution)/shard_map/ppermute | solution.py:103
  38.1 3.4 %shard_map.119 = (bf16[256,1024]{1,0:T(8,128)(2,1)}, f32[256,1024]{1,0:T(8,128)S(1)}, f32[256,1024]{1,0:T(8,128)S(1)}, f32[8,256,128]{2,1,0:T(8,128)S(1)}) custom-call(bf16[256,1024]{1,0:T(8,128)(2,1)S(1)} %get-tuple-element.83.attn_grad_ref, bf16[256,1024]{1,0:T(8,128)(2,1)S(1)} %copy-done.2, bf16[256,1024]{1,0:T(8,128)(2,1)S(1)} %copy-done, ...), custom_call_target="tpu_custom_call" | custom-call | flops 671088640 | tf_op jit(solution)/shard_map/pallas_call | solution.py:25
  41.5 0.7 %collective-permute-done.17.refs_2_ = f32[256,128]{1,0:T(8,128)S(1)} collective-permute-done((f32[256,128]{1,0:T(8,128)S(1)}, f32[256,128]{1,0:T(8,128)S(1)}, u32[]{:S(2)}, u32[]{:S(2)}) %collective-permute-start.17) | collective-permute-done | bytes 131104 | tf_op jit(solution)/shard_map/ppermute | solution.py:103
  42.2 0.2 shard_map.120
  42.4 1.5 %collective-permute-start.19 = (f32[264,128]{1,0:T(8,128)S(1)}, f32[264,128]{1,0:T(8,128)S(1)}, u32[]{:S(2)}, u32[]{:S(2)}) collective-permute-start(f32[264,128]{1,0:T(8,128)S(1)} %get-tuple-element.92), channel_id=1, source_target_pairs={{0,12},{4,8},{8,4},{12,0},{16,28},{20,24},{24,20},{28,16},{1,13},{... | collective-permute-start | bytes 405512 | tf_op jit(solution)/shard_map/ppermute | solution.py:103
  44.0 2.8 %collective-permute-start.22 = (f32[256,128]{1,0:T(8,128)S(1)}, f32[256,128]{1,0:T(8,128)S(1)}, u32[]{:S(2)}, u32[]{:S(2)}) collective-permute-start(f32[256,128]{1,0:T(8,128)S(1)} %shard_map.121.refs_4_), channel_id=1, source_target_pairs={{0,16},{4,20},{8,24},{12,28},{16,0},{20,4},{24,8},{28,12},{1,17},{... | collective-permute-start | bytes 393224 | tf_op jit(solution)/shard_map/ppermute | solution.py:117
  46.8 1.0 %collective-permute-start.20 = (f32[256,128]{1,0:T(8,128)S(1)}, f32[256,128]{1,0:T(8,128)S(1)}, u32[]{:S(2)}, u32[]{:S(2)}) collective-permute-start(f32[256,128]{1,0:T(8,128)S(1)} %get-tuple-element.93), channel_id=1, source_target_pairs={{0,4},{4,0},{8,12},{12,8},{16,20},{20,16},{24,28},{28,24},{1,5},{5... | collective-permute-start | bytes 393224 | tf_op jit(solution)/shard_map/ppermute | solution.py:103
  47.8 1.0 %collective-permute-start.21 = (f32[256,128]{1,0:T(8,128)S(1)}, f32[256,128]{1,0:T(8,128)S(1)}, u32[]{:S(2)}, u32[]{:S(2)}) collective-permute-start(f32[256,128]{1,0:T(8,128)S(1)} %get-tuple-element.94), channel_id=1, source_target_pairs={{0,8},{4,12},{8,0},{12,4},{16,24},{20,28},{24,16},{28,20},{1,9},{5... | collective-permute-start | bytes 393224 | tf_op jit(solution)/shard_map/ppermute | solution.py:103
  48.8 1.5 %collective-permute-done.22.refs_5_ = f32[256,128]{1,0:T(8,128)S(1)} collective-permute-done((f32[256,128]{1,0:T(8,128)S(1)}, f32[256,128]{1,0:T(8,128)S(1)}, u32[]{:S(2)}, u32[]{:S(2)}) %collective-permute-start.22) | collective-permute-done | bytes 131104 | tf_op jit(solution)/shard_map/ppermute | solution.py:117
  50.3 0.5 collective-permute-done.19.refs_9_.refs_0_
  50.8 0.2 shard_map.122
  51.0 2.6 %collective-permute-start.23 = (f32[256,128]{1,0:T(8,128)S(1)}, f32[256,128]{1,0:T(8,128)S(1)}, u32[]{:S(2)}, u32[]{:S(2)}) collective-permute-start(f32[256,128]{1,0:T(8,128)S(1)} %get-tuple-element.96), channel_id=1, source_target_pairs={{0,12},{4,8},{8,4},{12,0},{16,28},{20,24},{24,20},{28,16},{1,13},{... | collective-permute-start | bytes 393224 | tf_op jit(solution)/shard_map/ppermute | solution.py:103
  53.7 2.2 %collective-permute-start.24 = (f32[256,128]{1,0:T(8,128)S(1)}, f32[256,128]{1,0:T(8,128)S(1)}, u32[]{:S(2)}, u32[]{:S(2)}) collective-permute-start(f32[256,128]{1,0:T(8,128)S(1)} %get-tuple-element.97), channel_id=1, source_target_pairs={{0,4},{4,0},{8,12},{12,8},{16,20},{20,16},{24,28},{28,24},{1,5},{5... | collective-permute-start | bytes 393224 | tf_op jit(solution)/shard_map/ppermute | solution.py:103
  55.9 1.0 %shard_map.123 = (bf16[256,1024]{1,0:T(8,128)(2,1)}, bf16[256,1024]{1,0:T(8,128)(2,1)}, f32[1024,128]{1,0:T(8,128)}) custom-call(f32[256,128]{1,0:T(8,128)S(1)} %get-tuple-element.95.refs_5_.refs_0_, f32[256,128]{1,0:T(8,128)S(1)} %get-tuple-element.103.refs_1_, f32[256,1024]{1,0:T(8,128)S(1)} %get-tuple-element.91.refs_6_.refs_2_, ...), custom_call_target="tpu_custom_call" | custom-call | tf_op jit(solution)/shard_map/pallas_call | solution.py:25
  56.9 0.1 collective-permute-done.23.refs_3_
  57.0 1.9 %collective-permute-done.24.refs_4_ = f32[256,128]{1,0:T(8,128)S(1)} collective-permute-done((f32[256,128]{1,0:T(8,128)S(1)}, f32[256,128]{1,0:T(8,128)S(1)}, u32[]{:S(2)}, u32[]{:S(2)}) %collective-permute-start.24) | collective-permute-done | bytes 131104 | tf_op jit(solution)/shard_map/ppermute | solution.py:103
  58.8 2.0 %collective-permute-done.25.refs_5_ = f32[256,128]{1,0:T(8,128)S(1)} collective-permute-done((f32[256,128]{1,0:T(8,128)S(1)}, f32[256,128]{1,0:T(8,128)S(1)}, u32[]{:S(2)}, u32[]{:S(2)}) %collective-permute-start.25) | collective-permute-done | bytes 131104 | tf_op jit(solution)/shard_map/ppermute | solution.py:103
  60.9 1.4 %shard_map.124 = (bf16[256,1024]{1,0:T(8,128)(2,1)}, bf16[256,1024]{1,0:T(8,128)(2,1)}, f32[1024,128]{1,0:T(8,128)}) custom-call(f32[264,128]{1,0:T(8,128)S(1)} %collective-permute-done.19.refs_9_.refs_0_, f32[256,128]{1,0:T(8,128)S(1)} %collective-permute-done.20.refs_1_, ...), custom_call_target="tpu_custom_call", output_to_operand_aliasing={{0}: (14, {}), {1}: (15, {}), {2}: (16, {})} | custom-call | tf_op jit(solution)/shard_map/pallas_call | solution.py:25
  (32 shorter events, 0.4 us)
Async XLA Ops:
  2.8 8.0 %collective-permute-start = (f32[136,128]{1,0:T(8,128)S(1)}, f32[136,128]{1,0:T(8,128)S(1)}, u32[]{:S(2)}, u32[]{:S(2)}) collective-permute-start(f32[136,128]{1,0:T(8,128)S(1)} %get-tuple-element.58), channel_id=1, source_target_pairs={{0,12},{4,8},{8,4},{12,0},{16,28},{20,24},{24,20},{28,16},{1,13},{... | collective-permute-start | bytes 208904 | tf_op jit(solution)/shard_map/ppermute | solution.py:103
  6.9 5.1 %collective-permute-start.1 = (f32[136,128]{1,0:T(8,128)S(1)}, f32[136,128]{1,0:T(8,128)S(1)}, u32[]{:S(2)}, u32[]{:S(2)}) collective-permute-start(f32[136,128]{1,0:T(8,128)S(1)} %get-tuple-element.59), channel_id=1, source_target_pairs={{0,4},{4,0},{8,12},{12,8},{16,20},{20,16},{24,28},{28,24},{1,5},{5... | collective-permute-start | bytes 208904 | tf_op jit(solution)/shard_map/ppermute | solution.py:103
  7.4 4.6 %collective-permute-start.2 = (f32[136,128]{1,0:T(8,128)S(1)}, f32[136,128]{1,0:T(8,128)S(1)}, u32[]{:S(2)}, u32[]{:S(2)}) collective-permute-start(f32[136,128]{1,0:T(8,128)S(1)} %get-tuple-element.60), channel_id=1, source_target_pairs={{0,8},{4,12},{8,0},{12,4},{16,24},{20,28},{24,16},{28,20},{1,9},{5... | collective-permute-start | bytes 208904 | tf_op jit(solution)/shard_map/ppermute | solution.py:103
  7.5 7.2 %collective-permute-start.6 = (f32[128,128]{1,0:T(8,128)S(1)}, f32[128,128]{1,0:T(8,128)S(1)}, u32[]{:S(2)}, u32[]{:S(2)}) collective-permute-start(f32[128,128]{1,0:T(8,128)S(1)} %get-tuple-element.67), channel_id=1, source_target_pairs={{0,12},{4,8},{8,4},{12,0},{16,28},{20,24},{24,20},{28,16},{1,13},{... | collective-permute-start | bytes 196616 | tf_op jit(solution)/shard_map/ppermute | solution.py:103
  10.3 4.3 %collective-permute-start.7 = (f32[128,128]{1,0:T(8,128)S(1)}, f32[128,128]{1,0:T(8,128)S(1)}, u32[]{:S(2)}, u32[]{:S(2)}) collective-permute-start(f32[128,128]{1,0:T(8,128)S(1)} %get-tuple-element.68), channel_id=1, source_target_pairs={{0,4},{4,0},{8,12},{12,8},{16,20},{20,16},{24,28},{28,24},{1,5},{5... | collective-permute-start | bytes 196616 | tf_op jit(solution)/shard_map/ppermute | solution.py:103
  10.9 4.3 %collective-permute-start.8 = (f32[128,128]{1,0:T(8,128)S(1)}, f32[128,128]{1,0:T(8,128)S(1)}, u32[]{:S(2)}, u32[]{:S(2)}) collective-permute-start(f32[128,128]{1,0:T(8,128)S(1)} %get-tuple-element.69), channel_id=1, source_target_pairs={{0,8},{4,12},{8,0},{12,4},{16,24},{20,28},{24,16},{28,20},{1,9},{5... | collective-permute-start | bytes 196616 | tf_op jit(solution)/shard_map/ppermute | solution.py:103
  12.0 7.3 %collective-permute-start.3 = (f32[136,128]{1,0:T(8,128)S(1)}, f32[136,128]{1,0:T(8,128)S(1)}, u32[]{:S(2)}, u32[]{:S(2)}) collective-permute-start(f32[136,128]{1,0:T(8,128)S(1)} %get-tuple-element.61.refs_4_), channel_id=1, source_target_pairs={{0,16},{4,20},{8,24},{12,28},{16,0},{20,4},{24,8},{28,12},{1,17},{... | collective-permute-start | bytes 208904 | tf_op jit(solution)/shard_map/ppermute | solution.py:117
  15.2 4.2 %copy-start.3 = (f32[8,128,128]{2,1,0:T(8,128)S(1)}, f32[8,128,128]{2,1,0:T(8,128)}, u32[]{:S(2)}) copy-start(f32[8,128,128]{2,1,0:T(8,128)} %param.14) | copy-start | bytes 1572868
  15.2 10.4 %copy-start.5 = (bf16[256,1024]{1,0:T(8,128)(2,1)S(1)}, bf16[256,1024]{1,0:T(8,128)(2,1)}, u32[]{:S(2)}) copy-start(bf16[256,1024]{1,0:T(8,128)(2,1)} %upstream_ref.1) | copy-start | bytes 1572868
  15.3 5.7 %collective-permute-start.9 = (f32[128,128]{1,0:T(8,128)S(1)}, f32[128,128]{1,0:T(8,128)S(1)}, u32[]{:S(2)}, u32[]{:S(2)}) collective-permute-start(f32[128,128]{1,0:T(8,128)S(1)} %shard_map.114.refs_4_), channel_id=1, source_target_pairs={{0,16},{4,20},{8,24},{12,28},{16,0},{20,4},{24,8},{28,12},{1,17},{... | collective-permute-start | bytes 196616 | tf_op jit(solution)/shard_map/ppermute | solution.py:117
  19.4 6.3 %copy-start.1 = (bf16[256,1024]{1,0:T(8,128)(2,1)S(1)}, bf16[256,1024]{1,0:T(8,128)(2,1)}, u32[]{:S(2)}) copy-start(bf16[256,1024]{1,0:T(8,128)(2,1)} %refs_9_.1) | copy-start | bytes 1572868
  19.4 6.3 %copy-start.2 = (bf16[256,1024]{1,0:T(8,128)(2,1)S(1)}, bf16[256,1024]{1,0:T(8,128)(2,1)}, u32[]{:S(2)}) copy-start(bf16[256,1024]{1,0:T(8,128)(2,1)} %query_ref.3) | copy-start | bytes 1572868
  19.5 6.2 %copy-start = (bf16[256,1024]{1,0:T(8,128)(2,1)S(1)}, bf16[256,1024]{1,0:T(8,128)(2,1)}, u32[]{:S(2)}) copy-start(bf16[256,1024]{1,0:T(8,128)(2,1)} %refs_8_.3) | copy-start | bytes 1572868
  19.5 5.7 %collective-permute-start.4 = (f32[128,128]{1,0:T(8,128)S(1)}, f32[128,128]{1,0:T(8,128)S(1)}, u32[]{:S(2)}, u32[]{:S(2)}) collective-permute-start(f32[128,128]{1,0:T(8,128)S(1)} %get-tuple-element.64), channel_id=1, source_target_pairs={{0,4},{4,0},{8,12},{12,8},{16,20},{20,16},{24,28},{28,24},{1,5},{5... | collective-permute-start | bytes 196616 | tf_op jit(solution)/shard_map/ppermute | solution.py:103
  20.6 5.0 %collective-permute-start.5 = (f32[128,128]{1,0:T(8,128)S(1)}, f32[128,128]{1,0:T(8,128)S(1)}, u32[]{:S(2)}, u32[]{:S(2)}) collective-permute-start(f32[128,128]{1,0:T(8,128)S(1)} %get-tuple-element.65), channel_id=1, source_target_pairs={{0,8},{4,12},{8,0},{12,4},{16,24},{20,28},{24,16},{28,20},{1,9},{5... | collective-permute-start | bytes 196616 | tf_op jit(solution)/shard_map/ppermute | solution.py:103
  21.1 7.5 %collective-permute-start.12 = (f32[256,128]{1,0:T(8,128)S(1)}, f32[256,128]{1,0:T(8,128)S(1)}, u32[]{:S(2)}, u32[]{:S(2)}) collective-permute-start(f32[256,128]{1,0:T(8,128)S(1)} %get-tuple-element.75), channel_id=1, source_target_pairs={{0,12},{4,8},{8,4},{12,0},{16,28},{20,24},{24,20},{28,16},{1,13},{... | collective-permute-start | bytes 393224 | tf_op jit(solution)/shard_map/ppermute | solution.py:103
  23.2 2.5 %copy-start.6 = (f32[1024]{0:T(1024)S(1)}, f32[1024]{0:T(1024)}, u32[]{:S(2)}) copy-start(f32[1024]{0:T(1024)} %param.13) | copy-start | bytes 12292
  23.2 4.9 %collective-permute-start.10 = (f32[128,128]{1,0:T(8,128)S(1)}, f32[128,128]{1,0:T(8,128)S(1)}, u32[]{:S(2)}, u32[]{:S(2)}) collective-permute-start(f32[128,128]{1,0:T(8,128)S(1)} %get-tuple-element.73), channel_id=1, source_target_pairs={{0,4},{4,0},{8,12},{12,8},{16,20},{20,16},{24,28},{28,24},{1,5},{5... | collective-permute-start | bytes 196616 | tf_op jit(solution)/shard_map/ppermute | solution.py:103
  24.3 4.3 %collective-permute-start.11 = (f32[128,128]{1,0:T(8,128)S(1)}, f32[128,128]{1,0:T(8,128)S(1)}, u32[]{:S(2)}, u32[]{:S(2)}) collective-permute-start(f32[128,128]{1,0:T(8,128)S(1)} %get-tuple-element.74), channel_id=1, source_target_pairs={{0,8},{4,12},{8,0},{12,4},{16,24},{20,28},{24,16},{28,20},{1,9},{5... | collective-permute-start | bytes 196616 | tf_op jit(solution)/shard_map/ppermute | solution.py:103
  29.2 1.8 %collective-permute-start.15 = (f32[8,256]{1,0:T(8,128)S(1)}, f32[8,256]{1,0:T(8,128)S(1)}, u32[]{:S(2)}, u32[]{:S(2)}) collective-permute-start(f32[8,256]{1,0:T(8,128)S(1)} %get-tuple-element.80.refs_0_), channel_id=1, source_target_pairs={{0,3},{1,0},{2,1},{3,2},{4,7},{5,4},{6,5},{7,6},{8,11},{9,8},{10,9... | collective-permute-start | bytes 24584 | tf_op jit(solution)/shard_map/ppermute | solution.py:575
  29.2 3.7 %collective-permute-start.14 = (f32[8,256]{1,0:T(8,128)S(1)}, f32[8,256]{1,0:T(8,128)S(1)}, u32[]{:S(2)}, u32[]{:S(2)}) collective-permute-start(f32[8,256]{1,0:T(8,128)S(1)} %get-tuple-element.80.refs_0_), channel_id=1, source_target_pairs={{0,2},{1,3},{2,0},{3,1},{4,6},{5,7},{6,4},{7,5},{8,10},{9,11},{10,... | collective-permute-start | bytes 24584 | tf_op jit(solution)/shard_map/ppermute | solution.py:575
  30.8 3.1 %collective-permute-start.13 = (f32[8,256]{1,0:T(8,128)S(1)}, f32[8,256]{1,0:T(8,128)S(1)}, u32[]{:S(2)}, u32[]{:S(2)}) collective-permute-start(f32[8,256]{1,0:T(8,128)S(1)} %get-tuple-element.80.refs_0_), channel_id=1, source_target_pairs={{0,1},{1,2},{2,3},{3,0},{4,5},{5,6},{6,7},{7,4},{8,9},{9,10},{10,1... | collective-permute-start | bytes 24584 | tf_op jit(solution)/shard_map/ppermute | solution.py:575
  34.6 6.9 %collective-permute-start.16 = (f32[256,128]{1,0:T(8,128)S(1)}, f32[256,128]{1,0:T(8,128)S(1)}, u32[]{:S(2)}, u32[]{:S(2)}) collective-permute-start(f32[256,128]{1,0:T(8,128)S(1)} %get-tuple-element.88), channel_id=1, source_target_pairs={{0,12},{4,8},{8,4},{12,0},{16,28},{20,24},{24,20},{28,16},{1,13},{... | collective-permute-start | bytes 393224 | tf_op jit(solution)/shard_map/ppermute | solution.py:103
  36.0 6.2 %collective-permute-start.17 = (f32[256,128]{1,0:T(8,128)S(1)}, f32[256,128]{1,0:T(8,128)S(1)}, u32[]{:S(2)}, u32[]{:S(2)}) collective-permute-start(f32[256,128]{1,0:T(8,128)S(1)} %get-tuple-element.89), channel_id=1, source_target_pairs={{0,4},{4,0},{8,12},{12,8},{16,20},{20,16},{24,28},{28,24},{1,5},{5... | collective-permute-start | bytes 393224 | tf_op jit(solution)/shard_map/ppermute | solution.py:103
  37.0 5.3 %collective-permute-start.18 = (f32[256,128]{1,0:T(8,128)S(1)}, f32[256,128]{1,0:T(8,128)S(1)}, u32[]{:S(2)}, u32[]{:S(2)}) collective-permute-start(f32[256,128]{1,0:T(8,128)S(1)} %get-tuple-element.90), channel_id=1, source_target_pairs={{0,8},{4,12},{8,0},{12,4},{16,24},{20,28},{24,16},{28,20},{1,9},{5... | collective-permute-start | bytes 393224 | tf_op jit(solution)/shard_map/ppermute | solution.py:103
  38.1 4.1 %copy-start.4 = (f32[8,128,128]{2,1,0:T(8,128)S(1)}, f32[8,128,128]{2,1,0:T(8,128)}, u32[]{:S(2)}) copy-start(f32[8,128,128]{2,1,0:T(8,128)} %param.15) | copy-start | bytes 1572868
  42.4 8.4 %collective-permute-start.19 = (f32[264,128]{1,0:T(8,128)S(1)}, f32[264,128]{1,0:T(8,128)S(1)}, u32[]{:S(2)}, u32[]{:S(2)}) collective-permute-start(f32[264,128]{1,0:T(8,128)S(1)} %get-tuple-element.92), channel_id=1, source_target_pairs={{0,12},{4,8},{8,4},{12,0},{16,28},{20,24},{24,20},{28,16},{1,13},{... | collective-permute-start | bytes 405512 | tf_op jit(solution)/shard_map/ppermute | solution.py:103
  44.0 6.3 %collective-permute-start.22 = (f32[256,128]{1,0:T(8,128)S(1)}, f32[256,128]{1,0:T(8,128)S(1)}, u32[]{:S(2)}, u32[]{:S(2)}) collective-permute-start(f32[256,128]{1,0:T(8,128)S(1)} %shard_map.121.refs_4_), channel_id=1, source_target_pairs={{0,16},{4,20},{8,24},{12,28},{16,0},{20,4},{24,8},{28,12},{1,17},{... | collective-permute-start | bytes 393224 | tf_op jit(solution)/shard_map/ppermute | solution.py:117
  46.8 10.1 %collective-permute-start.20 = (f32[256,128]{1,0:T(8,128)S(1)}, f32[256,128]{1,0:T(8,128)S(1)}, u32[]{:S(2)}, u32[]{:S(2)}) collective-permute-start(f32[256,128]{1,0:T(8,128)S(1)} %get-tuple-element.93), channel_id=1, source_target_pairs={{0,4},{4,0},{8,12},{12,8},{16,20},{20,16},{24,28},{28,24},{1,5},{5... | collective-permute-start | bytes 393224 | tf_op jit(solution)/shard_map/ppermute | solution.py:103
  47.8 9.1 %collective-permute-start.21 = (f32[256,128]{1,0:T(8,128)S(1)}, f32[256,128]{1,0:T(8,128)S(1)}, u32[]{:S(2)}, u32[]{:S(2)}) collective-permute-start(f32[256,128]{1,0:T(8,128)S(1)} %get-tuple-element.94), channel_id=1, source_target_pairs={{0,8},{4,12},{8,0},{12,4},{16,24},{20,28},{24,16},{28,20},{1,9},{5... | collective-permute-start | bytes 393224 | tf_op jit(solution)/shard_map/ppermute | solution.py:103
  51.0 5.9 %collective-permute-start.23 = (f32[256,128]{1,0:T(8,128)S(1)}, f32[256,128]{1,0:T(8,128)S(1)}, u32[]{:S(2)}, u32[]{:S(2)}) collective-permute-start(f32[256,128]{1,0:T(8,128)S(1)} %get-tuple-element.96), channel_id=1, source_target_pairs={{0,12},{4,8},{8,4},{12,0},{16,28},{20,24},{24,20},{28,16},{1,13},{... | collective-permute-start | bytes 393224 | tf_op jit(solution)/shard_map/ppermute | solution.py:103
  53.7 5.2 %collective-permute-start.24 = (f32[256,128]{1,0:T(8,128)S(1)}, f32[256,128]{1,0:T(8,128)S(1)}, u32[]{:S(2)}, u32[]{:S(2)}) collective-permute-start(f32[256,128]{1,0:T(8,128)S(1)} %get-tuple-element.97), channel_id=1, source_target_pairs={{0,4},{4,0},{8,12},{12,8},{16,20},{20,16},{24,28},{28,24},{1,5},{5... | collective-permute-start | bytes 393224 | tf_op jit(solution)/shard_map/ppermute | solution.py:103
  55.9 5.0 %collective-permute-start.25 = (f32[256,128]{1,0:T(8,128)S(1)}, f32[256,128]{1,0:T(8,128)S(1)}, u32[]{:S(2)}, u32[]{:S(2)}) collective-permute-start(f32[256,128]{1,0:T(8,128)S(1)} %get-tuple-element.98), channel_id=1, source_target_pairs={{0,8},{4,12},{8,0},{12,4},{16,24},{20,28},{24,16},{28,20},{1,9},{5... | collective-permute-start | bytes 393224 | tf_op jit(solution)/shard_map/ppermute | solution.py:103

commit v13 on v12

--- a/solution.py
+++ b/solution.py
@@ -76,7 +76,8 @@
         self.near = [way for way in range(self.members) if way.bit_count() == 1]
         self.far = [way for way in range(self.members) if way.bit_count() > 1]
         self.ways = [0] + self.far + self.near
-        self.early_ways = [0] + self.far + self.near[::-1]
+        self.early_ways = [0] + self.near[::-1] + self.far
+        self.late_ways = [0] + self.far + self.near[::-1]
 
     def member(self):
         return lax.rem(lax.axis_index("seq"), self.members)
@@ -308,7 +309,7 @@
         for b in range(plan.members):
             held_ref[b] = values[b]
         for k in range(plan.members):
-            send_refs[i * plan.members + k][...] = held_ref[plan.peer(k)]
+            send_refs[i * plan.members + k][...] = held_ref[plan.toward(plan.late_ways[k])]
 
 
 def decay_matrix(cum_ref, cum_col, causal, h):
@@ -429,8 +430,10 @@
 
 
 def finish_body(plan, ways, *refs):
-    early_refs, refs = refs[: len(ways)], refs[len(ways) :]
-    late_refs, refs = refs[: len(ways)], refs[len(ways) :]
+    count = len(ways)
+    early_refs = dict(zip([way for way in plan.early_ways if way in ways], refs[:count]))
+    late_refs = dict(zip(ways, refs[count : 2 * count]))
+    refs = refs[2 * count :]
     key_part_ref, value_part_ref, key_ref, value_ref, shrink_ref = refs[:5]
     summary_ref, before_ref, logs_ref = refs[5:8]
     key_out, value_out, total_out, key_grad_ref, value_grad_ref, total_ref, sems = refs[-7:]
@@ -439,7 +442,7 @@
     copies = []
     for i, way in enumerate(ways):
         owner = plan.toward(way)
-        before, after = early_refs[i][:rows], late_refs[i][:rows]
+        before, after = early_refs[way][:rows], late_refs[way][:rows]
         if plan.groups == 2:
             before, after = jnp.where(first, before, after), jnp.where(first, after, before)
         for j in range(plan.own):
@@ -616,14 +619,15 @@
         specs=[VMEM] * (plan.members + plan.groups + 3) + [ANY],
     )
     for first in range(0, len(sends), plan.members):
-        pieces_back = plan.swap_in_group(sends[first : first + plan.members])
-        swapped.append(dict(zip(plan.ways, pieces_back)))
+        pieces_back = plan.swap_in_group(sends[first : first + plan.members], plan.late_ways)
+        swapped.append(dict(zip(plan.late_ways, pieces_back)))
     outs = []
-    for ways in ([0], plan.far + plan.near):
+    for ways in ([0], plan.late_ways[1:]):
         if not ways:
             continue
         operands = [
-            *[pieces_back[way] for pieces_back in swapped for way in ways],
+            *[swapped[0][way] for way in plan.early_ways if way in ways],
+            *[swapped[1][way] for way in ways],
             key_part,
             value_part,
             key_rows,

time: 62.5 us -> 60.9 us (0.974)
  waiting for transfers between devices: 14.6 us -> 12.7 us
    ppermute x20, waiting for transfers between devices: 8.75 us -> 7.59 us  [swap(): return lax.ppermute(piece, 'seq', pairs) if way else piece]
    ppermute x3, waiting for transfers between devices: 3 us -> 2.24 us  [from_groups(): lax.ppermute(piece, 'seq', [(i, (i + step * self.members) % self.blocks)...]
  transfers between devices with their start and end apart: 26 -> 26, of which waited for: 15 -> 14; matrix products, arithmetic and copies ran while one was open for 0% -> 0% of each run, Pallas kernels for 10% -> 10%
where the time goes in v13:
time: 60.9 us; the launch traced here: 60.7 us
  starting transfers between devices  35.9 us (59%)
  waiting for transfers between devices  12.7 us (21%)
  Pallas kernels  11.3 us (19%)
  between operations  0.76 us (1%)
    ppermute x20, starting transfers between devices, swap(): return lax.ppermute(piece, 'seq', pairs) if way else piece  26 us
    pallas_call x14, Pallas kernels, call(): pl.pallas_call(body, out_shape=outs, in_specs=specs or [VMEM] * len(opera...  11.3 us
    ppermute x3, starting transfers between devices, from_groups(): lax.ppermute(piece, 'seq', [(i, (i + step * self.members) % self.blocks)...  8.11 us
    ppermute x20, waiting for transfers between devices, swap(): return lax.ppermute(piece, 'seq', pairs) if way else piece  7.59 us
    ppermute x3, waiting for transfers between devices, on_device(): lax.ppermute(sums, 'head', [(i, (i + step) % parties) for i in range(part...  2.85 us
    ppermute x3, waiting for transfers between devices, from_groups(): lax.ppermute(piece, 'seq', [(i, (i + step * self.members) % self.blocks)...  2.24 us
    ppermute x3, starting transfers between devices, on_device(): lax.ppermute(sums, 'head', [(i, (i + step) % parties) for i in range(part...  1.8 us
  transfers between devices with their start and end apart: 26, of which 14 were waited for; matrix products, arithmetic and copies ran while one was open for 0% of the time, Pallas kernels for 10%

profile of v13, /device:TPU:0, one launch (start us, length us, event | category | flops | bytes accessed | tf_op | source)
XLA Modules:
  0.0 60.7 jit_solution(14419029176332143866)
XLA Ops:
  0.6 2.2 %shard_map.111 = (f32[136,128]{1,0:T(8,128)S(1)}, f32[136,128]{1,0:T(8,128)S(1)}, f32[136,128]{1,0:T(8,128)S(1)}, f32[136,128]{1,0:T(8,128)S(1)}, f32[128,128]{1...) custom-call(bf16[256,1024]{1,0:T(8,128)(2,1)} %refs_8_.3, ...), custom_call_target="tpu_custom_call" | custom-call | tf_op jit(solution)/shard_map/pallas_call | solution.py:25
  2.8 4.0 %collective-permute-start = (f32[136,128]{1,0:T(8,128)S(1)}, f32[136,128]{1,0:T(8,128)S(1)}, u32[]{:S(2)}, u32[]{:S(2)}) collective-permute-start(f32[136,128]{1,0:T(8,128)S(1)} %get-tuple-element.58), channel_id=1, source_target_pairs={{0,12},{4,8},{8,4},{12,0},{16,28},{20,24},{24,20},{28,16},{1,13},{... | collective-permute-start | bytes 208904 | tf_op jit(solution)/shard_map/ppermute | solution.py:104
  6.9 0.5 collective-permute-start.1
  7.4 0.1 collective-permute-start.2
  7.5 2.8 %collective-permute-start.6 = (f32[128,128]{1,0:T(8,128)S(1)}, f32[128,128]{1,0:T(8,128)S(1)}, u32[]{:S(2)}, u32[]{:S(2)}) collective-permute-start(f32[128,128]{1,0:T(8,128)S(1)} %get-tuple-element.67), channel_id=1, source_target_pairs={{0,12},{4,8},{8,4},{12,0},{16,28},{20,24},{24,20},{28,16},{1,13},{... | collective-permute-start | bytes 196616 | tf_op jit(solution)/shard_map/ppermute | solution.py:104
  10.3 0.5 collective-permute-start.7
  10.9 0.8 %collective-permute-start.8 = (f32[128,128]{1,0:T(8,128)S(1)}, f32[128,128]{1,0:T(8,128)S(1)}, u32[]{:S(2)}, u32[]{:S(2)}) collective-permute-start(f32[128,128]{1,0:T(8,128)S(1)} %get-tuple-element.69), channel_id=1, source_target_pairs={{0,8},{4,12},{8,0},{12,4},{16,24},{20,28},{24,16},{28,20},{1,9},{5... | collective-permute-start | bytes 196616 | tf_op jit(solution)/shard_map/ppermute | solution.py:104
  11.6 0.4 collective-permute-done.1.refs_2_
  12.0 2.7 %collective-permute-start.3 = (f32[136,128]{1,0:T(8,128)S(1)}, f32[136,128]{1,0:T(8,128)S(1)}, u32[]{:S(2)}, u32[]{:S(2)}) collective-permute-start(f32[136,128]{1,0:T(8,128)S(1)} %get-tuple-element.61.refs_4_), channel_id=1, source_target_pairs={{0,16},{4,20},{8,24},{12,28},{16,0},{20,4},{24,8},{28,12},{1,17},{... | collective-permute-start | bytes 208904 | tf_op jit(solution)/shard_map/ppermute | solution.py:118
  14.7 0.5 collective-permute-done.8.refs_3_
  15.3 2.6 %collective-permute-start.9 = (f32[128,128]{1,0:T(8,128)S(1)}, f32[128,128]{1,0:T(8,128)S(1)}, u32[]{:S(2)}, u32[]{:S(2)}) collective-permute-start(f32[128,128]{1,0:T(8,128)S(1)} %shard_map.114.refs_4_), channel_id=1, source_target_pairs={{0,16},{4,20},{8,24},{12,28},{16,0},{20,4},{24,8},{28,12},{1,17},{... | collective-permute-start | bytes 196616 | tf_op jit(solution)/shard_map/ppermute | solution.py:118
  17.8 1.5 %collective-permute-done.3.refs_5_ = f32[136,128]{1,0:T(8,128)S(1)} collective-permute-done((f32[136,128]{1,0:T(8,128)S(1)}, f32[136,128]{1,0:T(8,128)S(1)}, u32[]{:S(2)}, u32[]{:S(2)}) %collective-permute-start.3) | collective-permute-done | bytes 69664 | tf_op jit(solution)/shard_map/ppermute | solution.py:118
  19.5 1.1 %collective-permute-start.4 = (f32[128,128]{1,0:T(8,128)S(1)}, f32[128,128]{1,0:T(8,128)S(1)}, u32[]{:S(2)}, u32[]{:S(2)}) collective-permute-start(f32[128,128]{1,0:T(8,128)S(1)} %get-tuple-element.64), channel_id=1, source_target_pairs={{0,4},{4,0},{8,12},{12,8},{16,20},{20,16},{24,28},{28,24},{1,5},{5... | collective-permute-start | bytes 196616 | tf_op jit(solution)/shard_map/ppermute | solution.py:104
  20.6 0.3 collective-permute-start.5
  21.1 2.1 %collective-permute-start.12 = (f32[256,128]{1,0:T(8,128)S(1)}, f32[256,128]{1,0:T(8,128)S(1)}, u32[]{:S(2)}, u32[]{:S(2)}) collective-permute-start(f32[256,128]{1,0:T(8,128)S(1)} %get-tuple-element.75), channel_id=1, source_target_pairs={{0,12},{4,8},{8,4},{12,0},{16,28},{20,24},{24,20},{28,16},{1,13},{... | collective-permute-start | bytes 393224 | tf_op jit(solution)/shard_map/ppermute | solution.py:104
  23.2 1.1 %collective-permute-start.10 = (f32[128,128]{1,0:T(8,128)S(1)}, f32[128,128]{1,0:T(8,128)S(1)}, u32[]{:S(2)}, u32[]{:S(2)}) collective-permute-start(f32[128,128]{1,0:T(8,128)S(1)} %get-tuple-element.73), channel_id=1, source_target_pairs={{0,4},{4,0},{8,12},{12,8},{16,20},{20,16},{24,28},{28,24},{1,5},{5... | collective-permute-start | bytes 196616 | tf_op jit(solution)/shard_map/ppermute | solution.py:104
  24.3 0.3 collective-permute-start.11
  24.6 0.6 collective-permute-done.4.refs_0_.refs_1_
  25.2 0.4 collective-permute-done.5.refs_1_.refs_2_
  25.7 1.2 %shard_map.116 = (bf16[8,256,256]{2,1,0:T(8,128)(2,1)S(1)}, f32[256,1024]{1,0:T(8,128)S(1)}, f32[256,1024]{1,0:T(8,128)S(1)}, bf16[8,128,256]{2,1,0:T(8,128)(2,1)S(1)}) custom-call(bf16[256,1024]{1,0:T(8,128)(2,1)S(1)} %copy-done.2, bf16[256,1024]{1,0:T(8,128)(2,1)S(1)} %copy-done, bf16[256,1024]{1,0:T(8,128)(2,1)S(1)} %copy-done.1, ...), custom_call_target="tpu_custom_call" | custom-call | flops 1000000000 | tf_op jit(solution)/shard_map/pallas_call | solution.py:25
  26.9 1.2 %collective-permute-done.10.refs_4_ = f32[128,128]{1,0:T(8,128)S(1)} collective-permute-done((f32[128,128]{1,0:T(8,128)S(1)}, f32[128,128]{1,0:T(8,128)S(1)}, u32[]{:S(2)}, u32[]{:S(2)}) %collective-permute-start.10) | collective-permute-done | bytes 65568 | tf_op jit(solution)/shard_map/ppermute | solution.py:104
  28.1 0.4 collective-permute-done.11.refs_5_
  28.5 0.7 %shard_map.117 = (f32[256,1024]{1,0:T(8,128)S(1)}, f32[8,256]{1,0:T(8,128)S(1)}, bf16[1024,128]{1,0:T(8,128)(2,1)S(1)}) custom-call(f32[128,128]{1,0:T(8,128)S(1)} %get-tuple-element.63.refs_0_, f32[128,128]{1,0:T(8,128)S(1)} %collective-permute-done.4.refs_0_.refs_1_, f32[128,128]{1,0:T(8,128)S(1)} %collective-permute-done.5.refs_1_.refs_2_, ...), custom_call_target="tpu_custom_call" | custom-call | tf_op jit(solution)/shard_map/pallas_call | solution.py:25
  29.2 1.6 %collective-permute-start.14 = (f32[8,256]{1,0:T(8,128)S(1)}, f32[8,256]{1,0:T(8,128)S(1)}, u32[]{:S(2)}, u32[]{:S(2)}) collective-permute-start(f32[8,256]{1,0:T(8,128)S(1)} %get-tuple-element.80.refs_0_), channel_id=1, source_target_pairs={{0,2},{1,3},{2,0},{3,1},{4,6},{5,7},{6,4},{7,5},{8,10},{9,11},{10,... | collective-permute-start | bytes 24584 | tf_op jit(solution)/shard_map/ppermute | solution.py:578
  30.8 0.2 collective-permute-start.13
  31.0 1.9 %collective-permute-done.14.refs_2_ = f32[8,256]{1,0:T(8,128)S(1)} collective-permute-done((f32[8,256]{1,0:T(8,128)S(1)}, f32[8,256]{1,0:T(8,128)S(1)}, u32[]{:S(2)}, u32[]{:S(2)}) %collective-permute-start.14) | collective-permute-done | bytes 8224 | tf_op jit(solution)/shard_map/ppermute | solution.py:578
  32.9 1.0 %collective-permute-done.13.refs_1_ = f32[8,256]{1,0:T(8,128)S(1)} collective-permute-done((f32[8,256]{1,0:T(8,128)S(1)}, f32[8,256]{1,0:T(8,128)S(1)}, u32[]{:S(2)}, u32[]{:S(2)}) %collective-permute-start.13) | collective-permute-done | bytes 8224 | tf_op jit(solution)/shard_map/ppermute | solution.py:578
  33.9 0.7 %shard_map.118 = (bf16[256,1024]{1,0:T(8,128)(2,1)S(1)}, f32[1024,128]{1,0:T(8,128)S(1)}, f32[256,128]{1,0:T(8,128)S(1)}, f32[256,128]{1,0:T(8,128)S(1)}, f32[25...) custom-call(f32[8,256]{1,0:T(8,128)S(1)} %get-tuple-element.80.refs_0_, f32[8,256]{1,0:T(8,128)S(1)} %collective-permute-done.13.refs_1_, ...), custom_call_target="tpu_custom_call" | custom-call | tf_op jit(solution)/shard_map/pallas_call | solution.py:25
  34.6 1.4 %collective-permute-start.16 = (f32[256,128]{1,0:T(8,128)S(1)}, f32[256,128]{1,0:T(8,128)S(1)}, u32[]{:S(2)}, u32[]{:S(2)}) collective-permute-start(f32[256,128]{1,0:T(8,128)S(1)} %get-tuple-element.88), channel_id=1, source_target_pairs={{0,12},{4,8},{8,4},{12,0},{16,28},{20,24},{24,20},{28,16},{1,13},{... | collective-permute-start | bytes 393224 | tf_op jit(solution)/shard_map/ppermute | solution.py:104
  36.0 0.9 %collective-permute-start.17 = (f32[256,128]{1,0:T(8,128)S(1)}, f32[256,128]{1,0:T(8,128)S(1)}, u32[]{:S(2)}, u32[]{:S(2)}) collective-permute-start(f32[256,128]{1,0:T(8,128)S(1)} %get-tuple-element.89), channel_id=1, source_target_pairs={{0,4},{4,0},{8,12},{12,8},{16,20},{20,16},{24,28},{28,24},{1,5},{5... | collective-permute-start | bytes 393224 | tf_op jit(solution)/shard_map/ppermute | solution.py:104
  37.0 1.2 %collective-permute-start.18 = (f32[256,128]{1,0:T(8,128)S(1)}, f32[256,128]{1,0:T(8,128)S(1)}, u32[]{:S(2)}, u32[]{:S(2)}) collective-permute-start(f32[256,128]{1,0:T(8,128)S(1)} %get-tuple-element.90), channel_id=1, source_target_pairs={{0,8},{4,12},{8,0},{12,4},{16,24},{20,28},{24,16},{28,20},{1,9},{5... | collective-permute-start | bytes 393224 | tf_op jit(solution)/shard_map/ppermute | solution.py:104
  38.1 3.4 %shard_map.119 = (bf16[256,1024]{1,0:T(8,128)(2,1)}, f32[256,1024]{1,0:T(8,128)S(1)}, f32[256,1024]{1,0:T(8,128)S(1)}, f32[8,256,128]{2,1,0:T(8,128)S(1)}) custom-call(bf16[256,1024]{1,0:T(8,128)(2,1)S(1)} %get-tuple-element.83.attn_grad_ref, bf16[256,1024]{1,0:T(8,128)(2,1)S(1)} %copy-done.2, bf16[256,1024]{1,0:T(8,128)(2,1)S(1)} %copy-done, ...), custom_call_target="tpu_custom_call" | custom-call | flops 671088640 | tf_op jit(solution)/shard_map/pallas_call | solution.py:25
  41.5 0.7 %collective-permute-done.17.refs_2_ = f32[256,128]{1,0:T(8,128)S(1)} collective-permute-done((f32[256,128]{1,0:T(8,128)S(1)}, f32[256,128]{1,0:T(8,128)S(1)}, u32[]{:S(2)}, u32[]{:S(2)}) %collective-permute-start.17) | collective-permute-done | bytes 131104 | tf_op jit(solution)/shard_map/ppermute | solution.py:104
  42.2 0.2 shard_map.120
  42.4 1.0 %collective-permute-start.19 = (f32[264,128]{1,0:T(8,128)S(1)}, f32[264,128]{1,0:T(8,128)S(1)}, u32[]{:S(2)}, u32[]{:S(2)}) collective-permute-start(f32[264,128]{1,0:T(8,128)S(1)} %get-tuple-element.92), channel_id=1, source_target_pairs={{0,8},{4,12},{8,0},{12,4},{16,24},{20,28},{24,16},{28,20},{1,9},{5... | collective-permute-start | bytes 405512 | tf_op jit(solution)/shard_map/ppermute | solution.py:104
  43.4 0.1 shard_map.121.refs_4_
  43.5 2.9 %collective-permute-start.22 = (f32[256,128]{1,0:T(8,128)S(1)}, f32[256,128]{1,0:T(8,128)S(1)}, u32[]{:S(2)}, u32[]{:S(2)}) collective-permute-start(f32[256,128]{1,0:T(8,128)S(1)} %shard_map.121.refs_4_), channel_id=1, source_target_pairs={{0,16},{4,20},{8,24},{12,28},{16,0},{20,4},{24,8},{28,12},{1,17},{... | collective-permute-start | bytes 393224 | tf_op jit(solution)/shard_map/ppermute | solution.py:118
  46.3 1.0 %collective-permute-start.20 = (f32[256,128]{1,0:T(8,128)S(1)}, f32[256,128]{1,0:T(8,128)S(1)}, u32[]{:S(2)}, u32[]{:S(2)}) collective-permute-start(f32[256,128]{1,0:T(8,128)S(1)} %get-tuple-element.93), channel_id=1, source_target_pairs={{0,4},{4,0},{8,12},{12,8},{16,20},{20,16},{24,28},{28,24},{1,5},{5... | collective-permute-start | bytes 393224 | tf_op jit(solution)/shard_map/ppermute | solution.py:104
  47.3 1.4 %collective-permute-start.21 = (f32[256,128]{1,0:T(8,128)S(1)}, f32[256,128]{1,0:T(8,128)S(1)}, u32[]{:S(2)}, u32[]{:S(2)}) collective-permute-start(f32[256,128]{1,0:T(8,128)S(1)} %get-tuple-element.94), channel_id=1, source_target_pairs={{0,12},{4,8},{8,4},{12,0},{16,28},{20,24},{24,20},{28,16},{1,13},{... | collective-permute-start | bytes 393224 | tf_op jit(solution)/shard_map/ppermute | solution.py:104
  48.8 0.7 %collective-permute-done.22.refs_5_ = f32[256,128]{1,0:T(8,128)S(1)} collective-permute-done((f32[256,128]{1,0:T(8,128)S(1)}, f32[256,128]{1,0:T(8,128)S(1)}, u32[]{:S(2)}, u32[]{:S(2)}) %collective-permute-start.22) | collective-permute-done | bytes 131104 | tf_op jit(solution)/shard_map/ppermute | solution.py:118
  49.5 0.2 shard_map.122
  49.8 4.6 %collective-permute-start.23 = (f32[256,128]{1,0:T(8,128)S(1)}, f32[256,128]{1,0:T(8,128)S(1)}, u32[]{:S(2)}, u32[]{:S(2)}) collective-permute-start(f32[256,128]{1,0:T(8,128)S(1)} %get-tuple-element.96), channel_id=1, source_target_pairs={{0,12},{4,8},{8,4},{12,0},{16,28},{20,24},{24,20},{28,16},{1,13},{... | collective-permute-start | bytes 393224 | tf_op jit(solution)/shard_map/ppermute | solution.py:104
  54.3 0.6 %collective-permute-start.25 = (f32[256,128]{1,0:T(8,128)S(1)}, f32[256,128]{1,0:T(8,128)S(1)}, u32[]{:S(2)}, u32[]{:S(2)}) collective-permute-start(f32[256,128]{1,0:T(8,128)S(1)} %get-tuple-element.98), channel_id=1, source_target_pairs={{0,4},{4,0},{8,12},{12,8},{16,20},{20,16},{24,28},{28,24},{1,5},{5... | collective-permute-start | bytes 393224 | tf_op jit(solution)/shard_map/ppermute | solution.py:104
  55.0 1.0 %shard_map.123 = (bf16[256,1024]{1,0:T(8,128)(2,1)}, bf16[256,1024]{1,0:T(8,128)(2,1)}, f32[1024,128]{1,0:T(8,128)}) custom-call(f32[256,128]{1,0:T(8,128)S(1)} %get-tuple-element.95.refs_5_.refs_0_, f32[256,128]{1,0:T(8,128)S(1)} %get-tuple-element.103.refs_1_, f32[256,1024]{1,0:T(8,128)S(1)} %get-tuple-element.91.refs_6_.refs_2_, ...), custom_call_target="tpu_custom_call" | custom-call | tf_op jit(solution)/shard_map/pallas_call | solution.py:25
  55.9 0.2 collective-permute-done.20.refs_1_
  56.1 1.3 %collective-permute-done.23.refs_3_ = f32[256,128]{1,0:T(8,128)S(1)} collective-permute-done((f32[256,128]{1,0:T(8,128)S(1)}, f32[256,128]{1,0:T(8,128)S(1)}, u32[]{:S(2)}, u32[]{:S(2)}) %collective-permute-start.23) | collective-permute-done | bytes 131104 | tf_op jit(solution)/shard_map/ppermute | solution.py:104
  57.4 1.9 %collective-permute-done.24.refs_4_ = f32[256,128]{1,0:T(8,128)S(1)} collective-permute-done((f32[256,128]{1,0:T(8,128)S(1)}, f32[256,128]{1,0:T(8,128)S(1)}, u32[]{:S(2)}, u32[]{:S(2)}) %collective-permute-start.24) | collective-permute-done | bytes 131104 | tf_op jit(solution)/shard_map/ppermute | solution.py:104
  59.3 1.4 %shard_map.124 = (bf16[256,1024]{1,0:T(8,128)(2,1)}, bf16[256,1024]{1,0:T(8,128)(2,1)}, f32[1024,128]{1,0:T(8,128)}) custom-call(f32[264,128]{1,0:T(8,128)S(1)} %collective-permute-done.19.refs_9_.refs_0_, f32[256,128]{1,0:T(8,128)S(1)} %collective-permute-done.20.refs_1_, ...), custom_call_target="tpu_custom_call", output_to_operand_aliasing={{0}: (14, {}), {1}: (15, {}), {2}: (16, {})} | custom-call | tf_op jit(solution)/shard_map/pallas_call | solution.py:25
  (32 shorter events, 0.3 us)
Async XLA Ops:
  2.8 8.0 %collective-permute-start = (f32[136,128]{1,0:T(8,128)S(1)}, f32[136,128]{1,0:T(8,128)S(1)}, u32[]{:S(2)}, u32[]{:S(2)}) collective-permute-start(f32[136,128]{1,0:T(8,128)S(1)} %get-tuple-element.58), channel_id=1, source_target_pairs={{0,12},{4,8},{8,4},{12,0},{16,28},{20,24},{24,20},{28,16},{1,13},{... | collective-permute-start | bytes 208904 | tf_op jit(solution)/shard_map/ppermute | solution.py:104
  6.9 5.1 %collective-permute-start.1 = (f32[136,128]{1,0:T(8,128)S(1)}, f32[136,128]{1,0:T(8,128)S(1)}, u32[]{:S(2)}, u32[]{:S(2)}) collective-permute-start(f32[136,128]{1,0:T(8,128)S(1)} %get-tuple-element.59), channel_id=1, source_target_pairs={{0,4},{4,0},{8,12},{12,8},{16,20},{20,16},{24,28},{28,24},{1,5},{5... | collective-permute-start | bytes 208904 | tf_op jit(solution)/shard_map/ppermute | solution.py:104
  7.4 4.6 %collective-permute-start.2 = (f32[136,128]{1,0:T(8,128)S(1)}, f32[136,128]{1,0:T(8,128)S(1)}, u32[]{:S(2)}, u32[]{:S(2)}) collective-permute-start(f32[136,128]{1,0:T(8,128)S(1)} %get-tuple-element.60), channel_id=1, source_target_pairs={{0,8},{4,12},{8,0},{12,4},{16,24},{20,28},{24,16},{28,20},{1,9},{5... | collective-permute-start | bytes 208904 | tf_op jit(solution)/shard_map/ppermute | solution.py:104
  7.5 7.2 %collective-permute-start.6 = (f32[128,128]{1,0:T(8,128)S(1)}, f32[128,128]{1,0:T(8,128)S(1)}, u32[]{:S(2)}, u32[]{:S(2)}) collective-permute-start(f32[128,128]{1,0:T(8,128)S(1)} %get-tuple-element.67), channel_id=1, source_target_pairs={{0,12},{4,8},{8,4},{12,0},{16,28},{20,24},{24,20},{28,16},{1,13},{... | collective-permute-start | bytes 196616 | tf_op jit(solution)/shard_map/ppermute | solution.py:104
  10.3 4.3 %collective-permute-start.7 = (f32[128,128]{1,0:T(8,128)S(1)}, f32[128,128]{1,0:T(8,128)S(1)}, u32[]{:S(2)}, u32[]{:S(2)}) collective-permute-start(f32[128,128]{1,0:T(8,128)S(1)} %get-tuple-element.68), channel_id=1, source_target_pairs={{0,4},{4,0},{8,12},{12,8},{16,20},{20,16},{24,28},{28,24},{1,5},{5... | collective-permute-start | bytes 196616 | tf_op jit(solution)/shard_map/ppermute | solution.py:104
  10.9 4.3 %collective-permute-start.8 = (f32[128,128]{1,0:T(8,128)S(1)}, f32[128,128]{1,0:T(8,128)S(1)}, u32[]{:S(2)}, u32[]{:S(2)}) collective-permute-start(f32[128,128]{1,0:T(8,128)S(1)} %get-tuple-element.69), channel_id=1, source_target_pairs={{0,8},{4,12},{8,0},{12,4},{16,24},{20,28},{24,16},{28,20},{1,9},{5... | collective-permute-start | bytes 196616 | tf_op jit(solution)/shard_map/ppermute | solution.py:104
  12.0 7.3 %collective-permute-start.3 = (f32[136,128]{1,0:T(8,128)S(1)}, f32[136,128]{1,0:T(8,128)S(1)}, u32[]{:S(2)}, u32[]{:S(2)}) collective-permute-start(f32[136,128]{1,0:T(8,128)S(1)} %get-tuple-element.61.refs_4_), channel_id=1, source_target_pairs={{0,16},{4,20},{8,24},{12,28},{16,0},{20,4},{24,8},{28,12},{1,17},{... | collective-permute-start | bytes 208904 | tf_op jit(solution)/shard_map/ppermute | solution.py:118
  15.2 4.2 %copy-start.3 = (f32[8,128,128]{2,1,0:T(8,128)S(1)}, f32[8,128,128]{2,1,0:T(8,128)}, u32[]{:S(2)}) copy-start(f32[8,128,128]{2,1,0:T(8,128)} %param.14) | copy-start | bytes 1572868
  15.2 10.4 %copy-start.5 = (bf16[256,1024]{1,0:T(8,128)(2,1)S(1)}, bf16[256,1024]{1,0:T(8,128)(2,1)}, u32[]{:S(2)}) copy-start(bf16[256,1024]{1,0:T(8,128)(2,1)} %upstream_ref.1) | copy-start | bytes 1572868
  15.3 5.7 %collective-permute-start.9 = (f32[128,128]{1,0:T(8,128)S(1)}, f32[128,128]{1,0:T(8,128)S(1)}, u32[]{:S(2)}, u32[]{:S(2)}) collective-permute-start(f32[128,128]{1,0:T(8,128)S(1)} %shard_map.114.refs_4_), channel_id=1, source_target_pairs={{0,16},{4,20},{8,24},{12,28},{16,0},{20,4},{24,8},{28,12},{1,17},{... | collective-permute-start | bytes 196616 | tf_op jit(solution)/shard_map/ppermute | solution.py:118
  19.4 6.3 %copy-start.1 = (bf16[256,1024]{1,0:T(8,128)(2,1)S(1)}, bf16[256,1024]{1,0:T(8,128)(2,1)}, u32[]{:S(2)}) copy-start(bf16[256,1024]{1,0:T(8,128)(2,1)} %refs_9_.1) | copy-start | bytes 1572868
  19.4 6.3 %copy-start.2 = (bf16[256,1024]{1,0:T(8,128)(2,1)S(1)}, bf16[256,1024]{1,0:T(8,128)(2,1)}, u32[]{:S(2)}) copy-start(bf16[256,1024]{1,0:T(8,128)(2,1)} %query_ref.3) | copy-start | bytes 1572868
  19.5 6.2 %copy-start = (bf16[256,1024]{1,0:T(8,128)(2,1)S(1)}, bf16[256,1024]{1,0:T(8,128)(2,1)}, u32[]{:S(2)}) copy-start(bf16[256,1024]{1,0:T(8,128)(2,1)} %refs_8_.3) | copy-start | bytes 1572868
  19.5 5.7 %collective-permute-start.4 = (f32[128,128]{1,0:T(8,128)S(1)}, f32[128,128]{1,0:T(8,128)S(1)}, u32[]{:S(2)}, u32[]{:S(2)}) collective-permute-start(f32[128,128]{1,0:T(8,128)S(1)} %get-tuple-element.64), channel_id=1, source_target_pairs={{0,4},{4,0},{8,12},{12,8},{16,20},{20,16},{24,28},{28,24},{1,5},{5... | collective-permute-start | bytes 196616 | tf_op jit(solution)/shard_map/ppermute | solution.py:104
  20.6 5.0 %collective-permute-start.5 = (f32[128,128]{1,0:T(8,128)S(1)}, f32[128,128]{1,0:T(8,128)S(1)}, u32[]{:S(2)}, u32[]{:S(2)}) collective-permute-start(f32[128,128]{1,0:T(8,128)S(1)} %get-tuple-element.65), channel_id=1, source_target_pairs={{0,8},{4,12},{8,0},{12,4},{16,24},{20,28},{24,16},{28,20},{1,9},{5... | collective-permute-start | bytes 196616 | tf_op jit(solution)/shard_map/ppermute | solution.py:104
  21.1 7.5 %collective-permute-start.12 = (f32[256,128]{1,0:T(8,128)S(1)}, f32[256,128]{1,0:T(8,128)S(1)}, u32[]{:S(2)}, u32[]{:S(2)}) collective-permute-start(f32[256,128]{1,0:T(8,128)S(1)} %get-tuple-element.75), channel_id=1, source_target_pairs={{0,12},{4,8},{8,4},{12,0},{16,28},{20,24},{24,20},{28,16},{1,13},{... | collective-permute-start | bytes 393224 | tf_op jit(solution)/shard_map/ppermute | solution.py:104
  23.2 2.5 %copy-start.6 = (f32[1024]{0:T(1024)S(1)}, f32[1024]{0:T(1024)}, u32[]{:S(2)}) copy-start(f32[1024]{0:T(1024)} %param.13) | copy-start | bytes 12292
  23.2 4.9 %collective-permute-start.10 = (f32[128,128]{1,0:T(8,128)S(1)}, f32[128,128]{1,0:T(8,128)S(1)}, u32[]{:S(2)}, u32[]{:S(2)}) collective-permute-start(f32[128,128]{1,0:T(8,128)S(1)} %get-tuple-element.73), channel_id=1, source_target_pairs={{0,4},{4,0},{8,12},{12,8},{16,20},{20,16},{24,28},{28,24},{1,5},{5... | collective-permute-start | bytes 196616 | tf_op jit(solution)/shard_map/ppermute | solution.py:104
  24.3 4.3 %collective-permute-start.11 = (f32[128,128]{1,0:T(8,128)S(1)}, f32[128,128]{1,0:T(8,128)S(1)}, u32[]{:S(2)}, u32[]{:S(2)}) collective-permute-start(f32[128,128]{1,0:T(8,128)S(1)} %get-tuple-element.74), channel_id=1, source_target_pairs={{0,8},{4,12},{8,0},{12,4},{16,24},{20,28},{24,16},{28,20},{1,9},{5... | collective-permute-start | bytes 196616 | tf_op jit(solution)/shard_map/ppermute | solution.py:104
  29.2 1.8 %collective-permute-start.15 = (f32[8,256]{1,0:T(8,128)S(1)}, f32[8,256]{1,0:T(8,128)S(1)}, u32[]{:S(2)}, u32[]{:S(2)}) collective-permute-start(f32[8,256]{1,0:T(8,128)S(1)} %get-tuple-element.80.refs_0_), channel_id=1, source_target_pairs={{0,3},{1,0},{2,1},{3,2},{4,7},{5,4},{6,5},{7,6},{8,11},{9,8},{10,9... | collective-permute-start | bytes 24584 | tf_op jit(solution)/shard_map/ppermute | solution.py:578
  29.2 3.7 %collective-permute-start.14 = (f32[8,256]{1,0:T(8,128)S(1)}, f32[8,256]{1,0:T(8,128)S(1)}, u32[]{:S(2)}, u32[]{:S(2)}) collective-permute-start(f32[8,256]{1,0:T(8,128)S(1)} %get-tuple-element.80.refs_0_), channel_id=1, source_target_pairs={{0,2},{1,3},{2,0},{3,1},{4,6},{5,7},{6,4},{7,5},{8,10},{9,11},{10,... | collective-permute-start | bytes 24584 | tf_op jit(solution)/shard_map/ppermute | solution.py:578
  30.8 3.1 %collective-permute-start.13 = (f32[8,256]{1,0:T(8,128)S(1)}, f32[8,256]{1,0:T(8,128)S(1)}, u32[]{:S(2)}, u32[]{:S(2)}) collective-permute-start(f32[8,256]{1,0:T(8,128)S(1)} %get-tuple-element.80.refs_0_), channel_id=1, source_target_pairs={{0,1},{1,2},{2,3},{3,0},{4,5},{5,6},{6,7},{7,4},{8,9},{9,10},{10,1... | collective-permute-start | bytes 24584 | tf_op jit(solution)/shard_map/ppermute | solution.py:578
  34.6 6.9 %collective-permute-start.16 = (f32[256,128]{1,0:T(8,128)S(1)}, f32[256,128]{1,0:T(8,128)S(1)}, u32[]{:S(2)}, u32[]{:S(2)}) collective-permute-start(f32[256,128]{1,0:T(8,128)S(1)} %get-tuple-element.88), channel_id=1, source_target_pairs={{0,12},{4,8},{8,4},{12,0},{16,28},{20,24},{24,20},{28,16},{1,13},{... | collective-permute-start | bytes 393224 | tf_op jit(solution)/shard_map/ppermute | solution.py:104
  36.0 6.2 %collective-permute-start.17 = (f32[256,128]{1,0:T(8,128)S(1)}, f32[256,128]{1,0:T(8,128)S(1)}, u32[]{:S(2)}, u32[]{:S(2)}) collective-permute-start(f32[256,128]{1,0:T(8,128)S(1)} %get-tuple-element.89), channel_id=1, source_target_pairs={{0,4},{4,0},{8,12},{12,8},{16,20},{20,16},{24,28},{28,24},{1,5},{5... | collective-permute-start | bytes 393224 | tf_op jit(solution)/shard_map/ppermute | solution.py:104
  37.0 5.3 %collective-permute-start.18 = (f32[256,128]{1,0:T(8,128)S(1)}, f32[256,128]{1,0:T(8,128)S(1)}, u32[]{:S(2)}, u32[]{:S(2)}) collective-permute-start(f32[256,128]{1,0:T(8,128)S(1)} %get-tuple-element.90), channel_id=1, source_target_pairs={{0,8},{4,12},{8,0},{12,4},{16,24},{20,28},{24,16},{28,20},{1,9},{5... | collective-permute-start | bytes 393224 | tf_op jit(solution)/shard_map/ppermute | solution.py:104
  38.1 4.1 %copy-start.4 = (f32[8,128,128]{2,1,0:T(8,128)S(1)}, f32[8,128,128]{2,1,0:T(8,128)}, u32[]{:S(2)}) copy-start(f32[8,128,128]{2,1,0:T(8,128)} %param.15) | copy-start | bytes 1572868
  42.4 7.1 %collective-permute-start.19 = (f32[264,128]{1,0:T(8,128)S(1)}, f32[264,128]{1,0:T(8,128)S(1)}, u32[]{:S(2)}, u32[]{:S(2)}) collective-permute-start(f32[264,128]{1,0:T(8,128)S(1)} %get-tuple-element.92), channel_id=1, source_target_pairs={{0,8},{4,12},{8,0},{12,4},{16,24},{20,28},{24,16},{28,20},{1,9},{5... | collective-permute-start | bytes 405512 | tf_op jit(solution)/shard_map/ppermute | solution.py:104
  43.5 6.0 %collective-permute-start.22 = (f32[256,128]{1,0:T(8,128)S(1)}, f32[256,128]{1,0:T(8,128)S(1)}, u32[]{:S(2)}, u32[]{:S(2)}) collective-permute-start(f32[256,128]{1,0:T(8,128)S(1)} %shard_map.121.refs_4_), channel_id=1, source_target_pairs={{0,16},{4,20},{8,24},{12,28},{16,0},{20,4},{24,8},{28,12},{1,17},{... | collective-permute-start | bytes 393224 | tf_op jit(solution)/shard_map/ppermute | solution.py:118
  46.3 9.8 %collective-permute-start.20 = (f32[256,128]{1,0:T(8,128)S(1)}, f32[256,128]{1,0:T(8,128)S(1)}, u32[]{:S(2)}, u32[]{:S(2)}) collective-permute-start(f32[256,128]{1,0:T(8,128)S(1)} %get-tuple-element.93), channel_id=1, source_target_pairs={{0,4},{4,0},{8,12},{12,8},{16,20},{20,16},{24,28},{28,24},{1,5},{5... | collective-permute-start | bytes 393224 | tf_op jit(solution)/shard_map/ppermute | solution.py:104
  47.3 8.8 %collective-permute-start.21 = (f32[256,128]{1,0:T(8,128)S(1)}, f32[256,128]{1,0:T(8,128)S(1)}, u32[]{:S(2)}, u32[]{:S(2)}) collective-permute-start(f32[256,128]{1,0:T(8,128)S(1)} %get-tuple-element.94), channel_id=1, source_target_pairs={{0,12},{4,8},{8,4},{12,0},{16,28},{20,24},{24,20},{28,16},{1,13},{... | collective-permute-start | bytes 393224 | tf_op jit(solution)/shard_map/ppermute | solution.py:104
  49.8 7.6 %collective-permute-start.23 = (f32[256,128]{1,0:T(8,128)S(1)}, f32[256,128]{1,0:T(8,128)S(1)}, u32[]{:S(2)}, u32[]{:S(2)}) collective-permute-start(f32[256,128]{1,0:T(8,128)S(1)} %get-tuple-element.96), channel_id=1, source_target_pairs={{0,12},{4,8},{8,4},{12,0},{16,28},{20,24},{24,20},{28,16},{1,13},{... | collective-permute-start | bytes 393224 | tf_op jit(solution)/shard_map/ppermute | solution.py:104
  54.3 5.0 %collective-permute-start.24 = (f32[256,128]{1,0:T(8,128)S(1)}, f32[256,128]{1,0:T(8,128)S(1)}, u32[]{:S(2)}, u32[]{:S(2)}) collective-permute-start(f32[256,128]{1,0:T(8,128)S(1)} %get-tuple-element.97), channel_id=1, source_target_pairs={{0,8},{4,12},{8,0},{12,4},{16,24},{20,28},{24,16},{28,20},{1,9},{5... | collective-permute-start | bytes 393224 | tf_op jit(solution)/shard_map/ppermute | solution.py:104
  54.3 5.0 %collective-permute-start.25 = (f32[256,128]{1,0:T(8,128)S(1)}, f32[256,128]{1,0:T(8,128)S(1)}, u32[]{:S(2)}, u32[]{:S(2)}) collective-permute-start(f32[256,128]{1,0:T(8,128)S(1)} %get-tuple-element.98), channel_id=1, source_target_pairs={{0,4},{4,0},{8,12},{12,8},{16,20},{20,16},{24,28},{28,24},{1,5},{5... | collective-permute-start | bytes 393224 | tf_op jit(solution)/shard_map/ppermute | solution.py:104

commit v14 on v13

--- a/solution.py
+++ b/solution.py
@@ -77,7 +77,7 @@
         self.far = [way for way in range(self.members) if way.bit_count() > 1]
         self.ways = [0] + self.far + self.near
         self.early_ways = [0] + self.near[::-1] + self.far
-        self.late_ways = [0] + self.far + self.near[::-1]
+        self.late_ways = [0] + self.near[::-1] + self.far
 
     def member(self):
         return lax.rem(lax.axis_index("seq"), self.members)
@@ -576,7 +576,7 @@
     )
     all_sums = [sums] + [
         lax.ppermute(sums, "head", [(i, (i + step) % parties) for i in range(parties)])
-        for step in range(1, parties)
+        for step in reversed(range(1, parties))
     ]
     attn_grad, summary, *sends = call(
         bind(attn_grad_body, parties),

time: 60.9 us -> 65.2 us (1.071)
  waiting for transfers between devices: 12.7 us -> 16.9 us
    ppermute x20, waiting for transfers between devices: 7.59 us -> 11.8 us  [swap(): return lax.ppermute(piece, 'seq', pairs) if way else piece]
    ppermute x3, waiting for transfers between devices: 2.24 us -> 3.81 us  [from_groups(): lax.ppermute(piece, 'seq', [(i, (i + step * self.members) % self.blocks)...]
    ppermute x3, waiting for transfers between devices: 2.85 us -> 1.37 us  [on_device(): lax.ppermute(sums, 'head', [(i, (i + step) % parties) for i in range(part...]
    ppermute x20, starting transfers between devices: 26 us -> 24.7 us  [swap(): return lax.ppermute(piece, 'seq', pairs) if way else piece]
    ppermute x3, starting transfers between devices: 1.8 us -> 3.04 us  [on_device(): lax.ppermute(sums, 'head', [(i, (i + step) % parties) for i in range(part...]
  transfers between devices with their start and end apart: 26 -> 26, of which waited for: 14 -> 17; matrix products, arithmetic and copies ran while one was open for 0% -> 0% of each run, Pallas kernels for 10% -> 9%
where the time goes in v14:
time: 65.2 us; the launch traced here: 65 us
  starting transfers between devices  35.9 us (55%)
  waiting for transfers between devices  16.9 us (26%)
  Pallas kernels  11.3 us (17%)
  between operations  0.77 us (1%)
    ppermute x20, starting transfers between devices, swap(): return lax.ppermute(piece, 'seq', pairs) if way else piece  24.7 us
    ppermute x20, waiting for transfers between devices, swap(): return lax.ppermute(piece, 'seq', pairs) if way else piece  11.8 us
    pallas_call x14, Pallas kernels, call(): pl.pallas_call(body, out_shape=outs, in_specs=specs or [VMEM] * len(opera...  11.3 us
    ppermute x3, starting transfers between devices, from_groups(): lax.ppermute(piece, 'seq', [(i, (i + step * self.members) % self.blocks)...  8.18 us
    ppermute x3, waiting for transfers between devices, from_groups(): lax.ppermute(piece, 'seq', [(i, (i + step * self.members) % self.blocks)...  3.81 us
    ppermute x3, starting transfers between devices, on_device(): lax.ppermute(sums, 'head', [(i, (i + step) % parties) for i in range(part...  3.04 us
    ppermute x3, waiting for transfers between devices, on_device(): lax.ppermute(sums, 'head', [(i, (i + step) % parties) for i in range(part...  1.37 us
  transfers between devices with their start and end apart: 26, of which 17 were waited for; matrix products, arithmetic and copies ran while one was open for 0% of the time, Pallas kernels for 9%

profile of v14, /device:TPU:0, one launch (start us, length us, event | category | flops | bytes accessed | tf_op | source)
XLA Modules:
  0.0 65.0 jit_solution(3847560353276786668)
XLA Ops:
  0.6 2.2 %shard_map.111 = (f32[136,128]{1,0:T(8,128)S(1)}, f32[136,128]{1,0:T(8,128)S(1)}, f32[136,128]{1,0:T(8,128)S(1)}, f32[136,128]{1,0:T(8,128)S(1)}, f32[128,128]{1...) custom-call(bf16[256,1024]{1,0:T(8,128)(2,1)} %refs_8_.3, ...), custom_call_target="tpu_custom_call" | custom-call | tf_op jit(solution)/shard_map/pallas_call | solution.py:25
  2.8 4.0 %collective-permute-start = (f32[136,128]{1,0:T(8,128)S(1)}, f32[136,128]{1,0:T(8,128)S(1)}, u32[]{:S(2)}, u32[]{:S(2)}) collective-permute-start(f32[136,128]{1,0:T(8,128)S(1)} %get-tuple-element.58), channel_id=1, source_target_pairs={{0,12},{4,8},{8,4},{12,0},{16,28},{20,24},{24,20},{28,16},{1,13},{... | collective-permute-start | bytes 208904 | tf_op jit(solution)/shard_map/ppermute | solution.py:104
  6.9 0.5 collective-permute-start.1
  7.5 2.8 %collective-permute-start.6 = (f32[128,128]{1,0:T(8,128)S(1)}, f32[128,128]{1,0:T(8,128)S(1)}, u32[]{:S(2)}, u32[]{:S(2)}) collective-permute-start(f32[128,128]{1,0:T(8,128)S(1)} %get-tuple-element.67), channel_id=1, source_target_pairs={{0,12},{4,8},{8,4},{12,0},{16,28},{20,24},{24,20},{28,16},{1,13},{... | collective-permute-start | bytes 196616 | tf_op jit(solution)/shard_map/ppermute | solution.py:104
  10.3 0.5 collective-permute-start.7
  10.9 0.8 %collective-permute-start.8 = (f32[128,128]{1,0:T(8,128)S(1)}, f32[128,128]{1,0:T(8,128)S(1)}, u32[]{:S(2)}, u32[]{:S(2)}) collective-permute-start(f32[128,128]{1,0:T(8,128)S(1)} %get-tuple-element.69), channel_id=1, source_target_pairs={{0,8},{4,12},{8,0},{12,4},{16,24},{20,28},{24,16},{28,20},{1,9},{5... | collective-permute-start | bytes 196616 | tf_op jit(solution)/shard_map/ppermute | solution.py:104
  11.6 0.4 collective-permute-done.1.refs_2_
  12.0 2.7 %collective-permute-start.3 = (f32[136,128]{1,0:T(8,128)S(1)}, f32[136,128]{1,0:T(8,128)S(1)}, u32[]{:S(2)}, u32[]{:S(2)}) collective-permute-start(f32[136,128]{1,0:T(8,128)S(1)} %get-tuple-element.61.refs_4_), channel_id=1, source_target_pairs={{0,16},{4,20},{8,24},{12,28},{16,0},{20,4},{24,8},{28,12},{1,17},{... | collective-permute-start | bytes 208904 | tf_op jit(solution)/shard_map/ppermute | solution.py:118
  14.7 0.5 collective-permute-done.8.refs_3_
  15.3 2.6 %collective-permute-start.9 = (f32[128,128]{1,0:T(8,128)S(1)}, f32[128,128]{1,0:T(8,128)S(1)}, u32[]{:S(2)}, u32[]{:S(2)}) collective-permute-start(f32[128,128]{1,0:T(8,128)S(1)} %shard_map.114.refs_4_), channel_id=1, source_target_pairs={{0,16},{4,20},{8,24},{12,28},{16,0},{20,4},{24,8},{28,12},{1,17},{... | collective-permute-start | bytes 196616 | tf_op jit(solution)/shard_map/ppermute | solution.py:118
  17.8 1.5 %collective-permute-done.3.refs_5_ = f32[136,128]{1,0:T(8,128)S(1)} collective-permute-done((f32[136,128]{1,0:T(8,128)S(1)}, f32[136,128]{1,0:T(8,128)S(1)}, u32[]{:S(2)}, u32[]{:S(2)}) %collective-permute-start.3) | collective-permute-done | bytes 69664 | tf_op jit(solution)/shard_map/ppermute | solution.py:118
  19.5 1.1 %collective-permute-start.4 = (f32[128,128]{1,0:T(8,128)S(1)}, f32[128,128]{1,0:T(8,128)S(1)}, u32[]{:S(2)}, u32[]{:S(2)}) collective-permute-start(f32[128,128]{1,0:T(8,128)S(1)} %get-tuple-element.64), channel_id=1, source_target_pairs={{0,4},{4,0},{8,12},{12,8},{16,20},{20,16},{24,28},{28,24},{1,5},{5... | collective-permute-start | bytes 196616 | tf_op jit(solution)/shard_map/ppermute | solution.py:104
  20.6 0.3 collective-permute-start.5
  21.1 2.1 %collective-permute-start.12 = (f32[256,128]{1,0:T(8,128)S(1)}, f32[256,128]{1,0:T(8,128)S(1)}, u32[]{:S(2)}, u32[]{:S(2)}) collective-permute-start(f32[256,128]{1,0:T(8,128)S(1)} %get-tuple-element.75), channel_id=1, source_target_pairs={{0,12},{4,8},{8,4},{12,0},{16,28},{20,24},{24,20},{28,16},{1,13},{... | collective-permute-start | bytes 393224 | tf_op jit(solution)/shard_map/ppermute | solution.py:104
  23.2 1.1 %collective-permute-start.10 = (f32[128,128]{1,0:T(8,128)S(1)}, f32[128,128]{1,0:T(8,128)S(1)}, u32[]{:S(2)}, u32[]{:S(2)}) collective-permute-start(f32[128,128]{1,0:T(8,128)S(1)} %get-tuple-element.73), channel_id=1, source_target_pairs={{0,4},{4,0},{8,12},{12,8},{16,20},{20,16},{24,28},{28,24},{1,5},{5... | collective-permute-start | bytes 196616 | tf_op jit(solution)/shard_map/ppermute | solution.py:104
  24.3 0.3 collective-permute-start.11
  24.6 0.6 collective-permute-done.4.refs_0_.refs_1_
  25.2 0.4 collective-permute-done.5.refs_1_.refs_2_
  25.7 1.2 %shard_map.116 = (bf16[8,256,256]{2,1,0:T(8,128)(2,1)S(1)}, f32[256,1024]{1,0:T(8,128)S(1)}, f32[256,1024]{1,0:T(8,128)S(1)}, bf16[8,128,256]{2,1,0:T(8,128)(2,1)S(1)}) custom-call(bf16[256,1024]{1,0:T(8,128)(2,1)S(1)} %copy-done.2, bf16[256,1024]{1,0:T(8,128)(2,1)S(1)} %copy-done, bf16[256,1024]{1,0:T(8,128)(2,1)S(1)} %copy-done.1, ...), custom_call_target="tpu_custom_call" | custom-call | flops 1000000000 | tf_op jit(solution)/shard_map/pallas_call | solution.py:25
  26.9 1.2 %collective-permute-done.10.refs_4_ = f32[128,128]{1,0:T(8,128)S(1)} collective-permute-done((f32[128,128]{1,0:T(8,128)S(1)}, f32[128,128]{1,0:T(8,128)S(1)}, u32[]{:S(2)}, u32[]{:S(2)}) %collective-permute-start.10) | collective-permute-done | bytes 65568 | tf_op jit(solution)/shard_map/ppermute | solution.py:104
  28.1 0.4 collective-permute-done.11.refs_5_
  28.5 0.7 %shard_map.117 = (f32[256,1024]{1,0:T(8,128)S(1)}, f32[8,256]{1,0:T(8,128)S(1)}, bf16[1024,128]{1,0:T(8,128)(2,1)S(1)}) custom-call(f32[128,128]{1,0:T(8,128)S(1)} %get-tuple-element.63.refs_0_, f32[128,128]{1,0:T(8,128)S(1)} %collective-permute-done.4.refs_0_.refs_1_, f32[128,128]{1,0:T(8,128)S(1)} %collective-permute-done.5.refs_1_.refs_2_, ...), custom_call_target="tpu_custom_call" | custom-call | tf_op jit(solution)/shard_map/pallas_call | solution.py:25
  29.2 1.6 %collective-permute-start.14 = (f32[8,256]{1,0:T(8,128)S(1)}, f32[8,256]{1,0:T(8,128)S(1)}, u32[]{:S(2)}, u32[]{:S(2)}) collective-permute-start(f32[8,256]{1,0:T(8,128)S(1)} %get-tuple-element.80.refs_0_), channel_id=1, source_target_pairs={{0,2},{1,3},{2,0},{3,1},{4,6},{5,7},{6,4},{7,5},{8,10},{9,11},{10,... | collective-permute-start | bytes 24584 | tf_op jit(solution)/shard_map/ppermute | solution.py:578
  30.8 1.4 %collective-permute-start.13 = (f32[8,256]{1,0:T(8,128)S(1)}, f32[8,256]{1,0:T(8,128)S(1)}, u32[]{:S(2)}, u32[]{:S(2)}) collective-permute-start(f32[8,256]{1,0:T(8,128)S(1)} %get-tuple-element.80.refs_0_), channel_id=1, source_target_pairs={{0,3},{1,0},{2,1},{3,2},{4,7},{5,4},{6,5},{7,6},{8,11},{9,8},{10,9... | collective-permute-start | bytes 24584 | tf_op jit(solution)/shard_map/ppermute | solution.py:578
  32.3 0.6 collective-permute-done.14.refs_2_
  32.9 0.7 %collective-permute-done.13.refs_1_ = f32[8,256]{1,0:T(8,128)S(1)} collective-permute-done((f32[8,256]{1,0:T(8,128)S(1)}, f32[8,256]{1,0:T(8,128)S(1)}, u32[]{:S(2)}, u32[]{:S(2)}) %collective-permute-start.13) | collective-permute-done | bytes 8224 | tf_op jit(solution)/shard_map/ppermute | solution.py:578
  33.6 0.7 %shard_map.118 = (bf16[256,1024]{1,0:T(8,128)(2,1)S(1)}, f32[1024,128]{1,0:T(8,128)S(1)}, f32[256,128]{1,0:T(8,128)S(1)}, f32[256,128]{1,0:T(8,128)S(1)}, f32[25...) custom-call(f32[8,256]{1,0:T(8,128)S(1)} %get-tuple-element.80.refs_0_, f32[8,256]{1,0:T(8,128)S(1)} %collective-permute-done.13.refs_1_, ...), custom_call_target="tpu_custom_call" | custom-call | tf_op jit(solution)/shard_map/pallas_call | solution.py:25
  34.3 1.4 %collective-permute-start.16 = (f32[256,128]{1,0:T(8,128)S(1)}, f32[256,128]{1,0:T(8,128)S(1)}, u32[]{:S(2)}, u32[]{:S(2)}) collective-permute-start(f32[256,128]{1,0:T(8,128)S(1)} %get-tuple-element.88), channel_id=1, source_target_pairs={{0,12},{4,8},{8,4},{12,0},{16,28},{20,24},{24,20},{28,16},{1,13},{... | collective-permute-start | bytes 393224 | tf_op jit(solution)/shard_map/ppermute | solution.py:104
  35.8 0.9 %collective-permute-start.17 = (f32[256,128]{1,0:T(8,128)S(1)}, f32[256,128]{1,0:T(8,128)S(1)}, u32[]{:S(2)}, u32[]{:S(2)}) collective-permute-start(f32[256,128]{1,0:T(8,128)S(1)} %get-tuple-element.89), channel_id=1, source_target_pairs={{0,4},{4,0},{8,12},{12,8},{16,20},{20,16},{24,28},{28,24},{1,5},{5... | collective-permute-start | bytes 393224 | tf_op jit(solution)/shard_map/ppermute | solution.py:104
  36.7 1.2 %collective-permute-start.18 = (f32[256,128]{1,0:T(8,128)S(1)}, f32[256,128]{1,0:T(8,128)S(1)}, u32[]{:S(2)}, u32[]{:S(2)}) collective-permute-start(f32[256,128]{1,0:T(8,128)S(1)} %get-tuple-element.90), channel_id=1, source_target_pairs={{0,8},{4,12},{8,0},{12,4},{16,24},{20,28},{24,16},{28,20},{1,9},{5... | collective-permute-start | bytes 393224 | tf_op jit(solution)/shard_map/ppermute | solution.py:104
  37.9 3.4 %shard_map.119 = (bf16[256,1024]{1,0:T(8,128)(2,1)}, f32[256,1024]{1,0:T(8,128)S(1)}, f32[256,1024]{1,0:T(8,128)S(1)}, f32[8,256,128]{2,1,0:T(8,128)S(1)}) custom-call(bf16[256,1024]{1,0:T(8,128)(2,1)S(1)} %get-tuple-element.83.attn_grad_ref, bf16[256,1024]{1,0:T(8,128)(2,1)S(1)} %copy-done.2, bf16[256,1024]{1,0:T(8,128)(2,1)S(1)} %copy-done, ...), custom_call_target="tpu_custom_call" | custom-call | flops 671088640 | tf_op jit(solution)/shard_map/pallas_call | solution.py:25
  41.3 0.4 collective-permute-done.16.refs_1_
  41.6 2.5 %collective-permute-done.17.refs_2_ = f32[256,128]{1,0:T(8,128)S(1)} collective-permute-done((f32[256,128]{1,0:T(8,128)S(1)}, f32[256,128]{1,0:T(8,128)S(1)}, u32[]{:S(2)}, u32[]{:S(2)}) %collective-permute-start.17) | collective-permute-done | bytes 131104 | tf_op jit(solution)/shard_map/ppermute | solution.py:104
  44.3 0.9 %collective-permute-start.19 = (f32[264,128]{1,0:T(8,128)S(1)}, f32[264,128]{1,0:T(8,128)S(1)}, u32[]{:S(2)}, u32[]{:S(2)}) collective-permute-start(f32[264,128]{1,0:T(8,128)S(1)} %get-tuple-element.92), channel_id=1, source_target_pairs={{0,8},{4,12},{8,0},{12,4},{16,24},{20,28},{24,16},{28,20},{1,9},{5... | collective-permute-start | bytes 405512 | tf_op jit(solution)/shard_map/ppermute | solution.py:104
  45.3 2.9 %collective-permute-start.22 = (f32[256,128]{1,0:T(8,128)S(1)}, f32[256,128]{1,0:T(8,128)S(1)}, u32[]{:S(2)}, u32[]{:S(2)}) collective-permute-start(f32[256,128]{1,0:T(8,128)S(1)} %shard_map.121.refs_4_), channel_id=1, source_target_pairs={{0,16},{4,20},{8,24},{12,28},{16,0},{20,4},{24,8},{28,12},{1,17},{... | collective-permute-start | bytes 393224 | tf_op jit(solution)/shard_map/ppermute | solution.py:118
  48.2 0.9 %collective-permute-start.20 = (f32[256,128]{1,0:T(8,128)S(1)}, f32[256,128]{1,0:T(8,128)S(1)}, u32[]{:S(2)}, u32[]{:S(2)}) collective-permute-start(f32[256,128]{1,0:T(8,128)S(1)} %get-tuple-element.93), channel_id=1, source_target_pairs={{0,4},{4,0},{8,12},{12,8},{16,20},{20,16},{24,28},{28,24},{1,5},{5... | collective-permute-start | bytes 393224 | tf_op jit(solution)/shard_map/ppermute | solution.py:104
  49.2 1.2 %collective-permute-start.21 = (f32[256,128]{1,0:T(8,128)S(1)}, f32[256,128]{1,0:T(8,128)S(1)}, u32[]{:S(2)}, u32[]{:S(2)}) collective-permute-start(f32[256,128]{1,0:T(8,128)S(1)} %get-tuple-element.94), channel_id=1, source_target_pairs={{0,12},{4,8},{8,4},{12,0},{16,28},{20,24},{24,20},{28,16},{1,13},{... | collective-permute-start | bytes 393224 | tf_op jit(solution)/shard_map/ppermute | solution.py:104
  50.3 2.3 %collective-permute-done.22.refs_5_ = f32[256,128]{1,0:T(8,128)S(1)} collective-permute-done((f32[256,128]{1,0:T(8,128)S(1)}, f32[256,128]{1,0:T(8,128)S(1)}, u32[]{:S(2)}, u32[]{:S(2)}) %collective-permute-start.22) | collective-permute-done | bytes 131104 | tf_op jit(solution)/shard_map/ppermute | solution.py:118
  52.6 0.7 %collective-permute-done.19.refs_9_.refs_0_ = f32[264,128]{1,0:T(8,128)S(1)} collective-permute-done((f32[264,128]{1,0:T(8,128)S(1)}, f32[264,128]{1,0:T(8,128)S(1)}, u32[]{:S(2)}, u32[]{:S(2)}) %collective-permute-start.19) | collective-permute-done | bytes 135200 | tf_op jit(solution)/shard_map/ppermute | solution.py:104
  53.3 0.2 shard_map.122
  53.5 2.7 %collective-permute-start.23 = (f32[256,128]{1,0:T(8,128)S(1)}, f32[256,128]{1,0:T(8,128)S(1)}, u32[]{:S(2)}, u32[]{:S(2)}) collective-permute-start(f32[256,128]{1,0:T(8,128)S(1)} %get-tuple-element.96), channel_id=1, source_target_pairs={{0,8},{4,12},{8,0},{12,4},{16,24},{20,28},{24,16},{28,20},{1,9},{5... | collective-permute-start | bytes 393224 | tf_op jit(solution)/shard_map/ppermute | solution.py:104
  56.3 1.3 %collective-permute-start.24 = (f32[256,128]{1,0:T(8,128)S(1)}, f32[256,128]{1,0:T(8,128)S(1)}, u32[]{:S(2)}, u32[]{:S(2)}) collective-permute-start(f32[256,128]{1,0:T(8,128)S(1)} %get-tuple-element.97), channel_id=1, source_target_pairs={{0,4},{4,0},{8,12},{12,8},{16,20},{20,16},{24,28},{28,24},{1,5},{5... | collective-permute-start | bytes 393224 | tf_op jit(solution)/shard_map/ppermute | solution.py:104
  57.6 0.2 collective-permute-start.25
  57.8 1.0 %shard_map.123 = (bf16[256,1024]{1,0:T(8,128)(2,1)}, bf16[256,1024]{1,0:T(8,128)(2,1)}, f32[1024,128]{1,0:T(8,128)}) custom-call(f32[256,128]{1,0:T(8,128)S(1)} %get-tuple-element.95.refs_5_.refs_0_, f32[256,128]{1,0:T(8,128)S(1)} %get-tuple-element.103.refs_1_, f32[256,1024]{1,0:T(8,128)S(1)} %get-tuple-element.91.refs_6_.refs_2_, ...), custom_call_target="tpu_custom_call" | custom-call | tf_op jit(solution)/shard_map/pallas_call | solution.py:25
  58.8 1.6 %collective-permute-done.23.refs_3_ = f32[256,128]{1,0:T(8,128)S(1)} collective-permute-done((f32[256,128]{1,0:T(8,128)S(1)}, f32[256,128]{1,0:T(8,128)S(1)}, u32[]{:S(2)}, u32[]{:S(2)}) %collective-permute-start.23) | collective-permute-done | bytes 131104 | tf_op jit(solution)/shard_map/ppermute | solution.py:104
  60.4 1.8 %collective-permute-done.24.refs_4_ = f32[256,128]{1,0:T(8,128)S(1)} collective-permute-done((f32[256,128]{1,0:T(8,128)S(1)}, f32[256,128]{1,0:T(8,128)S(1)}, u32[]{:S(2)}, u32[]{:S(2)}) %collective-permute-start.24) | collective-permute-done | bytes 131104 | tf_op jit(solution)/shard_map/ppermute | solution.py:104
  62.2 1.4 %collective-permute-done.25.refs_5_ = f32[256,128]{1,0:T(8,128)S(1)} collective-permute-done((f32[256,128]{1,0:T(8,128)S(1)}, f32[256,128]{1,0:T(8,128)S(1)}, u32[]{:S(2)}, u32[]{:S(2)}) %collective-permute-start.25) | collective-permute-done | bytes 131104 | tf_op jit(solution)/shard_map/ppermute | solution.py:104
  63.5 1.4 %shard_map.124 = (bf16[256,1024]{1,0:T(8,128)(2,1)}, bf16[256,1024]{1,0:T(8,128)(2,1)}, f32[1024,128]{1,0:T(8,128)}) custom-call(f32[264,128]{1,0:T(8,128)S(1)} %collective-permute-done.19.refs_9_.refs_0_, f32[256,128]{1,0:T(8,128)S(1)} %collective-permute-done.20.refs_1_, ...), custom_call_target="tpu_custom_call", output_to_operand_aliasing={{0}: (14, {}), {1}: (15, {}), {2}: (16, {})} | custom-call | tf_op jit(solution)/shard_map/pallas_call | solution.py:25
  (32 shorter events, 0.8 us)
Async XLA Ops:
  2.8 8.0 %collective-permute-start = (f32[136,128]{1,0:T(8,128)S(1)}, f32[136,128]{1,0:T(8,128)S(1)}, u32[]{:S(2)}, u32[]{:S(2)}) collective-permute-start(f32[136,128]{1,0:T(8,128)S(1)} %get-tuple-element.58), channel_id=1, source_target_pairs={{0,12},{4,8},{8,4},{12,0},{16,28},{20,24},{24,20},{28,16},{1,13},{... | collective-permute-start | bytes 208904 | tf_op jit(solution)/shard_map/ppermute | solution.py:104
  6.9 5.1 %collective-permute-start.1 = (f32[136,128]{1,0:T(8,128)S(1)}, f32[136,128]{1,0:T(8,128)S(1)}, u32[]{:S(2)}, u32[]{:S(2)}) collective-permute-start(f32[136,128]{1,0:T(8,128)S(1)} %get-tuple-element.59), channel_id=1, source_target_pairs={{0,4},{4,0},{8,12},{12,8},{16,20},{20,16},{24,28},{28,24},{1,5},{5... | collective-permute-start | bytes 208904 | tf_op jit(solution)/shard_map/ppermute | solution.py:104
  7.4 4.6 %collective-permute-start.2 = (f32[136,128]{1,0:T(8,128)S(1)}, f32[136,128]{1,0:T(8,128)S(1)}, u32[]{:S(2)}, u32[]{:S(2)}) collective-permute-start(f32[136,128]{1,0:T(8,128)S(1)} %get-tuple-element.60), channel_id=1, source_target_pairs={{0,8},{4,12},{8,0},{12,4},{16,24},{20,28},{24,16},{28,20},{1,9},{5... | collective-permute-start | bytes 208904 | tf_op jit(solution)/shard_map/ppermute | solution.py:104
  7.5 7.2 %collective-permute-start.6 = (f32[128,128]{1,0:T(8,128)S(1)}, f32[128,128]{1,0:T(8,128)S(1)}, u32[]{:S(2)}, u32[]{:S(2)}) collective-permute-start(f32[128,128]{1,0:T(8,128)S(1)} %get-tuple-element.67), channel_id=1, source_target_pairs={{0,12},{4,8},{8,4},{12,0},{16,28},{20,24},{24,20},{28,16},{1,13},{... | collective-permute-start | bytes 196616 | tf_op jit(solution)/shard_map/ppermute | solution.py:104
  10.3 4.3 %collective-permute-start.7 = (f32[128,128]{1,0:T(8,128)S(1)}, f32[128,128]{1,0:T(8,128)S(1)}, u32[]{:S(2)}, u32[]{:S(2)}) collective-permute-start(f32[128,128]{1,0:T(8,128)S(1)} %get-tuple-element.68), channel_id=1, source_target_pairs={{0,4},{4,0},{8,12},{12,8},{16,20},{20,16},{24,28},{28,24},{1,5},{5... | collective-permute-start | bytes 196616 | tf_op jit(solution)/shard_map/ppermute | solution.py:104
  10.9 4.3 %collective-permute-start.8 = (f32[128,128]{1,0:T(8,128)S(1)}, f32[128,128]{1,0:T(8,128)S(1)}, u32[]{:S(2)}, u32[]{:S(2)}) collective-permute-start(f32[128,128]{1,0:T(8,128)S(1)} %get-tuple-element.69), channel_id=1, source_target_pairs={{0,8},{4,12},{8,0},{12,4},{16,24},{20,28},{24,16},{28,20},{1,9},{5... | collective-permute-start | bytes 196616 | tf_op jit(solution)/shard_map/ppermute | solution.py:104
  12.0 7.3 %collective-permute-start.3 = (f32[136,128]{1,0:T(8,128)S(1)}, f32[136,128]{1,0:T(8,128)S(1)}, u32[]{:S(2)}, u32[]{:S(2)}) collective-permute-start(f32[136,128]{1,0:T(8,128)S(1)} %get-tuple-element.61.refs_4_), channel_id=1, source_target_pairs={{0,16},{4,20},{8,24},{12,28},{16,0},{20,4},{24,8},{28,12},{1,17},{... | collective-permute-start | bytes 208904 | tf_op jit(solution)/shard_map/ppermute | solution.py:118
  15.2 4.2 %copy-start.3 = (f32[8,128,128]{2,1,0:T(8,128)S(1)}, f32[8,128,128]{2,1,0:T(8,128)}, u32[]{:S(2)}) copy-start(f32[8,128,128]{2,1,0:T(8,128)} %param.14) | copy-start | bytes 1572868
  15.2 10.4 %copy-start.5 = (bf16[256,1024]{1,0:T(8,128)(2,1)S(1)}, bf16[256,1024]{1,0:T(8,128)(2,1)}, u32[]{:S(2)}) copy-start(bf16[256,1024]{1,0:T(8,128)(2,1)} %upstream_ref.1) | copy-start | bytes 1572868
  15.3 5.7 %collective-permute-start.9 = (f32[128,128]{1,0:T(8,128)S(1)}, f32[128,128]{1,0:T(8,128)S(1)}, u32[]{:S(2)}, u32[]{:S(2)}) collective-permute-start(f32[128,128]{1,0:T(8,128)S(1)} %shard_map.114.refs_4_), channel_id=1, source_target_pairs={{0,16},{4,20},{8,24},{12,28},{16,0},{20,4},{24,8},{28,12},{1,17},{... | collective-permute-start | bytes 196616 | tf_op jit(solution)/shard_map/ppermute | solution.py:118
  19.4 6.3 %copy-start.1 = (bf16[256,1024]{1,0:T(8,128)(2,1)S(1)}, bf16[256,1024]{1,0:T(8,128)(2,1)}, u32[]{:S(2)}) copy-start(bf16[256,1024]{1,0:T(8,128)(2,1)} %refs_9_.1) | copy-start | bytes 1572868
  19.4 6.3 %copy-start.2 = (bf16[256,1024]{1,0:T(8,128)(2,1)S(1)}, bf16[256,1024]{1,0:T(8,128)(2,1)}, u32[]{:S(2)}) copy-start(bf16[256,1024]{1,0:T(8,128)(2,1)} %query_ref.3) | copy-start | bytes 1572868
  19.5 6.2 %copy-start = (bf16[256,1024]{1,0:T(8,128)(2,1)S(1)}, bf16[256,1024]{1,0:T(8,128)(2,1)}, u32[]{:S(2)}) copy-start(bf16[256,1024]{1,0:T(8,128)(2,1)} %refs_8_.3) | copy-start | bytes 1572868
  19.5 5.7 %collective-permute-start.4 = (f32[128,128]{1,0:T(8,128)S(1)}, f32[128,128]{1,0:T(8,128)S(1)}, u32[]{:S(2)}, u32[]{:S(2)}) collective-permute-start(f32[128,128]{1,0:T(8,128)S(1)} %get-tuple-element.64), channel_id=1, source_target_pairs={{0,4},{4,0},{8,12},{12,8},{16,20},{20,16},{24,28},{28,24},{1,5},{5... | collective-permute-start | bytes 196616 | tf_op jit(solution)/shard_map/ppermute | solution.py:104
  20.6 5.0 %collective-permute-start.5 = (f32[128,128]{1,0:T(8,128)S(1)}, f32[128,128]{1,0:T(8,128)S(1)}, u32[]{:S(2)}, u32[]{:S(2)}) collective-permute-start(f32[128,128]{1,0:T(8,128)S(1)} %get-tuple-element.65), channel_id=1, source_target_pairs={{0,8},{4,12},{8,0},{12,4},{16,24},{20,28},{24,16},{28,20},{1,9},{5... | collective-permute-start | bytes 196616 | tf_op jit(solution)/shard_map/ppermute | solution.py:104
  21.1 7.5 %collective-permute-start.12 = (f32[256,128]{1,0:T(8,128)S(1)}, f32[256,128]{1,0:T(8,128)S(1)}, u32[]{:S(2)}, u32[]{:S(2)}) collective-permute-start(f32[256,128]{1,0:T(8,128)S(1)} %get-tuple-element.75), channel_id=1, source_target_pairs={{0,12},{4,8},{8,4},{12,0},{16,28},{20,24},{24,20},{28,16},{1,13},{... | collective-permute-start | bytes 393224 | tf_op jit(solution)/shard_map/ppermute | solution.py:104
  23.2 2.5 %copy-start.6 = (f32[1024]{0:T(1024)S(1)}, f32[1024]{0:T(1024)}, u32[]{:S(2)}) copy-start(f32[1024]{0:T(1024)} %param.13) | copy-start | bytes 12292
  23.2 4.9 %collective-permute-start.10 = (f32[128,128]{1,0:T(8,128)S(1)}, f32[128,128]{1,0:T(8,128)S(1)}, u32[]{:S(2)}, u32[]{:S(2)}) collective-permute-start(f32[128,128]{1,0:T(8,128)S(1)} %get-tuple-element.73), channel_id=1, source_target_pairs={{0,4},{4,0},{8,12},{12,8},{16,20},{20,16},{24,28},{28,24},{1,5},{5... | collective-permute-start | bytes 196616 | tf_op jit(solution)/shard_map/ppermute | solution.py:104
  24.3 4.3 %collective-permute-start.11 = (f32[128,128]{1,0:T(8,128)S(1)}, f32[128,128]{1,0:T(8,128)S(1)}, u32[]{:S(2)}, u32[]{:S(2)}) collective-permute-start(f32[128,128]{1,0:T(8,128)S(1)} %get-tuple-element.74), channel_id=1, source_target_pairs={{0,8},{4,12},{8,0},{12,4},{16,24},{20,28},{24,16},{28,20},{1,9},{5... | collective-permute-start | bytes 196616 | tf_op jit(solution)/shard_map/ppermute | solution.py:104
  29.2 3.1 %collective-permute-start.15 = (f32[8,256]{1,0:T(8,128)S(1)}, f32[8,256]{1,0:T(8,128)S(1)}, u32[]{:S(2)}, u32[]{:S(2)}) collective-permute-start(f32[8,256]{1,0:T(8,128)S(1)} %get-tuple-element.80.refs_0_), channel_id=1, source_target_pairs={{0,1},{1,2},{2,3},{3,0},{4,5},{5,6},{6,7},{7,4},{8,9},{9,10},{10,1... | collective-permute-start | bytes 24584 | tf_op jit(solution)/shard_map/ppermute | solution.py:578
  29.2 3.7 %collective-permute-start.14 = (f32[8,256]{1,0:T(8,128)S(1)}, f32[8,256]{1,0:T(8,128)S(1)}, u32[]{:S(2)}, u32[]{:S(2)}) collective-permute-start(f32[8,256]{1,0:T(8,128)S(1)} %get-tuple-element.80.refs_0_), channel_id=1, source_target_pairs={{0,2},{1,3},{2,0},{3,1},{4,6},{5,7},{6,4},{7,5},{8,10},{9,11},{10,... | collective-permute-start | bytes 24584 | tf_op jit(solution)/shard_map/ppermute | solution.py:578
  30.8 2.8 %collective-permute-start.13 = (f32[8,256]{1,0:T(8,128)S(1)}, f32[8,256]{1,0:T(8,128)S(1)}, u32[]{:S(2)}, u32[]{:S(2)}) collective-permute-start(f32[8,256]{1,0:T(8,128)S(1)} %get-tuple-element.80.refs_0_), channel_id=1, source_target_pairs={{0,3},{1,0},{2,1},{3,2},{4,7},{5,4},{6,5},{7,6},{8,11},{9,8},{10,9... | collective-permute-start | bytes 24584 | tf_op jit(solution)/shard_map/ppermute | solution.py:578
  34.3 7.3 %collective-permute-start.16 = (f32[256,128]{1,0:T(8,128)S(1)}, f32[256,128]{1,0:T(8,128)S(1)}, u32[]{:S(2)}, u32[]{:S(2)}) collective-permute-start(f32[256,128]{1,0:T(8,128)S(1)} %get-tuple-element.88), channel_id=1, source_target_pairs={{0,12},{4,8},{8,4},{12,0},{16,28},{20,24},{24,20},{28,16},{1,13},{... | collective-permute-start | bytes 393224 | tf_op jit(solution)/shard_map/ppermute | solution.py:104
  35.8 8.3 %collective-permute-start.17 = (f32[256,128]{1,0:T(8,128)S(1)}, f32[256,128]{1,0:T(8,128)S(1)}, u32[]{:S(2)}, u32[]{:S(2)}) collective-permute-start(f32[256,128]{1,0:T(8,128)S(1)} %get-tuple-element.89), channel_id=1, source_target_pairs={{0,4},{4,0},{8,12},{12,8},{16,20},{20,16},{24,28},{28,24},{1,5},{5... | collective-permute-start | bytes 393224 | tf_op jit(solution)/shard_map/ppermute | solution.py:104
  36.7 7.4 %collective-permute-start.18 = (f32[256,128]{1,0:T(8,128)S(1)}, f32[256,128]{1,0:T(8,128)S(1)}, u32[]{:S(2)}, u32[]{:S(2)}) collective-permute-start(f32[256,128]{1,0:T(8,128)S(1)} %get-tuple-element.90), channel_id=1, source_target_pairs={{0,8},{4,12},{8,0},{12,4},{16,24},{20,28},{24,16},{28,20},{1,9},{5... | collective-permute-start | bytes 393224 | tf_op jit(solution)/shard_map/ppermute | solution.py:104
  37.9 6.2 %copy-start.4 = (f32[8,128,128]{2,1,0:T(8,128)S(1)}, f32[8,128,128]{2,1,0:T(8,128)}, u32[]{:S(2)}) copy-start(f32[8,128,128]{2,1,0:T(8,128)} %param.15) | copy-start | bytes 1572868
  44.3 9.0 %collective-permute-start.19 = (f32[264,128]{1,0:T(8,128)S(1)}, f32[264,128]{1,0:T(8,128)S(1)}, u32[]{:S(2)}, u32[]{:S(2)}) collective-permute-start(f32[264,128]{1,0:T(8,128)S(1)} %get-tuple-element.92), channel_id=1, source_target_pairs={{0,8},{4,12},{8,0},{12,4},{16,24},{20,28},{24,16},{28,20},{1,9},{5... | collective-permute-start | bytes 405512 | tf_op jit(solution)/shard_map/ppermute | solution.py:104
  45.3 7.3 %collective-permute-start.22 = (f32[256,128]{1,0:T(8,128)S(1)}, f32[256,128]{1,0:T(8,128)S(1)}, u32[]{:S(2)}, u32[]{:S(2)}) collective-permute-start(f32[256,128]{1,0:T(8,128)S(1)} %shard_map.121.refs_4_), channel_id=1, source_target_pairs={{0,16},{4,20},{8,24},{12,28},{16,0},{20,4},{24,8},{28,12},{1,17},{... | collective-permute-start | bytes 393224 | tf_op jit(solution)/shard_map/ppermute | solution.py:118
  48.2 10.6 %collective-permute-start.20 = (f32[256,128]{1,0:T(8,128)S(1)}, f32[256,128]{1,0:T(8,128)S(1)}, u32[]{:S(2)}, u32[]{:S(2)}) collective-permute-start(f32[256,128]{1,0:T(8,128)S(1)} %get-tuple-element.93), channel_id=1, source_target_pairs={{0,4},{4,0},{8,12},{12,8},{16,20},{20,16},{24,28},{28,24},{1,5},{5... | collective-permute-start | bytes 393224 | tf_op jit(solution)/shard_map/ppermute | solution.py:104
  49.2 9.6 %collective-permute-start.21 = (f32[256,128]{1,0:T(8,128)S(1)}, f32[256,128]{1,0:T(8,128)S(1)}, u32[]{:S(2)}, u32[]{:S(2)}) collective-permute-start(f32[256,128]{1,0:T(8,128)S(1)} %get-tuple-element.94), channel_id=1, source_target_pairs={{0,12},{4,8},{8,4},{12,0},{16,28},{20,24},{24,20},{28,16},{1,13},{... | collective-permute-start | bytes 393224 | tf_op jit(solution)/shard_map/ppermute | solution.py:104
  53.5 6.8 %collective-permute-start.23 = (f32[256,128]{1,0:T(8,128)S(1)}, f32[256,128]{1,0:T(8,128)S(1)}, u32[]{:S(2)}, u32[]{:S(2)}) collective-permute-start(f32[256,128]{1,0:T(8,128)S(1)} %get-tuple-element.96), channel_id=1, source_target_pairs={{0,8},{4,12},{8,0},{12,4},{16,24},{20,28},{24,16},{28,20},{1,9},{5... | collective-permute-start | bytes 393224 | tf_op jit(solution)/shard_map/ppermute | solution.py:104
  56.3 5.9 %collective-permute-start.24 = (f32[256,128]{1,0:T(8,128)S(1)}, f32[256,128]{1,0:T(8,128)S(1)}, u32[]{:S(2)}, u32[]{:S(2)}) collective-permute-start(f32[256,128]{1,0:T(8,128)S(1)} %get-tuple-element.97), channel_id=1, source_target_pairs={{0,4},{4,0},{8,12},{12,8},{16,20},{20,16},{24,28},{28,24},{1,5},{5... | collective-permute-start | bytes 393224 | tf_op jit(solution)/shard_map/ppermute | solution.py:104
  57.6 5.9 %collective-permute-start.25 = (f32[256,128]{1,0:T(8,128)S(1)}, f32[256,128]{1,0:T(8,128)S(1)}, u32[]{:S(2)}, u32[]{:S(2)}) collective-permute-start(f32[256,128]{1,0:T(8,128)S(1)} %get-tuple-element.98), channel_id=1, source_target_pairs={{0,12},{4,8},{8,4},{12,0},{16,28},{20,24},{24,20},{28,16},{1,13},{... | collective-permute-start | bytes 393224 | tf_op jit(solution)/shard_map/ppermute | solution.py:104

commit v15 on v14

--- a/solution.py
+++ b/solution.py
@@ -576,7 +576,7 @@
     )
     all_sums = [sums] + [
         lax.ppermute(sums, "head", [(i, (i + step) % parties) for i in range(parties)])
-        for step in reversed(range(1, parties))
+        for step in range(1, parties)
     ]
     attn_grad, summary, *sends = call(
         bind(attn_grad_body, parties),

time: 65.2 us -> 62.5 us (0.959)
  waiting for transfers between devices: 16.9 us -> 15 us
  starting transfers between devices: 35.9 us -> 35.2 us
    ppermute x20, waiting for transfers between devices: 11.8 us -> 9.1 us  [swap(): return lax.ppermute(piece, 'seq', pairs) if way else piece]
    ppermute x3, waiting for transfers between devices: 1.37 us -> 2.85 us  [on_device(): lax.ppermute(sums, 'head', [(i, (i + step) % parties) for i in range(part...]
    ppermute x3, starting transfers between devices: 3.04 us -> 1.8 us  [on_device(): lax.ppermute(sums, 'head', [(i, (i + step) % parties) for i in range(part...]
    ppermute x3, waiting for transfers between devices: 3.81 us -> 3.04 us  [from_groups(): lax.ppermute(piece, 'seq', [(i, (i + step * self.members) % self.blocks)...]
  transfers between devices with their start and end apart: 26 -> 26, of which waited for: 17 -> 13; matrix products, arithmetic and copies ran while one was open for 0% -> 0% of each run, Pallas kernels for 9% -> 10%
where the time goes in v15:
time: 62.5 us; the launch traced here: 62.3 us
  starting transfers between devices  35.2 us (56%)
  waiting for transfers between devices  15 us (24%)
  Pallas kernels  11.3 us (18%)
  between operations  0.78 us (1%)
    ppermute x20, starting transfers between devices, swap(): return lax.ppermute(piece, 'seq', pairs) if way else piece  25.2 us
    pallas_call x14, Pallas kernels, call(): pl.pallas_call(body, out_shape=outs, in_specs=specs or [VMEM] * len(opera...  11.3 us
    ppermute x20, waiting for transfers between devices, swap(): return lax.ppermute(piece, 'seq', pairs) if way else piece  9.1 us
    ppermute x3, starting transfers between devices, from_groups(): lax.ppermute(piece, 'seq', [(i, (i + step * self.members) % self.blocks)...  8.11 us
    ppermute x3, waiting for transfers between devices, from_groups(): lax.ppermute(piece, 'seq', [(i, (i + step * self.members) % self.blocks)...  3.04 us
    ppermute x3, waiting for transfers between devices, on_device(): lax.ppermute(sums, 'head', [(i, (i + step) % parties) for i in range(part...  2.85 us
    ppermute x3, starting transfers between devices, on_device(): lax.ppermute(sums, 'head', [(i, (i + step) % parties) for i in range(part...  1.8 us
  transfers between devices with their start and end apart: 26, of which 13 were waited for; matrix products, arithmetic and copies ran while one was open for 0% of the time, Pallas kernels for 10%

profile of v15, /device:TPU:0, one launch (start us, length us, event | category | flops | bytes accessed | tf_op | source)
XLA Modules:
  0.0 62.3 jit_solution(4897134732621334027)
XLA Ops:
  0.6 2.2 %shard_map.111 = (f32[136,128]{1,0:T(8,128)S(1)}, f32[136,128]{1,0:T(8,128)S(1)}, f32[136,128]{1,0:T(8,128)S(1)}, f32[136,128]{1,0:T(8,128)S(1)}, f32[128,128]{1...) custom-call(bf16[256,1024]{1,0:T(8,128)(2,1)} %refs_8_.3, ...), custom_call_target="tpu_custom_call" | custom-call | tf_op jit(solution)/shard_map/pallas_call | solution.py:25
  2.8 4.0 %collective-permute-start = (f32[136,128]{1,0:T(8,128)S(1)}, f32[136,128]{1,0:T(8,128)S(1)}, u32[]{:S(2)}, u32[]{:S(2)}) collective-permute-start(f32[136,128]{1,0:T(8,128)S(1)} %get-tuple-element.58), channel_id=1, source_target_pairs={{0,12},{4,8},{8,4},{12,0},{16,28},{20,24},{24,20},{28,16},{1,13},{... | collective-permute-start | bytes 208904 | tf_op jit(solution)/shard_map/ppermute | solution.py:104
  6.9 0.5 collective-permute-start.1
  7.4 0.1 collective-permute-start.2
  7.5 2.8 %collective-permute-start.6 = (f32[128,128]{1,0:T(8,128)S(1)}, f32[128,128]{1,0:T(8,128)S(1)}, u32[]{:S(2)}, u32[]{:S(2)}) collective-permute-start(f32[128,128]{1,0:T(8,128)S(1)} %get-tuple-element.67), channel_id=1, source_target_pairs={{0,12},{4,8},{8,4},{12,0},{16,28},{20,24},{24,20},{28,16},{1,13},{... | collective-permute-start | bytes 196616 | tf_op jit(solution)/shard_map/ppermute | solution.py:104
  10.3 0.5 collective-permute-start.7
  10.9 0.8 %collective-permute-start.8 = (f32[128,128]{1,0:T(8,128)S(1)}, f32[128,128]{1,0:T(8,128)S(1)}, u32[]{:S(2)}, u32[]{:S(2)}) collective-permute-start(f32[128,128]{1,0:T(8,128)S(1)} %get-tuple-element.69), channel_id=1, source_target_pairs={{0,8},{4,12},{8,0},{12,4},{16,24},{20,28},{24,16},{28,20},{1,9},{5... | collective-permute-start | bytes 196616 | tf_op jit(solution)/shard_map/ppermute | solution.py:104
  11.6 0.4 collective-permute-done.1.refs_2_
  12.0 2.7 %collective-permute-start.3 = (f32[136,128]{1,0:T(8,128)S(1)}, f32[136,128]{1,0:T(8,128)S(1)}, u32[]{:S(2)}, u32[]{:S(2)}) collective-permute-start(f32[136,128]{1,0:T(8,128)S(1)} %get-tuple-element.61.refs_4_), channel_id=1, source_target_pairs={{0,16},{4,20},{8,24},{12,28},{16,0},{20,4},{24,8},{28,12},{1,17},{... | collective-permute-start | bytes 208904 | tf_op jit(solution)/shard_map/ppermute | solution.py:118
  14.7 0.5 collective-permute-done.8.refs_3_
  15.3 2.6 %collective-permute-start.9 = (f32[128,128]{1,0:T(8,128)S(1)}, f32[128,128]{1,0:T(8,128)S(1)}, u32[]{:S(2)}, u32[]{:S(2)}) collective-permute-start(f32[128,128]{1,0:T(8,128)S(1)} %shard_map.114.refs_4_), channel_id=1, source_target_pairs={{0,16},{4,20},{8,24},{12,28},{16,0},{20,4},{24,8},{28,12},{1,17},{... | collective-permute-start | bytes 196616 | tf_op jit(solution)/shard_map/ppermute | solution.py:118
  17.8 1.5 %collective-permute-done.3.refs_5_ = f32[136,128]{1,0:T(8,128)S(1)} collective-permute-done((f32[136,128]{1,0:T(8,128)S(1)}, f32[136,128]{1,0:T(8,128)S(1)}, u32[]{:S(2)}, u32[]{:S(2)}) %collective-permute-start.3) | collective-permute-done | bytes 69664 | tf_op jit(solution)/shard_map/ppermute | solution.py:118
  19.4 0.1 shard_map.113
  19.5 1.1 %collective-permute-start.4 = (f32[128,128]{1,0:T(8,128)S(1)}, f32[128,128]{1,0:T(8,128)S(1)}, u32[]{:S(2)}, u32[]{:S(2)}) collective-permute-start(f32[128,128]{1,0:T(8,128)S(1)} %get-tuple-element.64), channel_id=1, source_target_pairs={{0,4},{4,0},{8,12},{12,8},{16,20},{20,16},{24,28},{28,24},{1,5},{5... | collective-permute-start | bytes 196616 | tf_op jit(solution)/shard_map/ppermute | solution.py:104
  20.6 0.3 collective-permute-start.5
  21.1 2.1 %collective-permute-start.12 = (f32[256,128]{1,0:T(8,128)S(1)}, f32[256,128]{1,0:T(8,128)S(1)}, u32[]{:S(2)}, u32[]{:S(2)}) collective-permute-start(f32[256,128]{1,0:T(8,128)S(1)} %get-tuple-element.75), channel_id=1, source_target_pairs={{0,12},{4,8},{8,4},{12,0},{16,28},{20,24},{24,20},{28,16},{1,13},{... | collective-permute-start | bytes 393224 | tf_op jit(solution)/shard_map/ppermute | solution.py:104
  23.2 1.1 %collective-permute-start.10 = (f32[128,128]{1,0:T(8,128)S(1)}, f32[128,128]{1,0:T(8,128)S(1)}, u32[]{:S(2)}, u32[]{:S(2)}) collective-permute-start(f32[128,128]{1,0:T(8,128)S(1)} %get-tuple-element.73), channel_id=1, source_target_pairs={{0,4},{4,0},{8,12},{12,8},{16,20},{20,16},{24,28},{28,24},{1,5},{5... | collective-permute-start | bytes 196616 | tf_op jit(solution)/shard_map/ppermute | solution.py:104
  24.3 0.3 collective-permute-start.11
  24.6 0.6 collective-permute-done.4.refs_0_.refs_1_
  25.2 0.4 collective-permute-done.5.refs_1_.refs_2_
  25.7 1.2 %shard_map.116 = (bf16[8,256,256]{2,1,0:T(8,128)(2,1)S(1)}, f32[256,1024]{1,0:T(8,128)S(1)}, f32[256,1024]{1,0:T(8,128)S(1)}, bf16[8,128,256]{2,1,0:T(8,128)(2,1)S(1)}) custom-call(bf16[256,1024]{1,0:T(8,128)(2,1)S(1)} %copy-done.2, bf16[256,1024]{1,0:T(8,128)(2,1)S(1)} %copy-done, bf16[256,1024]{1,0:T(8,128)(2,1)S(1)} %copy-done.1, ...), custom_call_target="tpu_custom_call" | custom-call | flops 1000000000 | tf_op jit(solution)/shard_map/pallas_call | solution.py:25
  26.9 1.2 %collective-permute-done.10.refs_4_ = f32[128,128]{1,0:T(8,128)S(1)} collective-permute-done((f32[128,128]{1,0:T(8,128)S(1)}, f32[128,128]{1,0:T(8,128)S(1)}, u32[]{:S(2)}, u32[]{:S(2)}) %collective-permute-start.10) | collective-permute-done | bytes 65568 | tf_op jit(solution)/shard_map/ppermute | solution.py:104
  28.1 0.4 collective-permute-done.11.refs_5_
  28.5 0.7 %shard_map.117 = (f32[256,1024]{1,0:T(8,128)S(1)}, f32[8,256]{1,0:T(8,128)S(1)}, bf16[1024,128]{1,0:T(8,128)(2,1)S(1)}) custom-call(f32[128,128]{1,0:T(8,128)S(1)} %get-tuple-element.63.refs_0_, f32[128,128]{1,0:T(8,128)S(1)} %collective-permute-done.4.refs_0_.refs_1_, f32[128,128]{1,0:T(8,128)S(1)} %collective-permute-done.5.refs_1_.refs_2_, ...), custom_call_target="tpu_custom_call" | custom-call | tf_op jit(solution)/shard_map/pallas_call | solution.py:25
  29.2 1.6 %collective-permute-start.14 = (f32[8,256]{1,0:T(8,128)S(1)}, f32[8,256]{1,0:T(8,128)S(1)}, u32[]{:S(2)}, u32[]{:S(2)}) collective-permute-start(f32[8,256]{1,0:T(8,128)S(1)} %get-tuple-element.80.refs_0_), channel_id=1, source_target_pairs={{0,2},{1,3},{2,0},{3,1},{4,6},{5,7},{6,4},{7,5},{8,10},{9,11},{10,... | collective-permute-start | bytes 24584 | tf_op jit(solution)/shard_map/ppermute | solution.py:578
  30.8 0.2 collective-permute-start.13
  31.0 1.9 %collective-permute-done.14.refs_2_ = f32[8,256]{1,0:T(8,128)S(1)} collective-permute-done((f32[8,256]{1,0:T(8,128)S(1)}, f32[8,256]{1,0:T(8,128)S(1)}, u32[]{:S(2)}, u32[]{:S(2)}) %collective-permute-start.14) | collective-permute-done | bytes 8224 | tf_op jit(solution)/shard_map/ppermute | solution.py:578
  32.9 1.0 %collective-permute-done.13.refs_1_ = f32[8,256]{1,0:T(8,128)S(1)} collective-permute-done((f32[8,256]{1,0:T(8,128)S(1)}, f32[8,256]{1,0:T(8,128)S(1)}, u32[]{:S(2)}, u32[]{:S(2)}) %collective-permute-start.13) | collective-permute-done | bytes 8224 | tf_op jit(solution)/shard_map/ppermute | solution.py:578
  33.9 0.7 %shard_map.118 = (bf16[256,1024]{1,0:T(8,128)(2,1)S(1)}, f32[1024,128]{1,0:T(8,128)S(1)}, f32[256,128]{1,0:T(8,128)S(1)}, f32[256,128]{1,0:T(8,128)S(1)}, f32[25...) custom-call(f32[8,256]{1,0:T(8,128)S(1)} %get-tuple-element.80.refs_0_, f32[8,256]{1,0:T(8,128)S(1)} %collective-permute-done.13.refs_1_, ...), custom_call_target="tpu_custom_call" | custom-call | tf_op jit(solution)/shard_map/pallas_call | solution.py:25
  34.6 1.4 %collective-permute-start.16 = (f32[256,128]{1,0:T(8,128)S(1)}, f32[256,128]{1,0:T(8,128)S(1)}, u32[]{:S(2)}, u32[]{:S(2)}) collective-permute-start(f32[256,128]{1,0:T(8,128)S(1)} %get-tuple-element.88), channel_id=1, source_target_pairs={{0,12},{4,8},{8,4},{12,0},{16,28},{20,24},{24,20},{28,16},{1,13},{... | collective-permute-start | bytes 393224 | tf_op jit(solution)/shard_map/ppermute | solution.py:104
  36.0 0.9 %collective-permute-start.17 = (f32[256,128]{1,0:T(8,128)S(1)}, f32[256,128]{1,0:T(8,128)S(1)}, u32[]{:S(2)}, u32[]{:S(2)}) collective-permute-start(f32[256,128]{1,0:T(8,128)S(1)} %get-tuple-element.89), channel_id=1, source_target_pairs={{0,4},{4,0},{8,12},{12,8},{16,20},{20,16},{24,28},{28,24},{1,5},{5... | collective-permute-start | bytes 393224 | tf_op jit(solution)/shard_map/ppermute | solution.py:104
  37.0 1.2 %collective-permute-start.18 = (f32[256,128]{1,0:T(8,128)S(1)}, f32[256,128]{1,0:T(8,128)S(1)}, u32[]{:S(2)}, u32[]{:S(2)}) collective-permute-start(f32[256,128]{1,0:T(8,128)S(1)} %get-tuple-element.90), channel_id=1, source_target_pairs={{0,8},{4,12},{8,0},{12,4},{16,24},{20,28},{24,16},{28,20},{1,9},{5... | collective-permute-start | bytes 393224 | tf_op jit(solution)/shard_map/ppermute | solution.py:104
  38.1 3.4 %shard_map.119 = (bf16[256,1024]{1,0:T(8,128)(2,1)}, f32[256,1024]{1,0:T(8,128)S(1)}, f32[256,1024]{1,0:T(8,128)S(1)}, f32[8,256,128]{2,1,0:T(8,128)S(1)}) custom-call(bf16[256,1024]{1,0:T(8,128)(2,1)S(1)} %get-tuple-element.83.attn_grad_ref, bf16[256,1024]{1,0:T(8,128)(2,1)S(1)} %copy-done.2, bf16[256,1024]{1,0:T(8,128)(2,1)S(1)} %copy-done, ...), custom_call_target="tpu_custom_call" | custom-call | flops 671088640 | tf_op jit(solution)/shard_map/pallas_call | solution.py:25
  41.5 0.7 %collective-permute-done.17.refs_2_ = f32[256,128]{1,0:T(8,128)S(1)} collective-permute-done((f32[256,128]{1,0:T(8,128)S(1)}, f32[256,128]{1,0:T(8,128)S(1)}, u32[]{:S(2)}, u32[]{:S(2)}) %collective-permute-start.17) | collective-permute-done | bytes 131104 | tf_op jit(solution)/shard_map/ppermute | solution.py:104
  42.2 0.2 shard_map.120
  42.4 1.0 %collective-permute-start.19 = (f32[264,128]{1,0:T(8,128)S(1)}, f32[264,128]{1,0:T(8,128)S(1)}, u32[]{:S(2)}, u32[]{:S(2)}) collective-permute-start(f32[264,128]{1,0:T(8,128)S(1)} %get-tuple-element.92), channel_id=1, source_target_pairs={{0,8},{4,12},{8,0},{12,4},{16,24},{20,28},{24,16},{28,20},{1,9},{5... | collective-permute-start | bytes 405512 | tf_op jit(solution)/shard_map/ppermute | solution.py:104
  43.4 0.1 shard_map.121.refs_4_
  43.5 2.9 %collective-permute-start.22 = (f32[256,128]{1,0:T(8,128)S(1)}, f32[256,128]{1,0:T(8,128)S(1)}, u32[]{:S(2)}, u32[]{:S(2)}) collective-permute-start(f32[256,128]{1,0:T(8,128)S(1)} %shard_map.121.refs_4_), channel_id=1, source_target_pairs={{0,16},{4,20},{8,24},{12,28},{16,0},{20,4},{24,8},{28,12},{1,17},{... | collective-permute-start | bytes 393224 | tf_op jit(solution)/shard_map/ppermute | solution.py:118
  46.3 1.0 %collective-permute-start.20 = (f32[256,128]{1,0:T(8,128)S(1)}, f32[256,128]{1,0:T(8,128)S(1)}, u32[]{:S(2)}, u32[]{:S(2)}) collective-permute-start(f32[256,128]{1,0:T(8,128)S(1)} %get-tuple-element.93), channel_id=1, source_target_pairs={{0,4},{4,0},{8,12},{12,8},{16,20},{20,16},{24,28},{28,24},{1,5},{5... | collective-permute-start | bytes 393224 | tf_op jit(solution)/shard_map/ppermute | solution.py:104
  47.3 1.4 %collective-permute-start.21 = (f32[256,128]{1,0:T(8,128)S(1)}, f32[256,128]{1,0:T(8,128)S(1)}, u32[]{:S(2)}, u32[]{:S(2)}) collective-permute-start(f32[256,128]{1,0:T(8,128)S(1)} %get-tuple-element.94), channel_id=1, source_target_pairs={{0,12},{4,8},{8,4},{12,0},{16,28},{20,24},{24,20},{28,16},{1,13},{... | collective-permute-start | bytes 393224 | tf_op jit(solution)/shard_map/ppermute | solution.py:104
  48.8 1.5 %collective-permute-done.22.refs_5_ = f32[256,128]{1,0:T(8,128)S(1)} collective-permute-done((f32[256,128]{1,0:T(8,128)S(1)}, f32[256,128]{1,0:T(8,128)S(1)}, u32[]{:S(2)}, u32[]{:S(2)}) %collective-permute-start.22) | collective-permute-done | bytes 131104 | tf_op jit(solution)/shard_map/ppermute | solution.py:118
  50.3 0.2 shard_map.122
  50.5 2.1 %collective-permute-start.23 = (f32[256,128]{1,0:T(8,128)S(1)}, f32[256,128]{1,0:T(8,128)S(1)}, u32[]{:S(2)}, u32[]{:S(2)}) collective-permute-start(f32[256,128]{1,0:T(8,128)S(1)} %get-tuple-element.96), channel_id=1, source_target_pairs={{0,8},{4,12},{8,0},{12,4},{16,24},{20,28},{24,16},{28,20},{1,9},{5... | collective-permute-start | bytes 393224 | tf_op jit(solution)/shard_map/ppermute | solution.py:104
  52.6 2.4 %collective-permute-start.24 = (f32[256,128]{1,0:T(8,128)S(1)}, f32[256,128]{1,0:T(8,128)S(1)}, u32[]{:S(2)}, u32[]{:S(2)}) collective-permute-start(f32[256,128]{1,0:T(8,128)S(1)} %get-tuple-element.97), channel_id=1, source_target_pairs={{0,4},{4,0},{8,12},{12,8},{16,20},{20,16},{24,28},{28,24},{1,5},{5... | collective-permute-start | bytes 393224 | tf_op jit(solution)/shard_map/ppermute | solution.py:104
  55.0 1.0 %shard_map.123 = (bf16[256,1024]{1,0:T(8,128)(2,1)}, bf16[256,1024]{1,0:T(8,128)(2,1)}, f32[1024,128]{1,0:T(8,128)}) custom-call(f32[256,128]{1,0:T(8,128)S(1)} %get-tuple-element.95.refs_5_.refs_0_, f32[256,128]{1,0:T(8,128)S(1)} %get-tuple-element.103.refs_1_, f32[256,1024]{1,0:T(8,128)S(1)} %get-tuple-element.91.refs_6_.refs_2_, ...), custom_call_target="tpu_custom_call" | custom-call | tf_op jit(solution)/shard_map/pallas_call | solution.py:25
  56.0 2.9 %collective-permute-done.24.refs_4_ = f32[256,128]{1,0:T(8,128)S(1)} collective-permute-done((f32[256,128]{1,0:T(8,128)S(1)}, f32[256,128]{1,0:T(8,128)S(1)}, u32[]{:S(2)}, u32[]{:S(2)}) %collective-permute-start.24) | collective-permute-done | bytes 131104 | tf_op jit(solution)/shard_map/ppermute | solution.py:104
  58.9 1.9 %collective-permute-done.25.refs_5_ = f32[256,128]{1,0:T(8,128)S(1)} collective-permute-done((f32[256,128]{1,0:T(8,128)S(1)}, f32[256,128]{1,0:T(8,128)S(1)}, u32[]{:S(2)}, u32[]{:S(2)}) %collective-permute-start.25) | collective-permute-done | bytes 131104 | tf_op jit(solution)/shard_map/ppermute | solution.py:104
  60.9 1.4 %shard_map.124 = (bf16[256,1024]{1,0:T(8,128)(2,1)}, bf16[256,1024]{1,0:T(8,128)(2,1)}, f32[1024,128]{1,0:T(8,128)}) custom-call(f32[264,128]{1,0:T(8,128)S(1)} %collective-permute-done.19.refs_9_.refs_0_, f32[256,128]{1,0:T(8,128)S(1)} %collective-permute-done.20.refs_1_, ...), custom_call_target="tpu_custom_call", output_to_operand_aliasing={{0}: (14, {}), {1}: (15, {}), {2}: (16, {})} | custom-call | tf_op jit(solution)/shard_map/pallas_call | solution.py:25
  (32 shorter events, 0.3 us)
Async XLA Ops:
  2.8 8.0 %collective-permute-start = (f32[136,128]{1,0:T(8,128)S(1)}, f32[136,128]{1,0:T(8,128)S(1)}, u32[]{:S(2)}, u32[]{:S(2)}) collective-permute-start(f32[136,128]{1,0:T(8,128)S(1)} %get-tuple-element.58), channel_id=1, source_target_pairs={{0,12},{4,8},{8,4},{12,0},{16,28},{20,24},{24,20},{28,16},{1,13},{... | collective-permute-start | bytes 208904 | tf_op jit(solution)/shard_map/ppermute | solution.py:104
  6.9 5.1 %collective-permute-start.1 = (f32[136,128]{1,0:T(8,128)S(1)}, f32[136,128]{1,0:T(8,128)S(1)}, u32[]{:S(2)}, u32[]{:S(2)}) collective-permute-start(f32[136,128]{1,0:T(8,128)S(1)} %get-tuple-element.59), channel_id=1, source_target_pairs={{0,4},{4,0},{8,12},{12,8},{16,20},{20,16},{24,28},{28,24},{1,5},{5... | collective-permute-start | bytes 208904 | tf_op jit(solution)/shard_map/ppermute | solution.py:104
  7.4 4.6 %collective-permute-start.2 = (f32[136,128]{1,0:T(8,128)S(1)}, f32[136,128]{1,0:T(8,128)S(1)}, u32[]{:S(2)}, u32[]{:S(2)}) collective-permute-start(f32[136,128]{1,0:T(8,128)S(1)} %get-tuple-element.60), channel_id=1, source_target_pairs={{0,8},{4,12},{8,0},{12,4},{16,24},{20,28},{24,16},{28,20},{1,9},{5... | collective-permute-start | bytes 208904 | tf_op jit(solution)/shard_map/ppermute | solution.py:104
  7.5 7.2 %collective-permute-start.6 = (f32[128,128]{1,0:T(8,128)S(1)}, f32[128,128]{1,0:T(8,128)S(1)}, u32[]{:S(2)}, u32[]{:S(2)}) collective-permute-start(f32[128,128]{1,0:T(8,128)S(1)} %get-tuple-element.67), channel_id=1, source_target_pairs={{0,12},{4,8},{8,4},{12,0},{16,28},{20,24},{24,20},{28,16},{1,13},{... | collective-permute-start | bytes 196616 | tf_op jit(solution)/shard_map/ppermute | solution.py:104
  10.3 4.3 %collective-permute-start.7 = (f32[128,128]{1,0:T(8,128)S(1)}, f32[128,128]{1,0:T(8,128)S(1)}, u32[]{:S(2)}, u32[]{:S(2)}) collective-permute-start(f32[128,128]{1,0:T(8,128)S(1)} %get-tuple-element.68), channel_id=1, source_target_pairs={{0,4},{4,0},{8,12},{12,8},{16,20},{20,16},{24,28},{28,24},{1,5},{5... | collective-permute-start | bytes 196616 | tf_op jit(solution)/shard_map/ppermute | solution.py:104
  10.9 4.3 %collective-permute-start.8 = (f32[128,128]{1,0:T(8,128)S(1)}, f32[128,128]{1,0:T(8,128)S(1)}, u32[]{:S(2)}, u32[]{:S(2)}) collective-permute-start(f32[128,128]{1,0:T(8,128)S(1)} %get-tuple-element.69), channel_id=1, source_target_pairs={{0,8},{4,12},{8,0},{12,4},{16,24},{20,28},{24,16},{28,20},{1,9},{5... | collective-permute-start | bytes 196616 | tf_op jit(solution)/shard_map/ppermute | solution.py:104
  12.0 7.3 %collective-permute-start.3 = (f32[136,128]{1,0:T(8,128)S(1)}, f32[136,128]{1,0:T(8,128)S(1)}, u32[]{:S(2)}, u32[]{:S(2)}) collective-permute-start(f32[136,128]{1,0:T(8,128)S(1)} %get-tuple-element.61.refs_4_), channel_id=1, source_target_pairs={{0,16},{4,20},{8,24},{12,28},{16,0},{20,4},{24,8},{28,12},{1,17},{... | collective-permute-start | bytes 208904 | tf_op jit(solution)/shard_map/ppermute | solution.py:118
  15.2 4.2 %copy-start.3 = (f32[8,128,128]{2,1,0:T(8,128)S(1)}, f32[8,128,128]{2,1,0:T(8,128)}, u32[]{:S(2)}) copy-start(f32[8,128,128]{2,1,0:T(8,128)} %param.14) | copy-start | bytes 1572868
  15.2 10.4 %copy-start.5 = (bf16[256,1024]{1,0:T(8,128)(2,1)S(1)}, bf16[256,1024]{1,0:T(8,128)(2,1)}, u32[]{:S(2)}) copy-start(bf16[256,1024]{1,0:T(8,128)(2,1)} %upstream_ref.1) | copy-start | bytes 1572868
  15.3 5.7 %collective-permute-start.9 = (f32[128,128]{1,0:T(8,128)S(1)}, f32[128,128]{1,0:T(8,128)S(1)}, u32[]{:S(2)}, u32[]{:S(2)}) collective-permute-start(f32[128,128]{1,0:T(8,128)S(1)} %shard_map.114.refs_4_), channel_id=1, source_target_pairs={{0,16},{4,20},{8,24},{12,28},{16,0},{20,4},{24,8},{28,12},{1,17},{... | collective-permute-start | bytes 196616 | tf_op jit(solution)/shard_map/ppermute | solution.py:118
  19.4 6.3 %copy-start.1 = (bf16[256,1024]{1,0:T(8,128)(2,1)S(1)}, bf16[256,1024]{1,0:T(8,128)(2,1)}, u32[]{:S(2)}) copy-start(bf16[256,1024]{1,0:T(8,128)(2,1)} %refs_9_.1) | copy-start | bytes 1572868
  19.4 6.3 %copy-start.2 = (bf16[256,1024]{1,0:T(8,128)(2,1)S(1)}, bf16[256,1024]{1,0:T(8,128)(2,1)}, u32[]{:S(2)}) copy-start(bf16[256,1024]{1,0:T(8,128)(2,1)} %query_ref.3) | copy-start | bytes 1572868
  19.5 6.2 %copy-start = (bf16[256,1024]{1,0:T(8,128)(2,1)S(1)}, bf16[256,1024]{1,0:T(8,128)(2,1)}, u32[]{:S(2)}) copy-start(bf16[256,1024]{1,0:T(8,128)(2,1)} %refs_8_.3) | copy-start | bytes 1572868
  19.5 5.7 %collective-permute-start.4 = (f32[128,128]{1,0:T(8,128)S(1)}, f32[128,128]{1,0:T(8,128)S(1)}, u32[]{:S(2)}, u32[]{:S(2)}) collective-permute-start(f32[128,128]{1,0:T(8,128)S(1)} %get-tuple-element.64), channel_id=1, source_target_pairs={{0,4},{4,0},{8,12},{12,8},{16,20},{20,16},{24,28},{28,24},{1,5},{5... | collective-permute-start | bytes 196616 | tf_op jit(solution)/shard_map/ppermute | solution.py:104
  20.6 5.0 %collective-permute-start.5 = (f32[128,128]{1,0:T(8,128)S(1)}, f32[128,128]{1,0:T(8,128)S(1)}, u32[]{:S(2)}, u32[]{:S(2)}) collective-permute-start(f32[128,128]{1,0:T(8,128)S(1)} %get-tuple-element.65), channel_id=1, source_target_pairs={{0,8},{4,12},{8,0},{12,4},{16,24},{20,28},{24,16},{28,20},{1,9},{5... | collective-permute-start | bytes 196616 | tf_op jit(solution)/shard_map/ppermute | solution.py:104
  21.1 7.5 %collective-permute-start.12 = (f32[256,128]{1,0:T(8,128)S(1)}, f32[256,128]{1,0:T(8,128)S(1)}, u32[]{:S(2)}, u32[]{:S(2)}) collective-permute-start(f32[256,128]{1,0:T(8,128)S(1)} %get-tuple-element.75), channel_id=1, source_target_pairs={{0,12},{4,8},{8,4},{12,0},{16,28},{20,24},{24,20},{28,16},{1,13},{... | collective-permute-start | bytes 393224 | tf_op jit(solution)/shard_map/ppermute | solution.py:104
  23.2 2.5 %copy-start.6 = (f32[1024]{0:T(1024)S(1)}, f32[1024]{0:T(1024)}, u32[]{:S(2)}) copy-start(f32[1024]{0:T(1024)} %param.13) | copy-start | bytes 12292
  23.2 4.9 %collective-permute-start.10 = (f32[128,128]{1,0:T(8,128)S(1)}, f32[128,128]{1,0:T(8,128)S(1)}, u32[]{:S(2)}, u32[]{:S(2)}) collective-permute-start(f32[128,128]{1,0:T(8,128)S(1)} %get-tuple-element.73), channel_id=1, source_target_pairs={{0,4},{4,0},{8,12},{12,8},{16,20},{20,16},{24,28},{28,24},{1,5},{5... | collective-permute-start | bytes 196616 | tf_op jit(solution)/shard_map/ppermute | solution.py:104
  24.3 4.3 %collective-permute-start.11 = (f32[128,128]{1,0:T(8,128)S(1)}, f32[128,128]{1,0:T(8,128)S(1)}, u32[]{:S(2)}, u32[]{:S(2)}) collective-permute-start(f32[128,128]{1,0:T(8,128)S(1)} %get-tuple-element.74), channel_id=1, source_target_pairs={{0,8},{4,12},{8,0},{12,4},{16,24},{20,28},{24,16},{28,20},{1,9},{5... | collective-permute-start | bytes 196616 | tf_op jit(solution)/shard_map/ppermute | solution.py:104
  29.2 1.8 %collective-permute-start.15 = (f32[8,256]{1,0:T(8,128)S(1)}, f32[8,256]{1,0:T(8,128)S(1)}, u32[]{:S(2)}, u32[]{:S(2)}) collective-permute-start(f32[8,256]{1,0:T(8,128)S(1)} %get-tuple-element.80.refs_0_), channel_id=1, source_target_pairs={{0,3},{1,0},{2,1},{3,2},{4,7},{5,4},{6,5},{7,6},{8,11},{9,8},{10,9... | collective-permute-start | bytes 24584 | tf_op jit(solution)/shard_map/ppermute | solution.py:578
  29.2 3.7 %collective-permute-start.14 = (f32[8,256]{1,0:T(8,128)S(1)}, f32[8,256]{1,0:T(8,128)S(1)}, u32[]{:S(2)}, u32[]{:S(2)}) collective-permute-start(f32[8,256]{1,0:T(8,128)S(1)} %get-tuple-element.80.refs_0_), channel_id=1, source_target_pairs={{0,2},{1,3},{2,0},{3,1},{4,6},{5,7},{6,4},{7,5},{8,10},{9,11},{10,... | collective-permute-start | bytes 24584 | tf_op jit(solution)/shard_map/ppermute | solution.py:578
  30.8 3.1 %collective-permute-start.13 = (f32[8,256]{1,0:T(8,128)S(1)}, f32[8,256]{1,0:T(8,128)S(1)}, u32[]{:S(2)}, u32[]{:S(2)}) collective-permute-start(f32[8,256]{1,0:T(8,128)S(1)} %get-tuple-element.80.refs_0_), channel_id=1, source_target_pairs={{0,1},{1,2},{2,3},{3,0},{4,5},{5,6},{6,7},{7,4},{8,9},{9,10},{10,1... | collective-permute-start | bytes 24584 | tf_op jit(solution)/shard_map/ppermute | solution.py:578
  34.6 6.9 %collective-permute-start.16 = (f32[256,128]{1,0:T(8,128)S(1)}, f32[256,128]{1,0:T(8,128)S(1)}, u32[]{:S(2)}, u32[]{:S(2)}) collective-permute-start(f32[256,128]{1,0:T(8,128)S(1)} %get-tuple-element.88), channel_id=1, source_target_pairs={{0,12},{4,8},{8,4},{12,0},{16,28},{20,24},{24,20},{28,16},{1,13},{... | collective-permute-start | bytes 393224 | tf_op jit(solution)/shard_map/ppermute | solution.py:104
  36.0 6.2 %collective-permute-start.17 = (f32[256,128]{1,0:T(8,128)S(1)}, f32[256,128]{1,0:T(8,128)S(1)}, u32[]{:S(2)}, u32[]{:S(2)}) collective-permute-start(f32[256,128]{1,0:T(8,128)S(1)} %get-tuple-element.89), channel_id=1, source_target_pairs={{0,4},{4,0},{8,12},{12,8},{16,20},{20,16},{24,28},{28,24},{1,5},{5... | collective-permute-start | bytes 393224 | tf_op jit(solution)/shard_map/ppermute | solution.py:104
  37.0 5.3 %collective-permute-start.18 = (f32[256,128]{1,0:T(8,128)S(1)}, f32[256,128]{1,0:T(8,128)S(1)}, u32[]{:S(2)}, u32[]{:S(2)}) collective-permute-start(f32[256,128]{1,0:T(8,128)S(1)} %get-tuple-element.90), channel_id=1, source_target_pairs={{0,8},{4,12},{8,0},{12,4},{16,24},{20,28},{24,16},{28,20},{1,9},{5... | collective-permute-start | bytes 393224 | tf_op jit(solution)/shard_map/ppermute | solution.py:104
  38.1 4.1 %copy-start.4 = (f32[8,128,128]{2,1,0:T(8,128)S(1)}, f32[8,128,128]{2,1,0:T(8,128)}, u32[]{:S(2)}) copy-start(f32[8,128,128]{2,1,0:T(8,128)} %param.15) | copy-start | bytes 1572868
  42.4 7.9 %collective-permute-start.19 = (f32[264,128]{1,0:T(8,128)S(1)}, f32[264,128]{1,0:T(8,128)S(1)}, u32[]{:S(2)}, u32[]{:S(2)}) collective-permute-start(f32[264,128]{1,0:T(8,128)S(1)} %get-tuple-element.92), channel_id=1, source_target_pairs={{0,8},{4,12},{8,0},{12,4},{16,24},{20,28},{24,16},{28,20},{1,9},{5... | collective-permute-start | bytes 405512 | tf_op jit(solution)/shard_map/ppermute | solution.py:104
  43.5 6.8 %collective-permute-start.22 = (f32[256,128]{1,0:T(8,128)S(1)}, f32[256,128]{1,0:T(8,128)S(1)}, u32[]{:S(2)}, u32[]{:S(2)}) collective-permute-start(f32[256,128]{1,0:T(8,128)S(1)} %shard_map.121.refs_4_), channel_id=1, source_target_pairs={{0,16},{4,20},{8,24},{12,28},{16,0},{20,4},{24,8},{28,12},{1,17},{... | collective-permute-start | bytes 393224 | tf_op jit(solution)/shard_map/ppermute | solution.py:118
  46.3 9.6 %collective-permute-start.20 = (f32[256,128]{1,0:T(8,128)S(1)}, f32[256,128]{1,0:T(8,128)S(1)}, u32[]{:S(2)}, u32[]{:S(2)}) collective-permute-start(f32[256,128]{1,0:T(8,128)S(1)} %get-tuple-element.93), channel_id=1, source_target_pairs={{0,4},{4,0},{8,12},{12,8},{16,20},{20,16},{24,28},{28,24},{1,5},{5... | collective-permute-start | bytes 393224 | tf_op jit(solution)/shard_map/ppermute | solution.py:104
  47.3 8.6 %collective-permute-start.21 = (f32[256,128]{1,0:T(8,128)S(1)}, f32[256,128]{1,0:T(8,128)S(1)}, u32[]{:S(2)}, u32[]{:S(2)}) collective-permute-start(f32[256,128]{1,0:T(8,128)S(1)} %get-tuple-element.94), channel_id=1, source_target_pairs={{0,12},{4,8},{8,4},{12,0},{16,28},{20,24},{24,20},{28,16},{1,13},{... | collective-permute-start | bytes 393224 | tf_op jit(solution)/shard_map/ppermute | solution.py:104
  50.5 5.5 %collective-permute-start.23 = (f32[256,128]{1,0:T(8,128)S(1)}, f32[256,128]{1,0:T(8,128)S(1)}, u32[]{:S(2)}, u32[]{:S(2)}) collective-permute-start(f32[256,128]{1,0:T(8,128)S(1)} %get-tuple-element.96), channel_id=1, source_target_pairs={{0,8},{4,12},{8,0},{12,4},{16,24},{20,28},{24,16},{28,20},{1,9},{5... | collective-permute-start | bytes 393224 | tf_op jit(solution)/shard_map/ppermute | solution.py:104
  52.6 6.3 %collective-permute-start.24 = (f32[256,128]{1,0:T(8,128)S(1)}, f32[256,128]{1,0:T(8,128)S(1)}, u32[]{:S(2)}, u32[]{:S(2)}) collective-permute-start(f32[256,128]{1,0:T(8,128)S(1)} %get-tuple-element.97), channel_id=1, source_target_pairs={{0,4},{4,0},{8,12},{12,8},{16,20},{20,16},{24,28},{28,24},{1,5},{5... | collective-permute-start | bytes 393224 | tf_op jit(solution)/shard_map/ppermute | solution.py:104
  55.0 5.9 %collective-permute-start.25 = (f32[256,128]{1,0:T(8,128)S(1)}, f32[256,128]{1,0:T(8,128)S(1)}, u32[]{:S(2)}, u32[]{:S(2)}) collective-permute-start(f32[256,128]{1,0:T(8,128)S(1)} %get-tuple-element.98), channel_id=1, source_target_pairs={{0,12},{4,8},{8,4},{12,0},{16,28},{20,24},{24,20},{28,16},{1,13},{... | collective-permute-start | bytes 393224 | tf_op jit(solution)/shard_map/ppermute | solution.py:104

commit v16 on v13

--- a/solution.py
+++ b/solution.py
@@ -76,7 +76,7 @@
         self.near = [way for way in range(self.members) if way.bit_count() == 1]
         self.far = [way for way in range(self.members) if way.bit_count() > 1]
         self.ways = [0] + self.far + self.near
-        self.early_ways = [0] + self.near[::-1] + self.far
+        self.early_ways = [0] + self.near + self.far
         self.late_ways = [0] + self.far + self.near[::-1]
 
     def member(self):

time: 60.9 us -> 62 us (1.018)
  waiting for transfers between devices: 12.7 us -> 15.4 us
  starting transfers between devices: 35.9 us -> 34.2 us
    ppermute x20, starting transfers between devices: 26 us -> 24.2 us  [swap(): return lax.ppermute(piece, 'seq', pairs) if way else piece]
    ppermute x3, waiting for transfers between devices: 2.24 us -> 3.72 us  [from_groups(): lax.ppermute(piece, 'seq', [(i, (i + step * self.members) % self.blocks)...]
    ppermute x20, waiting for transfers between devices: 7.59 us -> 8.79 us  [swap(): return lax.ppermute(piece, 'seq', pairs) if way else piece]
where the time goes in v16:
time: 62 us; the launch traced here: 61.7 us
  starting transfers between devices  34.2 us (55%)
  waiting for transfers between devices  15.4 us (25%)
  Pallas kernels  11.3 us (18%)
  between operations  0.76 us (1%)
    ppermute x20, starting transfers between devices, swap(): return lax.ppermute(piece, 'seq', pairs) if way else piece  24.2 us
    pallas_call x14, Pallas kernels, call(): pl.pallas_call(body, out_shape=outs, in_specs=specs or [VMEM] * len(opera...  11.3 us
    ppermute x20, waiting for transfers between devices, swap(): return lax.ppermute(piece, 'seq', pairs) if way else piece  8.79 us
    ppermute x3, starting transfers between devices, from_groups(): lax.ppermute(piece, 'seq', [(i, (i + step * self.members) % self.blocks)...  8.25 us
    ppermute x3, waiting for transfers between devices, from_groups(): lax.ppermute(piece, 'seq', [(i, (i + step * self.members) % self.blocks)...  3.72 us
    ppermute x3, waiting for transfers between devices, on_device(): lax.ppermute(sums, 'head', [(i, (i + step) % parties) for i in range(part...  2.85 us
    ppermute x3, starting transfers between devices, on_device(): lax.ppermute(sums, 'head', [(i, (i + step) % parties) for i in range(part...  1.8 us
  transfers between devices with their start and end apart: 26, of which 14 were waited for; matrix products, arithmetic and copies ran while one was open for 0% of the time, Pallas kernels for 10%

profile of v16, /device:TPU:0, one launch (start us, length us, event | category | flops | bytes accessed | tf_op | source)
XLA Modules:
  0.0 61.7 jit_solution(11623425843552500962)
XLA Ops:
  0.6 2.2 %shard_map.111 = (f32[136,128]{1,0:T(8,128)S(1)}, f32[136,128]{1,0:T(8,128)S(1)}, f32[136,128]{1,0:T(8,128)S(1)}, f32[136,128]{1,0:T(8,128)S(1)}, f32[128,128]{1...) custom-call(bf16[256,1024]{1,0:T(8,128)(2,1)} %refs_8_.3, ...), custom_call_target="tpu_custom_call" | custom-call | tf_op jit(solution)/shard_map/pallas_call | solution.py:25
  2.8 4.0 %collective-permute-start = (f32[136,128]{1,0:T(8,128)S(1)}, f32[136,128]{1,0:T(8,128)S(1)}, u32[]{:S(2)}, u32[]{:S(2)}) collective-permute-start(f32[136,128]{1,0:T(8,128)S(1)} %get-tuple-element.58), channel_id=1, source_target_pairs={{0,12},{4,8},{8,4},{12,0},{16,28},{20,24},{24,20},{28,16},{1,13},{... | collective-permute-start | bytes 208904 | tf_op jit(solution)/shard_map/ppermute | solution.py:104
  6.9 0.5 collective-permute-start.1
  7.4 0.1 collective-permute-start.2
  7.5 2.8 %collective-permute-start.6 = (f32[128,128]{1,0:T(8,128)S(1)}, f32[128,128]{1,0:T(8,128)S(1)}, u32[]{:S(2)}, u32[]{:S(2)}) collective-permute-start(f32[128,128]{1,0:T(8,128)S(1)} %get-tuple-element.67), channel_id=1, source_target_pairs={{0,12},{4,8},{8,4},{12,0},{16,28},{20,24},{24,20},{28,16},{1,13},{... | collective-permute-start | bytes 196616 | tf_op jit(solution)/shard_map/ppermute | solution.py:104
  10.3 0.5 collective-permute-start.7
  10.9 0.8 %collective-permute-start.8 = (f32[128,128]{1,0:T(8,128)S(1)}, f32[128,128]{1,0:T(8,128)S(1)}, u32[]{:S(2)}, u32[]{:S(2)}) collective-permute-start(f32[128,128]{1,0:T(8,128)S(1)} %get-tuple-element.69), channel_id=1, source_target_pairs={{0,8},{4,12},{8,0},{12,4},{16,24},{20,28},{24,16},{28,20},{1,9},{5... | collective-permute-start | bytes 196616 | tf_op jit(solution)/shard_map/ppermute | solution.py:104
  11.6 0.4 collective-permute-done.1.refs_2_
  12.0 2.7 %collective-permute-start.3 = (f32[136,128]{1,0:T(8,128)S(1)}, f32[136,128]{1,0:T(8,128)S(1)}, u32[]{:S(2)}, u32[]{:S(2)}) collective-permute-start(f32[136,128]{1,0:T(8,128)S(1)} %get-tuple-element.61.refs_4_), channel_id=1, source_target_pairs={{0,16},{4,20},{8,24},{12,28},{16,0},{20,4},{24,8},{28,12},{1,17},{... | collective-permute-start | bytes 208904 | tf_op jit(solution)/shard_map/ppermute | solution.py:118
  14.7 0.5 collective-permute-done.8.refs_3_
  15.3 2.6 %collective-permute-start.9 = (f32[128,128]{1,0:T(8,128)S(1)}, f32[128,128]{1,0:T(8,128)S(1)}, u32[]{:S(2)}, u32[]{:S(2)}) collective-permute-start(f32[128,128]{1,0:T(8,128)S(1)} %shard_map.114.refs_4_), channel_id=1, source_target_pairs={{0,16},{4,20},{8,24},{12,28},{16,0},{20,4},{24,8},{28,12},{1,17},{... | collective-permute-start | bytes 196616 | tf_op jit(solution)/shard_map/ppermute | solution.py:118
  17.8 1.5 %collective-permute-done.3.refs_5_ = f32[136,128]{1,0:T(8,128)S(1)} collective-permute-done((f32[136,128]{1,0:T(8,128)S(1)}, f32[136,128]{1,0:T(8,128)S(1)}, u32[]{:S(2)}, u32[]{:S(2)}) %collective-permute-start.3) | collective-permute-done | bytes 69664 | tf_op jit(solution)/shard_map/ppermute | solution.py:118
  19.5 1.1 %collective-permute-start.4 = (f32[128,128]{1,0:T(8,128)S(1)}, f32[128,128]{1,0:T(8,128)S(1)}, u32[]{:S(2)}, u32[]{:S(2)}) collective-permute-start(f32[128,128]{1,0:T(8,128)S(1)} %get-tuple-element.64), channel_id=1, source_target_pairs={{0,4},{4,0},{8,12},{12,8},{16,20},{20,16},{24,28},{28,24},{1,5},{5... | collective-permute-start | bytes 196616 | tf_op jit(solution)/shard_map/ppermute | solution.py:104
  20.6 0.3 collective-permute-start.5
  21.1 2.1 %collective-permute-start.12 = (f32[256,128]{1,0:T(8,128)S(1)}, f32[256,128]{1,0:T(8,128)S(1)}, u32[]{:S(2)}, u32[]{:S(2)}) collective-permute-start(f32[256,128]{1,0:T(8,128)S(1)} %get-tuple-element.75), channel_id=1, source_target_pairs={{0,12},{4,8},{8,4},{12,0},{16,28},{20,24},{24,20},{28,16},{1,13},{... | collective-permute-start | bytes 393224 | tf_op jit(solution)/shard_map/ppermute | solution.py:104
  23.2 1.1 %collective-permute-start.10 = (f32[128,128]{1,0:T(8,128)S(1)}, f32[128,128]{1,0:T(8,128)S(1)}, u32[]{:S(2)}, u32[]{:S(2)}) collective-permute-start(f32[128,128]{1,0:T(8,128)S(1)} %get-tuple-element.73), channel_id=1, source_target_pairs={{0,4},{4,0},{8,12},{12,8},{16,20},{20,16},{24,28},{28,24},{1,5},{5... | collective-permute-start | bytes 196616 | tf_op jit(solution)/shard_map/ppermute | solution.py:104
  24.3 0.3 collective-permute-start.11
  24.6 0.6 collective-permute-done.4.refs_0_.refs_1_
  25.2 0.4 collective-permute-done.5.refs_1_.refs_2_
  25.7 1.2 %shard_map.116 = (bf16[8,256,256]{2,1,0:T(8,128)(2,1)S(1)}, f32[256,1024]{1,0:T(8,128)S(1)}, f32[256,1024]{1,0:T(8,128)S(1)}, bf16[8,128,256]{2,1,0:T(8,128)(2,1)S(1)}) custom-call(bf16[256,1024]{1,0:T(8,128)(2,1)S(1)} %copy-done.2, bf16[256,1024]{1,0:T(8,128)(2,1)S(1)} %copy-done, bf16[256,1024]{1,0:T(8,128)(2,1)S(1)} %copy-done.1, ...), custom_call_target="tpu_custom_call" | custom-call | flops 1000000000 | tf_op jit(solution)/shard_map/pallas_call | solution.py:25
  26.9 1.2 %collective-permute-done.10.refs_4_ = f32[128,128]{1,0:T(8,128)S(1)} collective-permute-done((f32[128,128]{1,0:T(8,128)S(1)}, f32[128,128]{1,0:T(8,128)S(1)}, u32[]{:S(2)}, u32[]{:S(2)}) %collective-permute-start.10) | collective-permute-done | bytes 65568 | tf_op jit(solution)/shard_map/ppermute | solution.py:104
  28.1 0.4 collective-permute-done.11.refs_5_
  28.5 0.7 %shard_map.117 = (f32[256,1024]{1,0:T(8,128)S(1)}, f32[8,256]{1,0:T(8,128)S(1)}, bf16[1024,128]{1,0:T(8,128)(2,1)S(1)}) custom-call(f32[128,128]{1,0:T(8,128)S(1)} %get-tuple-element.63.refs_0_, f32[128,128]{1,0:T(8,128)S(1)} %collective-permute-done.4.refs_0_.refs_1_, f32[128,128]{1,0:T(8,128)S(1)} %collective-permute-done.5.refs_1_.refs_2_, ...), custom_call_target="tpu_custom_call" | custom-call | tf_op jit(solution)/shard_map/pallas_call | solution.py:25
  29.2 1.6 %collective-permute-start.14 = (f32[8,256]{1,0:T(8,128)S(1)}, f32[8,256]{1,0:T(8,128)S(1)}, u32[]{:S(2)}, u32[]{:S(2)}) collective-permute-start(f32[8,256]{1,0:T(8,128)S(1)} %get-tuple-element.80.refs_0_), channel_id=1, source_target_pairs={{0,2},{1,3},{2,0},{3,1},{4,6},{5,7},{6,4},{7,5},{8,10},{9,11},{10,... | collective-permute-start | bytes 24584 | tf_op jit(solution)/shard_map/ppermute | solution.py:578
  30.8 0.2 collective-permute-start.13
  31.0 1.9 %collective-permute-done.14.refs_2_ = f32[8,256]{1,0:T(8,128)S(1)} collective-permute-done((f32[8,256]{1,0:T(8,128)S(1)}, f32[8,256]{1,0:T(8,128)S(1)}, u32[]{:S(2)}, u32[]{:S(2)}) %collective-permute-start.14) | collective-permute-done | bytes 8224 | tf_op jit(solution)/shard_map/ppermute | solution.py:578
  32.9 1.0 %collective-permute-done.13.refs_1_ = f32[8,256]{1,0:T(8,128)S(1)} collective-permute-done((f32[8,256]{1,0:T(8,128)S(1)}, f32[8,256]{1,0:T(8,128)S(1)}, u32[]{:S(2)}, u32[]{:S(2)}) %collective-permute-start.13) | collective-permute-done | bytes 8224 | tf_op jit(solution)/shard_map/ppermute | solution.py:578
  33.9 0.7 %shard_map.118 = (bf16[256,1024]{1,0:T(8,128)(2,1)S(1)}, f32[1024,128]{1,0:T(8,128)S(1)}, f32[256,128]{1,0:T(8,128)S(1)}, f32[256,128]{1,0:T(8,128)S(1)}, f32[25...) custom-call(f32[8,256]{1,0:T(8,128)S(1)} %get-tuple-element.80.refs_0_, f32[8,256]{1,0:T(8,128)S(1)} %collective-permute-done.13.refs_1_, ...), custom_call_target="tpu_custom_call" | custom-call | tf_op jit(solution)/shard_map/pallas_call | solution.py:25
  34.6 1.4 %collective-permute-start.16 = (f32[256,128]{1,0:T(8,128)S(1)}, f32[256,128]{1,0:T(8,128)S(1)}, u32[]{:S(2)}, u32[]{:S(2)}) collective-permute-start(f32[256,128]{1,0:T(8,128)S(1)} %get-tuple-element.88), channel_id=1, source_target_pairs={{0,12},{4,8},{8,4},{12,0},{16,28},{20,24},{24,20},{28,16},{1,13},{... | collective-permute-start | bytes 393224 | tf_op jit(solution)/shard_map/ppermute | solution.py:104
  36.0 0.9 %collective-permute-start.17 = (f32[256,128]{1,0:T(8,128)S(1)}, f32[256,128]{1,0:T(8,128)S(1)}, u32[]{:S(2)}, u32[]{:S(2)}) collective-permute-start(f32[256,128]{1,0:T(8,128)S(1)} %get-tuple-element.89), channel_id=1, source_target_pairs={{0,4},{4,0},{8,12},{12,8},{16,20},{20,16},{24,28},{28,24},{1,5},{5... | collective-permute-start | bytes 393224 | tf_op jit(solution)/shard_map/ppermute | solution.py:104
  37.0 1.2 %collective-permute-start.18 = (f32[256,128]{1,0:T(8,128)S(1)}, f32[256,128]{1,0:T(8,128)S(1)}, u32[]{:S(2)}, u32[]{:S(2)}) collective-permute-start(f32[256,128]{1,0:T(8,128)S(1)} %get-tuple-element.90), channel_id=1, source_target_pairs={{0,8},{4,12},{8,0},{12,4},{16,24},{20,28},{24,16},{28,20},{1,9},{5... | collective-permute-start | bytes 393224 | tf_op jit(solution)/shard_map/ppermute | solution.py:104
  38.1 3.4 %shard_map.119 = (bf16[256,1024]{1,0:T(8,128)(2,1)}, f32[256,1024]{1,0:T(8,128)S(1)}, f32[256,1024]{1,0:T(8,128)S(1)}, f32[8,256,128]{2,1,0:T(8,128)S(1)}) custom-call(bf16[256,1024]{1,0:T(8,128)(2,1)S(1)} %get-tuple-element.83.attn_grad_ref, bf16[256,1024]{1,0:T(8,128)(2,1)S(1)} %copy-done.2, bf16[256,1024]{1,0:T(8,128)(2,1)S(1)} %copy-done, ...), custom_call_target="tpu_custom_call" | custom-call | flops 671088640 | tf_op jit(solution)/shard_map/pallas_call | solution.py:25
  41.5 0.7 %collective-permute-done.17.refs_2_ = f32[256,128]{1,0:T(8,128)S(1)} collective-permute-done((f32[256,128]{1,0:T(8,128)S(1)}, f32[256,128]{1,0:T(8,128)S(1)}, u32[]{:S(2)}, u32[]{:S(2)}) %collective-permute-start.17) | collective-permute-done | bytes 131104 | tf_op jit(solution)/shard_map/ppermute | solution.py:104
  42.2 0.2 shard_map.120
  42.4 1.0 %collective-permute-start.19 = (f32[264,128]{1,0:T(8,128)S(1)}, f32[264,128]{1,0:T(8,128)S(1)}, u32[]{:S(2)}, u32[]{:S(2)}) collective-permute-start(f32[264,128]{1,0:T(8,128)S(1)} %get-tuple-element.92), channel_id=1, source_target_pairs={{0,4},{4,0},{8,12},{12,8},{16,20},{20,16},{24,28},{28,24},{1,5},{5... | collective-permute-start | bytes 405512 | tf_op jit(solution)/shard_map/ppermute | solution.py:104
  43.5 3.0 %collective-permute-start.22 = (f32[256,128]{1,0:T(8,128)S(1)}, f32[256,128]{1,0:T(8,128)S(1)}, u32[]{:S(2)}, u32[]{:S(2)}) collective-permute-start(f32[256,128]{1,0:T(8,128)S(1)} %shard_map.121.refs_4_), channel_id=1, source_target_pairs={{0,16},{4,20},{8,24},{12,28},{16,0},{20,4},{24,8},{28,12},{1,17},{... | collective-permute-start | bytes 393224 | tf_op jit(solution)/shard_map/ppermute | solution.py:118
  46.5 0.8 %collective-permute-start.20 = (f32[256,128]{1,0:T(8,128)S(1)}, f32[256,128]{1,0:T(8,128)S(1)}, u32[]{:S(2)}, u32[]{:S(2)}) collective-permute-start(f32[256,128]{1,0:T(8,128)S(1)} %get-tuple-element.93), channel_id=1, source_target_pairs={{0,8},{4,12},{8,0},{12,4},{16,24},{20,28},{24,16},{28,20},{1,9},{5... | collective-permute-start | bytes 393224 | tf_op jit(solution)/shard_map/ppermute | solution.py:104
  47.3 1.4 %collective-permute-start.21 = (f32[256,128]{1,0:T(8,128)S(1)}, f32[256,128]{1,0:T(8,128)S(1)}, u32[]{:S(2)}, u32[]{:S(2)}) collective-permute-start(f32[256,128]{1,0:T(8,128)S(1)} %get-tuple-element.94), channel_id=1, source_target_pairs={{0,12},{4,8},{8,4},{12,0},{16,28},{20,24},{24,20},{28,16},{1,13},{... | collective-permute-start | bytes 393224 | tf_op jit(solution)/shard_map/ppermute | solution.py:104
  48.8 2.2 %collective-permute-done.22.refs_5_ = f32[256,128]{1,0:T(8,128)S(1)} collective-permute-done((f32[256,128]{1,0:T(8,128)S(1)}, f32[256,128]{1,0:T(8,128)S(1)}, u32[]{:S(2)}, u32[]{:S(2)}) %collective-permute-start.22) | collective-permute-done | bytes 131104 | tf_op jit(solution)/shard_map/ppermute | solution.py:118
  51.0 0.2 shard_map.122
  51.2 0.8 %collective-permute-start.23 = (f32[256,128]{1,0:T(8,128)S(1)}, f32[256,128]{1,0:T(8,128)S(1)}, u32[]{:S(2)}, u32[]{:S(2)}) collective-permute-start(f32[256,128]{1,0:T(8,128)S(1)} %get-tuple-element.96), channel_id=1, source_target_pairs={{0,12},{4,8},{8,4},{12,0},{16,28},{20,24},{24,20},{28,16},{1,13},{... | collective-permute-start | bytes 393224 | tf_op jit(solution)/shard_map/ppermute | solution.py:104
  52.1 1.8 %collective-permute-start.24 = (f32[256,128]{1,0:T(8,128)S(1)}, f32[256,128]{1,0:T(8,128)S(1)}, u32[]{:S(2)}, u32[]{:S(2)}) collective-permute-start(f32[256,128]{1,0:T(8,128)S(1)} %get-tuple-element.97), channel_id=1, source_target_pairs={{0,8},{4,12},{8,0},{12,4},{16,24},{20,28},{24,16},{28,20},{1,9},{5... | collective-permute-start | bytes 393224 | tf_op jit(solution)/shard_map/ppermute | solution.py:104
  53.8 1.0 %collective-permute-start.25 = (f32[256,128]{1,0:T(8,128)S(1)}, f32[256,128]{1,0:T(8,128)S(1)}, u32[]{:S(2)}, u32[]{:S(2)}) collective-permute-start(f32[256,128]{1,0:T(8,128)S(1)} %get-tuple-element.98), channel_id=1, source_target_pairs={{0,4},{4,0},{8,12},{12,8},{16,20},{20,16},{24,28},{28,24},{1,5},{5... | collective-permute-start | bytes 393224 | tf_op jit(solution)/shard_map/ppermute | solution.py:104
  54.8 1.0 %shard_map.123 = (bf16[256,1024]{1,0:T(8,128)(2,1)}, bf16[256,1024]{1,0:T(8,128)(2,1)}, f32[1024,128]{1,0:T(8,128)}) custom-call(f32[256,128]{1,0:T(8,128)S(1)} %get-tuple-element.95.refs_5_.refs_0_, f32[256,128]{1,0:T(8,128)S(1)} %get-tuple-element.103.refs_1_, f32[256,1024]{1,0:T(8,128)S(1)} %get-tuple-element.91.refs_6_.refs_2_, ...), custom_call_target="tpu_custom_call" | custom-call | tf_op jit(solution)/shard_map/pallas_call | solution.py:25
  55.8 0.6 collective-permute-done.21.refs_2_
  56.4 2.0 %collective-permute-done.23.refs_3_ = f32[256,128]{1,0:T(8,128)S(1)} collective-permute-done((f32[256,128]{1,0:T(8,128)S(1)}, f32[256,128]{1,0:T(8,128)S(1)}, u32[]{:S(2)}, u32[]{:S(2)}) %collective-permute-start.23) | collective-permute-done | bytes 131104 | tf_op jit(solution)/shard_map/ppermute | solution.py:104
  58.4 1.9 %collective-permute-done.24.refs_4_ = f32[256,128]{1,0:T(8,128)S(1)} collective-permute-done((f32[256,128]{1,0:T(8,128)S(1)}, f32[256,128]{1,0:T(8,128)S(1)}, u32[]{:S(2)}, u32[]{:S(2)}) %collective-permute-start.24) | collective-permute-done | bytes 131104 | tf_op jit(solution)/shard_map/ppermute | solution.py:104
  60.3 1.4 %shard_map.124 = (bf16[256,1024]{1,0:T(8,128)(2,1)}, bf16[256,1024]{1,0:T(8,128)(2,1)}, f32[1024,128]{1,0:T(8,128)}) custom-call(f32[264,128]{1,0:T(8,128)S(1)} %collective-permute-done.19.refs_9_.refs_0_, f32[256,128]{1,0:T(8,128)S(1)} %collective-permute-done.20.refs_1_, ...), custom_call_target="tpu_custom_call", output_to_operand_aliasing={{0}: (14, {}), {1}: (15, {}), {2}: (16, {})} | custom-call | tf_op jit(solution)/shard_map/pallas_call | solution.py:25
  (32 shorter events, 0.4 us)
Async XLA Ops:
  2.8 8.0 %collective-permute-start = (f32[136,128]{1,0:T(8,128)S(1)}, f32[136,128]{1,0:T(8,128)S(1)}, u32[]{:S(2)}, u32[]{:S(2)}) collective-permute-start(f32[136,128]{1,0:T(8,128)S(1)} %get-tuple-element.58), channel_id=1, source_target_pairs={{0,12},{4,8},{8,4},{12,0},{16,28},{20,24},{24,20},{28,16},{1,13},{... | collective-permute-start | bytes 208904 | tf_op jit(solution)/shard_map/ppermute | solution.py:104
  6.9 5.1 %collective-permute-start.1 = (f32[136,128]{1,0:T(8,128)S(1)}, f32[136,128]{1,0:T(8,128)S(1)}, u32[]{:S(2)}, u32[]{:S(2)}) collective-permute-start(f32[136,128]{1,0:T(8,128)S(1)} %get-tuple-element.59), channel_id=1, source_target_pairs={{0,4},{4,0},{8,12},{12,8},{16,20},{20,16},{24,28},{28,24},{1,5},{5... | collective-permute-start | bytes 208904 | tf_op jit(solution)/shard_map/ppermute | solution.py:104
  7.4 4.6 %collective-permute-start.2 = (f32[136,128]{1,0:T(8,128)S(1)}, f32[136,128]{1,0:T(8,128)S(1)}, u32[]{:S(2)}, u32[]{:S(2)}) collective-permute-start(f32[136,128]{1,0:T(8,128)S(1)} %get-tuple-element.60), channel_id=1, source_target_pairs={{0,8},{4,12},{8,0},{12,4},{16,24},{20,28},{24,16},{28,20},{1,9},{5... | collective-permute-start | bytes 208904 | tf_op jit(solution)/shard_map/ppermute | solution.py:104
  7.5 7.2 %collective-permute-start.6 = (f32[128,128]{1,0:T(8,128)S(1)}, f32[128,128]{1,0:T(8,128)S(1)}, u32[]{:S(2)}, u32[]{:S(2)}) collective-permute-start(f32[128,128]{1,0:T(8,128)S(1)} %get-tuple-element.67), channel_id=1, source_target_pairs={{0,12},{4,8},{8,4},{12,0},{16,28},{20,24},{24,20},{28,16},{1,13},{... | collective-permute-start | bytes 196616 | tf_op jit(solution)/shard_map/ppermute | solution.py:104
  10.3 4.3 %collective-permute-start.7 = (f32[128,128]{1,0:T(8,128)S(1)}, f32[128,128]{1,0:T(8,128)S(1)}, u32[]{:S(2)}, u32[]{:S(2)}) collective-permute-start(f32[128,128]{1,0:T(8,128)S(1)} %get-tuple-element.68), channel_id=1, source_target_pairs={{0,4},{4,0},{8,12},{12,8},{16,20},{20,16},{24,28},{28,24},{1,5},{5... | collective-permute-start | bytes 196616 | tf_op jit(solution)/shard_map/ppermute | solution.py:104
  10.9 4.3 %collective-permute-start.8 = (f32[128,128]{1,0:T(8,128)S(1)}, f32[128,128]{1,0:T(8,128)S(1)}, u32[]{:S(2)}, u32[]{:S(2)}) collective-permute-start(f32[128,128]{1,0:T(8,128)S(1)} %get-tuple-element.69), channel_id=1, source_target_pairs={{0,8},{4,12},{8,0},{12,4},{16,24},{20,28},{24,16},{28,20},{1,9},{5... | collective-permute-start | bytes 196616 | tf_op jit(solution)/shard_map/ppermute | solution.py:104
  12.0 7.3 %collective-permute-start.3 = (f32[136,128]{1,0:T(8,128)S(1)}, f32[136,128]{1,0:T(8,128)S(1)}, u32[]{:S(2)}, u32[]{:S(2)}) collective-permute-start(f32[136,128]{1,0:T(8,128)S(1)} %get-tuple-element.61.refs_4_), channel_id=1, source_target_pairs={{0,16},{4,20},{8,24},{12,28},{16,0},{20,4},{24,8},{28,12},{1,17},{... | collective-permute-start | bytes 208904 | tf_op jit(solution)/shard_map/ppermute | solution.py:118
  15.2 4.2 %copy-start.3 = (f32[8,128,128]{2,1,0:T(8,128)S(1)}, f32[8,128,128]{2,1,0:T(8,128)}, u32[]{:S(2)}) copy-start(f32[8,128,128]{2,1,0:T(8,128)} %param.14) | copy-start | bytes 1572868
  15.2 10.4 %copy-start.5 = (bf16[256,1024]{1,0:T(8,128)(2,1)S(1)}, bf16[256,1024]{1,0:T(8,128)(2,1)}, u32[]{:S(2)}) copy-start(bf16[256,1024]{1,0:T(8,128)(2,1)} %upstream_ref.1) | copy-start | bytes 1572868
  15.3 5.7 %collective-permute-start.9 = (f32[128,128]{1,0:T(8,128)S(1)}, f32[128,128]{1,0:T(8,128)S(1)}, u32[]{:S(2)}, u32[]{:S(2)}) collective-permute-start(f32[128,128]{1,0:T(8,128)S(1)} %shard_map.114.refs_4_), channel_id=1, source_target_pairs={{0,16},{4,20},{8,24},{12,28},{16,0},{20,4},{24,8},{28,12},{1,17},{... | collective-permute-start | bytes 196616 | tf_op jit(solution)/shard_map/ppermute | solution.py:118
  19.4 6.3 %copy-start.1 = (bf16[256,1024]{1,0:T(8,128)(2,1)S(1)}, bf16[256,1024]{1,0:T(8,128)(2,1)}, u32[]{:S(2)}) copy-start(bf16[256,1024]{1,0:T(8,128)(2,1)} %refs_9_.1) | copy-start | bytes 1572868
  19.4 6.3 %copy-start.2 = (bf16[256,1024]{1,0:T(8,128)(2,1)S(1)}, bf16[256,1024]{1,0:T(8,128)(2,1)}, u32[]{:S(2)}) copy-start(bf16[256,1024]{1,0:T(8,128)(2,1)} %query_ref.3) | copy-start | bytes 1572868
  19.5 6.2 %copy-start = (bf16[256,1024]{1,0:T(8,128)(2,1)S(1)}, bf16[256,1024]{1,0:T(8,128)(2,1)}, u32[]{:S(2)}) copy-start(bf16[256,1024]{1,0:T(8,128)(2,1)} %refs_8_.3) | copy-start | bytes 1572868
  19.5 5.7 %collective-permute-start.4 = (f32[128,128]{1,0:T(8,128)S(1)}, f32[128,128]{1,0:T(8,128)S(1)}, u32[]{:S(2)}, u32[]{:S(2)}) collective-permute-start(f32[128,128]{1,0:T(8,128)S(1)} %get-tuple-element.64), channel_id=1, source_target_pairs={{0,4},{4,0},{8,12},{12,8},{16,20},{20,16},{24,28},{28,24},{1,5},{5... | collective-permute-start | bytes 196616 | tf_op jit(solution)/shard_map/ppermute | solution.py:104
  20.6 5.0 %collective-permute-start.5 = (f32[128,128]{1,0:T(8,128)S(1)}, f32[128,128]{1,0:T(8,128)S(1)}, u32[]{:S(2)}, u32[]{:S(2)}) collective-permute-start(f32[128,128]{1,0:T(8,128)S(1)} %get-tuple-element.65), channel_id=1, source_target_pairs={{0,8},{4,12},{8,0},{12,4},{16,24},{20,28},{24,16},{28,20},{1,9},{5... | collective-permute-start | bytes 196616 | tf_op jit(solution)/shard_map/ppermute | solution.py:104
  21.1 7.5 %collective-permute-start.12 = (f32[256,128]{1,0:T(8,128)S(1)}, f32[256,128]{1,0:T(8,128)S(1)}, u32[]{:S(2)}, u32[]{:S(2)}) collective-permute-start(f32[256,128]{1,0:T(8,128)S(1)} %get-tuple-element.75), channel_id=1, source_target_pairs={{0,12},{4,8},{8,4},{12,0},{16,28},{20,24},{24,20},{28,16},{1,13},{... | collective-permute-start | bytes 393224 | tf_op jit(solution)/shard_map/ppermute | solution.py:104
  23.2 2.5 %copy-start.6 = (f32[1024]{0:T(1024)S(1)}, f32[1024]{0:T(1024)}, u32[]{:S(2)}) copy-start(f32[1024]{0:T(1024)} %param.13) | copy-start | bytes 12292
  23.2 4.9 %collective-permute-start.10 = (f32[128,128]{1,0:T(8,128)S(1)}, f32[128,128]{1,0:T(8,128)S(1)}, u32[]{:S(2)}, u32[]{:S(2)}) collective-permute-start(f32[128,128]{1,0:T(8,128)S(1)} %get-tuple-element.73), channel_id=1, source_target_pairs={{0,4},{4,0},{8,12},{12,8},{16,20},{20,16},{24,28},{28,24},{1,5},{5... | collective-permute-start | bytes 196616 | tf_op jit(solution)/shard_map/ppermute | solution.py:104
  24.3 4.3 %collective-permute-start.11 = (f32[128,128]{1,0:T(8,128)S(1)}, f32[128,128]{1,0:T(8,128)S(1)}, u32[]{:S(2)}, u32[]{:S(2)}) collective-permute-start(f32[128,128]{1,0:T(8,128)S(1)} %get-tuple-element.74), channel_id=1, source_target_pairs={{0,8},{4,12},{8,0},{12,4},{16,24},{20,28},{24,16},{28,20},{1,9},{5... | collective-permute-start | bytes 196616 | tf_op jit(solution)/shard_map/ppermute | solution.py:104
  29.2 1.8 %collective-permute-start.15 = (f32[8,256]{1,0:T(8,128)S(1)}, f32[8,256]{1,0:T(8,128)S(1)}, u32[]{:S(2)}, u32[]{:S(2)}) collective-permute-start(f32[8,256]{1,0:T(8,128)S(1)} %get-tuple-element.80.refs_0_), channel_id=1, source_target_pairs={{0,3},{1,0},{2,1},{3,2},{4,7},{5,4},{6,5},{7,6},{8,11},{9,8},{10,9... | collective-permute-start | bytes 24584 | tf_op jit(solution)/shard_map/ppermute | solution.py:578
  29.2 3.7 %collective-permute-start.14 = (f32[8,256]{1,0:T(8,128)S(1)}, f32[8,256]{1,0:T(8,128)S(1)}, u32[]{:S(2)}, u32[]{:S(2)}) collective-permute-start(f32[8,256]{1,0:T(8,128)S(1)} %get-tuple-element.80.refs_0_), channel_id=1, source_target_pairs={{0,2},{1,3},{2,0},{3,1},{4,6},{5,7},{6,4},{7,5},{8,10},{9,11},{10,... | collective-permute-start | bytes 24584 | tf_op jit(solution)/shard_map/ppermute | solution.py:578
  30.8 3.1 %collective-permute-start.13 = (f32[8,256]{1,0:T(8,128)S(1)}, f32[8,256]{1,0:T(8,128)S(1)}, u32[]{:S(2)}, u32[]{:S(2)}) collective-permute-start(f32[8,256]{1,0:T(8,128)S(1)} %get-tuple-element.80.refs_0_), channel_id=1, source_target_pairs={{0,1},{1,2},{2,3},{3,0},{4,5},{5,6},{6,7},{7,4},{8,9},{9,10},{10,1... | collective-permute-start | bytes 24584 | tf_op jit(solution)/shard_map/ppermute | solution.py:578
  34.6 6.9 %collective-permute-start.16 = (f32[256,128]{1,0:T(8,128)S(1)}, f32[256,128]{1,0:T(8,128)S(1)}, u32[]{:S(2)}, u32[]{:S(2)}) collective-permute-start(f32[256,128]{1,0:T(8,128)S(1)} %get-tuple-element.88), channel_id=1, source_target_pairs={{0,12},{4,8},{8,4},{12,0},{16,28},{20,24},{24,20},{28,16},{1,13},{... | collective-permute-start | bytes 393224 | tf_op jit(solution)/shard_map/ppermute | solution.py:104
  36.0 6.2 %collective-permute-start.17 = (f32[256,128]{1,0:T(8,128)S(1)}, f32[256,128]{1,0:T(8,128)S(1)}, u32[]{:S(2)}, u32[]{:S(2)}) collective-permute-start(f32[256,128]{1,0:T(8,128)S(1)} %get-tuple-element.89), channel_id=1, source_target_pairs={{0,4},{4,0},{8,12},{12,8},{16,20},{20,16},{24,28},{28,24},{1,5},{5... | collective-permute-start | bytes 393224 | tf_op jit(solution)/shard_map/ppermute | solution.py:104
  37.0 5.3 %collective-permute-start.18 = (f32[256,128]{1,0:T(8,128)S(1)}, f32[256,128]{1,0:T(8,128)S(1)}, u32[]{:S(2)}, u32[]{:S(2)}) collective-permute-start(f32[256,128]{1,0:T(8,128)S(1)} %get-tuple-element.90), channel_id=1, source_target_pairs={{0,8},{4,12},{8,0},{12,4},{16,24},{20,28},{24,16},{28,20},{1,9},{5... | collective-permute-start | bytes 393224 | tf_op jit(solution)/shard_map/ppermute | solution.py:104
  38.1 4.1 %copy-start.4 = (f32[8,128,128]{2,1,0:T(8,128)S(1)}, f32[8,128,128]{2,1,0:T(8,128)}, u32[]{:S(2)}) copy-start(f32[8,128,128]{2,1,0:T(8,128)} %param.15) | copy-start | bytes 1572868
  42.4 8.6 %collective-permute-start.19 = (f32[264,128]{1,0:T(8,128)S(1)}, f32[264,128]{1,0:T(8,128)S(1)}, u32[]{:S(2)}, u32[]{:S(2)}) collective-permute-start(f32[264,128]{1,0:T(8,128)S(1)} %get-tuple-element.92), channel_id=1, source_target_pairs={{0,4},{4,0},{8,12},{12,8},{16,20},{20,16},{24,28},{28,24},{1,5},{5... | collective-permute-start | bytes 405512 | tf_op jit(solution)/shard_map/ppermute | solution.py:104
  43.5 7.5 %collective-permute-start.22 = (f32[256,128]{1,0:T(8,128)S(1)}, f32[256,128]{1,0:T(8,128)S(1)}, u32[]{:S(2)}, u32[]{:S(2)}) collective-permute-start(f32[256,128]{1,0:T(8,128)S(1)} %shard_map.121.refs_4_), channel_id=1, source_target_pairs={{0,16},{4,20},{8,24},{12,28},{16,0},{20,4},{24,8},{28,12},{1,17},{... | collective-permute-start | bytes 393224 | tf_op jit(solution)/shard_map/ppermute | solution.py:118
  46.5 9.2 %collective-permute-start.20 = (f32[256,128]{1,0:T(8,128)S(1)}, f32[256,128]{1,0:T(8,128)S(1)}, u32[]{:S(2)}, u32[]{:S(2)}) collective-permute-start(f32[256,128]{1,0:T(8,128)S(1)} %get-tuple-element.93), channel_id=1, source_target_pairs={{0,8},{4,12},{8,0},{12,4},{16,24},{20,28},{24,16},{28,20},{1,9},{5... | collective-permute-start | bytes 393224 | tf_op jit(solution)/shard_map/ppermute | solution.py:104
  47.3 9.0 %collective-permute-start.21 = (f32[256,128]{1,0:T(8,128)S(1)}, f32[256,128]{1,0:T(8,128)S(1)}, u32[]{:S(2)}, u32[]{:S(2)}) collective-permute-start(f32[256,128]{1,0:T(8,128)S(1)} %get-tuple-element.94), channel_id=1, source_target_pairs={{0,12},{4,8},{8,4},{12,0},{16,28},{20,24},{24,20},{28,16},{1,13},{... | collective-permute-start | bytes 393224 | tf_op jit(solution)/shard_map/ppermute | solution.py:104
  51.2 7.2 %collective-permute-start.23 = (f32[256,128]{1,0:T(8,128)S(1)}, f32[256,128]{1,0:T(8,128)S(1)}, u32[]{:S(2)}, u32[]{:S(2)}) collective-permute-start(f32[256,128]{1,0:T(8,128)S(1)} %get-tuple-element.96), channel_id=1, source_target_pairs={{0,12},{4,8},{8,4},{12,0},{16,28},{20,24},{24,20},{28,16},{1,13},{... | collective-permute-start | bytes 393224 | tf_op jit(solution)/shard_map/ppermute | solution.py:104
  52.1 8.3 %collective-permute-start.24 = (f32[256,128]{1,0:T(8,128)S(1)}, f32[256,128]{1,0:T(8,128)S(1)}, u32[]{:S(2)}, u32[]{:S(2)}) collective-permute-start(f32[256,128]{1,0:T(8,128)S(1)} %get-tuple-element.97), channel_id=1, source_target_pairs={{0,8},{4,12},{8,0},{12,4},{16,24},{20,28},{24,16},{28,20},{1,9},{5... | collective-permute-start | bytes 393224 | tf_op jit(solution)/shard_map/ppermute | solution.py:104
  53.8 6.5 %collective-permute-start.25 = (f32[256,128]{1,0:T(8,128)S(1)}, f32[256,128]{1,0:T(8,128)S(1)}, u32[]{:S(2)}, u32[]{:S(2)}) collective-permute-start(f32[256,128]{1,0:T(8,128)S(1)} %get-tuple-element.98), channel_id=1, source_target_pairs={{0,4},{4,0},{8,12},{12,8},{16,20},{20,16},{24,28},{28,24},{1,5},{5... | collective-permute-start | bytes 393224 | tf_op jit(solution)/shard_map/ppermute | solution.py:104

commit v17 on v16

--- a/solution.py
+++ b/solution.py
@@ -76,7 +76,7 @@
         self.near = [way for way in range(self.members) if way.bit_count() == 1]
         self.far = [way for way in range(self.members) if way.bit_count() > 1]
         self.ways = [0] + self.far + self.near
-        self.early_ways = [0] + self.near + self.far
+        self.early_ways = [0] + self.near[1:] + self.far + self.near[:1]
         self.late_ways = [0] + self.far + self.near[::-1]
 
     def member(self):

time: 62 us -> 60.9 us (0.982)
  waiting for transfers between devices: 15.4 us -> 13.3 us
  starting transfers between devices: 34.2 us -> 35.3 us
    ppermute x3, waiting for transfers between devices: 3.72 us -> 2.24 us  [from_groups(): lax.ppermute(piece, 'seq', [(i, (i + step * self.members) % self.blocks)...]
    ppermute x20, starting transfers between devices: 24.2 us -> 25.4 us  [swap(): return lax.ppermute(piece, 'seq', pairs) if way else piece]
where the time goes in v17:
time: 60.9 us; the launch traced here: 60.7 us
  starting transfers between devices  35.3 us (58%)
  waiting for transfers between devices  13.3 us (22%)
  Pallas kernels  11.3 us (19%)
  between operations  0.76 us (1%)
    ppermute x20, starting transfers between devices, swap(): return lax.ppermute(piece, 'seq', pairs) if way else piece  25.4 us
    pallas_call x14, Pallas kernels, call(): pl.pallas_call(body, out_shape=outs, in_specs=specs or [VMEM] * len(opera...  11.3 us
    ppermute x20, waiting for transfers between devices, swap(): return lax.ppermute(piece, 'seq', pairs) if way else piece  8.17 us
    ppermute x3, starting transfers between devices, from_groups(): lax.ppermute(piece, 'seq', [(i, (i + step * self.members) % self.blocks)...  8.11 us
    ppermute x3, waiting for transfers between devices, on_device(): lax.ppermute(sums, 'head', [(i, (i + step) % parties) for i in range(part...  2.85 us
    ppermute x3, waiting for transfers between devices, from_groups(): lax.ppermute(piece, 'seq', [(i, (i + step * self.members) % self.blocks)...  2.24 us
    ppermute x3, starting transfers between devices, on_device(): lax.ppermute(sums, 'head', [(i, (i + step) % parties) for i in range(part...  1.8 us
  transfers between devices with their start and end apart: 26, of which 14 were waited for; matrix products, arithmetic and copies ran while one was open for 0% of the time, Pallas kernels for 10%

profile of v17, /device:TPU:0, one launch (start us, length us, event | category | flops | bytes accessed | tf_op | source)
XLA Modules:
  0.0 60.7 jit_solution(17028393579772791956)
XLA Ops:
  0.6 2.2 %shard_map.111 = (f32[136,128]{1,0:T(8,128)S(1)}, f32[136,128]{1,0:T(8,128)S(1)}, f32[136,128]{1,0:T(8,128)S(1)}, f32[136,128]{1,0:T(8,128)S(1)}, f32[128,128]{1...) custom-call(bf16[256,1024]{1,0:T(8,128)(2,1)} %refs_8_.3, ...), custom_call_target="tpu_custom_call" | custom-call | tf_op jit(solution)/shard_map/pallas_call | solution.py:25
  2.8 4.0 %collective-permute-start = (f32[136,128]{1,0:T(8,128)S(1)}, f32[136,128]{1,0:T(8,128)S(1)}, u32[]{:S(2)}, u32[]{:S(2)}) collective-permute-start(f32[136,128]{1,0:T(8,128)S(1)} %get-tuple-element.58), channel_id=1, source_target_pairs={{0,12},{4,8},{8,4},{12,0},{16,28},{20,24},{24,20},{28,16},{1,13},{... | collective-permute-start | bytes 208904 | tf_op jit(solution)/shard_map/ppermute | solution.py:104
  6.9 0.5 collective-permute-start.1
  7.4 0.1 collective-permute-start.2
  7.5 2.8 %collective-permute-start.6 = (f32[128,128]{1,0:T(8,128)S(1)}, f32[128,128]{1,0:T(8,128)S(1)}, u32[]{:S(2)}, u32[]{:S(2)}) collective-permute-start(f32[128,128]{1,0:T(8,128)S(1)} %get-tuple-element.67), channel_id=1, source_target_pairs={{0,12},{4,8},{8,4},{12,0},{16,28},{20,24},{24,20},{28,16},{1,13},{... | collective-permute-start | bytes 196616 | tf_op jit(solution)/shard_map/ppermute | solution.py:104
  10.3 0.5 collective-permute-start.7
  10.9 0.8 %collective-permute-start.8 = (f32[128,128]{1,0:T(8,128)S(1)}, f32[128,128]{1,0:T(8,128)S(1)}, u32[]{:S(2)}, u32[]{:S(2)}) collective-permute-start(f32[128,128]{1,0:T(8,128)S(1)} %get-tuple-element.69), channel_id=1, source_target_pairs={{0,8},{4,12},{8,0},{12,4},{16,24},{20,28},{24,16},{28,20},{1,9},{5... | collective-permute-start | bytes 196616 | tf_op jit(solution)/shard_map/ppermute | solution.py:104
  11.6 0.4 collective-permute-done.1.refs_2_
  12.0 2.7 %collective-permute-start.3 = (f32[136,128]{1,0:T(8,128)S(1)}, f32[136,128]{1,0:T(8,128)S(1)}, u32[]{:S(2)}, u32[]{:S(2)}) collective-permute-start(f32[136,128]{1,0:T(8,128)S(1)} %get-tuple-element.61.refs_4_), channel_id=1, source_target_pairs={{0,16},{4,20},{8,24},{12,28},{16,0},{20,4},{24,8},{28,12},{1,17},{... | collective-permute-start | bytes 208904 | tf_op jit(solution)/shard_map/ppermute | solution.py:118
  14.7 0.5 collective-permute-done.8.refs_3_
  15.3 2.6 %collective-permute-start.9 = (f32[128,128]{1,0:T(8,128)S(1)}, f32[128,128]{1,0:T(8,128)S(1)}, u32[]{:S(2)}, u32[]{:S(2)}) collective-permute-start(f32[128,128]{1,0:T(8,128)S(1)} %shard_map.114.refs_4_), channel_id=1, source_target_pairs={{0,16},{4,20},{8,24},{12,28},{16,0},{20,4},{24,8},{28,12},{1,17},{... | collective-permute-start | bytes 196616 | tf_op jit(solution)/shard_map/ppermute | solution.py:118
  17.8 1.5 %collective-permute-done.3.refs_5_ = f32[136,128]{1,0:T(8,128)S(1)} collective-permute-done((f32[136,128]{1,0:T(8,128)S(1)}, f32[136,128]{1,0:T(8,128)S(1)}, u32[]{:S(2)}, u32[]{:S(2)}) %collective-permute-start.3) | collective-permute-done | bytes 69664 | tf_op jit(solution)/shard_map/ppermute | solution.py:118
  19.5 1.1 %collective-permute-start.4 = (f32[128,128]{1,0:T(8,128)S(1)}, f32[128,128]{1,0:T(8,128)S(1)}, u32[]{:S(2)}, u32[]{:S(2)}) collective-permute-start(f32[128,128]{1,0:T(8,128)S(1)} %get-tuple-element.64), channel_id=1, source_target_pairs={{0,4},{4,0},{8,12},{12,8},{16,20},{20,16},{24,28},{28,24},{1,5},{5... | collective-permute-start | bytes 196616 | tf_op jit(solution)/shard_map/ppermute | solution.py:104
  20.6 0.3 collective-permute-start.5
  21.1 2.1 %collective-permute-start.12 = (f32[256,128]{1,0:T(8,128)S(1)}, f32[256,128]{1,0:T(8,128)S(1)}, u32[]{:S(2)}, u32[]{:S(2)}) collective-permute-start(f32[256,128]{1,0:T(8,128)S(1)} %get-tuple-element.75), channel_id=1, source_target_pairs={{0,12},{4,8},{8,4},{12,0},{16,28},{20,24},{24,20},{28,16},{1,13},{... | collective-permute-start | bytes 393224 | tf_op jit(solution)/shard_map/ppermute | solution.py:104
  23.2 1.1 %collective-permute-start.10 = (f32[128,128]{1,0:T(8,128)S(1)}, f32[128,128]{1,0:T(8,128)S(1)}, u32[]{:S(2)}, u32[]{:S(2)}) collective-permute-start(f32[128,128]{1,0:T(8,128)S(1)} %get-tuple-element.73), channel_id=1, source_target_pairs={{0,4},{4,0},{8,12},{12,8},{16,20},{20,16},{24,28},{28,24},{1,5},{5... | collective-permute-start | bytes 196616 | tf_op jit(solution)/shard_map/ppermute | solution.py:104
  24.3 0.3 collective-permute-start.11
  24.6 0.6 collective-permute-done.4.refs_0_.refs_1_
  25.2 0.4 collective-permute-done.5.refs_1_.refs_2_
  25.7 1.2 %shard_map.116 = (bf16[8,256,256]{2,1,0:T(8,128)(2,1)S(1)}, f32[256,1024]{1,0:T(8,128)S(1)}, f32[256,1024]{1,0:T(8,128)S(1)}, bf16[8,128,256]{2,1,0:T(8,128)(2,1)S(1)}) custom-call(bf16[256,1024]{1,0:T(8,128)(2,1)S(1)} %copy-done.2, bf16[256,1024]{1,0:T(8,128)(2,1)S(1)} %copy-done, bf16[256,1024]{1,0:T(8,128)(2,1)S(1)} %copy-done.1, ...), custom_call_target="tpu_custom_call" | custom-call | flops 1000000000 | tf_op jit(solution)/shard_map/pallas_call | solution.py:25
  26.9 1.2 %collective-permute-done.10.refs_4_ = f32[128,128]{1,0:T(8,128)S(1)} collective-permute-done((f32[128,128]{1,0:T(8,128)S(1)}, f32[128,128]{1,0:T(8,128)S(1)}, u32[]{:S(2)}, u32[]{:S(2)}) %collective-permute-start.10) | collective-permute-done | bytes 65568 | tf_op jit(solution)/shard_map/ppermute | solution.py:104
  28.1 0.4 collective-permute-done.11.refs_5_
  28.5 0.7 %shard_map.117 = (f32[256,1024]{1,0:T(8,128)S(1)}, f32[8,256]{1,0:T(8,128)S(1)}, bf16[1024,128]{1,0:T(8,128)(2,1)S(1)}) custom-call(f32[128,128]{1,0:T(8,128)S(1)} %get-tuple-element.63.refs_0_, f32[128,128]{1,0:T(8,128)S(1)} %collective-permute-done.4.refs_0_.refs_1_, f32[128,128]{1,0:T(8,128)S(1)} %collective-permute-done.5.refs_1_.refs_2_, ...), custom_call_target="tpu_custom_call" | custom-call | tf_op jit(solution)/shard_map/pallas_call | solution.py:25
  29.2 1.6 %collective-permute-start.14 = (f32[8,256]{1,0:T(8,128)S(1)}, f32[8,256]{1,0:T(8,128)S(1)}, u32[]{:S(2)}, u32[]{:S(2)}) collective-permute-start(f32[8,256]{1,0:T(8,128)S(1)} %get-tuple-element.80.refs_0_), channel_id=1, source_target_pairs={{0,2},{1,3},{2,0},{3,1},{4,6},{5,7},{6,4},{7,5},{8,10},{9,11},{10,... | collective-permute-start | bytes 24584 | tf_op jit(solution)/shard_map/ppermute | solution.py:578
  30.8 0.2 collective-permute-start.13
  31.0 1.9 %collective-permute-done.14.refs_2_ = f32[8,256]{1,0:T(8,128)S(1)} collective-permute-done((f32[8,256]{1,0:T(8,128)S(1)}, f32[8,256]{1,0:T(8,128)S(1)}, u32[]{:S(2)}, u32[]{:S(2)}) %collective-permute-start.14) | collective-permute-done | bytes 8224 | tf_op jit(solution)/shard_map/ppermute | solution.py:578
  32.9 1.0 %collective-permute-done.13.refs_1_ = f32[8,256]{1,0:T(8,128)S(1)} collective-permute-done((f32[8,256]{1,0:T(8,128)S(1)}, f32[8,256]{1,0:T(8,128)S(1)}, u32[]{:S(2)}, u32[]{:S(2)}) %collective-permute-start.13) | collective-permute-done | bytes 8224 | tf_op jit(solution)/shard_map/ppermute | solution.py:578
  33.9 0.7 %shard_map.118 = (bf16[256,1024]{1,0:T(8,128)(2,1)S(1)}, f32[1024,128]{1,0:T(8,128)S(1)}, f32[256,128]{1,0:T(8,128)S(1)}, f32[256,128]{1,0:T(8,128)S(1)}, f32[25...) custom-call(f32[8,256]{1,0:T(8,128)S(1)} %get-tuple-element.80.refs_0_, f32[8,256]{1,0:T(8,128)S(1)} %collective-permute-done.13.refs_1_, ...), custom_call_target="tpu_custom_call" | custom-call | tf_op jit(solution)/shard_map/pallas_call | solution.py:25
  34.6 1.4 %collective-permute-start.16 = (f32[256,128]{1,0:T(8,128)S(1)}, f32[256,128]{1,0:T(8,128)S(1)}, u32[]{:S(2)}, u32[]{:S(2)}) collective-permute-start(f32[256,128]{1,0:T(8,128)S(1)} %get-tuple-element.88), channel_id=1, source_target_pairs={{0,12},{4,8},{8,4},{12,0},{16,28},{20,24},{24,20},{28,16},{1,13},{... | collective-permute-start | bytes 393224 | tf_op jit(solution)/shard_map/ppermute | solution.py:104
  36.0 0.9 %collective-permute-start.17 = (f32[256,128]{1,0:T(8,128)S(1)}, f32[256,128]{1,0:T(8,128)S(1)}, u32[]{:S(2)}, u32[]{:S(2)}) collective-permute-start(f32[256,128]{1,0:T(8,128)S(1)} %get-tuple-element.89), channel_id=1, source_target_pairs={{0,4},{4,0},{8,12},{12,8},{16,20},{20,16},{24,28},{28,24},{1,5},{5... | collective-permute-start | bytes 393224 | tf_op jit(solution)/shard_map/ppermute | solution.py:104
  37.0 1.2 %collective-permute-start.18 = (f32[256,128]{1,0:T(8,128)S(1)}, f32[256,128]{1,0:T(8,128)S(1)}, u32[]{:S(2)}, u32[]{:S(2)}) collective-permute-start(f32[256,128]{1,0:T(8,128)S(1)} %get-tuple-element.90), channel_id=1, source_target_pairs={{0,8},{4,12},{8,0},{12,4},{16,24},{20,28},{24,16},{28,20},{1,9},{5... | collective-permute-start | bytes 393224 | tf_op jit(solution)/shard_map/ppermute | solution.py:104
  38.1 3.4 %shard_map.119 = (bf16[256,1024]{1,0:T(8,128)(2,1)}, f32[256,1024]{1,0:T(8,128)S(1)}, f32[256,1024]{1,0:T(8,128)S(1)}, f32[8,256,128]{2,1,0:T(8,128)S(1)}) custom-call(bf16[256,1024]{1,0:T(8,128)(2,1)S(1)} %get-tuple-element.83.attn_grad_ref, bf16[256,1024]{1,0:T(8,128)(2,1)S(1)} %copy-done.2, bf16[256,1024]{1,0:T(8,128)(2,1)S(1)} %copy-done, ...), custom_call_target="tpu_custom_call" | custom-call | flops 671088640 | tf_op jit(solution)/shard_map/pallas_call | solution.py:25
  41.5 0.7 %collective-permute-done.17.refs_2_ = f32[256,128]{1,0:T(8,128)S(1)} collective-permute-done((f32[256,128]{1,0:T(8,128)S(1)}, f32[256,128]{1,0:T(8,128)S(1)}, u32[]{:S(2)}, u32[]{:S(2)}) %collective-permute-start.17) | collective-permute-done | bytes 131104 | tf_op jit(solution)/shard_map/ppermute | solution.py:104
  42.2 0.2 shard_map.120
  42.4 1.0 %collective-permute-start.19 = (f32[264,128]{1,0:T(8,128)S(1)}, f32[264,128]{1,0:T(8,128)S(1)}, u32[]{:S(2)}, u32[]{:S(2)}) collective-permute-start(f32[264,128]{1,0:T(8,128)S(1)} %get-tuple-element.92), channel_id=1, source_target_pairs={{0,8},{4,12},{8,0},{12,4},{16,24},{20,28},{24,16},{28,20},{1,9},{5... | collective-permute-start | bytes 405512 | tf_op jit(solution)/shard_map/ppermute | solution.py:104
  43.4 0.1 shard_map.121.refs_4_
  43.5 2.9 %collective-permute-start.22 = (f32[256,128]{1,0:T(8,128)S(1)}, f32[256,128]{1,0:T(8,128)S(1)}, u32[]{:S(2)}, u32[]{:S(2)}) collective-permute-start(f32[256,128]{1,0:T(8,128)S(1)} %shard_map.121.refs_4_), channel_id=1, source_target_pairs={{0,16},{4,20},{8,24},{12,28},{16,0},{20,4},{24,8},{28,12},{1,17},{... | collective-permute-start | bytes 393224 | tf_op jit(solution)/shard_map/ppermute | solution.py:118
  46.3 1.6 %collective-permute-start.20 = (f32[256,128]{1,0:T(8,128)S(1)}, f32[256,128]{1,0:T(8,128)S(1)}, u32[]{:S(2)}, u32[]{:S(2)}) collective-permute-start(f32[256,128]{1,0:T(8,128)S(1)} %get-tuple-element.93), channel_id=1, source_target_pairs={{0,12},{4,8},{8,4},{12,0},{16,28},{20,24},{24,20},{28,16},{1,13},{... | collective-permute-start | bytes 393224 | tf_op jit(solution)/shard_map/ppermute | solution.py:104
  48.0 0.8 %collective-permute-start.21 = (f32[256,128]{1,0:T(8,128)S(1)}, f32[256,128]{1,0:T(8,128)S(1)}, u32[]{:S(2)}, u32[]{:S(2)}) collective-permute-start(f32[256,128]{1,0:T(8,128)S(1)} %get-tuple-element.94), channel_id=1, source_target_pairs={{0,4},{4,0},{8,12},{12,8},{16,20},{20,16},{24,28},{28,24},{1,5},{5... | collective-permute-start | bytes 393224 | tf_op jit(solution)/shard_map/ppermute | solution.py:104
  48.8 0.7 %collective-permute-done.22.refs_5_ = f32[256,128]{1,0:T(8,128)S(1)} collective-permute-done((f32[256,128]{1,0:T(8,128)S(1)}, f32[256,128]{1,0:T(8,128)S(1)}, u32[]{:S(2)}, u32[]{:S(2)}) %collective-permute-start.22) | collective-permute-done | bytes 131104 | tf_op jit(solution)/shard_map/ppermute | solution.py:118
  49.5 0.6 collective-permute-done.19.refs_9_.refs_0_
  50.1 0.2 shard_map.122
  50.3 4.0 %collective-permute-start.23 = (f32[256,128]{1,0:T(8,128)S(1)}, f32[256,128]{1,0:T(8,128)S(1)}, u32[]{:S(2)}, u32[]{:S(2)}) collective-permute-start(f32[256,128]{1,0:T(8,128)S(1)} %get-tuple-element.96), channel_id=1, source_target_pairs={{0,12},{4,8},{8,4},{12,0},{16,28},{20,24},{24,20},{28,16},{1,13},{... | collective-permute-start | bytes 393224 | tf_op jit(solution)/shard_map/ppermute | solution.py:104
  54.3 0.6 %collective-permute-start.25 = (f32[256,128]{1,0:T(8,128)S(1)}, f32[256,128]{1,0:T(8,128)S(1)}, u32[]{:S(2)}, u32[]{:S(2)}) collective-permute-start(f32[256,128]{1,0:T(8,128)S(1)} %get-tuple-element.98), channel_id=1, source_target_pairs={{0,4},{4,0},{8,12},{12,8},{16,20},{20,16},{24,28},{28,24},{1,5},{5... | collective-permute-start | bytes 393224 | tf_op jit(solution)/shard_map/ppermute | solution.py:104
  55.0 1.0 %shard_map.123 = (bf16[256,1024]{1,0:T(8,128)(2,1)}, bf16[256,1024]{1,0:T(8,128)(2,1)}, f32[1024,128]{1,0:T(8,128)}) custom-call(f32[256,128]{1,0:T(8,128)S(1)} %get-tuple-element.95.refs_5_.refs_0_, f32[256,128]{1,0:T(8,128)S(1)} %get-tuple-element.103.refs_1_, f32[256,1024]{1,0:T(8,128)S(1)} %get-tuple-element.91.refs_6_.refs_2_, ...), custom_call_target="tpu_custom_call" | custom-call | tf_op jit(solution)/shard_map/pallas_call | solution.py:25
  55.9 1.7 %collective-permute-done.21.refs_2_ = f32[256,128]{1,0:T(8,128)S(1)} collective-permute-done((f32[256,128]{1,0:T(8,128)S(1)}, f32[256,128]{1,0:T(8,128)S(1)}, u32[]{:S(2)}, u32[]{:S(2)}) %collective-permute-start.21) | collective-permute-done | bytes 131104 | tf_op jit(solution)/shard_map/ppermute | solution.py:104
  57.7 1.6 %collective-permute-done.24.refs_4_ = f32[256,128]{1,0:T(8,128)S(1)} collective-permute-done((f32[256,128]{1,0:T(8,128)S(1)}, f32[256,128]{1,0:T(8,128)S(1)}, u32[]{:S(2)}, u32[]{:S(2)}) %collective-permute-start.24) | collective-permute-done | bytes 131104 | tf_op jit(solution)/shard_map/ppermute | solution.py:104
  59.3 1.4 %shard_map.124 = (bf16[256,1024]{1,0:T(8,128)(2,1)}, bf16[256,1024]{1,0:T(8,128)(2,1)}, f32[1024,128]{1,0:T(8,128)}) custom-call(f32[264,128]{1,0:T(8,128)S(1)} %collective-permute-done.19.refs_9_.refs_0_, f32[256,128]{1,0:T(8,128)S(1)} %collective-permute-done.20.refs_1_, ...), custom_call_target="tpu_custom_call", output_to_operand_aliasing={{0}: (14, {}), {1}: (15, {}), {2}: (16, {})} | custom-call | tf_op jit(solution)/shard_map/pallas_call | solution.py:25
  (32 shorter events, 0.3 us)
Async XLA Ops:
  2.8 8.0 %collective-permute-start = (f32[136,128]{1,0:T(8,128)S(1)}, f32[136,128]{1,0:T(8,128)S(1)}, u32[]{:S(2)}, u32[]{:S(2)}) collective-permute-start(f32[136,128]{1,0:T(8,128)S(1)} %get-tuple-element.58), channel_id=1, source_target_pairs={{0,12},{4,8},{8,4},{12,0},{16,28},{20,24},{24,20},{28,16},{1,13},{... | collective-permute-start | bytes 208904 | tf_op jit(solution)/shard_map/ppermute | solution.py:104
  6.9 5.1 %collective-permute-start.1 = (f32[136,128]{1,0:T(8,128)S(1)}, f32[136,128]{1,0:T(8,128)S(1)}, u32[]{:S(2)}, u32[]{:S(2)}) collective-permute-start(f32[136,128]{1,0:T(8,128)S(1)} %get-tuple-element.59), channel_id=1, source_target_pairs={{0,4},{4,0},{8,12},{12,8},{16,20},{20,16},{24,28},{28,24},{1,5},{5... | collective-permute-start | bytes 208904 | tf_op jit(solution)/shard_map/ppermute | solution.py:104
  7.4 4.6 %collective-permute-start.2 = (f32[136,128]{1,0:T(8,128)S(1)}, f32[136,128]{1,0:T(8,128)S(1)}, u32[]{:S(2)}, u32[]{:S(2)}) collective-permute-start(f32[136,128]{1,0:T(8,128)S(1)} %get-tuple-element.60), channel_id=1, source_target_pairs={{0,8},{4,12},{8,0},{12,4},{16,24},{20,28},{24,16},{28,20},{1,9},{5... | collective-permute-start | bytes 208904 | tf_op jit(solution)/shard_map/ppermute | solution.py:104
  7.5 7.2 %collective-permute-start.6 = (f32[128,128]{1,0:T(8,128)S(1)}, f32[128,128]{1,0:T(8,128)S(1)}, u32[]{:S(2)}, u32[]{:S(2)}) collective-permute-start(f32[128,128]{1,0:T(8,128)S(1)} %get-tuple-element.67), channel_id=1, source_target_pairs={{0,12},{4,8},{8,4},{12,0},{16,28},{20,24},{24,20},{28,16},{1,13},{... | collective-permute-start | bytes 196616 | tf_op jit(solution)/shard_map/ppermute | solution.py:104
  10.3 4.3 %collective-permute-start.7 = (f32[128,128]{1,0:T(8,128)S(1)}, f32[128,128]{1,0:T(8,128)S(1)}, u32[]{:S(2)}, u32[]{:S(2)}) collective-permute-start(f32[128,128]{1,0:T(8,128)S(1)} %get-tuple-element.68), channel_id=1, source_target_pairs={{0,4},{4,0},{8,12},{12,8},{16,20},{20,16},{24,28},{28,24},{1,5},{5... | collective-permute-start | bytes 196616 | tf_op jit(solution)/shard_map/ppermute | solution.py:104
  10.9 4.3 %collective-permute-start.8 = (f32[128,128]{1,0:T(8,128)S(1)}, f32[128,128]{1,0:T(8,128)S(1)}, u32[]{:S(2)}, u32[]{:S(2)}) collective-permute-start(f32[128,128]{1,0:T(8,128)S(1)} %get-tuple-element.69), channel_id=1, source_target_pairs={{0,8},{4,12},{8,0},{12,4},{16,24},{20,28},{24,16},{28,20},{1,9},{5... | collective-permute-start | bytes 196616 | tf_op jit(solution)/shard_map/ppermute | solution.py:104
  12.0 7.3 %collective-permute-start.3 = (f32[136,128]{1,0:T(8,128)S(1)}, f32[136,128]{1,0:T(8,128)S(1)}, u32[]{:S(2)}, u32[]{:S(2)}) collective-permute-start(f32[136,128]{1,0:T(8,128)S(1)} %get-tuple-element.61.refs_4_), channel_id=1, source_target_pairs={{0,16},{4,20},{8,24},{12,28},{16,0},{20,4},{24,8},{28,12},{1,17},{... | collective-permute-start | bytes 208904 | tf_op jit(solution)/shard_map/ppermute | solution.py:118
  15.2 4.2 %copy-start.3 = (f32[8,128,128]{2,1,0:T(8,128)S(1)}, f32[8,128,128]{2,1,0:T(8,128)}, u32[]{:S(2)}) copy-start(f32[8,128,128]{2,1,0:T(8,128)} %param.14) | copy-start | bytes 1572868
  15.2 10.4 %copy-start.5 = (bf16[256,1024]{1,0:T(8,128)(2,1)S(1)}, bf16[256,1024]{1,0:T(8,128)(2,1)}, u32[]{:S(2)}) copy-start(bf16[256,1024]{1,0:T(8,128)(2,1)} %upstream_ref.1) | copy-start | bytes 1572868
  15.3 5.7 %collective-permute-start.9 = (f32[128,128]{1,0:T(8,128)S(1)}, f32[128,128]{1,0:T(8,128)S(1)}, u32[]{:S(2)}, u32[]{:S(2)}) collective-permute-start(f32[128,128]{1,0:T(8,128)S(1)} %shard_map.114.refs_4_), channel_id=1, source_target_pairs={{0,16},{4,20},{8,24},{12,28},{16,0},{20,4},{24,8},{28,12},{1,17},{... | collective-permute-start | bytes 196616 | tf_op jit(solution)/shard_map/ppermute | solution.py:118
  19.4 6.3 %copy-start.1 = (bf16[256,1024]{1,0:T(8,128)(2,1)S(1)}, bf16[256,1024]{1,0:T(8,128)(2,1)}, u32[]{:S(2)}) copy-start(bf16[256,1024]{1,0:T(8,128)(2,1)} %refs_9_.1) | copy-start | bytes 1572868
  19.4 6.3 %copy-start.2 = (bf16[256,1024]{1,0:T(8,128)(2,1)S(1)}, bf16[256,1024]{1,0:T(8,128)(2,1)}, u32[]{:S(2)}) copy-start(bf16[256,1024]{1,0:T(8,128)(2,1)} %query_ref.3) | copy-start | bytes 1572868
  19.5 6.2 %copy-start = (bf16[256,1024]{1,0:T(8,128)(2,1)S(1)}, bf16[256,1024]{1,0:T(8,128)(2,1)}, u32[]{:S(2)}) copy-start(bf16[256,1024]{1,0:T(8,128)(2,1)} %refs_8_.3) | copy-start | bytes 1572868
  19.5 5.7 %collective-permute-start.4 = (f32[128,128]{1,0:T(8,128)S(1)}, f32[128,128]{1,0:T(8,128)S(1)}, u32[]{:S(2)}, u32[]{:S(2)}) collective-permute-start(f32[128,128]{1,0:T(8,128)S(1)} %get-tuple-element.64), channel_id=1, source_target_pairs={{0,4},{4,0},{8,12},{12,8},{16,20},{20,16},{24,28},{28,24},{1,5},{5... | collective-permute-start | bytes 196616 | tf_op jit(solution)/shard_map/ppermute | solution.py:104
  20.6 5.0 %collective-permute-start.5 = (f32[128,128]{1,0:T(8,128)S(1)}, f32[128,128]{1,0:T(8,128)S(1)}, u32[]{:S(2)}, u32[]{:S(2)}) collective-permute-start(f32[128,128]{1,0:T(8,128)S(1)} %get-tuple-element.65), channel_id=1, source_target_pairs={{0,8},{4,12},{8,0},{12,4},{16,24},{20,28},{24,16},{28,20},{1,9},{5... | collective-permute-start | bytes 196616 | tf_op jit(solution)/shard_map/ppermute | solution.py:104
  21.1 7.5 %collective-permute-start.12 = (f32[256,128]{1,0:T(8,128)S(1)}, f32[256,128]{1,0:T(8,128)S(1)}, u32[]{:S(2)}, u32[]{:S(2)}) collective-permute-start(f32[256,128]{1,0:T(8,128)S(1)} %get-tuple-element.75), channel_id=1, source_target_pairs={{0,12},{4,8},{8,4},{12,0},{16,28},{20,24},{24,20},{28,16},{1,13},{... | collective-permute-start | bytes 393224 | tf_op jit(solution)/shard_map/ppermute | solution.py:104
  23.2 2.5 %copy-start.6 = (f32[1024]{0:T(1024)S(1)}, f32[1024]{0:T(1024)}, u32[]{:S(2)}) copy-start(f32[1024]{0:T(1024)} %param.13) | copy-start | bytes 12292
  23.2 4.9 %collective-permute-start.10 = (f32[128,128]{1,0:T(8,128)S(1)}, f32[128,128]{1,0:T(8,128)S(1)}, u32[]{:S(2)}, u32[]{:S(2)}) collective-permute-start(f32[128,128]{1,0:T(8,128)S(1)} %get-tuple-element.73), channel_id=1, source_target_pairs={{0,4},{4,0},{8,12},{12,8},{16,20},{20,16},{24,28},{28,24},{1,5},{5... | collective-permute-start | bytes 196616 | tf_op jit(solution)/shard_map/ppermute | solution.py:104
  24.3 4.3 %collective-permute-start.11 = (f32[128,128]{1,0:T(8,128)S(1)}, f32[128,128]{1,0:T(8,128)S(1)}, u32[]{:S(2)}, u32[]{:S(2)}) collective-permute-start(f32[128,128]{1,0:T(8,128)S(1)} %get-tuple-element.74), channel_id=1, source_target_pairs={{0,8},{4,12},{8,0},{12,4},{16,24},{20,28},{24,16},{28,20},{1,9},{5... | collective-permute-start | bytes 196616 | tf_op jit(solution)/shard_map/ppermute | solution.py:104
  29.2 1.8 %collective-permute-start.15 = (f32[8,256]{1,0:T(8,128)S(1)}, f32[8,256]{1,0:T(8,128)S(1)}, u32[]{:S(2)}, u32[]{:S(2)}) collective-permute-start(f32[8,256]{1,0:T(8,128)S(1)} %get-tuple-element.80.refs_0_), channel_id=1, source_target_pairs={{0,3},{1,0},{2,1},{3,2},{4,7},{5,4},{6,5},{7,6},{8,11},{9,8},{10,9... | collective-permute-start | bytes 24584 | tf_op jit(solution)/shard_map/ppermute | solution.py:578
  29.2 3.7 %collective-permute-start.14 = (f32[8,256]{1,0:T(8,128)S(1)}, f32[8,256]{1,0:T(8,128)S(1)}, u32[]{:S(2)}, u32[]{:S(2)}) collective-permute-start(f32[8,256]{1,0:T(8,128)S(1)} %get-tuple-element.80.refs_0_), channel_id=1, source_target_pairs={{0,2},{1,3},{2,0},{3,1},{4,6},{5,7},{6,4},{7,5},{8,10},{9,11},{10,... | collective-permute-start | bytes 24584 | tf_op jit(solution)/shard_map/ppermute | solution.py:578
  30.8 3.1 %collective-permute-start.13 = (f32[8,256]{1,0:T(8,128)S(1)}, f32[8,256]{1,0:T(8,128)S(1)}, u32[]{:S(2)}, u32[]{:S(2)}) collective-permute-start(f32[8,256]{1,0:T(8,128)S(1)} %get-tuple-element.80.refs_0_), channel_id=1, source_target_pairs={{0,1},{1,2},{2,3},{3,0},{4,5},{5,6},{6,7},{7,4},{8,9},{9,10},{10,1... | collective-permute-start | bytes 24584 | tf_op jit(solution)/shard_map/ppermute | solution.py:578
  34.6 6.9 %collective-permute-start.16 = (f32[256,128]{1,0:T(8,128)S(1)}, f32[256,128]{1,0:T(8,128)S(1)}, u32[]{:S(2)}, u32[]{:S(2)}) collective-permute-start(f32[256,128]{1,0:T(8,128)S(1)} %get-tuple-element.88), channel_id=1, source_target_pairs={{0,12},{4,8},{8,4},{12,0},{16,28},{20,24},{24,20},{28,16},{1,13},{... | collective-permute-start | bytes 393224 | tf_op jit(solution)/shard_map/ppermute | solution.py:104
  36.0 6.2 %collective-permute-start.17 = (f32[256,128]{1,0:T(8,128)S(1)}, f32[256,128]{1,0:T(8,128)S(1)}, u32[]{:S(2)}, u32[]{:S(2)}) collective-permute-start(f32[256,128]{1,0:T(8,128)S(1)} %get-tuple-element.89), channel_id=1, source_target_pairs={{0,4},{4,0},{8,12},{12,8},{16,20},{20,16},{24,28},{28,24},{1,5},{5... | collective-permute-start | bytes 393224 | tf_op jit(solution)/shard_map/ppermute | solution.py:104
  37.0 5.3 %collective-permute-start.18 = (f32[256,128]{1,0:T(8,128)S(1)}, f32[256,128]{1,0:T(8,128)S(1)}, u32[]{:S(2)}, u32[]{:S(2)}) collective-permute-start(f32[256,128]{1,0:T(8,128)S(1)} %get-tuple-element.90), channel_id=1, source_target_pairs={{0,8},{4,12},{8,0},{12,4},{16,24},{20,28},{24,16},{28,20},{1,9},{5... | collective-permute-start | bytes 393224 | tf_op jit(solution)/shard_map/ppermute | solution.py:104
  38.1 4.1 %copy-start.4 = (f32[8,128,128]{2,1,0:T(8,128)S(1)}, f32[8,128,128]{2,1,0:T(8,128)}, u32[]{:S(2)}) copy-start(f32[8,128,128]{2,1,0:T(8,128)} %param.15) | copy-start | bytes 1572868
  42.4 7.7 %collective-permute-start.19 = (f32[264,128]{1,0:T(8,128)S(1)}, f32[264,128]{1,0:T(8,128)S(1)}, u32[]{:S(2)}, u32[]{:S(2)}) collective-permute-start(f32[264,128]{1,0:T(8,128)S(1)} %get-tuple-element.92), channel_id=1, source_target_pairs={{0,8},{4,12},{8,0},{12,4},{16,24},{20,28},{24,16},{28,20},{1,9},{5... | collective-permute-start | bytes 405512 | tf_op jit(solution)/shard_map/ppermute | solution.py:104
  43.5 6.0 %collective-permute-start.22 = (f32[256,128]{1,0:T(8,128)S(1)}, f32[256,128]{1,0:T(8,128)S(1)}, u32[]{:S(2)}, u32[]{:S(2)}) collective-permute-start(f32[256,128]{1,0:T(8,128)S(1)} %shard_map.121.refs_4_), channel_id=1, source_target_pairs={{0,16},{4,20},{8,24},{12,28},{16,0},{20,4},{24,8},{28,12},{1,17},{... | collective-permute-start | bytes 393224 | tf_op jit(solution)/shard_map/ppermute | solution.py:118
  46.3 9.6 %collective-permute-start.20 = (f32[256,128]{1,0:T(8,128)S(1)}, f32[256,128]{1,0:T(8,128)S(1)}, u32[]{:S(2)}, u32[]{:S(2)}) collective-permute-start(f32[256,128]{1,0:T(8,128)S(1)} %get-tuple-element.93), channel_id=1, source_target_pairs={{0,12},{4,8},{8,4},{12,0},{16,28},{20,24},{24,20},{28,16},{1,13},{... | collective-permute-start | bytes 393224 | tf_op jit(solution)/shard_map/ppermute | solution.py:104
  48.0 9.7 %collective-permute-start.21 = (f32[256,128]{1,0:T(8,128)S(1)}, f32[256,128]{1,0:T(8,128)S(1)}, u32[]{:S(2)}, u32[]{:S(2)}) collective-permute-start(f32[256,128]{1,0:T(8,128)S(1)} %get-tuple-element.94), channel_id=1, source_target_pairs={{0,4},{4,0},{8,12},{12,8},{16,20},{20,16},{24,28},{28,24},{1,5},{5... | collective-permute-start | bytes 393224 | tf_op jit(solution)/shard_map/ppermute | solution.py:104
  50.3 7.4 %collective-permute-start.23 = (f32[256,128]{1,0:T(8,128)S(1)}, f32[256,128]{1,0:T(8,128)S(1)}, u32[]{:S(2)}, u32[]{:S(2)}) collective-permute-start(f32[256,128]{1,0:T(8,128)S(1)} %get-tuple-element.96), channel_id=1, source_target_pairs={{0,12},{4,8},{8,4},{12,0},{16,28},{20,24},{24,20},{28,16},{1,13},{... | collective-permute-start | bytes 393224 | tf_op jit(solution)/shard_map/ppermute | solution.py:104
  54.3 5.0 %collective-permute-start.24 = (f32[256,128]{1,0:T(8,128)S(1)}, f32[256,128]{1,0:T(8,128)S(1)}, u32[]{:S(2)}, u32[]{:S(2)}) collective-permute-start(f32[256,128]{1,0:T(8,128)S(1)} %get-tuple-element.97), channel_id=1, source_target_pairs={{0,8},{4,12},{8,0},{12,4},{16,24},{20,28},{24,16},{28,20},{1,9},{5... | collective-permute-start | bytes 393224 | tf_op jit(solution)/shard_map/ppermute | solution.py:104
  54.3 5.0 %collective-permute-start.25 = (f32[256,128]{1,0:T(8,128)S(1)}, f32[256,128]{1,0:T(8,128)S(1)}, u32[]{:S(2)}, u32[]{:S(2)}) collective-permute-start(f32[256,128]{1,0:T(8,128)S(1)} %get-tuple-element.98), channel_id=1, source_target_pairs={{0,4},{4,0},{8,12},{12,8},{16,20},{20,16},{24,28},{28,24},{1,5},{5... | collective-permute-start | bytes 393224 | tf_op jit(solution)/shard_map/ppermute | solution.py:104

commit v18 on v13

--- a/solution.py
+++ b/solution.py
@@ -110,7 +110,7 @@
         return [(way, c) for c in range(self.chunks) for way in self.ways]
 
     def last_messages(self):
-        cuts = [(way, c) for c in range(self.chunks) for way in [0] + self.near]
+        cuts = [(way, c) for c in range(self.chunks) for way in [0] + self.near[:: -1 if c else 1]]
         return cuts + [(way, None) for way in self.far]
 
     def from_groups(self, piece):

time: 60.9 us -> 61.2 us (level)
  waiting for transfers between devices: 12.7 us -> 14.6 us
  starting transfers between devices: 35.9 us -> 34.3 us
    ppermute x20, starting transfers between devices: 26 us -> 24.2 us  [swap(): return lax.ppermute(piece, 'seq', pairs) if way else piece]
    ppermute x3, waiting for transfers between devices: 2.24 us -> 3.31 us  [from_groups(): lax.ppermute(piece, 'seq', [(i, (i + step * self.members) % self.blocks)...]
    ppermute x20, waiting for transfers between devices: 7.59 us -> 8.44 us  [swap(): return lax.ppermute(piece, 'seq', pairs) if way else piece]
where the time goes in v18:
time: 61.2 us; the launch traced here: 61 us
  starting transfers between devices  34.3 us (56%)
  waiting for transfers between devices  14.6 us (24%)
  Pallas kernels  11.3 us (18%)
  between operations  0.76 us (1%)
    ppermute x20, starting transfers between devices, swap(): return lax.ppermute(piece, 'seq', pairs) if way else piece  24.2 us
    pallas_call x14, Pallas kernels, call(): pl.pallas_call(body, out_shape=outs, in_specs=specs or [VMEM] * len(opera...  11.3 us
    ppermute x20, waiting for transfers between devices, swap(): return lax.ppermute(piece, 'seq', pairs) if way else piece  8.44 us
    ppermute x3, starting transfers between devices, from_groups(): lax.ppermute(piece, 'seq', [(i, (i + step * self.members) % self.blocks)...  8.24 us
    ppermute x3, waiting for transfers between devices, from_groups(): lax.ppermute(piece, 'seq', [(i, (i + step * self.members) % self.blocks)...  3.31 us
    ppermute x3, waiting for transfers between devices, on_device(): lax.ppermute(sums, 'head', [(i, (i + step) % parties) for i in range(part...  2.85 us
    ppermute x3, starting transfers between devices, on_device(): lax.ppermute(sums, 'head', [(i, (i + step) % parties) for i in range(part...  1.84 us
  transfers between devices with their start and end apart: 26, of which 14 were waited for; matrix products, arithmetic and copies ran while one was open for 0% of the time, Pallas kernels for 10%

profile of v18, /device:TPU:0, one launch (start us, length us, event | category | flops | bytes accessed | tf_op | source)
XLA Modules:
  0.0 61.0 jit_solution(18309451664040044580)
XLA Ops:
  0.6 2.2 %shard_map.111 = (f32[136,128]{1,0:T(8,128)S(1)}, f32[136,128]{1,0:T(8,128)S(1)}, f32[136,128]{1,0:T(8,128)S(1)}, f32[136,128]{1,0:T(8,128)S(1)}, f32[128,128]{1...) custom-call(bf16[256,1024]{1,0:T(8,128)(2,1)} %refs_8_.3, ...), custom_call_target="tpu_custom_call" | custom-call | tf_op jit(solution)/shard_map/pallas_call | solution.py:25
  2.8 4.0 %collective-permute-start = (f32[136,128]{1,0:T(8,128)S(1)}, f32[136,128]{1,0:T(8,128)S(1)}, u32[]{:S(2)}, u32[]{:S(2)}) collective-permute-start(f32[136,128]{1,0:T(8,128)S(1)} %get-tuple-element.58), channel_id=1, source_target_pairs={{0,12},{4,8},{8,4},{12,0},{16,28},{20,24},{24,20},{28,16},{1,13},{... | collective-permute-start | bytes 208904 | tf_op jit(solution)/shard_map/ppermute | solution.py:104
  6.9 0.5 collective-permute-start.1
  7.4 0.1 collective-permute-start.2
  7.5 2.8 %collective-permute-start.6 = (f32[128,128]{1,0:T(8,128)S(1)}, f32[128,128]{1,0:T(8,128)S(1)}, u32[]{:S(2)}, u32[]{:S(2)}) collective-permute-start(f32[128,128]{1,0:T(8,128)S(1)} %get-tuple-element.67), channel_id=1, source_target_pairs={{0,12},{4,8},{8,4},{12,0},{16,28},{20,24},{24,20},{28,16},{1,13},{... | collective-permute-start | bytes 196616 | tf_op jit(solution)/shard_map/ppermute | solution.py:104
  10.3 0.5 collective-permute-start.7
  10.9 0.8 %collective-permute-start.8 = (f32[128,128]{1,0:T(8,128)S(1)}, f32[128,128]{1,0:T(8,128)S(1)}, u32[]{:S(2)}, u32[]{:S(2)}) collective-permute-start(f32[128,128]{1,0:T(8,128)S(1)} %get-tuple-element.69), channel_id=1, source_target_pairs={{0,8},{4,12},{8,0},{12,4},{16,24},{20,28},{24,16},{28,20},{1,9},{5... | collective-permute-start | bytes 196616 | tf_op jit(solution)/shard_map/ppermute | solution.py:104
  11.6 0.4 collective-permute-done.1.refs_2_
  12.0 2.7 %collective-permute-start.3 = (f32[136,128]{1,0:T(8,128)S(1)}, f32[136,128]{1,0:T(8,128)S(1)}, u32[]{:S(2)}, u32[]{:S(2)}) collective-permute-start(f32[136,128]{1,0:T(8,128)S(1)} %get-tuple-element.61.refs_4_), channel_id=1, source_target_pairs={{0,16},{4,20},{8,24},{12,28},{16,0},{20,4},{24,8},{28,12},{1,17},{... | collective-permute-start | bytes 208904 | tf_op jit(solution)/shard_map/ppermute | solution.py:118
  14.7 0.5 collective-permute-done.8.refs_3_
  15.3 2.6 %collective-permute-start.9 = (f32[128,128]{1,0:T(8,128)S(1)}, f32[128,128]{1,0:T(8,128)S(1)}, u32[]{:S(2)}, u32[]{:S(2)}) collective-permute-start(f32[128,128]{1,0:T(8,128)S(1)} %shard_map.114.refs_4_), channel_id=1, source_target_pairs={{0,16},{4,20},{8,24},{12,28},{16,0},{20,4},{24,8},{28,12},{1,17},{... | collective-permute-start | bytes 196616 | tf_op jit(solution)/shard_map/ppermute | solution.py:118
  17.8 1.5 %collective-permute-done.3.refs_5_ = f32[136,128]{1,0:T(8,128)S(1)} collective-permute-done((f32[136,128]{1,0:T(8,128)S(1)}, f32[136,128]{1,0:T(8,128)S(1)}, u32[]{:S(2)}, u32[]{:S(2)}) %collective-permute-start.3) | collective-permute-done | bytes 69664 | tf_op jit(solution)/shard_map/ppermute | solution.py:118
  19.5 1.1 %collective-permute-start.4 = (f32[128,128]{1,0:T(8,128)S(1)}, f32[128,128]{1,0:T(8,128)S(1)}, u32[]{:S(2)}, u32[]{:S(2)}) collective-permute-start(f32[128,128]{1,0:T(8,128)S(1)} %get-tuple-element.64), channel_id=1, source_target_pairs={{0,4},{4,0},{8,12},{12,8},{16,20},{20,16},{24,28},{28,24},{1,5},{5... | collective-permute-start | bytes 196616 | tf_op jit(solution)/shard_map/ppermute | solution.py:104
  20.6 0.3 collective-permute-start.5
  21.1 2.1 %collective-permute-start.12 = (f32[256,128]{1,0:T(8,128)S(1)}, f32[256,128]{1,0:T(8,128)S(1)}, u32[]{:S(2)}, u32[]{:S(2)}) collective-permute-start(f32[256,128]{1,0:T(8,128)S(1)} %get-tuple-element.75), channel_id=1, source_target_pairs={{0,12},{4,8},{8,4},{12,0},{16,28},{20,24},{24,20},{28,16},{1,13},{... | collective-permute-start | bytes 393224 | tf_op jit(solution)/shard_map/ppermute | solution.py:104
  23.2 0.9 %collective-permute-start.10 = (f32[128,128]{1,0:T(8,128)S(1)}, f32[128,128]{1,0:T(8,128)S(1)}, u32[]{:S(2)}, u32[]{:S(2)}) collective-permute-start(f32[128,128]{1,0:T(8,128)S(1)} %get-tuple-element.73), channel_id=1, source_target_pairs={{0,8},{4,12},{8,0},{12,4},{16,24},{20,28},{24,16},{28,20},{1,9},{5... | collective-permute-start | bytes 196616 | tf_op jit(solution)/shard_map/ppermute | solution.py:104
  24.1 0.5 collective-permute-start.11
  24.6 1.2 %collective-permute-done.4.refs_0_.refs_1_ = f32[128,128]{1,0:T(8,128)S(1)} collective-permute-done((f32[128,128]{1,0:T(8,128)S(1)}, f32[128,128]{1,0:T(8,128)S(1)}, u32[]{:S(2)}, u32[]{:S(2)}) %collective-permute-start.4) | collective-permute-done | bytes 65568 | tf_op jit(solution)/shard_map/ppermute | solution.py:104
  25.8 1.2 %shard_map.116 = (bf16[8,256,256]{2,1,0:T(8,128)(2,1)S(1)}, f32[256,1024]{1,0:T(8,128)S(1)}, f32[256,1024]{1,0:T(8,128)S(1)}, bf16[8,128,256]{2,1,0:T(8,128)(2,1)S(1)}) custom-call(bf16[256,1024]{1,0:T(8,128)(2,1)S(1)} %copy-done.2, bf16[256,1024]{1,0:T(8,128)(2,1)S(1)} %copy-done, bf16[256,1024]{1,0:T(8,128)(2,1)S(1)} %copy-done.1, ...), custom_call_target="tpu_custom_call" | custom-call | flops 1000000000 | tf_op jit(solution)/shard_map/pallas_call | solution.py:25
  27.1 0.7 %collective-permute-done.10.refs_4_ = f32[128,128]{1,0:T(8,128)S(1)} collective-permute-done((f32[128,128]{1,0:T(8,128)S(1)}, f32[128,128]{1,0:T(8,128)S(1)}, u32[]{:S(2)}, u32[]{:S(2)}) %collective-permute-start.10) | collective-permute-done | bytes 65568 | tf_op jit(solution)/shard_map/ppermute | solution.py:104
  27.8 0.6 %collective-permute-done.11.refs_5_ = f32[128,128]{1,0:T(8,128)S(1)} collective-permute-done((f32[128,128]{1,0:T(8,128)S(1)}, f32[128,128]{1,0:T(8,128)S(1)}, u32[]{:S(2)}, u32[]{:S(2)}) %collective-permute-start.11) | collective-permute-done | bytes 65568 | tf_op jit(solution)/shard_map/ppermute | solution.py:104
  28.4 0.7 %shard_map.117 = (f32[256,1024]{1,0:T(8,128)S(1)}, f32[8,256]{1,0:T(8,128)S(1)}, bf16[1024,128]{1,0:T(8,128)(2,1)S(1)}) custom-call(f32[128,128]{1,0:T(8,128)S(1)} %get-tuple-element.63.refs_0_, f32[128,128]{1,0:T(8,128)S(1)} %collective-permute-done.4.refs_0_.refs_1_, f32[128,128]{1,0:T(8,128)S(1)} %collective-permute-done.5.refs_1_.refs_2_, ...), custom_call_target="tpu_custom_call" | custom-call | tf_op jit(solution)/shard_map/pallas_call | solution.py:25
  29.1 1.6 %collective-permute-start.14 = (f32[8,256]{1,0:T(8,128)S(1)}, f32[8,256]{1,0:T(8,128)S(1)}, u32[]{:S(2)}, u32[]{:S(2)}) collective-permute-start(f32[8,256]{1,0:T(8,128)S(1)} %get-tuple-element.80.refs_0_), channel_id=1, source_target_pairs={{0,2},{1,3},{2,0},{3,1},{4,6},{5,7},{6,4},{7,5},{8,10},{9,11},{10,... | collective-permute-start | bytes 24584 | tf_op jit(solution)/shard_map/ppermute | solution.py:578
  30.7 0.2 collective-permute-start.13
  30.9 1.8 %collective-permute-done.14.refs_2_ = f32[8,256]{1,0:T(8,128)S(1)} collective-permute-done((f32[8,256]{1,0:T(8,128)S(1)}, f32[8,256]{1,0:T(8,128)S(1)}, u32[]{:S(2)}, u32[]{:S(2)}) %collective-permute-start.14) | collective-permute-done | bytes 8224 | tf_op jit(solution)/shard_map/ppermute | solution.py:578
  32.8 1.0 %collective-permute-done.13.refs_1_ = f32[8,256]{1,0:T(8,128)S(1)} collective-permute-done((f32[8,256]{1,0:T(8,128)S(1)}, f32[8,256]{1,0:T(8,128)S(1)}, u32[]{:S(2)}, u32[]{:S(2)}) %collective-permute-start.13) | collective-permute-done | bytes 8224 | tf_op jit(solution)/shard_map/ppermute | solution.py:578
  33.8 0.7 %shard_map.118 = (bf16[256,1024]{1,0:T(8,128)(2,1)S(1)}, f32[1024,128]{1,0:T(8,128)S(1)}, f32[256,128]{1,0:T(8,128)S(1)}, f32[256,128]{1,0:T(8,128)S(1)}, f32[25...) custom-call(f32[8,256]{1,0:T(8,128)S(1)} %get-tuple-element.80.refs_0_, f32[8,256]{1,0:T(8,128)S(1)} %collective-permute-done.13.refs_1_, ...), custom_call_target="tpu_custom_call" | custom-call | tf_op jit(solution)/shard_map/pallas_call | solution.py:25
  34.5 1.6 %collective-permute-start.16 = (f32[256,128]{1,0:T(8,128)S(1)}, f32[256,128]{1,0:T(8,128)S(1)}, u32[]{:S(2)}, u32[]{:S(2)}) collective-permute-start(f32[256,128]{1,0:T(8,128)S(1)} %get-tuple-element.88), channel_id=1, source_target_pairs={{0,12},{4,8},{8,4},{12,0},{16,28},{20,24},{24,20},{28,16},{1,13},{... | collective-permute-start | bytes 393224 | tf_op jit(solution)/shard_map/ppermute | solution.py:104
  36.1 0.9 %collective-permute-start.17 = (f32[256,128]{1,0:T(8,128)S(1)}, f32[256,128]{1,0:T(8,128)S(1)}, u32[]{:S(2)}, u32[]{:S(2)}) collective-permute-start(f32[256,128]{1,0:T(8,128)S(1)} %get-tuple-element.89), channel_id=1, source_target_pairs={{0,4},{4,0},{8,12},{12,8},{16,20},{20,16},{24,28},{28,24},{1,5},{5... | collective-permute-start | bytes 393224 | tf_op jit(solution)/shard_map/ppermute | solution.py:104
  37.1 1.0 %collective-permute-start.18 = (f32[256,128]{1,0:T(8,128)S(1)}, f32[256,128]{1,0:T(8,128)S(1)}, u32[]{:S(2)}, u32[]{:S(2)}) collective-permute-start(f32[256,128]{1,0:T(8,128)S(1)} %get-tuple-element.90), channel_id=1, source_target_pairs={{0,8},{4,12},{8,0},{12,4},{16,24},{20,28},{24,16},{28,20},{1,9},{5... | collective-permute-start | bytes 393224 | tf_op jit(solution)/shard_map/ppermute | solution.py:104
  38.0 3.4 %shard_map.119 = (bf16[256,1024]{1,0:T(8,128)(2,1)}, f32[256,1024]{1,0:T(8,128)S(1)}, f32[256,1024]{1,0:T(8,128)S(1)}, f32[8,256,128]{2,1,0:T(8,128)S(1)}) custom-call(bf16[256,1024]{1,0:T(8,128)(2,1)S(1)} %get-tuple-element.83.attn_grad_ref, bf16[256,1024]{1,0:T(8,128)(2,1)S(1)} %copy-done.2, bf16[256,1024]{1,0:T(8,128)(2,1)S(1)} %copy-done, ...), custom_call_target="tpu_custom_call" | custom-call | flops 671088640 | tf_op jit(solution)/shard_map/pallas_call | solution.py:25
  41.4 0.7 %collective-permute-done.17.refs_2_ = f32[256,128]{1,0:T(8,128)S(1)} collective-permute-done((f32[256,128]{1,0:T(8,128)S(1)}, f32[256,128]{1,0:T(8,128)S(1)}, u32[]{:S(2)}, u32[]{:S(2)}) %collective-permute-start.17) | collective-permute-done | bytes 131104 | tf_op jit(solution)/shard_map/ppermute | solution.py:104
  42.2 0.2 shard_map.120
  42.4 1.1 %collective-permute-start.19 = (f32[264,128]{1,0:T(8,128)S(1)}, f32[264,128]{1,0:T(8,128)S(1)}, u32[]{:S(2)}, u32[]{:S(2)}) collective-permute-start(f32[264,128]{1,0:T(8,128)S(1)} %get-tuple-element.92), channel_id=1, source_target_pairs={{0,8},{4,12},{8,0},{12,4},{16,24},{20,28},{24,16},{28,20},{1,9},{5... | collective-permute-start | bytes 405512 | tf_op jit(solution)/shard_map/ppermute | solution.py:104
  43.4 0.1 shard_map.121.refs_4_
  43.5 3.0 %collective-permute-start.22 = (f32[256,128]{1,0:T(8,128)S(1)}, f32[256,128]{1,0:T(8,128)S(1)}, u32[]{:S(2)}, u32[]{:S(2)}) collective-permute-start(f32[256,128]{1,0:T(8,128)S(1)} %shard_map.121.refs_4_), channel_id=1, source_target_pairs={{0,16},{4,20},{8,24},{12,28},{16,0},{20,4},{24,8},{28,12},{1,17},{... | collective-permute-start | bytes 393224 | tf_op jit(solution)/shard_map/ppermute | solution.py:118
  46.5 0.8 %collective-permute-start.20 = (f32[256,128]{1,0:T(8,128)S(1)}, f32[256,128]{1,0:T(8,128)S(1)}, u32[]{:S(2)}, u32[]{:S(2)}) collective-permute-start(f32[256,128]{1,0:T(8,128)S(1)} %get-tuple-element.93), channel_id=1, source_target_pairs={{0,4},{4,0},{8,12},{12,8},{16,20},{20,16},{24,28},{28,24},{1,5},{5... | collective-permute-start | bytes 393224 | tf_op jit(solution)/shard_map/ppermute | solution.py:104
  47.4 1.3 %collective-permute-start.21 = (f32[256,128]{1,0:T(8,128)S(1)}, f32[256,128]{1,0:T(8,128)S(1)}, u32[]{:S(2)}, u32[]{:S(2)}) collective-permute-start(f32[256,128]{1,0:T(8,128)S(1)} %get-tuple-element.94), channel_id=1, source_target_pairs={{0,12},{4,8},{8,4},{12,0},{16,28},{20,24},{24,20},{28,16},{1,13},{... | collective-permute-start | bytes 393224 | tf_op jit(solution)/shard_map/ppermute | solution.py:104
  48.7 1.8 %collective-permute-done.22.refs_5_ = f32[256,128]{1,0:T(8,128)S(1)} collective-permute-done((f32[256,128]{1,0:T(8,128)S(1)}, f32[256,128]{1,0:T(8,128)S(1)}, u32[]{:S(2)}, u32[]{:S(2)}) %collective-permute-start.22) | collective-permute-done | bytes 131104 | tf_op jit(solution)/shard_map/ppermute | solution.py:118
  50.5 0.2 shard_map.122
  50.7 2.4 %collective-permute-start.23 = (f32[256,128]{1,0:T(8,128)S(1)}, f32[256,128]{1,0:T(8,128)S(1)}, u32[]{:S(2)}, u32[]{:S(2)}) collective-permute-start(f32[256,128]{1,0:T(8,128)S(1)} %get-tuple-element.96), channel_id=1, source_target_pairs={{0,12},{4,8},{8,4},{12,0},{16,28},{20,24},{24,20},{28,16},{1,13},{... | collective-permute-start | bytes 393224 | tf_op jit(solution)/shard_map/ppermute | solution.py:104
  53.1 1.1 %collective-permute-start.25 = (f32[256,128]{1,0:T(8,128)S(1)}, f32[256,128]{1,0:T(8,128)S(1)}, u32[]{:S(2)}, u32[]{:S(2)}) collective-permute-start(f32[256,128]{1,0:T(8,128)S(1)} %get-tuple-element.98), channel_id=1, source_target_pairs={{0,4},{4,0},{8,12},{12,8},{16,20},{20,16},{24,28},{28,24},{1,5},{5... | collective-permute-start | bytes 393224 | tf_op jit(solution)/shard_map/ppermute | solution.py:104
  54.3 1.0 %shard_map.123 = (bf16[256,1024]{1,0:T(8,128)(2,1)}, bf16[256,1024]{1,0:T(8,128)(2,1)}, f32[1024,128]{1,0:T(8,128)}) custom-call(f32[256,128]{1,0:T(8,128)S(1)} %get-tuple-element.95.refs_5_.refs_0_, f32[256,128]{1,0:T(8,128)S(1)} %get-tuple-element.103.refs_1_, f32[256,1024]{1,0:T(8,128)S(1)} %get-tuple-element.91.refs_6_.refs_2_, ...), custom_call_target="tpu_custom_call" | custom-call | tf_op jit(solution)/shard_map/pallas_call | solution.py:25
  55.2 1.4 %collective-permute-done.20.refs_1_ = f32[256,128]{1,0:T(8,128)S(1)} collective-permute-done((f32[256,128]{1,0:T(8,128)S(1)}, f32[256,128]{1,0:T(8,128)S(1)}, u32[]{:S(2)}, u32[]{:S(2)}) %collective-permute-start.20) | collective-permute-done | bytes 131104 | tf_op jit(solution)/shard_map/ppermute | solution.py:104
  56.7 0.8 %collective-permute-done.23.refs_3_ = f32[256,128]{1,0:T(8,128)S(1)} collective-permute-done((f32[256,128]{1,0:T(8,128)S(1)}, f32[256,128]{1,0:T(8,128)S(1)}, u32[]{:S(2)}, u32[]{:S(2)}) %collective-permute-start.23) | collective-permute-done | bytes 131104 | tf_op jit(solution)/shard_map/ppermute | solution.py:104
  57.5 0.6 %collective-permute-done.24.refs_4_ = f32[256,128]{1,0:T(8,128)S(1)} collective-permute-done((f32[256,128]{1,0:T(8,128)S(1)}, f32[256,128]{1,0:T(8,128)S(1)}, u32[]{:S(2)}, u32[]{:S(2)}) %collective-permute-start.24) | collective-permute-done | bytes 131104 | tf_op jit(solution)/shard_map/ppermute | solution.py:104
  58.1 1.5 %collective-permute-done.25.refs_5_ = f32[256,128]{1,0:T(8,128)S(1)} collective-permute-done((f32[256,128]{1,0:T(8,128)S(1)}, f32[256,128]{1,0:T(8,128)S(1)}, u32[]{:S(2)}, u32[]{:S(2)}) %collective-permute-start.25) | collective-permute-done | bytes 131104 | tf_op jit(solution)/shard_map/ppermute | solution.py:104
  59.6 1.4 %shard_map.124 = (bf16[256,1024]{1,0:T(8,128)(2,1)}, bf16[256,1024]{1,0:T(8,128)(2,1)}, f32[1024,128]{1,0:T(8,128)}) custom-call(f32[264,128]{1,0:T(8,128)S(1)} %collective-permute-done.19.refs_9_.refs_0_, f32[256,128]{1,0:T(8,128)S(1)} %collective-permute-done.20.refs_1_, ...), custom_call_target="tpu_custom_call", output_to_operand_aliasing={{0}: (14, {}), {1}: (15, {}), {2}: (16, {})} | custom-call | tf_op jit(solution)/shard_map/pallas_call | solution.py:25
  (32 shorter events, 0.3 us)
Async XLA Ops:
  2.8 8.0 %collective-permute-start = (f32[136,128]{1,0:T(8,128)S(1)}, f32[136,128]{1,0:T(8,128)S(1)}, u32[]{:S(2)}, u32[]{:S(2)}) collective-permute-start(f32[136,128]{1,0:T(8,128)S(1)} %get-tuple-element.58), channel_id=1, source_target_pairs={{0,12},{4,8},{8,4},{12,0},{16,28},{20,24},{24,20},{28,16},{1,13},{... | collective-permute-start | bytes 208904 | tf_op jit(solution)/shard_map/ppermute | solution.py:104
  6.9 5.1 %collective-permute-start.1 = (f32[136,128]{1,0:T(8,128)S(1)}, f32[136,128]{1,0:T(8,128)S(1)}, u32[]{:S(2)}, u32[]{:S(2)}) collective-permute-start(f32[136,128]{1,0:T(8,128)S(1)} %get-tuple-element.59), channel_id=1, source_target_pairs={{0,4},{4,0},{8,12},{12,8},{16,20},{20,16},{24,28},{28,24},{1,5},{5... | collective-permute-start | bytes 208904 | tf_op jit(solution)/shard_map/ppermute | solution.py:104
  7.4 4.6 %collective-permute-start.2 = (f32[136,128]{1,0:T(8,128)S(1)}, f32[136,128]{1,0:T(8,128)S(1)}, u32[]{:S(2)}, u32[]{:S(2)}) collective-permute-start(f32[136,128]{1,0:T(8,128)S(1)} %get-tuple-element.60), channel_id=1, source_target_pairs={{0,8},{4,12},{8,0},{12,4},{16,24},{20,28},{24,16},{28,20},{1,9},{5... | collective-permute-start | bytes 208904 | tf_op jit(solution)/shard_map/ppermute | solution.py:104
  7.5 7.2 %collective-permute-start.6 = (f32[128,128]{1,0:T(8,128)S(1)}, f32[128,128]{1,0:T(8,128)S(1)}, u32[]{:S(2)}, u32[]{:S(2)}) collective-permute-start(f32[128,128]{1,0:T(8,128)S(1)} %get-tuple-element.67), channel_id=1, source_target_pairs={{0,12},{4,8},{8,4},{12,0},{16,28},{20,24},{24,20},{28,16},{1,13},{... | collective-permute-start | bytes 196616 | tf_op jit(solution)/shard_map/ppermute | solution.py:104
  10.3 4.3 %collective-permute-start.7 = (f32[128,128]{1,0:T(8,128)S(1)}, f32[128,128]{1,0:T(8,128)S(1)}, u32[]{:S(2)}, u32[]{:S(2)}) collective-permute-start(f32[128,128]{1,0:T(8,128)S(1)} %get-tuple-element.68), channel_id=1, source_target_pairs={{0,4},{4,0},{8,12},{12,8},{16,20},{20,16},{24,28},{28,24},{1,5},{5... | collective-permute-start | bytes 196616 | tf_op jit(solution)/shard_map/ppermute | solution.py:104
  10.9 4.3 %collective-permute-start.8 = (f32[128,128]{1,0:T(8,128)S(1)}, f32[128,128]{1,0:T(8,128)S(1)}, u32[]{:S(2)}, u32[]{:S(2)}) collective-permute-start(f32[128,128]{1,0:T(8,128)S(1)} %get-tuple-element.69), channel_id=1, source_target_pairs={{0,8},{4,12},{8,0},{12,4},{16,24},{20,28},{24,16},{28,20},{1,9},{5... | collective-permute-start | bytes 196616 | tf_op jit(solution)/shard_map/ppermute | solution.py:104
  12.0 7.3 %collective-permute-start.3 = (f32[136,128]{1,0:T(8,128)S(1)}, f32[136,128]{1,0:T(8,128)S(1)}, u32[]{:S(2)}, u32[]{:S(2)}) collective-permute-start(f32[136,128]{1,0:T(8,128)S(1)} %get-tuple-element.61.refs_4_), channel_id=1, source_target_pairs={{0,16},{4,20},{8,24},{12,28},{16,0},{20,4},{24,8},{28,12},{1,17},{... | collective-permute-start | bytes 208904 | tf_op jit(solution)/shard_map/ppermute | solution.py:118
  15.2 4.2 %copy-start.3 = (f32[8,128,128]{2,1,0:T(8,128)S(1)}, f32[8,128,128]{2,1,0:T(8,128)}, u32[]{:S(2)}) copy-start(f32[8,128,128]{2,1,0:T(8,128)} %param.14) | copy-start | bytes 1572868
  15.2 10.6 %copy-start.5 = (bf16[256,1024]{1,0:T(8,128)(2,1)S(1)}, bf16[256,1024]{1,0:T(8,128)(2,1)}, u32[]{:S(2)}) copy-start(bf16[256,1024]{1,0:T(8,128)(2,1)} %upstream_ref.1) | copy-start | bytes 1572868
  15.3 5.7 %collective-permute-start.9 = (f32[128,128]{1,0:T(8,128)S(1)}, f32[128,128]{1,0:T(8,128)S(1)}, u32[]{:S(2)}, u32[]{:S(2)}) collective-permute-start(f32[128,128]{1,0:T(8,128)S(1)} %shard_map.114.refs_4_), channel_id=1, source_target_pairs={{0,16},{4,20},{8,24},{12,28},{16,0},{20,4},{24,8},{28,12},{1,17},{... | collective-permute-start | bytes 196616 | tf_op jit(solution)/shard_map/ppermute | solution.py:118
  19.4 6.4 %copy-start.1 = (bf16[256,1024]{1,0:T(8,128)(2,1)S(1)}, bf16[256,1024]{1,0:T(8,128)(2,1)}, u32[]{:S(2)}) copy-start(bf16[256,1024]{1,0:T(8,128)(2,1)} %refs_9_.1) | copy-start | bytes 1572868
  19.4 6.4 %copy-start.2 = (bf16[256,1024]{1,0:T(8,128)(2,1)S(1)}, bf16[256,1024]{1,0:T(8,128)(2,1)}, u32[]{:S(2)}) copy-start(bf16[256,1024]{1,0:T(8,128)(2,1)} %query_ref.3) | copy-start | bytes 1572868
  19.5 6.4 %copy-start = (bf16[256,1024]{1,0:T(8,128)(2,1)S(1)}, bf16[256,1024]{1,0:T(8,128)(2,1)}, u32[]{:S(2)}) copy-start(bf16[256,1024]{1,0:T(8,128)(2,1)} %refs_8_.3) | copy-start | bytes 1572868
  19.5 6.3 %collective-permute-start.4 = (f32[128,128]{1,0:T(8,128)S(1)}, f32[128,128]{1,0:T(8,128)S(1)}, u32[]{:S(2)}, u32[]{:S(2)}) collective-permute-start(f32[128,128]{1,0:T(8,128)S(1)} %get-tuple-element.64), channel_id=1, source_target_pairs={{0,4},{4,0},{8,12},{12,8},{16,20},{20,16},{24,28},{28,24},{1,5},{5... | collective-permute-start | bytes 196616 | tf_op jit(solution)/shard_map/ppermute | solution.py:104
  20.6 5.2 %collective-permute-start.5 = (f32[128,128]{1,0:T(8,128)S(1)}, f32[128,128]{1,0:T(8,128)S(1)}, u32[]{:S(2)}, u32[]{:S(2)}) collective-permute-start(f32[128,128]{1,0:T(8,128)S(1)} %get-tuple-element.65), channel_id=1, source_target_pairs={{0,8},{4,12},{8,0},{12,4},{16,24},{20,28},{24,16},{28,20},{1,9},{5... | collective-permute-start | bytes 196616 | tf_op jit(solution)/shard_map/ppermute | solution.py:104
  21.1 7.3 %collective-permute-start.12 = (f32[256,128]{1,0:T(8,128)S(1)}, f32[256,128]{1,0:T(8,128)S(1)}, u32[]{:S(2)}, u32[]{:S(2)}) collective-permute-start(f32[256,128]{1,0:T(8,128)S(1)} %get-tuple-element.75), channel_id=1, source_target_pairs={{0,12},{4,8},{8,4},{12,0},{16,28},{20,24},{24,20},{28,16},{1,13},{... | collective-permute-start | bytes 393224 | tf_op jit(solution)/shard_map/ppermute | solution.py:104
  23.2 2.6 %copy-start.6 = (f32[1024]{0:T(1024)S(1)}, f32[1024]{0:T(1024)}, u32[]{:S(2)}) copy-start(f32[1024]{0:T(1024)} %param.13) | copy-start | bytes 12292
  23.2 4.6 %collective-permute-start.10 = (f32[128,128]{1,0:T(8,128)S(1)}, f32[128,128]{1,0:T(8,128)S(1)}, u32[]{:S(2)}, u32[]{:S(2)}) collective-permute-start(f32[128,128]{1,0:T(8,128)S(1)} %get-tuple-element.73), channel_id=1, source_target_pairs={{0,8},{4,12},{8,0},{12,4},{16,24},{20,28},{24,16},{28,20},{1,9},{5... | collective-permute-start | bytes 196616 | tf_op jit(solution)/shard_map/ppermute | solution.py:104
  24.1 4.3 %collective-permute-start.11 = (f32[128,128]{1,0:T(8,128)S(1)}, f32[128,128]{1,0:T(8,128)S(1)}, u32[]{:S(2)}, u32[]{:S(2)}) collective-permute-start(f32[128,128]{1,0:T(8,128)S(1)} %get-tuple-element.74), channel_id=1, source_target_pairs={{0,4},{4,0},{8,12},{12,8},{16,20},{20,16},{24,28},{28,24},{1,5},{5... | collective-permute-start | bytes 196616 | tf_op jit(solution)/shard_map/ppermute | solution.py:104
  29.1 1.8 %collective-permute-start.15 = (f32[8,256]{1,0:T(8,128)S(1)}, f32[8,256]{1,0:T(8,128)S(1)}, u32[]{:S(2)}, u32[]{:S(2)}) collective-permute-start(f32[8,256]{1,0:T(8,128)S(1)} %get-tuple-element.80.refs_0_), channel_id=1, source_target_pairs={{0,3},{1,0},{2,1},{3,2},{4,7},{5,4},{6,5},{7,6},{8,11},{9,8},{10,9... | collective-permute-start | bytes 24584 | tf_op jit(solution)/shard_map/ppermute | solution.py:578
  29.1 3.7 %collective-permute-start.14 = (f32[8,256]{1,0:T(8,128)S(1)}, f32[8,256]{1,0:T(8,128)S(1)}, u32[]{:S(2)}, u32[]{:S(2)}) collective-permute-start(f32[8,256]{1,0:T(8,128)S(1)} %get-tuple-element.80.refs_0_), channel_id=1, source_target_pairs={{0,2},{1,3},{2,0},{3,1},{4,6},{5,7},{6,4},{7,5},{8,10},{9,11},{10,... | collective-permute-start | bytes 24584 | tf_op jit(solution)/shard_map/ppermute | solution.py:578
  30.7 3.1 %collective-permute-start.13 = (f32[8,256]{1,0:T(8,128)S(1)}, f32[8,256]{1,0:T(8,128)S(1)}, u32[]{:S(2)}, u32[]{:S(2)}) collective-permute-start(f32[8,256]{1,0:T(8,128)S(1)} %get-tuple-element.80.refs_0_), channel_id=1, source_target_pairs={{0,1},{1,2},{2,3},{3,0},{4,5},{5,6},{6,7},{7,4},{8,9},{9,10},{10,1... | collective-permute-start | bytes 24584 | tf_op jit(solution)/shard_map/ppermute | solution.py:578
  34.5 6.9 %collective-permute-start.16 = (f32[256,128]{1,0:T(8,128)S(1)}, f32[256,128]{1,0:T(8,128)S(1)}, u32[]{:S(2)}, u32[]{:S(2)}) collective-permute-start(f32[256,128]{1,0:T(8,128)S(1)} %get-tuple-element.88), channel_id=1, source_target_pairs={{0,12},{4,8},{8,4},{12,0},{16,28},{20,24},{24,20},{28,16},{1,13},{... | collective-permute-start | bytes 393224 | tf_op jit(solution)/shard_map/ppermute | solution.py:104
  36.1 6.0 %collective-permute-start.17 = (f32[256,128]{1,0:T(8,128)S(1)}, f32[256,128]{1,0:T(8,128)S(1)}, u32[]{:S(2)}, u32[]{:S(2)}) collective-permute-start(f32[256,128]{1,0:T(8,128)S(1)} %get-tuple-element.89), channel_id=1, source_target_pairs={{0,4},{4,0},{8,12},{12,8},{16,20},{20,16},{24,28},{28,24},{1,5},{5... | collective-permute-start | bytes 393224 | tf_op jit(solution)/shard_map/ppermute | solution.py:104
  37.1 5.1 %collective-permute-start.18 = (f32[256,128]{1,0:T(8,128)S(1)}, f32[256,128]{1,0:T(8,128)S(1)}, u32[]{:S(2)}, u32[]{:S(2)}) collective-permute-start(f32[256,128]{1,0:T(8,128)S(1)} %get-tuple-element.90), channel_id=1, source_target_pairs={{0,8},{4,12},{8,0},{12,4},{16,24},{20,28},{24,16},{28,20},{1,9},{5... | collective-permute-start | bytes 393224 | tf_op jit(solution)/shard_map/ppermute | solution.py:104
  38.0 4.1 %copy-start.4 = (f32[8,128,128]{2,1,0:T(8,128)S(1)}, f32[8,128,128]{2,1,0:T(8,128)}, u32[]{:S(2)}) copy-start(f32[8,128,128]{2,1,0:T(8,128)} %param.15) | copy-start | bytes 1572868
  42.4 8.1 %collective-permute-start.19 = (f32[264,128]{1,0:T(8,128)S(1)}, f32[264,128]{1,0:T(8,128)S(1)}, u32[]{:S(2)}, u32[]{:S(2)}) collective-permute-start(f32[264,128]{1,0:T(8,128)S(1)} %get-tuple-element.92), channel_id=1, source_target_pairs={{0,8},{4,12},{8,0},{12,4},{16,24},{20,28},{24,16},{28,20},{1,9},{5... | collective-permute-start | bytes 405512 | tf_op jit(solution)/shard_map/ppermute | solution.py:104
  43.5 7.0 %collective-permute-start.22 = (f32[256,128]{1,0:T(8,128)S(1)}, f32[256,128]{1,0:T(8,128)S(1)}, u32[]{:S(2)}, u32[]{:S(2)}) collective-permute-start(f32[256,128]{1,0:T(8,128)S(1)} %shard_map.121.refs_4_), channel_id=1, source_target_pairs={{0,16},{4,20},{8,24},{12,28},{16,0},{20,4},{24,8},{28,12},{1,17},{... | collective-permute-start | bytes 393224 | tf_op jit(solution)/shard_map/ppermute | solution.py:118
  46.5 10.2 %collective-permute-start.20 = (f32[256,128]{1,0:T(8,128)S(1)}, f32[256,128]{1,0:T(8,128)S(1)}, u32[]{:S(2)}, u32[]{:S(2)}) collective-permute-start(f32[256,128]{1,0:T(8,128)S(1)} %get-tuple-element.93), channel_id=1, source_target_pairs={{0,4},{4,0},{8,12},{12,8},{16,20},{20,16},{24,28},{28,24},{1,5},{5... | collective-permute-start | bytes 393224 | tf_op jit(solution)/shard_map/ppermute | solution.py:104
  47.4 9.3 %collective-permute-start.21 = (f32[256,128]{1,0:T(8,128)S(1)}, f32[256,128]{1,0:T(8,128)S(1)}, u32[]{:S(2)}, u32[]{:S(2)}) collective-permute-start(f32[256,128]{1,0:T(8,128)S(1)} %get-tuple-element.94), channel_id=1, source_target_pairs={{0,12},{4,8},{8,4},{12,0},{16,28},{20,24},{24,20},{28,16},{1,13},{... | collective-permute-start | bytes 393224 | tf_op jit(solution)/shard_map/ppermute | solution.py:104
  50.7 6.7 %collective-permute-start.23 = (f32[256,128]{1,0:T(8,128)S(1)}, f32[256,128]{1,0:T(8,128)S(1)}, u32[]{:S(2)}, u32[]{:S(2)}) collective-permute-start(f32[256,128]{1,0:T(8,128)S(1)} %get-tuple-element.96), channel_id=1, source_target_pairs={{0,12},{4,8},{8,4},{12,0},{16,28},{20,24},{24,20},{28,16},{1,13},{... | collective-permute-start | bytes 393224 | tf_op jit(solution)/shard_map/ppermute | solution.py:104
  53.1 5.0 %collective-permute-start.24 = (f32[256,128]{1,0:T(8,128)S(1)}, f32[256,128]{1,0:T(8,128)S(1)}, u32[]{:S(2)}, u32[]{:S(2)}) collective-permute-start(f32[256,128]{1,0:T(8,128)S(1)} %get-tuple-element.97), channel_id=1, source_target_pairs={{0,8},{4,12},{8,0},{12,4},{16,24},{20,28},{24,16},{28,20},{1,9},{5... | collective-permute-start | bytes 393224 | tf_op jit(solution)/shard_map/ppermute | solution.py:104
  53.1 6.4 %collective-permute-start.25 = (f32[256,128]{1,0:T(8,128)S(1)}, f32[256,128]{1,0:T(8,128)S(1)}, u32[]{:S(2)}, u32[]{:S(2)}) collective-permute-start(f32[256,128]{1,0:T(8,128)S(1)} %get-tuple-element.98), channel_id=1, source_target_pairs={{0,4},{4,0},{8,12},{12,8},{16,20},{20,16},{24,28},{28,24},{1,5},{5... | collective-permute-start | bytes 393224 | tf_op jit(solution)/shard_map/ppermute | solution.py:104
